TPU v7x, 32 devices: a whole 2x2x4 slice. The times are simulated.
32 devices in a mesh: dp: 4 (over z), mp: 8 (over y, x, core).
Axes of the slice: x: 2, y: 2, z: 4, core: 2. Of those that a mesh axis runs over, the one named last changes fastest.
Arguments:
- h_first: bfloat16 [512, 8192], P('dp', 'mp'), may hold values from -8 to 8
- h_second: bfloat16 [512, 8192], P('dp', 'mp'), may hold values from -8 to 8
- weight: bfloat16 [8192, 8192], P('dp', 'mp'), may hold values from -0.0625 to 0.0625
Outputs:
- grad_first: bfloat16 [512, 8192], P('dp', 'mp')
- grad_second: bfloat16 [512, 8192], P('dp', 'mp')
- loss: float32 [], replicated
All inputs are finite; a program needn't handle non-finite values.
Results may differ from a plain program's by a relative error of at most 0.0016.
Values may be sent and summed in bfloat16 or wider, within the bound.
No kernel may reach another device: no remote copies, remote signals or barrier semaphores. Data moves between devices by JAX's collectives and lax.ppermute only.
A program may use at most 64 MiB of HBM per device.

v0:
```python
import functools

import jax
import jax.numpy as jnp
from jax import lax
from jax.experimental import pallas as pl
from jax.experimental.pallas import tpu as pltpu
from jax.sharding import PartitionSpec as P

D = 8192


off_weight = 0.0051
bn_eps = 1e-05

F32 = jnp.float32
BF16 = jnp.bfloat16
VMEM_BYTES = 24 * 1024 * 1024
SHARED = 4
BITS = 3
LEVELS = 1 << BITS


class Place:
    def __init__(self):
        self.n = lax.axis_size("dp")
        self.k = lax.axis_size("mp") // self.n
        self.z = lax.axis_index("dp")
        self.a = lax.axis_index("mp") // self.k
        self.b = lax.axis_index("mp") % self.k

    def send(self, value, target):
        n, k = self.n, self.k
        pairs = []
        for z in range(n):
            for a in range(n):
                for b in range(k):
                    to_z, to_a, to_b = target(z, a, b)
                    pairs.append(((z * n + a) * k + b, (to_z * n + to_a) * k + to_b))
        return lax.ppermute(value, ("dp", "mp"), pairs)

    def along(self, axis):
        if axis == "z":
            return self.n, self.z, lambda step: lambda z, a, b: (z ^ step, a, b)
        if axis == "a":
            return self.n, self.a, lambda step: lambda z, a, b: (z, a ^ step, b)
        return self.k, self.b, lambda step: lambda z, a, b: (z, a, b ^ step)


def ordered(parts, place):
    bit = 1
    while bit < len(parts):
        odd = (place & bit) != 0
        parts = [jnp.where(odd, parts[i ^ bit], parts[i]) for i in range(len(parts))]
        bit *= 2
    return parts


def tree_sum(parts):
    while len(parts) > 1:
        parts = [parts[i] + parts[i + 1] for i in range(0, len(parts), 2)]
    return parts[0]


def pick(value, index):
    return lax.dynamic_index_in_dim(value, index, 0, keepdims=False)


def exchange(place, axis, value, few=False):
    size, here, toward = place.along(axis)
    return sends(place, axis, [pick(value, here ^ step) for step in range(size)], few)


def sends(place, axis, parts, few=False):
    size, here, toward = place.along(axis)
    met = [parts[0]]
    for step in range(1, size):
        part = parts[step]
        if few and step > 2:
            met[step - 2], part = lax.optimization_barrier((met[step - 2], part))
        met.append(place.send(part, toward(step)))
    return met


def reduce_scatter(place, axis, value, few=False):
    size, here, toward = place.along(axis)
    value = value.reshape((size, value.shape[0] // size) + value.shape[1:])
    return tree_sum(exchange(place, axis, value, few))


def gather(place, axis, value, few=False):
    size, here, toward = place.along(axis)
    parts = sends(place, axis, [value] * size, few)
    return jnp.concatenate(ordered(parts, here), 0)


def finish_kernel(place_ref, *refs, n, k, share):
    out_ref = refs[n]
    total = tree_sum([ref[...] for ref in refs[:n]])
    if share:
        last = (place_ref[0] == n - 1) & (place_ref[1] == n - 1) & (place_ref[2] == k - 1)
        edge = total[-8:, :128]
        row = lax.broadcasted_iota(jnp.int32, edge.shape, 0)
        column = lax.broadcasted_iota(jnp.int32, edge.shape, 1)
        taken = (row == 7) & last
        whole = jnp.sum(jnp.where(taken & (column == 0), edge, 0.0), keepdims=True)
        high = whole.astype(BF16).astype(F32)
        middle = (whole - high).astype(BF16).astype(F32)
        three = jnp.where(column == 0, high, jnp.where(column == 1, middle, whole - high - middle))
        edge = jnp.where(taken & (column < 3), three, edge)
        edge = jnp.concatenate([edge, total[-8:, 128:]], 1)
        total = jnp.concatenate([total[:-8], edge], 0)
    out_ref[...] = total.astype(BF16)


def finish(place, place_array, parts, share):
    space = pl.BlockSpec(memory_space=pltpu.VMEM)
    return pl.pallas_call(
        functools.partial(finish_kernel, n=place.n, k=place.k, share=share),
        in_specs=[pl.BlockSpec(memory_space=pltpu.SMEM)] + [space] * place.n,
        out_specs=space,
        out_shape=jax.ShapeDtypeStruct(parts[0].shape, BF16),
        name="finish",
    )(place_array, *parts)


def rounded_gram(place, place_array, part, last):
    few = not last
    part = reduce_scatter(place, "a", part, few)
    height, width = part.shape
    part = part.reshape(place.n, height // place.n, width)
    part = finish(place, place_array, exchange(place, "z", part, few), last)
    for axis in ("z", "a", "b"):
        part = gather(place, axis, part, few)
    return part


def plain_gram(place, part):
    for axis in ("b", "a", "z"):
        part = reduce_scatter(place, axis, part)
    part = part.astype(BF16)
    for axis in ("z", "a", "b"):
        part = gather(place, axis, part)
    return part


def spread(place, views):
    n = place.n
    rows, width = views[0].shape
    few = rows // n
    values = jnp.stack([view.reshape(n, few, width) for view in views], 1)
    values = values.reshape(n, len(views) * few, width)
    parts = ordered(exchange(place, "a", values), place.a ^ place.z)
    parts = ordered(sends(place, "z", parts), place.z)
    return [
        jnp.concatenate([part[view * few : (view + 1) * few] for part in parts], 0)
        for view in range(len(views))
    ]


def met_rows(place, values):
    return sends(place, "a", [values] * place.n)


def project_kernel(place_ref, *refs, n, k):
    met, others = refs[:n], refs[n : n + k - 1]
    weight_ref = refs[n + k - 1]
    own_ref, coded = refs[n + k], refs[n + k + 1 :]
    width = met[0].shape[1]
    columns = own_ref.shape[1]
    own = jnp.concatenate([ref[...] for ref in met], 0)
    for step in [*range(1, n), 0]:
        at = pl.ds(pl.multiple_of((place_ref[0] ^ step) * columns, columns), columns)
        total = 0.0
        for i in range(k):
            rows = pl.ds(pl.multiple_of((place_ref[2] ^ i) * width, width), width)
            values = own if i == 0 else others[i - 1][...]
            total += jnp.dot(values, weight_ref[rows, at], preferred_element_type=F32)
        if step == 0:
            own_ref[...] = total
        else:
            encode(total, coded[step - 1])


def unit(near):
    near = jnp.abs(near)
    return (near * (1.0 + 1.01 / 256.0)).astype(BF16).astype(F32) - near


def encode(total, coded_ref):
    coarse = total.astype(BF16)
    batch = total.shape[0]
    coded_ref[:batch] = coarse
    near = coarse.astype(F32)
    step = unit(near)
    level = (total - near) / jnp.where(step > 0.0, step, 1.0)
    level = jnp.clip(jnp.floor((level + 0.5) * LEVELS), 0.0, LEVELS - 1.0).astype(jnp.int32)
    height = batch // SHARED
    first, second, third, fourth = [level[i * height : (i + 1) * height] for i in range(SHARED)]
    word = 128 + (first << BITS) + second + ((fourth & 1) << 6)
    word = word << (third + ((fourth & 4) << 1))
    word = jnp.where((fourth & 2) != 0, -word, word)
    coded_ref[batch:] = word.astype(F32).astype(BF16)


def decode(coded_ref):
    height = coded_ref.shape[0] // (SHARED + 1)
    word = coded_ref[SHARED * height :].astype(F32).astype(jnp.int32)
    negative = word < 0
    word = jnp.abs(word)
    power = jnp.zeros_like(word)
    for shift in (8, 4, 2, 1):
        large = word >= (128 << shift)
        word = jnp.where(large, word >> shift, word)
        power = power + jnp.where(large, shift, 0)
    levels = [
        (word >> BITS) & (LEVELS - 1),
        word & (LEVELS - 1),
        power & (LEVELS - 1),
        ((word >> 6) & 1) + jnp.where(negative, 2, 0) + ((power >> 3) << 2),
    ]
    blocks = []
    for i, level in enumerate(levels):
        near = coded_ref[i * height : (i + 1) * height].astype(F32)
        offset = (level.astype(F32) + (0.5 - LEVELS / 2)) * (1.0 / LEVELS)
        blocks.append(near + unit(near) * offset)
    return blocks


def project(place, place_array, met, others, weight):
    n, k = place.n, place.k
    rows, width = met[0].shape
    batch, columns = rows * n, weight.shape[1] // n
    coded = batch + batch // SHARED
    out_shape = [jax.ShapeDtypeStruct((batch, columns), F32)]
    out_shape += [jax.ShapeDtypeStruct((coded, columns), BF16)] * (n - 1)
    args = [*met, *others, weight]
    space = pl.BlockSpec(memory_space=pltpu.VMEM)
    own, *parts = pl.pallas_call(
        functools.partial(project_kernel, n=n, k=k),
        in_specs=[pl.BlockSpec(memory_space=pltpu.SMEM)] + [space] * len(args),
        out_specs=[space] * n,
        out_shape=out_shape,
        compiler_params=pltpu.CompilerParams(vmem_limit_bytes=VMEM_BYTES),
        cost_estimate=pl.CostEstimate(
            flops=2 * batch * k * width * n * columns,
            bytes_accessed=2 * k * width * (batch + n * columns) + 3 * n * batch * columns,
            transcendentals=0,
        ),
        name="project",
    )(place_array, *args)
    return own, parts


def normalize_kernel(place_ref, *refs, n, k, second):
    own_ref, parts = refs[0], refs[1:n]
    refs = refs[n:]
    if second:
        other_ref, refs = refs[0], refs[1:]
    norm_ref, packed_ref, scale_ref = refs[:3]
    grams = refs[3 : 3 + k]
    batch, columns = own_ref.shape
    height = batch // SHARED
    met = [[own_ref[i * height : (i + 1) * height] for i in range(SHARED)]]
    for step in range(1, n):
        met.append(decode(parts[step - 1]))
    blocks = [tree_sum([met[step][i] for step in range(n)]) for i in range(SHARED)]
    total = tree_sum([jnp.sum(block, 0, keepdims=True) for block in blocks])
    squares = tree_sum([jnp.sum(block * block, 0, keepdims=True) for block in blocks])
    mean = total / batch
    scale = lax.rsqrt(squares / batch - mean * mean + bn_eps)
    scale_ref[...] = scale
    rows, few = batch // n, batch // (n * n)
    for i, block in enumerate(blocks):
        normed = (block - mean) * scale
        for first in range(0, height, few):
            step, plane = divmod((i * height + first) // few, n)
            at = pl.multiple_of(plane * rows + (place_ref[1] ^ step) * few, few)
            norm_ref[pl.ds(at, few), :] = normed[first : first + few]
            packed_ref[pl.ds(at, few), :] = normed[first : first + few].astype(BF16)
    dims = (((1,), (1,)), ((), ()))
    packed = packed_ref[...]
    size = batch // k
    for i in range(k):
        at = pl.multiple_of((place_ref[2] ^ i) * size, size)
        gram = lax.dot_general(packed_ref[pl.ds(at, size), :], packed, dims, preferred_element_type=F32)
        grams[i][...] = gram
    if second:
        coeff_ref = refs[3 + k]
        diag = jnp.sum(norm_ref[...] * other_ref[...], 0, keepdims=True) / batch
        coeff_ref[...] = 2.0 * ((1.0 - off_weight) * diag - 1.0)
        share = jnp.sum((1.0 - diag) ** 2 - off_weight * diag * diag, 1, keepdims=True)
        for i in range(k):

            @pl.when((place_ref[2] ^ i) == k - 1)
            def _():
                row = grams[i][size - 8 :, :128]
                first = (lax.broadcasted_iota(jnp.int32, row.shape, 0) == 7) & (
                    lax.broadcasted_iota(jnp.int32, row.shape, 1) == 0
                )
                grams[i][size - 8 :, :128] = jnp.where(first, share, row)


def normalize_parts(place, place_array, own, parts, other=None):
    n, k = place.n, place.k
    batch, columns = own.shape
    second = other is not None
    out_shape = [
        jax.ShapeDtypeStruct((batch, columns), F32),
        jax.ShapeDtypeStruct((batch, columns), BF16),
        jax.ShapeDtypeStruct((1, columns), F32),
    ] + [jax.ShapeDtypeStruct((batch // k, batch), F32)] * k
    if second:
        out_shape.append(jax.ShapeDtypeStruct((1, columns), F32))
    args = [own, *parts] + ([other] if second else [])
    space = pl.BlockSpec(memory_space=pltpu.VMEM)
    return pl.pallas_call(
        functools.partial(normalize_kernel, n=n, k=k, second=second),
        in_specs=[pl.BlockSpec(memory_space=pltpu.SMEM)] + [space] * len(args),
        out_specs=[space] * len(out_shape),
        out_shape=out_shape,
        compiler_params=pltpu.CompilerParams(vmem_limit_bytes=VMEM_BYTES),
        cost_estimate=pl.CostEstimate(
            flops=2 * batch * batch * columns,
            bytes_accessed=16 * batch * columns + 4 * batch * batch,
            transcendentals=0,
        ),
        name="normalize",
    )(place_array, *args)


def gradient_kernel(place_ref, *refs, n, last):
    gram_ref, packed_ref, norm_ref, other_ref, scale_ref, coeff_ref = refs[:6]
    refs = refs[6:]
    if last:
        first_ref, refs = refs[0], refs[1:]
    outs, whole_ref = refs[:n], refs[-1]
    batch, columns = norm_ref.shape
    gram = gram_ref[...]
    if last:
        edge = batch - 128
        tail = gram[edge:, :128]
        row = lax.broadcasted_iota(jnp.int32, tail.shape, 0)
        column = lax.broadcasted_iota(jnp.int32, tail.shape, 1)
        taken = (row == 127) & (column < 3)
        mirror = gram[:128, edge:].astype(F32).T
        share = jnp.sum(jnp.where(taken, tail.astype(F32), 0.0), keepdims=True)
        fixed = jnp.where(taken, mirror, tail.astype(F32)).astype(BF16)
        gram = jnp.concatenate(
            [gram[:edge], jnp.concatenate([fixed, gram[edge:, 128:]], 1)], 0
        )
        frob = jnp.sum(gram.astype(F32) * first_ref[...].astype(F32), keepdims=True)
        refs[n][...] = (share + off_weight * (frob / (batch * batch))) / D
    factor = 2.0 * off_weight / batch
    norm = norm_ref[...]
    grad = (
        factor * jnp.dot(gram, packed_ref[...], preferred_element_type=F32)
        + coeff_ref[...] * other_ref[...]
    )
    first = jnp.sum(grad, 0, keepdims=True) / batch
    second = jnp.sum(grad * norm, 0, keepdims=True) / batch
    whole_ref[...] = (scale_ref[...] * (grad - first - norm * second)).astype(BF16)
    rows = batch // n
    for step in range(n):
        at = pl.multiple_of((place_ref[0] ^ step) * rows, rows)
        outs[step][...] = whole_ref[pl.ds(at, rows), :]


def gradient(place, place_array, gram, packed, norm, other, scale, coeff, first=None):
    n = place.n
    batch, columns = norm.shape
    last = first is not None
    out_shape = [jax.ShapeDtypeStruct((batch // n, columns), BF16)] * n
    if last:
        out_shape.append(jax.ShapeDtypeStruct((1, 1), F32))
    args = [gram, packed, norm, other, scale, coeff] + ([first] if last else [])
    space = pl.BlockSpec(memory_space=pltpu.VMEM)
    return pl.pallas_call(
        functools.partial(gradient_kernel, n=n, last=last),
        in_specs=[pl.BlockSpec(memory_space=pltpu.SMEM)] + [space] * len(args),
        out_specs=[space] * len(out_shape),
        out_shape=out_shape,
        scratch_shapes=[pltpu.VMEM((batch, columns), BF16)],
        compiler_params=pltpu.CompilerParams(vmem_limit_bytes=VMEM_BYTES),
        cost_estimate=pl.CostEstimate(
            flops=2 * batch * batch * columns,
            bytes_accessed=14 * batch * columns + 2 * batch * batch,
            transcendentals=0,
        ),
        name="gradient",
    )(place_array, *args)


def joined(place, parts):
    return jnp.concatenate(ordered(sends(place, "z", parts), place.z), 1)


def with_kernels(place, h_first, h_second, weight):
    n, k, z, a, b = place.n, place.k, place.z, place.a, place.b
    place_array = jnp.stack([z, a, b]).astype(jnp.int32)
    both = spread(place, (h_first, h_second))

    def projected(values):
        met = met_rows(place, values)
        own = jnp.concatenate(met, 0)
        others = [
            place.send(own, lambda z, a, b, s=step: (z, a, b ^ s)) for step in range(1, k)
        ]
        return project(place, place_array, met, others, weight)

    def halves(grams):
        part = grams[0]
        for step in range(1, k):
            part = part + place.send(grams[step], lambda z, a, b, s=step: (z, a, b ^ s))
        return part

    def sent(parts):
        return sends(place, "z", [parts[0], *parts])[1:]

    own_1, parts_1 = projected(both[0])
    parts_1 = sent(parts_1)
    own_2, parts_2 = projected(both[1])
    own_1, parts_1, own_2, parts_2 = lax.optimization_barrier((own_1, parts_1, own_2, parts_2))
    parts_2 = sent(parts_2)
    norm_1, packed_1, scale_1, *grams = normalize_parts(place, place_array, own_1, parts_1)
    gram_1 = rounded_gram(place, place_array, halves(grams), False)
    own_2, parts_2, gram_1 = lax.optimization_barrier((own_2, parts_2, gram_1))
    norm_2, packed_2, scale_2, *grams, coeff = normalize_parts(
        place, place_array, own_2, parts_2, norm_1
    )
    grads_2 = gradient(
        place, place_array, gram_1, packed_2, norm_2, norm_1, scale_2, coeff
    )
    out_2 = joined(place, grads_2)
    gram_2 = rounded_gram(place, place_array, halves(grams), True)
    *grads_1, loss = gradient(
        place, place_array, gram_2, packed_1, norm_1, norm_2, scale_1, coeff, gram_1
    )
    return (joined(place, grads_1), out_2, loss.reshape(()))


def plain(place, h_first, h_second, weight):
    n, k, z, a, b = place.n, place.k, place.z, place.a, place.b
    rows, width = h_first.shape
    batch = rows * n
    columns = weight.shape[1] // n
    weight_parts = weight.reshape(k, width, n * columns)
    zs = []
    for values in (h_first, h_second):
        moved = place.send(values, lambda z, a, b: (a, z, b))
        own = jnp.concatenate(met_rows(place, moved), 0)
        total = jnp.dot(own, pick(weight_parts, b), preferred_element_type=F32)
        for step in range(1, k):
            other = place.send(own, lambda z, a, b, s=step: (z, a, b ^ s))
            total += jnp.dot(other, pick(weight_parts, b ^ step), preferred_element_type=F32)
        cut = total.reshape(batch, n, columns).transpose(1, 0, 2)
        whole = tree_sum(exchange(place, "z", cut)).reshape(n, rows, columns)
        zs.append(jnp.concatenate(ordered([whole[i] for i in range(n)], a), 0))
    normed, scales = [], []
    for values in zs:
        mean = jnp.sum(values, 0) / batch
        scale = lax.rsqrt(jnp.sum(values * values, 0) / batch - mean * mean + bn_eps)
        normed.append((values - mean) * scale)
        scales.append(scale)
    diag = jnp.sum(normed[0] * normed[1], 0) / batch
    packed = [values.astype(BF16) for values in normed]
    dims = (((1,), (1,)), ((), ()))
    grams = []
    for values in packed:
        gram = lax.dot_general(values, values, dims, preferred_element_type=F32)
        grams.append(plain_gram(place, gram))
    frob = jnp.sum(grams[0].astype(F32) * grams[1].astype(F32)) / (batch * batch)
    coeff = 2.0 * ((1.0 - off_weight) * diag - 1.0)
    factor = 2.0 * off_weight / batch
    outs = []
    for view in range(2):
        grad = (
            factor * jnp.dot(grams[1 - view], packed[view], preferred_element_type=F32)
            + coeff * normed[1 - view]
        )
        first = jnp.sum(grad, 0) / batch
        second = jnp.sum(grad * normed[view], 0) / batch
        out = (scales[view] * (grad - first - normed[view] * second)).astype(BF16)
        parts = exchange(place, "z", out.reshape(n, rows, columns))
        outs.append(jnp.concatenate(ordered(parts, z), 1))
    share = jnp.sum((1.0 - diag) ** 2) - off_weight * jnp.sum(diag * diag)
    loss = (lax.psum(share, ("dp", "mp")) + off_weight * frob) / D
    return (outs[0], outs[1], loss)


def per_device(h_first, h_second, weight):
    place = Place()
    columns = weight.shape[1] // place.n
    fits = columns % 128 == 0 and place.n == SHARED
    return (with_kernels if fits else plain)(place, h_first, h_second, weight)


def solution(mesh):
    in_specs = (P("dp", "mp"), P("dp", "mp"), P("dp", "mp"))
    out_specs = (P("dp", "mp"), P("dp", "mp"), P())
    return jax.shard_map(
        per_device, mesh=mesh, in_specs=in_specs, out_specs=out_specs, check_vma=False
    )
```

profile of v0, /device:TPU:0, one launch (start us, length us, event | category | flops | bytes accessed | tf_op | source)
XLA Modules:
  0.0 226.0 jit_solution(2752870722306967559)
XLA Ops:
  1.8 3.0 %collective-permute-start = (bf16[64,1024]{1,0:T(8,128)(2,1)S(1)}, bf16[64,1024]{1,0:T(8,128)(2,1)S(1)}, u32[]{:S(2)}, u32[]{:S(2)}) collective-permute-start(bf16[64,1024]{1,0:T(8,128)(2,1)S(1)} %get-tuple-element.119), channel_id=1, source_target_pairs={{0,2},{1,3},{2,0},{3,1},{4,6},{5,7},{6,4},{7,5},{8,10},{9,11},{10,... | collective-permute-start | bytes 393224 | tf_op jit(solution)/shard_map/ppermute | solution.py:40
  4.8 1.5 collective-permute-start.1
  6.4 2.4 %collective-permute-done = bf16[64,1024]{1,0:T(8,128)(2,1)S(1)} collective-permute-done((bf16[64,1024]{1,0:T(8,128)(2,1)S(1)}, bf16[64,1024]{1,0:T(8,128)(2,1)S(1)}, u32[]{:S(2)}, u32[]{:S(2)}) %collective-permute-start) | collective-permute-done | bytes 131104 | tf_op jit(solution)/shard_map/ppermute | solution.py:40
  8.7 3.9 %collective-permute-done.1 = bf16[64,1024]{1,0:T(8,128)(2,1)S(1)} collective-permute-done((bf16[64,1024]{1,0:T(8,128)(2,1)S(1)}, bf16[64,1024]{1,0:T(8,128)(2,1)S(1)}, u32[]{:S(2)}, u32[]{:S(2)}) %collective-permute-start.1) | collective-permute-done | bytes 131104 | tf_op jit(solution)/shard_map/ppermute | solution.py:40
  12.7 3.7 %collective-permute-start.3 = (bf16[64,1024]{1,0:T(8,128)(2,1)S(1)}, bf16[64,1024]{1,0:T(8,128)(2,1)S(1)}, u32[]{:S(2)}, u32[]{:S(2)}) collective-permute-start(bf16[64,1024]{1,0:T(8,128)(2,1)S(1)} %get-tuple-element.105), channel_id=1, source_target_pairs={{0,24},{1,25},{2,26},{3,27},{4,28},{5,29},{6,30},{7,31},{8,16},{9,... | collective-permute-start | bytes 393224 | tf_op jit(solution)/shard_map/ppermute | solution.py:40
  17.1 3.6 %collective-permute-done.3 = bf16[64,1024]{1,0:T(8,128)(2,1)S(1)} collective-permute-done((bf16[64,1024]{1,0:T(8,128)(2,1)S(1)}, bf16[64,1024]{1,0:T(8,128)(2,1)S(1)}, u32[]{:S(2)}, u32[]{:S(2)}) %collective-permute-start.3) | collective-permute-done | bytes 131104 | tf_op jit(solution)/shard_map/ppermute | solution.py:40
  20.7 5.4 %collective-permute-done.4 = bf16[64,1024]{1,0:T(8,128)(2,1)S(1)} collective-permute-done((bf16[64,1024]{1,0:T(8,128)(2,1)S(1)}, bf16[64,1024]{1,0:T(8,128)(2,1)S(1)}, u32[]{:S(2)}, u32[]{:S(2)}) %collective-permute-start.4) | collective-permute-done | bytes 131104 | tf_op jit(solution)/shard_map/ppermute | solution.py:40
  28.8 1.7 collective-permute-start.6
  32.4 1.7 collective-permute-start.13
  34.6 3.5 %collective-permute-done.6.refs_1_ = bf16[128,1024]{1,0:T(8,128)(2,1)S(1)} collective-permute-done((bf16[128,1024]{1,0:T(8,128)(2,1)S(1)}, bf16[128,1024]{1,0:T(8,128)(2,1)S(1)}, u32[]{:S(2)}, u32[]{:S(2)}) %collective-permute-start.6) | collective-permute-done | bytes 262176 | tf_op jit(solution)/shard_map/ppermute | solution.py:40
  38.1 1.6 collective-permute-start.15
  40.4 4.9 %collective-permute-done.7.refs_2_ = bf16[128,1024]{1,0:T(8,128)(2,1)S(1)} collective-permute-done((bf16[128,1024]{1,0:T(8,128)(2,1)S(1)}, bf16[128,1024]{1,0:T(8,128)(2,1)S(1)}, u32[]{:S(2)}, u32[]{:S(2)}) %collective-permute-start.7) | collective-permute-done | bytes 262176 | tf_op jit(solution)/shard_map/ppermute | solution.py:40
  46.8 2.6 %collective-permute-done.13.refs_1_ = bf16[128,1024]{1,0:T(8,128)(2,1)S(1)} collective-permute-done((bf16[128,1024]{1,0:T(8,128)(2,1)S(1)}, bf16[128,1024]{1,0:T(8,128)(2,1)S(1)}, u32[]{:S(2)}, u32[]{:S(2)}) %collective-permute-start.13) | collective-permute-done | bytes 262176 | tf_op jit(solution)/shard_map/ppermute | solution.py:40
  49.4 5.0 %collective-permute-done.14.refs_2_ = bf16[128,1024]{1,0:T(8,128)(2,1)S(1)} collective-permute-done((bf16[128,1024]{1,0:T(8,128)(2,1)S(1)}, bf16[128,1024]{1,0:T(8,128)(2,1)S(1)}, u32[]{:S(2)}, u32[]{:S(2)}) %collective-permute-start.14) | collective-permute-done | bytes 262176 | tf_op jit(solution)/shard_map/ppermute | solution.py:40
  54.6 2.2 copy-done.3
  56.8 4.6 %project.2 = (f32[512,256]{1,0:T(8,128)S(1)}, bf16[640,256]{1,0:T(8,128)(2,1)S(1)}, bf16[640,256]{1,0:T(8,128)(2,1)S(1)}, bf16[640,256]{1,0:T(8,128)(2,1)S(1)}) custom-call(s32[3]{0:T(128)S(1)} %pad_add_fusion.place_ref, bf16[128,1024]{1,0:T(8,128)(2,1)S(1)} %pad_maximum_fusion.3.refs_0_, bf16[128,1024]{1,0:T(8,128)(2,1)S(1)} %collective-permute-done.6.refs_1_, ...), custom_call_target="tpu_custom_call" | custom-call | flops 2147483648 | bytes 7864320 | tf_op jit(solution)/shard_map/project/pallas_call | solution.py:239
  61.5 1.7 collective-permute-start.11
  63.2 2.7 %collective-permute-start.12 = (bf16[640,256]{1,0:T(8,128)(2,1)S(1)}, bf16[640,256]{1,0:T(8,128)(2,1)S(1)}, u32[]{:S(2)}, u32[]{:S(2)}) collective-permute-start(bf16[640,256]{1,0:T(8,128)(2,1)S(1)} %get-tuple-element.55), channel_id=1, source_target_pairs={{0,24},{1,25},{2,26},{3,27},{4,28},{5,29},{6,30},{7,31},{8,16},{9,... | collective-permute-start | bytes 983048 | tf_op jit(solution)/shard_map/ppermute | solution.py:40
  65.9 4.5 %project.3 = (f32[512,256]{1,0:T(8,128)S(1)}, bf16[640,256]{1,0:T(8,128)(2,1)S(1)}, bf16[640,256]{1,0:T(8,128)(2,1)S(1)}, bf16[640,256]{1,0:T(8,128)(2,1)S(1)}) custom-call(s32[3]{0:T(128)S(1)} %pad_add_fusion.place_ref, bf16[128,1024]{1,0:T(8,128)(2,1)S(1)} %pad_maximum_fusion.4.refs_0_, bf16[128,1024]{1,0:T(8,128)(2,1)S(1)} %collective-permute-done.13.refs_1_, ...), custom_call_target="tpu_custom_call" | custom-call | flops 2147483648 | bytes 7864320 | tf_op jit(solution)/shard_map/project/pallas_call | solution.py:239
  70.3 6.7 %collective-permute-done.10.refs_1_ = bf16[640,256]{1,0:T(8,128)(2,1)S(1)} collective-permute-done((bf16[640,256]{1,0:T(8,128)(2,1)S(1)}, bf16[640,256]{1,0:T(8,128)(2,1)S(1)}, u32[]{:S(2)}, u32[]{:S(2)}) %collective-permute-start.10) | collective-permute-done | bytes 327712 | tf_op jit(solution)/shard_map/ppermute | solution.py:40
  77.1 10.0 %collective-permute-done.11.refs_2_ = bf16[640,256]{1,0:T(8,128)(2,1)S(1)} collective-permute-done((bf16[640,256]{1,0:T(8,128)(2,1)S(1)}, bf16[640,256]{1,0:T(8,128)(2,1)S(1)}, u32[]{:S(2)}, u32[]{:S(2)}) %collective-permute-start.11) | collective-permute-done | bytes 327712 | tf_op jit(solution)/shard_map/ppermute | solution.py:40
  87.1 2.3 %normalize.2 = (f32[512,256]{1,0:T(8,128)S(1)}, bf16[512,256]{1,0:T(8,128)(2,1)S(1)}, f32[1,256]{1,0:T(1,128)S(1)}, f32[256,512]{1,0:T(8,128)S(1)}, f32[256,512]{1,0:T(8,128)S(1)}) custom-call(s32[3]{0:T(128)S(1)} %pad_add_fusion.place_ref, f32[512,256]{1,0:T(8,128)S(1)} %get-tuple-element.64.refs_0_, bf16[640,256]{1,0:T(8,128)(2,1)S(1)} %collective-permute-done.10.refs_1_, ...), custom_call_target="tpu_custom_call" | custom-call | flops 134217728 | bytes 3145728 | tf_op jit(solution)/shard_map/normalize/pallas_call | solution.py:317
  89.5 1.9 collective-permute-done.20
  92.0 1.4 collective-permute-start.22
  93.3 3.8 %collective-permute-done.21 = f32[64,512]{1,0:T(8,128)S(1)} collective-permute-done((f32[64,512]{1,0:T(8,128)S(1)}, f32[64,512]{1,0:T(8,128)S(1)}, u32[]{:S(2)}, u32[]{:S(2)}) %collective-permute-start.21) | collective-permute-done | bytes 131104 | tf_op jit(solution)/shard_map/ppermute | solution.py:40
  98.3 4.7 %collective-permute-done.23 = f32[64,512]{1,0:T(8,128)S(1)} collective-permute-done((f32[64,512]{1,0:T(8,128)S(1)}, f32[64,512]{1,0:T(8,128)S(1)}, u32[]{:S(2)}, u32[]{:S(2)}) %collective-permute-start.23) | collective-permute-done | bytes 131104 | tf_op jit(solution)/shard_map/ppermute | solution.py:40
  103.7 7.2 %collective-permute-start.24 = (f32[16,512]{1,0:T(8,128)S(1)}, f32[16,512]{1,0:T(8,128)S(1)}, u32[]{:S(2)}, u32[]{:S(2)}) collective-permute-start(f32[16,512]{1,0:T(8,128)S(1)} %get-tuple-element.142), channel_id=1, source_target_pairs={{0,8},{1,9},{2,10},{3,11},{4,12},{5,13},{6,14},{7,15},{8,0},{9,1},... | collective-permute-start | bytes 98312 | tf_op jit(solution)/shard_map/ppermute | solution.py:40
  110.9 2.1 collective-permute-done.24.refs_1_
  115.7 3.0 %collective-permute-done.26.refs_3_ = f32[16,512]{1,0:T(8,128)S(1)} collective-permute-done((f32[16,512]{1,0:T(8,128)S(1)}, f32[16,512]{1,0:T(8,128)S(1)}, u32[]{:S(2)}, u32[]{:S(2)}) %collective-permute-start.26) | collective-permute-done | bytes 32800 | tf_op jit(solution)/shard_map/ppermute | solution.py:40
  119.3 1.4 finish.2
  120.7 1.9 collective-permute-start.29
  122.6 2.1 collective-permute-done.27
  126.0 4.4 %collective-permute-done.28 = bf16[16,512]{1,0:T(8,128)(2,1)S(1)} collective-permute-done((bf16[16,512]{1,0:T(8,128)(2,1)}, bf16[16,512]{1,0:T(8,128)(2,1)S(1)}, u32[]{:S(2)}, u32[]{:S(2)}) %collective-permute-start.28) | collective-permute-done | bytes 16416 | tf_op jit(solution)/shard_map/ppermute | solution.py:40
  131.6 1.4 collective-permute-start.32
  133.0 2.5 %collective-permute-done.30 = bf16[64,512]{1,0:T(8,128)(2,1)S(1)} collective-permute-done((bf16[64,512]{1,0:T(8,128)(2,1)S(1)}, bf16[64,512]{1,0:T(8,128)(2,1)S(1)}, u32[]{:S(2)}, u32[]{:S(2)}) %collective-permute-start.30) | collective-permute-done | bytes 65568 | tf_op jit(solution)/shard_map/ppermute | solution.py:40
  136.7 4.0 %collective-permute-done.31 = bf16[64,512]{1,0:T(8,128)(2,1)S(1)} collective-permute-done((bf16[64,512]{1,0:T(8,128)(2,1)S(1)}, bf16[64,512]{1,0:T(8,128)(2,1)S(1)}, u32[]{:S(2)}, u32[]{:S(2)}) %collective-permute-start.31) | collective-permute-done | bytes 65568 | tf_op jit(solution)/shard_map/ppermute | solution.py:40
  141.0 1.9 collective-permute-start.18
  142.8 2.5 %collective-permute-start.19 = (bf16[640,256]{1,0:T(8,128)(2,1)S(1)}, bf16[640,256]{1,0:T(8,128)(2,1)S(1)}, u32[]{:S(2)}, u32[]{:S(2)}) collective-permute-start(bf16[640,256]{1,0:T(8,128)(2,1)S(1)} %get-tuple-element.63), channel_id=1, source_target_pairs={{0,24},{1,25},{2,26},{3,27},{4,28},{5,29},{6,30},{7,31},{8,16},{9,... | collective-permute-start | bytes 983048 | tf_op jit(solution)/shard_map/ppermute | solution.py:40
  145.5 11.7 %collective-permute-done.17.refs_1_ = bf16[640,256]{1,0:T(8,128)(2,1)S(1)} collective-permute-done((bf16[640,256]{1,0:T(8,128)(2,1)}, bf16[640,256]{1,0:T(8,128)(2,1)S(1)}, u32[]{:S(2)}, u32[]{:S(2)}) %collective-permute-start.17) | collective-permute-done | bytes 327712 | tf_op jit(solution)/shard_map/ppermute | solution.py:40
  157.2 9.4 %collective-permute-done.18.refs_2_ = bf16[640,256]{1,0:T(8,128)(2,1)S(1)} collective-permute-done((bf16[640,256]{1,0:T(8,128)(2,1)S(1)}, bf16[640,256]{1,0:T(8,128)(2,1)S(1)}, u32[]{:S(2)}, u32[]{:S(2)}) %collective-permute-start.18) | collective-permute-done | bytes 327712 | tf_op jit(solution)/shard_map/ppermute | solution.py:40
  166.6 2.5 %normalize.3 = (f32[512,256]{1,0:T(8,128)S(1)}, bf16[512,256]{1,0:T(8,128)(2,1)S(1)}, f32[1,256]{1,0:T(1,128)S(1)}, f32[256,512]{1,0:T(8,128)S(1)}, f32[256,512]{1,0:T(8,128)S(1)}, /*index=5*/f32[1,256]{1,0:T(1,128)S(1)}) custom-call(s32[3]{0:T(128)S(1)} %copy-done.1, f32[512,256]{1,0:T(8,128)S(1)} %get-tuple-element.78.refs_0_, ...), custom_call_target="tpu_custom_call" | custom-call | flops 134217728 | bytes 3145728 | tf_op jit(solution)/shard_map/normalize/pallas_call | solution.py:317
  169.2 1.9 collective-permute-done.34
  171.6 1.4 collective-permute-start.36
  173.0 1.7 collective-permute-start.37
  174.8 2.9 %collective-permute-done.35 = f32[64,512]{1,0:T(8,128)S(1)} collective-permute-done((f32[64,512]{1,0:T(8,128)S(1)}, f32[64,512]{1,0:T(8,128)S(1)}, u32[]{:S(2)}, u32[]{:S(2)}) %collective-permute-start.35) | collective-permute-done | bytes 131104 | tf_op jit(solution)/shard_map/ppermute | solution.py:40
  177.6 2.1 collective-permute-done.36
  180.4 7.0 %collective-permute-start.38 = (f32[16,512]{1,0:T(8,128)S(1)}, f32[16,512]{1,0:T(8,128)S(1)}, u32[]{:S(2)}, u32[]{:S(2)}) collective-permute-start(f32[16,512]{1,0:T(8,128)S(1)} %get-tuple-element.138), channel_id=1, source_target_pairs={{0,8},{1,9},{2,10},{3,11},{4,12},{5,13},{6,14},{7,15},{8,0},{9,1},... | collective-permute-start | bytes 98312 | tf_op jit(solution)/shard_map/ppermute | solution.py:40
  187.4 2.3 %collective-permute-start.40 = (f32[16,512]{1,0:T(8,128)S(1)}, f32[16,512]{1,0:T(8,128)S(1)}, u32[]{:S(2)}, u32[]{:S(2)}) collective-permute-start(f32[16,512]{1,0:T(8,128)S(1)} %get-tuple-element.136), channel_id=1, source_target_pairs={{0,24},{1,25},{2,26},{3,27},{4,28},{5,29},{6,30},{7,31},{8,16},{9,... | collective-permute-start | bytes 98312 | tf_op jit(solution)/shard_map/ppermute | solution.py:40
  189.8 2.4 %collective-permute-done.39.refs_2_ = f32[16,512]{1,0:T(8,128)S(1)} collective-permute-done((f32[16,512]{1,0:T(8,128)S(1)}, f32[16,512]{1,0:T(8,128)S(1)}, u32[]{:S(2)}, u32[]{:S(2)}) %collective-permute-start.39) | collective-permute-done | bytes 32800 | tf_op jit(solution)/shard_map/ppermute | solution.py:40
  193.8 1.5 finish.3
  195.3 2.3 %collective-permute-start.41 = (bf16[16,512]{1,0:T(8,128)(2,1)}, bf16[16,512]{1,0:T(8,128)(2,1)S(1)}, u32[]{:S(2)}, u32[]{:S(2)}) collective-permute-start(bf16[16,512]{1,0:T(8,128)(2,1)} %finish.3), channel_id=1, source_target_pairs={{0,24},{1,25},{2,26},{3,27},{4,28},{5,29},{6,30},{7,31},{8,16},{9,... | collective-permute-start | bytes 49160 | tf_op jit(solution)/shard_map/ppermute | solution.py:40
  197.7 2.0 collective-permute-start.43
  199.7 1.4 collective-permute-done.41
  201.1 1.5 collective-permute-done.42
  203.2 1.7 collective-permute-start.44
  204.9 1.5 collective-permute-start.45
  207.8 1.7 collective-permute-start.51
  210.5 1.8 collective-permute-start.53
  212.5 1.4 collective-permute-done.51
  214.0 1.4 collective-permute-done.52
  215.6 1.7 gradient.2
  217.3 2.4 %collective-permute-start.48 = (bf16[128,256]{1,0:T(8,128)(2,1)S(1)}, bf16[128,256]{1,0:T(8,128)(2,1)S(1)}, u32[]{:S(2)}, u32[]{:S(2)}) collective-permute-start(bf16[128,256]{1,0:T(8,128)(2,1)S(1)} %get-tuple-element.90), channel_id=1, source_target_pairs={{0,24},{1,25},{2,26},{3,27},{4,28},{5,29},{6,30},{7,31},{8,16},{9,... | collective-permute-start | bytes 196616 | tf_op jit(solution)/shard_map/ppermute | solution.py:40
  219.9 1.8 collective-permute-start.50
  223.4 1.8 collective-permute-done.49
  (121 shorter events, 28.4 us)
Async XLA Ops:
  1.8 6.9 %collective-permute-start = (bf16[64,1024]{1,0:T(8,128)(2,1)S(1)}, bf16[64,1024]{1,0:T(8,128)(2,1)S(1)}, u32[]{:S(2)}, u32[]{:S(2)}) collective-permute-start(bf16[64,1024]{1,0:T(8,128)(2,1)S(1)} %get-tuple-element.119), channel_id=1, source_target_pairs={{0,2},{1,3},{2,0},{3,1},{4,6},{5,7},{6,4},{7,5},{8,10},{9,11},{10,... | collective-permute-start | bytes 393224 | tf_op jit(solution)/shard_map/ppermute | solution.py:40
  4.8 7.8 %collective-permute-start.1 = (bf16[64,1024]{1,0:T(8,128)(2,1)S(1)}, bf16[64,1024]{1,0:T(8,128)(2,1)S(1)}, u32[]{:S(2)}, u32[]{:S(2)}) collective-permute-start(bf16[64,1024]{1,0:T(8,128)(2,1)S(1)} %get-tuple-element.121), channel_id=1, source_target_pairs={{0,4},{1,5},{2,6},{3,7},{4,0},{5,1},{6,2},{7,3},{8,12},{9,13},{10,... | collective-permute-start | bytes 393224 | tf_op jit(solution)/shard_map/ppermute | solution.py:40
  6.4 6.3 %collective-permute-start.2 = (bf16[64,1024]{1,0:T(8,128)(2,1)S(1)}, bf16[64,1024]{1,0:T(8,128)(2,1)S(1)}, u32[]{:S(2)}, u32[]{:S(2)}) collective-permute-start(bf16[64,1024]{1,0:T(8,128)(2,1)S(1)} %get-tuple-element.120), channel_id=1, source_target_pairs={{0,6},{1,7},{2,4},{3,5},{4,2},{5,3},{6,0},{7,1},{8,14},{9,15},{10,... | collective-permute-start | bytes 393224 | tf_op jit(solution)/shard_map/ppermute | solution.py:40
  12.7 8.0 %collective-permute-start.3 = (bf16[64,1024]{1,0:T(8,128)(2,1)S(1)}, bf16[64,1024]{1,0:T(8,128)(2,1)S(1)}, u32[]{:S(2)}, u32[]{:S(2)}) collective-permute-start(bf16[64,1024]{1,0:T(8,128)(2,1)S(1)} %get-tuple-element.105), channel_id=1, source_target_pairs={{0,24},{1,25},{2,26},{3,27},{4,28},{5,29},{6,30},{7,31},{8,16},{9,... | collective-permute-start | bytes 393224 | tf_op jit(solution)/shard_map/ppermute | solution.py:40
  16.3 9.8 %collective-permute-start.4 = (bf16[64,1024]{1,0:T(8,128)(2,1)S(1)}, bf16[64,1024]{1,0:T(8,128)(2,1)S(1)}, u32[]{:S(2)}, u32[]{:S(2)}) collective-permute-start(bf16[64,1024]{1,0:T(8,128)(2,1)S(1)} %get-tuple-element.104), channel_id=1, source_target_pairs={{0,16},{1,17},{2,18},{3,19},{4,20},{5,21},{6,22},{7,23},{8,24},{9,... | collective-permute-start | bytes 393224 | tf_op jit(solution)/shard_map/ppermute | solution.py:40
  16.3 9.8 %collective-permute-start.5 = (bf16[64,1024]{1,0:T(8,128)(2,1)S(1)}, bf16[64,1024]{1,0:T(8,128)(2,1)S(1)}, u32[]{:S(2)}, u32[]{:S(2)}) collective-permute-start(bf16[64,1024]{1,0:T(8,128)(2,1)S(1)} %get-tuple-element.103), channel_id=1, source_target_pairs={{0,8},{1,9},{2,10},{3,11},{4,12},{5,13},{6,14},{7,15},{8,0},{9,1},... | collective-permute-start | bytes 393224 | tf_op jit(solution)/shard_map/ppermute | solution.py:40
  28.8 9.3 %collective-permute-start.6 = (bf16[128,1024]{1,0:T(8,128)(2,1)S(1)}, bf16[128,1024]{1,0:T(8,128)(2,1)S(1)}, u32[]{:S(2)}, u32[]{:S(2)}) collective-permute-start(bf16[128,1024]{1,0:T(8,128)(2,1)S(1)} %pad_maximum_fusion.3.refs_0_), channel_id=1, source_target_pairs={{0,2},{1,3},{2,0},{3,1},{4,6},{5,7},{6,4},{7,5},{8,10},{9,11},{10,... | collective-permute-start | bytes 786440 | tf_op jit(solution)/shard_map/ppermute | solution.py:40
  30.5 14.9 %collective-permute-start.7 = (bf16[128,1024]{1,0:T(8,128)(2,1)S(1)}, bf16[128,1024]{1,0:T(8,128)(2,1)S(1)}, u32[]{:S(2)}, u32[]{:S(2)}) collective-permute-start(bf16[128,1024]{1,0:T(8,128)(2,1)S(1)} %pad_maximum_fusion.3.refs_0_), channel_id=1, source_target_pairs={{0,4},{1,5},{2,6},{3,7},{4,0},{5,1},{6,2},{7,3},{8,12},{9,13},{10,... | collective-permute-start | bytes 786440 | tf_op jit(solution)/shard_map/ppermute | solution.py:40
  31.0 15.1 %collective-permute-start.8 = (bf16[128,1024]{1,0:T(8,128)(2,1)S(1)}, bf16[128,1024]{1,0:T(8,128)(2,1)S(1)}, u32[]{:S(2)}, u32[]{:S(2)}) collective-permute-start(bf16[128,1024]{1,0:T(8,128)(2,1)S(1)} %pad_maximum_fusion.3.refs_0_), channel_id=1, source_target_pairs={{0,6},{1,7},{2,4},{3,5},{4,2},{5,3},{6,0},{7,1},{8,14},{9,15},{10,... | collective-permute-start | bytes 786440 | tf_op jit(solution)/shard_map/ppermute | solution.py:40
  32.4 17.0 %collective-permute-start.13 = (bf16[128,1024]{1,0:T(8,128)(2,1)S(1)}, bf16[128,1024]{1,0:T(8,128)(2,1)S(1)}, u32[]{:S(2)}, u32[]{:S(2)}) collective-permute-start(bf16[128,1024]{1,0:T(8,128)(2,1)S(1)} %pad_maximum_fusion.4.refs_0_), channel_id=1, source_target_pairs={{0,2},{1,3},{2,0},{3,1},{4,6},{5,7},{6,4},{7,5},{8,10},{9,11},{10,... | collective-permute-start | bytes 786440 | tf_op jit(solution)/shard_map/ppermute | solution.py:40
  34.1 20.3 %collective-permute-start.14 = (bf16[128,1024]{1,0:T(8,128)(2,1)S(1)}, bf16[128,1024]{1,0:T(8,128)(2,1)S(1)}, u32[]{:S(2)}, u32[]{:S(2)}) collective-permute-start(bf16[128,1024]{1,0:T(8,128)(2,1)S(1)} %pad_maximum_fusion.4.refs_0_), channel_id=1, source_target_pairs={{0,4},{1,5},{2,6},{3,7},{4,0},{5,1},{6,2},{7,3},{8,12},{9,13},{10,... | collective-permute-start | bytes 786440 | tf_op jit(solution)/shard_map/ppermute | solution.py:40
  38.1 16.3 %collective-permute-start.15 = (bf16[128,1024]{1,0:T(8,128)(2,1)S(1)}, bf16[128,1024]{1,0:T(8,128)(2,1)S(1)}, u32[]{:S(2)}, u32[]{:S(2)}) collective-permute-start(bf16[128,1024]{1,0:T(8,128)(2,1)S(1)} %pad_maximum_fusion.4.refs_0_), channel_id=1, source_target_pairs={{0,6},{1,7},{2,4},{3,5},{4,2},{5,3},{6,0},{7,1},{8,14},{9,15},{10,... | collective-permute-start | bytes 786440 | tf_op jit(solution)/shard_map/ppermute | solution.py:40
  46.8 7.8 %collective-permute-start.9 = (bf16[512,1024]{1,0:T(8,128)(2,1)}, bf16[512,1024]{1,0:T(8,128)(2,1)}, u32[]{:S(2)}, u32[]{:S(2)}) collective-permute-start(bf16[512,1024]{1,0:T(8,128)(2,1)} %constant_dynamic-update-slice_fusion), channel_id=1, source_target_pairs={{0,1},{1,0},{2,3},{3,2},{4,5},{5,4},{6,7},{7,6},{8,9},{9,8},{10,11... | collective-permute-start | bytes 3145736 | tf_op jit(solution)/shard_map/ppermute | solution.py:40
  54.4 11.4 %collective-permute-start.16 = (bf16[512,1024]{1,0:T(8,128)(2,1)S(1)}, bf16[512,1024]{1,0:T(8,128)(2,1)}, u32[]{:S(2)}, u32[]{:S(2)}) collective-permute-start(bf16[512,1024]{1,0:T(8,128)(2,1)S(1)} %constant_dynamic-update-slice_fusion.7), channel_id=1, source_target_pairs={{0,1},{1,0},{2,3},{3,2},{4,5},{5,4},{6,7},{7,6},{8,9},{9,8},{10,11... | collective-permute-start | bytes 3145736 | tf_op jit(solution)/shard_map/ppermute | solution.py:40
  54.6 32.5 %copy-start = (s32[3]{0:T(128)}, s32[3]{0:T(128)S(1)}, u32[]{:S(2)}) copy-start(s32[3]{0:T(128)S(1)} %pad_add_fusion.place_ref) | copy-start | bytes 40
  54.6 2.2 copy-start.3
  56.8 9.1 %copy-start.4 = (bf16[2048,1024]{1,0:T(8,128)(2,1)S(1)}, bf16[2048,1024]{1,0:T(8,128)(2,1)}, u32[]{:S(2)}) copy-start(bf16[2048,1024]{1,0:T(8,128)(2,1)} %refs_5_.3) | copy-start | bytes 12582916
  61.4 15.7 %collective-permute-start.10 = (bf16[640,256]{1,0:T(8,128)(2,1)S(1)}, bf16[640,256]{1,0:T(8,128)(2,1)S(1)}, u32[]{:S(2)}, u32[]{:S(2)}) collective-permute-start(bf16[640,256]{1,0:T(8,128)(2,1)S(1)} %get-tuple-element.53), channel_id=1, source_target_pairs={{0,8},{1,9},{2,10},{3,11},{4,12},{5,13},{6,14},{7,15},{8,0},{9,1},... | collective-permute-start | bytes 983048 | tf_op jit(solution)/shard_map/ppermute | solution.py:40
  61.5 25.6 %collective-permute-start.11 = (bf16[640,256]{1,0:T(8,128)(2,1)S(1)}, bf16[640,256]{1,0:T(8,128)(2,1)S(1)}, u32[]{:S(2)}, u32[]{:S(2)}) collective-permute-start(bf16[640,256]{1,0:T(8,128)(2,1)S(1)} %get-tuple-element.54), channel_id=1, source_target_pairs={{0,16},{1,17},{2,18},{3,19},{4,20},{5,21},{6,22},{7,23},{8,24},{9,... | collective-permute-start | bytes 983048 | tf_op jit(solution)/shard_map/ppermute | solution.py:40
  63.2 23.9 %collective-permute-start.12 = (bf16[640,256]{1,0:T(8,128)(2,1)S(1)}, bf16[640,256]{1,0:T(8,128)(2,1)S(1)}, u32[]{:S(2)}, u32[]{:S(2)}) collective-permute-start(bf16[640,256]{1,0:T(8,128)(2,1)S(1)} %get-tuple-element.55), channel_id=1, source_target_pairs={{0,24},{1,25},{2,26},{3,27},{4,28},{5,29},{6,30},{7,31},{8,16},{9,... | collective-permute-start | bytes 983048 | tf_op jit(solution)/shard_map/ppermute | solution.py:40
  70.3 21.1 %copy-start.5 = (bf16[640,256]{1,0:T(8,128)(2,1)}, bf16[640,256]{1,0:T(8,128)(2,1)S(1)}, u32[]{:S(2)}) copy-start(bf16[640,256]{1,0:T(8,128)(2,1)S(1)} %get-tuple-element.61) | copy-start | bytes 983044
  89.4 77.2 %copy-start.1 = (s32[3]{0:T(128)S(1)}, s32[3]{0:T(128)}, u32[]{:S(2)}) copy-start(s32[3]{0:T(128)} %copy-done) | copy-start | bytes 40
  89.4 2.0 collective-permute-start.20
  91.5 5.6 %collective-permute-start.21 = (f32[64,512]{1,0:T(8,128)S(1)}, f32[64,512]{1,0:T(8,128)S(1)}, u32[]{:S(2)}, u32[]{:S(2)}) collective-permute-start(f32[64,512]{1,0:T(8,128)S(1)} %get-tuple-element.115), channel_id=1, source_target_pairs={{0,2},{1,3},{2,0},{3,1},{4,6},{5,7},{6,4},{7,5},{8,10},{9,11},{10,... | collective-permute-start | bytes 393224 | tf_op jit(solution)/shard_map/ppermute | solution.py:40
  92.0 6.3 %collective-permute-start.22 = (f32[64,512]{1,0:T(8,128)S(1)}, f32[64,512]{1,0:T(8,128)S(1)}, u32[]{:S(2)}, u32[]{:S(2)}) collective-permute-start(f32[64,512]{1,0:T(8,128)S(1)} %get-tuple-element.113), channel_id=1, source_target_pairs={{0,4},{1,5},{2,6},{3,7},{4,0},{5,1},{6,2},{7,3},{8,12},{9,13},{10,... | collective-permute-start | bytes 393224 | tf_op jit(solution)/shard_map/ppermute | solution.py:40
  97.1 5.9 %collective-permute-start.23 = (f32[64,512]{1,0:T(8,128)S(1)}, f32[64,512]{1,0:T(8,128)S(1)}, u32[]{:S(2)}, u32[]{:S(2)}) collective-permute-start(f32[64,512]{1,0:T(8,128)S(1)} %get-tuple-element.71), channel_id=1, source_target_pairs={{0,6},{1,7},{2,4},{3,5},{4,2},{5,3},{6,0},{7,1},{8,14},{9,15},{10,... | collective-permute-start | bytes 393224 | tf_op jit(solution)/shard_map/ppermute | solution.py:40
  103.7 9.3 %collective-permute-start.24 = (f32[16,512]{1,0:T(8,128)S(1)}, f32[16,512]{1,0:T(8,128)S(1)}, u32[]{:S(2)}, u32[]{:S(2)}) collective-permute-start(f32[16,512]{1,0:T(8,128)S(1)} %get-tuple-element.142), channel_id=1, source_target_pairs={{0,8},{1,9},{2,10},{3,11},{4,12},{5,13},{6,14},{7,15},{8,0},{9,1},... | collective-permute-start | bytes 98312 | tf_op jit(solution)/shard_map/ppermute | solution.py:40
  110.8 4.8 %collective-permute-start.25 = (f32[16,512]{1,0:T(8,128)S(1)}, f32[16,512]{1,0:T(8,128)S(1)}, u32[]{:S(2)}, u32[]{:S(2)}) collective-permute-start(f32[16,512]{1,0:T(8,128)S(1)} %get-tuple-element.140), channel_id=1, source_target_pairs={{0,16},{1,17},{2,18},{3,19},{4,20},{5,21},{6,22},{7,23},{8,24},{9,... | collective-permute-start | bytes 98312 | tf_op jit(solution)/shard_map/ppermute | solution.py:40
  113.0 5.7 %copy-start.6 = (f32[16,512]{1,0:T(8,128)}, f32[16,512]{1,0:T(8,128)S(1)}, u32[]{:S(2)}) copy-start(f32[16,512]{1,0:T(8,128)S(1)} %collective-permute-done.24.refs_1_) | copy-start | bytes 98308
  113.0 5.7 %collective-permute-start.26 = (f32[16,512]{1,0:T(8,128)S(1)}, f32[16,512]{1,0:T(8,128)S(1)}, u32[]{:S(2)}, u32[]{:S(2)}) collective-permute-start(f32[16,512]{1,0:T(8,128)S(1)} %get-tuple-element.73), channel_id=1, source_target_pairs={{0,24},{1,25},{2,26},{3,27},{4,28},{5,29},{6,30},{7,31},{8,16},{9,... | collective-permute-start | bytes 98312 | tf_op jit(solution)/shard_map/ppermute | solution.py:40
  115.7 3.1 %copy-start.8 = (f32[16,512]{1,0:T(8,128)}, f32[16,512]{1,0:T(8,128)S(1)}, u32[]{:S(2)}) copy-start(f32[16,512]{1,0:T(8,128)S(1)} %collective-permute-done.25.refs_2_) | copy-start | bytes 98308
  120.7 3.9 %collective-permute-start.27 = (bf16[16,512]{1,0:T(8,128)(2,1)}, bf16[16,512]{1,0:T(8,128)(2,1)S(1)}, u32[]{:S(2)}, u32[]{:S(2)}) collective-permute-start(bf16[16,512]{1,0:T(8,128)(2,1)} %finish.2), channel_id=1, source_target_pairs={{0,8},{1,9},{2,10},{3,11},{4,12},{5,13},{6,14},{7,15},{8,0},{9,1},... | collective-permute-start | bytes 49160 | tf_op jit(solution)/shard_map/ppermute | solution.py:40
  120.7 5.3 %collective-permute-start.29 = (bf16[16,512]{1,0:T(8,128)(2,1)}, bf16[16,512]{1,0:T(8,128)(2,1)S(1)}, u32[]{:S(2)}, u32[]{:S(2)}) collective-permute-start(bf16[16,512]{1,0:T(8,128)(2,1)} %finish.2), channel_id=1, source_target_pairs={{0,16},{1,17},{2,18},{3,19},{4,20},{5,21},{6,22},{7,23},{8,24},{9,... | collective-permute-start | bytes 49160 | tf_op jit(solution)/shard_map/ppermute | solution.py:40
  124.7 5.7 %collective-permute-start.28 = (bf16[16,512]{1,0:T(8,128)(2,1)}, bf16[16,512]{1,0:T(8,128)(2,1)S(1)}, u32[]{:S(2)}, u32[]{:S(2)}) collective-permute-start(bf16[16,512]{1,0:T(8,128)(2,1)} %finish.2), channel_id=1, source_target_pairs={{0,24},{1,25},{2,26},{3,27},{4,28},{5,29},{6,30},{7,31},{8,16},{9,... | collective-permute-start | bytes 49160 | tf_op jit(solution)/shard_map/ppermute | solution.py:40
  131.2 4.3 %collective-permute-start.30 = (bf16[64,512]{1,0:T(8,128)(2,1)S(1)}, bf16[64,512]{1,0:T(8,128)(2,1)S(1)}, u32[]{:S(2)}, u32[]{:S(2)}) collective-permute-start(bf16[64,512]{1,0:T(8,128)(2,1)S(1)} %pad_maximum_fusion.9), channel_id=1, source_target_pairs={{0,2},{1,3},{2,0},{3,1},{4,6},{5,7},{6,4},{7,5},{8,10},{9,11},{10,... | collective-permute-start | bytes 196616 | tf_op jit(solution)/shard_map/ppermute | solution.py:40
  131.6 5.1 %collective-permute-start.32 = (bf16[64,512]{1,0:T(8,128)(2,1)S(1)}, bf16[64,512]{1,0:T(8,128)(2,1)S(1)}, u32[]{:S(2)}, u32[]{:S(2)}) collective-permute-start(bf16[64,512]{1,0:T(8,128)(2,1)S(1)} %pad_maximum_fusion.9), channel_id=1, source_target_pairs={{0,4},{1,5},{2,6},{3,7},{4,0},{5,1},{6,2},{7,3},{8,12},{9,13},{10,... | collective-permute-start | bytes 196616 | tf_op jit(solution)/shard_map/ppermute | solution.py:40
  135.5 5.2 %collective-permute-start.31 = (bf16[64,512]{1,0:T(8,128)(2,1)S(1)}, bf16[64,512]{1,0:T(8,128)(2,1)S(1)}, u32[]{:S(2)}, u32[]{:S(2)}) collective-permute-start(bf16[64,512]{1,0:T(8,128)(2,1)S(1)} %pad_maximum_fusion.9), channel_id=1, source_target_pairs={{0,6},{1,7},{2,4},{3,5},{4,2},{5,3},{6,0},{7,1},{8,14},{9,15},{10,... | collective-permute-start | bytes 196616 | tf_op jit(solution)/shard_map/ppermute | solution.py:40
  140.8 66.0 %copy-start.2 = (s32[3]{0:T(128)S(1)}, s32[3]{0:T(128)}, u32[]{:S(2)}) copy-start(s32[3]{0:T(128)} %copy-done) | copy-start | bytes 40
  140.8 4.5 %collective-permute-start.33 = (bf16[256,512]{1,0:T(8,128)(2,1)S(1)}, bf16[256,512]{1,0:T(8,128)(2,1)S(1)}, u32[]{:S(2)}, u32[]{:S(2)}) collective-permute-start(bf16[256,512]{1,0:T(8,128)(2,1)S(1)} %pad_maximum_fusion.5), channel_id=1, source_target_pairs={{0,1},{1,0},{2,3},{3,2},{4,5},{5,4},{6,7},{7,6},{8,9},{9,8},{10,11... | collective-permute-start | bytes 786440 | tf_op jit(solution)/shard_map/ppermute | solution.py:40
  140.9 16.3 %collective-permute-start.17 = (bf16[640,256]{1,0:T(8,128)(2,1)}, bf16[640,256]{1,0:T(8,128)(2,1)S(1)}, u32[]{:S(2)}, u32[]{:S(2)}) collective-permute-start(bf16[640,256]{1,0:T(8,128)(2,1)} %copy-done.5), channel_id=1, source_target_pairs={{0,8},{1,9},{2,10},{3,11},{4,12},{5,13},{6,14},{7,15},{8,0},{9,1},... | collective-permute-start | bytes 983048 | tf_op jit(solution)/shard_map/ppermute | solution.py:40
  141.0 25.6 %collective-permute-start.18 = (bf16[640,256]{1,0:T(8,128)(2,1)S(1)}, bf16[640,256]{1,0:T(8,128)(2,1)S(1)}, u32[]{:S(2)}, u32[]{:S(2)}) collective-permute-start(bf16[640,256]{1,0:T(8,128)(2,1)S(1)} %get-tuple-element.62), channel_id=1, source_target_pairs={{0,16},{1,17},{2,18},{3,19},{4,20},{5,21},{6,22},{7,23},{8,24},{9,... | collective-permute-start | bytes 983048 | tf_op jit(solution)/shard_map/ppermute | solution.py:40
  142.8 23.7 %collective-permute-start.19 = (bf16[640,256]{1,0:T(8,128)(2,1)S(1)}, bf16[640,256]{1,0:T(8,128)(2,1)S(1)}, u32[]{:S(2)}, u32[]{:S(2)}) collective-permute-start(bf16[640,256]{1,0:T(8,128)(2,1)S(1)} %get-tuple-element.63), channel_id=1, source_target_pairs={{0,24},{1,25},{2,26},{3,27},{4,28},{5,29},{6,30},{7,31},{8,16},{9,... | collective-permute-start | bytes 983048 | tf_op jit(solution)/shard_map/ppermute | solution.py:40
  169.1 2.0 collective-permute-start.34
  171.2 6.4 %collective-permute-start.35 = (f32[64,512]{1,0:T(8,128)S(1)}, f32[64,512]{1,0:T(8,128)S(1)}, u32[]{:S(2)}, u32[]{:S(2)}) collective-permute-start(f32[64,512]{1,0:T(8,128)S(1)} %get-tuple-element.110), channel_id=1, source_target_pairs={{0,2},{1,3},{2,0},{3,1},{4,6},{5,7},{6,4},{7,5},{8,10},{9,11},{10,... | collective-permute-start | bytes 393224 | tf_op jit(solution)/shard_map/ppermute | solution.py:40
  171.6 8.1 %collective-permute-start.36 = (f32[64,512]{1,0:T(8,128)S(1)}, f32[64,512]{1,0:T(8,128)S(1)}, u32[]{:S(2)}, u32[]{:S(2)}) collective-permute-start(f32[64,512]{1,0:T(8,128)S(1)} %get-tuple-element.109), channel_id=1, source_target_pairs={{0,4},{1,5},{2,6},{3,7},{4,0},{5,1},{6,2},{7,3},{8,12},{9,13},{10,... | collective-permute-start | bytes 393224 | tf_op jit(solution)/shard_map/ppermute | solution.py:40
  173.0 6.7 %collective-permute-start.37 = (f32[64,512]{1,0:T(8,128)S(1)}, f32[64,512]{1,0:T(8,128)S(1)}, u32[]{:S(2)}, u32[]{:S(2)}) collective-permute-start(f32[64,512]{1,0:T(8,128)S(1)} %get-tuple-element.108), channel_id=1, source_target_pairs={{0,6},{1,7},{2,4},{3,5},{4,2},{5,3},{6,0},{7,1},{8,14},{9,15},{10,... | collective-permute-start | bytes 393224 | tf_op jit(solution)/shard_map/ppermute | solution.py:40
  180.4 9.4 %collective-permute-start.38 = (f32[16,512]{1,0:T(8,128)S(1)}, f32[16,512]{1,0:T(8,128)S(1)}, u32[]{:S(2)}, u32[]{:S(2)}) collective-permute-start(f32[16,512]{1,0:T(8,128)S(1)} %get-tuple-element.138), channel_id=1, source_target_pairs={{0,8},{1,9},{2,10},{3,11},{4,12},{5,13},{6,14},{7,15},{8,0},{9,1},... | collective-permute-start | bytes 98312 | tf_op jit(solution)/shard_map/ppermute | solution.py:40
  187.4 4.8 %collective-permute-start.39 = (f32[16,512]{1,0:T(8,128)S(1)}, f32[16,512]{1,0:T(8,128)S(1)}, u32[]{:S(2)}, u32[]{:S(2)}) collective-permute-start(f32[16,512]{1,0:T(8,128)S(1)} %get-tuple-element.137), channel_id=1, source_target_pairs={{0,16},{1,17},{2,18},{3,19},{4,20},{5,21},{6,22},{7,23},{8,24},{9,... | collective-permute-start | bytes 98312 | tf_op jit(solution)/shard_map/ppermute | solution.py:40
  187.4 5.7 %collective-permute-start.40 = (f32[16,512]{1,0:T(8,128)S(1)}, f32[16,512]{1,0:T(8,128)S(1)}, u32[]{:S(2)}, u32[]{:S(2)}) collective-permute-start(f32[16,512]{1,0:T(8,128)S(1)} %get-tuple-element.136), channel_id=1, source_target_pairs={{0,24},{1,25},{2,26},{3,27},{4,28},{5,29},{6,30},{7,31},{8,16},{9,... | collective-permute-start | bytes 98312 | tf_op jit(solution)/shard_map/ppermute | solution.py:40
  189.8 3.4 %copy-start.7 = (f32[16,512]{1,0:T(8,128)}, f32[16,512]{1,0:T(8,128)S(1)}, u32[]{:S(2)}) copy-start(f32[16,512]{1,0:T(8,128)S(1)} %collective-permute-done.38.refs_1_) | copy-start | bytes 98308
  192.2 0.9 copy-start.9
  195.3 5.7 %collective-permute-start.41 = (bf16[16,512]{1,0:T(8,128)(2,1)}, bf16[16,512]{1,0:T(8,128)(2,1)S(1)}, u32[]{:S(2)}, u32[]{:S(2)}) collective-permute-start(bf16[16,512]{1,0:T(8,128)(2,1)} %finish.3), channel_id=1, source_target_pairs={{0,24},{1,25},{2,26},{3,27},{4,28},{5,29},{6,30},{7,31},{8,16},{9,... | collective-permute-start | bytes 49160 | tf_op jit(solution)/shard_map/ppermute | solution.py:40
  197.7 4.8 %collective-permute-start.42 = (bf16[16,512]{1,0:T(8,128)(2,1)}, bf16[16,512]{1,0:T(8,128)(2,1)S(1)}, u32[]{:S(2)}, u32[]{:S(2)}) collective-permute-start(bf16[16,512]{1,0:T(8,128)(2,1)} %finish.3), channel_id=1, source_target_pairs={{0,16},{1,17},{2,18},{3,19},{4,20},{5,21},{6,22},{7,23},{8,24},{9,... | collective-permute-start | bytes 49160 | tf_op jit(solution)/shard_map/ppermute | solution.py:40
  197.7 4.8 %collective-permute-start.43 = (bf16[16,512]{1,0:T(8,128)(2,1)}, bf16[16,512]{1,0:T(8,128)(2,1)S(1)}, u32[]{:S(2)}, u32[]{:S(2)}) collective-permute-start(bf16[16,512]{1,0:T(8,128)(2,1)} %finish.3), channel_id=1, source_target_pairs={{0,8},{1,9},{2,10},{3,11},{4,12},{5,13},{6,14},{7,15},{8,0},{9,1},... | collective-permute-start | bytes 49160 | tf_op jit(solution)/shard_map/ppermute | solution.py:40
  203.2 7.2 %collective-permute-start.44 = (bf16[64,512]{1,0:T(8,128)(2,1)S(1)}, bf16[64,512]{1,0:T(8,128)(2,1)S(1)}, u32[]{:S(2)}, u32[]{:S(2)}) collective-permute-start(bf16[64,512]{1,0:T(8,128)(2,1)S(1)} %pad_maximum_fusion.10), channel_id=1, source_target_pairs={{0,6},{1,7},{2,4},{3,5},{4,2},{5,3},{6,0},{7,1},{8,14},{9,15},{10,... | collective-permute-start | bytes 196616 | tf_op jit(solution)/shard_map/ppermute | solution.py:40
  204.9 7.4 %collective-permute-start.45 = (bf16[64,512]{1,0:T(8,128)(2,1)S(1)}, bf16[64,512]{1,0:T(8,128)(2,1)S(1)}, u32[]{:S(2)}, u32[]{:S(2)}) collective-permute-start(bf16[64,512]{1,0:T(8,128)(2,1)S(1)} %pad_maximum_fusion.10), channel_id=1, source_target_pairs={{0,4},{1,5},{2,6},{3,7},{4,0},{5,1},{6,2},{7,3},{8,12},{9,13},{10,... | collective-permute-start | bytes 196616 | tf_op jit(solution)/shard_map/ppermute | solution.py:40
  206.4 5.9 %collective-permute-start.46 = (bf16[64,512]{1,0:T(8,128)(2,1)S(1)}, bf16[64,512]{1,0:T(8,128)(2,1)S(1)}, u32[]{:S(2)}, u32[]{:S(2)}) collective-permute-start(bf16[64,512]{1,0:T(8,128)(2,1)S(1)} %pad_maximum_fusion.10), channel_id=1, source_target_pairs={{0,2},{1,3},{2,0},{3,1},{4,6},{5,7},{6,4},{7,5},{8,10},{9,11},{10,... | collective-permute-start | bytes 196616 | tf_op jit(solution)/shard_map/ppermute | solution.py:40
  207.8 6.1 %collective-permute-start.51 = (bf16[128,256]{1,0:T(8,128)(2,1)S(1)}, bf16[128,256]{1,0:T(8,128)(2,1)S(1)}, u32[]{:S(2)}, u32[]{:S(2)}) collective-permute-start(bf16[128,256]{1,0:T(8,128)(2,1)S(1)} %get-tuple-element.96), channel_id=1, source_target_pairs={{0,24},{1,25},{2,26},{3,27},{4,28},{5,29},{6,30},{7,31},{8,16},{9,... | collective-permute-start | bytes 196616 | tf_op jit(solution)/shard_map/ppermute | solution.py:40
  209.5 5.9 %collective-permute-start.52 = (bf16[128,256]{1,0:T(8,128)(2,1)S(1)}, bf16[128,256]{1,0:T(8,128)(2,1)S(1)}, u32[]{:S(2)}, u32[]{:S(2)}) collective-permute-start(bf16[128,256]{1,0:T(8,128)(2,1)S(1)} %get-tuple-element.97), channel_id=1, source_target_pairs={{0,16},{1,17},{2,18},{3,19},{4,20},{5,21},{6,22},{7,23},{8,24},{9,... | collective-permute-start | bytes 196616 | tf_op jit(solution)/shard_map/ppermute | solution.py:40
  210.5 4.9 %collective-permute-start.53 = (bf16[128,256]{1,0:T(8,128)(2,1)S(1)}, bf16[128,256]{1,0:T(8,128)(2,1)S(1)}, u32[]{:S(2)}, u32[]{:S(2)}) collective-permute-start(bf16[128,256]{1,0:T(8,128)(2,1)S(1)} %get-tuple-element.98), channel_id=1, source_target_pairs={{0,8},{1,9},{2,10},{3,11},{4,12},{5,13},{6,14},{7,15},{8,0},{9,1},... | collective-permute-start | bytes 196616 | tf_op jit(solution)/shard_map/ppermute | solution.py:40
  212.4 3.0 %collective-permute-start.47 = (bf16[256,512]{1,0:T(8,128)(2,1)S(1)}, bf16[256,512]{1,0:T(8,128)(2,1)S(1)}, u32[]{:S(2)}, u32[]{:S(2)}) collective-permute-start(bf16[256,512]{1,0:T(8,128)(2,1)S(1)} %pad_maximum_fusion.6), channel_id=1, source_target_pairs={{0,1},{1,0},{2,3},{3,2},{4,5},{5,4},{6,7},{7,6},{8,9},{9,8},{10,11... | collective-permute-start | bytes 786440 | tf_op jit(solution)/shard_map/ppermute | solution.py:40
  217.3 6.2 %collective-permute-start.48 = (bf16[128,256]{1,0:T(8,128)(2,1)S(1)}, bf16[128,256]{1,0:T(8,128)(2,1)S(1)}, u32[]{:S(2)}, u32[]{:S(2)}) collective-permute-start(bf16[128,256]{1,0:T(8,128)(2,1)S(1)} %get-tuple-element.90), channel_id=1, source_target_pairs={{0,24},{1,25},{2,26},{3,27},{4,28},{5,29},{6,30},{7,31},{8,16},{9,... | collective-permute-start | bytes 196616 | tf_op jit(solution)/shard_map/ppermute | solution.py:40
  219.7 5.6 %collective-permute-start.49 = (bf16[128,256]{1,0:T(8,128)(2,1)S(1)}, bf16[128,256]{1,0:T(8,128)(2,1)S(1)}, u32[]{:S(2)}, u32[]{:S(2)}) collective-permute-start(bf16[128,256]{1,0:T(8,128)(2,1)S(1)} %get-tuple-element.91), channel_id=1, source_target_pairs={{0,16},{1,17},{2,18},{3,19},{4,20},{5,21},{6,22},{7,23},{8,24},{9,... | collective-permute-start | bytes 196616 | tf_op jit(solution)/shard_map/ppermute | solution.py:40
  219.9 5.4 %collective-permute-start.50 = (bf16[128,256]{1,0:T(8,128)(2,1)S(1)}, bf16[128,256]{1,0:T(8,128)(2,1)S(1)}, u32[]{:S(2)}, u32[]{:S(2)}) collective-permute-start(bf16[128,256]{1,0:T(8,128)(2,1)S(1)} %get-tuple-element.92), channel_id=1, source_target_pairs={{0,8},{1,9},{2,10},{3,11},{4,12},{5,13},{6,14},{7,15},{8,0},{9,1},... | collective-permute-start | bytes 196616 | tf_op jit(solution)/shard_map/ppermute | solution.py:40
  (2 other events, 1.2 us)
where the time goes:
time: 227 us; the launch traced here: 226 us
  waiting for transfers between devices  118 us (52%)
  starting transfers between devices  73 us (32%)
  Pallas kernels  19.5 us (9%)
  local copies, waits for them, and re-layouts  9.58 us (4%)
  other arithmetic  5.04 us (2%)
    ppermute x54, waiting for transfers between devices, send(): return lax.ppermute(value, ('dp', 'mp'), pairs)  118 us
    ppermute x54, starting transfers between devices, send(): return lax.ppermute(value, ('dp', 'mp'), pairs)  73 us
    pallas_call x2, Pallas kernels, project(): pl.pallas_call(functools.partial(project_kernel, n=n, k=k), in_specs=[pl....  9.05 us
    unnamed x32, local copies, waits for them, and re-layouts  7.43 us
    pallas_call x2, Pallas kernels, normalize_parts(): pl.pallas_call(functools.partial(normalize_kernel, n=n, k=k, second=secon...  4.85 us
  transfers between devices with their start and end apart: 54, of which 33 were waited for; matrix products, arithmetic and copies ran while one was open for 1% of the time, Pallas kernels for 4%

commit v1 on v0

--- a/solution.py
+++ b/solution.py
@@ -15,7 +15,7 @@
 
 F32 = jnp.float32
 BF16 = jnp.bfloat16
-VMEM_BYTES = 24 * 1024 * 1024
+VMEM_BYTES = 16 * 1024 * 1024
 SHARED = 4
 BITS = 3
 LEVELS = 1 << BITS
@@ -120,19 +120,36 @@
         in_specs=[pl.BlockSpec(memory_space=pltpu.SMEM)] + [space] * place.n,
         out_specs=space,
         out_shape=jax.ShapeDtypeStruct(parts[0].shape, BF16),
+        compiler_params=pltpu.CompilerParams(vmem_limit_bytes=VMEM_BYTES // 4),
         name="finish",
     )(place_array, *parts)
 
 
-def rounded_gram(place, place_array, part, last):
+def gram_rows(place, place_array, grams, last):
     few = not last
+    part = grams[0]
+    for step in range(1, place.k):
+        part = part + place.send(grams[step], lambda z, a, b, s=step: (z, a, b ^ s))
     part = reduce_scatter(place, "a", part, few)
     height, width = part.shape
     part = part.reshape(place.n, height // place.n, width)
-    part = finish(place, place_array, exchange(place, "z", part, few), last)
+    return finish(place, place_array, exchange(place, "z", part, few), last)
+
+
+def whole_gram(place, part):
     for axis in ("z", "a", "b"):
-        part = gather(place, axis, part, few)
+        part = gather(place, axis, part)
     return part
+
+
+def in_one(place, run, args):
+    shapes = jax.eval_shape(run, *args)
+    return lax.cond(
+        place.z < place.n,
+        run,
+        lambda *args: jax.tree.map(lambda leaf: jnp.zeros(leaf.shape, leaf.dtype), shapes),
+        *args,
+    )
 
 
 def plain_gram(place, part):
@@ -158,24 +175,32 @@
     ]
 
 
-def met_rows(place, values):
-    return sends(place, "a", [values] * place.n)
+def met_rows(place, values, few=False):
+    return sends(place, "a", [values] * place.n, few)
 
 
 def project_kernel(place_ref, *refs, n, k):
     met, others = refs[:n], refs[n : n + k - 1]
     weight_ref = refs[n + k - 1]
-    own_ref, coded = refs[n + k], refs[n + k + 1 :]
+    own_ref, coded = refs[n + k], refs[n + k + 1 : 2 * n + k]
+    held_ref, arrived = refs[2 * n + k :]
     width = met[0].shape[1]
     columns = own_ref.shape[1]
+    copies = {}
+    for step in [*range(1, n), 0]:
+        at = pl.ds(pl.multiple_of((place_ref[0] ^ step) * columns, columns), columns)
+        copies[step] = pltpu.make_async_copy(
+            weight_ref.at[:, at], held_ref.at[step], arrived.at[step]
+        )
+        copies[step].start()
     own = jnp.concatenate([ref[...] for ref in met], 0)
     for step in [*range(1, n), 0]:
-        at = pl.ds(pl.multiple_of((place_ref[0] ^ step) * columns, columns), columns)
+        copies[step].wait()
         total = 0.0
         for i in range(k):
             rows = pl.ds(pl.multiple_of((place_ref[2] ^ i) * width, width), width)
             values = own if i == 0 else others[i - 1][...]
-            total += jnp.dot(values, weight_ref[rows, at], preferred_element_type=F32)
+            total += jnp.dot(values, held_ref[step, rows, :], preferred_element_type=F32)
         if step == 0:
             own_ref[...] = total
         else:
@@ -238,9 +263,15 @@
     space = pl.BlockSpec(memory_space=pltpu.VMEM)
     own, *parts = pl.pallas_call(
         functools.partial(project_kernel, n=n, k=k),
-        in_specs=[pl.BlockSpec(memory_space=pltpu.SMEM)] + [space] * len(args),
+        in_specs=[pl.BlockSpec(memory_space=pltpu.SMEM)]
+        + [space] * (len(args) - 1)
+        + [pl.BlockSpec(memory_space=pl.ANY)],
         out_specs=[space] * n,
         out_shape=out_shape,
+        scratch_shapes=[
+            pltpu.VMEM((n, k * width, columns), BF16),
+            pltpu.SemaphoreType.DMA((n,)),
+        ],
         compiler_params=pltpu.CompilerParams(vmem_limit_bytes=VMEM_BYTES),
         cost_estimate=pl.CostEstimate(
             flops=2 * batch * k * width * n * columns,
@@ -398,41 +429,42 @@
 def with_kernels(place, h_first, h_second, weight):
     n, k, z, a, b = place.n, place.k, place.z, place.a, place.b
     place_array = jnp.stack([z, a, b]).astype(jnp.int32)
-    both = spread(place, (h_first, h_second))
-
-    def projected(values):
-        met = met_rows(place, values)
+    first, second = spread(place, (h_first, h_second))
+
+    def projected(values, weight, few):
+        met = met_rows(place, values, few)
         own = jnp.concatenate(met, 0)
         others = [
             place.send(own, lambda z, a, b, s=step: (z, a, b ^ s)) for step in range(1, k)
         ]
         return project(place, place_array, met, others, weight)
 
-    def halves(grams):
-        part = grams[0]
-        for step in range(1, k):
-            part = part + place.send(grams[step], lambda z, a, b, s=step: (z, a, b ^ s))
-        return part
-
     def sent(parts):
         return sends(place, "z", [parts[0], *parts])[1:]
 
-    own_1, parts_1 = projected(both[0])
+    own_1, parts_1 = projected(first, weight, False)
+    second, own_1 = lax.optimization_barrier((second, own_1))
     parts_1 = sent(parts_1)
-    own_2, parts_2 = projected(both[1])
-    own_1, parts_1, own_2, parts_2 = lax.optimization_barrier((own_1, parts_1, own_2, parts_2))
+    own_2, parts_2 = in_one(
+        place, lambda values, weight: projected(values, weight, True), (second, weight)
+    )
+    own_1, own_2 = lax.optimization_barrier((own_1, own_2))
     parts_2 = sent(parts_2)
     norm_1, packed_1, scale_1, *grams = normalize_parts(place, place_array, own_1, parts_1)
-    gram_1 = rounded_gram(place, place_array, halves(grams), False)
-    own_2, parts_2, gram_1 = lax.optimization_barrier((own_2, parts_2, gram_1))
+    rows_1 = in_one(place, lambda *grams: gram_rows(place, place_array, grams, False), grams)
+    own_2, parts_2, rows_1 = lax.optimization_barrier((own_2, parts_2, rows_1))
     norm_2, packed_2, scale_2, *grams, coeff = normalize_parts(
         place, place_array, own_2, parts_2, norm_1
     )
+    gram_1 = whole_gram(place, rows_1)
     grads_2 = gradient(
         place, place_array, gram_1, packed_2, norm_2, norm_1, scale_2, coeff
     )
+    rows_2 = gram_rows(place, place_array, grams, True)
+    grads_2, rows_2 = lax.optimization_barrier((grads_2, rows_2))
     out_2 = joined(place, grads_2)
-    gram_2 = rounded_gram(place, place_array, halves(grams), True)
+    gram_2 = whole_gram(place, rows_2)
+    out_2, gram_2 = lax.optimization_barrier((out_2, gram_2))
     *grads_1, loss = gradient(
         place, place_array, gram_2, packed_1, norm_1, norm_2, scale_1, coeff, gram_1
     )

time: 227 us -> 184 us (0.81)
  waiting for transfers between devices: 118 us -> 84.2 us
  starting transfers between devices: 73 us -> 61 us
  Pallas kernels: 19.5 us -> 26.8 us
  local copies, waits for them, and re-layouts: 9.58 us -> 4.9 us
    ppermute x54, waiting for transfers between devices: 118 us -> 84.2 us  [send(): return lax.ppermute(value, ('dp', 'mp'), pairs)]
    ppermute x54, starting transfers between devices: 73 us -> 61 us  [send(): return lax.ppermute(value, ('dp', 'mp'), pairs)]
    pallas_call x2, Pallas kernels: 9.05 us -> 15.7 us  [project(): pl.pallas_call(functools.partial(project_kernel, n=n, k=k), in_specs=[pl....]
    unnamed x32 -> x6, local copies, waits for them, and re-layouts: 7.43 us -> 3.98 us
  transfers between devices with their start and end apart: 54 -> 54, of which waited for: 33 -> 30; matrix products, arithmetic and copies ran while one was open for 1% -> 3% of each run, Pallas kernels for 4% -> 9%
where the time goes in v1:
time: 184 us
  waiting for transfers between devices  84.2 us (46%)
  starting transfers between devices  61 us (33%)
  Pallas kernels  26.8 us (15%)
  other arithmetic  5.68 us (3%)
  local copies, waits for them, and re-layouts  4.9 us (3%)
    ppermute x54, waiting for transfers between devices, send(): return lax.ppermute(value, ('dp', 'mp'), pairs)  84.2 us
    ppermute x54, starting transfers between devices, send(): return lax.ppermute(value, ('dp', 'mp'), pairs)  61 us
    pallas_call x2, Pallas kernels, project(): pl.pallas_call(functools.partial(project_kernel, n=n, k=k), in_specs=[pl....  15.7 us
    pallas_call x2, Pallas kernels, normalize_parts(): pl.pallas_call(functools.partial(normalize_kernel, n=n, k=k, second=secon...  7.12 us
    unnamed x6, local copies, waits for them, and re-layouts  3.98 us
  transfers between devices with their start and end apart: 54, of which 30 were waited for; matrix products, arithmetic and copies ran while one was open for 3% of the time, Pallas kernels for 9%

profile of v1, /device:TPU:0, one launch (start us, length us, event | category | flops | bytes accessed | tf_op | source)
XLA Modules:
  0.0 183.6 jit_solution(11498588862761162147)
XLA Ops:
  0.7 1.1 pad_maximum_fusion.1
  1.8 3.0 %collective-permute-start.11 = (bf16[64,1024]{1,0:T(8,128)(2,1)S(1)}, bf16[64,1024]{1,0:T(8,128)(2,1)S(1)}, u32[]{:S(2)}, u32[]{:S(2)}) collective-permute-start(bf16[64,1024]{1,0:T(8,128)(2,1)S(1)} %get-tuple-element.146), channel_id=1, source_target_pairs={{0,2},{1,3},{2,0},{3,1},{4,6},{5,7},{6,4},{7,5},{8,10},{9,11},{10,... | collective-permute-start | bytes 393224 | tf_op jit(solution)/shard_map/ppermute | solution.py:40
  4.8 1.5 collective-permute-start.12
  6.4 2.4 %collective-permute-done.11 = bf16[64,1024]{1,0:T(8,128)(2,1)S(1)} collective-permute-done((bf16[64,1024]{1,0:T(8,128)(2,1)S(1)}, bf16[64,1024]{1,0:T(8,128)(2,1)S(1)}, u32[]{:S(2)}, u32[]{:S(2)}) %collective-permute-start.11) | collective-permute-done | bytes 131104 | tf_op jit(solution)/shard_map/ppermute | solution.py:40
  8.8 3.9 %collective-permute-done.12 = bf16[64,1024]{1,0:T(8,128)(2,1)S(1)} collective-permute-done((bf16[64,1024]{1,0:T(8,128)(2,1)S(1)}, bf16[64,1024]{1,0:T(8,128)(2,1)S(1)}, u32[]{:S(2)}, u32[]{:S(2)}) %collective-permute-start.12) | collective-permute-done | bytes 131104 | tf_op jit(solution)/shard_map/ppermute | solution.py:40
  12.7 3.7 %collective-permute-start.14 = (bf16[64,1024]{1,0:T(8,128)(2,1)S(1)}, bf16[64,1024]{1,0:T(8,128)(2,1)S(1)}, u32[]{:S(2)}, u32[]{:S(2)}) collective-permute-start(bf16[64,1024]{1,0:T(8,128)(2,1)S(1)} %get-tuple-element.135), channel_id=1, source_target_pairs={{0,24},{1,25},{2,26},{3,27},{4,28},{5,29},{6,30},{7,31},{8,16},{9,... | collective-permute-start | bytes 393224 | tf_op jit(solution)/shard_map/ppermute | solution.py:40
  17.1 3.6 %collective-permute-done.14 = bf16[64,1024]{1,0:T(8,128)(2,1)S(1)} collective-permute-done((bf16[64,1024]{1,0:T(8,128)(2,1)S(1)}, bf16[64,1024]{1,0:T(8,128)(2,1)S(1)}, u32[]{:S(2)}, u32[]{:S(2)}) %collective-permute-start.14) | collective-permute-done | bytes 131104 | tf_op jit(solution)/shard_map/ppermute | solution.py:40
  20.7 5.4 %collective-permute-done.15 = bf16[64,1024]{1,0:T(8,128)(2,1)S(1)} collective-permute-done((bf16[64,1024]{1,0:T(8,128)(2,1)S(1)}, bf16[64,1024]{1,0:T(8,128)(2,1)S(1)}, u32[]{:S(2)}, u32[]{:S(2)}) %collective-permute-start.15) | collective-permute-done | bytes 131104 | tf_op jit(solution)/shard_map/ppermute | solution.py:40
  28.8 1.7 collective-permute-start.17
  31.0 1.3 collective-permute-start.19
  32.3 5.8 %collective-permute-done.17.refs_1_ = bf16[128,1024]{1,0:T(8,128)(2,1)S(1)} collective-permute-done((bf16[128,1024]{1,0:T(8,128)(2,1)S(1)}, bf16[128,1024]{1,0:T(8,128)(2,1)S(1)}, u32[]{:S(2)}, u32[]{:S(2)}) %collective-permute-start.17) | collective-permute-done | bytes 262176 | tf_op jit(solution)/shard_map/ppermute | solution.py:40
  38.8 4.3 %collective-permute-done.18.refs_2_ = bf16[128,1024]{1,0:T(8,128)(2,1)S(1)} collective-permute-done((bf16[128,1024]{1,0:T(8,128)(2,1)S(1)}, bf16[128,1024]{1,0:T(8,128)(2,1)S(1)}, u32[]{:S(2)}, u32[]{:S(2)}) %collective-permute-start.18) | collective-permute-done | bytes 262176 | tf_op jit(solution)/shard_map/ppermute | solution.py:40
  44.7 2.8 %collective-permute-done.20.refs_4_ = bf16[512,1024]{1,0:T(8,128)(2,1)S(1)} collective-permute-done((bf16[512,1024]{1,0:T(8,128)(2,1)}, bf16[512,1024]{1,0:T(8,128)(2,1)S(1)}, u32[]{:S(2)}, u32[]{:S(2)}) %collective-permute-start.20) | collective-permute-done | bytes 1048608 | tf_op jit(solution)/shard_map/ppermute | solution.py:40
  47.5 7.5 %project.3 = (f32[512,256]{1,0:T(8,128)S(1)}, bf16[640,256]{1,0:T(8,128)(2,1)}, bf16[640,256]{1,0:T(8,128)(2,1)}, bf16[640,256]{1,0:T(8,128)(2,1)S(1)}) custom-call(s32[3]{0:T(128)S(1)} %pad_add_fusion.place_ref, bf16[128,1024]{1,0:T(8,128)(2,1)S(1)} %pad_maximum_fusion.5.refs_0_, bf16[128,1024]{1,0:T(8,128)(2,1)S(1)} %collective-permute-done.17.refs_1_, ...), custom_call_target="tpu_custom_call" | custom-call | flops 2147483648 | bytes 7864320 | tf_op jit(solution)/shard_map/project/pallas_call | solution.py:264
  55.0 1.7 collective-permute-start.25
  56.7 2.7 %collective-permute-start.26 = (bf16[640,256]{1,0:T(8,128)(2,1)S(1)}, bf16[640,256]{1,0:T(8,128)(2,1)S(1)}, u32[]{:S(2)}, u32[]{:S(2)}) collective-permute-start(bf16[640,256]{1,0:T(8,128)(2,1)S(1)} %get-tuple-element.91), channel_id=1, source_target_pairs={{0,24},{1,25},{2,26},{3,27},{4,28},{5,29},{6,30},{7,31},{8,16},{9,... | collective-permute-start | bytes 983048 | tf_op jit(solution)/shard_map/ppermute | solution.py:40
  59.4 26.1 %conditional.2 = ((f32[512,256]{1,0:T(8,128)}, bf16[640,256]{1,0:T(8,128)(2,1)}, bf16[640,256]{1,0:T(8,128)(2,1)}, bf16[640,256]{1,0:T(8,128)(2,1)})) conditional(s32[]{:T(128)} %convert_element_type.4, () %tuple.30, (bf16[128,1024]{1,0:T(8,128)(2,1)S(1)}, s32[3]{0:T(128)S(1)}, bf16[2048,1024]{1,0:T(8,128)(2,1)}) %tuple.31), branch_computations={%region_0.1_spmd, %region_1.2_spmd} | conditional | flops 2151677952 | bytes 17301672 | solution.py:147
  60.5 6.5 %collective-permute-done.refs_1_ = bf16[128,1024]{1,0:T(8,128)(2,1)S(1)} collective-permute-done((bf16[128,1024]{1,0:T(8,128)(2,1)S(1)}, bf16[128,1024]{1,0:T(8,128)(2,1)S(1)}, u32[]{:S(2)}, u32[]{:S(2)}) %collective-permute-start) | collective-permute-done | bytes 262176 | tf_op jit(solution)/shard_map/cond/branch_1_fun/ppermute | solution.py:40
  67.5 7.0 %collective-permute-done.2.refs_3_ = bf16[128,1024]{1,0:T(8,128)(2,1)S(1)} collective-permute-done((bf16[128,1024]{1,0:T(8,128)(2,1)S(1)}, bf16[128,1024]{1,0:T(8,128)(2,1)S(1)}, u32[]{:S(2)}, u32[]{:S(2)}) %collective-permute-start.2) | collective-permute-done | bytes 262176 | tf_op jit(solution)/shard_map/cond/branch_1_fun/ppermute | solution.py:40
  74.6 2.6 %collective-permute-done.3.refs_4_ = bf16[512,1024]{1,0:T(8,128)(2,1)S(1)} collective-permute-done((bf16[512,1024]{1,0:T(8,128)(2,1)S(1)}, bf16[512,1024]{1,0:T(8,128)(2,1)S(1)}, u32[]{:S(2)}, u32[]{:S(2)}) %collective-permute-start.3) | collective-permute-done | bytes 1048608 | tf_op jit(solution)/shard_map/cond/branch_1_fun/ppermute | solution.py:40
  77.3 8.3 %project.2 = (f32[512,256]{1,0:T(8,128)}, bf16[640,256]{1,0:T(8,128)(2,1)}, bf16[640,256]{1,0:T(8,128)(2,1)}, bf16[640,256]{1,0:T(8,128)(2,1)}) custom-call(s32[3]{0:T(128)S(1)} %get-tuple-element.10.place_ref, bf16[128,1024]{1,0:T(8,128)(2,1)S(1)} %get-tuple-element.22.refs_0_, bf16[128,1024]{1,0:T(8,128)(2,1)S(1)} %collective-permute-done.refs_1_, ...), custom_call_target="tpu_custom_call" | custom-call | flops 2147483648 | bytes 7864320 | tf_op jit(solution)/shard_map/cond/branch_1_fun/project/pallas_call | solution.py:264
  85.6 1.7 collective-permute-start.22
  87.3 2.7 %collective-permute-start.23 = (bf16[640,256]{1,0:T(8,128)(2,1)}, bf16[640,256]{1,0:T(8,128)(2,1)S(1)}, u32[]{:S(2)}, u32[]{:S(2)}) collective-permute-start(bf16[640,256]{1,0:T(8,128)(2,1)} %get-tuple-element.87), channel_id=1, source_target_pairs={{0,24},{1,25},{2,26},{3,27},{4,28},{5,29},{6,30},{7,31},{8,16},{9,... | collective-permute-start | bytes 983048 | tf_op jit(solution)/shard_map/ppermute | solution.py:40
  90.0 3.2 %normalize.2 = (f32[512,256]{1,0:T(8,128)S(1)}, bf16[512,256]{1,0:T(8,128)(2,1)S(1)}, f32[1,256]{1,0:T(1,128)S(1)}, f32[256,512]{1,0:T(8,128)}, f32[256,512]{1,0:T(8,128)}) custom-call(s32[3]{0:T(128)S(1)} %pad_add_fusion.place_ref, f32[512,256]{1,0:T(8,128)S(1)} %get-tuple-element.88.refs_0_, bf16[640,256]{1,0:T(8,128)(2,1)S(1)} %collective-permute-done.24.refs_1_, ...), custom_call_target="tpu_custom_call" | custom-call | flops 134217728 | bytes 3145728 | tf_op jit(solution)/shard_map/normalize/pallas_call | solution.py:348
  93.3 27.4 %conditional.3 = (bf16[16,512]{1,0:T(8,128)(2,1)S(1)}) conditional(s32[]{:T(128)} %convert_element_type.4, () %tuple.33, (f32[256,512]{1,0:T(8,128)}, f32[256,512]{1,0:T(8,128)}, s32[]{:T(128)}, s32[]{:T(128)}, s32[3]{0:T(128)S(1)}) %tuple.34), branch_computations={%region_2.3_spmd, %region_3.4_spmd} | conditional | flops 229406 | bytes 7340696 | solution.py:147
  93.3 2.1 %collective-permute-done.4 = f32[256,512]{1,0:T(8,128)S(1)} collective-permute-done((f32[256,512]{1,0:T(8,128)}, f32[256,512]{1,0:T(8,128)S(1)}, u32[]{:S(2)}, u32[]{:S(2)}) %collective-permute-start.4) | collective-permute-done | bytes 524320 | tf_op jit(solution)/shard_map/cond/branch_1_fun/ppermute | solution.py:40
  95.4 1.1 add.59
  97.7 4.5 %collective-permute-done.5 = f32[64,512]{1,0:T(8,128)S(1)} collective-permute-done((f32[64,512]{1,0:T(8,128)S(1)}, f32[64,512]{1,0:T(8,128)S(1)}, u32[]{:S(2)}, u32[]{:S(2)}) %collective-permute-start.5) | collective-permute-done | bytes 131104 | tf_op jit(solution)/shard_map/cond/branch_1_fun/ppermute | solution.py:40
  102.6 5.4 %collective-permute-done.7 = f32[64,512]{1,0:T(8,128)S(1)} collective-permute-done((f32[64,512]{1,0:T(8,128)S(1)}, f32[64,512]{1,0:T(8,128)S(1)}, u32[]{:S(2)}, u32[]{:S(2)}) %collective-permute-start.7) | collective-permute-done | bytes 131104 | tf_op jit(solution)/shard_map/cond/branch_1_fun/ppermute | solution.py:40
  108.2 1.7 collective-permute-start.9
  109.9 2.2 %collective-permute-done.8.refs_1_ = f32[16,512]{1,0:T(8,128)S(1)} collective-permute-done((f32[16,512]{1,0:T(8,128)S(1)}, f32[16,512]{1,0:T(8,128)S(1)}, u32[]{:S(2)}, u32[]{:S(2)}) %collective-permute-start.8) | collective-permute-done | bytes 32800 | tf_op jit(solution)/shard_map/cond/branch_1_fun/ppermute | solution.py:40
  112.1 1.3 collective-permute-start.10
  113.4 6.7 %collective-permute-done.9.refs_2_ = f32[16,512]{1,0:T(8,128)S(1)} collective-permute-done((f32[16,512]{1,0:T(8,128)S(1)}, f32[16,512]{1,0:T(8,128)S(1)}, u32[]{:S(2)}, u32[]{:S(2)}) %collective-permute-start.9) | collective-permute-done | bytes 32800 | tf_op jit(solution)/shard_map/cond/branch_1_fun/ppermute | solution.py:40
  120.7 1.5 collective-permute-start.27
  123.2 2.0 %collective-permute-start.29 = (bf16[16,512]{1,0:T(8,128)(2,1)S(1)}, bf16[16,512]{1,0:T(8,128)(2,1)S(1)}, u32[]{:S(2)}, u32[]{:S(2)}) collective-permute-start(bf16[16,512]{1,0:T(8,128)(2,1)S(1)} %get-tuple-element.196), channel_id=1, source_target_pairs={{0,8},{1,9},{2,10},{3,11},{4,12},{5,13},{6,14},{7,15},{8,0},{9,1},... | collective-permute-start | bytes 49160 | tf_op jit(solution)/shard_map/ppermute | solution.py:40
  125.2 1.1 collective-permute-done.27
  127.5 1.4 collective-permute-start.31
  128.9 1.6 collective-permute-start.32
  130.6 3.9 %normalize.3 = (f32[512,256]{1,0:T(8,128)S(1)}, bf16[512,256]{1,0:T(8,128)(2,1)S(1)}, f32[1,256]{1,0:T(1,128)S(1)}, f32[256,512]{1,0:T(8,128)S(1)}, f32[256,512]{1,0:T(8,128)}, /*index=5*/f32[1,256]{1,0:T(1,128)S(1)}) custom-call(s32[3]{0:T(128)S(1)} %pad_add_fusion.place_ref, f32[512,256]{1,0:T(8,128)} %get-tuple-element.95.refs_0_, ...), custom_call_target="tpu_custom_call" | custom-call | flops 134217728 | bytes 3145728 | tf_op jit(solution)/shard_map/normalize/pallas_call | solution.py:348
  135.2 1.4 collective-permute-done.34
  137.8 2.5 %collective-permute-start.37 = (f32[64,512]{1,0:T(8,128)S(1)}, f32[64,512]{1,0:T(8,128)S(1)}, u32[]{:S(2)}, u32[]{:S(2)}) collective-permute-start(f32[64,512]{1,0:T(8,128)S(1)} %get-tuple-element.138), channel_id=1, source_target_pairs={{0,6},{1,7},{2,4},{3,5},{4,2},{5,3},{6,0},{7,1},{8,14},{9,15},{10,... | collective-permute-start | bytes 393224 | tf_op jit(solution)/shard_map/ppermute | solution.py:40
  140.3 1.0 broadcast_select_fusion.3
  141.3 1.8 collective-permute-done.35
  143.1 2.1 %collective-permute-done.36 = f32[64,512]{1,0:T(8,128)S(1)} collective-permute-done((f32[64,512]{1,0:T(8,128)S(1)}, f32[64,512]{1,0:T(8,128)S(1)}, u32[]{:S(2)}, u32[]{:S(2)}) %collective-permute-start.36) | collective-permute-done | bytes 131104 | tf_op jit(solution)/shard_map/ppermute | solution.py:40
  145.3 2.0 %collective-permute-start.38 = (f32[16,512]{1,0:T(8,128)S(1)}, f32[16,512]{1,0:T(8,128)S(1)}, u32[]{:S(2)}, u32[]{:S(2)}) collective-permute-start(f32[16,512]{1,0:T(8,128)S(1)} %get-tuple-element.165), channel_id=1, source_target_pairs={{0,8},{1,9},{2,10},{3,11},{4,12},{5,13},{6,14},{7,15},{8,0},{9,1},... | collective-permute-start | bytes 98312 | tf_op jit(solution)/shard_map/ppermute | solution.py:40
  148.2 1.6 collective-permute-start.40
  149.8 1.0 gradient.2
  150.8 1.4 collective-permute-done.39.refs_2_
  152.3 1.6 collective-permute-done.40.refs_3_
  154.6 1.6 collective-permute-start.44
  156.2 2.8 %collective-permute-start.46 = (bf16[16,512]{1,0:T(8,128)(2,1)S(1)}, bf16[16,512]{1,0:T(8,128)(2,1)S(1)}, u32[]{:S(2)}, u32[]{:S(2)}) collective-permute-start(bf16[16,512]{1,0:T(8,128)(2,1)S(1)} %finish.3), channel_id=1, source_target_pairs={{0,8},{1,9},{2,10},{3,11},{4,12},{5,13},{6,14},{7,15},{8,0},{9,1},... | collective-permute-start | bytes 49160 | tf_op jit(solution)/shard_map/ppermute | solution.py:40
  159.0 1.1 collective-permute-done.44
  161.0 1.6 collective-permute-start.47
  162.6 1.5 collective-permute-start.48
  164.5 2.2 %collective-permute-start.41 = (bf16[128,256]{1,0:T(8,128)(2,1)S(1)}, bf16[128,256]{1,0:T(8,128)(2,1)S(1)}, u32[]{:S(2)}, u32[]{:S(2)}) collective-permute-start(bf16[128,256]{1,0:T(8,128)(2,1)S(1)} %get-tuple-element.110), channel_id=1, source_target_pairs={{0,24},{1,25},{2,26},{3,27},{4,28},{5,29},{6,30},{7,31},{8,16},{9,... | collective-permute-start | bytes 196616 | tf_op jit(solution)/shard_map/ppermute | solution.py:40
  166.7 1.1 collective-permute-start.42
  167.8 1.1 collective-permute-start.43
  169.1 1.6 collective-permute-done.41
  170.7 1.7 collective-permute-done.42
  173.7 1.7 gradient.3
  175.4 1.4 collective-permute-start.51
  177.2 2.6 %collective-permute-start.53 = (bf16[128,256]{1,0:T(8,128)(2,1)S(1)}, bf16[128,256]{1,0:T(8,128)(2,1)S(1)}, u32[]{:S(2)}, u32[]{:S(2)}) collective-permute-start(bf16[128,256]{1,0:T(8,128)(2,1)S(1)} %get-tuple-element.120), channel_id=1, source_target_pairs={{0,8},{1,9},{2,10},{3,11},{4,12},{5,13},{6,14},{7,15},{8,0},{9,1},... | collective-permute-start | bytes 196616 | tf_op jit(solution)/shard_map/ppermute | solution.py:40
  179.8 1.7 collective-permute-done.51
  181.5 1.4 collective-permute-done.52
  (97 shorter events, 20.0 us)
Async XLA Ops:
  1.8 6.9 %collective-permute-start.11 = (bf16[64,1024]{1,0:T(8,128)(2,1)S(1)}, bf16[64,1024]{1,0:T(8,128)(2,1)S(1)}, u32[]{:S(2)}, u32[]{:S(2)}) collective-permute-start(bf16[64,1024]{1,0:T(8,128)(2,1)S(1)} %get-tuple-element.146), channel_id=1, source_target_pairs={{0,2},{1,3},{2,0},{3,1},{4,6},{5,7},{6,4},{7,5},{8,10},{9,11},{10,... | collective-permute-start | bytes 393224 | tf_op jit(solution)/shard_map/ppermute | solution.py:40
  4.8 7.8 %collective-permute-start.12 = (bf16[64,1024]{1,0:T(8,128)(2,1)S(1)}, bf16[64,1024]{1,0:T(8,128)(2,1)S(1)}, u32[]{:S(2)}, u32[]{:S(2)}) collective-permute-start(bf16[64,1024]{1,0:T(8,128)(2,1)S(1)} %get-tuple-element.148), channel_id=1, source_target_pairs={{0,4},{1,5},{2,6},{3,7},{4,0},{5,1},{6,2},{7,3},{8,12},{9,13},{10,... | collective-permute-start | bytes 393224 | tf_op jit(solution)/shard_map/ppermute | solution.py:40
  6.4 6.3 %collective-permute-start.13 = (bf16[64,1024]{1,0:T(8,128)(2,1)S(1)}, bf16[64,1024]{1,0:T(8,128)(2,1)S(1)}, u32[]{:S(2)}, u32[]{:S(2)}) collective-permute-start(bf16[64,1024]{1,0:T(8,128)(2,1)S(1)} %get-tuple-element.147), channel_id=1, source_target_pairs={{0,6},{1,7},{2,4},{3,5},{4,2},{5,3},{6,0},{7,1},{8,14},{9,15},{10,... | collective-permute-start | bytes 393224 | tf_op jit(solution)/shard_map/ppermute | solution.py:40
  12.7 8.0 %collective-permute-start.14 = (bf16[64,1024]{1,0:T(8,128)(2,1)S(1)}, bf16[64,1024]{1,0:T(8,128)(2,1)S(1)}, u32[]{:S(2)}, u32[]{:S(2)}) collective-permute-start(bf16[64,1024]{1,0:T(8,128)(2,1)S(1)} %get-tuple-element.135), channel_id=1, source_target_pairs={{0,24},{1,25},{2,26},{3,27},{4,28},{5,29},{6,30},{7,31},{8,16},{9,... | collective-permute-start | bytes 393224 | tf_op jit(solution)/shard_map/ppermute | solution.py:40
  16.3 9.8 %collective-permute-start.15 = (bf16[64,1024]{1,0:T(8,128)(2,1)S(1)}, bf16[64,1024]{1,0:T(8,128)(2,1)S(1)}, u32[]{:S(2)}, u32[]{:S(2)}) collective-permute-start(bf16[64,1024]{1,0:T(8,128)(2,1)S(1)} %get-tuple-element.134), channel_id=1, source_target_pairs={{0,16},{1,17},{2,18},{3,19},{4,20},{5,21},{6,22},{7,23},{8,24},{9,... | collective-permute-start | bytes 393224 | tf_op jit(solution)/shard_map/ppermute | solution.py:40
  16.3 9.8 %collective-permute-start.16 = (bf16[64,1024]{1,0:T(8,128)(2,1)S(1)}, bf16[64,1024]{1,0:T(8,128)(2,1)S(1)}, u32[]{:S(2)}, u32[]{:S(2)}) collective-permute-start(bf16[64,1024]{1,0:T(8,128)(2,1)S(1)} %get-tuple-element.133), channel_id=1, source_target_pairs={{0,8},{1,9},{2,10},{3,11},{4,12},{5,13},{6,14},{7,15},{8,0},{9,1},... | collective-permute-start | bytes 393224 | tf_op jit(solution)/shard_map/ppermute | solution.py:40
  28.8 9.3 %collective-permute-start.17 = (bf16[128,1024]{1,0:T(8,128)(2,1)S(1)}, bf16[128,1024]{1,0:T(8,128)(2,1)S(1)}, u32[]{:S(2)}, u32[]{:S(2)}) collective-permute-start(bf16[128,1024]{1,0:T(8,128)(2,1)S(1)} %pad_maximum_fusion.5.refs_0_), channel_id=1, source_target_pairs={{0,2},{1,3},{2,0},{3,1},{4,6},{5,7},{6,4},{7,5},{8,10},{9,11},{10,... | collective-permute-start | bytes 786440 | tf_op jit(solution)/shard_map/ppermute | solution.py:40
  30.5 12.6 %collective-permute-start.18 = (bf16[128,1024]{1,0:T(8,128)(2,1)S(1)}, bf16[128,1024]{1,0:T(8,128)(2,1)S(1)}, u32[]{:S(2)}, u32[]{:S(2)}) collective-permute-start(bf16[128,1024]{1,0:T(8,128)(2,1)S(1)} %pad_maximum_fusion.5.refs_0_), channel_id=1, source_target_pairs={{0,4},{1,5},{2,6},{3,7},{4,0},{5,1},{6,2},{7,3},{8,12},{9,13},{10,... | collective-permute-start | bytes 786440 | tf_op jit(solution)/shard_map/ppermute | solution.py:40
  31.0 12.9 %collective-permute-start.19 = (bf16[128,1024]{1,0:T(8,128)(2,1)S(1)}, bf16[128,1024]{1,0:T(8,128)(2,1)S(1)}, u32[]{:S(2)}, u32[]{:S(2)}) collective-permute-start(bf16[128,1024]{1,0:T(8,128)(2,1)S(1)} %pad_maximum_fusion.5.refs_0_), channel_id=1, source_target_pairs={{0,6},{1,7},{2,4},{3,5},{4,2},{5,3},{6,0},{7,1},{8,14},{9,15},{10,... | collective-permute-start | bytes 786440 | tf_op jit(solution)/shard_map/ppermute | solution.py:40
  44.6 2.9 %collective-permute-start.20 = (bf16[512,1024]{1,0:T(8,128)(2,1)}, bf16[512,1024]{1,0:T(8,128)(2,1)S(1)}, u32[]{:S(2)}, u32[]{:S(2)}) collective-permute-start(bf16[512,1024]{1,0:T(8,128)(2,1)} %constant_dynamic-update-slice_fusion), channel_id=1, source_target_pairs={{0,1},{1,0},{2,3},{3,2},{4,5},{5,4},{6,7},{7,6},{8,9},{9,8},{10,11... | collective-permute-start | bytes 3145736 | tf_op jit(solution)/shard_map/ppermute | solution.py:40
  54.9 32.4 %collective-permute-start.24 = (bf16[640,256]{1,0:T(8,128)(2,1)}, bf16[640,256]{1,0:T(8,128)(2,1)S(1)}, u32[]{:S(2)}, u32[]{:S(2)}) collective-permute-start(bf16[640,256]{1,0:T(8,128)(2,1)} %get-tuple-element.89), channel_id=1, source_target_pairs={{0,8},{1,9},{2,10},{3,11},{4,12},{5,13},{6,14},{7,15},{8,0},{9,1},... | collective-permute-start | bytes 983048 | tf_op jit(solution)/shard_map/ppermute | solution.py:40
  55.0 35.0 %collective-permute-start.25 = (bf16[640,256]{1,0:T(8,128)(2,1)}, bf16[640,256]{1,0:T(8,128)(2,1)S(1)}, u32[]{:S(2)}, u32[]{:S(2)}) collective-permute-start(bf16[640,256]{1,0:T(8,128)(2,1)} %get-tuple-element.90), channel_id=1, source_target_pairs={{0,16},{1,17},{2,18},{3,19},{4,20},{5,21},{6,22},{7,23},{8,24},{9,... | collective-permute-start | bytes 983048 | tf_op jit(solution)/shard_map/ppermute | solution.py:40
  56.7 33.3 %collective-permute-start.26 = (bf16[640,256]{1,0:T(8,128)(2,1)S(1)}, bf16[640,256]{1,0:T(8,128)(2,1)S(1)}, u32[]{:S(2)}, u32[]{:S(2)}) collective-permute-start(bf16[640,256]{1,0:T(8,128)(2,1)S(1)} %get-tuple-element.91), channel_id=1, source_target_pairs={{0,24},{1,25},{2,26},{3,27},{4,28},{5,29},{6,30},{7,31},{8,16},{9,... | collective-permute-start | bytes 983048 | tf_op jit(solution)/shard_map/ppermute | solution.py:40
  59.4 7.6 %collective-permute-start = (bf16[128,1024]{1,0:T(8,128)(2,1)S(1)}, bf16[128,1024]{1,0:T(8,128)(2,1)S(1)}, u32[]{:S(2)}, u32[]{:S(2)}) collective-permute-start(bf16[128,1024]{1,0:T(8,128)(2,1)S(1)} %get-tuple-element.22.refs_0_), channel_id=1, source_target_pairs={{0,2},{1,3},{2,0},{3,1},{4,6},{5,7},{6,4},{7,5},{8,10},{9,11},{10,... | collective-permute-start | bytes 786440 | tf_op jit(solution)/shard_map/cond/branch_1_fun/ppermute | solution.py:40
  59.9 7.6 %collective-permute-start.1 = (bf16[128,1024]{1,0:T(8,128)(2,1)S(1)}, bf16[128,1024]{1,0:T(8,128)(2,1)S(1)}, u32[]{:S(2)}, u32[]{:S(2)}) collective-permute-start(bf16[128,1024]{1,0:T(8,128)(2,1)S(1)} %get-tuple-element.22.refs_0_), channel_id=1, source_target_pairs={{0,4},{1,5},{2,6},{3,7},{4,0},{5,1},{6,2},{7,3},{8,12},{9,13},{10,... | collective-permute-start | bytes 786440 | tf_op jit(solution)/shard_map/cond/branch_1_fun/ppermute | solution.py:40
  67.0 7.5 %collective-permute-start.2 = (bf16[128,1024]{1,0:T(8,128)(2,1)S(1)}, bf16[128,1024]{1,0:T(8,128)(2,1)S(1)}, u32[]{:S(2)}, u32[]{:S(2)}) collective-permute-start(bf16[128,1024]{1,0:T(8,128)(2,1)S(1)} %get-tuple-element.22.refs_0_), channel_id=1, source_target_pairs={{0,6},{1,7},{2,4},{3,5},{4,2},{5,3},{6,0},{7,1},{8,14},{9,15},{10,... | collective-permute-start | bytes 786440 | tf_op jit(solution)/shard_map/cond/branch_1_fun/ppermute | solution.py:40
  74.6 2.7 %collective-permute-start.3 = (bf16[512,1024]{1,0:T(8,128)(2,1)S(1)}, bf16[512,1024]{1,0:T(8,128)(2,1)S(1)}, u32[]{:S(2)}, u32[]{:S(2)}) collective-permute-start(bf16[512,1024]{1,0:T(8,128)(2,1)S(1)} %pad_maximum_fusion), channel_id=1, source_target_pairs={{0,1},{1,0},{2,3},{3,2},{4,5},{5,4},{6,7},{7,6},{8,9},{9,8},{10,11... | collective-permute-start | bytes 3145736 | tf_op jit(solution)/shard_map/cond/branch_1_fun/ppermute | solution.py:40
  85.6 35.1 %collective-permute-start.21 = (bf16[640,256]{1,0:T(8,128)(2,1)}, bf16[640,256]{1,0:T(8,128)(2,1)S(1)}, u32[]{:S(2)}, u32[]{:S(2)}) collective-permute-start(bf16[640,256]{1,0:T(8,128)(2,1)} %get-tuple-element.85), channel_id=1, source_target_pairs={{0,8},{1,9},{2,10},{3,11},{4,12},{5,13},{6,14},{7,15},{8,0},{9,1},... | collective-permute-start | bytes 983048 | tf_op jit(solution)/shard_map/ppermute | solution.py:40
  85.6 35.1 %collective-permute-start.22 = (bf16[640,256]{1,0:T(8,128)(2,1)}, bf16[640,256]{1,0:T(8,128)(2,1)S(1)}, u32[]{:S(2)}, u32[]{:S(2)}) collective-permute-start(bf16[640,256]{1,0:T(8,128)(2,1)} %get-tuple-element.86), channel_id=1, source_target_pairs={{0,16},{1,17},{2,18},{3,19},{4,20},{5,21},{6,22},{7,23},{8,24},{9,... | collective-permute-start | bytes 983048 | tf_op jit(solution)/shard_map/ppermute | solution.py:40
  87.3 33.4 %collective-permute-start.23 = (bf16[640,256]{1,0:T(8,128)(2,1)}, bf16[640,256]{1,0:T(8,128)(2,1)S(1)}, u32[]{:S(2)}, u32[]{:S(2)}) collective-permute-start(bf16[640,256]{1,0:T(8,128)(2,1)} %get-tuple-element.87), channel_id=1, source_target_pairs={{0,24},{1,25},{2,26},{3,27},{4,28},{5,29},{6,30},{7,31},{8,16},{9,... | collective-permute-start | bytes 983048 | tf_op jit(solution)/shard_map/ppermute | solution.py:40
  93.3 2.1 %collective-permute-start.4 = (f32[256,512]{1,0:T(8,128)}, f32[256,512]{1,0:T(8,128)S(1)}, u32[]{:S(2)}, u32[]{:S(2)}) collective-permute-start(f32[256,512]{1,0:T(8,128)} %get-tuple-element.26), channel_id=1, source_target_pairs={{0,1},{1,0},{2,3},{3,2},{4,5},{5,4},{6,7},{7,6},{8,9},{9,8},{10,11... | collective-permute-start | bytes 1572872 | tf_op jit(solution)/shard_map/cond/branch_1_fun/ppermute | solution.py:40
  96.6 5.6 %collective-permute-start.5 = (f32[64,512]{1,0:T(8,128)S(1)}, f32[64,512]{1,0:T(8,128)S(1)}, u32[]{:S(2)}, u32[]{:S(2)}) collective-permute-start(f32[64,512]{1,0:T(8,128)S(1)} %get-tuple-element.128), channel_id=1, source_target_pairs={{0,2},{1,3},{2,0},{3,1},{4,6},{5,7},{6,4},{7,5},{8,10},{9,11},{10,... | collective-permute-start | bytes 393224 | tf_op jit(solution)/shard_map/cond/branch_1_fun/ppermute | solution.py:40
  97.0 5.6 %collective-permute-start.6 = (f32[64,512]{1,0:T(8,128)S(1)}, f32[64,512]{1,0:T(8,128)S(1)}, u32[]{:S(2)}, u32[]{:S(2)}) collective-permute-start(f32[64,512]{1,0:T(8,128)S(1)} %get-tuple-element.126), channel_id=1, source_target_pairs={{0,4},{1,5},{2,6},{3,7},{4,0},{5,1},{6,2},{7,3},{8,12},{9,13},{10,... | collective-permute-start | bytes 393224 | tf_op jit(solution)/shard_map/cond/branch_1_fun/ppermute | solution.py:40
  102.2 5.9 %collective-permute-start.7 = (f32[64,512]{1,0:T(8,128)S(1)}, f32[64,512]{1,0:T(8,128)S(1)}, u32[]{:S(2)}, u32[]{:S(2)}) collective-permute-start(f32[64,512]{1,0:T(8,128)S(1)} %get-tuple-element.29), channel_id=1, source_target_pairs={{0,6},{1,7},{2,4},{3,5},{4,2},{5,3},{6,0},{7,1},{8,14},{9,15},{10,... | collective-permute-start | bytes 393224 | tf_op jit(solution)/shard_map/cond/branch_1_fun/ppermute | solution.py:40
  108.1 4.0 %collective-permute-start.8 = (f32[16,512]{1,0:T(8,128)S(1)}, f32[16,512]{1,0:T(8,128)S(1)}, u32[]{:S(2)}, u32[]{:S(2)}) collective-permute-start(f32[16,512]{1,0:T(8,128)S(1)} %get-tuple-element.131), channel_id=1, source_target_pairs={{0,8},{1,9},{2,10},{3,11},{4,12},{5,13},{6,14},{7,15},{8,0},{9,1},... | collective-permute-start | bytes 98312 | tf_op jit(solution)/shard_map/cond/branch_1_fun/ppermute | solution.py:40
  108.2 11.9 %collective-permute-start.9 = (f32[16,512]{1,0:T(8,128)S(1)}, f32[16,512]{1,0:T(8,128)S(1)}, u32[]{:S(2)}, u32[]{:S(2)}) collective-permute-start(f32[16,512]{1,0:T(8,128)S(1)} %get-tuple-element.129), channel_id=1, source_target_pairs={{0,16},{1,17},{2,18},{3,19},{4,20},{5,21},{6,22},{7,23},{8,24},{9,... | collective-permute-start | bytes 98312 | tf_op jit(solution)/shard_map/cond/branch_1_fun/ppermute | solution.py:40
  112.1 8.0 %collective-permute-start.10 = (f32[16,512]{1,0:T(8,128)S(1)}, f32[16,512]{1,0:T(8,128)S(1)}, u32[]{:S(2)}, u32[]{:S(2)}) collective-permute-start(f32[16,512]{1,0:T(8,128)S(1)} %get-tuple-element.32), channel_id=1, source_target_pairs={{0,24},{1,25},{2,26},{3,27},{4,28},{5,29},{6,30},{7,31},{8,16},{9,... | collective-permute-start | bytes 98312 | tf_op jit(solution)/shard_map/cond/branch_1_fun/ppermute | solution.py:40
  120.7 5.6 %collective-permute-start.27 = (bf16[16,512]{1,0:T(8,128)(2,1)S(1)}, bf16[16,512]{1,0:T(8,128)(2,1)S(1)}, u32[]{:S(2)}, u32[]{:S(2)}) collective-permute-start(bf16[16,512]{1,0:T(8,128)(2,1)S(1)} %get-tuple-element.196), channel_id=1, source_target_pairs={{0,24},{1,25},{2,26},{3,27},{4,28},{5,29},{6,30},{7,31},{8,16},{9,... | collective-permute-start | bytes 49160 | tf_op jit(solution)/shard_map/ppermute | solution.py:40
  122.2 4.6 %collective-permute-start.28 = (bf16[16,512]{1,0:T(8,128)(2,1)S(1)}, bf16[16,512]{1,0:T(8,128)(2,1)S(1)}, u32[]{:S(2)}, u32[]{:S(2)}) collective-permute-start(bf16[16,512]{1,0:T(8,128)(2,1)S(1)} %get-tuple-element.196), channel_id=1, source_target_pairs={{0,16},{1,17},{2,18},{3,19},{4,20},{5,21},{6,22},{7,23},{8,24},{9,... | collective-permute-start | bytes 49160 | tf_op jit(solution)/shard_map/ppermute | solution.py:40
  123.2 3.8 %collective-permute-start.29 = (bf16[16,512]{1,0:T(8,128)(2,1)S(1)}, bf16[16,512]{1,0:T(8,128)(2,1)S(1)}, u32[]{:S(2)}, u32[]{:S(2)}) collective-permute-start(bf16[16,512]{1,0:T(8,128)(2,1)S(1)} %get-tuple-element.196), channel_id=1, source_target_pairs={{0,8},{1,9},{2,10},{3,11},{4,12},{5,13},{6,14},{7,15},{8,0},{9,1},... | collective-permute-start | bytes 49160 | tf_op jit(solution)/shard_map/ppermute | solution.py:40
  127.0 7.4 %collective-permute-start.30 = (bf16[64,512]{1,0:T(8,128)(2,1)S(1)}, bf16[64,512]{1,0:T(8,128)(2,1)S(1)}, u32[]{:S(2)}, u32[]{:S(2)}) collective-permute-start(bf16[64,512]{1,0:T(8,128)(2,1)S(1)} %pad_maximum_fusion.10), channel_id=1, source_target_pairs={{0,6},{1,7},{2,4},{3,5},{4,2},{5,3},{6,0},{7,1},{8,14},{9,15},{10,... | collective-permute-start | bytes 196616 | tf_op jit(solution)/shard_map/ppermute | solution.py:40
  127.5 6.9 %collective-permute-start.31 = (bf16[64,512]{1,0:T(8,128)(2,1)S(1)}, bf16[64,512]{1,0:T(8,128)(2,1)S(1)}, u32[]{:S(2)}, u32[]{:S(2)}) collective-permute-start(bf16[64,512]{1,0:T(8,128)(2,1)S(1)} %pad_maximum_fusion.10), channel_id=1, source_target_pairs={{0,4},{1,5},{2,6},{3,7},{4,0},{5,1},{6,2},{7,3},{8,12},{9,13},{10,... | collective-permute-start | bytes 196616 | tf_op jit(solution)/shard_map/ppermute | solution.py:40
  128.9 5.5 %collective-permute-start.32 = (bf16[64,512]{1,0:T(8,128)(2,1)S(1)}, bf16[64,512]{1,0:T(8,128)(2,1)S(1)}, u32[]{:S(2)}, u32[]{:S(2)}) collective-permute-start(bf16[64,512]{1,0:T(8,128)(2,1)S(1)} %pad_maximum_fusion.10), channel_id=1, source_target_pairs={{0,2},{1,3},{2,0},{3,1},{4,6},{5,7},{6,4},{7,5},{8,10},{9,11},{10,... | collective-permute-start | bytes 196616 | tf_op jit(solution)/shard_map/ppermute | solution.py:40
  134.5 2.1 %collective-permute-start.34 = (f32[256,512]{1,0:T(8,128)}, f32[256,512]{1,0:T(8,128)S(1)}, u32[]{:S(2)}, u32[]{:S(2)}) collective-permute-start(f32[256,512]{1,0:T(8,128)} %get-tuple-element.109), channel_id=1, source_target_pairs={{0,1},{1,0},{2,3},{3,2},{4,5},{5,4},{6,7},{7,6},{8,9},{9,8},{10,11... | collective-permute-start | bytes 1572872 | tf_op jit(solution)/shard_map/ppermute | solution.py:40
  134.6 5.6 %collective-permute-start.33 = (bf16[256,512]{1,0:T(8,128)(2,1)S(1)}, bf16[256,512]{1,0:T(8,128)(2,1)}, u32[]{:S(2)}, u32[]{:S(2)}) collective-permute-start(bf16[256,512]{1,0:T(8,128)(2,1)S(1)} %pad_maximum_fusion.6), channel_id=1, source_target_pairs={{0,1},{1,0},{2,3},{3,2},{4,5},{5,4},{6,7},{7,6},{8,9},{9,8},{10,11... | collective-permute-start | bytes 786440 | tf_op jit(solution)/shard_map/ppermute | solution.py:40
  136.7 6.4 %collective-permute-start.35 = (f32[64,512]{1,0:T(8,128)S(1)}, f32[64,512]{1,0:T(8,128)S(1)}, u32[]{:S(2)}, u32[]{:S(2)}) collective-permute-start(f32[64,512]{1,0:T(8,128)S(1)} %get-tuple-element.140), channel_id=1, source_target_pairs={{0,2},{1,3},{2,0},{3,1},{4,6},{5,7},{6,4},{7,5},{8,10},{9,11},{10,... | collective-permute-start | bytes 393224 | tf_op jit(solution)/shard_map/ppermute | solution.py:40
  137.2 8.1 %collective-permute-start.36 = (f32[64,512]{1,0:T(8,128)S(1)}, f32[64,512]{1,0:T(8,128)S(1)}, u32[]{:S(2)}, u32[]{:S(2)}) collective-permute-start(f32[64,512]{1,0:T(8,128)S(1)} %get-tuple-element.139), channel_id=1, source_target_pairs={{0,4},{1,5},{2,6},{3,7},{4,0},{5,1},{6,2},{7,3},{8,12},{9,13},{10,... | collective-permute-start | bytes 393224 | tf_op jit(solution)/shard_map/ppermute | solution.py:40
  137.8 7.4 %collective-permute-start.37 = (f32[64,512]{1,0:T(8,128)S(1)}, f32[64,512]{1,0:T(8,128)S(1)}, u32[]{:S(2)}, u32[]{:S(2)}) collective-permute-start(f32[64,512]{1,0:T(8,128)S(1)} %get-tuple-element.138), channel_id=1, source_target_pairs={{0,6},{1,7},{2,4},{3,5},{4,2},{5,3},{6,0},{7,1},{8,14},{9,15},{10,... | collective-permute-start | bytes 393224 | tf_op jit(solution)/shard_map/ppermute | solution.py:40
  145.3 5.5 %collective-permute-start.38 = (f32[16,512]{1,0:T(8,128)S(1)}, f32[16,512]{1,0:T(8,128)S(1)}, u32[]{:S(2)}, u32[]{:S(2)}) collective-permute-start(f32[16,512]{1,0:T(8,128)S(1)} %get-tuple-element.165), channel_id=1, source_target_pairs={{0,8},{1,9},{2,10},{3,11},{4,12},{5,13},{6,14},{7,15},{8,0},{9,1},... | collective-permute-start | bytes 98312 | tf_op jit(solution)/shard_map/ppermute | solution.py:40
  147.3 5.0 %collective-permute-start.39 = (f32[16,512]{1,0:T(8,128)S(1)}, f32[16,512]{1,0:T(8,128)S(1)}, u32[]{:S(2)}, u32[]{:S(2)}) collective-permute-start(f32[16,512]{1,0:T(8,128)S(1)} %get-tuple-element.164), channel_id=1, source_target_pairs={{0,16},{1,17},{2,18},{3,19},{4,20},{5,21},{6,22},{7,23},{8,24},{9,... | collective-permute-start | bytes 98312 | tf_op jit(solution)/shard_map/ppermute | solution.py:40
  148.2 5.7 %collective-permute-start.40 = (f32[16,512]{1,0:T(8,128)S(1)}, f32[16,512]{1,0:T(8,128)S(1)}, u32[]{:S(2)}, u32[]{:S(2)}) collective-permute-start(f32[16,512]{1,0:T(8,128)S(1)} %get-tuple-element.163), channel_id=1, source_target_pairs={{0,24},{1,25},{2,26},{3,27},{4,28},{5,29},{6,30},{7,31},{8,16},{9,... | collective-permute-start | bytes 98312 | tf_op jit(solution)/shard_map/ppermute | solution.py:40
  154.6 5.6 %collective-permute-start.44 = (bf16[16,512]{1,0:T(8,128)(2,1)S(1)}, bf16[16,512]{1,0:T(8,128)(2,1)S(1)}, u32[]{:S(2)}, u32[]{:S(2)}) collective-permute-start(bf16[16,512]{1,0:T(8,128)(2,1)S(1)} %finish.3), channel_id=1, source_target_pairs={{0,24},{1,25},{2,26},{3,27},{4,28},{5,29},{6,30},{7,31},{8,16},{9,... | collective-permute-start | bytes 49160 | tf_op jit(solution)/shard_map/ppermute | solution.py:40
  156.2 4.7 %collective-permute-start.45 = (bf16[16,512]{1,0:T(8,128)(2,1)S(1)}, bf16[16,512]{1,0:T(8,128)(2,1)S(1)}, u32[]{:S(2)}, u32[]{:S(2)}) collective-permute-start(bf16[16,512]{1,0:T(8,128)(2,1)S(1)} %finish.3), channel_id=1, source_target_pairs={{0,16},{1,17},{2,18},{3,19},{4,20},{5,21},{6,22},{7,23},{8,24},{9,... | collective-permute-start | bytes 49160 | tf_op jit(solution)/shard_map/ppermute | solution.py:40
  156.2 4.7 %collective-permute-start.46 = (bf16[16,512]{1,0:T(8,128)(2,1)S(1)}, bf16[16,512]{1,0:T(8,128)(2,1)S(1)}, u32[]{:S(2)}, u32[]{:S(2)}) collective-permute-start(bf16[16,512]{1,0:T(8,128)(2,1)S(1)} %finish.3), channel_id=1, source_target_pairs={{0,8},{1,9},{2,10},{3,11},{4,12},{5,13},{6,14},{7,15},{8,0},{9,1},... | collective-permute-start | bytes 49160 | tf_op jit(solution)/shard_map/ppermute | solution.py:40
  161.0 6.9 %collective-permute-start.47 = (bf16[64,512]{1,0:T(8,128)(2,1)S(1)}, bf16[64,512]{1,0:T(8,128)(2,1)S(1)}, u32[]{:S(2)}, u32[]{:S(2)}) collective-permute-start(bf16[64,512]{1,0:T(8,128)(2,1)S(1)} %pad_maximum_fusion.11), channel_id=1, source_target_pairs={{0,6},{1,7},{2,4},{3,5},{4,2},{5,3},{6,0},{7,1},{8,14},{9,15},{10,... | collective-permute-start | bytes 196616 | tf_op jit(solution)/shard_map/ppermute | solution.py:40
  162.6 6.3 %collective-permute-start.48 = (bf16[64,512]{1,0:T(8,128)(2,1)S(1)}, bf16[64,512]{1,0:T(8,128)(2,1)S(1)}, u32[]{:S(2)}, u32[]{:S(2)}) collective-permute-start(bf16[64,512]{1,0:T(8,128)(2,1)S(1)} %pad_maximum_fusion.11), channel_id=1, source_target_pairs={{0,4},{1,5},{2,6},{3,7},{4,0},{5,1},{6,2},{7,3},{8,12},{9,13},{10,... | collective-permute-start | bytes 196616 | tf_op jit(solution)/shard_map/ppermute | solution.py:40
  164.1 4.8 %collective-permute-start.49 = (bf16[64,512]{1,0:T(8,128)(2,1)S(1)}, bf16[64,512]{1,0:T(8,128)(2,1)S(1)}, u32[]{:S(2)}, u32[]{:S(2)}) collective-permute-start(bf16[64,512]{1,0:T(8,128)(2,1)S(1)} %pad_maximum_fusion.11), channel_id=1, source_target_pairs={{0,2},{1,3},{2,0},{3,1},{4,6},{5,7},{6,4},{7,5},{8,10},{9,11},{10,... | collective-permute-start | bytes 196616 | tf_op jit(solution)/shard_map/ppermute | solution.py:40
  164.5 6.2 %collective-permute-start.41 = (bf16[128,256]{1,0:T(8,128)(2,1)S(1)}, bf16[128,256]{1,0:T(8,128)(2,1)S(1)}, u32[]{:S(2)}, u32[]{:S(2)}) collective-permute-start(bf16[128,256]{1,0:T(8,128)(2,1)S(1)} %get-tuple-element.110), channel_id=1, source_target_pairs={{0,24},{1,25},{2,26},{3,27},{4,28},{5,29},{6,30},{7,31},{8,16},{9,... | collective-permute-start | bytes 196616 | tf_op jit(solution)/shard_map/ppermute | solution.py:40
  166.7 5.7 %collective-permute-start.42 = (bf16[128,256]{1,0:T(8,128)(2,1)S(1)}, bf16[128,256]{1,0:T(8,128)(2,1)S(1)}, u32[]{:S(2)}, u32[]{:S(2)}) collective-permute-start(bf16[128,256]{1,0:T(8,128)(2,1)S(1)} %get-tuple-element.111), channel_id=1, source_target_pairs={{0,16},{1,17},{2,18},{3,19},{4,20},{5,21},{6,22},{7,23},{8,24},{9,... | collective-permute-start | bytes 196616 | tf_op jit(solution)/shard_map/ppermute | solution.py:40
  167.8 5.0 %collective-permute-start.43 = (bf16[128,256]{1,0:T(8,128)(2,1)S(1)}, bf16[128,256]{1,0:T(8,128)(2,1)S(1)}, u32[]{:S(2)}, u32[]{:S(2)}) collective-permute-start(bf16[128,256]{1,0:T(8,128)(2,1)S(1)} %get-tuple-element.112), channel_id=1, source_target_pairs={{0,8},{1,9},{2,10},{3,11},{4,12},{5,13},{6,14},{7,15},{8,0},{9,1},... | collective-permute-start | bytes 196616 | tf_op jit(solution)/shard_map/ppermute | solution.py:40
  169.1 4.5 %collective-permute-start.50 = (bf16[256,512]{1,0:T(8,128)(2,1)S(1)}, bf16[256,512]{1,0:T(8,128)(2,1)S(1)}, u32[]{:S(2)}, u32[]{:S(2)}) collective-permute-start(bf16[256,512]{1,0:T(8,128)(2,1)S(1)} %pad_maximum_fusion.8), channel_id=1, source_target_pairs={{0,1},{1,0},{2,3},{3,2},{4,5},{5,4},{6,7},{7,6},{8,9},{9,8},{10,11... | collective-permute-start | bytes 786440 | tf_op jit(solution)/shard_map/ppermute | solution.py:40
  175.4 6.1 %collective-permute-start.51 = (bf16[128,256]{1,0:T(8,128)(2,1)S(1)}, bf16[128,256]{1,0:T(8,128)(2,1)S(1)}, u32[]{:S(2)}, u32[]{:S(2)}) collective-permute-start(bf16[128,256]{1,0:T(8,128)(2,1)S(1)} %get-tuple-element.118), channel_id=1, source_target_pairs={{0,24},{1,25},{2,26},{3,27},{4,28},{5,29},{6,30},{7,31},{8,16},{9,... | collective-permute-start | bytes 196616 | tf_op jit(solution)/shard_map/ppermute | solution.py:40
  176.8 6.0 %collective-permute-start.52 = (bf16[128,256]{1,0:T(8,128)(2,1)S(1)}, bf16[128,256]{1,0:T(8,128)(2,1)S(1)}, u32[]{:S(2)}, u32[]{:S(2)}) collective-permute-start(bf16[128,256]{1,0:T(8,128)(2,1)S(1)} %get-tuple-element.119), channel_id=1, source_target_pairs={{0,16},{1,17},{2,18},{3,19},{4,20},{5,21},{6,22},{7,23},{8,24},{9,... | collective-permute-start | bytes 196616 | tf_op jit(solution)/shard_map/ppermute | solution.py:40
  177.2 5.6 %collective-permute-start.53 = (bf16[128,256]{1,0:T(8,128)(2,1)S(1)}, bf16[128,256]{1,0:T(8,128)(2,1)S(1)}, u32[]{:S(2)}, u32[]{:S(2)}) collective-permute-start(bf16[128,256]{1,0:T(8,128)(2,1)S(1)} %get-tuple-element.120), channel_id=1, source_target_pairs={{0,8},{1,9},{2,10},{3,11},{4,12},{5,13},{6,14},{7,15},{8,0},{9,1},... | collective-permute-start | bytes 196616 | tf_op jit(solution)/shard_map/ppermute | solution.py:40

commit v2 on v1

--- a/solution.py
+++ b/solution.py
@@ -125,21 +125,16 @@
     )(place_array, *parts)
 
 
-def gram_rows(place, place_array, grams, last):
-    few = not last
+def plane_rows(place, grams, few=False):
     part = grams[0]
     for step in range(1, place.k):
         part = part + place.send(grams[step], lambda z, a, b, s=step: (z, a, b ^ s))
-    part = reduce_scatter(place, "a", part, few)
+    return reduce_scatter(place, "a", part, few)
+
+
+def plane_parts(place, part):
     height, width = part.shape
-    part = part.reshape(place.n, height // place.n, width)
-    return finish(place, place_array, exchange(place, "z", part, few), last)
-
-
-def whole_gram(place, part):
-    for axis in ("z", "a", "b"):
-        part = gather(place, axis, part)
-    return part
+    return exchange(place, "z", part.reshape(place.n, height // place.n, width))
 
 
 def in_one(place, run, args):
@@ -161,46 +156,110 @@
     return part
 
 
-def spread(place, views):
-    n = place.n
+def cut_kernel(place_ref, *refs, n):
+    views, outs = refs[:-n], refs[-n:]
+    few = outs[0].shape[0] // len(views)
+    for step in range(n):
+        at = pl.ds(pl.multiple_of((place_ref[1] ^ step) * few, few), few)
+        for i, view in enumerate(views):
+            outs[step][i * few : (i + 1) * few, :] = view[at, :]
+
+
+def lay_kernel(place_ref, *refs, n):
+    parts, outs = refs[:n], refs[n:]
+    few = parts[0].shape[0] // len(outs)
+    for step in range(n):
+        at = pl.ds(pl.multiple_of((place_ref[0] ^ step) * few, few), few)
+        for i, out in enumerate(outs):
+            out[at, :] = parts[step][i * few : (i + 1) * few, :]
+
+
+def fetch_kernel(place_ref, weight_ref, held_ref, arrived, *, n, k):
+    width, columns = held_ref.shape[1] // k, held_ref.shape[2]
+    copies = []
+    for step in [*range(1, n), 0]:
+        at = pl.ds(pl.multiple_of((place_ref[0] ^ step) * columns, columns), columns)
+        for i in range(k):
+            rows = pl.ds(pl.multiple_of((place_ref[2] ^ i) * width, width), width)
+            copies.append(
+                pltpu.make_async_copy(
+                    weight_ref.at[rows, at],
+                    held_ref.at[step, i * width : (i + 1) * width],
+                    arrived.at[step, i],
+                )
+            )
+            copies[-1].start()
+    for copy in copies:
+        copy.wait()
+
+
+def local(kernel, place_array, args, shapes, name, spaces=None, **more):
+    space = pl.BlockSpec(memory_space=pltpu.VMEM)
+    spaces = [space] * len(args) if spaces is None else spaces
+    return pl.pallas_call(
+        kernel,
+        in_specs=[pl.BlockSpec(memory_space=pltpu.SMEM)] + spaces,
+        out_specs=[space] * len(shapes),
+        out_shape=[jax.ShapeDtypeStruct(shape, dtype) for shape, dtype in shapes],
+        name=name,
+        **more,
+    )(place_array, *args)
+
+
+def spread(place, place_array, views, weight):
+    n, k = place.n, place.k
     rows, width = views[0].shape
     few = rows // n
-    values = jnp.stack([view.reshape(n, few, width) for view in views], 1)
-    values = values.reshape(n, len(views) * few, width)
-    parts = ordered(exchange(place, "a", values), place.a ^ place.z)
-    parts = ordered(sends(place, "z", parts), place.z)
-    return [
-        jnp.concatenate([part[view * few : (view + 1) * few] for part in parts], 0)
-        for view in range(len(views))
-    ]
+    limit = pltpu.CompilerParams(vmem_limit_bytes=VMEM_BYTES // 2)
+    parts = local(
+        functools.partial(cut_kernel, n=n),
+        place_array,
+        views,
+        [((len(views) * few, width), BF16)] * n,
+        "cut",
+        compiler_params=limit,
+    )
+    parts = sends(place, "a", parts)
+    (held,) = local(
+        functools.partial(fetch_kernel, n=n, k=k),
+        place_array,
+        (weight,),
+        [((n, weight.shape[0], weight.shape[1] // n), BF16)],
+        "fetch",
+        [pl.BlockSpec(memory_space=pl.ANY)],
+        scratch_shapes=[pltpu.SemaphoreType.DMA((n, k))],
+        compiler_params=limit,
+    )
+    parts, held = lax.optimization_barrier((parts, held))
+    parts = sends(place, "z", ordered(parts, place.a ^ place.z))
+    laid = local(
+        functools.partial(lay_kernel, n=n),
+        place_array,
+        parts,
+        [((rows, width), BF16)] * len(views),
+        "lay",
+        compiler_params=limit,
+    )
+    return laid, held
 
 
 def met_rows(place, values, few=False):
     return sends(place, "a", [values] * place.n, few)
 
 
-def project_kernel(place_ref, *refs, n, k):
-    met, others = refs[:n], refs[n : n + k - 1]
-    weight_ref = refs[n + k - 1]
-    own_ref, coded = refs[n + k], refs[n + k + 1 : 2 * n + k]
-    held_ref, arrived = refs[2 * n + k :]
+def project_kernel(*refs, counts, n, k):
+    met = refs[: sum(counts)]
+    weight_ref, own_ref, *coded = refs[sum(counts) :]
     width = met[0].shape[1]
-    columns = own_ref.shape[1]
-    copies = {}
+    values = []
+    for count in counts:
+        values.append(jnp.concatenate([ref[...] for ref in met[:count]], 0))
+        met = met[count:]
     for step in [*range(1, n), 0]:
-        at = pl.ds(pl.multiple_of((place_ref[0] ^ step) * columns, columns), columns)
-        copies[step] = pltpu.make_async_copy(
-            weight_ref.at[:, at], held_ref.at[step], arrived.at[step]
-        )
-        copies[step].start()
-    own = jnp.concatenate([ref[...] for ref in met], 0)
-    for step in [*range(1, n), 0]:
-        copies[step].wait()
         total = 0.0
         for i in range(k):
-            rows = pl.ds(pl.multiple_of((place_ref[2] ^ i) * width, width), width)
-            values = own if i == 0 else others[i - 1][...]
-            total += jnp.dot(values, held_ref[step, rows, :], preferred_element_type=F32)
+            part = weight_ref[step, i * width : (i + 1) * width, :]
+            total += jnp.dot(values[i], part, preferred_element_type=F32)
         if step == 0:
             own_ref[...] = total
         else:
@@ -252,26 +311,21 @@
     return blocks
 
 
-def project(place, place_array, met, others, weight):
+def project(place, met, held):
     n, k = place.n, place.k
-    rows, width = met[0].shape
-    batch, columns = rows * n, weight.shape[1] // n
+    rows, width = met[0][0].shape
+    batch, columns = rows * n, held.shape[2]
+    counts = [len(parts) for parts in met]
+    met = [part for parts in met for part in parts]
     coded = batch + batch // SHARED
     out_shape = [jax.ShapeDtypeStruct((batch, columns), F32)]
     out_shape += [jax.ShapeDtypeStruct((coded, columns), BF16)] * (n - 1)
-    args = [*met, *others, weight]
     space = pl.BlockSpec(memory_space=pltpu.VMEM)
     own, *parts = pl.pallas_call(
-        functools.partial(project_kernel, n=n, k=k),
-        in_specs=[pl.BlockSpec(memory_space=pltpu.SMEM)]
-        + [space] * (len(args) - 1)
-        + [pl.BlockSpec(memory_space=pl.ANY)],
+        functools.partial(project_kernel, counts=counts, n=n, k=k),
+        in_specs=[space] * (len(met) + 1),
         out_specs=[space] * n,
         out_shape=out_shape,
-        scratch_shapes=[
-            pltpu.VMEM((n, k * width, columns), BF16),
-            pltpu.SemaphoreType.DMA((n,)),
-        ],
         compiler_params=pltpu.CompilerParams(vmem_limit_bytes=VMEM_BYTES),
         cost_estimate=pl.CostEstimate(
             flops=2 * batch * k * width * n * columns,
@@ -279,7 +333,7 @@
             transcendentals=0,
         ),
         name="project",
-    )(place_array, *args)
+    )(*met, held)
     return own, parts
 
 
@@ -350,7 +404,7 @@
         in_specs=[pl.BlockSpec(memory_space=pltpu.SMEM)] + [space] * len(args),
         out_specs=[space] * len(out_shape),
         out_shape=out_shape,
-        compiler_params=pltpu.CompilerParams(vmem_limit_bytes=VMEM_BYTES),
+        compiler_params=pltpu.CompilerParams(vmem_limit_bytes=VMEM_BYTES // 2),
         cost_estimate=pl.CostEstimate(
             flops=2 * batch * batch * columns,
             bytes_accessed=16 * batch * columns + 4 * batch * batch,
@@ -412,7 +466,7 @@
         out_specs=[space] * len(out_shape),
         out_shape=out_shape,
         scratch_shapes=[pltpu.VMEM((batch, columns), BF16)],
-        compiler_params=pltpu.CompilerParams(vmem_limit_bytes=VMEM_BYTES),
+        compiler_params=pltpu.CompilerParams(vmem_limit_bytes=VMEM_BYTES // 2),
         cost_estimate=pl.CostEstimate(
             flops=2 * batch * batch * columns,
             bytes_accessed=14 * batch * columns + 2 * batch * batch,
@@ -422,53 +476,67 @@
     )(place_array, *args)
 
 
-def joined(place, parts):
-    return jnp.concatenate(ordered(sends(place, "z", parts), place.z), 1)
-
-
 def with_kernels(place, h_first, h_second, weight):
     n, k, z, a, b = place.n, place.k, place.z, place.a, place.b
+    batch = h_first.shape[0] * n
     place_array = jnp.stack([z, a, b]).astype(jnp.int32)
-    first, second = spread(place, (h_first, h_second))
-
-    def projected(values, weight, few):
+    (first, second), held = spread(place, place_array, (h_first, h_second), weight)
+
+    def projected(values, held, few):
         met = met_rows(place, values, few)
-        own = jnp.concatenate(met, 0)
+        own = [jnp.concatenate(met, 0)] if few else met
         others = [
-            place.send(own, lambda z, a, b, s=step: (z, a, b ^ s)) for step in range(1, k)
+            [place.send(part, lambda z, a, b, s=step: (z, a, b ^ s)) for part in own]
+            for step in range(1, k)
         ]
-        return project(place, place_array, met, others, weight)
+        return project(place, [met, *others], held)
 
     def sent(parts):
         return sends(place, "z", [parts[0], *parts])[1:]
 
-    own_1, parts_1 = projected(first, weight, False)
+    own_1, parts_1 = projected(first, held, False)
     second, own_1 = lax.optimization_barrier((second, own_1))
     parts_1 = sent(parts_1)
     own_2, parts_2 = in_one(
-        place, lambda values, weight: projected(values, weight, True), (second, weight)
+        place, lambda values, held: projected(values, held, True), (second, held)
     )
     own_1, own_2 = lax.optimization_barrier((own_1, own_2))
     parts_2 = sent(parts_2)
     norm_1, packed_1, scale_1, *grams = normalize_parts(place, place_array, own_1, parts_1)
-    rows_1 = in_one(place, lambda *grams: gram_rows(place, place_array, grams, False), grams)
-    own_2, parts_2, rows_1 = lax.optimization_barrier((own_2, parts_2, rows_1))
+    rows_1 = in_one(place, lambda *grams: plane_rows(place, grams, True), grams)
+    met_1 = plane_parts(place, rows_1)
+    own_2, parts_2, met_1 = lax.optimization_barrier((own_2, parts_2, met_1))
     norm_2, packed_2, scale_2, *grams, coeff = normalize_parts(
         place, place_array, own_2, parts_2, norm_1
     )
-    gram_1 = whole_gram(place, rows_1)
-    grads_2 = gradient(
-        place, place_array, gram_1, packed_2, norm_2, norm_1, scale_2, coeff
-    )
-    rows_2 = gram_rows(place, place_array, grams, True)
-    grads_2, rows_2 = lax.optimization_barrier((grads_2, rows_2))
-    out_2 = joined(place, grads_2)
-    gram_2 = whole_gram(place, rows_2)
-    out_2, gram_2 = lax.optimization_barrier((out_2, gram_2))
-    *grads_1, loss = gradient(
+    met_1, norm_2 = lax.optimization_barrier((met_1, norm_2))
+    rows_1 = finish(place, place_array, met_1, False)
+    part_2 = grams[0]
+    for step in range(1, k):
+        part_2 = part_2 + place.send(grams[step], lambda z, a, b, s=step: (z, a, b ^ s))
+    height = part_2.shape[0] // n
+    met_2 = exchange(place, "a", part_2.reshape(n, height, batch))
+    met_1 = sends(place, "z", [rows_1] * n)
+    met_1, met_2 = lax.optimization_barrier((met_1, met_2))
+    met_2 = plane_parts(place, tree_sum(met_2))
+    met_1 = sends(place, "a", [jnp.concatenate(ordered(met_1, z), 0)] * n)
+    met_1, met_2 = lax.optimization_barrier((met_1, met_2))
+    met_2 = sends(place, "z", [finish(place, place_array, met_2, True)] * n)
+    met_1 = sends(place, "b", [jnp.concatenate(ordered(met_1, a), 0)] * k)
+    met_1, met_2 = lax.optimization_barrier((met_1, met_2))
+    gram_1 = jnp.concatenate(ordered(met_1, b), 0)
+    met_2 = sends(place, "a", [jnp.concatenate(ordered(met_2, z), 0)] * n)
+    met_1 = gradient(place, place_array, gram_1, packed_2, norm_2, norm_1, scale_2, coeff)
+    met_1 = sends(place, "z", met_1)
+    met_1, met_2 = lax.optimization_barrier((met_1, met_2))
+    met_2 = sends(place, "b", [jnp.concatenate(ordered(met_2, a), 0)] * k)
+    out_2 = jnp.concatenate(ordered(met_1, z), 1)
+    gram_2 = jnp.concatenate(ordered(met_2, b), 0)
+    *met_1, loss = gradient(
         place, place_array, gram_2, packed_1, norm_1, norm_2, scale_1, coeff, gram_1
     )
-    return (joined(place, grads_1), out_2, loss.reshape(()))
+    out_1 = jnp.concatenate(ordered(sends(place, "z", met_1), z), 1)
+    return (out_1, out_2, loss.reshape(()))
 
 
 def plain(place, h_first, h_second, weight):

time: 184 us -> 185 us (level)
  starting transfers between devices: 61 us -> 71.2 us
  waiting for transfers between devices: 84.2 us -> 74.5 us
    ppermute x54 -> x57, starting transfers between devices: 61 us -> 71.2 us  [send(): return lax.ppermute(value, ('dp', 'mp'), pairs)]
    ppermute x54 -> x57, waiting for transfers between devices: 84.2 us -> 74.5 us  [send(): return lax.ppermute(value, ('dp', 'mp'), pairs)]
    unnamed x6 -> x8, local copies, waits for them, and re-layouts: 3.98 us -> 4.88 us
    pallas_call x2 -> x5, Pallas kernels: 15.7 us -> 16.6 us  [the longest x2 11.5 us: project(): pl.pallas_call(functools.partial(project_kernel, counts=counts, n=n, k=k)...]
  transfers between devices with their start and end apart: 54 -> 57, of which waited for: 30 -> 27; matrix products, arithmetic and copies ran while one was open for 3% -> 2% of each run, Pallas kernels for 9% -> 8%
where the time goes in v2:
time: 185 us
  waiting for transfers between devices  74.5 us (40%)
  starting transfers between devices  71.2 us (38%)
  Pallas kernels  27.6 us (15%)
  other arithmetic  5.38 us (3%)
  local copies, waits for them, and re-layouts  5.01 us (3%)
    ppermute x57, waiting for transfers between devices, send(): return lax.ppermute(value, ('dp', 'mp'), pairs)  74.5 us
    ppermute x57, starting transfers between devices, send(): return lax.ppermute(value, ('dp', 'mp'), pairs)  71.2 us
    pallas_call x2, Pallas kernels, project(): pl.pallas_call(functools.partial(project_kernel, counts=counts, n=n, k=k)...  11.5 us
    pallas_call x2, Pallas kernels, normalize_parts(): pl.pallas_call(functools.partial(normalize_kernel, n=n, k=k, second=secon...  7.04 us
    pallas_call x3, Pallas kernels, local(): pl.pallas_call(kernel, in_specs=[pl.BlockSpec(memory_space=pltpu.SMEM)] +...  5.1 us
    unnamed x8, local copies, waits for them, and re-layouts  4.88 us
  transfers between devices with their start and end apart: 57, of which 27 were waited for; matrix products, arithmetic and copies ran while one was open for 2% of the time, Pallas kernels for 8%

profile of v2, /device:TPU:0, one launch (start us, length us, event | category | flops | bytes accessed | tf_op | source)
XLA Modules:
  0.0 184.6 jit_solution(7617300632777615956)
XLA Ops:
  3.2 4.0 %collective-permute-start.10 = (bf16[64,1024]{1,0:T(8,128)(2,1)S(1)}, bf16[64,1024]{1,0:T(8,128)(2,1)S(1)}, u32[]{:S(2)}, u32[]{:S(2)}) collective-permute-start(bf16[64,1024]{1,0:T(8,128)(2,1)S(1)} %get-tuple-element.115), channel_id=1, source_target_pairs={{0,6},{1,7},{2,4},{3,5},{4,2},{5,3},{6,0},{7,1},{8,14},{9,15},{10,... | collective-permute-start | bytes 393224 | tf_op jit(solution)/shard_map/ppermute | solution.py:40
  7.8 2.2 %copy-done = bf16[2048,1024]{1,0:T(8,128)(2,1)S(1)} copy-done((bf16[2048,1024]{1,0:T(8,128)(2,1)S(1)}, bf16[2048,1024]{1,0:T(8,128)(2,1)}, u32[]{:S(2)}) %copy-start) | copy-done | bytes 4194328
  10.0 3.2 %fetch.1.refs_8_ = bf16[4,2048,256]{2,1,0:T(8,128)(2,1)} custom-call(s32[3]{0:T(128)S(1)} %pad_add_fusion.place_ref, bf16[2048,1024]{1,0:T(8,128)(2,1)S(1)} %copy-done), custom_call_target="tpu_custom_call" | custom-call | tf_op jit(solution)/shard_map/fetch/pallas_call | solution.py:199
  13.8 1.6 collective-permute-start.11
  15.4 2.6 %collective-permute-start.12 = (bf16[64,1024]{1,0:T(8,128)(2,1)S(1)}, bf16[64,1024]{1,0:T(8,128)(2,1)S(1)}, u32[]{:S(2)}, u32[]{:S(2)}) collective-permute-start(bf16[64,1024]{1,0:T(8,128)(2,1)S(1)} %get-tuple-element.211), channel_id=1, source_target_pairs={{0,16},{1,17},{2,18},{3,19},{4,20},{5,21},{6,22},{7,23},{8,24},{9,... | collective-permute-start | bytes 393224 | tf_op jit(solution)/shard_map/ppermute | solution.py:40
  18.2 2.0 %collective-permute-done.11.refs_1_ = bf16[64,1024]{1,0:T(8,128)(2,1)S(1)} collective-permute-done((bf16[64,1024]{1,0:T(8,128)(2,1)S(1)}, bf16[64,1024]{1,0:T(8,128)(2,1)S(1)}, u32[]{:S(2)}, u32[]{:S(2)}) %collective-permute-start.11) | collective-permute-done | bytes 131104 | tf_op jit(solution)/shard_map/ppermute | solution.py:40
  20.3 7.4 %collective-permute-done.12.refs_2_ = bf16[64,1024]{1,0:T(8,128)(2,1)S(1)} collective-permute-done((bf16[64,1024]{1,0:T(8,128)(2,1)S(1)}, bf16[64,1024]{1,0:T(8,128)(2,1)S(1)}, u32[]{:S(2)}, u32[]{:S(2)}) %collective-permute-start.12) | collective-permute-done | bytes 131104 | tf_op jit(solution)/shard_map/ppermute | solution.py:40
  27.7 1.3 lay.1
  29.0 1.5 collective-permute-start.14
  30.5 2.1 %collective-permute-start.15 = (bf16[128,1024]{1,0:T(8,128)(2,1)S(1)}, bf16[128,1024]{1,0:T(8,128)(2,1)S(1)}, u32[]{:S(2)}, u32[]{:S(2)}) collective-permute-start(bf16[128,1024]{1,0:T(8,128)(2,1)S(1)} %get-tuple-element.121.refs_0_), channel_id=1, source_target_pairs={{0,4},{1,5},{2,6},{3,7},{4,0},{5,1},{6,2},{7,3},{8,12},{9,13},{10,... | collective-permute-start | bytes 786440 | tf_op jit(solution)/shard_map/ppermute | solution.py:40
  32.6 4.7 %collective-permute-done.14.refs_1_ = bf16[128,1024]{1,0:T(8,128)(2,1)S(1)} collective-permute-done((bf16[128,1024]{1,0:T(8,128)(2,1)S(1)}, bf16[128,1024]{1,0:T(8,128)(2,1)S(1)}, u32[]{:S(2)}, u32[]{:S(2)}) %collective-permute-start.14) | collective-permute-done | bytes 262176 | tf_op jit(solution)/shard_map/ppermute | solution.py:40
  37.3 3.7 %collective-permute-done.15.refs_2_ = bf16[128,1024]{1,0:T(8,128)(2,1)S(1)} collective-permute-done((bf16[128,1024]{1,0:T(8,128)(2,1)S(1)}, bf16[128,1024]{1,0:T(8,128)(2,1)S(1)}, u32[]{:S(2)}, u32[]{:S(2)}) %collective-permute-start.15) | collective-permute-done | bytes 262176 | tf_op jit(solution)/shard_map/ppermute | solution.py:40
  43.3 5.3 %project.3 = (f32[512,256]{1,0:T(8,128)S(1)}, bf16[640,256]{1,0:T(8,128)(2,1)S(1)}, bf16[640,256]{1,0:T(8,128)(2,1)}, bf16[640,256]{1,0:T(8,128)(2,1)S(1)}) custom-call(bf16[128,1024]{1,0:T(8,128)(2,1)S(1)} %get-tuple-element.121.refs_0_, bf16[128,1024]{1,0:T(8,128)(2,1)S(1)} %collective-permute-done.14.refs_1_, ...), custom_call_target="tpu_custom_call" | custom-call | flops 2147483648 | bytes 7864320 | tf_op jit(solution)/shard_map/project/pallas_call | solution.py:324
  48.7 3.0 %collective-permute-start.24 = (bf16[640,256]{1,0:T(8,128)(2,1)S(1)}, bf16[640,256]{1,0:T(8,128)(2,1)S(1)}, u32[]{:S(2)}, u32[]{:S(2)}) collective-permute-start(bf16[640,256]{1,0:T(8,128)(2,1)S(1)} %get-tuple-element.132), channel_id=1, source_target_pairs={{0,8},{1,9},{2,10},{3,11},{4,12},{5,13},{6,14},{7,15},{8,0},{9,1},... | collective-permute-start | bytes 983048 | tf_op jit(solution)/shard_map/ppermute | solution.py:40
  51.7 1.6 collective-permute-start.25
  53.3 1.4 collective-permute-start.26
  54.7 26.0 %conditional.2 = ((f32[512,256]{1,0:T(8,128)}, bf16[640,256]{1,0:T(8,128)(2,1)}, bf16[640,256]{1,0:T(8,128)(2,1)}, bf16[640,256]{1,0:T(8,128)(2,1)})) conditional(s32[]{:T(128)} %convert_element_type.4, () %tuple.36, (bf16[128,1024]{1,0:T(8,128)(2,1)}, bf16[4,2048,256]{2,1,0:T(8,128)(2,1)}) %tuple.37), branch_computations={%region_0.1_spmd, %region_1.2_spmd} | conditional | flops 2151677952 | bytes 18350276 | solution.py:142
  54.7 1.5 collective-permute-start
  56.1 1.2 collective-permute-start.1
  57.3 5.3 %collective-permute-done.refs_1_ = bf16[128,1024]{1,0:T(8,128)(2,1)S(1)} collective-permute-done((bf16[128,1024]{1,0:T(8,128)(2,1)}, bf16[128,1024]{1,0:T(8,128)(2,1)S(1)}, u32[]{:S(2)}, u32[]{:S(2)}) %collective-permute-start) | collective-permute-done | bytes 262176 | tf_op jit(solution)/shard_map/cond/branch_1_fun/ppermute | solution.py:40
  62.6 2.1 %collective-permute-start.2 = (bf16[128,1024]{1,0:T(8,128)(2,1)}, bf16[128,1024]{1,0:T(8,128)(2,1)S(1)}, u32[]{:S(2)}, u32[]{:S(2)}) collective-permute-start(bf16[128,1024]{1,0:T(8,128)(2,1)} %get-tuple-element.16.refs_0_), channel_id=1, source_target_pairs={{0,6},{1,7},{2,4},{3,5},{4,2},{5,3},{6,0},{7,1},{8,14},{9,15},{10,... | collective-permute-start | bytes 786440 | tf_op jit(solution)/shard_map/cond/branch_1_fun/ppermute | solution.py:40
  64.8 5.9 %collective-permute-done.2.refs_3_ = bf16[128,1024]{1,0:T(8,128)(2,1)S(1)} collective-permute-done((bf16[128,1024]{1,0:T(8,128)(2,1)}, bf16[128,1024]{1,0:T(8,128)(2,1)S(1)}, u32[]{:S(2)}, u32[]{:S(2)}) %collective-permute-start.2) | collective-permute-done | bytes 262176 | tf_op jit(solution)/shard_map/cond/branch_1_fun/ppermute | solution.py:40
  71.8 2.6 %collective-permute-done.3.refs_4_ = bf16[512,1024]{1,0:T(8,128)(2,1)S(1)} collective-permute-done((bf16[512,1024]{1,0:T(8,128)(2,1)S(1)}, bf16[512,1024]{1,0:T(8,128)(2,1)S(1)}, u32[]{:S(2)}, u32[]{:S(2)}) %collective-permute-start.3) | collective-permute-done | bytes 1048608 | tf_op jit(solution)/shard_map/cond/branch_1_fun/ppermute | solution.py:40
  74.4 6.2 %project.2 = (f32[512,256]{1,0:T(8,128)}, bf16[640,256]{1,0:T(8,128)(2,1)}, bf16[640,256]{1,0:T(8,128)(2,1)}, bf16[640,256]{1,0:T(8,128)(2,1)}) custom-call(bf16[128,1024]{1,0:T(8,128)(2,1)S(1)} %copy-done.4, bf16[128,1024]{1,0:T(8,128)(2,1)S(1)} %collective-permute-done.refs_1_, bf16[128,1024]{1,0:T(8,128)(2,1)S(1)} %collective-permute-done.1.refs_2_, ...), custom_call_target="tpu_custom_call" | custom-call | flops 2147483648 | bytes 7864320 | tf_op jit(solution)/shard_map/cond/branch_1_fun/project/pallas_call | solution.py:324
  81.2 2.5 %collective-permute-start.22 = (bf16[640,256]{1,0:T(8,128)(2,1)}, bf16[640,256]{1,0:T(8,128)(2,1)S(1)}, u32[]{:S(2)}, u32[]{:S(2)}) collective-permute-start(bf16[640,256]{1,0:T(8,128)(2,1)} %get-tuple-element.129), channel_id=1, source_target_pairs={{0,16},{1,17},{2,18},{3,19},{4,20},{5,21},{6,22},{7,23},{8,24},{9,... | collective-permute-start | bytes 983048 | tf_op jit(solution)/shard_map/ppermute | solution.py:40
  83.6 1.4 collective-permute-start.23
  85.0 3.2 %normalize.2 = (f32[512,256]{1,0:T(8,128)S(1)}, bf16[512,256]{1,0:T(8,128)(2,1)S(1)}, f32[1,256]{1,0:T(1,128)S(1)}, f32[256,512]{1,0:T(8,128)}, f32[256,512]{1,0:T(8,128)}) custom-call(s32[3]{0:T(128)S(1)} %pad_add_fusion.place_ref, f32[512,256]{1,0:T(8,128)S(1)} %get-tuple-element.131.refs_0_, bf16[640,256]{1,0:T(8,128)(2,1)S(1)} %collective-permute-done.24.refs_1_, ...), custom_call_target="tpu_custom_call" | custom-call | flops 134217728 | bytes 3145728 | tf_op jit(solution)/shard_map/normalize/pallas_call | solution.py:402
  88.3 14.8 %conditional.3 = (f32[4,16,512]{2,1,0:T(8,128)S(1)}) conditional(s32[]{:T(128)} %convert_element_type.4, () %tuple.39, (f32[256,512]{1,0:T(8,128)}, f32[256,512]{1,0:T(8,128)}, s32[]{:T(128)}) %tuple.40), branch_computations={%region_2.3_spmd, %region_3.4_spmd} | conditional | flops 229391 | bytes 6685028 | solution.py:142
  88.3 2.1 %collective-permute-done.4 = f32[256,512]{1,0:T(8,128)S(1)} collective-permute-done((f32[256,512]{1,0:T(8,128)}, f32[256,512]{1,0:T(8,128)S(1)}, u32[]{:S(2)}, u32[]{:S(2)}) %collective-permute-start.4) | collective-permute-done | bytes 524320 | tf_op jit(solution)/shard_map/cond/branch_1_fun/ppermute | solution.py:40
  91.6 1.6 collective-permute-start.5
  93.1 1.2 collective-permute-start.6
  94.3 2.9 %collective-permute-done.5 = f32[64,512]{1,0:T(8,128)S(1)} collective-permute-done((f32[64,512]{1,0:T(8,128)S(1)}, f32[64,512]{1,0:T(8,128)S(1)}, u32[]{:S(2)}, u32[]{:S(2)}) %collective-permute-start.5) | collective-permute-done | bytes 131104 | tf_op jit(solution)/shard_map/cond/branch_1_fun/ppermute | solution.py:40
  97.2 2.1 %collective-permute-start.7 = (f32[64,512]{1,0:T(8,128)S(1)}, f32[64,512]{1,0:T(8,128)S(1)}, u32[]{:S(2)}, u32[]{:S(2)}) collective-permute-start(f32[64,512]{1,0:T(8,128)S(1)} %get-tuple-element.22), channel_id=1, source_target_pairs={{0,6},{1,7},{2,4},{3,5},{4,2},{5,3},{6,0},{7,1},{8,14},{9,15},{10,... | collective-permute-start | bytes 393224 | tf_op jit(solution)/shard_map/cond/branch_1_fun/ppermute | solution.py:40
  99.3 3.8 %collective-permute-done.7 = f32[64,512]{1,0:T(8,128)S(1)} collective-permute-done((f32[64,512]{1,0:T(8,128)S(1)}, f32[64,512]{1,0:T(8,128)S(1)}, u32[]{:S(2)}, u32[]{:S(2)}) %collective-permute-start.7) | collective-permute-done | bytes 131104 | tf_op jit(solution)/shard_map/cond/branch_1_fun/ppermute | solution.py:40
  103.2 3.0 %collective-permute-start.28 = (f32[16,512]{1,0:T(8,128)S(1)}, f32[16,512]{1,0:T(8,128)S(1)}, u32[]{:S(2)}, u32[]{:S(2)}) collective-permute-start(f32[16,512]{1,0:T(8,128)S(1)} %get-tuple-element.234), channel_id=1, source_target_pairs={{0,16},{1,17},{2,18},{3,19},{4,20},{5,21},{6,22},{7,23},{8,24},{9,... | collective-permute-start | bytes 98312 | tf_op jit(solution)/shard_map/ppermute | solution.py:40
  106.2 1.4 collective-permute-start.29
  107.6 7.8 %collective-permute-done.28.refs_2_ = f32[16,512]{1,0:T(8,128)S(1)} collective-permute-done((f32[16,512]{1,0:T(8,128)S(1)}, f32[16,512]{1,0:T(8,128)S(1)}, u32[]{:S(2)}, u32[]{:S(2)}) %collective-permute-start.28) | collective-permute-done | bytes 32800 | tf_op jit(solution)/shard_map/ppermute | solution.py:40
  115.4 3.8 %normalize.3 = (f32[512,256]{1,0:T(8,128)S(1)}, bf16[512,256]{1,0:T(8,128)(2,1)S(1)}, f32[1,256]{1,0:T(1,128)S(1)}, f32[256,512]{1,0:T(8,128)S(1)}, f32[256,512]{1,0:T(8,128)}, /*index=5*/f32[1,256]{1,0:T(1,128)S(1)}) custom-call(s32[3]{0:T(128)S(1)} %pad_add_fusion.place_ref, f32[512,256]{1,0:T(8,128)} %get-tuple-element.141.refs_0_, ...), custom_call_target="tpu_custom_call" | custom-call | flops 134217728 | bytes 3145728 | tf_op jit(solution)/shard_map/normalize/pallas_call | solution.py:402
  119.2 2.1 %collective-permute-done.33 = f32[256,512]{1,0:T(8,128)S(1)} collective-permute-done((f32[256,512]{1,0:T(8,128)}, f32[256,512]{1,0:T(8,128)S(1)}, u32[]{:S(2)}, u32[]{:S(2)}) %collective-permute-start.33) | collective-permute-done | bytes 524320 | tf_op jit(solution)/shard_map/ppermute | solution.py:40
  123.2 1.6 collective-permute-start.34
  124.8 1.2 collective-permute-start.35
  128.5 2.0 %collective-permute-start.31 = (bf16[16,512]{1,0:T(8,128)(2,1)S(1)}, bf16[16,512]{1,0:T(8,128)(2,1)S(1)}, u32[]{:S(2)}, u32[]{:S(2)}) collective-permute-start(bf16[16,512]{1,0:T(8,128)(2,1)S(1)} %finish.2), channel_id=1, source_target_pairs={{0,16},{1,17},{2,18},{3,19},{4,20},{5,21},{6,22},{7,23},{8,24},{9,... | collective-permute-start | bytes 49160 | tf_op jit(solution)/shard_map/ppermute | solution.py:40
  131.3 2.4 %collective-permute-start.32 = (bf16[16,512]{1,0:T(8,128)(2,1)S(1)}, bf16[16,512]{1,0:T(8,128)(2,1)S(1)}, u32[]{:S(2)}, u32[]{:S(2)}) collective-permute-start(bf16[16,512]{1,0:T(8,128)(2,1)S(1)} %finish.2), channel_id=1, source_target_pairs={{0,24},{1,25},{2,26},{3,27},{4,28},{5,29},{6,30},{7,31},{8,16},{9,... | collective-permute-start | bytes 49160 | tf_op jit(solution)/shard_map/ppermute | solution.py:40
  133.6 3.2 %collective-permute-done.32 = bf16[16,512]{1,0:T(8,128)(2,1)S(1)} collective-permute-done((bf16[16,512]{1,0:T(8,128)(2,1)S(1)}, bf16[16,512]{1,0:T(8,128)(2,1)S(1)}, u32[]{:S(2)}, u32[]{:S(2)}) %collective-permute-start.32) | collective-permute-done | bytes 16416 | tf_op jit(solution)/shard_map/ppermute | solution.py:40
  137.0 1.5 collective-permute-start.37
  138.5 1.2 collective-permute-start.38
  140.6 3.1 %collective-permute-start.41 = (f32[16,512]{1,0:T(8,128)S(1)}, f32[16,512]{1,0:T(8,128)S(1)}, u32[]{:S(2)}, u32[]{:S(2)}) collective-permute-start(f32[16,512]{1,0:T(8,128)S(1)} %get-tuple-element.230), channel_id=1, source_target_pairs={{0,16},{1,17},{2,18},{3,19},{4,20},{5,21},{6,22},{7,23},{8,24},{9,... | collective-permute-start | bytes 98312 | tf_op jit(solution)/shard_map/ppermute | solution.py:40
  143.7 1.3 collective-permute-start.42
  145.6 3.8 %collective-permute-done.42.refs_3_ = f32[16,512]{1,0:T(8,128)S(1)} collective-permute-done((f32[16,512]{1,0:T(8,128)S(1)}, f32[16,512]{1,0:T(8,128)S(1)}, u32[]{:S(2)}, u32[]{:S(2)}) %collective-permute-start.42) | collective-permute-done | bytes 32800 | tf_op jit(solution)/shard_map/ppermute | solution.py:40
  150.3 1.9 %collective-permute-start.45 = (bf16[16,512]{1,0:T(8,128)(2,1)S(1)}, bf16[16,512]{1,0:T(8,128)(2,1)S(1)}, u32[]{:S(2)}, u32[]{:S(2)}) collective-permute-start(bf16[16,512]{1,0:T(8,128)(2,1)S(1)} %finish.3), channel_id=1, source_target_pairs={{0,16},{1,17},{2,18},{3,19},{4,20},{5,21},{6,22},{7,23},{8,24},{9,... | collective-permute-start | bytes 49160 | tf_op jit(solution)/shard_map/ppermute | solution.py:40
  152.2 2.5 %collective-permute-start.46 = (bf16[16,512]{1,0:T(8,128)(2,1)S(1)}, bf16[16,512]{1,0:T(8,128)(2,1)S(1)}, u32[]{:S(2)}, u32[]{:S(2)}) collective-permute-start(bf16[16,512]{1,0:T(8,128)(2,1)S(1)} %finish.3), channel_id=1, source_target_pairs={{0,24},{1,25},{2,26},{3,27},{4,28},{5,29},{6,30},{7,31},{8,16},{9,... | collective-permute-start | bytes 49160 | tf_op jit(solution)/shard_map/ppermute | solution.py:40
  155.0 2.7 %collective-permute-done.46 = bf16[16,512]{1,0:T(8,128)(2,1)S(1)} collective-permute-done((bf16[16,512]{1,0:T(8,128)(2,1)S(1)}, bf16[16,512]{1,0:T(8,128)(2,1)S(1)}, u32[]{:S(2)}, u32[]{:S(2)}) %collective-permute-start.46) | collective-permute-done | bytes 16416 | tf_op jit(solution)/shard_map/ppermute | solution.py:40
  157.7 1.4 collective-permute-start.50
  159.2 1.2 collective-permute-start.51
  162.5 3.1 %collective-permute-start.48 = (bf16[128,256]{1,0:T(8,128)(2,1)S(1)}, bf16[128,256]{1,0:T(8,128)(2,1)S(1)}, u32[]{:S(2)}, u32[]{:S(2)}) collective-permute-start(bf16[128,256]{1,0:T(8,128)(2,1)S(1)} %get-tuple-element.177), channel_id=1, source_target_pairs={{0,16},{1,17},{2,18},{3,19},{4,20},{5,21},{6,22},{7,23},{8,24},{9,... | collective-permute-start | bytes 196616 | tf_op jit(solution)/shard_map/ppermute | solution.py:40
  165.6 1.3 collective-permute-start.49
  166.9 2.3 %collective-permute-done.48 = bf16[128,256]{1,0:T(8,128)(2,1)S(1)} collective-permute-done((bf16[128,256]{1,0:T(8,128)(2,1)S(1)}, bf16[128,256]{1,0:T(8,128)(2,1)S(1)}, u32[]{:S(2)}, u32[]{:S(2)}) %collective-permute-start.48) | collective-permute-done | bytes 65568 | tf_op jit(solution)/shard_map/ppermute | solution.py:40
  169.2 2.4 %collective-permute-done.49 = bf16[128,256]{1,0:T(8,128)(2,1)S(1)} collective-permute-done((bf16[128,256]{1,0:T(8,128)(2,1)S(1)}, bf16[128,256]{1,0:T(8,128)(2,1)S(1)}, u32[]{:S(2)}, u32[]{:S(2)}) %collective-permute-start.49) | collective-permute-done | bytes 65568 | tf_op jit(solution)/shard_map/ppermute | solution.py:40
  171.8 1.5 collective-permute-done.53
  173.4 1.7 gradient.3
  175.1 1.3 collective-permute-start.54
  176.4 3.1 %collective-permute-start.56 = (bf16[128,256]{1,0:T(8,128)(2,1)S(1)}, bf16[128,256]{1,0:T(8,128)(2,1)S(1)}, u32[]{:S(2)}, u32[]{:S(2)}) collective-permute-start(bf16[128,256]{1,0:T(8,128)(2,1)S(1)} %get-tuple-element.191), channel_id=1, source_target_pairs={{0,8},{1,9},{2,10},{3,11},{4,12},{5,13},{6,14},{7,15},{8,0},{9,1},... | collective-permute-start | bytes 196616 | tf_op jit(solution)/shard_map/ppermute | solution.py:40
  180.2 1.7 collective-permute-done.54
  181.9 2.0 %collective-permute-done.55 = bf16[128,256]{1,0:T(8,128)(2,1)S(1)} collective-permute-done((bf16[128,256]{1,0:T(8,128)(2,1)S(1)}, bf16[128,256]{1,0:T(8,128)(2,1)S(1)}, u32[]{:S(2)}, u32[]{:S(2)}) %collective-permute-start.55) | collective-permute-done | bytes 65568 | tf_op jit(solution)/shard_map/ppermute | solution.py:40
  (100 shorter events, 21.3 us)
Async XLA Ops:
  0.7 1.0 copy-start.1
  1.7 0.9 copy-start.2
  3.2 10.0 %collective-permute-start.10 = (bf16[64,1024]{1,0:T(8,128)(2,1)S(1)}, bf16[64,1024]{1,0:T(8,128)(2,1)S(1)}, u32[]{:S(2)}, u32[]{:S(2)}) collective-permute-start(bf16[64,1024]{1,0:T(8,128)(2,1)S(1)} %get-tuple-element.115), channel_id=1, source_target_pairs={{0,6},{1,7},{2,4},{3,5},{4,2},{5,3},{6,0},{7,1},{8,14},{9,15},{10,... | collective-permute-start | bytes 393224 | tf_op jit(solution)/shard_map/ppermute | solution.py:40
  7.2 6.6 %collective-permute-start.8 = (bf16[64,1024]{1,0:T(8,128)(2,1)S(1)}, bf16[64,1024]{1,0:T(8,128)(2,1)S(1)}, u32[]{:S(2)}, u32[]{:S(2)}) collective-permute-start(bf16[64,1024]{1,0:T(8,128)(2,1)S(1)} %get-tuple-element.113), channel_id=1, source_target_pairs={{0,2},{1,3},{2,0},{3,1},{4,6},{5,7},{6,4},{7,5},{8,10},{9,11},{10,... | collective-permute-start | bytes 393224 | tf_op jit(solution)/shard_map/ppermute | solution.py:40
  7.7 6.0 %collective-permute-start.9 = (bf16[64,1024]{1,0:T(8,128)(2,1)S(1)}, bf16[64,1024]{1,0:T(8,128)(2,1)S(1)}, u32[]{:S(2)}, u32[]{:S(2)}) collective-permute-start(bf16[64,1024]{1,0:T(8,128)(2,1)S(1)} %get-tuple-element.114), channel_id=1, source_target_pairs={{0,4},{1,5},{2,6},{3,7},{4,0},{5,1},{6,2},{7,3},{8,12},{9,13},{10,... | collective-permute-start | bytes 393224 | tf_op jit(solution)/shard_map/ppermute | solution.py:40
  7.8 2.2 %copy-start = (bf16[2048,1024]{1,0:T(8,128)(2,1)S(1)}, bf16[2048,1024]{1,0:T(8,128)(2,1)}, u32[]{:S(2)}) copy-start(bf16[2048,1024]{1,0:T(8,128)(2,1)} %weight_ref.1) | copy-start | bytes 12582916
  13.8 6.5 %collective-permute-start.11 = (bf16[64,1024]{1,0:T(8,128)(2,1)S(1)}, bf16[64,1024]{1,0:T(8,128)(2,1)S(1)}, u32[]{:S(2)}, u32[]{:S(2)}) collective-permute-start(bf16[64,1024]{1,0:T(8,128)(2,1)S(1)} %get-tuple-element.210), channel_id=1, source_target_pairs={{0,8},{1,9},{2,10},{3,11},{4,12},{5,13},{6,14},{7,15},{8,0},{9,1},... | collective-permute-start | bytes 393224 | tf_op jit(solution)/shard_map/ppermute | solution.py:40
  15.4 12.3 %collective-permute-start.12 = (bf16[64,1024]{1,0:T(8,128)(2,1)S(1)}, bf16[64,1024]{1,0:T(8,128)(2,1)S(1)}, u32[]{:S(2)}, u32[]{:S(2)}) collective-permute-start(bf16[64,1024]{1,0:T(8,128)(2,1)S(1)} %get-tuple-element.211), channel_id=1, source_target_pairs={{0,16},{1,17},{2,18},{3,19},{4,20},{5,21},{6,22},{7,23},{8,24},{9,... | collective-permute-start | bytes 393224 | tf_op jit(solution)/shard_map/ppermute | solution.py:40
  18.0 9.7 %collective-permute-start.13 = (bf16[64,1024]{1,0:T(8,128)(2,1)S(1)}, bf16[64,1024]{1,0:T(8,128)(2,1)S(1)}, u32[]{:S(2)}, u32[]{:S(2)}) collective-permute-start(bf16[64,1024]{1,0:T(8,128)(2,1)S(1)} %get-tuple-element.209), channel_id=1, source_target_pairs={{0,24},{1,25},{2,26},{3,27},{4,28},{5,29},{6,30},{7,31},{8,16},{9,... | collective-permute-start | bytes 393224 | tf_op jit(solution)/shard_map/ppermute | solution.py:40
  29.0 8.3 %collective-permute-start.14 = (bf16[128,1024]{1,0:T(8,128)(2,1)S(1)}, bf16[128,1024]{1,0:T(8,128)(2,1)S(1)}, u32[]{:S(2)}, u32[]{:S(2)}) collective-permute-start(bf16[128,1024]{1,0:T(8,128)(2,1)S(1)} %get-tuple-element.121.refs_0_), channel_id=1, source_target_pairs={{0,2},{1,3},{2,0},{3,1},{4,6},{5,7},{6,4},{7,5},{8,10},{9,11},{10,... | collective-permute-start | bytes 786440 | tf_op jit(solution)/shard_map/ppermute | solution.py:40
  30.5 10.5 %collective-permute-start.15 = (bf16[128,1024]{1,0:T(8,128)(2,1)S(1)}, bf16[128,1024]{1,0:T(8,128)(2,1)S(1)}, u32[]{:S(2)}, u32[]{:S(2)}) collective-permute-start(bf16[128,1024]{1,0:T(8,128)(2,1)S(1)} %get-tuple-element.121.refs_0_), channel_id=1, source_target_pairs={{0,4},{1,5},{2,6},{3,7},{4,0},{5,1},{6,2},{7,3},{8,12},{9,13},{10,... | collective-permute-start | bytes 786440 | tf_op jit(solution)/shard_map/ppermute | solution.py:40
  32.6 9.2 %collective-permute-start.16 = (bf16[128,1024]{1,0:T(8,128)(2,1)S(1)}, bf16[128,1024]{1,0:T(8,128)(2,1)S(1)}, u32[]{:S(2)}, u32[]{:S(2)}) collective-permute-start(bf16[128,1024]{1,0:T(8,128)(2,1)S(1)} %get-tuple-element.121.refs_0_), channel_id=1, source_target_pairs={{0,6},{1,7},{2,4},{3,5},{4,2},{5,3},{6,0},{7,1},{8,14},{9,15},{10,... | collective-permute-start | bytes 786440 | tf_op jit(solution)/shard_map/ppermute | solution.py:40
  32.6 9.2 %collective-permute-start.17 = (bf16[128,1024]{1,0:T(8,128)(2,1)S(1)}, bf16[128,1024]{1,0:T(8,128)(2,1)S(1)}, u32[]{:S(2)}, u32[]{:S(2)}) collective-permute-start(bf16[128,1024]{1,0:T(8,128)(2,1)S(1)} %get-tuple-element.121.refs_0_), channel_id=1, source_target_pairs={{0,1},{1,0},{2,3},{3,2},{4,5},{5,4},{6,7},{7,6},{8,9},{9,8},{10,11... | collective-permute-start | bytes 786440 | tf_op jit(solution)/shard_map/ppermute | solution.py:40
  37.3 4.4 %collective-permute-start.18 = (bf16[128,1024]{1,0:T(8,128)(2,1)S(1)}, bf16[128,1024]{1,0:T(8,128)(2,1)S(1)}, u32[]{:S(2)}, u32[]{:S(2)}) collective-permute-start(bf16[128,1024]{1,0:T(8,128)(2,1)S(1)} %collective-permute-done.14.refs_1_), channel_id=1, source_target_pairs={{0,1},{1,0},{2,3},{3,2},{4,5},{5,4},{6,7},{7,6},{8,9},{9,8},{10,11... | collective-permute-start | bytes 786440 | tf_op jit(solution)/shard_map/ppermute | solution.py:40
  41.0 1.5 collective-permute-start.19
  41.8 1.5 collective-permute-start.20
  48.7 35.0 %collective-permute-start.24 = (bf16[640,256]{1,0:T(8,128)(2,1)S(1)}, bf16[640,256]{1,0:T(8,128)(2,1)S(1)}, u32[]{:S(2)}, u32[]{:S(2)}) collective-permute-start(bf16[640,256]{1,0:T(8,128)(2,1)S(1)} %get-tuple-element.132), channel_id=1, source_target_pairs={{0,8},{1,9},{2,10},{3,11},{4,12},{5,13},{6,14},{7,15},{8,0},{9,1},... | collective-permute-start | bytes 983048 | tf_op jit(solution)/shard_map/ppermute | solution.py:40
  51.7 33.3 %collective-permute-start.25 = (bf16[640,256]{1,0:T(8,128)(2,1)}, bf16[640,256]{1,0:T(8,128)(2,1)S(1)}, u32[]{:S(2)}, u32[]{:S(2)}) collective-permute-start(bf16[640,256]{1,0:T(8,128)(2,1)} %get-tuple-element.133), channel_id=1, source_target_pairs={{0,16},{1,17},{2,18},{3,19},{4,20},{5,21},{6,22},{7,23},{8,24},{9,... | collective-permute-start | bytes 983048 | tf_op jit(solution)/shard_map/ppermute | solution.py:40
  53.3 31.8 %collective-permute-start.26 = (bf16[640,256]{1,0:T(8,128)(2,1)S(1)}, bf16[640,256]{1,0:T(8,128)(2,1)S(1)}, u32[]{:S(2)}, u32[]{:S(2)}) collective-permute-start(bf16[640,256]{1,0:T(8,128)(2,1)S(1)} %get-tuple-element.134), channel_id=1, source_target_pairs={{0,24},{1,25},{2,26},{3,27},{4,28},{5,29},{6,30},{7,31},{8,16},{9,... | collective-permute-start | bytes 983048 | tf_op jit(solution)/shard_map/ppermute | solution.py:40
  54.7 19.8 %copy-start.4 = (bf16[128,1024]{1,0:T(8,128)(2,1)S(1)}, bf16[128,1024]{1,0:T(8,128)(2,1)}, u32[]{:S(2)}) copy-start(bf16[128,1024]{1,0:T(8,128)(2,1)} %get-tuple-element.16.refs_0_) | copy-start | bytes 786436 | tf_op jit(solution)/shard_map/cond
  54.7 8.0 %collective-permute-start = (bf16[128,1024]{1,0:T(8,128)(2,1)}, bf16[128,1024]{1,0:T(8,128)(2,1)S(1)}, u32[]{:S(2)}, u32[]{:S(2)}) collective-permute-start(bf16[128,1024]{1,0:T(8,128)(2,1)} %get-tuple-element.16.refs_0_), channel_id=1, source_target_pairs={{0,2},{1,3},{2,0},{3,1},{4,6},{5,7},{6,4},{7,5},{8,10},{9,11},{10,... | collective-permute-start | bytes 786440 | tf_op jit(solution)/shard_map/cond/branch_1_fun/ppermute | solution.py:40
  56.1 8.6 %collective-permute-start.1 = (bf16[128,1024]{1,0:T(8,128)(2,1)}, bf16[128,1024]{1,0:T(8,128)(2,1)S(1)}, u32[]{:S(2)}, u32[]{:S(2)}) collective-permute-start(bf16[128,1024]{1,0:T(8,128)(2,1)} %get-tuple-element.16.refs_0_), channel_id=1, source_target_pairs={{0,4},{1,5},{2,6},{3,7},{4,0},{5,1},{6,2},{7,3},{8,12},{9,13},{10,... | collective-permute-start | bytes 786440 | tf_op jit(solution)/shard_map/cond/branch_1_fun/ppermute | solution.py:40
  62.6 8.0 %collective-permute-start.2 = (bf16[128,1024]{1,0:T(8,128)(2,1)}, bf16[128,1024]{1,0:T(8,128)(2,1)S(1)}, u32[]{:S(2)}, u32[]{:S(2)}) collective-permute-start(bf16[128,1024]{1,0:T(8,128)(2,1)} %get-tuple-element.16.refs_0_), channel_id=1, source_target_pairs={{0,6},{1,7},{2,4},{3,5},{4,2},{5,3},{6,0},{7,1},{8,14},{9,15},{10,... | collective-permute-start | bytes 786440 | tf_op jit(solution)/shard_map/cond/branch_1_fun/ppermute | solution.py:40
  71.7 2.7 %collective-permute-start.3 = (bf16[512,1024]{1,0:T(8,128)(2,1)S(1)}, bf16[512,1024]{1,0:T(8,128)(2,1)S(1)}, u32[]{:S(2)}, u32[]{:S(2)}) collective-permute-start(bf16[512,1024]{1,0:T(8,128)(2,1)S(1)} %pad_maximum_fusion), channel_id=1, source_target_pairs={{0,1},{1,0},{2,3},{3,2},{4,5},{5,4},{6,7},{7,6},{8,9},{9,8},{10,11... | collective-permute-start | bytes 3145736 | tf_op jit(solution)/shard_map/cond/branch_1_fun/ppermute | solution.py:40
  80.6 25.6 %collective-permute-start.21 = (bf16[640,256]{1,0:T(8,128)(2,1)}, bf16[640,256]{1,0:T(8,128)(2,1)S(1)}, u32[]{:S(2)}, u32[]{:S(2)}) collective-permute-start(bf16[640,256]{1,0:T(8,128)(2,1)} %get-tuple-element.128), channel_id=1, source_target_pairs={{0,8},{1,9},{2,10},{3,11},{4,12},{5,13},{6,14},{7,15},{8,0},{9,1},... | collective-permute-start | bytes 983048 | tf_op jit(solution)/shard_map/ppermute | solution.py:40
  81.2 26.4 %collective-permute-start.22 = (bf16[640,256]{1,0:T(8,128)(2,1)}, bf16[640,256]{1,0:T(8,128)(2,1)S(1)}, u32[]{:S(2)}, u32[]{:S(2)}) collective-permute-start(bf16[640,256]{1,0:T(8,128)(2,1)} %get-tuple-element.129), channel_id=1, source_target_pairs={{0,16},{1,17},{2,18},{3,19},{4,20},{5,21},{6,22},{7,23},{8,24},{9,... | collective-permute-start | bytes 983048 | tf_op jit(solution)/shard_map/ppermute | solution.py:40
  83.6 23.9 %collective-permute-start.23 = (bf16[640,256]{1,0:T(8,128)(2,1)}, bf16[640,256]{1,0:T(8,128)(2,1)S(1)}, u32[]{:S(2)}, u32[]{:S(2)}) collective-permute-start(bf16[640,256]{1,0:T(8,128)(2,1)} %get-tuple-element.130), channel_id=1, source_target_pairs={{0,24},{1,25},{2,26},{3,27},{4,28},{5,29},{6,30},{7,31},{8,16},{9,... | collective-permute-start | bytes 983048 | tf_op jit(solution)/shard_map/ppermute | solution.py:40
  88.3 2.1 %collective-permute-start.4 = (f32[256,512]{1,0:T(8,128)}, f32[256,512]{1,0:T(8,128)S(1)}, u32[]{:S(2)}, u32[]{:S(2)}) collective-permute-start(f32[256,512]{1,0:T(8,128)} %get-tuple-element.19), channel_id=1, source_target_pairs={{0,1},{1,0},{2,3},{3,2},{4,5},{5,4},{6,7},{7,6},{8,9},{9,8},{10,11... | collective-permute-start | bytes 1572872 | tf_op jit(solution)/shard_map/cond/branch_1_fun/ppermute | solution.py:40
  91.6 5.6 %collective-permute-start.5 = (f32[64,512]{1,0:T(8,128)S(1)}, f32[64,512]{1,0:T(8,128)S(1)}, u32[]{:S(2)}, u32[]{:S(2)}) collective-permute-start(f32[64,512]{1,0:T(8,128)S(1)} %get-tuple-element.200), channel_id=1, source_target_pairs={{0,2},{1,3},{2,0},{3,1},{4,6},{5,7},{6,4},{7,5},{8,10},{9,11},{10,... | collective-permute-start | bytes 393224 | tf_op jit(solution)/shard_map/cond/branch_1_fun/ppermute | solution.py:40
  93.1 6.2 %collective-permute-start.6 = (f32[64,512]{1,0:T(8,128)S(1)}, f32[64,512]{1,0:T(8,128)S(1)}, u32[]{:S(2)}, u32[]{:S(2)}) collective-permute-start(f32[64,512]{1,0:T(8,128)S(1)} %get-tuple-element.198), channel_id=1, source_target_pairs={{0,4},{1,5},{2,6},{3,7},{4,0},{5,1},{6,2},{7,3},{8,12},{9,13},{10,... | collective-permute-start | bytes 393224 | tf_op jit(solution)/shard_map/cond/branch_1_fun/ppermute | solution.py:40
  97.2 5.9 %collective-permute-start.7 = (f32[64,512]{1,0:T(8,128)S(1)}, f32[64,512]{1,0:T(8,128)S(1)}, u32[]{:S(2)}, u32[]{:S(2)}) collective-permute-start(f32[64,512]{1,0:T(8,128)S(1)} %get-tuple-element.22), channel_id=1, source_target_pairs={{0,6},{1,7},{2,4},{3,5},{4,2},{5,3},{6,0},{7,1},{8,14},{9,15},{10,... | collective-permute-start | bytes 393224 | tf_op jit(solution)/shard_map/cond/branch_1_fun/ppermute | solution.py:40
  103.1 4.5 %collective-permute-start.27 = (f32[16,512]{1,0:T(8,128)S(1)}, f32[16,512]{1,0:T(8,128)S(1)}, u32[]{:S(2)}, u32[]{:S(2)}) collective-permute-start(f32[16,512]{1,0:T(8,128)S(1)} %get-tuple-element.235), channel_id=1, source_target_pairs={{0,8},{1,9},{2,10},{3,11},{4,12},{5,13},{6,14},{7,15},{8,0},{9,1},... | collective-permute-start | bytes 98312 | tf_op jit(solution)/shard_map/ppermute | solution.py:40
  103.2 12.2 %collective-permute-start.28 = (f32[16,512]{1,0:T(8,128)S(1)}, f32[16,512]{1,0:T(8,128)S(1)}, u32[]{:S(2)}, u32[]{:S(2)}) collective-permute-start(f32[16,512]{1,0:T(8,128)S(1)} %get-tuple-element.234), channel_id=1, source_target_pairs={{0,16},{1,17},{2,18},{3,19},{4,20},{5,21},{6,22},{7,23},{8,24},{9,... | collective-permute-start | bytes 98312 | tf_op jit(solution)/shard_map/ppermute | solution.py:40
  106.2 9.2 %collective-permute-start.29 = (f32[16,512]{1,0:T(8,128)S(1)}, f32[16,512]{1,0:T(8,128)S(1)}, u32[]{:S(2)}, u32[]{:S(2)}) collective-permute-start(f32[16,512]{1,0:T(8,128)S(1)} %get-tuple-element.233), channel_id=1, source_target_pairs={{0,24},{1,25},{2,26},{3,27},{4,28},{5,29},{6,30},{7,31},{8,16},{9,... | collective-permute-start | bytes 98312 | tf_op jit(solution)/shard_map/ppermute | solution.py:40
  119.2 2.1 %collective-permute-start.33 = (f32[256,512]{1,0:T(8,128)}, f32[256,512]{1,0:T(8,128)S(1)}, u32[]{:S(2)}, u32[]{:S(2)}) collective-permute-start(f32[256,512]{1,0:T(8,128)} %get-tuple-element.152), channel_id=1, source_target_pairs={{0,1},{1,0},{2,3},{3,2},{4,5},{5,4},{6,7},{7,6},{8,9},{9,8},{10,11... | collective-permute-start | bytes 1572872 | tf_op jit(solution)/shard_map/ppermute | solution.py:40
  121.3 0.8 copy-start.3
  123.2 13.6 %collective-permute-start.34 = (f32[64,512]{1,0:T(8,128)S(1)}, f32[64,512]{1,0:T(8,128)S(1)}, u32[]{:S(2)}, u32[]{:S(2)}) collective-permute-start(f32[64,512]{1,0:T(8,128)S(1)} %get-tuple-element.207), channel_id=1, source_target_pairs={{0,2},{1,3},{2,0},{3,1},{4,6},{5,7},{6,4},{7,5},{8,10},{9,11},{10,... | collective-permute-start | bytes 393224 | tf_op jit(solution)/shard_map/ppermute | solution.py:40
  124.8 12.0 %collective-permute-start.35 = (f32[64,512]{1,0:T(8,128)S(1)}, f32[64,512]{1,0:T(8,128)S(1)}, u32[]{:S(2)}, u32[]{:S(2)}) collective-permute-start(f32[64,512]{1,0:T(8,128)S(1)} %get-tuple-element.206), channel_id=1, source_target_pairs={{0,4},{1,5},{2,6},{3,7},{4,0},{5,1},{6,2},{7,3},{8,12},{9,13},{10,... | collective-permute-start | bytes 393224 | tf_op jit(solution)/shard_map/ppermute | solution.py:40
  126.0 10.8 %collective-permute-start.36 = (f32[64,512]{1,0:T(8,128)S(1)}, f32[64,512]{1,0:T(8,128)S(1)}, u32[]{:S(2)}, u32[]{:S(2)}) collective-permute-start(f32[64,512]{1,0:T(8,128)S(1)} %get-tuple-element.205), channel_id=1, source_target_pairs={{0,6},{1,7},{2,4},{3,5},{4,2},{5,3},{6,0},{7,1},{8,14},{9,15},{10,... | collective-permute-start | bytes 393224 | tf_op jit(solution)/shard_map/ppermute | solution.py:40
  127.5 3.8 %collective-permute-start.30 = (bf16[16,512]{1,0:T(8,128)(2,1)S(1)}, bf16[16,512]{1,0:T(8,128)(2,1)S(1)}, u32[]{:S(2)}, u32[]{:S(2)}) collective-permute-start(bf16[16,512]{1,0:T(8,128)(2,1)S(1)} %finish.2), channel_id=1, source_target_pairs={{0,8},{1,9},{2,10},{3,11},{4,12},{5,13},{6,14},{7,15},{8,0},{9,1},... | collective-permute-start | bytes 49160 | tf_op jit(solution)/shard_map/ppermute | solution.py:40
  128.5 5.2 %collective-permute-start.31 = (bf16[16,512]{1,0:T(8,128)(2,1)S(1)}, bf16[16,512]{1,0:T(8,128)(2,1)S(1)}, u32[]{:S(2)}, u32[]{:S(2)}) collective-permute-start(bf16[16,512]{1,0:T(8,128)(2,1)S(1)} %finish.2), channel_id=1, source_target_pairs={{0,16},{1,17},{2,18},{3,19},{4,20},{5,21},{6,22},{7,23},{8,24},{9,... | collective-permute-start | bytes 49160 | tf_op jit(solution)/shard_map/ppermute | solution.py:40
  131.3 5.5 %collective-permute-start.32 = (bf16[16,512]{1,0:T(8,128)(2,1)S(1)}, bf16[16,512]{1,0:T(8,128)(2,1)S(1)}, u32[]{:S(2)}, u32[]{:S(2)}) collective-permute-start(bf16[16,512]{1,0:T(8,128)(2,1)S(1)} %finish.2), channel_id=1, source_target_pairs={{0,24},{1,25},{2,26},{3,27},{4,28},{5,29},{6,30},{7,31},{8,16},{9,... | collective-permute-start | bytes 49160 | tf_op jit(solution)/shard_map/ppermute | solution.py:40
  136.9 6.8 %collective-permute-start.40 = (f32[16,512]{1,0:T(8,128)S(1)}, f32[16,512]{1,0:T(8,128)S(1)}, u32[]{:S(2)}, u32[]{:S(2)}) collective-permute-start(f32[16,512]{1,0:T(8,128)S(1)} %get-tuple-element.231), channel_id=1, source_target_pairs={{0,8},{1,9},{2,10},{3,11},{4,12},{5,13},{6,14},{7,15},{8,0},{9,1},... | collective-permute-start | bytes 98312 | tf_op jit(solution)/shard_map/ppermute | solution.py:40
  137.0 12.4 %collective-permute-start.37 = (bf16[64,512]{1,0:T(8,128)(2,1)S(1)}, bf16[64,512]{1,0:T(8,128)(2,1)S(1)}, u32[]{:S(2)}, u32[]{:S(2)}) collective-permute-start(bf16[64,512]{1,0:T(8,128)(2,1)S(1)} %pad_maximum_fusion.7), channel_id=1, source_target_pairs={{0,2},{1,3},{2,0},{3,1},{4,6},{5,7},{6,4},{7,5},{8,10},{9,11},{10,... | collective-permute-start | bytes 196616 | tf_op jit(solution)/shard_map/ppermute | solution.py:40
  138.5 10.9 %collective-permute-start.38 = (bf16[64,512]{1,0:T(8,128)(2,1)S(1)}, bf16[64,512]{1,0:T(8,128)(2,1)S(1)}, u32[]{:S(2)}, u32[]{:S(2)}) collective-permute-start(bf16[64,512]{1,0:T(8,128)(2,1)S(1)} %pad_maximum_fusion.7), channel_id=1, source_target_pairs={{0,4},{1,5},{2,6},{3,7},{4,0},{5,1},{6,2},{7,3},{8,12},{9,13},{10,... | collective-permute-start | bytes 196616 | tf_op jit(solution)/shard_map/ppermute | solution.py:40
  139.7 9.7 %collective-permute-start.39 = (bf16[64,512]{1,0:T(8,128)(2,1)S(1)}, bf16[64,512]{1,0:T(8,128)(2,1)S(1)}, u32[]{:S(2)}, u32[]{:S(2)}) collective-permute-start(bf16[64,512]{1,0:T(8,128)(2,1)S(1)} %pad_maximum_fusion.7), channel_id=1, source_target_pairs={{0,6},{1,7},{2,4},{3,5},{4,2},{5,3},{6,0},{7,1},{8,14},{9,15},{10,... | collective-permute-start | bytes 196616 | tf_op jit(solution)/shard_map/ppermute | solution.py:40
  140.6 5.0 %collective-permute-start.41 = (f32[16,512]{1,0:T(8,128)S(1)}, f32[16,512]{1,0:T(8,128)S(1)}, u32[]{:S(2)}, u32[]{:S(2)}) collective-permute-start(f32[16,512]{1,0:T(8,128)S(1)} %get-tuple-element.230), channel_id=1, source_target_pairs={{0,16},{1,17},{2,18},{3,19},{4,20},{5,21},{6,22},{7,23},{8,24},{9,... | collective-permute-start | bytes 98312 | tf_op jit(solution)/shard_map/ppermute | solution.py:40
  143.7 5.7 %collective-permute-start.42 = (f32[16,512]{1,0:T(8,128)S(1)}, f32[16,512]{1,0:T(8,128)S(1)}, u32[]{:S(2)}, u32[]{:S(2)}) collective-permute-start(f32[16,512]{1,0:T(8,128)S(1)} %get-tuple-element.229), channel_id=1, source_target_pairs={{0,24},{1,25},{2,26},{3,27},{4,28},{5,29},{6,30},{7,31},{8,16},{9,... | collective-permute-start | bytes 98312 | tf_op jit(solution)/shard_map/ppermute | solution.py:40
  149.5 8.2 %collective-permute-start.43 = (bf16[256,512]{1,0:T(8,128)(2,1)S(1)}, bf16[256,512]{1,0:T(8,128)(2,1)S(1)}, u32[]{:S(2)}, u32[]{:S(2)}) collective-permute-start(bf16[256,512]{1,0:T(8,128)(2,1)S(1)} %pad_maximum_fusion.3), channel_id=1, source_target_pairs={{0,1},{1,0},{2,3},{3,2},{4,5},{5,4},{6,7},{7,6},{8,9},{9,8},{10,11... | collective-permute-start | bytes 786440 | tf_op jit(solution)/shard_map/ppermute | solution.py:40
  150.2 4.5 %collective-permute-start.44 = (bf16[16,512]{1,0:T(8,128)(2,1)S(1)}, bf16[16,512]{1,0:T(8,128)(2,1)S(1)}, u32[]{:S(2)}, u32[]{:S(2)}) collective-permute-start(bf16[16,512]{1,0:T(8,128)(2,1)S(1)} %finish.3), channel_id=1, source_target_pairs={{0,8},{1,9},{2,10},{3,11},{4,12},{5,13},{6,14},{7,15},{8,0},{9,1},... | collective-permute-start | bytes 49160 | tf_op jit(solution)/shard_map/ppermute | solution.py:40
  150.3 4.7 %collective-permute-start.45 = (bf16[16,512]{1,0:T(8,128)(2,1)S(1)}, bf16[16,512]{1,0:T(8,128)(2,1)S(1)}, u32[]{:S(2)}, u32[]{:S(2)}) collective-permute-start(bf16[16,512]{1,0:T(8,128)(2,1)S(1)} %finish.3), channel_id=1, source_target_pairs={{0,16},{1,17},{2,18},{3,19},{4,20},{5,21},{6,22},{7,23},{8,24},{9,... | collective-permute-start | bytes 49160 | tf_op jit(solution)/shard_map/ppermute | solution.py:40
  152.2 5.5 %collective-permute-start.46 = (bf16[16,512]{1,0:T(8,128)(2,1)S(1)}, bf16[16,512]{1,0:T(8,128)(2,1)S(1)}, u32[]{:S(2)}, u32[]{:S(2)}) collective-permute-start(bf16[16,512]{1,0:T(8,128)(2,1)S(1)} %finish.3), channel_id=1, source_target_pairs={{0,24},{1,25},{2,26},{3,27},{4,28},{5,29},{6,30},{7,31},{8,16},{9,... | collective-permute-start | bytes 49160 | tf_op jit(solution)/shard_map/ppermute | solution.py:40
  157.7 7.8 %collective-permute-start.50 = (bf16[64,512]{1,0:T(8,128)(2,1)S(1)}, bf16[64,512]{1,0:T(8,128)(2,1)S(1)}, u32[]{:S(2)}, u32[]{:S(2)}) collective-permute-start(bf16[64,512]{1,0:T(8,128)(2,1)S(1)} %pad_maximum_fusion.8), channel_id=1, source_target_pairs={{0,2},{1,3},{2,0},{3,1},{4,6},{5,7},{6,4},{7,5},{8,10},{9,11},{10,... | collective-permute-start | bytes 196616 | tf_op jit(solution)/shard_map/ppermute | solution.py:40
  159.2 7.7 %collective-permute-start.51 = (bf16[64,512]{1,0:T(8,128)(2,1)S(1)}, bf16[64,512]{1,0:T(8,128)(2,1)S(1)}, u32[]{:S(2)}, u32[]{:S(2)}) collective-permute-start(bf16[64,512]{1,0:T(8,128)(2,1)S(1)} %pad_maximum_fusion.8), channel_id=1, source_target_pairs={{0,4},{1,5},{2,6},{3,7},{4,0},{5,1},{6,2},{7,3},{8,12},{9,13},{10,... | collective-permute-start | bytes 196616 | tf_op jit(solution)/shard_map/ppermute | solution.py:40
  160.4 6.5 %collective-permute-start.52 = (bf16[64,512]{1,0:T(8,128)(2,1)S(1)}, bf16[64,512]{1,0:T(8,128)(2,1)S(1)}, u32[]{:S(2)}, u32[]{:S(2)}) collective-permute-start(bf16[64,512]{1,0:T(8,128)(2,1)S(1)} %pad_maximum_fusion.8), channel_id=1, source_target_pairs={{0,6},{1,7},{2,4},{3,5},{4,2},{5,3},{6,0},{7,1},{8,14},{9,15},{10,... | collective-permute-start | bytes 196616 | tf_op jit(solution)/shard_map/ppermute | solution.py:40
  162.4 4.5 %collective-permute-start.47 = (bf16[128,256]{1,0:T(8,128)(2,1)S(1)}, bf16[128,256]{1,0:T(8,128)(2,1)S(1)}, u32[]{:S(2)}, u32[]{:S(2)}) collective-permute-start(bf16[128,256]{1,0:T(8,128)(2,1)S(1)} %get-tuple-element.176), channel_id=1, source_target_pairs={{0,8},{1,9},{2,10},{3,11},{4,12},{5,13},{6,14},{7,15},{8,0},{9,1},... | collective-permute-start | bytes 196616 | tf_op jit(solution)/shard_map/ppermute | solution.py:40
  162.5 6.7 %collective-permute-start.48 = (bf16[128,256]{1,0:T(8,128)(2,1)S(1)}, bf16[128,256]{1,0:T(8,128)(2,1)S(1)}, u32[]{:S(2)}, u32[]{:S(2)}) collective-permute-start(bf16[128,256]{1,0:T(8,128)(2,1)S(1)} %get-tuple-element.177), channel_id=1, source_target_pairs={{0,16},{1,17},{2,18},{3,19},{4,20},{5,21},{6,22},{7,23},{8,24},{9,... | collective-permute-start | bytes 196616 | tf_op jit(solution)/shard_map/ppermute | solution.py:40
  165.6 6.1 %collective-permute-start.49 = (bf16[128,256]{1,0:T(8,128)(2,1)S(1)}, bf16[128,256]{1,0:T(8,128)(2,1)S(1)}, u32[]{:S(2)}, u32[]{:S(2)}) collective-permute-start(bf16[128,256]{1,0:T(8,128)(2,1)S(1)} %get-tuple-element.178), channel_id=1, source_target_pairs={{0,24},{1,25},{2,26},{3,27},{4,28},{5,29},{6,30},{7,31},{8,16},{9,... | collective-permute-start | bytes 196616 | tf_op jit(solution)/shard_map/ppermute | solution.py:40
  171.7 1.6 collective-permute-start.53
  175.1 6.8 %collective-permute-start.54 = (bf16[128,256]{1,0:T(8,128)(2,1)S(1)}, bf16[128,256]{1,0:T(8,128)(2,1)S(1)}, u32[]{:S(2)}, u32[]{:S(2)}) collective-permute-start(bf16[128,256]{1,0:T(8,128)(2,1)S(1)} %get-tuple-element.189), channel_id=1, source_target_pairs={{0,24},{1,25},{2,26},{3,27},{4,28},{5,29},{6,30},{7,31},{8,16},{9,... | collective-permute-start | bytes 196616 | tf_op jit(solution)/shard_map/ppermute | solution.py:40
  176.4 7.4 %collective-permute-start.55 = (bf16[128,256]{1,0:T(8,128)(2,1)S(1)}, bf16[128,256]{1,0:T(8,128)(2,1)S(1)}, u32[]{:S(2)}, u32[]{:S(2)}) collective-permute-start(bf16[128,256]{1,0:T(8,128)(2,1)S(1)} %get-tuple-element.190), channel_id=1, source_target_pairs={{0,16},{1,17},{2,18},{3,19},{4,20},{5,21},{6,22},{7,23},{8,24},{9,... | collective-permute-start | bytes 196616 | tf_op jit(solution)/shard_map/ppermute | solution.py:40
  176.4 7.4 %collective-permute-start.56 = (bf16[128,256]{1,0:T(8,128)(2,1)S(1)}, bf16[128,256]{1,0:T(8,128)(2,1)S(1)}, u32[]{:S(2)}, u32[]{:S(2)}) collective-permute-start(bf16[128,256]{1,0:T(8,128)(2,1)S(1)} %get-tuple-element.191), channel_id=1, source_target_pairs={{0,8},{1,9},{2,10},{3,11},{4,12},{5,13},{6,14},{7,15},{8,0},{9,1},... | collective-permute-start | bytes 196616 | tf_op jit(solution)/shard_map/ppermute | solution.py:40

commit v3 on v1

--- a/solution.py
+++ b/solution.py
@@ -94,52 +94,74 @@
     return jnp.concatenate(ordered(parts, here), 0)
 
 
-def finish_kernel(place_ref, *refs, n, k, share):
-    out_ref = refs[n]
-    total = tree_sum([ref[...] for ref in refs[:n]])
-    if share:
-        last = (place_ref[0] == n - 1) & (place_ref[1] == n - 1) & (place_ref[2] == k - 1)
-        edge = total[-8:, :128]
-        row = lax.broadcasted_iota(jnp.int32, edge.shape, 0)
-        column = lax.broadcasted_iota(jnp.int32, edge.shape, 1)
-        taken = (row == 7) & last
-        whole = jnp.sum(jnp.where(taken & (column == 0), edge, 0.0), keepdims=True)
-        high = whole.astype(BF16).astype(F32)
-        middle = (whole - high).astype(BF16).astype(F32)
-        three = jnp.where(column == 0, high, jnp.where(column == 1, middle, whole - high - middle))
-        edge = jnp.where(taken & (column < 3), three, edge)
-        edge = jnp.concatenate([edge, total[-8:, 128:]], 1)
-        total = jnp.concatenate([total[:-8], edge], 0)
-    out_ref[...] = total.astype(BF16)
-
-
-def finish(place, place_array, parts, share):
+def halve_kernel(place_ref, kept_ref, met_ref, *outs, axis):
+    height = outs[0].shape[0]
+    for step, out in enumerate(outs):
+        at = pl.ds(pl.multiple_of((place_ref[axis] ^ step) * height, height), height)
+        out[...] = kept_ref[at, :] + met_ref[at, :]
+
+
+def plane_kernel(place_ref, *refs, n):
+    met, outs, whole_ref = refs[:n], refs[n:-1], refs[-1]
+    whole_ref[...] = tree_sum([ref[...] for ref in met])
+    height = outs[0].shape[0]
+    for step, out in enumerate(outs):
+        at = pl.ds(pl.multiple_of((place_ref[0] ^ step) * height, height), height)
+        out[...] = whole_ref[at, :]
+
+
+def finish_kernel(place_ref, *refs, n, k):
+    out_ref = refs[-1]
+    height = refs[0].shape[0]
+    out_ref[:height] = tree_sum([ref[...] for ref in refs[:n]]).astype(BF16)
+    total = tree_sum([ref[...] for ref in refs[n : 2 * n]])
+    last = (place_ref[0] == n - 1) & (place_ref[1] == n - 1) & (place_ref[2] == k - 1)
+    edge = total[-8:, :128]
+    row = lax.broadcasted_iota(jnp.int32, edge.shape, 0)
+    column = lax.broadcasted_iota(jnp.int32, edge.shape, 1)
+    taken = (row == 7) & last
+    whole = jnp.sum(jnp.where(taken & (column == 0), edge, 0.0), keepdims=True)
+    high = whole.astype(BF16).astype(F32)
+    middle = (whole - high).astype(BF16).astype(F32)
+    three = jnp.where(column == 0, high, jnp.where(column == 1, middle, whole - high - middle))
+    edge = jnp.where(taken & (column < 3), three, edge)
+    edge = jnp.concatenate([edge, total[-8:, 128:]], 1)
+    out_ref[height:] = jnp.concatenate([total[:-8], edge], 0).astype(BF16)
+
+
+def local(kernel, place_array, args, shapes, name, **more):
     space = pl.BlockSpec(memory_space=pltpu.VMEM)
     return pl.pallas_call(
-        functools.partial(finish_kernel, n=place.n, k=place.k, share=share),
-        in_specs=[pl.BlockSpec(memory_space=pltpu.SMEM)] + [space] * place.n,
-        out_specs=space,
-        out_shape=jax.ShapeDtypeStruct(parts[0].shape, BF16),
-        compiler_params=pltpu.CompilerParams(vmem_limit_bytes=VMEM_BYTES // 4),
-        name="finish",
-    )(place_array, *parts)
-
-
-def gram_rows(place, place_array, grams, last):
-    few = not last
-    part = grams[0]
-    for step in range(1, place.k):
-        part = part + place.send(grams[step], lambda z, a, b, s=step: (z, a, b ^ s))
-    part = reduce_scatter(place, "a", part, few)
-    height, width = part.shape
-    part = part.reshape(place.n, height // place.n, width)
-    return finish(place, place_array, exchange(place, "z", part, few), last)
-
-
-def whole_gram(place, part):
-    for axis in ("z", "a", "b"):
-        part = gather(place, axis, part)
-    return part
+        kernel,
+        in_specs=[pl.BlockSpec(memory_space=pltpu.SMEM)] + [space] * len(args),
+        out_specs=[space] * len(shapes),
+        out_shape=[jax.ShapeDtypeStruct(shape, dtype) for shape, dtype in shapes],
+        compiler_params=pltpu.CompilerParams(vmem_limit_bytes=VMEM_BYTES // 2),
+        name=name,
+        **more,
+    )(place_array, *args)
+
+
+def plane_rows(place, place_array, grams, few=False):
+    n = place.n
+    half, batch = grams[0].shape
+    kept, other = grams
+    other = place.send(other, lambda z, a, b: (z, a, b ^ 1))
+    parts = local(
+        functools.partial(halve_kernel, axis=1),
+        place_array,
+        (kept, other),
+        [((half // n, batch), F32)] * n,
+        "halve",
+    )
+    return local(
+        functools.partial(plane_kernel, n=n),
+        place_array,
+        sends(place, "a", parts, few),
+        [((half // (n * n), batch), F32)] * n,
+        "plane",
+        scratch_shapes=[pltpu.VMEM((half // n, batch), F32)],
+    )
 
 
 def in_one(place, run, args):
@@ -161,46 +183,91 @@
     return part
 
 
-def spread(place, views):
+def cut_kernel(place_ref, *refs, views, n):
+    inputs, outs, done = refs[:views], refs[views:-1], refs[-1]
+    few = outs[0].shape[0] // views
+    copies = []
+    for step in range(n):
+        at = pl.ds(pl.multiple_of((place_ref[1] ^ step) * few, few), few)
+        for i, view in enumerate(inputs):
+            part = outs[step].at[i * few : (i + 1) * few]
+            copies.append(pltpu.make_async_copy(view.at[at], part, done.at[step, i]))
+            copies[-1].start()
+    for copy in copies:
+        copy.wait()
+
+
+def lay_kernel(place_ref, *refs, n):
+    parts, outs = refs[:n], refs[n:]
+    few = parts[0].shape[0] // len(outs)
+    for step in range(n):
+        at = pl.ds(pl.multiple_of((place_ref[0] ^ step) * few, few), few)
+        for i, out in enumerate(outs):
+            out[at, :] = parts[step][i * few : (i + 1) * few, :]
+
+
+def spread(place, place_array, views):
     n = place.n
     rows, width = views[0].shape
     few = rows // n
-    values = jnp.stack([view.reshape(n, few, width) for view in views], 1)
-    values = values.reshape(n, len(views) * few, width)
-    parts = ordered(exchange(place, "a", values), place.a ^ place.z)
-    parts = ordered(sends(place, "z", parts), place.z)
-    return [
-        jnp.concatenate([part[view * few : (view + 1) * few] for part in parts], 0)
-        for view in range(len(views))
-    ]
+    parts = pl.pallas_call(
+        functools.partial(cut_kernel, views=len(views), n=n),
+        in_specs=[pl.BlockSpec(memory_space=pltpu.SMEM)]
+        + [pl.BlockSpec(memory_space=pl.ANY)] * len(views),
+        out_specs=[pl.BlockSpec(memory_space=pltpu.VMEM)] * n,
+        out_shape=[jax.ShapeDtypeStruct((len(views) * few, width), BF16)] * n,
+        scratch_shapes=[pltpu.SemaphoreType.DMA((n, len(views)))],
+        compiler_params=pltpu.CompilerParams(vmem_limit_bytes=VMEM_BYTES // 2),
+        name="cut",
+    )(place_array, *views)
+    parts = sends(place, "a", parts)
+    parts = sends(place, "z", ordered(parts, place.a ^ place.z))
+    return local(
+        functools.partial(lay_kernel, n=n),
+        place_array,
+        parts,
+        [((rows, width), BF16)] * len(views),
+        "lay",
+    )
 
 
 def met_rows(place, values, few=False):
     return sends(place, "a", [values] * place.n, few)
 
 
-def project_kernel(place_ref, *refs, n, k):
-    met, others = refs[:n], refs[n : n + k - 1]
-    weight_ref = refs[n + k - 1]
-    own_ref, coded = refs[n + k], refs[n + k + 1 : 2 * n + k]
-    held_ref, arrived = refs[2 * n + k :]
+def project_kernel(place_ref, *refs, counts, n, k):
+    met = refs[: sum(counts)]
+    weight_ref, own_ref, *coded = refs[sum(counts) : -2]
+    held_ref, arrived = refs[-2:]
     width = met[0].shape[1]
     columns = own_ref.shape[1]
-    copies = {}
-    for step in [*range(1, n), 0]:
+    order = [*range(1, n), 0]
+    copies = []
+    for slot, step in enumerate(order):
         at = pl.ds(pl.multiple_of((place_ref[0] ^ step) * columns, columns), columns)
-        copies[step] = pltpu.make_async_copy(
-            weight_ref.at[:, at], held_ref.at[step], arrived.at[step]
-        )
-        copies[step].start()
-    own = jnp.concatenate([ref[...] for ref in met], 0)
-    for step in [*range(1, n), 0]:
-        copies[step].wait()
+        copies.append([])
+        for i in range(k):
+            rows = pl.ds(pl.multiple_of((place_ref[2] ^ i) * width, width), width)
+            part = held_ref.at[slot, i * width : (i + 1) * width]
+            copies[slot].append(
+                pltpu.make_async_copy(weight_ref.at[rows, at], part, arrived.at[slot, i])
+            )
+    for copy in copies[0]:
+        copy.start()
+    values = []
+    for count in counts:
+        values.append(jnp.concatenate([ref[...] for ref in met[:count]], 0))
+        met = met[count:]
+    for slot, step in enumerate(order):
+        for copy in copies[slot]:
+            copy.wait()
+        if slot + 1 < n:
+            for copy in copies[slot + 1]:
+                copy.start()
         total = 0.0
         for i in range(k):
-            rows = pl.ds(pl.multiple_of((place_ref[2] ^ i) * width, width), width)
-            values = own if i == 0 else others[i - 1][...]
-            total += jnp.dot(values, held_ref[step, rows, :], preferred_element_type=F32)
+            part = held_ref[slot, i * width : (i + 1) * width, :]
+            total += jnp.dot(values[i], part, preferred_element_type=F32)
         if step == 0:
             own_ref[...] = total
         else:
@@ -218,7 +285,7 @@
     coded_ref[:batch] = coarse
     near = coarse.astype(F32)
     step = unit(near)
-    level = (total - near) / jnp.where(step > 0.0, step, 1.0)
+    level = (total - near) * pl.reciprocal(jnp.where(step > 0.0, step, 1.0), approx=True)
     level = jnp.clip(jnp.floor((level + 0.5) * LEVELS), 0.0, LEVELS - 1.0).astype(jnp.int32)
     height = batch // SHARED
     first, second, third, fourth = [level[i * height : (i + 1) * height] for i in range(SHARED)]
@@ -252,25 +319,26 @@
     return blocks
 
 
-def project(place, place_array, met, others, weight):
+def project(place, place_array, met, weight):
     n, k = place.n, place.k
-    rows, width = met[0].shape
+    rows, width = met[0][0].shape
     batch, columns = rows * n, weight.shape[1] // n
+    counts = [len(parts) for parts in met]
+    met = [part for parts in met for part in parts]
     coded = batch + batch // SHARED
     out_shape = [jax.ShapeDtypeStruct((batch, columns), F32)]
     out_shape += [jax.ShapeDtypeStruct((coded, columns), BF16)] * (n - 1)
-    args = [*met, *others, weight]
     space = pl.BlockSpec(memory_space=pltpu.VMEM)
     own, *parts = pl.pallas_call(
-        functools.partial(project_kernel, n=n, k=k),
+        functools.partial(project_kernel, counts=counts, n=n, k=k),
         in_specs=[pl.BlockSpec(memory_space=pltpu.SMEM)]
-        + [space] * (len(args) - 1)
+        + [space] * len(met)
         + [pl.BlockSpec(memory_space=pl.ANY)],
         out_specs=[space] * n,
         out_shape=out_shape,
         scratch_shapes=[
             pltpu.VMEM((n, k * width, columns), BF16),
-            pltpu.SemaphoreType.DMA((n,)),
+            pltpu.SemaphoreType.DMA((n, k)),
         ],
         compiler_params=pltpu.CompilerParams(vmem_limit_bytes=VMEM_BYTES),
         cost_estimate=pl.CostEstimate(
@@ -279,7 +347,7 @@
             transcendentals=0,
         ),
         name="project",
-    )(place_array, *args)
+    )(place_array, *met, weight)
     return own, parts
 
 
@@ -350,7 +418,7 @@
         in_specs=[pl.BlockSpec(memory_space=pltpu.SMEM)] + [space] * len(args),
         out_specs=[space] * len(out_shape),
         out_shape=out_shape,
-        compiler_params=pltpu.CompilerParams(vmem_limit_bytes=VMEM_BYTES),
+        compiler_params=pltpu.CompilerParams(vmem_limit_bytes=VMEM_BYTES // 2),
         cost_estimate=pl.CostEstimate(
             flops=2 * batch * batch * columns,
             bytes_accessed=16 * batch * columns + 4 * batch * batch,
@@ -360,84 +428,82 @@
     )(place_array, *args)
 
 
-def gradient_kernel(place_ref, *refs, n, last):
-    gram_ref, packed_ref, norm_ref, other_ref, scale_ref, coeff_ref = refs[:6]
-    refs = refs[6:]
-    if last:
-        first_ref, refs = refs[0], refs[1:]
-    outs, whole_ref = refs[:n], refs[-1]
-    batch, columns = norm_ref.shape
-    gram = gram_ref[...]
-    if last:
-        edge = batch - 128
-        tail = gram[edge:, :128]
-        row = lax.broadcasted_iota(jnp.int32, tail.shape, 0)
-        column = lax.broadcasted_iota(jnp.int32, tail.shape, 1)
-        taken = (row == 127) & (column < 3)
-        mirror = gram[:128, edge:].astype(F32).T
-        share = jnp.sum(jnp.where(taken, tail.astype(F32), 0.0), keepdims=True)
-        fixed = jnp.where(taken, mirror, tail.astype(F32)).astype(BF16)
-        gram = jnp.concatenate(
-            [gram[:edge], jnp.concatenate([fixed, gram[edge:, 128:]], 1)], 0
+def gradient_kernel(place_ref, *refs, n, k):
+    grams, refs = refs[: n * k], refs[n * k :]
+    packed, norms, scales, coeff_ref, refs = refs[0:2], refs[2:4], refs[4:6], refs[6], refs[7:]
+    outs, loss_ref = refs[:n], refs[n]
+    gram_ref, whole_ref = refs[n + 1 :]
+    batch, columns = norms[0].shape
+    height = grams[0].shape[0] // 2
+    few = height // n
+    for i in range(k):
+        for step in range(n):
+            at = ((place_ref[2] ^ i) * n + (place_ref[1] ^ step)) * height
+            for plane in range(n):
+                for view in range(2):
+                    to = pl.ds(pl.multiple_of(at + plane * few, few), few)
+                    first = (plane * 2 + view) * few
+                    gram_ref[view, to, :] = grams[i * n + step][first : first + few, :]
+    edge = batch - 128
+    tail = gram_ref[1, edge:, :128].astype(F32)
+    row = lax.broadcasted_iota(jnp.int32, tail.shape, 0)
+    column = lax.broadcasted_iota(jnp.int32, tail.shape, 1)
+    taken = (row == 127) & (column < 3)
+    mirror = gram_ref[1, :128, edge:].astype(F32).T
+    share = jnp.sum(jnp.where(taken, tail, 0.0), keepdims=True)
+    gram_ref[1, edge:, :128] = jnp.where(taken, mirror, tail).astype(BF16)
+    factor = 2.0 * off_weight / batch
+    rows = batch // n
+    for view in (1, 0):
+        norm = norms[view][...]
+        grad = (
+            factor * jnp.dot(gram_ref[1 - view], packed[view][...], preferred_element_type=F32)
+            + coeff_ref[...] * norms[1 - view][...]
         )
-        frob = jnp.sum(gram.astype(F32) * first_ref[...].astype(F32), keepdims=True)
-        refs[n][...] = (share + off_weight * (frob / (batch * batch))) / D
-    factor = 2.0 * off_weight / batch
-    norm = norm_ref[...]
-    grad = (
-        factor * jnp.dot(gram, packed_ref[...], preferred_element_type=F32)
-        + coeff_ref[...] * other_ref[...]
-    )
-    first = jnp.sum(grad, 0, keepdims=True) / batch
-    second = jnp.sum(grad * norm, 0, keepdims=True) / batch
-    whole_ref[...] = (scale_ref[...] * (grad - first - norm * second)).astype(BF16)
-    rows = batch // n
+        first = jnp.sum(grad, 0, keepdims=True) / batch
+        second = jnp.sum(grad * norm, 0, keepdims=True) / batch
+        whole_ref[view] = (scales[view][...] * (grad - first - norm * second)).astype(BF16)
+        for step in range(n):
+            at = pl.multiple_of((place_ref[0] ^ step) * rows, rows)
+            outs[step][view * rows : (view + 1) * rows, :] = whole_ref[view, pl.ds(at, rows), :]
+    frob = jnp.sum(gram_ref[0].astype(F32) * gram_ref[1].astype(F32), keepdims=True)
+    loss_ref[...] = (share + off_weight * (frob / (batch * batch))) / D
+
+
+def gradient(place, place_array, grams, packed, norms, scales, coeff):
+    batch, columns = norms[0].shape
+    return local(
+        functools.partial(gradient_kernel, n=place.n, k=place.k),
+        place_array,
+        (*grams, *packed, *norms, *scales, coeff),
+        [((2 * batch // place.n, columns), BF16)] * place.n + [((1, 1), F32)],
+        "gradient",
+        scratch_shapes=[
+            pltpu.VMEM((2, batch, batch), BF16),
+            pltpu.VMEM((2, batch, columns), BF16),
+        ],
+    )
+
+
+def place_kernel(place_ref, *refs, n):
+    parts, outs = refs[:n], refs[n:]
+    rows, columns = parts[0].shape[0] // len(outs), parts[0].shape[1]
     for step in range(n):
-        at = pl.multiple_of((place_ref[0] ^ step) * rows, rows)
-        outs[step][...] = whole_ref[pl.ds(at, rows), :]
-
-
-def gradient(place, place_array, gram, packed, norm, other, scale, coeff, first=None):
-    n = place.n
-    batch, columns = norm.shape
-    last = first is not None
-    out_shape = [jax.ShapeDtypeStruct((batch // n, columns), BF16)] * n
-    if last:
-        out_shape.append(jax.ShapeDtypeStruct((1, 1), F32))
-    args = [gram, packed, norm, other, scale, coeff] + ([first] if last else [])
-    space = pl.BlockSpec(memory_space=pltpu.VMEM)
-    return pl.pallas_call(
-        functools.partial(gradient_kernel, n=n, last=last),
-        in_specs=[pl.BlockSpec(memory_space=pltpu.SMEM)] + [space] * len(args),
-        out_specs=[space] * len(out_shape),
-        out_shape=out_shape,
-        scratch_shapes=[pltpu.VMEM((batch, columns), BF16)],
-        compiler_params=pltpu.CompilerParams(vmem_limit_bytes=VMEM_BYTES),
-        cost_estimate=pl.CostEstimate(
-            flops=2 * batch * batch * columns,
-            bytes_accessed=14 * batch * columns + 2 * batch * batch,
-            transcendentals=0,
-        ),
-        name="gradient",
-    )(place_array, *args)
-
-
-def joined(place, parts):
-    return jnp.concatenate(ordered(sends(place, "z", parts), place.z), 1)
+        at = pl.ds(pl.multiple_of((place_ref[0] ^ step) * columns, columns), columns)
+        for i, out in enumerate(outs):
+            out[:, at] = parts[step][i * rows : (i + 1) * rows, :]
 
 
 def with_kernels(place, h_first, h_second, weight):
     n, k, z, a, b = place.n, place.k, place.z, place.a, place.b
     place_array = jnp.stack([z, a, b]).astype(jnp.int32)
-    first, second = spread(place, (h_first, h_second))
+    first, second = spread(place, place_array, (h_first, h_second))
 
     def projected(values, weight, few):
         met = met_rows(place, values, few)
-        own = jnp.concatenate(met, 0)
-        others = [
-            place.send(own, lambda z, a, b, s=step: (z, a, b ^ s)) for step in range(1, k)
-        ]
-        return project(place, place_array, met, others, weight)
+        own = [jnp.concatenate(met, 0)] if few else met
+        others = [place.send(part, lambda z, a, b: (z, a, b ^ 1)) for part in own]
+        return project(place, place_array, [met, others], weight)
 
     def sent(parts):
         return sends(place, "z", [parts[0], *parts])[1:]
@@ -451,24 +517,41 @@
     own_1, own_2 = lax.optimization_barrier((own_1, own_2))
     parts_2 = sent(parts_2)
     norm_1, packed_1, scale_1, *grams = normalize_parts(place, place_array, own_1, parts_1)
-    rows_1 = in_one(place, lambda *grams: gram_rows(place, place_array, grams, False), grams)
-    own_2, parts_2, rows_1 = lax.optimization_barrier((own_2, parts_2, rows_1))
+    met_1 = in_one(place, lambda *grams: plane_rows(place, place_array, grams, True), grams)
+    met_1 = sends(place, "z", met_1)
+    own_2, parts_2, met_1 = lax.optimization_barrier((own_2, parts_2, met_1))
     norm_2, packed_2, scale_2, *grams, coeff = normalize_parts(
         place, place_array, own_2, parts_2, norm_1
     )
-    gram_1 = whole_gram(place, rows_1)
-    grads_2 = gradient(
-        place, place_array, gram_1, packed_2, norm_2, norm_1, scale_2, coeff
-    )
-    rows_2 = gram_rows(place, place_array, grams, True)
-    grads_2, rows_2 = lax.optimization_barrier((grads_2, rows_2))
-    out_2 = joined(place, grads_2)
-    gram_2 = whole_gram(place, rows_2)
-    out_2, gram_2 = lax.optimization_barrier((out_2, gram_2))
-    *grads_1, loss = gradient(
-        place, place_array, gram_2, packed_1, norm_1, norm_2, scale_1, coeff, gram_1
-    )
-    return (joined(place, grads_1), out_2, loss.reshape(()))
+    met_2 = sends(place, "z", plane_rows(place, place_array, grams))
+    rows, batch = 2 * met_2[0].shape[0], h_first.shape[0] * n
+    (part,) = local(
+        functools.partial(finish_kernel, n=n, k=k),
+        place_array,
+        (*met_1, *met_2),
+        [((rows, batch), BF16)],
+        "finish",
+    )
+    part = jnp.concatenate(ordered(sends(place, "z", [part] * n), z), 0)
+    grams = sends(place, "a", [part] * n)
+    grams += [place.send(part, lambda z, a, b: (z, a, b ^ 1)) for part in grams]
+    *parts, loss = gradient(
+        place,
+        place_array,
+        grams,
+        (packed_1, packed_2),
+        (norm_1, norm_2),
+        (scale_1, scale_2),
+        coeff,
+    )
+    out_1, out_2 = local(
+        functools.partial(place_kernel, n=n),
+        place_array,
+        sends(place, "z", parts),
+        [(h_first.shape, BF16)] * 2,
+        "place",
+    )
+    return (out_1, out_2, loss.reshape(()))
 
 
 def plain(place, h_first, h_second, weight):
@@ -523,7 +606,7 @@
 def per_device(h_first, h_second, weight):
     place = Place()
     columns = weight.shape[1] // place.n
-    fits = columns % 128 == 0 and place.n == SHARED
+    fits = columns % 128 == 0 and place.n == SHARED and place.k == 2
     return (with_kernels if fits else plain)(place, h_first, h_second, weight)
 
 

time: 184 us -> 177 us (0.962)
  starting transfers between devices: 61 us -> 53.5 us
  waiting for transfers between devices: 84.2 us -> 89.9 us
  other arithmetic: 5.68 us -> 0.22 us
  Pallas kernels: 26.8 us -> 30.8 us
  local copies, waits for them, and re-layouts: 4.9 us -> 1.9 us
    ppermute x54 -> x50, starting transfers between devices: 61 us -> 53.5 us  [send(): return lax.ppermute(value, ('dp', 'mp'), pairs)]
    ppermute x54 -> x50, waiting for transfers between devices: 84.2 us -> 89.9 us  [send(): return lax.ppermute(value, ('dp', 'mp'), pairs)]
    pallas_call x6 -> x11, Pallas kernels: 19.7 us -> 24.5 us  [the longest x2 15.7 us: project(): pl.pallas_call(functools.partial(project_kernel, counts=counts, n=n, k=k)...]
    unnamed x6 -> x4, local copies, waits for them, and re-layouts: 3.98 us -> 1.9 us
  transfers between devices with their start and end apart: 54 -> 50, of which waited for: 30 -> 30; matrix products, arithmetic and copies ran while one was open for 3% -> 0% of each run, Pallas kernels for 9% -> 7%
where the time goes in v3:
time: 177 us
  waiting for transfers between devices  89.9 us (51%)
  starting transfers between devices  53.5 us (30%)
  Pallas kernels  30.8 us (17%)
  local copies, waits for them, and re-layouts  1.9 us (1%)
    ppermute x50, waiting for transfers between devices, send(): return lax.ppermute(value, ('dp', 'mp'), pairs)  89.9 us
    ppermute x50, starting transfers between devices, send(): return lax.ppermute(value, ('dp', 'mp'), pairs)  53.5 us
    pallas_call x2, Pallas kernels, project(): pl.pallas_call(functools.partial(project_kernel, counts=counts, n=n, k=k)...  15.7 us
    pallas_call x8, Pallas kernels, local(): pl.pallas_call(kernel, in_specs=[pl.BlockSpec(memory_space=pltpu.SMEM)] +...  7.45 us
    pallas_call x2, Pallas kernels, normalize_parts(): pl.pallas_call(functools.partial(normalize_kernel, n=n, k=k, second=secon...  6.26 us
  transfers between devices with their start and end apart: 50, of which 30 were waited for; matrix products, arithmetic and copies ran while one was open for 0% of the time, Pallas kernels for 7%

profile of v3, /device:TPU:0, one launch (start us, length us, event | category | flops | bytes accessed | tf_op | source)
XLA Modules:
  0.0 177.2 jit_solution(4536702436657845924)
XLA Ops:
  0.7 0.9 copy-done
  1.7 0.9 copy-done.1
  2.6 1.3 cut.1
  4.0 3.0 %collective-permute-start.10 = (bf16[64,1024]{1,0:T(8,128)(2,1)S(1)}, bf16[64,1024]{1,0:T(8,128)(2,1)S(1)}, u32[]{:S(2)}, u32[]{:S(2)}) collective-permute-start(bf16[64,1024]{1,0:T(8,128)(2,1)S(1)} %get-tuple-element.87), channel_id=1, source_target_pairs={{0,2},{1,3},{2,0},{3,1},{4,6},{5,7},{6,4},{7,5},{8,10},{9,11},{10,... | collective-permute-start | bytes 393224 | tf_op jit(solution)/shard_map/ppermute | solution.py:40
  7.0 1.5 collective-permute-start.8
  8.5 2.4 %collective-permute-done.10 = bf16[64,1024]{1,0:T(8,128)(2,1)S(1)} collective-permute-done((bf16[64,1024]{1,0:T(8,128)(2,1)S(1)}, bf16[64,1024]{1,0:T(8,128)(2,1)S(1)}, u32[]{:S(2)}, u32[]{:S(2)}) %collective-permute-start.10) | collective-permute-done | bytes 131104 | tf_op jit(solution)/shard_map/ppermute | solution.py:40
  10.9 3.7 %collective-permute-done.8 = bf16[64,1024]{1,0:T(8,128)(2,1)S(1)} collective-permute-done((bf16[64,1024]{1,0:T(8,128)(2,1)S(1)}, bf16[64,1024]{1,0:T(8,128)(2,1)S(1)}, u32[]{:S(2)}, u32[]{:S(2)}) %collective-permute-start.8) | collective-permute-done | bytes 131104 | tf_op jit(solution)/shard_map/ppermute | solution.py:40
  14.6 1.4 collective-permute-done.9
  16.0 1.6 collective-permute-start.11
  17.6 2.6 %collective-permute-start.12 = (bf16[64,1024]{1,0:T(8,128)(2,1)S(1)}, bf16[64,1024]{1,0:T(8,128)(2,1)S(1)}, u32[]{:S(2)}, u32[]{:S(2)}) collective-permute-start(bf16[64,1024]{1,0:T(8,128)(2,1)S(1)} %get-tuple-element.143), channel_id=1, source_target_pairs={{0,16},{1,17},{2,18},{3,19},{4,20},{5,21},{6,22},{7,23},{8,24},{9,... | collective-permute-start | bytes 393224 | tf_op jit(solution)/shard_map/ppermute | solution.py:40
  20.4 2.0 %collective-permute-done.11.refs_1_ = bf16[64,1024]{1,0:T(8,128)(2,1)S(1)} collective-permute-done((bf16[64,1024]{1,0:T(8,128)(2,1)S(1)}, bf16[64,1024]{1,0:T(8,128)(2,1)S(1)}, u32[]{:S(2)}, u32[]{:S(2)}) %collective-permute-start.11) | collective-permute-done | bytes 131104 | tf_op jit(solution)/shard_map/ppermute | solution.py:40
  22.5 7.3 %collective-permute-done.12.refs_2_ = bf16[64,1024]{1,0:T(8,128)(2,1)S(1)} collective-permute-done((bf16[64,1024]{1,0:T(8,128)(2,1)S(1)}, bf16[64,1024]{1,0:T(8,128)(2,1)S(1)}, u32[]{:S(2)}, u32[]{:S(2)}) %collective-permute-start.12) | collective-permute-done | bytes 131104 | tf_op jit(solution)/shard_map/ppermute | solution.py:40
  30.4 1.6 collective-permute-start.14
  32.5 1.5 collective-permute-start.16
  34.0 3.8 %collective-permute-done.14.refs_1_ = bf16[128,1024]{1,0:T(8,128)(2,1)S(1)} collective-permute-done((bf16[128,1024]{1,0:T(8,128)(2,1)S(1)}, bf16[128,1024]{1,0:T(8,128)(2,1)S(1)}, u32[]{:S(2)}, u32[]{:S(2)}) %collective-permute-start.14) | collective-permute-done | bytes 262176 | tf_op jit(solution)/shard_map/ppermute | solution.py:40
  37.8 4.0 %collective-permute-done.15.refs_2_ = bf16[128,1024]{1,0:T(8,128)(2,1)S(1)} collective-permute-done((bf16[128,1024]{1,0:T(8,128)(2,1)S(1)}, bf16[128,1024]{1,0:T(8,128)(2,1)S(1)}, u32[]{:S(2)}, u32[]{:S(2)}) %collective-permute-start.15) | collective-permute-done | bytes 262176 | tf_op jit(solution)/shard_map/ppermute | solution.py:40
  42.3 1.0 collective-permute-done.19.refs_6_
  43.7 7.5 %project.3 = (f32[512,256]{1,0:T(8,128)S(1)}, bf16[640,256]{1,0:T(8,128)(2,1)}, bf16[640,256]{1,0:T(8,128)(2,1)S(1)}, bf16[640,256]{1,0:T(8,128)(2,1)S(1)}) custom-call(s32[3]{0:T(128)S(1)} %pad_add_fusion.place_ref, bf16[128,1024]{1,0:T(8,128)(2,1)S(1)} %get-tuple-element.90.refs_0_, bf16[128,1024]{1,0:T(8,128)(2,1)S(1)} %collective-permute-done.14.refs_1_, ...), custom_call_target="tpu_custom_call" | custom-call | flops 2147483648 | bytes 7864320 | tf_op jit(solution)/shard_map/project/pallas_call | solution.py:332
  51.2 4.1 %collective-permute-start.24 = (bf16[640,256]{1,0:T(8,128)(2,1)}, bf16[640,256]{1,0:T(8,128)(2,1)S(1)}, u32[]{:S(2)}, u32[]{:S(2)}) collective-permute-start(bf16[640,256]{1,0:T(8,128)(2,1)} %get-tuple-element.100), channel_id=1, source_target_pairs={{0,8},{1,9},{2,10},{3,11},{4,12},{5,13},{6,14},{7,15},{8,0},{9,1},... | collective-permute-start | bytes 983048 | tf_op jit(solution)/shard_map/ppermute | solution.py:40
  55.3 1.0 collective-permute-start.25
  56.3 1.5 collective-permute-start.26
  57.7 26.6 %conditional.2 = ((f32[512,256]{1,0:T(8,128)}, bf16[640,256]{1,0:T(8,128)(2,1)}, bf16[640,256]{1,0:T(8,128)(2,1)}, bf16[640,256]{1,0:T(8,128)(2,1)})) conditional(s32[]{:T(128)} %convert_element_type.4, () %tuple.28, (bf16[128,1024]{1,0:T(8,128)(2,1)S(1)}, s32[3]{0:T(128)S(1)}, bf16[2048,1024]{1,0:T(8,128)(2,1)}) %tuple.29), branch_computations={%region_0.1_spmd, %region_1.2_spmd} | conditional | flops 2151677952 | bytes 17301672 | solution.py:169
  59.1 6.4 %collective-permute-done.4.refs_1_ = bf16[128,1024]{1,0:T(8,128)(2,1)S(1)} collective-permute-done((bf16[128,1024]{1,0:T(8,128)(2,1)S(1)}, bf16[128,1024]{1,0:T(8,128)(2,1)S(1)}, u32[]{:S(2)}, u32[]{:S(2)}) %collective-permute-start.4) | collective-permute-done | bytes 262176 | tf_op jit(solution)/shard_map/cond/branch_1_fun/ppermute | solution.py:40
  66.3 7.0 %collective-permute-done.6.refs_3_ = bf16[128,1024]{1,0:T(8,128)(2,1)S(1)} collective-permute-done((bf16[128,1024]{1,0:T(8,128)(2,1)S(1)}, bf16[128,1024]{1,0:T(8,128)(2,1)S(1)}, u32[]{:S(2)}, u32[]{:S(2)}) %collective-permute-start.6) | collective-permute-done | bytes 262176 | tf_op jit(solution)/shard_map/cond/branch_1_fun/ppermute | solution.py:40
  73.5 2.6 %collective-permute-done.7.refs_4_ = bf16[512,1024]{1,0:T(8,128)(2,1)S(1)} collective-permute-done((bf16[512,1024]{1,0:T(8,128)(2,1)S(1)}, bf16[512,1024]{1,0:T(8,128)(2,1)S(1)}, u32[]{:S(2)}, u32[]{:S(2)}) %collective-permute-start.7) | collective-permute-done | bytes 1048608 | tf_op jit(solution)/shard_map/cond/branch_1_fun/ppermute | solution.py:40
  76.1 8.3 %project.2 = (f32[512,256]{1,0:T(8,128)}, bf16[640,256]{1,0:T(8,128)(2,1)}, bf16[640,256]{1,0:T(8,128)(2,1)}, bf16[640,256]{1,0:T(8,128)(2,1)}) custom-call(s32[3]{0:T(128)S(1)} %get-tuple-element.12.place_ref, bf16[128,1024]{1,0:T(8,128)(2,1)S(1)} %get-tuple-element.15.refs_0_, bf16[128,1024]{1,0:T(8,128)(2,1)S(1)} %collective-permute-done.4.refs_1_, ...), custom_call_target="tpu_custom_call" | custom-call | flops 2147483648 | bytes 7864320 | tf_op jit(solution)/shard_map/cond/branch_1_fun/project/pallas_call | solution.py:332
  84.9 2.4 %collective-permute-start.22 = (bf16[640,256]{1,0:T(8,128)(2,1)}, bf16[640,256]{1,0:T(8,128)(2,1)S(1)}, u32[]{:S(2)}, u32[]{:S(2)}) collective-permute-start(bf16[640,256]{1,0:T(8,128)(2,1)} %get-tuple-element.97), channel_id=1, source_target_pairs={{0,16},{1,17},{2,18},{3,19},{4,20},{5,21},{6,22},{7,23},{8,24},{9,... | collective-permute-start | bytes 983048 | tf_op jit(solution)/shard_map/ppermute | solution.py:40
  87.4 1.5 collective-permute-start.23
  88.9 3.2 %normalize.2 = (f32[512,256]{1,0:T(8,128)S(1)}, bf16[512,256]{1,0:T(8,128)(2,1)S(1)}, f32[1,256]{1,0:T(1,128)S(1)}, f32[256,512]{1,0:T(8,128)}, f32[256,512]{1,0:T(8,128)}) custom-call(s32[3]{0:T(128)S(1)} %pad_add_fusion.place_ref, f32[512,256]{1,0:T(8,128)S(1)} %get-tuple-element.99.refs_0_, bf16[640,256]{1,0:T(8,128)(2,1)S(1)} %collective-permute-done.24.refs_1_, ...), custom_call_target="tpu_custom_call" | custom-call | flops 134217728 | bytes 3145728 | tf_op jit(solution)/shard_map/normalize/pallas_call | solution.py:416
  92.1 15.3 %conditional.3 = ((f32[16,512]{1,0:T(8,128)S(1)}, f32[16,512]{1,0:T(8,128)S(1)}, f32[16,512]{1,0:T(8,128)S(1)}, f32[16,512]{1,0:T(8,128)S(1)})) conditional(s32[]{:T(128)} %convert_element_type.4, () %tuple.31, (f32[256,512]{1,0:T(8,128)}, s32[3]{0:T(128)S(1)}, f32[256,512]{1,0:T(8,128)}) %tuple.32), branch_computations={%region_2.3_spmd, %region_3.4_spmd} | conditional | bytes 3670184 | solution.py:169
  92.1 2.1 %collective-permute-done.met_ref = f32[256,512]{1,0:T(8,128)S(1)} collective-permute-done((f32[256,512]{1,0:T(8,128)}, f32[256,512]{1,0:T(8,128)S(1)}, u32[]{:S(2)}, u32[]{:S(2)}) %collective-permute-start) | collective-permute-done | bytes 524320 | tf_op jit(solution)/shard_map/cond/branch_1_fun/ppermute | solution.py:40
  94.2 1.1 halve.2
  95.9 0.8 collective-permute-start.2
  96.8 4.2 %collective-permute-done.1.refs_1_ = f32[64,512]{1,0:T(8,128)S(1)} collective-permute-done((f32[64,512]{1,0:T(8,128)S(1)}, f32[64,512]{1,0:T(8,128)S(1)}, u32[]{:S(2)}, u32[]{:S(2)}) %collective-permute-start.1) | collective-permute-done | bytes 131104 | tf_op jit(solution)/shard_map/cond/branch_1_fun/ppermute | solution.py:40
  101.7 5.1 %collective-permute-done.3.refs_3_ = f32[64,512]{1,0:T(8,128)S(1)} collective-permute-done((f32[64,512]{1,0:T(8,128)S(1)}, f32[64,512]{1,0:T(8,128)S(1)}, u32[]{:S(2)}, u32[]{:S(2)}) %collective-permute-start.3) | collective-permute-done | bytes 131104 | tf_op jit(solution)/shard_map/cond/branch_1_fun/ppermute | solution.py:40
  107.5 2.9 %collective-permute-start.28 = (f32[16,512]{1,0:T(8,128)S(1)}, f32[16,512]{1,0:T(8,128)S(1)}, u32[]{:S(2)}, u32[]{:S(2)}) collective-permute-start(f32[16,512]{1,0:T(8,128)S(1)} %get-tuple-element.107), channel_id=1, source_target_pairs={{0,16},{1,17},{2,18},{3,19},{4,20},{5,21},{6,22},{7,23},{8,24},{9,... | collective-permute-start | bytes 98312 | tf_op jit(solution)/shard_map/ppermute | solution.py:40
  110.4 1.5 collective-permute-start.29
  111.9 7.2 %collective-permute-done.28.refs_2_ = f32[16,512]{1,0:T(8,128)S(1)} collective-permute-done((f32[16,512]{1,0:T(8,128)S(1)}, f32[16,512]{1,0:T(8,128)S(1)}, u32[]{:S(2)}, u32[]{:S(2)}) %collective-permute-start.28) | collective-permute-done | bytes 32800 | tf_op jit(solution)/shard_map/ppermute | solution.py:40
  119.1 3.0 %normalize.3 = (f32[512,256]{1,0:T(8,128)S(1)}, bf16[512,256]{1,0:T(8,128)(2,1)S(1)}, f32[1,256]{1,0:T(1,128)S(1)}, f32[256,512]{1,0:T(8,128)S(1)}, f32[256,512]{1,0:T(8,128)S(1)}, /*index=5*/f32[1,256]{1,0:T(1,128)S(1)}) custom-call(s32[3]{0:T(128)S(1)} %pad_add_fusion.place_ref, f32[512,256]{1,0:T(8,128)} %get-tuple-element.113.refs_0_, ...), custom_call_target="tpu_custom_call" | custom-call | flops 134217728 | bytes 3145728 | tf_op jit(solution)/shard_map/normalize/pallas_call | solution.py:416
  122.2 1.9 %collective-permute-done.30.met_ref = f32[256,512]{1,0:T(8,128)S(1)} collective-permute-done((f32[256,512]{1,0:T(8,128)S(1)}, f32[256,512]{1,0:T(8,128)S(1)}, u32[]{:S(2)}, u32[]{:S(2)}) %collective-permute-start.30) | collective-permute-done | bytes 524320 | tf_op jit(solution)/shard_map/ppermute | solution.py:40
  126.1 2.1 %collective-permute-start.33 = (f32[64,512]{1,0:T(8,128)S(1)}, f32[64,512]{1,0:T(8,128)S(1)}, u32[]{:S(2)}, u32[]{:S(2)}) collective-permute-start(f32[64,512]{1,0:T(8,128)S(1)} %get-tuple-element.123), channel_id=1, source_target_pairs={{0,6},{1,7},{2,4},{3,5},{4,2},{5,3},{6,0},{7,1},{8,14},{9,15},{10,... | collective-permute-start | bytes 393224 | tf_op jit(solution)/shard_map/ppermute | solution.py:40
  128.3 2.9 %collective-permute-done.31.refs_1_ = f32[64,512]{1,0:T(8,128)S(1)} collective-permute-done((f32[64,512]{1,0:T(8,128)S(1)}, f32[64,512]{1,0:T(8,128)S(1)}, u32[]{:S(2)}, u32[]{:S(2)}) %collective-permute-start.31) | collective-permute-done | bytes 131104 | tf_op jit(solution)/shard_map/ppermute | solution.py:40
  131.1 2.3 %collective-permute-done.32.refs_2_ = f32[64,512]{1,0:T(8,128)S(1)} collective-permute-done((f32[64,512]{1,0:T(8,128)S(1)}, f32[64,512]{1,0:T(8,128)S(1)}, u32[]{:S(2)}, u32[]{:S(2)}) %collective-permute-start.32) | collective-permute-done | bytes 131104 | tf_op jit(solution)/shard_map/ppermute | solution.py:40
  134.0 1.0 collective-permute-start.34
  134.9 2.0 %collective-permute-start.35 = (f32[16,512]{1,0:T(8,128)S(1)}, f32[16,512]{1,0:T(8,128)S(1)}, u32[]{:S(2)}, u32[]{:S(2)}) collective-permute-start(f32[16,512]{1,0:T(8,128)S(1)} %get-tuple-element.126), channel_id=1, source_target_pairs={{0,16},{1,17},{2,18},{3,19},{4,20},{5,21},{6,22},{7,23},{8,24},{9,... | collective-permute-start | bytes 98312 | tf_op jit(solution)/shard_map/ppermute | solution.py:40
  137.0 1.5 collective-permute-start.36
  138.4 1.3 collective-permute-done.35.refs_6_
  139.8 2.9 %collective-permute-done.36.refs_7_ = f32[16,512]{1,0:T(8,128)S(1)} collective-permute-done((f32[16,512]{1,0:T(8,128)S(1)}, f32[16,512]{1,0:T(8,128)S(1)}, u32[]{:S(2)}, u32[]{:S(2)}) %collective-permute-start.36) | collective-permute-done | bytes 32800 | tf_op jit(solution)/shard_map/ppermute | solution.py:40
  143.4 1.5 collective-permute-start.37
  144.9 2.9 %collective-permute-start.39 = (bf16[32,512]{1,0:T(8,128)(2,1)S(1)}, bf16[32,512]{1,0:T(8,128)(2,1)S(1)}, u32[]{:S(2)}, u32[]{:S(2)}) collective-permute-start(bf16[32,512]{1,0:T(8,128)(2,1)S(1)} %finish.1), channel_id=1, source_target_pairs={{0,8},{1,9},{2,10},{3,11},{4,12},{5,13},{6,14},{7,15},{8,0},{9,1},... | collective-permute-start | bytes 98312 | tf_op jit(solution)/shard_map/ppermute | solution.py:40
  147.8 1.3 collective-permute-done.37
  150.1 1.6 collective-permute-start.40
  152.2 1.5 collective-permute-start.42
  153.7 1.5 collective-permute-done.40.refs_1_
  155.1 1.5 collective-permute-done.41.refs_2_
  156.6 1.4 collective-permute-done.42.refs_3_
  158.0 1.3 collective-permute-done.46.refs_7_
  159.4 1.9 %gradient.1 = (bf16[256,256]{1,0:T(8,128)(2,1)S(1)}, bf16[256,256]{1,0:T(8,128)(2,1)S(1)}, bf16[256,256]{1,0:T(8,128)(2,1)S(1)}, bf16[256,256]{1,0:T(8,128)(2,1)S(1)}, f32[1,1]{1,0:T(1,128)}) custom-call(s32[3]{0:T(128)S(1)} %pad_add_fusion.place_ref, bf16[128,512]{1,0:T(8,128)(2,1)S(1)} %pad_maximum_fusion.1.refs_0_, ...), custom_call_target="tpu_custom_call" | custom-call | tf_op jit(solution)/shard_map/gradient/pallas_call | solution.py:134
  161.3 1.7 collective-permute-start.47
  163.0 0.9 collective-permute-start.48
  163.9 1.8 %collective-permute-start.49 = (bf16[256,256]{1,0:T(8,128)(2,1)S(1)}, bf16[256,256]{1,0:T(8,128)(2,1)S(1)}, u32[]{:S(2)}, u32[]{:S(2)}) collective-permute-start(bf16[256,256]{1,0:T(8,128)(2,1)S(1)} %get-tuple-element.137), channel_id=1, source_target_pairs={{0,24},{1,25},{2,26},{3,27},{4,28},{5,29},{6,30},{7,31},{8,16},{9,... | collective-permute-start | bytes 393224 | tf_op jit(solution)/shard_map/ppermute | solution.py:40
  165.7 2.5 %collective-permute-done.47.refs_1_ = bf16[256,256]{1,0:T(8,128)(2,1)S(1)} collective-permute-done((bf16[256,256]{1,0:T(8,128)(2,1)S(1)}, bf16[256,256]{1,0:T(8,128)(2,1)S(1)}, u32[]{:S(2)}, u32[]{:S(2)}) %collective-permute-start.47) | collective-permute-done | bytes 131104 | tf_op jit(solution)/shard_map/ppermute | solution.py:40
  168.2 7.6 %collective-permute-done.48.refs_2_ = bf16[256,256]{1,0:T(8,128)(2,1)S(1)} collective-permute-done((bf16[256,256]{1,0:T(8,128)(2,1)S(1)}, bf16[256,256]{1,0:T(8,128)(2,1)S(1)}, u32[]{:S(2)}, u32[]{:S(2)}) %collective-permute-start.48) | collective-permute-done | bytes 131104 | tf_op jit(solution)/shard_map/ppermute | solution.py:40
  175.8 1.4 place.1
  (60 shorter events, 12.1 us)
Async XLA Ops:
  0.7 1.0 copy-start
  1.7 0.9 copy-start.1
  4.0 6.9 %collective-permute-start.10 = (bf16[64,1024]{1,0:T(8,128)(2,1)S(1)}, bf16[64,1024]{1,0:T(8,128)(2,1)S(1)}, u32[]{:S(2)}, u32[]{:S(2)}) collective-permute-start(bf16[64,1024]{1,0:T(8,128)(2,1)S(1)} %get-tuple-element.87), channel_id=1, source_target_pairs={{0,2},{1,3},{2,0},{3,1},{4,6},{5,7},{6,4},{7,5},{8,10},{9,11},{10,... | collective-permute-start | bytes 393224 | tf_op jit(solution)/shard_map/ppermute | solution.py:40
  7.0 7.6 %collective-permute-start.8 = (bf16[64,1024]{1,0:T(8,128)(2,1)S(1)}, bf16[64,1024]{1,0:T(8,128)(2,1)S(1)}, u32[]{:S(2)}, u32[]{:S(2)}) collective-permute-start(bf16[64,1024]{1,0:T(8,128)(2,1)S(1)} %get-tuple-element.85), channel_id=1, source_target_pairs={{0,6},{1,7},{2,4},{3,5},{4,2},{5,3},{6,0},{7,1},{8,14},{9,15},{10,... | collective-permute-start | bytes 393224 | tf_op jit(solution)/shard_map/ppermute | solution.py:40
  8.5 7.5 %collective-permute-start.9 = (bf16[64,1024]{1,0:T(8,128)(2,1)S(1)}, bf16[64,1024]{1,0:T(8,128)(2,1)S(1)}, u32[]{:S(2)}, u32[]{:S(2)}) collective-permute-start(bf16[64,1024]{1,0:T(8,128)(2,1)S(1)} %get-tuple-element.86), channel_id=1, source_target_pairs={{0,4},{1,5},{2,6},{3,7},{4,0},{5,1},{6,2},{7,3},{8,12},{9,13},{10,... | collective-permute-start | bytes 393224 | tf_op jit(solution)/shard_map/ppermute | solution.py:40
  16.0 6.5 %collective-permute-start.11 = (bf16[64,1024]{1,0:T(8,128)(2,1)S(1)}, bf16[64,1024]{1,0:T(8,128)(2,1)S(1)}, u32[]{:S(2)}, u32[]{:S(2)}) collective-permute-start(bf16[64,1024]{1,0:T(8,128)(2,1)S(1)} %get-tuple-element.142), channel_id=1, source_target_pairs={{0,8},{1,9},{2,10},{3,11},{4,12},{5,13},{6,14},{7,15},{8,0},{9,1},... | collective-permute-start | bytes 393224 | tf_op jit(solution)/shard_map/ppermute | solution.py:40
  17.6 12.2 %collective-permute-start.12 = (bf16[64,1024]{1,0:T(8,128)(2,1)S(1)}, bf16[64,1024]{1,0:T(8,128)(2,1)S(1)}, u32[]{:S(2)}, u32[]{:S(2)}) collective-permute-start(bf16[64,1024]{1,0:T(8,128)(2,1)S(1)} %get-tuple-element.143), channel_id=1, source_target_pairs={{0,16},{1,17},{2,18},{3,19},{4,20},{5,21},{6,22},{7,23},{8,24},{9,... | collective-permute-start | bytes 393224 | tf_op jit(solution)/shard_map/ppermute | solution.py:40
  20.2 9.6 %collective-permute-start.13 = (bf16[64,1024]{1,0:T(8,128)(2,1)S(1)}, bf16[64,1024]{1,0:T(8,128)(2,1)S(1)}, u32[]{:S(2)}, u32[]{:S(2)}) collective-permute-start(bf16[64,1024]{1,0:T(8,128)(2,1)S(1)} %get-tuple-element.141), channel_id=1, source_target_pairs={{0,24},{1,25},{2,26},{3,27},{4,28},{5,29},{6,30},{7,31},{8,16},{9,... | collective-permute-start | bytes 393224 | tf_op jit(solution)/shard_map/ppermute | solution.py:40
  30.4 7.4 %collective-permute-start.14 = (bf16[128,1024]{1,0:T(8,128)(2,1)S(1)}, bf16[128,1024]{1,0:T(8,128)(2,1)S(1)}, u32[]{:S(2)}, u32[]{:S(2)}) collective-permute-start(bf16[128,1024]{1,0:T(8,128)(2,1)S(1)} %get-tuple-element.90.refs_0_), channel_id=1, source_target_pairs={{0,2},{1,3},{2,0},{3,1},{4,6},{5,7},{6,4},{7,5},{8,10},{9,11},{10,... | collective-permute-start | bytes 786440 | tf_op jit(solution)/shard_map/ppermute | solution.py:40
  32.0 9.8 %collective-permute-start.15 = (bf16[128,1024]{1,0:T(8,128)(2,1)S(1)}, bf16[128,1024]{1,0:T(8,128)(2,1)S(1)}, u32[]{:S(2)}, u32[]{:S(2)}) collective-permute-start(bf16[128,1024]{1,0:T(8,128)(2,1)S(1)} %get-tuple-element.90.refs_0_), channel_id=1, source_target_pairs={{0,4},{1,5},{2,6},{3,7},{4,0},{5,1},{6,2},{7,3},{8,12},{9,13},{10,... | collective-permute-start | bytes 786440 | tf_op jit(solution)/shard_map/ppermute | solution.py:40
  32.5 9.3 %collective-permute-start.16 = (bf16[128,1024]{1,0:T(8,128)(2,1)S(1)}, bf16[128,1024]{1,0:T(8,128)(2,1)S(1)}, u32[]{:S(2)}, u32[]{:S(2)}) collective-permute-start(bf16[128,1024]{1,0:T(8,128)(2,1)S(1)} %get-tuple-element.90.refs_0_), channel_id=1, source_target_pairs={{0,6},{1,7},{2,4},{3,5},{4,2},{5,3},{6,0},{7,1},{8,14},{9,15},{10,... | collective-permute-start | bytes 786440 | tf_op jit(solution)/shard_map/ppermute | solution.py:40
  34.0 8.3 %collective-permute-start.17 = (bf16[128,1024]{1,0:T(8,128)(2,1)S(1)}, bf16[128,1024]{1,0:T(8,128)(2,1)S(1)}, u32[]{:S(2)}, u32[]{:S(2)}) collective-permute-start(bf16[128,1024]{1,0:T(8,128)(2,1)S(1)} %get-tuple-element.90.refs_0_), channel_id=1, source_target_pairs={{0,1},{1,0},{2,3},{3,2},{4,5},{5,4},{6,7},{7,6},{8,9},{9,8},{10,11... | collective-permute-start | bytes 786440 | tf_op jit(solution)/shard_map/ppermute | solution.py:40
  37.8 4.5 %collective-permute-start.18 = (bf16[128,1024]{1,0:T(8,128)(2,1)S(1)}, bf16[128,1024]{1,0:T(8,128)(2,1)S(1)}, u32[]{:S(2)}, u32[]{:S(2)}) collective-permute-start(bf16[128,1024]{1,0:T(8,128)(2,1)S(1)} %collective-permute-done.14.refs_1_), channel_id=1, source_target_pairs={{0,1},{1,0},{2,3},{3,2},{4,5},{5,4},{6,7},{7,6},{8,9},{9,8},{10,11... | collective-permute-start | bytes 786440 | tf_op jit(solution)/shard_map/ppermute | solution.py:40
  41.8 1.5 collective-permute-start.19
  41.8 1.9 %collective-permute-start.20 = (bf16[128,1024]{1,0:T(8,128)(2,1)S(1)}, bf16[128,1024]{1,0:T(8,128)(2,1)S(1)}, u32[]{:S(2)}, u32[]{:S(2)}) collective-permute-start(bf16[128,1024]{1,0:T(8,128)(2,1)S(1)} %collective-permute-done.16.refs_3_), channel_id=1, source_target_pairs={{0,1},{1,0},{2,3},{3,2},{4,5},{5,4},{6,7},{7,6},{8,9},{9,8},{10,11... | collective-permute-start | bytes 786440 | tf_op jit(solution)/shard_map/ppermute | solution.py:40
  51.2 36.2 %collective-permute-start.24 = (bf16[640,256]{1,0:T(8,128)(2,1)}, bf16[640,256]{1,0:T(8,128)(2,1)S(1)}, u32[]{:S(2)}, u32[]{:S(2)}) collective-permute-start(bf16[640,256]{1,0:T(8,128)(2,1)} %get-tuple-element.100), channel_id=1, source_target_pairs={{0,8},{1,9},{2,10},{3,11},{4,12},{5,13},{6,14},{7,15},{8,0},{9,1},... | collective-permute-start | bytes 983048 | tf_op jit(solution)/shard_map/ppermute | solution.py:40
  55.3 33.6 %collective-permute-start.25 = (bf16[640,256]{1,0:T(8,128)(2,1)S(1)}, bf16[640,256]{1,0:T(8,128)(2,1)S(1)}, u32[]{:S(2)}, u32[]{:S(2)}) collective-permute-start(bf16[640,256]{1,0:T(8,128)(2,1)S(1)} %get-tuple-element.101), channel_id=1, source_target_pairs={{0,16},{1,17},{2,18},{3,19},{4,20},{5,21},{6,22},{7,23},{8,24},{9,... | collective-permute-start | bytes 983048 | tf_op jit(solution)/shard_map/ppermute | solution.py:40
  56.3 32.6 %collective-permute-start.26 = (bf16[640,256]{1,0:T(8,128)(2,1)S(1)}, bf16[640,256]{1,0:T(8,128)(2,1)S(1)}, u32[]{:S(2)}, u32[]{:S(2)}) collective-permute-start(bf16[640,256]{1,0:T(8,128)(2,1)S(1)} %get-tuple-element.102), channel_id=1, source_target_pairs={{0,24},{1,25},{2,26},{3,27},{4,28},{5,29},{6,30},{7,31},{8,16},{9,... | collective-permute-start | bytes 983048 | tf_op jit(solution)/shard_map/ppermute | solution.py:40
  57.7 7.8 %collective-permute-start.4 = (bf16[128,1024]{1,0:T(8,128)(2,1)S(1)}, bf16[128,1024]{1,0:T(8,128)(2,1)S(1)}, u32[]{:S(2)}, u32[]{:S(2)}) collective-permute-start(bf16[128,1024]{1,0:T(8,128)(2,1)S(1)} %get-tuple-element.15.refs_0_), channel_id=1, source_target_pairs={{0,2},{1,3},{2,0},{3,1},{4,6},{5,7},{6,4},{7,5},{8,10},{9,11},{10,... | collective-permute-start | bytes 786440 | tf_op jit(solution)/shard_map/cond/branch_1_fun/ppermute | solution.py:40
  58.3 8.1 %collective-permute-start.5 = (bf16[128,1024]{1,0:T(8,128)(2,1)S(1)}, bf16[128,1024]{1,0:T(8,128)(2,1)S(1)}, u32[]{:S(2)}, u32[]{:S(2)}) collective-permute-start(bf16[128,1024]{1,0:T(8,128)(2,1)S(1)} %get-tuple-element.15.refs_0_), channel_id=1, source_target_pairs={{0,4},{1,5},{2,6},{3,7},{4,0},{5,1},{6,2},{7,3},{8,12},{9,13},{10,... | collective-permute-start | bytes 786440 | tf_op jit(solution)/shard_map/cond/branch_1_fun/ppermute | solution.py:40
  65.5 7.8 %collective-permute-start.6 = (bf16[128,1024]{1,0:T(8,128)(2,1)S(1)}, bf16[128,1024]{1,0:T(8,128)(2,1)S(1)}, u32[]{:S(2)}, u32[]{:S(2)}) collective-permute-start(bf16[128,1024]{1,0:T(8,128)(2,1)S(1)} %get-tuple-element.15.refs_0_), channel_id=1, source_target_pairs={{0,6},{1,7},{2,4},{3,5},{4,2},{5,3},{6,0},{7,1},{8,14},{9,15},{10,... | collective-permute-start | bytes 786440 | tf_op jit(solution)/shard_map/cond/branch_1_fun/ppermute | solution.py:40
  73.4 2.7 %collective-permute-start.7 = (bf16[512,1024]{1,0:T(8,128)(2,1)S(1)}, bf16[512,1024]{1,0:T(8,128)(2,1)S(1)}, u32[]{:S(2)}, u32[]{:S(2)}) collective-permute-start(bf16[512,1024]{1,0:T(8,128)(2,1)S(1)} %pad_maximum_fusion), channel_id=1, source_target_pairs={{0,1},{1,0},{2,3},{3,2},{4,5},{5,4},{6,7},{7,6},{8,9},{9,8},{10,11... | collective-permute-start | bytes 3145736 | tf_op jit(solution)/shard_map/cond/branch_1_fun/ppermute | solution.py:40
  84.4 26.0 %collective-permute-start.21 = (bf16[640,256]{1,0:T(8,128)(2,1)}, bf16[640,256]{1,0:T(8,128)(2,1)S(1)}, u32[]{:S(2)}, u32[]{:S(2)}) collective-permute-start(bf16[640,256]{1,0:T(8,128)(2,1)} %get-tuple-element.96), channel_id=1, source_target_pairs={{0,8},{1,9},{2,10},{3,11},{4,12},{5,13},{6,14},{7,15},{8,0},{9,1},... | collective-permute-start | bytes 983048 | tf_op jit(solution)/shard_map/ppermute | solution.py:40
  84.9 26.9 %collective-permute-start.22 = (bf16[640,256]{1,0:T(8,128)(2,1)}, bf16[640,256]{1,0:T(8,128)(2,1)S(1)}, u32[]{:S(2)}, u32[]{:S(2)}) collective-permute-start(bf16[640,256]{1,0:T(8,128)(2,1)} %get-tuple-element.97), channel_id=1, source_target_pairs={{0,16},{1,17},{2,18},{3,19},{4,20},{5,21},{6,22},{7,23},{8,24},{9,... | collective-permute-start | bytes 983048 | tf_op jit(solution)/shard_map/ppermute | solution.py:40
  87.4 24.5 %collective-permute-start.23 = (bf16[640,256]{1,0:T(8,128)(2,1)}, bf16[640,256]{1,0:T(8,128)(2,1)S(1)}, u32[]{:S(2)}, u32[]{:S(2)}) collective-permute-start(bf16[640,256]{1,0:T(8,128)(2,1)} %get-tuple-element.98), channel_id=1, source_target_pairs={{0,24},{1,25},{2,26},{3,27},{4,28},{5,29},{6,30},{7,31},{8,16},{9,... | collective-permute-start | bytes 983048 | tf_op jit(solution)/shard_map/ppermute | solution.py:40
  92.1 2.1 %collective-permute-start = (f32[256,512]{1,0:T(8,128)}, f32[256,512]{1,0:T(8,128)S(1)}, u32[]{:S(2)}, u32[]{:S(2)}) collective-permute-start(f32[256,512]{1,0:T(8,128)} %get-tuple-element.19), channel_id=1, source_target_pairs={{0,1},{1,0},{2,3},{3,2},{4,5},{5,4},{6,7},{7,6},{8,9},{9,8},{10,11... | collective-permute-start | bytes 1572872 | tf_op jit(solution)/shard_map/cond/branch_1_fun/ppermute | solution.py:40
  95.3 5.6 %collective-permute-start.1 = (f32[64,512]{1,0:T(8,128)S(1)}, f32[64,512]{1,0:T(8,128)S(1)}, u32[]{:S(2)}, u32[]{:S(2)}) collective-permute-start(f32[64,512]{1,0:T(8,128)S(1)} %get-tuple-element.21), channel_id=1, source_target_pairs={{0,2},{1,3},{2,0},{3,1},{4,6},{5,7},{6,4},{7,5},{8,10},{9,11},{10,... | collective-permute-start | bytes 393224 | tf_op jit(solution)/shard_map/cond/branch_1_fun/ppermute | solution.py:40
  95.9 5.8 %collective-permute-start.2 = (f32[64,512]{1,0:T(8,128)S(1)}, f32[64,512]{1,0:T(8,128)S(1)}, u32[]{:S(2)}, u32[]{:S(2)}) collective-permute-start(f32[64,512]{1,0:T(8,128)S(1)} %get-tuple-element.24), channel_id=1, source_target_pairs={{0,4},{1,5},{2,6},{3,7},{4,0},{5,1},{6,2},{7,3},{8,12},{9,13},{10,... | collective-permute-start | bytes 393224 | tf_op jit(solution)/shard_map/cond/branch_1_fun/ppermute | solution.py:40
  100.9 5.9 %collective-permute-start.3 = (f32[64,512]{1,0:T(8,128)S(1)}, f32[64,512]{1,0:T(8,128)S(1)}, u32[]{:S(2)}, u32[]{:S(2)}) collective-permute-start(f32[64,512]{1,0:T(8,128)S(1)} %get-tuple-element.25), channel_id=1, source_target_pairs={{0,6},{1,7},{2,4},{3,5},{4,2},{5,3},{6,0},{7,1},{8,14},{9,15},{10,... | collective-permute-start | bytes 393224 | tf_op jit(solution)/shard_map/cond/branch_1_fun/ppermute | solution.py:40
  107.4 4.5 %collective-permute-start.27 = (f32[16,512]{1,0:T(8,128)S(1)}, f32[16,512]{1,0:T(8,128)S(1)}, u32[]{:S(2)}, u32[]{:S(2)}) collective-permute-start(f32[16,512]{1,0:T(8,128)S(1)} %get-tuple-element.106), channel_id=1, source_target_pairs={{0,8},{1,9},{2,10},{3,11},{4,12},{5,13},{6,14},{7,15},{8,0},{9,1},... | collective-permute-start | bytes 98312 | tf_op jit(solution)/shard_map/ppermute | solution.py:40
  107.5 11.6 %collective-permute-start.28 = (f32[16,512]{1,0:T(8,128)S(1)}, f32[16,512]{1,0:T(8,128)S(1)}, u32[]{:S(2)}, u32[]{:S(2)}) collective-permute-start(f32[16,512]{1,0:T(8,128)S(1)} %get-tuple-element.107), channel_id=1, source_target_pairs={{0,16},{1,17},{2,18},{3,19},{4,20},{5,21},{6,22},{7,23},{8,24},{9,... | collective-permute-start | bytes 98312 | tf_op jit(solution)/shard_map/ppermute | solution.py:40
  110.4 8.7 %collective-permute-start.29 = (f32[16,512]{1,0:T(8,128)S(1)}, f32[16,512]{1,0:T(8,128)S(1)}, u32[]{:S(2)}, u32[]{:S(2)}) collective-permute-start(f32[16,512]{1,0:T(8,128)S(1)} %get-tuple-element.108), channel_id=1, source_target_pairs={{0,24},{1,25},{2,26},{3,27},{4,28},{5,29},{6,30},{7,31},{8,16},{9,... | collective-permute-start | bytes 98312 | tf_op jit(solution)/shard_map/ppermute | solution.py:40
  122.1 2.0 %collective-permute-start.30 = (f32[256,512]{1,0:T(8,128)S(1)}, f32[256,512]{1,0:T(8,128)S(1)}, u32[]{:S(2)}, u32[]{:S(2)}) collective-permute-start(f32[256,512]{1,0:T(8,128)S(1)} %get-tuple-element.119), channel_id=1, source_target_pairs={{0,1},{1,0},{2,3},{3,2},{4,5},{5,4},{6,7},{7,6},{8,9},{9,8},{10,11... | collective-permute-start | bytes 1572872 | tf_op jit(solution)/shard_map/ppermute | solution.py:40
  124.7 6.4 %collective-permute-start.31 = (f32[64,512]{1,0:T(8,128)S(1)}, f32[64,512]{1,0:T(8,128)S(1)}, u32[]{:S(2)}, u32[]{:S(2)}) collective-permute-start(f32[64,512]{1,0:T(8,128)S(1)} %get-tuple-element.121), channel_id=1, source_target_pairs={{0,2},{1,3},{2,0},{3,1},{4,6},{5,7},{6,4},{7,5},{8,10},{9,11},{10,... | collective-permute-start | bytes 393224 | tf_op jit(solution)/shard_map/ppermute | solution.py:40
  125.3 8.1 %collective-permute-start.32 = (f32[64,512]{1,0:T(8,128)S(1)}, f32[64,512]{1,0:T(8,128)S(1)}, u32[]{:S(2)}, u32[]{:S(2)}) collective-permute-start(f32[64,512]{1,0:T(8,128)S(1)} %get-tuple-element.122), channel_id=1, source_target_pairs={{0,4},{1,5},{2,6},{3,7},{4,0},{5,1},{6,2},{7,3},{8,12},{9,13},{10,... | collective-permute-start | bytes 393224 | tf_op jit(solution)/shard_map/ppermute | solution.py:40
  126.1 7.2 %collective-permute-start.33 = (f32[64,512]{1,0:T(8,128)S(1)}, f32[64,512]{1,0:T(8,128)S(1)}, u32[]{:S(2)}, u32[]{:S(2)}) collective-permute-start(f32[64,512]{1,0:T(8,128)S(1)} %get-tuple-element.123), channel_id=1, source_target_pairs={{0,6},{1,7},{2,4},{3,5},{4,2},{5,3},{6,0},{7,1},{8,14},{9,15},{10,... | collective-permute-start | bytes 393224 | tf_op jit(solution)/shard_map/ppermute | solution.py:40
  134.0 4.5 %collective-permute-start.34 = (f32[16,512]{1,0:T(8,128)S(1)}, f32[16,512]{1,0:T(8,128)S(1)}, u32[]{:S(2)}, u32[]{:S(2)}) collective-permute-start(f32[16,512]{1,0:T(8,128)S(1)} %get-tuple-element.125), channel_id=1, source_target_pairs={{0,8},{1,9},{2,10},{3,11},{4,12},{5,13},{6,14},{7,15},{8,0},{9,1},... | collective-permute-start | bytes 98312 | tf_op jit(solution)/shard_map/ppermute | solution.py:40
  134.9 4.8 %collective-permute-start.35 = (f32[16,512]{1,0:T(8,128)S(1)}, f32[16,512]{1,0:T(8,128)S(1)}, u32[]{:S(2)}, u32[]{:S(2)}) collective-permute-start(f32[16,512]{1,0:T(8,128)S(1)} %get-tuple-element.126), channel_id=1, source_target_pairs={{0,16},{1,17},{2,18},{3,19},{4,20},{5,21},{6,22},{7,23},{8,24},{9,... | collective-permute-start | bytes 98312 | tf_op jit(solution)/shard_map/ppermute | solution.py:40
  137.0 5.7 %collective-permute-start.36 = (f32[16,512]{1,0:T(8,128)S(1)}, f32[16,512]{1,0:T(8,128)S(1)}, u32[]{:S(2)}, u32[]{:S(2)}) collective-permute-start(f32[16,512]{1,0:T(8,128)S(1)} %get-tuple-element.127), channel_id=1, source_target_pairs={{0,24},{1,25},{2,26},{3,27},{4,28},{5,29},{6,30},{7,31},{8,16},{9,... | collective-permute-start | bytes 98312 | tf_op jit(solution)/shard_map/ppermute | solution.py:40
  143.4 5.8 %collective-permute-start.37 = (bf16[32,512]{1,0:T(8,128)(2,1)S(1)}, bf16[32,512]{1,0:T(8,128)(2,1)S(1)}, u32[]{:S(2)}, u32[]{:S(2)}) collective-permute-start(bf16[32,512]{1,0:T(8,128)(2,1)S(1)} %finish.1), channel_id=1, source_target_pairs={{0,24},{1,25},{2,26},{3,27},{4,28},{5,29},{6,30},{7,31},{8,16},{9,... | collective-permute-start | bytes 98312 | tf_op jit(solution)/shard_map/ppermute | solution.py:40
  144.9 5.1 %collective-permute-start.38 = (bf16[32,512]{1,0:T(8,128)(2,1)S(1)}, bf16[32,512]{1,0:T(8,128)(2,1)S(1)}, u32[]{:S(2)}, u32[]{:S(2)}) collective-permute-start(bf16[32,512]{1,0:T(8,128)(2,1)S(1)} %finish.1), channel_id=1, source_target_pairs={{0,16},{1,17},{2,18},{3,19},{4,20},{5,21},{6,22},{7,23},{8,24},{9,... | collective-permute-start | bytes 98312 | tf_op jit(solution)/shard_map/ppermute | solution.py:40
  144.9 5.2 %collective-permute-start.39 = (bf16[32,512]{1,0:T(8,128)(2,1)S(1)}, bf16[32,512]{1,0:T(8,128)(2,1)S(1)}, u32[]{:S(2)}, u32[]{:S(2)}) collective-permute-start(bf16[32,512]{1,0:T(8,128)(2,1)S(1)} %finish.1), channel_id=1, source_target_pairs={{0,8},{1,9},{2,10},{3,11},{4,12},{5,13},{6,14},{7,15},{8,0},{9,1},... | collective-permute-start | bytes 98312 | tf_op jit(solution)/shard_map/ppermute | solution.py:40
  150.1 5.0 %collective-permute-start.40 = (bf16[128,512]{1,0:T(8,128)(2,1)S(1)}, bf16[128,512]{1,0:T(8,128)(2,1)S(1)}, u32[]{:S(2)}, u32[]{:S(2)}) collective-permute-start(bf16[128,512]{1,0:T(8,128)(2,1)S(1)} %pad_maximum_fusion.1.refs_0_), channel_id=1, source_target_pairs={{0,2},{1,3},{2,0},{3,1},{4,6},{5,7},{6,4},{7,5},{8,10},{9,11},{10,... | collective-permute-start | bytes 393224 | tf_op jit(solution)/shard_map/ppermute | solution.py:40
  151.7 5.0 %collective-permute-start.41 = (bf16[128,512]{1,0:T(8,128)(2,1)S(1)}, bf16[128,512]{1,0:T(8,128)(2,1)S(1)}, u32[]{:S(2)}, u32[]{:S(2)}) collective-permute-start(bf16[128,512]{1,0:T(8,128)(2,1)S(1)} %pad_maximum_fusion.1.refs_0_), channel_id=1, source_target_pairs={{0,4},{1,5},{2,6},{3,7},{4,0},{5,1},{6,2},{7,3},{8,12},{9,13},{10,... | collective-permute-start | bytes 393224 | tf_op jit(solution)/shard_map/ppermute | solution.py:40
  152.2 5.9 %collective-permute-start.42 = (bf16[128,512]{1,0:T(8,128)(2,1)S(1)}, bf16[128,512]{1,0:T(8,128)(2,1)S(1)}, u32[]{:S(2)}, u32[]{:S(2)}) collective-permute-start(bf16[128,512]{1,0:T(8,128)(2,1)S(1)} %pad_maximum_fusion.1.refs_0_), channel_id=1, source_target_pairs={{0,6},{1,7},{2,4},{3,5},{4,2},{5,3},{6,0},{7,1},{8,14},{9,15},{10,... | collective-permute-start | bytes 393224 | tf_op jit(solution)/shard_map/ppermute | solution.py:40
  153.6 4.4 %collective-permute-start.43 = (bf16[128,512]{1,0:T(8,128)(2,1)S(1)}, bf16[128,512]{1,0:T(8,128)(2,1)S(1)}, u32[]{:S(2)}, u32[]{:S(2)}) collective-permute-start(bf16[128,512]{1,0:T(8,128)(2,1)S(1)} %pad_maximum_fusion.1.refs_0_), channel_id=1, source_target_pairs={{0,1},{1,0},{2,3},{3,2},{4,5},{5,4},{6,7},{7,6},{8,9},{9,8},{10,11... | collective-permute-start | bytes 393224 | tf_op jit(solution)/shard_map/ppermute | solution.py:40
  155.1 2.9 %collective-permute-start.44 = (bf16[128,512]{1,0:T(8,128)(2,1)S(1)}, bf16[128,512]{1,0:T(8,128)(2,1)S(1)}, u32[]{:S(2)}, u32[]{:S(2)}) collective-permute-start(bf16[128,512]{1,0:T(8,128)(2,1)S(1)} %collective-permute-done.40.refs_1_), channel_id=1, source_target_pairs={{0,1},{1,0},{2,3},{3,2},{4,5},{5,4},{6,7},{7,6},{8,9},{9,8},{10,11... | collective-permute-start | bytes 393224 | tf_op jit(solution)/shard_map/ppermute | solution.py:40
  156.6 1.4 collective-permute-start.45
  158.0 1.3 collective-permute-start.46
  161.3 6.9 %collective-permute-start.47 = (bf16[256,256]{1,0:T(8,128)(2,1)S(1)}, bf16[256,256]{1,0:T(8,128)(2,1)S(1)}, u32[]{:S(2)}, u32[]{:S(2)}) collective-permute-start(bf16[256,256]{1,0:T(8,128)(2,1)S(1)} %get-tuple-element.135), channel_id=1, source_target_pairs={{0,8},{1,9},{2,10},{3,11},{4,12},{5,13},{6,14},{7,15},{8,0},{9,1},... | collective-permute-start | bytes 393224 | tf_op jit(solution)/shard_map/ppermute | solution.py:40
  163.0 12.8 %collective-permute-start.48 = (bf16[256,256]{1,0:T(8,128)(2,1)S(1)}, bf16[256,256]{1,0:T(8,128)(2,1)S(1)}, u32[]{:S(2)}, u32[]{:S(2)}) collective-permute-start(bf16[256,256]{1,0:T(8,128)(2,1)S(1)} %get-tuple-element.136), channel_id=1, source_target_pairs={{0,16},{1,17},{2,18},{3,19},{4,20},{5,21},{6,22},{7,23},{8,24},{9,... | collective-permute-start | bytes 393224 | tf_op jit(solution)/shard_map/ppermute | solution.py:40
  163.9 11.9 %collective-permute-start.49 = (bf16[256,256]{1,0:T(8,128)(2,1)S(1)}, bf16[256,256]{1,0:T(8,128)(2,1)S(1)}, u32[]{:S(2)}, u32[]{:S(2)}) collective-permute-start(bf16[256,256]{1,0:T(8,128)(2,1)S(1)} %get-tuple-element.137), channel_id=1, source_target_pairs={{0,24},{1,25},{2,26},{3,27},{4,28},{5,29},{6,30},{7,31},{8,16},{9,... | collective-permute-start | bytes 393224 | tf_op jit(solution)/shard_map/ppermute | solution.py:40

commit v4 on v3

--- a/solution.py
+++ b/solution.py
@@ -110,12 +110,29 @@
         out[...] = whole_ref[at, :]
 
 
+def rows_kernel(place_ref, *refs):
+    refs[-1][...] = tree_sum([ref[...] for ref in refs[:-1]]).astype(BF16)
+
+
+def code_kernel(place_ref, *refs, n):
+    met, rows_ref, out_ref = refs[:n], refs[n], refs[n + 1]
+    total = tree_sum([ref[...] for ref in met])
+    coded = total.shape[0] + total.shape[0] // SHARED
+    encode(total, out_ref.at[:coded])
+    out_ref[coded:] = rows_ref[...]
+
+
 def finish_kernel(place_ref, *refs, n, k):
     out_ref = refs[-1]
-    height = refs[0].shape[0]
-    out_ref[:height] = tree_sum([ref[...] for ref in refs[:n]]).astype(BF16)
-    total = tree_sum([ref[...] for ref in refs[n : 2 * n]])
-    last = (place_ref[0] == n - 1) & (place_ref[1] == n - 1) & (place_ref[2] == k - 1)
+    height = out_ref.shape[0] // 2
+    coded, few = height + height // SHARED, height // n
+    met = []
+    for step in range(n):
+        at = pl.ds(pl.multiple_of((place_ref[0] ^ step) * few, few), few)
+        out_ref[at, :] = refs[step][coded:]
+        met.append(jnp.concatenate(decode(refs[step].at[:coded]), 0))
+    total = tree_sum(met)
+    last = (place_ref[1] == n - 1) & (place_ref[2] == k - 1)
     edge = total[-8:, :128]
     row = lax.broadcasted_iota(jnp.int32, edge.shape, 0)
     column = lax.broadcasted_iota(jnp.int32, edge.shape, 1)
@@ -143,7 +160,6 @@
 
 
 def plane_rows(place, place_array, grams, few=False):
-    n = place.n
     half, batch = grams[0].shape
     kept, other = grams
     other = place.send(other, lambda z, a, b: (z, a, b ^ 1))
@@ -151,16 +167,22 @@
         functools.partial(halve_kernel, axis=1),
         place_array,
         (kept, other),
-        [((half // n, batch), F32)] * n,
+        [((half // place.n, batch), F32)] * place.n,
         "halve",
     )
+    return sends(place, "a", parts, few)
+
+
+def first_rows(place, place_array, grams):
+    parts = plane_rows(place, place_array, grams, True)
+    height, batch = parts[0].shape
     return local(
-        functools.partial(plane_kernel, n=n),
-        place_array,
-        sends(place, "a", parts, few),
-        [((half // (n * n), batch), F32)] * n,
+        functools.partial(plane_kernel, n=place.n),
+        place_array,
+        parts,
+        [((height // place.n, batch), F32)] * place.n,
         "plane",
-        scratch_shapes=[pltpu.VMEM((half // n, batch), F32)],
+        scratch_shapes=[pltpu.VMEM((height, batch), F32)],
     )
 
 
@@ -183,20 +205,6 @@
     return part
 
 
-def cut_kernel(place_ref, *refs, views, n):
-    inputs, outs, done = refs[:views], refs[views:-1], refs[-1]
-    few = outs[0].shape[0] // views
-    copies = []
-    for step in range(n):
-        at = pl.ds(pl.multiple_of((place_ref[1] ^ step) * few, few), few)
-        for i, view in enumerate(inputs):
-            part = outs[step].at[i * few : (i + 1) * few]
-            copies.append(pltpu.make_async_copy(view.at[at], part, done.at[step, i]))
-            copies[-1].start()
-    for copy in copies:
-        copy.wait()
-
-
 def lay_kernel(place_ref, *refs, n):
     parts, outs = refs[:n], refs[n:]
     few = parts[0].shape[0] // len(outs)
@@ -206,29 +214,44 @@
             out[at, :] = parts[step][i * few : (i + 1) * few, :]
 
 
-def spread(place, place_array, views):
-    n = place.n
-    rows, width = views[0].shape
-    few = rows // n
-    parts = pl.pallas_call(
-        functools.partial(cut_kernel, views=len(views), n=n),
-        in_specs=[pl.BlockSpec(memory_space=pltpu.SMEM)]
-        + [pl.BlockSpec(memory_space=pl.ANY)] * len(views),
-        out_specs=[pl.BlockSpec(memory_space=pltpu.VMEM)] * n,
-        out_shape=[jax.ShapeDtypeStruct((len(views) * few, width), BF16)] * n,
-        scratch_shapes=[pltpu.SemaphoreType.DMA((n, len(views)))],
+def fetch_kernel(weight_ref, held_ref, arrived):
+    copy = pltpu.make_async_copy(weight_ref, held_ref, arrived)
+    copy.start()
+    copy.wait()
+
+
+def fetch(weight):
+    return pl.pallas_call(
+        fetch_kernel,
+        in_specs=[pl.BlockSpec(memory_space=pl.ANY)],
+        out_specs=pl.BlockSpec(memory_space=pltpu.VMEM),
+        out_shape=jax.ShapeDtypeStruct(weight.shape, BF16),
+        scratch_shapes=[pltpu.SemaphoreType.DMA],
         compiler_params=pltpu.CompilerParams(vmem_limit_bytes=VMEM_BYTES // 2),
-        name="cut",
-    )(place_array, *views)
-    parts = sends(place, "a", parts)
-    parts = sends(place, "z", ordered(parts, place.a ^ place.z))
-    return local(
-        functools.partial(lay_kernel, n=n),
+        cost_estimate=pl.CostEstimate(flops=0, bytes_accessed=4 * weight.size, transcendentals=0),
+        name="fetch",
+    )(weight)
+
+
+def to_columns(place, view):
+    rows, width = view.shape
+    return exchange(place, "a", view.reshape(place.n, rows // place.n, width))
+
+
+def to_planes(place, parts):
+    return sends(place, "z", ordered(parts, place.a ^ place.z))
+
+
+def lay(place, place_array, parts):
+    rows, width = parts[0].shape
+    (laid,) = local(
+        functools.partial(lay_kernel, n=place.n),
         place_array,
         parts,
-        [((rows, width), BF16)] * len(views),
+        [((rows * place.n, width), BF16)],
         "lay",
     )
+    return laid
 
 
 def met_rows(place, values, few=False):
@@ -237,37 +260,19 @@
 
 def project_kernel(place_ref, *refs, counts, n, k):
     met = refs[: sum(counts)]
-    weight_ref, own_ref, *coded = refs[sum(counts) : -2]
-    held_ref, arrived = refs[-2:]
+    weight_ref, own_ref, *coded = refs[sum(counts) :]
     width = met[0].shape[1]
     columns = own_ref.shape[1]
-    order = [*range(1, n), 0]
-    copies = []
-    for slot, step in enumerate(order):
-        at = pl.ds(pl.multiple_of((place_ref[0] ^ step) * columns, columns), columns)
-        copies.append([])
-        for i in range(k):
-            rows = pl.ds(pl.multiple_of((place_ref[2] ^ i) * width, width), width)
-            part = held_ref.at[slot, i * width : (i + 1) * width]
-            copies[slot].append(
-                pltpu.make_async_copy(weight_ref.at[rows, at], part, arrived.at[slot, i])
-            )
-    for copy in copies[0]:
-        copy.start()
     values = []
     for count in counts:
         values.append(jnp.concatenate([ref[...] for ref in met[:count]], 0))
         met = met[count:]
-    for slot, step in enumerate(order):
-        for copy in copies[slot]:
-            copy.wait()
-        if slot + 1 < n:
-            for copy in copies[slot + 1]:
-                copy.start()
+    for step in [*range(1, n), 0]:
+        at = pl.ds(pl.multiple_of((place_ref[0] ^ step) * columns, columns), columns)
         total = 0.0
         for i in range(k):
-            part = held_ref[slot, i * width : (i + 1) * width, :]
-            total += jnp.dot(values[i], part, preferred_element_type=F32)
+            rows = pl.ds(pl.multiple_of((place_ref[2] ^ i) * width, width), width)
+            total += jnp.dot(values[i], weight_ref[rows, at], preferred_element_type=F32)
         if step == 0:
             own_ref[...] = total
         else:
@@ -332,14 +337,9 @@
     own, *parts = pl.pallas_call(
         functools.partial(project_kernel, counts=counts, n=n, k=k),
         in_specs=[pl.BlockSpec(memory_space=pltpu.SMEM)]
-        + [space] * len(met)
-        + [pl.BlockSpec(memory_space=pl.ANY)],
+        + [space] * (len(met) + 1),
         out_specs=[space] * n,
         out_shape=out_shape,
-        scratch_shapes=[
-            pltpu.VMEM((n, k * width, columns), BF16),
-            pltpu.SemaphoreType.DMA((n, k)),
-        ],
         compiler_params=pltpu.CompilerParams(vmem_limit_bytes=VMEM_BYTES),
         cost_estimate=pl.CostEstimate(
             flops=2 * batch * k * width * n * columns,
@@ -435,15 +435,12 @@
     gram_ref, whole_ref = refs[n + 1 :]
     batch, columns = norms[0].shape
     height = grams[0].shape[0] // 2
-    few = height // n
     for i in range(k):
         for step in range(n):
             at = ((place_ref[2] ^ i) * n + (place_ref[1] ^ step)) * height
-            for plane in range(n):
-                for view in range(2):
-                    to = pl.ds(pl.multiple_of(at + plane * few, few), few)
-                    first = (plane * 2 + view) * few
-                    gram_ref[view, to, :] = grams[i * n + step][first : first + few, :]
+            to = pl.ds(pl.multiple_of(at, height), height)
+            for view in range(2):
+                gram_ref[view, to, :] = grams[i * n + step][view * height : (view + 1) * height, :]
     edge = batch - 128
     tail = gram_ref[1, edge:, :128].astype(F32)
     row = lax.broadcasted_iota(jnp.int32, tail.shape, 0)
@@ -497,42 +494,55 @@
 def with_kernels(place, h_first, h_second, weight):
     n, k, z, a, b = place.n, place.k, place.z, place.a, place.b
     place_array = jnp.stack([z, a, b]).astype(jnp.int32)
-    first, second = spread(place, place_array, (h_first, h_second))
-
-    def projected(values, weight, few):
-        met = met_rows(place, values, few)
-        own = [jnp.concatenate(met, 0)] if few else met
+    first = to_columns(place, h_first)
+    first, held = lax.optimization_barrier((first, fetch(weight)))
+    first, second = lax.optimization_barrier((to_planes(place, first), to_columns(place, h_second)))
+    met, second = lax.optimization_barrier(
+        (met_rows(place, lay(place, place_array, first)), to_planes(place, second))
+    )
+
+    def projected(met, held, whole):
+        own = [jnp.concatenate(met, 0)] if whole else met
         others = [place.send(part, lambda z, a, b: (z, a, b ^ 1)) for part in own]
-        return project(place, place_array, [met, others], weight)
+        return project(place, place_array, [met, others], held)
+
+    def second_projected(weight, *parts):
+        return projected(met_rows(place, lay(place, place_array, parts), True), fetch(weight), True)
 
     def sent(parts):
         return sends(place, "z", [parts[0], *parts])[1:]
 
-    own_1, parts_1 = projected(first, weight, False)
+    own_1, parts_1 = projected(met, held, False)
     second, own_1 = lax.optimization_barrier((second, own_1))
     parts_1 = sent(parts_1)
-    own_2, parts_2 = in_one(
-        place, lambda values, weight: projected(values, weight, True), (second, weight)
-    )
+    own_2, parts_2 = in_one(place, second_projected, (weight, *second))
     own_1, own_2 = lax.optimization_barrier((own_1, own_2))
     parts_2 = sent(parts_2)
     norm_1, packed_1, scale_1, *grams = normalize_parts(place, place_array, own_1, parts_1)
-    met_1 = in_one(place, lambda *grams: plane_rows(place, place_array, grams, True), grams)
+    met_1 = in_one(place, lambda *grams: first_rows(place, place_array, grams), grams)
     met_1 = sends(place, "z", met_1)
     own_2, parts_2, met_1 = lax.optimization_barrier((own_2, parts_2, met_1))
     norm_2, packed_2, scale_2, *grams, coeff = normalize_parts(
         place, place_array, own_2, parts_2, norm_1
     )
-    met_2 = sends(place, "z", plane_rows(place, place_array, grams))
-    rows, batch = 2 * met_2[0].shape[0], h_first.shape[0] * n
+    height, batch = met_1[0].shape
+    (rows_1,) = local(rows_kernel, place_array, met_1, [((height, batch), BF16)], "rows")
+    met_2 = plane_rows(place, place_array, grams)
+    rows = met_2[0].shape[0]
+    (part,) = local(
+        functools.partial(code_kernel, n=n),
+        place_array,
+        (*met_2, rows_1),
+        [((rows + rows // SHARED + height, batch), BF16)],
+        "code",
+    )
     (part,) = local(
         functools.partial(finish_kernel, n=n, k=k),
         place_array,
-        (*met_1, *met_2),
-        [((rows, batch), BF16)],
+        sends(place, "z", [part] * n),
+        [((2 * rows, batch), BF16)],
         "finish",
     )
-    part = jnp.concatenate(ordered(sends(place, "z", [part] * n), z), 0)
     grams = sends(place, "a", [part] * n)
     grams += [place.send(part, lambda z, a, b: (z, a, b ^ 1)) for part in grams]
     *parts, loss = gradient(

time: 177 us -> 166 us (0.938)
  waiting for transfers between devices: 89.9 us -> 68.7 us
  starting transfers between devices: 53.5 us -> 61.9 us
  local copies, waits for them, and re-layouts: 1.9 us -> 6.08 us
  Pallas kernels: 30.8 us -> 27.9 us
    ppermute x50 -> x53, waiting for transfers between devices: 89.9 us -> 68.7 us  [send(): return lax.ppermute(value, ('dp', 'mp'), pairs)]
    ppermute x50 -> x53, starting transfers between devices: 53.5 us -> 61.9 us  [send(): return lax.ppermute(value, ('dp', 'mp'), pairs)]
    pallas_call x2, Pallas kernels: 15.7 us -> 8.32 us  [project(): pl.pallas_call(functools.partial(project_kernel, counts=counts, n=n, k=k)...]
    pallas_call x1 -> x2, Pallas kernels: 1.32 us -> 4.39 us  [fetch(): pl.pallas_call(fetch_kernel, in_specs=[pl.BlockSpec(memory_space=pl.ANY)]...]
    unnamed x4, local copies, waits for them, and re-layouts: 1.9 us -> 4.17 us
    squeeze x0 -> x2, local copies, waits for them, and re-layouts: none -> 1.91 us  [pick(): return lax.dynamic_index_in_dim(value, index, 0, keepdims=False)]
    pallas_call x8 -> x10, Pallas kernels: 7.45 us -> 8.93 us  [local(): pl.pallas_call(kernel, in_specs=[pl.BlockSpec(memory_space=pltpu.SMEM)] +...]
  transfers between devices with their start and end apart: 50 -> 53, of which waited for: 30 -> 28; matrix products, arithmetic and copies ran while one was open for 0% -> 1% of each run, Pallas kernels for 7% -> 9%
where the time goes in v4:
time: 166 us
  waiting for transfers between devices  68.7 us (41%)
  starting transfers between devices  61.9 us (37%)
  Pallas kernels  27.9 us (17%)
  local copies, waits for them, and re-layouts  6.08 us (4%)
    ppermute x53, waiting for transfers between devices, send(): return lax.ppermute(value, ('dp', 'mp'), pairs)  68.7 us
    ppermute x53, starting transfers between devices, send(): return lax.ppermute(value, ('dp', 'mp'), pairs)  61.9 us
    pallas_call x10, Pallas kernels, local(): pl.pallas_call(kernel, in_specs=[pl.BlockSpec(memory_space=pltpu.SMEM)] +...  8.93 us
    pallas_call x2, Pallas kernels, project(): pl.pallas_call(functools.partial(project_kernel, counts=counts, n=n, k=k)...  8.32 us
    pallas_call x2, Pallas kernels, normalize_parts(): pl.pallas_call(functools.partial(normalize_kernel, n=n, k=k, second=secon...  6.29 us
    pallas_call x2, Pallas kernels, fetch(): pl.pallas_call(fetch_kernel, in_specs=[pl.BlockSpec(memory_space=pl.ANY)]...  4.39 us
    unnamed x4, local copies, waits for them, and re-layouts  4.17 us
  transfers between devices with their start and end apart: 53, of which 28 were waited for; matrix products, arithmetic and copies ran while one was open for 1% of the time, Pallas kernels for 9%

profile of v4, /device:TPU:0, one launch (start us, length us, event | category | flops | bytes accessed | tf_op | source)
XLA Modules:
  0.0 165.6 jit_solution(180280508960428793)
XLA Ops:
  0.7 1.0 dynamic-slice_bitcast_fusion.4
  1.6 4.0 %collective-permute-start.10 = (bf16[32,1024]{1,0:T(8,128)(2,1)S(1)}, bf16[32,1024]{1,0:T(8,128)(2,1)S(1)}, u32[]{:S(2)}, u32[]{:S(2)}) collective-permute-start(bf16[32,1024]{1,0:T(8,128)(2,1)S(1)} %get-tuple-element.190), channel_id=1, source_target_pairs={{0,6},{1,7},{2,4},{3,5},{4,2},{5,3},{6,0},{7,1},{8,14},{9,15},{10,... | collective-permute-start | bytes 196616 | tf_op jit(solution)/shard_map/ppermute | solution.py:40
  6.2 1.0 dynamic-slice_bitcast_fusion
  7.2 2.9 %collective-permute-start.16 = (bf16[32,1024]{1,0:T(8,128)(2,1)S(1)}, bf16[32,1024]{1,0:T(8,128)(2,1)S(1)}, u32[]{:S(2)}, u32[]{:S(2)}) collective-permute-start(bf16[32,1024]{1,0:T(8,128)(2,1)S(1)} %get-tuple-element.182), channel_id=1, source_target_pairs={{0,6},{1,7},{2,4},{3,5},{4,2},{5,3},{6,0},{7,1},{8,14},{9,15},{10,... | collective-permute-start | bytes 196616 | tf_op jit(solution)/shard_map/ppermute | solution.py:40
  10.6 2.2 %fetch.3.refs_8_ = bf16[2048,1024]{1,0:T(8,128)(2,1)S(1)} custom-call(bf16[2048,1024]{1,0:T(8,128)(2,1)} %weight_ref.1), custom_call_target="tpu_custom_call" | custom-call | bytes 8388608 | tf_op jit(solution)/shard_map/fetch/pallas_call | solution.py:224
  12.8 2.0 %copy-done = bf16[2048,1024]{1,0:T(8,128)(2,1)} copy-done((bf16[2048,1024]{1,0:T(8,128)(2,1)}, bf16[2048,1024]{1,0:T(8,128)(2,1)S(1)}, u32[]{:S(2)}) %copy-start) | copy-done | bytes 4194328
  15.0 4.1 %collective-permute-start.13 = (bf16[32,1024]{1,0:T(8,128)(2,1)S(1)}, bf16[32,1024]{1,0:T(8,128)(2,1)S(1)}, u32[]{:S(2)}, u32[]{:S(2)}) collective-permute-start(bf16[32,1024]{1,0:T(8,128)(2,1)S(1)} %get-tuple-element.186), channel_id=1, source_target_pairs={{0,24},{1,25},{2,26},{3,27},{4,28},{5,29},{6,30},{7,31},{8,16},{9,... | collective-permute-start | bytes 196616 | tf_op jit(solution)/shard_map/ppermute | solution.py:40
  19.8 1.6 collective-permute-done.13.refs_3_
  21.4 1.9 %collective-permute-done.11.refs_1_ = bf16[32,1024]{1,0:T(8,128)(2,1)S(1)} collective-permute-done((bf16[32,1024]{1,0:T(8,128)(2,1)S(1)}, bf16[32,1024]{1,0:T(8,128)(2,1)S(1)}, u32[]{:S(2)}, u32[]{:S(2)}) %collective-permute-start.11) | collective-permute-done | bytes 65568 | tf_op jit(solution)/shard_map/ppermute | solution.py:40
  23.3 0.9 collective-permute-done.12.refs_2_
  24.8 2.5 %collective-permute-start.19 = (bf16[128,1024]{1,0:T(8,128)(2,1)S(1)}, bf16[128,1024]{1,0:T(8,128)(2,1)S(1)}, u32[]{:S(2)}, u32[]{:S(2)}) collective-permute-start(bf16[128,1024]{1,0:T(8,128)(2,1)S(1)} %lay.3.refs_0_), channel_id=1, source_target_pairs={{0,6},{1,7},{2,4},{3,5},{4,2},{5,3},{6,0},{7,1},{8,14},{9,15},{10,... | collective-permute-start | bytes 786440 | tf_op jit(solution)/shard_map/ppermute | solution.py:40
  28.4 1.7 %collective-permute-start.22 = (bf16[32,1024]{1,0:T(8,128)(2,1)S(1)}, bf16[32,1024]{1,0:T(8,128)(2,1)S(1)}, u32[]{:S(2)}, u32[]{:S(2)}) collective-permute-start(bf16[32,1024]{1,0:T(8,128)(2,1)S(1)} %get-tuple-element.178), channel_id=1, source_target_pairs={{0,24},{1,25},{2,26},{3,27},{4,28},{5,29},{6,30},{7,31},{8,16},{9,... | collective-permute-start | bytes 196616 | tf_op jit(solution)/shard_map/ppermute | solution.py:40
  30.5 4.2 %collective-permute-done.22 = bf16[32,1024]{1,0:T(8,128)(2,1)S(1)} collective-permute-done((bf16[32,1024]{1,0:T(8,128)(2,1)S(1)}, bf16[32,1024]{1,0:T(8,128)(2,1)S(1)}, u32[]{:S(2)}, u32[]{:S(2)}) %collective-permute-start.22) | collective-permute-done | bytes 65568 | tf_op jit(solution)/shard_map/ppermute | solution.py:40
  35.5 4.4 %collective-permute-done.21 = bf16[32,1024]{1,0:T(8,128)(2,1)S(1)} collective-permute-done((bf16[32,1024]{1,0:T(8,128)(2,1)S(1)}, bf16[32,1024]{1,0:T(8,128)(2,1)S(1)}, u32[]{:S(2)}, u32[]{:S(2)}) %collective-permute-start.21) | collective-permute-done | bytes 65568 | tf_op jit(solution)/shard_map/ppermute | solution.py:40
  42.7 2.2 %copy-done.1 = bf16[2048,1024]{1,0:T(8,128)(2,1)S(1)} copy-done((bf16[2048,1024]{1,0:T(8,128)(2,1)S(1)}, bf16[2048,1024]{1,0:T(8,128)(2,1)}, u32[]{:S(2)}) %copy-start.1) | copy-done | bytes 4194328
  44.9 3.8 %project.3 = (f32[512,256]{1,0:T(8,128)S(1)}, bf16[640,256]{1,0:T(8,128)(2,1)S(1)}, bf16[640,256]{1,0:T(8,128)(2,1)S(1)}, bf16[640,256]{1,0:T(8,128)(2,1)S(1)}) custom-call(s32[3]{0:T(128)S(1)} %pad_add_fusion.place_ref, bf16[128,1024]{1,0:T(8,128)(2,1)S(1)} %lay.3.refs_0_, bf16[128,1024]{1,0:T(8,128)(2,1)S(1)} %collective-permute-done.17.refs_1_, ...), custom_call_target="tpu_custom_call" | custom-call | flops 2147483648 | bytes 7864320 | tf_op jit(solution)/shard_map/project/pallas_call | solution.py:337
  48.6 1.8 %collective-permute-start.30 = (bf16[640,256]{1,0:T(8,128)(2,1)S(1)}, bf16[640,256]{1,0:T(8,128)(2,1)S(1)}, u32[]{:S(2)}, u32[]{:S(2)}) collective-permute-start(bf16[640,256]{1,0:T(8,128)(2,1)S(1)} %get-tuple-element.141), channel_id=1, source_target_pairs={{0,8},{1,9},{2,10},{3,11},{4,12},{5,13},{6,14},{7,15},{8,0},{9,1},... | collective-permute-start | bytes 983048 | tf_op jit(solution)/shard_map/ppermute | solution.py:40
  50.4 1.2 collective-permute-start.31
  51.6 1.5 collective-permute-start.32
  53.1 23.1 %conditional.2 = ((f32[512,256]{1,0:T(8,128)}, bf16[640,256]{1,0:T(8,128)(2,1)}, bf16[640,256]{1,0:T(8,128)(2,1)}, bf16[640,256]{1,0:T(8,128)(2,1)})) conditional(s32[]{:T(128)} %convert_element_type.4, () %tuple.34, (s32[3]{0:T(128)S(1)}, bf16[32,1024]{1,0:T(8,128)(2,1)S(1)}, bf16[32,1024]{1,0:T(8,128)(2,1)S(1)}, bf16[32,1024]{1,0:T(8,128)(2,1)S(1)}, ...), branch_computations={%region_0.1_spmd, %region_1.2_spmd} | conditional | flops 2151677952 | bytes 25690280 | solution.py:191
  53.6 1.5 collective-permute-start.4
  55.2 1.5 collective-permute-start.5
  56.7 4.6 %collective-permute-done.4.refs_1_ = bf16[128,1024]{1,0:T(8,128)(2,1)S(1)} collective-permute-done((bf16[128,1024]{1,0:T(8,128)(2,1)S(1)}, bf16[128,1024]{1,0:T(8,128)(2,1)S(1)}, u32[]{:S(2)}, u32[]{:S(2)}) %collective-permute-start.4) | collective-permute-done | bytes 262176 | tf_op jit(solution)/shard_map/cond/branch_1_fun/ppermute | solution.py:40
  61.3 2.4 %collective-permute-start.6 = (bf16[128,1024]{1,0:T(8,128)(2,1)S(1)}, bf16[128,1024]{1,0:T(8,128)(2,1)S(1)}, u32[]{:S(2)}, u32[]{:S(2)}) collective-permute-start(bf16[128,1024]{1,0:T(8,128)(2,1)S(1)} %lay.2.refs_0_), channel_id=1, source_target_pairs={{0,6},{1,7},{2,4},{3,5},{4,2},{5,3},{6,0},{7,1},{8,14},{9,15},{10,... | collective-permute-start | bytes 786440 | tf_op jit(solution)/shard_map/cond/branch_1_fun/ppermute | solution.py:40
  63.7 5.1 %collective-permute-done.6.refs_3_ = bf16[128,1024]{1,0:T(8,128)(2,1)S(1)} collective-permute-done((bf16[128,1024]{1,0:T(8,128)(2,1)S(1)}, bf16[128,1024]{1,0:T(8,128)(2,1)S(1)}, u32[]{:S(2)}, u32[]{:S(2)}) %collective-permute-start.6) | collective-permute-done | bytes 262176 | tf_op jit(solution)/shard_map/cond/branch_1_fun/ppermute | solution.py:40
  69.0 2.2 %fetch.2.refs_5_ = bf16[2048,1024]{1,0:T(8,128)(2,1)S(1)} custom-call(bf16[2048,1024]{1,0:T(8,128)(2,1)} %get-tuple-element.25.weight_ref), custom_call_target="tpu_custom_call" | custom-call | bytes 8388608 | tf_op jit(solution)/shard_map/cond/branch_1_fun/fetch/pallas_call | solution.py:224
  71.6 4.6 %project.2 = (f32[512,256]{1,0:T(8,128)}, bf16[640,256]{1,0:T(8,128)(2,1)}, bf16[640,256]{1,0:T(8,128)(2,1)}, bf16[640,256]{1,0:T(8,128)(2,1)}) custom-call(s32[3]{0:T(128)S(1)} %get-tuple-element.18.place_ref, bf16[128,1024]{1,0:T(8,128)(2,1)S(1)} %lay.2.refs_0_, bf16[128,1024]{1,0:T(8,128)(2,1)S(1)} %collective-permute-done.4.refs_1_, ...), custom_call_target="tpu_custom_call" | custom-call | flops 2147483648 | bytes 7864320 | tf_op jit(solution)/shard_map/cond/branch_1_fun/project/pallas_call | solution.py:337
  76.9 2.1 %collective-permute-start.28 = (bf16[640,256]{1,0:T(8,128)(2,1)}, bf16[640,256]{1,0:T(8,128)(2,1)S(1)}, u32[]{:S(2)}, u32[]{:S(2)}) collective-permute-start(bf16[640,256]{1,0:T(8,128)(2,1)} %get-tuple-element.138), channel_id=1, source_target_pairs={{0,16},{1,17},{2,18},{3,19},{4,20},{5,21},{6,22},{7,23},{8,24},{9,... | collective-permute-start | bytes 983048 | tf_op jit(solution)/shard_map/ppermute | solution.py:40
  79.0 1.6 collective-permute-start.29
  80.6 3.2 %normalize.2 = (f32[512,256]{1,0:T(8,128)S(1)}, bf16[512,256]{1,0:T(8,128)(2,1)S(1)}, f32[1,256]{1,0:T(1,128)S(1)}, f32[256,512]{1,0:T(8,128)}, f32[256,512]{1,0:T(8,128)}) custom-call(s32[3]{0:T(128)S(1)} %pad_add_fusion.place_ref, f32[512,256]{1,0:T(8,128)S(1)} %get-tuple-element.140.refs_0_, bf16[640,256]{1,0:T(8,128)(2,1)S(1)} %collective-permute-done.30.refs_1_, ...), custom_call_target="tpu_custom_call" | custom-call | flops 134217728 | bytes 3145728 | tf_op jit(solution)/shard_map/normalize/pallas_call | solution.py:416
  83.8 15.3 %conditional.3 = ((f32[16,512]{1,0:T(8,128)S(1)}, f32[16,512]{1,0:T(8,128)S(1)}, f32[16,512]{1,0:T(8,128)S(1)}, f32[16,512]{1,0:T(8,128)S(1)})) conditional(s32[]{:T(128)} %convert_element_type.4, () %tuple.37, (f32[256,512]{1,0:T(8,128)}, s32[3]{0:T(128)S(1)}, f32[256,512]{1,0:T(8,128)}) %tuple.38), branch_computations={%region_2.3_spmd, %region_3.4_spmd} | conditional | bytes 3670184 | solution.py:191
  83.8 2.1 %collective-permute-done.met_ref = f32[256,512]{1,0:T(8,128)S(1)} collective-permute-done((f32[256,512]{1,0:T(8,128)}, f32[256,512]{1,0:T(8,128)S(1)}, u32[]{:S(2)}, u32[]{:S(2)}) %collective-permute-start) | collective-permute-done | bytes 524320 | tf_op jit(solution)/shard_map/cond/branch_1_fun/ppermute | solution.py:40
  86.0 1.1 halve.2
  87.1 1.6 collective-permute-start.1
  88.6 1.5 collective-permute-start.2
  90.2 2.5 %collective-permute-done.1.refs_1_ = f32[64,512]{1,0:T(8,128)S(1)} collective-permute-done((f32[64,512]{1,0:T(8,128)S(1)}, f32[64,512]{1,0:T(8,128)S(1)}, u32[]{:S(2)}, u32[]{:S(2)}) %collective-permute-start.1) | collective-permute-done | bytes 131104 | tf_op jit(solution)/shard_map/cond/branch_1_fun/ppermute | solution.py:40
  92.7 2.5 %collective-permute-start.3 = (f32[64,512]{1,0:T(8,128)S(1)}, f32[64,512]{1,0:T(8,128)S(1)}, u32[]{:S(2)}, u32[]{:S(2)}) collective-permute-start(f32[64,512]{1,0:T(8,128)S(1)} %get-tuple-element.34), channel_id=1, source_target_pairs={{0,6},{1,7},{2,4},{3,5},{4,2},{5,3},{6,0},{7,1},{8,14},{9,15},{10,... | collective-permute-start | bytes 393224 | tf_op jit(solution)/shard_map/cond/branch_1_fun/ppermute | solution.py:40
  95.2 3.4 %collective-permute-done.3.refs_3_ = f32[64,512]{1,0:T(8,128)S(1)} collective-permute-done((f32[64,512]{1,0:T(8,128)S(1)}, f32[64,512]{1,0:T(8,128)S(1)}, u32[]{:S(2)}, u32[]{:S(2)}) %collective-permute-start.3) | collective-permute-done | bytes 131104 | tf_op jit(solution)/shard_map/cond/branch_1_fun/ppermute | solution.py:40
  99.1 3.0 %collective-permute-start.33 = (f32[16,512]{1,0:T(8,128)S(1)}, f32[16,512]{1,0:T(8,128)S(1)}, u32[]{:S(2)}, u32[]{:S(2)}) collective-permute-start(f32[16,512]{1,0:T(8,128)S(1)} %get-tuple-element.147), channel_id=1, source_target_pairs={{0,8},{1,9},{2,10},{3,11},{4,12},{5,13},{6,14},{7,15},{8,0},{9,1},... | collective-permute-start | bytes 98312 | tf_op jit(solution)/shard_map/ppermute | solution.py:40
  102.2 2.4 %collective-permute-start.35 = (f32[16,512]{1,0:T(8,128)S(1)}, f32[16,512]{1,0:T(8,128)S(1)}, u32[]{:S(2)}, u32[]{:S(2)}) collective-permute-start(f32[16,512]{1,0:T(8,128)S(1)} %get-tuple-element.149), channel_id=1, source_target_pairs={{0,24},{1,25},{2,26},{3,27},{4,28},{5,29},{6,30},{7,31},{8,16},{9,... | collective-permute-start | bytes 98312 | tf_op jit(solution)/shard_map/ppermute | solution.py:40
  104.6 7.9 %collective-permute-done.34.refs_2_ = f32[16,512]{1,0:T(8,128)S(1)} collective-permute-done((f32[16,512]{1,0:T(8,128)S(1)}, f32[16,512]{1,0:T(8,128)S(1)}, u32[]{:S(2)}, u32[]{:S(2)}) %collective-permute-start.34) | collective-permute-done | bytes 32800 | tf_op jit(solution)/shard_map/ppermute | solution.py:40
  112.5 3.1 %normalize.3 = (f32[512,256]{1,0:T(8,128)S(1)}, bf16[512,256]{1,0:T(8,128)(2,1)S(1)}, f32[1,256]{1,0:T(1,128)S(1)}, f32[256,512]{1,0:T(8,128)S(1)}, f32[256,512]{1,0:T(8,128)S(1)}, /*index=5*/f32[1,256]{1,0:T(1,128)S(1)}) custom-call(s32[3]{0:T(128)S(1)} %pad_add_fusion.place_ref, f32[512,256]{1,0:T(8,128)} %get-tuple-element.150.refs_0_, ...), custom_call_target="tpu_custom_call" | custom-call | flops 134217728 | bytes 3145728 | tf_op jit(solution)/shard_map/normalize/pallas_call | solution.py:416
  115.6 1.9 %collective-permute-done.36.met_ref = f32[256,512]{1,0:T(8,128)S(1)} collective-permute-done((f32[256,512]{1,0:T(8,128)S(1)}, f32[256,512]{1,0:T(8,128)S(1)}, u32[]{:S(2)}, u32[]{:S(2)}) %collective-permute-start.36) | collective-permute-done | bytes 524320 | tf_op jit(solution)/shard_map/ppermute | solution.py:40
  118.1 1.5 collective-permute-start.37
  119.7 1.5 collective-permute-start.38
  122.2 1.9 %collective-permute-done.37.refs_1_ = f32[64,512]{1,0:T(8,128)S(1)} collective-permute-done((f32[64,512]{1,0:T(8,128)S(1)}, f32[64,512]{1,0:T(8,128)S(1)}, u32[]{:S(2)}, u32[]{:S(2)}) %collective-permute-start.37) | collective-permute-done | bytes 131104 | tf_op jit(solution)/shard_map/ppermute | solution.py:40
  124.1 3.6 %collective-permute-done.38.refs_2_ = f32[64,512]{1,0:T(8,128)S(1)} collective-permute-done((f32[64,512]{1,0:T(8,128)S(1)}, f32[64,512]{1,0:T(8,128)S(1)}, u32[]{:S(2)}, u32[]{:S(2)}) %collective-permute-start.38) | collective-permute-done | bytes 131104 | tf_op jit(solution)/shard_map/ppermute | solution.py:40
  128.4 1.0 collective-permute-start.42
  129.4 1.4 collective-permute-start.41
  130.8 2.0 %collective-permute-start.40 = (bf16[96,512]{1,0:T(8,128)(2,1)S(1)}, bf16[96,512]{1,0:T(8,128)(2,1)S(1)}, u32[]{:S(2)}, u32[]{:S(2)}) collective-permute-start(bf16[96,512]{1,0:T(8,128)(2,1)S(1)} %code.1.refs_0_), channel_id=1, source_target_pairs={{0,8},{1,9},{2,10},{3,11},{4,12},{5,13},{6,14},{7,15},{8,0},{9,1},... | collective-permute-start | bytes 294920 | tf_op jit(solution)/shard_map/ppermute | solution.py:40
  132.9 3.1 %collective-permute-done.42.refs_3_ = bf16[96,512]{1,0:T(8,128)(2,1)S(1)} collective-permute-done((bf16[96,512]{1,0:T(8,128)(2,1)S(1)}, bf16[96,512]{1,0:T(8,128)(2,1)S(1)}, u32[]{:S(2)}, u32[]{:S(2)}) %collective-permute-start.42) | collective-permute-done | bytes 98336 | tf_op jit(solution)/shard_map/ppermute | solution.py:40
  136.0 2.9 %collective-permute-done.41.refs_2_ = bf16[96,512]{1,0:T(8,128)(2,1)S(1)} collective-permute-done((bf16[96,512]{1,0:T(8,128)(2,1)S(1)}, bf16[96,512]{1,0:T(8,128)(2,1)S(1)}, u32[]{:S(2)}, u32[]{:S(2)}) %collective-permute-start.41) | collective-permute-done | bytes 98336 | tf_op jit(solution)/shard_map/ppermute | solution.py:40
  138.9 1.0 finish.1.refs_0_
  139.9 1.7 %collective-permute-start.45 = (bf16[128,512]{1,0:T(8,128)(2,1)S(1)}, bf16[128,512]{1,0:T(8,128)(2,1)S(1)}, u32[]{:S(2)}, u32[]{:S(2)}) collective-permute-start(bf16[128,512]{1,0:T(8,128)(2,1)S(1)} %finish.1.refs_0_), channel_id=1, source_target_pairs={{0,6},{1,7},{2,4},{3,5},{4,2},{5,3},{6,0},{7,1},{8,14},{9,15},{10,... | collective-permute-start | bytes 393224 | tf_op jit(solution)/shard_map/ppermute | solution.py:40
  141.6 1.5 collective-permute-start.44
  143.4 3.0 %collective-permute-done.45.refs_3_ = bf16[128,512]{1,0:T(8,128)(2,1)S(1)} collective-permute-done((bf16[128,512]{1,0:T(8,128)(2,1)S(1)}, bf16[128,512]{1,0:T(8,128)(2,1)S(1)}, u32[]{:S(2)}, u32[]{:S(2)}) %collective-permute-start.45) | collective-permute-done | bytes 131104 | tf_op jit(solution)/shard_map/ppermute | solution.py:40
  146.4 1.2 collective-permute-done.44.refs_2_
  148.1 0.8 collective-permute-done.48.refs_6_
  149.4 1.9 %gradient.1 = (bf16[256,256]{1,0:T(8,128)(2,1)S(1)}, bf16[256,256]{1,0:T(8,128)(2,1)S(1)}, bf16[256,256]{1,0:T(8,128)(2,1)S(1)}, bf16[256,256]{1,0:T(8,128)(2,1)S(1)}, f32[1,1]{1,0:T(1,128)}) custom-call(s32[3]{0:T(128)S(1)} %pad_add_fusion.place_ref, bf16[128,512]{1,0:T(8,128)(2,1)S(1)} %finish.1.refs_0_, ...), custom_call_target="tpu_custom_call" | custom-call | tf_op jit(solution)/shard_map/gradient/pallas_call | solution.py:151
  151.3 2.2 %collective-permute-start.51 = (bf16[256,256]{1,0:T(8,128)(2,1)S(1)}, bf16[256,256]{1,0:T(8,128)(2,1)S(1)}, u32[]{:S(2)}, u32[]{:S(2)}) collective-permute-start(bf16[256,256]{1,0:T(8,128)(2,1)S(1)} %get-tuple-element.173), channel_id=1, source_target_pairs={{0,16},{1,17},{2,18},{3,19},{4,20},{5,21},{6,22},{7,23},{8,24},{9,... | collective-permute-start | bytes 393224 | tf_op jit(solution)/shard_map/ppermute | solution.py:40
  153.6 2.2 %collective-permute-start.52 = (bf16[256,256]{1,0:T(8,128)(2,1)S(1)}, bf16[256,256]{1,0:T(8,128)(2,1)S(1)}, u32[]{:S(2)}, u32[]{:S(2)}) collective-permute-start(bf16[256,256]{1,0:T(8,128)(2,1)S(1)} %get-tuple-element.174), channel_id=1, source_target_pairs={{0,24},{1,25},{2,26},{3,27},{4,28},{5,29},{6,30},{7,31},{8,16},{9,... | collective-permute-start | bytes 393224 | tf_op jit(solution)/shard_map/ppermute | solution.py:40
  155.7 3.1 %collective-permute-done.50.refs_1_ = bf16[256,256]{1,0:T(8,128)(2,1)S(1)} collective-permute-done((bf16[256,256]{1,0:T(8,128)(2,1)S(1)}, bf16[256,256]{1,0:T(8,128)(2,1)S(1)}, u32[]{:S(2)}, u32[]{:S(2)}) %collective-permute-start.50) | collective-permute-done | bytes 131104 | tf_op jit(solution)/shard_map/ppermute | solution.py:40
  158.8 5.4 %collective-permute-done.51.refs_2_ = bf16[256,256]{1,0:T(8,128)(2,1)S(1)} collective-permute-done((bf16[256,256]{1,0:T(8,128)(2,1)S(1)}, bf16[256,256]{1,0:T(8,128)(2,1)S(1)}, u32[]{:S(2)}, u32[]{:S(2)}) %collective-permute-start.51) | collective-permute-done | bytes 131104 | tf_op jit(solution)/shard_map/ppermute | solution.py:40
  164.2 1.4 place.1
  (70 shorter events, 13.8 us)
Async XLA Ops:
  1.6 13.2 %collective-permute-start.10 = (bf16[32,1024]{1,0:T(8,128)(2,1)S(1)}, bf16[32,1024]{1,0:T(8,128)(2,1)S(1)}, u32[]{:S(2)}, u32[]{:S(2)}) collective-permute-start(bf16[32,1024]{1,0:T(8,128)(2,1)S(1)} %get-tuple-element.190), channel_id=1, source_target_pairs={{0,6},{1,7},{2,4},{3,5},{4,2},{5,3},{6,0},{7,1},{8,14},{9,15},{10,... | collective-permute-start | bytes 196616 | tf_op jit(solution)/shard_map/ppermute | solution.py:40
  5.6 9.4 %collective-permute-start.9 = (bf16[32,1024]{1,0:T(8,128)(2,1)S(1)}, bf16[32,1024]{1,0:T(8,128)(2,1)S(1)}, u32[]{:S(2)}, u32[]{:S(2)}) collective-permute-start(bf16[32,1024]{1,0:T(8,128)(2,1)S(1)} %get-tuple-element.191), channel_id=1, source_target_pairs={{0,4},{1,5},{2,6},{3,7},{4,0},{5,1},{6,2},{7,3},{8,12},{9,13},{10,... | collective-permute-start | bytes 196616 | tf_op jit(solution)/shard_map/ppermute | solution.py:40
  6.1 8.8 %collective-permute-start.8 = (bf16[32,1024]{1,0:T(8,128)(2,1)S(1)}, bf16[32,1024]{1,0:T(8,128)(2,1)S(1)}, u32[]{:S(2)}, u32[]{:S(2)}) collective-permute-start(bf16[32,1024]{1,0:T(8,128)(2,1)S(1)} %get-tuple-element.192), channel_id=1, source_target_pairs={{0,2},{1,3},{2,0},{3,1},{4,6},{5,7},{6,4},{7,5},{8,10},{9,11},{10,... | collective-permute-start | bytes 196616 | tf_op jit(solution)/shard_map/ppermute | solution.py:40
  7.2 11.9 %collective-permute-start.16 = (bf16[32,1024]{1,0:T(8,128)(2,1)S(1)}, bf16[32,1024]{1,0:T(8,128)(2,1)S(1)}, u32[]{:S(2)}, u32[]{:S(2)}) collective-permute-start(bf16[32,1024]{1,0:T(8,128)(2,1)S(1)} %get-tuple-element.182), channel_id=1, source_target_pairs={{0,6},{1,7},{2,4},{3,5},{4,2},{5,3},{6,0},{7,1},{8,14},{9,15},{10,... | collective-permute-start | bytes 196616 | tf_op jit(solution)/shard_map/ppermute | solution.py:40
  10.1 9.7 %collective-permute-start.15 = (bf16[32,1024]{1,0:T(8,128)(2,1)S(1)}, bf16[32,1024]{1,0:T(8,128)(2,1)S(1)}, u32[]{:S(2)}, u32[]{:S(2)}) collective-permute-start(bf16[32,1024]{1,0:T(8,128)(2,1)S(1)} %get-tuple-element.183), channel_id=1, source_target_pairs={{0,4},{1,5},{2,6},{3,7},{4,0},{5,1},{6,2},{7,3},{8,12},{9,13},{10,... | collective-permute-start | bytes 196616 | tf_op jit(solution)/shard_map/ppermute | solution.py:40
  12.8 2.0 %copy-start = (bf16[2048,1024]{1,0:T(8,128)(2,1)}, bf16[2048,1024]{1,0:T(8,128)(2,1)S(1)}, u32[]{:S(2)}) copy-start(bf16[2048,1024]{1,0:T(8,128)(2,1)S(1)} %fetch.3.refs_8_) | copy-start | bytes 12582916
  14.8 5.0 %collective-permute-start.14 = (bf16[32,1024]{1,0:T(8,128)(2,1)S(1)}, bf16[32,1024]{1,0:T(8,128)(2,1)S(1)}, u32[]{:S(2)}, u32[]{:S(2)}) collective-permute-start(bf16[32,1024]{1,0:T(8,128)(2,1)S(1)} %get-tuple-element.184), channel_id=1, source_target_pairs={{0,2},{1,3},{2,0},{3,1},{4,6},{5,7},{6,4},{7,5},{8,10},{9,11},{10,... | collective-permute-start | bytes 196616 | tf_op jit(solution)/shard_map/ppermute | solution.py:40
  15.0 6.4 %collective-permute-start.13 = (bf16[32,1024]{1,0:T(8,128)(2,1)S(1)}, bf16[32,1024]{1,0:T(8,128)(2,1)S(1)}, u32[]{:S(2)}, u32[]{:S(2)}) collective-permute-start(bf16[32,1024]{1,0:T(8,128)(2,1)S(1)} %get-tuple-element.186), channel_id=1, source_target_pairs={{0,24},{1,25},{2,26},{3,27},{4,28},{5,29},{6,30},{7,31},{8,16},{9,... | collective-permute-start | bytes 196616 | tf_op jit(solution)/shard_map/ppermute | solution.py:40
  19.0 4.3 %collective-permute-start.11 = (bf16[32,1024]{1,0:T(8,128)(2,1)S(1)}, bf16[32,1024]{1,0:T(8,128)(2,1)S(1)}, u32[]{:S(2)}, u32[]{:S(2)}) collective-permute-start(bf16[32,1024]{1,0:T(8,128)(2,1)S(1)} %get-tuple-element.187), channel_id=1, source_target_pairs={{0,8},{1,9},{2,10},{3,11},{4,12},{5,13},{6,14},{7,15},{8,0},{9,1},... | collective-permute-start | bytes 196616 | tf_op jit(solution)/shard_map/ppermute | solution.py:40
  19.1 5.2 %collective-permute-start.12 = (bf16[32,1024]{1,0:T(8,128)(2,1)S(1)}, bf16[32,1024]{1,0:T(8,128)(2,1)S(1)}, u32[]{:S(2)}, u32[]{:S(2)}) collective-permute-start(bf16[32,1024]{1,0:T(8,128)(2,1)S(1)} %get-tuple-element.188), channel_id=1, source_target_pairs={{0,16},{1,17},{2,18},{3,19},{4,20},{5,21},{6,22},{7,23},{8,24},{9,... | collective-permute-start | bytes 196616 | tf_op jit(solution)/shard_map/ppermute | solution.py:40
  24.8 15.1 %collective-permute-start.19 = (bf16[128,1024]{1,0:T(8,128)(2,1)S(1)}, bf16[128,1024]{1,0:T(8,128)(2,1)S(1)}, u32[]{:S(2)}, u32[]{:S(2)}) collective-permute-start(bf16[128,1024]{1,0:T(8,128)(2,1)S(1)} %lay.3.refs_0_), channel_id=1, source_target_pairs={{0,6},{1,7},{2,4},{3,5},{4,2},{5,3},{6,0},{7,1},{8,14},{9,15},{10,... | collective-permute-start | bytes 786440 | tf_op jit(solution)/shard_map/ppermute | solution.py:40
  27.3 12.6 %collective-permute-start.18 = (bf16[128,1024]{1,0:T(8,128)(2,1)S(1)}, bf16[128,1024]{1,0:T(8,128)(2,1)S(1)}, u32[]{:S(2)}, u32[]{:S(2)}) collective-permute-start(bf16[128,1024]{1,0:T(8,128)(2,1)S(1)} %lay.3.refs_0_), channel_id=1, source_target_pairs={{0,4},{1,5},{2,6},{3,7},{4,0},{5,1},{6,2},{7,3},{8,12},{9,13},{10,... | collective-permute-start | bytes 786440 | tf_op jit(solution)/shard_map/ppermute | solution.py:40
  27.8 12.1 %collective-permute-start.17 = (bf16[128,1024]{1,0:T(8,128)(2,1)S(1)}, bf16[128,1024]{1,0:T(8,128)(2,1)S(1)}, u32[]{:S(2)}, u32[]{:S(2)}) collective-permute-start(bf16[128,1024]{1,0:T(8,128)(2,1)S(1)} %lay.3.refs_0_), channel_id=1, source_target_pairs={{0,2},{1,3},{2,0},{3,1},{4,6},{5,7},{6,4},{7,5},{8,10},{9,11},{10,... | collective-permute-start | bytes 786440 | tf_op jit(solution)/shard_map/ppermute | solution.py:40
  28.4 6.4 %collective-permute-start.22 = (bf16[32,1024]{1,0:T(8,128)(2,1)S(1)}, bf16[32,1024]{1,0:T(8,128)(2,1)S(1)}, u32[]{:S(2)}, u32[]{:S(2)}) collective-permute-start(bf16[32,1024]{1,0:T(8,128)(2,1)S(1)} %get-tuple-element.178), channel_id=1, source_target_pairs={{0,24},{1,25},{2,26},{3,27},{4,28},{5,29},{6,30},{7,31},{8,16},{9,... | collective-permute-start | bytes 196616 | tf_op jit(solution)/shard_map/ppermute | solution.py:40
  30.0 5.5 %collective-permute-start.20 = (bf16[32,1024]{1,0:T(8,128)(2,1)S(1)}, bf16[32,1024]{1,0:T(8,128)(2,1)S(1)}, u32[]{:S(2)}, u32[]{:S(2)}) collective-permute-start(bf16[32,1024]{1,0:T(8,128)(2,1)S(1)} %get-tuple-element.180), channel_id=1, source_target_pairs={{0,8},{1,9},{2,10},{3,11},{4,12},{5,13},{6,14},{7,15},{8,0},{9,1},... | collective-permute-start | bytes 196616 | tf_op jit(solution)/shard_map/ppermute | solution.py:40
  34.8 5.2 %collective-permute-start.21 = (bf16[32,1024]{1,0:T(8,128)(2,1)S(1)}, bf16[32,1024]{1,0:T(8,128)(2,1)S(1)}, u32[]{:S(2)}, u32[]{:S(2)}) collective-permute-start(bf16[32,1024]{1,0:T(8,128)(2,1)S(1)} %get-tuple-element.181), channel_id=1, source_target_pairs={{0,16},{1,17},{2,18},{3,19},{4,20},{5,21},{6,22},{7,23},{8,24},{9,... | collective-permute-start | bytes 196616 | tf_op jit(solution)/shard_map/ppermute | solution.py:40
  39.9 1.6 collective-permute-start.23
  40.0 1.9 %collective-permute-start.24 = (bf16[128,1024]{1,0:T(8,128)(2,1)S(1)}, bf16[128,1024]{1,0:T(8,128)(2,1)S(1)}, u32[]{:S(2)}, u32[]{:S(2)}) collective-permute-start(bf16[128,1024]{1,0:T(8,128)(2,1)S(1)} %collective-permute-done.17.refs_1_), channel_id=1, source_target_pairs={{0,1},{1,0},{2,3},{3,2},{4,5},{5,4},{6,7},{7,6},{8,9},{9,8},{10,11... | collective-permute-start | bytes 786440 | tf_op jit(solution)/shard_map/ppermute | solution.py:40
  40.5 1.8 %collective-permute-start.25 = (bf16[128,1024]{1,0:T(8,128)(2,1)S(1)}, bf16[128,1024]{1,0:T(8,128)(2,1)S(1)}, u32[]{:S(2)}, u32[]{:S(2)}) collective-permute-start(bf16[128,1024]{1,0:T(8,128)(2,1)S(1)} %collective-permute-done.18.refs_2_), channel_id=1, source_target_pairs={{0,1},{1,0},{2,3},{3,2},{4,5},{5,4},{6,7},{7,6},{8,9},{9,8},{10,11... | collective-permute-start | bytes 786440 | tf_op jit(solution)/shard_map/ppermute | solution.py:40
  40.6 2.1 %collective-permute-start.26 = (bf16[128,1024]{1,0:T(8,128)(2,1)S(1)}, bf16[128,1024]{1,0:T(8,128)(2,1)S(1)}, u32[]{:S(2)}, u32[]{:S(2)}) collective-permute-start(bf16[128,1024]{1,0:T(8,128)(2,1)S(1)} %collective-permute-done.19.refs_3_), channel_id=1, source_target_pairs={{0,1},{1,0},{2,3},{3,2},{4,5},{5,4},{6,7},{7,6},{8,9},{9,8},{10,11... | collective-permute-start | bytes 786440 | tf_op jit(solution)/shard_map/ppermute | solution.py:40
  42.7 2.2 %copy-start.1 = (bf16[2048,1024]{1,0:T(8,128)(2,1)S(1)}, bf16[2048,1024]{1,0:T(8,128)(2,1)}, u32[]{:S(2)}) copy-start(bf16[2048,1024]{1,0:T(8,128)(2,1)} %copy-done) | copy-start | bytes 12582916
  48.6 30.4 %collective-permute-start.30 = (bf16[640,256]{1,0:T(8,128)(2,1)S(1)}, bf16[640,256]{1,0:T(8,128)(2,1)S(1)}, u32[]{:S(2)}, u32[]{:S(2)}) collective-permute-start(bf16[640,256]{1,0:T(8,128)(2,1)S(1)} %get-tuple-element.141), channel_id=1, source_target_pairs={{0,8},{1,9},{2,10},{3,11},{4,12},{5,13},{6,14},{7,15},{8,0},{9,1},... | collective-permute-start | bytes 983048 | tf_op jit(solution)/shard_map/ppermute | solution.py:40
  50.4 30.2 %collective-permute-start.31 = (bf16[640,256]{1,0:T(8,128)(2,1)S(1)}, bf16[640,256]{1,0:T(8,128)(2,1)S(1)}, u32[]{:S(2)}, u32[]{:S(2)}) collective-permute-start(bf16[640,256]{1,0:T(8,128)(2,1)S(1)} %get-tuple-element.142), channel_id=1, source_target_pairs={{0,16},{1,17},{2,18},{3,19},{4,20},{5,21},{6,22},{7,23},{8,24},{9,... | collective-permute-start | bytes 983048 | tf_op jit(solution)/shard_map/ppermute | solution.py:40
  51.6 29.0 %collective-permute-start.32 = (bf16[640,256]{1,0:T(8,128)(2,1)S(1)}, bf16[640,256]{1,0:T(8,128)(2,1)S(1)}, u32[]{:S(2)}, u32[]{:S(2)}) collective-permute-start(bf16[640,256]{1,0:T(8,128)(2,1)S(1)} %get-tuple-element.143), channel_id=1, source_target_pairs={{0,24},{1,25},{2,26},{3,27},{4,28},{5,29},{6,30},{7,31},{8,16},{9,... | collective-permute-start | bytes 983048 | tf_op jit(solution)/shard_map/ppermute | solution.py:40
  53.6 7.6 %collective-permute-start.4 = (bf16[128,1024]{1,0:T(8,128)(2,1)S(1)}, bf16[128,1024]{1,0:T(8,128)(2,1)S(1)}, u32[]{:S(2)}, u32[]{:S(2)}) collective-permute-start(bf16[128,1024]{1,0:T(8,128)(2,1)S(1)} %lay.2.refs_0_), channel_id=1, source_target_pairs={{0,2},{1,3},{2,0},{3,1},{4,6},{5,7},{6,4},{7,5},{8,10},{9,11},{10,... | collective-permute-start | bytes 786440 | tf_op jit(solution)/shard_map/cond/branch_1_fun/ppermute | solution.py:40
  55.2 8.6 %collective-permute-start.5 = (bf16[128,1024]{1,0:T(8,128)(2,1)S(1)}, bf16[128,1024]{1,0:T(8,128)(2,1)S(1)}, u32[]{:S(2)}, u32[]{:S(2)}) collective-permute-start(bf16[128,1024]{1,0:T(8,128)(2,1)S(1)} %lay.2.refs_0_), channel_id=1, source_target_pairs={{0,4},{1,5},{2,6},{3,7},{4,0},{5,1},{6,2},{7,3},{8,12},{9,13},{10,... | collective-permute-start | bytes 786440 | tf_op jit(solution)/shard_map/cond/branch_1_fun/ppermute | solution.py:40
  61.3 7.6 %collective-permute-start.6 = (bf16[128,1024]{1,0:T(8,128)(2,1)S(1)}, bf16[128,1024]{1,0:T(8,128)(2,1)S(1)}, u32[]{:S(2)}, u32[]{:S(2)}) collective-permute-start(bf16[128,1024]{1,0:T(8,128)(2,1)S(1)} %lay.2.refs_0_), channel_id=1, source_target_pairs={{0,6},{1,7},{2,4},{3,5},{4,2},{5,3},{6,0},{7,1},{8,14},{9,15},{10,... | collective-permute-start | bytes 786440 | tf_op jit(solution)/shard_map/cond/branch_1_fun/ppermute | solution.py:40
  68.9 2.7 %collective-permute-start.7 = (bf16[512,1024]{1,0:T(8,128)(2,1)S(1)}, bf16[512,1024]{1,0:T(8,128)(2,1)S(1)}, u32[]{:S(2)}, u32[]{:S(2)}) collective-permute-start(bf16[512,1024]{1,0:T(8,128)(2,1)S(1)} %pad_maximum_fusion), channel_id=1, source_target_pairs={{0,1},{1,0},{2,3},{3,2},{4,5},{5,4},{6,7},{7,6},{8,9},{9,8},{10,11... | collective-permute-start | bytes 3145736 | tf_op jit(solution)/shard_map/cond/branch_1_fun/ppermute | solution.py:40
  76.2 26.0 %collective-permute-start.27 = (bf16[640,256]{1,0:T(8,128)(2,1)}, bf16[640,256]{1,0:T(8,128)(2,1)S(1)}, u32[]{:S(2)}, u32[]{:S(2)}) collective-permute-start(bf16[640,256]{1,0:T(8,128)(2,1)} %get-tuple-element.137), channel_id=1, source_target_pairs={{0,8},{1,9},{2,10},{3,11},{4,12},{5,13},{6,14},{7,15},{8,0},{9,1},... | collective-permute-start | bytes 983048 | tf_op jit(solution)/shard_map/ppermute | solution.py:40
  76.9 27.7 %collective-permute-start.28 = (bf16[640,256]{1,0:T(8,128)(2,1)}, bf16[640,256]{1,0:T(8,128)(2,1)S(1)}, u32[]{:S(2)}, u32[]{:S(2)}) collective-permute-start(bf16[640,256]{1,0:T(8,128)(2,1)} %get-tuple-element.138), channel_id=1, source_target_pairs={{0,16},{1,17},{2,18},{3,19},{4,20},{5,21},{6,22},{7,23},{8,24},{9,... | collective-permute-start | bytes 983048 | tf_op jit(solution)/shard_map/ppermute | solution.py:40
  79.0 25.6 %collective-permute-start.29 = (bf16[640,256]{1,0:T(8,128)(2,1)}, bf16[640,256]{1,0:T(8,128)(2,1)S(1)}, u32[]{:S(2)}, u32[]{:S(2)}) collective-permute-start(bf16[640,256]{1,0:T(8,128)(2,1)} %get-tuple-element.139), channel_id=1, source_target_pairs={{0,24},{1,25},{2,26},{3,27},{4,28},{5,29},{6,30},{7,31},{8,16},{9,... | collective-permute-start | bytes 983048 | tf_op jit(solution)/shard_map/ppermute | solution.py:40
  83.8 2.1 %collective-permute-start = (f32[256,512]{1,0:T(8,128)}, f32[256,512]{1,0:T(8,128)S(1)}, u32[]{:S(2)}, u32[]{:S(2)}) collective-permute-start(f32[256,512]{1,0:T(8,128)} %get-tuple-element.28), channel_id=1, source_target_pairs={{0,1},{1,0},{2,3},{3,2},{4,5},{5,4},{6,7},{7,6},{8,9},{9,8},{10,11... | collective-permute-start | bytes 1572872 | tf_op jit(solution)/shard_map/cond/branch_1_fun/ppermute | solution.py:40
  87.1 5.6 %collective-permute-start.1 = (f32[64,512]{1,0:T(8,128)S(1)}, f32[64,512]{1,0:T(8,128)S(1)}, u32[]{:S(2)}, u32[]{:S(2)}) collective-permute-start(f32[64,512]{1,0:T(8,128)S(1)} %get-tuple-element.30), channel_id=1, source_target_pairs={{0,2},{1,3},{2,0},{3,1},{4,6},{5,7},{6,4},{7,5},{8,10},{9,11},{10,... | collective-permute-start | bytes 393224 | tf_op jit(solution)/shard_map/cond/branch_1_fun/ppermute | solution.py:40
  88.6 6.5 %collective-permute-start.2 = (f32[64,512]{1,0:T(8,128)S(1)}, f32[64,512]{1,0:T(8,128)S(1)}, u32[]{:S(2)}, u32[]{:S(2)}) collective-permute-start(f32[64,512]{1,0:T(8,128)S(1)} %get-tuple-element.33), channel_id=1, source_target_pairs={{0,4},{1,5},{2,6},{3,7},{4,0},{5,1},{6,2},{7,3},{8,12},{9,13},{10,... | collective-permute-start | bytes 393224 | tf_op jit(solution)/shard_map/cond/branch_1_fun/ppermute | solution.py:40
  92.7 5.9 %collective-permute-start.3 = (f32[64,512]{1,0:T(8,128)S(1)}, f32[64,512]{1,0:T(8,128)S(1)}, u32[]{:S(2)}, u32[]{:S(2)}) collective-permute-start(f32[64,512]{1,0:T(8,128)S(1)} %get-tuple-element.34), channel_id=1, source_target_pairs={{0,6},{1,7},{2,4},{3,5},{4,2},{5,3},{6,0},{7,1},{8,14},{9,15},{10,... | collective-permute-start | bytes 393224 | tf_op jit(solution)/shard_map/cond/branch_1_fun/ppermute | solution.py:40
  99.1 5.5 %collective-permute-start.33 = (f32[16,512]{1,0:T(8,128)S(1)}, f32[16,512]{1,0:T(8,128)S(1)}, u32[]{:S(2)}, u32[]{:S(2)}) collective-permute-start(f32[16,512]{1,0:T(8,128)S(1)} %get-tuple-element.147), channel_id=1, source_target_pairs={{0,8},{1,9},{2,10},{3,11},{4,12},{5,13},{6,14},{7,15},{8,0},{9,1},... | collective-permute-start | bytes 98312 | tf_op jit(solution)/shard_map/ppermute | solution.py:40
  102.1 10.4 %collective-permute-start.34 = (f32[16,512]{1,0:T(8,128)S(1)}, f32[16,512]{1,0:T(8,128)S(1)}, u32[]{:S(2)}, u32[]{:S(2)}) collective-permute-start(f32[16,512]{1,0:T(8,128)S(1)} %get-tuple-element.148), channel_id=1, source_target_pairs={{0,16},{1,17},{2,18},{3,19},{4,20},{5,21},{6,22},{7,23},{8,24},{9,... | collective-permute-start | bytes 98312 | tf_op jit(solution)/shard_map/ppermute | solution.py:40
  102.2 10.3 %collective-permute-start.35 = (f32[16,512]{1,0:T(8,128)S(1)}, f32[16,512]{1,0:T(8,128)S(1)}, u32[]{:S(2)}, u32[]{:S(2)}) collective-permute-start(f32[16,512]{1,0:T(8,128)S(1)} %get-tuple-element.149), channel_id=1, source_target_pairs={{0,24},{1,25},{2,26},{3,27},{4,28},{5,29},{6,30},{7,31},{8,16},{9,... | collective-permute-start | bytes 98312 | tf_op jit(solution)/shard_map/ppermute | solution.py:40
  115.6 2.0 %collective-permute-start.36 = (f32[256,512]{1,0:T(8,128)S(1)}, f32[256,512]{1,0:T(8,128)S(1)}, u32[]{:S(2)}, u32[]{:S(2)}) collective-permute-start(f32[256,512]{1,0:T(8,128)S(1)} %get-tuple-element.156), channel_id=1, source_target_pairs={{0,1},{1,0},{2,3},{3,2},{4,5},{5,4},{6,7},{7,6},{8,9},{9,8},{10,11... | collective-permute-start | bytes 1572872 | tf_op jit(solution)/shard_map/ppermute | solution.py:40
  118.1 6.0 %collective-permute-start.37 = (f32[64,512]{1,0:T(8,128)S(1)}, f32[64,512]{1,0:T(8,128)S(1)}, u32[]{:S(2)}, u32[]{:S(2)}) collective-permute-start(f32[64,512]{1,0:T(8,128)S(1)} %get-tuple-element.158), channel_id=1, source_target_pairs={{0,2},{1,3},{2,0},{3,1},{4,6},{5,7},{6,4},{7,5},{8,10},{9,11},{10,... | collective-permute-start | bytes 393224 | tf_op jit(solution)/shard_map/ppermute | solution.py:40
  119.7 8.1 %collective-permute-start.38 = (f32[64,512]{1,0:T(8,128)S(1)}, f32[64,512]{1,0:T(8,128)S(1)}, u32[]{:S(2)}, u32[]{:S(2)}) collective-permute-start(f32[64,512]{1,0:T(8,128)S(1)} %get-tuple-element.159), channel_id=1, source_target_pairs={{0,4},{1,5},{2,6},{3,7},{4,0},{5,1},{6,2},{7,3},{8,12},{9,13},{10,... | collective-permute-start | bytes 393224 | tf_op jit(solution)/shard_map/ppermute | solution.py:40
  121.2 6.5 %collective-permute-start.39 = (f32[64,512]{1,0:T(8,128)S(1)}, f32[64,512]{1,0:T(8,128)S(1)}, u32[]{:S(2)}, u32[]{:S(2)}) collective-permute-start(f32[64,512]{1,0:T(8,128)S(1)} %get-tuple-element.160), channel_id=1, source_target_pairs={{0,6},{1,7},{2,4},{3,5},{4,2},{5,3},{6,0},{7,1},{8,14},{9,15},{10,... | collective-permute-start | bytes 393224 | tf_op jit(solution)/shard_map/ppermute | solution.py:40
  128.4 7.6 %collective-permute-start.42 = (bf16[96,512]{1,0:T(8,128)(2,1)S(1)}, bf16[96,512]{1,0:T(8,128)(2,1)S(1)}, u32[]{:S(2)}, u32[]{:S(2)}) collective-permute-start(bf16[96,512]{1,0:T(8,128)(2,1)S(1)} %code.1.refs_0_), channel_id=1, source_target_pairs={{0,24},{1,25},{2,26},{3,27},{4,28},{5,29},{6,30},{7,31},{8,16},{9,... | collective-permute-start | bytes 294920 | tf_op jit(solution)/shard_map/ppermute | solution.py:40
  129.4 9.5 %collective-permute-start.41 = (bf16[96,512]{1,0:T(8,128)(2,1)S(1)}, bf16[96,512]{1,0:T(8,128)(2,1)S(1)}, u32[]{:S(2)}, u32[]{:S(2)}) collective-permute-start(bf16[96,512]{1,0:T(8,128)(2,1)S(1)} %code.1.refs_0_), channel_id=1, source_target_pairs={{0,16},{1,17},{2,18},{3,19},{4,20},{5,21},{6,22},{7,23},{8,24},{9,... | collective-permute-start | bytes 294920 | tf_op jit(solution)/shard_map/ppermute | solution.py:40
  130.8 8.0 %collective-permute-start.40 = (bf16[96,512]{1,0:T(8,128)(2,1)S(1)}, bf16[96,512]{1,0:T(8,128)(2,1)S(1)}, u32[]{:S(2)}, u32[]{:S(2)}) collective-permute-start(bf16[96,512]{1,0:T(8,128)(2,1)S(1)} %code.1.refs_0_), channel_id=1, source_target_pairs={{0,8},{1,9},{2,10},{3,11},{4,12},{5,13},{6,14},{7,15},{8,0},{9,1},... | collective-permute-start | bytes 294920 | tf_op jit(solution)/shard_map/ppermute | solution.py:40
  139.9 6.5 %collective-permute-start.45 = (bf16[128,512]{1,0:T(8,128)(2,1)S(1)}, bf16[128,512]{1,0:T(8,128)(2,1)S(1)}, u32[]{:S(2)}, u32[]{:S(2)}) collective-permute-start(bf16[128,512]{1,0:T(8,128)(2,1)S(1)} %finish.1.refs_0_), channel_id=1, source_target_pairs={{0,6},{1,7},{2,4},{3,5},{4,2},{5,3},{6,0},{7,1},{8,14},{9,15},{10,... | collective-permute-start | bytes 393224 | tf_op jit(solution)/shard_map/ppermute | solution.py:40
  141.6 6.0 %collective-permute-start.44 = (bf16[128,512]{1,0:T(8,128)(2,1)S(1)}, bf16[128,512]{1,0:T(8,128)(2,1)S(1)}, u32[]{:S(2)}, u32[]{:S(2)}) collective-permute-start(bf16[128,512]{1,0:T(8,128)(2,1)S(1)} %finish.1.refs_0_), channel_id=1, source_target_pairs={{0,4},{1,5},{2,6},{3,7},{4,0},{5,1},{6,2},{7,3},{8,12},{9,13},{10,... | collective-permute-start | bytes 393224 | tf_op jit(solution)/shard_map/ppermute | solution.py:40
  143.1 5.0 %collective-permute-start.43 = (bf16[128,512]{1,0:T(8,128)(2,1)S(1)}, bf16[128,512]{1,0:T(8,128)(2,1)S(1)}, u32[]{:S(2)}, u32[]{:S(2)}) collective-permute-start(bf16[128,512]{1,0:T(8,128)(2,1)S(1)} %finish.1.refs_0_), channel_id=1, source_target_pairs={{0,2},{1,3},{2,0},{3,1},{4,6},{5,7},{6,4},{7,5},{8,10},{9,11},{10,... | collective-permute-start | bytes 393224 | tf_op jit(solution)/shard_map/ppermute | solution.py:40
  143.4 4.7 %collective-permute-start.46 = (bf16[128,512]{1,0:T(8,128)(2,1)S(1)}, bf16[128,512]{1,0:T(8,128)(2,1)S(1)}, u32[]{:S(2)}, u32[]{:S(2)}) collective-permute-start(bf16[128,512]{1,0:T(8,128)(2,1)S(1)} %finish.1.refs_0_), channel_id=1, source_target_pairs={{0,1},{1,0},{2,3},{3,2},{4,5},{5,4},{6,7},{7,6},{8,9},{9,8},{10,11... | collective-permute-start | bytes 393224 | tf_op jit(solution)/shard_map/ppermute | solution.py:40
  146.4 1.7 %collective-permute-start.49 = (bf16[128,512]{1,0:T(8,128)(2,1)S(1)}, bf16[128,512]{1,0:T(8,128)(2,1)S(1)}, u32[]{:S(2)}, u32[]{:S(2)}) collective-permute-start(bf16[128,512]{1,0:T(8,128)(2,1)S(1)} %collective-permute-done.45.refs_3_), channel_id=1, source_target_pairs={{0,1},{1,0},{2,3},{3,2},{4,5},{5,4},{6,7},{7,6},{8,9},{9,8},{10,11... | collective-permute-start | bytes 393224 | tf_op jit(solution)/shard_map/ppermute | solution.py:40
  147.6 1.3 collective-permute-start.48
  148.1 1.3 collective-permute-start.47
  151.3 7.5 %collective-permute-start.50 = (bf16[256,256]{1,0:T(8,128)(2,1)S(1)}, bf16[256,256]{1,0:T(8,128)(2,1)S(1)}, u32[]{:S(2)}, u32[]{:S(2)}) collective-permute-start(bf16[256,256]{1,0:T(8,128)(2,1)S(1)} %get-tuple-element.172), channel_id=1, source_target_pairs={{0,8},{1,9},{2,10},{3,11},{4,12},{5,13},{6,14},{7,15},{8,0},{9,1},... | collective-permute-start | bytes 393224 | tf_op jit(solution)/shard_map/ppermute | solution.py:40
  151.3 12.9 %collective-permute-start.51 = (bf16[256,256]{1,0:T(8,128)(2,1)S(1)}, bf16[256,256]{1,0:T(8,128)(2,1)S(1)}, u32[]{:S(2)}, u32[]{:S(2)}) collective-permute-start(bf16[256,256]{1,0:T(8,128)(2,1)S(1)} %get-tuple-element.173), channel_id=1, source_target_pairs={{0,16},{1,17},{2,18},{3,19},{4,20},{5,21},{6,22},{7,23},{8,24},{9,... | collective-permute-start | bytes 393224 | tf_op jit(solution)/shard_map/ppermute | solution.py:40
  153.6 10.7 %collective-permute-start.52 = (bf16[256,256]{1,0:T(8,128)(2,1)S(1)}, bf16[256,256]{1,0:T(8,128)(2,1)S(1)}, u32[]{:S(2)}, u32[]{:S(2)}) collective-permute-start(bf16[256,256]{1,0:T(8,128)(2,1)S(1)} %get-tuple-element.174), channel_id=1, source_target_pairs={{0,24},{1,25},{2,26},{3,27},{4,28},{5,29},{6,30},{7,31},{8,16},{9,... | collective-permute-start | bytes 393224 | tf_op jit(solution)/shard_map/ppermute | solution.py:40

commit v5 on v4

--- a/solution.py
+++ b/solution.py
@@ -16,9 +16,9 @@
 F32 = jnp.float32
 BF16 = jnp.bfloat16
 VMEM_BYTES = 16 * 1024 * 1024
-SHARED = 4
-BITS = 3
-LEVELS = 1 << BITS
+POWERS = 240
+HIGHEST = 128 * POWERS - 1
+SCALE_ROWS = 16
 
 
 class Place:
@@ -117,7 +117,7 @@
 def code_kernel(place_ref, *refs, n):
     met, rows_ref, out_ref = refs[:n], refs[n], refs[n + 1]
     total = tree_sum([ref[...] for ref in met])
-    coded = total.shape[0] + total.shape[0] // SHARED
+    coded = total.shape[0] + SCALE_ROWS
     encode(total, out_ref.at[:coded])
     out_ref[coded:] = rows_ref[...]
 
@@ -125,12 +125,12 @@
 def finish_kernel(place_ref, *refs, n, k):
     out_ref = refs[-1]
     height = out_ref.shape[0] // 2
-    coded, few = height + height // SHARED, height // n
+    coded, few = height + SCALE_ROWS, height // n
     met = []
     for step in range(n):
         at = pl.ds(pl.multiple_of((place_ref[0] ^ step) * few, few), few)
         out_ref[at, :] = refs[step][coded:]
-        met.append(jnp.concatenate(decode(refs[step].at[:coded]), 0))
+        met += decode(refs[step].at[:coded], 1)
     total = tree_sum(met)
     last = (place_ref[1] == n - 1) & (place_ref[2] == k - 1)
     edge = total[-8:, :128]
@@ -225,12 +225,12 @@
         fetch_kernel,
         in_specs=[pl.BlockSpec(memory_space=pl.ANY)],
         out_specs=pl.BlockSpec(memory_space=pltpu.VMEM),
-        out_shape=jax.ShapeDtypeStruct(weight.shape, BF16),
+        out_shape=pltpu.VMEM(weight.shape, BF16),
         scratch_shapes=[pltpu.SemaphoreType.DMA],
         compiler_params=pltpu.CompilerParams(vmem_limit_bytes=VMEM_BYTES // 2),
         cost_estimate=pl.CostEstimate(flops=0, bytes_accessed=4 * weight.size, transcendentals=0),
         name="fetch",
-    )(weight)
+    )(pltpu.with_memory_space_constraint(weight, pltpu.HBM))
 
 
 def to_columns(place, view):
@@ -279,58 +279,39 @@
             encode(total, coded[step - 1])
 
 
-def unit(near):
-    near = jnp.abs(near)
-    return (near * (1.0 + 1.01 / 256.0)).astype(BF16).astype(F32) - near
-
-
 def encode(total, coded_ref):
-    coarse = total.astype(BF16)
-    batch = total.shape[0]
-    coded_ref[:batch] = coarse
-    near = coarse.astype(F32)
-    step = unit(near)
-    level = (total - near) * pl.reciprocal(jnp.where(step > 0.0, step, 1.0), approx=True)
-    level = jnp.clip(jnp.floor((level + 0.5) * LEVELS), 0.0, LEVELS - 1.0).astype(jnp.int32)
-    height = batch // SHARED
-    first, second, third, fourth = [level[i * height : (i + 1) * height] for i in range(SHARED)]
-    word = 128 + (first << BITS) + second + ((fourth & 1) << 6)
-    word = word << (third + ((fourth & 4) << 1))
-    word = jnp.where((fourth & 2) != 0, -word, word)
-    coded_ref[batch:] = word.astype(F32).astype(BF16)
-
-
-def decode(coded_ref):
-    height = coded_ref.shape[0] // (SHARED + 1)
-    word = coded_ref[SHARED * height :].astype(F32).astype(jnp.int32)
-    negative = word < 0
-    word = jnp.abs(word)
-    power = jnp.zeros_like(word)
-    for shift in (8, 4, 2, 1):
-        large = word >= (128 << shift)
-        word = jnp.where(large, word >> shift, word)
-        power = power + jnp.where(large, shift, 0)
-    levels = [
-        (word >> BITS) & (LEVELS - 1),
-        word & (LEVELS - 1),
-        power & (LEVELS - 1),
-        ((word >> 6) & 1) + jnp.where(negative, 2, 0) + ((power >> 3) << 2),
-    ]
+    rows = total.shape[0]
+    top = jnp.max(jnp.abs(total), 0, keepdims=True)
+    top = jnp.maximum(top * (1.0 + 1.0 / 128.0), 1e-30).astype(BF16)
+    coded_ref[rows:] = jnp.broadcast_to(top, (SCALE_ROWS, total.shape[1]))
+    whole = jnp.floor(jnp.abs(total) * (HIGHEST / top.astype(F32)) + 0.5)
+    power = jnp.floor(whole * (1.0 / 128.0))
+    word = (1.0 + (whole * (1.0 / 128.0) - power)) * jnp.exp2(power - POWERS // 2)
+    coded_ref[:rows] = jnp.where(total < 0.0, -word, word).astype(BF16)
+
+
+def decode(coded_ref, count):
+    rows = coded_ref.shape[0] - SCALE_ROWS
+    scale = coded_ref[rows:].astype(F32)[:1] * (1.0 / HIGHEST)
+    height = rows // count
     blocks = []
-    for i, level in enumerate(levels):
-        near = coded_ref[i * height : (i + 1) * height].astype(F32)
-        offset = (level.astype(F32) + (0.5 - LEVELS / 2)) * (1.0 / LEVELS)
-        blocks.append(near + unit(near) * offset)
+    for i in range(count):
+        word = coded_ref[i * height : (i + 1) * height].astype(F32)
+        size = jnp.abs(word)
+        power = jnp.floor(jnp.log(size) * 1.4426950408889634 + 0.002)
+        part = jnp.floor(size * jnp.exp2(-power) * 128.0 + 0.5)
+        whole = (power + (POWERS // 2 - 1)) * 128.0 + part
+        blocks.append(jnp.where(word < 0.0, -whole, whole) * scale)
     return blocks
 
 
-def project(place, place_array, met, weight):
+def project(place, place_array, met, held):
     n, k = place.n, place.k
     rows, width = met[0][0].shape
-    batch, columns = rows * n, weight.shape[1] // n
+    batch, columns = rows * n, held.shape[1] // n
     counts = [len(parts) for parts in met]
     met = [part for parts in met for part in parts]
-    coded = batch + batch // SHARED
+    coded = batch + SCALE_ROWS
     out_shape = [jax.ShapeDtypeStruct((batch, columns), F32)]
     out_shape += [jax.ShapeDtypeStruct((coded, columns), BF16)] * (n - 1)
     space = pl.BlockSpec(memory_space=pltpu.VMEM)
@@ -347,7 +328,7 @@
             transcendentals=0,
         ),
         name="project",
-    )(place_array, *met, weight)
+    )(place_array, *met, pltpu.with_memory_space_constraint(held, pltpu.VMEM))
     return own, parts
 
 
@@ -359,11 +340,11 @@
     norm_ref, packed_ref, scale_ref = refs[:3]
     grams = refs[3 : 3 + k]
     batch, columns = own_ref.shape
-    height = batch // SHARED
-    met = [[own_ref[i * height : (i + 1) * height] for i in range(SHARED)]]
+    height = batch // n
+    met = [[own_ref[i * height : (i + 1) * height] for i in range(n)]]
     for step in range(1, n):
-        met.append(decode(parts[step - 1]))
-    blocks = [tree_sum([met[step][i] for step in range(n)]) for i in range(SHARED)]
+        met.append(decode(parts[step - 1], n))
+    blocks = [tree_sum([met[step][i] for step in range(n)]) for i in range(n)]
     total = tree_sum([jnp.sum(block, 0, keepdims=True) for block in blocks])
     squares = tree_sum([jnp.sum(block * block, 0, keepdims=True) for block in blocks])
     mean = total / batch
@@ -533,7 +514,7 @@
         functools.partial(code_kernel, n=n),
         place_array,
         (*met_2, rows_1),
-        [((rows + rows // SHARED + height, batch), BF16)],
+        [((rows + SCALE_ROWS + height, batch), BF16)],
         "code",
     )
     (part,) = local(
@@ -616,7 +597,7 @@
 def per_device(h_first, h_second, weight):
     place = Place()
     columns = weight.shape[1] // place.n
-    fits = columns % 128 == 0 and place.n == SHARED and place.k == 2
+    fits = columns % 128 == 0 and place.n == 4 and place.k == 2
     return (with_kernels if fits else plain)(place, h_first, h_second, weight)
 
 

time: 166 us -> 162 us (0.976)
  waiting for transfers between devices: 68.7 us -> 65 us
    ppermute x53, waiting for transfers between devices: 68.7 us -> 65 us  [send(): return lax.ppermute(value, ('dp', 'mp'), pairs)]
    unnamed x4 -> x6, local copies, waits for them, and re-layouts: 4.17 us -> 4.17 us
  transfers between devices with their start and end apart: 53 -> 53, of which waited for: 28 -> 29; matrix products, arithmetic and copies ran while one was open for 1% -> 1% of each run, Pallas kernels for 9% -> 10%
where the time goes in v5:
time: 162 us; the launch traced here: 161 us
  waiting for transfers between devices  65 us (40%)
  starting transfers between devices  60.9 us (38%)
  Pallas kernels  28.3 us (17%)
  local copies, waits for them, and re-layouts  6.09 us (4%)
    ppermute x53, waiting for transfers between devices, send(): return lax.ppermute(value, ('dp', 'mp'), pairs)  65 us
    ppermute x53, starting transfers between devices, send(): return lax.ppermute(value, ('dp', 'mp'), pairs)  60.9 us
    pallas_call x10, Pallas kernels, local(): pl.pallas_call(kernel, in_specs=[pl.BlockSpec(memory_space=pltpu.SMEM)] +...  9.37 us
    pallas_call x2, Pallas kernels, project(): pl.pallas_call(functools.partial(project_kernel, counts=counts, n=n, k=k)...  8.52 us
    pallas_call x2, Pallas kernels, normalize_parts(): pl.pallas_call(functools.partial(normalize_kernel, n=n, k=k, second=secon...  6.01 us
    pallas_call x2, Pallas kernels, fetch(): pl.pallas_call(fetch_kernel, in_specs=[pl.BlockSpec(memory_space=pl.ANY)]...  4.39 us
    unnamed x6, local copies, waits for them, and re-layouts  4.17 us
  transfers between devices with their start and end apart: 53, of which 29 were waited for; matrix products, arithmetic and copies ran while one was open for 1% of the time, Pallas kernels for 10%

profile of v5, /device:TPU:0, one launch (start us, length us, event | category | flops | bytes accessed | tf_op | source)
XLA Modules:
  0.0 161.3 jit_solution(8054792053048291973)
XLA Ops:
  0.7 1.0 dynamic-slice_bitcast_fusion.4
  1.6 4.0 %collective-permute-start.10 = (bf16[32,1024]{1,0:T(8,128)(2,1)S(1)}, bf16[32,1024]{1,0:T(8,128)(2,1)S(1)}, u32[]{:S(2)}, u32[]{:S(2)}) collective-permute-start(bf16[32,1024]{1,0:T(8,128)(2,1)S(1)} %get-tuple-element.190), channel_id=1, source_target_pairs={{0,6},{1,7},{2,4},{3,5},{4,2},{5,3},{6,0},{7,1},{8,14},{9,15},{10,... | collective-permute-start | bytes 196616 | tf_op jit(solution)/shard_map/ppermute | solution.py:40
  6.2 1.0 dynamic-slice_bitcast_fusion
  7.2 2.9 %collective-permute-start.16 = (bf16[32,1024]{1,0:T(8,128)(2,1)S(1)}, bf16[32,1024]{1,0:T(8,128)(2,1)S(1)}, u32[]{:S(2)}, u32[]{:S(2)}) collective-permute-start(bf16[32,1024]{1,0:T(8,128)(2,1)S(1)} %get-tuple-element.182), channel_id=1, source_target_pairs={{0,6},{1,7},{2,4},{3,5},{4,2},{5,3},{6,0},{7,1},{8,14},{9,15},{10,... | collective-permute-start | bytes 196616 | tf_op jit(solution)/shard_map/ppermute | solution.py:40
  10.6 2.2 %fetch.3.refs_8_ = bf16[2048,1024]{1,0:T(8,128)(2,1)S(1)} custom-call(bf16[2048,1024]{1,0:T(8,128)(2,1)} %weight_ref.1), custom_call_target="tpu_custom_call" | custom-call | bytes 8388608 | tf_op jit(solution)/shard_map/fetch/pallas_call | solution.py:224
  12.8 2.0 %copy-done = bf16[2048,1024]{1,0:T(8,128)(2,1)} copy-done((bf16[2048,1024]{1,0:T(8,128)(2,1)}, bf16[2048,1024]{1,0:T(8,128)(2,1)S(1)}, u32[]{:S(2)}) %copy-start) | copy-done | bytes 4194328
  15.0 4.1 %collective-permute-start.13 = (bf16[32,1024]{1,0:T(8,128)(2,1)S(1)}, bf16[32,1024]{1,0:T(8,128)(2,1)S(1)}, u32[]{:S(2)}, u32[]{:S(2)}) collective-permute-start(bf16[32,1024]{1,0:T(8,128)(2,1)S(1)} %get-tuple-element.186), channel_id=1, source_target_pairs={{0,24},{1,25},{2,26},{3,27},{4,28},{5,29},{6,30},{7,31},{8,16},{9,... | collective-permute-start | bytes 196616 | tf_op jit(solution)/shard_map/ppermute | solution.py:40
  19.8 1.6 %collective-permute-done.13.refs_3_ = bf16[32,1024]{1,0:T(8,128)(2,1)S(1)} collective-permute-done((bf16[32,1024]{1,0:T(8,128)(2,1)S(1)}, bf16[32,1024]{1,0:T(8,128)(2,1)S(1)}, u32[]{:S(2)}, u32[]{:S(2)}) %collective-permute-start.13) | collective-permute-done | bytes 65568 | tf_op jit(solution)/shard_map/ppermute | solution.py:40
  21.4 1.9 %collective-permute-done.11.refs_1_ = bf16[32,1024]{1,0:T(8,128)(2,1)S(1)} collective-permute-done((bf16[32,1024]{1,0:T(8,128)(2,1)S(1)}, bf16[32,1024]{1,0:T(8,128)(2,1)S(1)}, u32[]{:S(2)}, u32[]{:S(2)}) %collective-permute-start.11) | collective-permute-done | bytes 65568 | tf_op jit(solution)/shard_map/ppermute | solution.py:40
  23.3 0.9 collective-permute-done.12.refs_2_
  24.8 2.5 %collective-permute-start.19 = (bf16[128,1024]{1,0:T(8,128)(2,1)S(1)}, bf16[128,1024]{1,0:T(8,128)(2,1)S(1)}, u32[]{:S(2)}, u32[]{:S(2)}) collective-permute-start(bf16[128,1024]{1,0:T(8,128)(2,1)S(1)} %lay.3.refs_0_), channel_id=1, source_target_pairs={{0,6},{1,7},{2,4},{3,5},{4,2},{5,3},{6,0},{7,1},{8,14},{9,15},{10,... | collective-permute-start | bytes 786440 | tf_op jit(solution)/shard_map/ppermute | solution.py:40
  28.4 1.7 %collective-permute-start.22 = (bf16[32,1024]{1,0:T(8,128)(2,1)S(1)}, bf16[32,1024]{1,0:T(8,128)(2,1)}, u32[]{:S(2)}, u32[]{:S(2)}) collective-permute-start(bf16[32,1024]{1,0:T(8,128)(2,1)S(1)} %get-tuple-element.178), channel_id=1, source_target_pairs={{0,24},{1,25},{2,26},{3,27},{4,28},{5,29},{6,30},{7,31},{8,16},{9,... | collective-permute-start | bytes 196616 | tf_op jit(solution)/shard_map/ppermute | solution.py:40
  30.5 4.4 %collective-permute-done.22 = bf16[32,1024]{1,0:T(8,128)(2,1)} collective-permute-done((bf16[32,1024]{1,0:T(8,128)(2,1)S(1)}, bf16[32,1024]{1,0:T(8,128)(2,1)}, u32[]{:S(2)}, u32[]{:S(2)}) %collective-permute-start.22) | collective-permute-done | bytes 65568 | tf_op jit(solution)/shard_map/ppermute | solution.py:40
  35.6 4.6 %collective-permute-done.21 = bf16[32,1024]{1,0:T(8,128)(2,1)S(1)} collective-permute-done((bf16[32,1024]{1,0:T(8,128)(2,1)S(1)}, bf16[32,1024]{1,0:T(8,128)(2,1)S(1)}, u32[]{:S(2)}, u32[]{:S(2)}) %collective-permute-start.21) | collective-permute-done | bytes 65568 | tf_op jit(solution)/shard_map/ppermute | solution.py:40
  42.9 2.2 %copy-done.1 = bf16[2048,1024]{1,0:T(8,128)(2,1)S(1)} copy-done((bf16[2048,1024]{1,0:T(8,128)(2,1)S(1)}, bf16[2048,1024]{1,0:T(8,128)(2,1)}, u32[]{:S(2)}) %copy-start.1) | copy-done | bytes 4194328
  45.1 3.9 %project.3 = (f32[512,256]{1,0:T(8,128)S(1)}, bf16[528,256]{1,0:T(8,128)(2,1)S(1)}, bf16[528,256]{1,0:T(8,128)(2,1)S(1)}, bf16[528,256]{1,0:T(8,128)(2,1)S(1)}) custom-call(s32[3]{0:T(128)S(1)} %pad_add_fusion.place_ref, bf16[128,1024]{1,0:T(8,128)(2,1)S(1)} %lay.3.refs_0_, bf16[128,1024]{1,0:T(8,128)(2,1)S(1)} %collective-permute-done.17.refs_1_, ...), custom_call_target="tpu_custom_call" | custom-call | flops 2147483648 | bytes 7864320 | tf_op jit(solution)/shard_map/project/pallas_call | solution.py:318
  49.0 1.8 %collective-permute-start.30 = (bf16[528,256]{1,0:T(8,128)(2,1)S(1)}, bf16[528,256]{1,0:T(8,128)(2,1)S(1)}, u32[]{:S(2)}, u32[]{:S(2)}) collective-permute-start(bf16[528,256]{1,0:T(8,128)(2,1)S(1)} %get-tuple-element.141), channel_id=1, source_target_pairs={{0,8},{1,9},{2,10},{3,11},{4,12},{5,13},{6,14},{7,15},{8,0},{9,1},... | collective-permute-start | bytes 811016 | tf_op jit(solution)/shard_map/ppermute | solution.py:40
  50.8 1.0 collective-permute-start.31
  51.8 1.6 %collective-permute-start.32 = (bf16[528,256]{1,0:T(8,128)(2,1)S(1)}, bf16[528,256]{1,0:T(8,128)(2,1)S(1)}, u32[]{:S(2)}, u32[]{:S(2)}) collective-permute-start(bf16[528,256]{1,0:T(8,128)(2,1)S(1)} %get-tuple-element.143), channel_id=1, source_target_pairs={{0,24},{1,25},{2,26},{3,27},{4,28},{5,29},{6,30},{7,31},{8,16},{9,... | collective-permute-start | bytes 811016 | tf_op jit(solution)/shard_map/ppermute | solution.py:40
  53.4 23.5 %conditional.2 = ((f32[512,256]{1,0:T(8,128)S(1)}, bf16[528,256]{1,0:T(8,128)(2,1)}, bf16[528,256]{1,0:T(8,128)(2,1)}, bf16[528,256]{1,0:T(8,128)(2,1)})) conditional(s32[]{:T(128)} %convert_element_type.4, () %tuple.34, (s32[3]{0:T(128)S(1)}, bf16[32,1024]{1,0:T(8,128)(2,1)S(1)}, bf16[32,1024]{1,0:T(8,128)(2,1)}, bf16[32,1024]{1,0:T(8,128)(2,1)}, ...), branch_computations={%region_0.1_spmd, %region_1.2_spmd} | conditional | flops 2151677952 | bytes 25690280 | solution.py:191
  53.4 0.9 lay.2.refs_0_
  54.4 1.5 collective-permute-start.4
  55.9 1.5 collective-permute-start.5
  57.4 4.6 %collective-permute-done.4.refs_1_ = bf16[128,1024]{1,0:T(8,128)(2,1)S(1)} collective-permute-done((bf16[128,1024]{1,0:T(8,128)(2,1)S(1)}, bf16[128,1024]{1,0:T(8,128)(2,1)S(1)}, u32[]{:S(2)}, u32[]{:S(2)}) %collective-permute-start.4) | collective-permute-done | bytes 262176 | tf_op jit(solution)/shard_map/cond/branch_1_fun/ppermute | solution.py:40
  62.0 2.4 %collective-permute-start.6 = (bf16[128,1024]{1,0:T(8,128)(2,1)S(1)}, bf16[128,1024]{1,0:T(8,128)(2,1)S(1)}, u32[]{:S(2)}, u32[]{:S(2)}) collective-permute-start(bf16[128,1024]{1,0:T(8,128)(2,1)S(1)} %lay.2.refs_0_), channel_id=1, source_target_pairs={{0,6},{1,7},{2,4},{3,5},{4,2},{5,3},{6,0},{7,1},{8,14},{9,15},{10,... | collective-permute-start | bytes 786440 | tf_op jit(solution)/shard_map/cond/branch_1_fun/ppermute | solution.py:40
  64.5 5.1 %collective-permute-done.6.refs_3_ = bf16[128,1024]{1,0:T(8,128)(2,1)S(1)} collective-permute-done((bf16[128,1024]{1,0:T(8,128)(2,1)S(1)}, bf16[128,1024]{1,0:T(8,128)(2,1)S(1)}, u32[]{:S(2)}, u32[]{:S(2)}) %collective-permute-start.6) | collective-permute-done | bytes 262176 | tf_op jit(solution)/shard_map/cond/branch_1_fun/ppermute | solution.py:40
  69.7 2.2 %fetch.2.refs_5_ = bf16[2048,1024]{1,0:T(8,128)(2,1)S(1)} custom-call(bf16[2048,1024]{1,0:T(8,128)(2,1)} %get-tuple-element.25.weight_ref), custom_call_target="tpu_custom_call" | custom-call | bytes 8388608 | tf_op jit(solution)/shard_map/cond/branch_1_fun/fetch/pallas_call | solution.py:224
  72.4 4.6 %project.2 = (f32[512,256]{1,0:T(8,128)S(1)}, bf16[528,256]{1,0:T(8,128)(2,1)}, bf16[528,256]{1,0:T(8,128)(2,1)}, bf16[528,256]{1,0:T(8,128)(2,1)}) custom-call(s32[3]{0:T(128)S(1)} %get-tuple-element.18.place_ref, bf16[128,1024]{1,0:T(8,128)(2,1)S(1)} %lay.2.refs_0_, bf16[128,1024]{1,0:T(8,128)(2,1)S(1)} %collective-permute-done.4.refs_1_, ...), custom_call_target="tpu_custom_call" | custom-call | flops 2147483648 | bytes 7864320 | tf_op jit(solution)/shard_map/cond/branch_1_fun/project/pallas_call | solution.py:318
  77.7 1.9 %collective-permute-start.28 = (bf16[528,256]{1,0:T(8,128)(2,1)}, bf16[528,256]{1,0:T(8,128)(2,1)S(1)}, u32[]{:S(2)}, u32[]{:S(2)}) collective-permute-start(bf16[528,256]{1,0:T(8,128)(2,1)} %get-tuple-element.138), channel_id=1, source_target_pairs={{0,16},{1,17},{2,18},{3,19},{4,20},{5,21},{6,22},{7,23},{8,24},{9,... | collective-permute-start | bytes 811016 | tf_op jit(solution)/shard_map/ppermute | solution.py:40
  79.6 1.8 %collective-permute-start.29 = (bf16[528,256]{1,0:T(8,128)(2,1)}, bf16[528,256]{1,0:T(8,128)(2,1)S(1)}, u32[]{:S(2)}, u32[]{:S(2)}) collective-permute-start(bf16[528,256]{1,0:T(8,128)(2,1)} %get-tuple-element.139), channel_id=1, source_target_pairs={{0,24},{1,25},{2,26},{3,27},{4,28},{5,29},{6,30},{7,31},{8,16},{9,... | collective-permute-start | bytes 811016 | tf_op jit(solution)/shard_map/ppermute | solution.py:40
  81.4 3.4 %normalize.2 = (f32[512,256]{1,0:T(8,128)S(1)}, bf16[512,256]{1,0:T(8,128)(2,1)S(1)}, f32[1,256]{1,0:T(1,128)S(1)}, f32[256,512]{1,0:T(8,128)}, f32[256,512]{1,0:T(8,128)}) custom-call(s32[3]{0:T(128)S(1)} %pad_add_fusion.place_ref, f32[512,256]{1,0:T(8,128)S(1)} %get-tuple-element.140.refs_0_, bf16[528,256]{1,0:T(8,128)(2,1)S(1)} %collective-permute-done.30.refs_1_, ...), custom_call_target="tpu_custom_call" | custom-call | flops 134217728 | bytes 3145728 | tf_op jit(solution)/shard_map/normalize/pallas_call | solution.py:397
  84.8 15.3 %conditional.3 = ((f32[16,512]{1,0:T(8,128)S(1)}, f32[16,512]{1,0:T(8,128)S(1)}, f32[16,512]{1,0:T(8,128)S(1)}, f32[16,512]{1,0:T(8,128)S(1)})) conditional(s32[]{:T(128)} %convert_element_type.4, () %tuple.37, (f32[256,512]{1,0:T(8,128)}, s32[3]{0:T(128)S(1)}, f32[256,512]{1,0:T(8,128)}) %tuple.38), branch_computations={%region_2.3_spmd, %region_3.4_spmd} | conditional | bytes 3670184 | solution.py:191
  84.8 2.1 %collective-permute-done.met_ref = f32[256,512]{1,0:T(8,128)S(1)} collective-permute-done((f32[256,512]{1,0:T(8,128)}, f32[256,512]{1,0:T(8,128)S(1)}, u32[]{:S(2)}, u32[]{:S(2)}) %collective-permute-start) | collective-permute-done | bytes 524320 | tf_op jit(solution)/shard_map/cond/branch_1_fun/ppermute | solution.py:40
  86.9 1.1 halve.2
  88.0 1.6 collective-permute-start.1
  89.6 1.5 collective-permute-start.2
  91.1 2.5 %collective-permute-done.1.refs_1_ = f32[64,512]{1,0:T(8,128)S(1)} collective-permute-done((f32[64,512]{1,0:T(8,128)S(1)}, f32[64,512]{1,0:T(8,128)S(1)}, u32[]{:S(2)}, u32[]{:S(2)}) %collective-permute-start.1) | collective-permute-done | bytes 131104 | tf_op jit(solution)/shard_map/cond/branch_1_fun/ppermute | solution.py:40
  93.6 2.4 %collective-permute-start.3 = (f32[64,512]{1,0:T(8,128)S(1)}, f32[64,512]{1,0:T(8,128)S(1)}, u32[]{:S(2)}, u32[]{:S(2)}) collective-permute-start(f32[64,512]{1,0:T(8,128)S(1)} %get-tuple-element.34), channel_id=1, source_target_pairs={{0,6},{1,7},{2,4},{3,5},{4,2},{5,3},{6,0},{7,1},{8,14},{9,15},{10,... | collective-permute-start | bytes 393224 | tf_op jit(solution)/shard_map/cond/branch_1_fun/ppermute | solution.py:40
  96.1 3.4 %collective-permute-done.3.refs_3_ = f32[64,512]{1,0:T(8,128)S(1)} collective-permute-done((f32[64,512]{1,0:T(8,128)S(1)}, f32[64,512]{1,0:T(8,128)S(1)}, u32[]{:S(2)}, u32[]{:S(2)}) %collective-permute-start.3) | collective-permute-done | bytes 131104 | tf_op jit(solution)/shard_map/cond/branch_1_fun/ppermute | solution.py:40
  100.1 2.6 %collective-permute-start.34 = (f32[16,512]{1,0:T(8,128)S(1)}, f32[16,512]{1,0:T(8,128)S(1)}, u32[]{:S(2)}, u32[]{:S(2)}) collective-permute-start(f32[16,512]{1,0:T(8,128)S(1)} %get-tuple-element.148), channel_id=1, source_target_pairs={{0,16},{1,17},{2,18},{3,19},{4,20},{5,21},{6,22},{7,23},{8,24},{9,... | collective-permute-start | bytes 98312 | tf_op jit(solution)/shard_map/ppermute | solution.py:40
  102.8 1.8 %collective-permute-start.35 = (f32[16,512]{1,0:T(8,128)S(1)}, f32[16,512]{1,0:T(8,128)S(1)}, u32[]{:S(2)}, u32[]{:S(2)}) collective-permute-start(f32[16,512]{1,0:T(8,128)S(1)} %get-tuple-element.149), channel_id=1, source_target_pairs={{0,24},{1,25},{2,26},{3,27},{4,28},{5,29},{6,30},{7,31},{8,16},{9,... | collective-permute-start | bytes 98312 | tf_op jit(solution)/shard_map/ppermute | solution.py:40
  104.5 2.0 %collective-permute-done.34.refs_2_ = f32[16,512]{1,0:T(8,128)S(1)} collective-permute-done((f32[16,512]{1,0:T(8,128)S(1)}, f32[16,512]{1,0:T(8,128)S(1)}, u32[]{:S(2)}, u32[]{:S(2)}) %collective-permute-start.34) | collective-permute-done | bytes 32800 | tf_op jit(solution)/shard_map/ppermute | solution.py:40
  106.6 1.9 %collective-permute-done.35.refs_3_ = f32[16,512]{1,0:T(8,128)S(1)} collective-permute-done((f32[16,512]{1,0:T(8,128)S(1)}, f32[16,512]{1,0:T(8,128)S(1)}, u32[]{:S(2)}, u32[]{:S(2)}) %collective-permute-start.35) | collective-permute-done | bytes 32800 | tf_op jit(solution)/shard_map/ppermute | solution.py:40
  108.5 2.6 %normalize.3 = (f32[512,256]{1,0:T(8,128)S(1)}, bf16[512,256]{1,0:T(8,128)(2,1)S(1)}, f32[1,256]{1,0:T(1,128)S(1)}, f32[256,512]{1,0:T(8,128)S(1)}, f32[256,512]{1,0:T(8,128)S(1)}, /*index=5*/f32[1,256]{1,0:T(1,128)S(1)}) custom-call(s32[3]{0:T(128)S(1)} %pad_add_fusion.place_ref, f32[512,256]{1,0:T(8,128)S(1)} %get-tuple-element.150.refs_0_, ...), custom_call_target="tpu_custom_call" | custom-call | flops 134217728 | bytes 3145728 | tf_op jit(solution)/shard_map/normalize/pallas_call | solution.py:397
  111.2 1.9 %collective-permute-done.36.met_ref = f32[256,512]{1,0:T(8,128)S(1)} collective-permute-done((f32[256,512]{1,0:T(8,128)S(1)}, f32[256,512]{1,0:T(8,128)S(1)}, u32[]{:S(2)}, u32[]{:S(2)}) %collective-permute-start.36) | collective-permute-done | bytes 524320 | tf_op jit(solution)/shard_map/ppermute | solution.py:40
  113.7 1.6 collective-permute-start.37
  115.2 1.5 collective-permute-start.38
  117.8 1.8 %collective-permute-done.37.refs_1_ = f32[64,512]{1,0:T(8,128)S(1)} collective-permute-done((f32[64,512]{1,0:T(8,128)S(1)}, f32[64,512]{1,0:T(8,128)S(1)}, u32[]{:S(2)}, u32[]{:S(2)}) %collective-permute-start.37) | collective-permute-done | bytes 131104 | tf_op jit(solution)/shard_map/ppermute | solution.py:40
  119.6 3.7 %collective-permute-done.38.refs_2_ = f32[64,512]{1,0:T(8,128)S(1)} collective-permute-done((f32[64,512]{1,0:T(8,128)S(1)}, f32[64,512]{1,0:T(8,128)S(1)}, u32[]{:S(2)}, u32[]{:S(2)}) %collective-permute-start.38) | collective-permute-done | bytes 131104 | tf_op jit(solution)/shard_map/ppermute | solution.py:40
  124.0 1.8 %collective-permute-start.42 = (bf16[96,512]{1,0:T(8,128)(2,1)S(1)}, bf16[96,512]{1,0:T(8,128)(2,1)S(1)}, u32[]{:S(2)}, u32[]{:S(2)}) collective-permute-start(bf16[96,512]{1,0:T(8,128)(2,1)S(1)} %code.1.refs_0_), channel_id=1, source_target_pairs={{0,24},{1,25},{2,26},{3,27},{4,28},{5,29},{6,30},{7,31},{8,16},{9,... | collective-permute-start | bytes 294920 | tf_op jit(solution)/shard_map/ppermute | solution.py:40
  125.8 2.6 %collective-permute-start.40 = (bf16[96,512]{1,0:T(8,128)(2,1)S(1)}, bf16[96,512]{1,0:T(8,128)(2,1)S(1)}, u32[]{:S(2)}, u32[]{:S(2)}) collective-permute-start(bf16[96,512]{1,0:T(8,128)(2,1)S(1)} %code.1.refs_0_), channel_id=1, source_target_pairs={{0,8},{1,9},{2,10},{3,11},{4,12},{5,13},{6,14},{7,15},{8,0},{9,1},... | collective-permute-start | bytes 294920 | tf_op jit(solution)/shard_map/ppermute | solution.py:40
  128.4 3.2 %collective-permute-done.42.refs_3_ = bf16[96,512]{1,0:T(8,128)(2,1)S(1)} collective-permute-done((bf16[96,512]{1,0:T(8,128)(2,1)S(1)}, bf16[96,512]{1,0:T(8,128)(2,1)S(1)}, u32[]{:S(2)}, u32[]{:S(2)}) %collective-permute-start.42) | collective-permute-done | bytes 98336 | tf_op jit(solution)/shard_map/ppermute | solution.py:40
  131.6 2.0 %collective-permute-done.41.refs_2_ = bf16[96,512]{1,0:T(8,128)(2,1)S(1)} collective-permute-done((bf16[96,512]{1,0:T(8,128)(2,1)S(1)}, bf16[96,512]{1,0:T(8,128)(2,1)S(1)}, u32[]{:S(2)}, u32[]{:S(2)}) %collective-permute-start.41) | collective-permute-done | bytes 98336 | tf_op jit(solution)/shard_map/ppermute | solution.py:40
  133.6 1.0 finish.1.refs_0_
  134.7 1.7 %collective-permute-start.45 = (bf16[128,512]{1,0:T(8,128)(2,1)S(1)}, bf16[128,512]{1,0:T(8,128)(2,1)S(1)}, u32[]{:S(2)}, u32[]{:S(2)}) collective-permute-start(bf16[128,512]{1,0:T(8,128)(2,1)S(1)} %finish.1.refs_0_), channel_id=1, source_target_pairs={{0,6},{1,7},{2,4},{3,5},{4,2},{5,3},{6,0},{7,1},{8,14},{9,15},{10,... | collective-permute-start | bytes 393224 | tf_op jit(solution)/shard_map/ppermute | solution.py:40
  136.4 1.5 collective-permute-start.44
  138.2 3.4 %collective-permute-done.45.refs_3_ = bf16[128,512]{1,0:T(8,128)(2,1)S(1)} collective-permute-done((bf16[128,512]{1,0:T(8,128)(2,1)S(1)}, bf16[128,512]{1,0:T(8,128)(2,1)S(1)}, u32[]{:S(2)}, u32[]{:S(2)}) %collective-permute-start.45) | collective-permute-done | bytes 131104 | tf_op jit(solution)/shard_map/ppermute | solution.py:40
  141.6 1.8 %collective-permute-done.44.refs_2_ = bf16[128,512]{1,0:T(8,128)(2,1)S(1)} collective-permute-done((bf16[128,512]{1,0:T(8,128)(2,1)S(1)}, bf16[128,512]{1,0:T(8,128)(2,1)S(1)}, u32[]{:S(2)}, u32[]{:S(2)}) %collective-permute-start.44) | collective-permute-done | bytes 131104 | tf_op jit(solution)/shard_map/ppermute | solution.py:40
  145.1 1.9 %gradient.1 = (bf16[256,256]{1,0:T(8,128)(2,1)S(1)}, bf16[256,256]{1,0:T(8,128)(2,1)S(1)}, bf16[256,256]{1,0:T(8,128)(2,1)S(1)}, bf16[256,256]{1,0:T(8,128)(2,1)S(1)}, f32[1,1]{1,0:T(1,128)}) custom-call(s32[3]{0:T(128)S(1)} %pad_add_fusion.place_ref, bf16[128,512]{1,0:T(8,128)(2,1)S(1)} %finish.1.refs_0_, ...), custom_call_target="tpu_custom_call" | custom-call | tf_op jit(solution)/shard_map/gradient/pallas_call | solution.py:151
  147.0 2.2 %collective-permute-start.51 = (bf16[256,256]{1,0:T(8,128)(2,1)S(1)}, bf16[256,256]{1,0:T(8,128)(2,1)S(1)}, u32[]{:S(2)}, u32[]{:S(2)}) collective-permute-start(bf16[256,256]{1,0:T(8,128)(2,1)S(1)} %get-tuple-element.173), channel_id=1, source_target_pairs={{0,16},{1,17},{2,18},{3,19},{4,20},{5,21},{6,22},{7,23},{8,24},{9,... | collective-permute-start | bytes 393224 | tf_op jit(solution)/shard_map/ppermute | solution.py:40
  149.2 2.2 %collective-permute-start.52 = (bf16[256,256]{1,0:T(8,128)(2,1)S(1)}, bf16[256,256]{1,0:T(8,128)(2,1)S(1)}, u32[]{:S(2)}, u32[]{:S(2)}) collective-permute-start(bf16[256,256]{1,0:T(8,128)(2,1)S(1)} %get-tuple-element.174), channel_id=1, source_target_pairs={{0,24},{1,25},{2,26},{3,27},{4,28},{5,29},{6,30},{7,31},{8,16},{9,... | collective-permute-start | bytes 393224 | tf_op jit(solution)/shard_map/ppermute | solution.py:40
  151.4 3.1 %collective-permute-done.50.refs_1_ = bf16[256,256]{1,0:T(8,128)(2,1)S(1)} collective-permute-done((bf16[256,256]{1,0:T(8,128)(2,1)S(1)}, bf16[256,256]{1,0:T(8,128)(2,1)S(1)}, u32[]{:S(2)}, u32[]{:S(2)}) %collective-permute-start.50) | collective-permute-done | bytes 131104 | tf_op jit(solution)/shard_map/ppermute | solution.py:40
  154.5 5.4 %collective-permute-done.51.refs_2_ = bf16[256,256]{1,0:T(8,128)(2,1)S(1)} collective-permute-done((bf16[256,256]{1,0:T(8,128)(2,1)S(1)}, bf16[256,256]{1,0:T(8,128)(2,1)S(1)}, u32[]{:S(2)}, u32[]{:S(2)}) %collective-permute-start.51) | collective-permute-done | bytes 131104 | tf_op jit(solution)/shard_map/ppermute | solution.py:40
  159.9 1.4 place.1
  (72 shorter events, 13.8 us)
Async XLA Ops:
  1.6 13.2 %collective-permute-start.10 = (bf16[32,1024]{1,0:T(8,128)(2,1)S(1)}, bf16[32,1024]{1,0:T(8,128)(2,1)S(1)}, u32[]{:S(2)}, u32[]{:S(2)}) collective-permute-start(bf16[32,1024]{1,0:T(8,128)(2,1)S(1)} %get-tuple-element.190), channel_id=1, source_target_pairs={{0,6},{1,7},{2,4},{3,5},{4,2},{5,3},{6,0},{7,1},{8,14},{9,15},{10,... | collective-permute-start | bytes 196616 | tf_op jit(solution)/shard_map/ppermute | solution.py:40
  5.6 9.4 %collective-permute-start.9 = (bf16[32,1024]{1,0:T(8,128)(2,1)S(1)}, bf16[32,1024]{1,0:T(8,128)(2,1)S(1)}, u32[]{:S(2)}, u32[]{:S(2)}) collective-permute-start(bf16[32,1024]{1,0:T(8,128)(2,1)S(1)} %get-tuple-element.191), channel_id=1, source_target_pairs={{0,4},{1,5},{2,6},{3,7},{4,0},{5,1},{6,2},{7,3},{8,12},{9,13},{10,... | collective-permute-start | bytes 196616 | tf_op jit(solution)/shard_map/ppermute | solution.py:40
  6.1 8.8 %collective-permute-start.8 = (bf16[32,1024]{1,0:T(8,128)(2,1)S(1)}, bf16[32,1024]{1,0:T(8,128)(2,1)S(1)}, u32[]{:S(2)}, u32[]{:S(2)}) collective-permute-start(bf16[32,1024]{1,0:T(8,128)(2,1)S(1)} %get-tuple-element.192), channel_id=1, source_target_pairs={{0,2},{1,3},{2,0},{3,1},{4,6},{5,7},{6,4},{7,5},{8,10},{9,11},{10,... | collective-permute-start | bytes 196616 | tf_op jit(solution)/shard_map/ppermute | solution.py:40
  7.2 11.9 %collective-permute-start.16 = (bf16[32,1024]{1,0:T(8,128)(2,1)S(1)}, bf16[32,1024]{1,0:T(8,128)(2,1)S(1)}, u32[]{:S(2)}, u32[]{:S(2)}) collective-permute-start(bf16[32,1024]{1,0:T(8,128)(2,1)S(1)} %get-tuple-element.182), channel_id=1, source_target_pairs={{0,6},{1,7},{2,4},{3,5},{4,2},{5,3},{6,0},{7,1},{8,14},{9,15},{10,... | collective-permute-start | bytes 196616 | tf_op jit(solution)/shard_map/ppermute | solution.py:40
  10.1 9.7 %collective-permute-start.15 = (bf16[32,1024]{1,0:T(8,128)(2,1)S(1)}, bf16[32,1024]{1,0:T(8,128)(2,1)S(1)}, u32[]{:S(2)}, u32[]{:S(2)}) collective-permute-start(bf16[32,1024]{1,0:T(8,128)(2,1)S(1)} %get-tuple-element.183), channel_id=1, source_target_pairs={{0,4},{1,5},{2,6},{3,7},{4,0},{5,1},{6,2},{7,3},{8,12},{9,13},{10,... | collective-permute-start | bytes 196616 | tf_op jit(solution)/shard_map/ppermute | solution.py:40
  12.8 2.0 %copy-start = (bf16[2048,1024]{1,0:T(8,128)(2,1)}, bf16[2048,1024]{1,0:T(8,128)(2,1)S(1)}, u32[]{:S(2)}) copy-start(bf16[2048,1024]{1,0:T(8,128)(2,1)S(1)} %fetch.3.refs_8_) | copy-start | bytes 12582916
  14.8 5.0 %collective-permute-start.14 = (bf16[32,1024]{1,0:T(8,128)(2,1)S(1)}, bf16[32,1024]{1,0:T(8,128)(2,1)S(1)}, u32[]{:S(2)}, u32[]{:S(2)}) collective-permute-start(bf16[32,1024]{1,0:T(8,128)(2,1)S(1)} %get-tuple-element.184), channel_id=1, source_target_pairs={{0,2},{1,3},{2,0},{3,1},{4,6},{5,7},{6,4},{7,5},{8,10},{9,11},{10,... | collective-permute-start | bytes 196616 | tf_op jit(solution)/shard_map/ppermute | solution.py:40
  15.0 6.4 %collective-permute-start.13 = (bf16[32,1024]{1,0:T(8,128)(2,1)S(1)}, bf16[32,1024]{1,0:T(8,128)(2,1)S(1)}, u32[]{:S(2)}, u32[]{:S(2)}) collective-permute-start(bf16[32,1024]{1,0:T(8,128)(2,1)S(1)} %get-tuple-element.186), channel_id=1, source_target_pairs={{0,24},{1,25},{2,26},{3,27},{4,28},{5,29},{6,30},{7,31},{8,16},{9,... | collective-permute-start | bytes 196616 | tf_op jit(solution)/shard_map/ppermute | solution.py:40
  19.0 4.3 %collective-permute-start.11 = (bf16[32,1024]{1,0:T(8,128)(2,1)S(1)}, bf16[32,1024]{1,0:T(8,128)(2,1)S(1)}, u32[]{:S(2)}, u32[]{:S(2)}) collective-permute-start(bf16[32,1024]{1,0:T(8,128)(2,1)S(1)} %get-tuple-element.187), channel_id=1, source_target_pairs={{0,8},{1,9},{2,10},{3,11},{4,12},{5,13},{6,14},{7,15},{8,0},{9,1},... | collective-permute-start | bytes 196616 | tf_op jit(solution)/shard_map/ppermute | solution.py:40
  19.0 5.2 %collective-permute-start.12 = (bf16[32,1024]{1,0:T(8,128)(2,1)S(1)}, bf16[32,1024]{1,0:T(8,128)(2,1)S(1)}, u32[]{:S(2)}, u32[]{:S(2)}) collective-permute-start(bf16[32,1024]{1,0:T(8,128)(2,1)S(1)} %get-tuple-element.188), channel_id=1, source_target_pairs={{0,16},{1,17},{2,18},{3,19},{4,20},{5,21},{6,22},{7,23},{8,24},{9,... | collective-permute-start | bytes 196616 | tf_op jit(solution)/shard_map/ppermute | solution.py:40
  24.8 15.4 %collective-permute-start.19 = (bf16[128,1024]{1,0:T(8,128)(2,1)S(1)}, bf16[128,1024]{1,0:T(8,128)(2,1)S(1)}, u32[]{:S(2)}, u32[]{:S(2)}) collective-permute-start(bf16[128,1024]{1,0:T(8,128)(2,1)S(1)} %lay.3.refs_0_), channel_id=1, source_target_pairs={{0,6},{1,7},{2,4},{3,5},{4,2},{5,3},{6,0},{7,1},{8,14},{9,15},{10,... | collective-permute-start | bytes 786440 | tf_op jit(solution)/shard_map/ppermute | solution.py:40
  27.3 12.8 %collective-permute-start.18 = (bf16[128,1024]{1,0:T(8,128)(2,1)S(1)}, bf16[128,1024]{1,0:T(8,128)(2,1)S(1)}, u32[]{:S(2)}, u32[]{:S(2)}) collective-permute-start(bf16[128,1024]{1,0:T(8,128)(2,1)S(1)} %lay.3.refs_0_), channel_id=1, source_target_pairs={{0,4},{1,5},{2,6},{3,7},{4,0},{5,1},{6,2},{7,3},{8,12},{9,13},{10,... | collective-permute-start | bytes 786440 | tf_op jit(solution)/shard_map/ppermute | solution.py:40
  27.8 12.3 %collective-permute-start.17 = (bf16[128,1024]{1,0:T(8,128)(2,1)S(1)}, bf16[128,1024]{1,0:T(8,128)(2,1)S(1)}, u32[]{:S(2)}, u32[]{:S(2)}) collective-permute-start(bf16[128,1024]{1,0:T(8,128)(2,1)S(1)} %lay.3.refs_0_), channel_id=1, source_target_pairs={{0,2},{1,3},{2,0},{3,1},{4,6},{5,7},{6,4},{7,5},{8,10},{9,11},{10,... | collective-permute-start | bytes 786440 | tf_op jit(solution)/shard_map/ppermute | solution.py:40
  28.4 6.6 %collective-permute-start.22 = (bf16[32,1024]{1,0:T(8,128)(2,1)S(1)}, bf16[32,1024]{1,0:T(8,128)(2,1)}, u32[]{:S(2)}, u32[]{:S(2)}) collective-permute-start(bf16[32,1024]{1,0:T(8,128)(2,1)S(1)} %get-tuple-element.178), channel_id=1, source_target_pairs={{0,24},{1,25},{2,26},{3,27},{4,28},{5,29},{6,30},{7,31},{8,16},{9,... | collective-permute-start | bytes 196616 | tf_op jit(solution)/shard_map/ppermute | solution.py:40
  30.0 5.6 %collective-permute-start.20 = (bf16[32,1024]{1,0:T(8,128)(2,1)S(1)}, bf16[32,1024]{1,0:T(8,128)(2,1)}, u32[]{:S(2)}, u32[]{:S(2)}) collective-permute-start(bf16[32,1024]{1,0:T(8,128)(2,1)S(1)} %get-tuple-element.180), channel_id=1, source_target_pairs={{0,8},{1,9},{2,10},{3,11},{4,12},{5,13},{6,14},{7,15},{8,0},{9,1},... | collective-permute-start | bytes 196616 | tf_op jit(solution)/shard_map/ppermute | solution.py:40
  35.0 5.2 %collective-permute-start.21 = (bf16[32,1024]{1,0:T(8,128)(2,1)S(1)}, bf16[32,1024]{1,0:T(8,128)(2,1)S(1)}, u32[]{:S(2)}, u32[]{:S(2)}) collective-permute-start(bf16[32,1024]{1,0:T(8,128)(2,1)S(1)} %get-tuple-element.181), channel_id=1, source_target_pairs={{0,16},{1,17},{2,18},{3,19},{4,20},{5,21},{6,22},{7,23},{8,24},{9,... | collective-permute-start | bytes 196616 | tf_op jit(solution)/shard_map/ppermute | solution.py:40
  40.1 2.4 %copy-start.2 = (bf16[32,1024]{1,0:T(8,128)(2,1)}, bf16[32,1024]{1,0:T(8,128)(2,1)S(1)}, u32[]{:S(2)}) copy-start(bf16[32,1024]{1,0:T(8,128)(2,1)S(1)} %collective-permute-done.21) | copy-start | bytes 196612
  40.2 1.6 collective-permute-start.23
  40.2 1.9 %collective-permute-start.24 = (bf16[128,1024]{1,0:T(8,128)(2,1)S(1)}, bf16[128,1024]{1,0:T(8,128)(2,1)S(1)}, u32[]{:S(2)}, u32[]{:S(2)}) collective-permute-start(bf16[128,1024]{1,0:T(8,128)(2,1)S(1)} %collective-permute-done.17.refs_1_), channel_id=1, source_target_pairs={{0,1},{1,0},{2,3},{3,2},{4,5},{5,4},{6,7},{7,6},{8,9},{9,8},{10,11... | collective-permute-start | bytes 786440 | tf_op jit(solution)/shard_map/ppermute | solution.py:40
  40.7 1.8 %collective-permute-start.25 = (bf16[128,1024]{1,0:T(8,128)(2,1)S(1)}, bf16[128,1024]{1,0:T(8,128)(2,1)S(1)}, u32[]{:S(2)}, u32[]{:S(2)}) collective-permute-start(bf16[128,1024]{1,0:T(8,128)(2,1)S(1)} %collective-permute-done.18.refs_2_), channel_id=1, source_target_pairs={{0,1},{1,0},{2,3},{3,2},{4,5},{5,4},{6,7},{7,6},{8,9},{9,8},{10,11... | collective-permute-start | bytes 786440 | tf_op jit(solution)/shard_map/ppermute | solution.py:40
  40.8 2.1 %collective-permute-start.26 = (bf16[128,1024]{1,0:T(8,128)(2,1)S(1)}, bf16[128,1024]{1,0:T(8,128)(2,1)S(1)}, u32[]{:S(2)}, u32[]{:S(2)}) collective-permute-start(bf16[128,1024]{1,0:T(8,128)(2,1)S(1)} %collective-permute-done.19.refs_3_), channel_id=1, source_target_pairs={{0,1},{1,0},{2,3},{3,2},{4,5},{5,4},{6,7},{7,6},{8,9},{9,8},{10,11... | collective-permute-start | bytes 786440 | tf_op jit(solution)/shard_map/ppermute | solution.py:40
  42.9 2.2 %copy-start.1 = (bf16[2048,1024]{1,0:T(8,128)(2,1)S(1)}, bf16[2048,1024]{1,0:T(8,128)(2,1)}, u32[]{:S(2)}) copy-start(bf16[2048,1024]{1,0:T(8,128)(2,1)} %copy-done) | copy-start | bytes 12582916
  49.0 30.6 %collective-permute-start.30 = (bf16[528,256]{1,0:T(8,128)(2,1)S(1)}, bf16[528,256]{1,0:T(8,128)(2,1)S(1)}, u32[]{:S(2)}, u32[]{:S(2)}) collective-permute-start(bf16[528,256]{1,0:T(8,128)(2,1)S(1)} %get-tuple-element.141), channel_id=1, source_target_pairs={{0,8},{1,9},{2,10},{3,11},{4,12},{5,13},{6,14},{7,15},{8,0},{9,1},... | collective-permute-start | bytes 811016 | tf_op jit(solution)/shard_map/ppermute | solution.py:40
  50.8 30.6 %collective-permute-start.31 = (bf16[528,256]{1,0:T(8,128)(2,1)S(1)}, bf16[528,256]{1,0:T(8,128)(2,1)S(1)}, u32[]{:S(2)}, u32[]{:S(2)}) collective-permute-start(bf16[528,256]{1,0:T(8,128)(2,1)S(1)} %get-tuple-element.142), channel_id=1, source_target_pairs={{0,16},{1,17},{2,18},{3,19},{4,20},{5,21},{6,22},{7,23},{8,24},{9,... | collective-permute-start | bytes 811016 | tf_op jit(solution)/shard_map/ppermute | solution.py:40
  51.8 29.6 %collective-permute-start.32 = (bf16[528,256]{1,0:T(8,128)(2,1)S(1)}, bf16[528,256]{1,0:T(8,128)(2,1)S(1)}, u32[]{:S(2)}, u32[]{:S(2)}) collective-permute-start(bf16[528,256]{1,0:T(8,128)(2,1)S(1)} %get-tuple-element.143), channel_id=1, source_target_pairs={{0,24},{1,25},{2,26},{3,27},{4,28},{5,29},{6,30},{7,31},{8,16},{9,... | collective-permute-start | bytes 811016 | tf_op jit(solution)/shard_map/ppermute | solution.py:40
  54.4 7.6 %collective-permute-start.4 = (bf16[128,1024]{1,0:T(8,128)(2,1)S(1)}, bf16[128,1024]{1,0:T(8,128)(2,1)S(1)}, u32[]{:S(2)}, u32[]{:S(2)}) collective-permute-start(bf16[128,1024]{1,0:T(8,128)(2,1)S(1)} %lay.2.refs_0_), channel_id=1, source_target_pairs={{0,2},{1,3},{2,0},{3,1},{4,6},{5,7},{6,4},{7,5},{8,10},{9,11},{10,... | collective-permute-start | bytes 786440 | tf_op jit(solution)/shard_map/cond/branch_1_fun/ppermute | solution.py:40
  55.9 8.5 %collective-permute-start.5 = (bf16[128,1024]{1,0:T(8,128)(2,1)S(1)}, bf16[128,1024]{1,0:T(8,128)(2,1)S(1)}, u32[]{:S(2)}, u32[]{:S(2)}) collective-permute-start(bf16[128,1024]{1,0:T(8,128)(2,1)S(1)} %lay.2.refs_0_), channel_id=1, source_target_pairs={{0,4},{1,5},{2,6},{3,7},{4,0},{5,1},{6,2},{7,3},{8,12},{9,13},{10,... | collective-permute-start | bytes 786440 | tf_op jit(solution)/shard_map/cond/branch_1_fun/ppermute | solution.py:40
  62.0 7.5 %collective-permute-start.6 = (bf16[128,1024]{1,0:T(8,128)(2,1)S(1)}, bf16[128,1024]{1,0:T(8,128)(2,1)S(1)}, u32[]{:S(2)}, u32[]{:S(2)}) collective-permute-start(bf16[128,1024]{1,0:T(8,128)(2,1)S(1)} %lay.2.refs_0_), channel_id=1, source_target_pairs={{0,6},{1,7},{2,4},{3,5},{4,2},{5,3},{6,0},{7,1},{8,14},{9,15},{10,... | collective-permute-start | bytes 786440 | tf_op jit(solution)/shard_map/cond/branch_1_fun/ppermute | solution.py:40
  69.6 2.7 %collective-permute-start.7 = (bf16[512,1024]{1,0:T(8,128)(2,1)S(1)}, bf16[512,1024]{1,0:T(8,128)(2,1)S(1)}, u32[]{:S(2)}, u32[]{:S(2)}) collective-permute-start(bf16[512,1024]{1,0:T(8,128)(2,1)S(1)} %pad_maximum_fusion), channel_id=1, source_target_pairs={{0,1},{1,0},{2,3},{3,2},{4,5},{5,4},{6,7},{7,6},{8,9},{9,8},{10,11... | collective-permute-start | bytes 3145736 | tf_op jit(solution)/shard_map/cond/branch_1_fun/ppermute | solution.py:40
  77.0 25.8 %collective-permute-start.27 = (bf16[528,256]{1,0:T(8,128)(2,1)}, bf16[528,256]{1,0:T(8,128)(2,1)S(1)}, u32[]{:S(2)}, u32[]{:S(2)}) collective-permute-start(bf16[528,256]{1,0:T(8,128)(2,1)} %get-tuple-element.137), channel_id=1, source_target_pairs={{0,8},{1,9},{2,10},{3,11},{4,12},{5,13},{6,14},{7,15},{8,0},{9,1},... | collective-permute-start | bytes 811016 | tf_op jit(solution)/shard_map/ppermute | solution.py:40
  77.7 26.8 %collective-permute-start.28 = (bf16[528,256]{1,0:T(8,128)(2,1)}, bf16[528,256]{1,0:T(8,128)(2,1)S(1)}, u32[]{:S(2)}, u32[]{:S(2)}) collective-permute-start(bf16[528,256]{1,0:T(8,128)(2,1)} %get-tuple-element.138), channel_id=1, source_target_pairs={{0,16},{1,17},{2,18},{3,19},{4,20},{5,21},{6,22},{7,23},{8,24},{9,... | collective-permute-start | bytes 811016 | tf_op jit(solution)/shard_map/ppermute | solution.py:40
  79.6 24.9 %collective-permute-start.29 = (bf16[528,256]{1,0:T(8,128)(2,1)}, bf16[528,256]{1,0:T(8,128)(2,1)S(1)}, u32[]{:S(2)}, u32[]{:S(2)}) collective-permute-start(bf16[528,256]{1,0:T(8,128)(2,1)} %get-tuple-element.139), channel_id=1, source_target_pairs={{0,24},{1,25},{2,26},{3,27},{4,28},{5,29},{6,30},{7,31},{8,16},{9,... | collective-permute-start | bytes 811016 | tf_op jit(solution)/shard_map/ppermute | solution.py:40
  84.8 2.1 %collective-permute-start = (f32[256,512]{1,0:T(8,128)}, f32[256,512]{1,0:T(8,128)S(1)}, u32[]{:S(2)}, u32[]{:S(2)}) collective-permute-start(f32[256,512]{1,0:T(8,128)} %get-tuple-element.28), channel_id=1, source_target_pairs={{0,1},{1,0},{2,3},{3,2},{4,5},{5,4},{6,7},{7,6},{8,9},{9,8},{10,11... | collective-permute-start | bytes 1572872 | tf_op jit(solution)/shard_map/cond/branch_1_fun/ppermute | solution.py:40
  88.0 5.6 %collective-permute-start.1 = (f32[64,512]{1,0:T(8,128)S(1)}, f32[64,512]{1,0:T(8,128)S(1)}, u32[]{:S(2)}, u32[]{:S(2)}) collective-permute-start(f32[64,512]{1,0:T(8,128)S(1)} %get-tuple-element.30), channel_id=1, source_target_pairs={{0,2},{1,3},{2,0},{3,1},{4,6},{5,7},{6,4},{7,5},{8,10},{9,11},{10,... | collective-permute-start | bytes 393224 | tf_op jit(solution)/shard_map/cond/branch_1_fun/ppermute | solution.py:40
  89.6 6.5 %collective-permute-start.2 = (f32[64,512]{1,0:T(8,128)S(1)}, f32[64,512]{1,0:T(8,128)S(1)}, u32[]{:S(2)}, u32[]{:S(2)}) collective-permute-start(f32[64,512]{1,0:T(8,128)S(1)} %get-tuple-element.33), channel_id=1, source_target_pairs={{0,4},{1,5},{2,6},{3,7},{4,0},{5,1},{6,2},{7,3},{8,12},{9,13},{10,... | collective-permute-start | bytes 393224 | tf_op jit(solution)/shard_map/cond/branch_1_fun/ppermute | solution.py:40
  93.6 5.9 %collective-permute-start.3 = (f32[64,512]{1,0:T(8,128)S(1)}, f32[64,512]{1,0:T(8,128)S(1)}, u32[]{:S(2)}, u32[]{:S(2)}) collective-permute-start(f32[64,512]{1,0:T(8,128)S(1)} %get-tuple-element.34), channel_id=1, source_target_pairs={{0,6},{1,7},{2,4},{3,5},{4,2},{5,3},{6,0},{7,1},{8,14},{9,15},{10,... | collective-permute-start | bytes 393224 | tf_op jit(solution)/shard_map/cond/branch_1_fun/ppermute | solution.py:40
  100.1 4.5 %collective-permute-start.33 = (f32[16,512]{1,0:T(8,128)S(1)}, f32[16,512]{1,0:T(8,128)S(1)}, u32[]{:S(2)}, u32[]{:S(2)}) collective-permute-start(f32[16,512]{1,0:T(8,128)S(1)} %get-tuple-element.147), channel_id=1, source_target_pairs={{0,8},{1,9},{2,10},{3,11},{4,12},{5,13},{6,14},{7,15},{8,0},{9,1},... | collective-permute-start | bytes 98312 | tf_op jit(solution)/shard_map/ppermute | solution.py:40
  100.1 6.4 %collective-permute-start.34 = (f32[16,512]{1,0:T(8,128)S(1)}, f32[16,512]{1,0:T(8,128)S(1)}, u32[]{:S(2)}, u32[]{:S(2)}) collective-permute-start(f32[16,512]{1,0:T(8,128)S(1)} %get-tuple-element.148), channel_id=1, source_target_pairs={{0,16},{1,17},{2,18},{3,19},{4,20},{5,21},{6,22},{7,23},{8,24},{9,... | collective-permute-start | bytes 98312 | tf_op jit(solution)/shard_map/ppermute | solution.py:40
  102.8 5.7 %collective-permute-start.35 = (f32[16,512]{1,0:T(8,128)S(1)}, f32[16,512]{1,0:T(8,128)S(1)}, u32[]{:S(2)}, u32[]{:S(2)}) collective-permute-start(f32[16,512]{1,0:T(8,128)S(1)} %get-tuple-element.149), channel_id=1, source_target_pairs={{0,24},{1,25},{2,26},{3,27},{4,28},{5,29},{6,30},{7,31},{8,16},{9,... | collective-permute-start | bytes 98312 | tf_op jit(solution)/shard_map/ppermute | solution.py:40
  111.1 2.0 %collective-permute-start.36 = (f32[256,512]{1,0:T(8,128)S(1)}, f32[256,512]{1,0:T(8,128)S(1)}, u32[]{:S(2)}, u32[]{:S(2)}) collective-permute-start(f32[256,512]{1,0:T(8,128)S(1)} %get-tuple-element.156), channel_id=1, source_target_pairs={{0,1},{1,0},{2,3},{3,2},{4,5},{5,4},{6,7},{7,6},{8,9},{9,8},{10,11... | collective-permute-start | bytes 1572872 | tf_op jit(solution)/shard_map/ppermute | solution.py:40
  113.7 5.9 %collective-permute-start.37 = (f32[64,512]{1,0:T(8,128)S(1)}, f32[64,512]{1,0:T(8,128)S(1)}, u32[]{:S(2)}, u32[]{:S(2)}) collective-permute-start(f32[64,512]{1,0:T(8,128)S(1)} %get-tuple-element.158), channel_id=1, source_target_pairs={{0,2},{1,3},{2,0},{3,1},{4,6},{5,7},{6,4},{7,5},{8,10},{9,11},{10,... | collective-permute-start | bytes 393224 | tf_op jit(solution)/shard_map/ppermute | solution.py:40
  115.2 8.1 %collective-permute-start.38 = (f32[64,512]{1,0:T(8,128)S(1)}, f32[64,512]{1,0:T(8,128)S(1)}, u32[]{:S(2)}, u32[]{:S(2)}) collective-permute-start(f32[64,512]{1,0:T(8,128)S(1)} %get-tuple-element.159), channel_id=1, source_target_pairs={{0,4},{1,5},{2,6},{3,7},{4,0},{5,1},{6,2},{7,3},{8,12},{9,13},{10,... | collective-permute-start | bytes 393224 | tf_op jit(solution)/shard_map/ppermute | solution.py:40
  116.8 6.5 %collective-permute-start.39 = (f32[64,512]{1,0:T(8,128)S(1)}, f32[64,512]{1,0:T(8,128)S(1)}, u32[]{:S(2)}, u32[]{:S(2)}) collective-permute-start(f32[64,512]{1,0:T(8,128)S(1)} %get-tuple-element.160), channel_id=1, source_target_pairs={{0,6},{1,7},{2,4},{3,5},{4,2},{5,3},{6,0},{7,1},{8,14},{9,15},{10,... | collective-permute-start | bytes 393224 | tf_op jit(solution)/shard_map/ppermute | solution.py:40
  124.0 7.6 %collective-permute-start.42 = (bf16[96,512]{1,0:T(8,128)(2,1)S(1)}, bf16[96,512]{1,0:T(8,128)(2,1)S(1)}, u32[]{:S(2)}, u32[]{:S(2)}) collective-permute-start(bf16[96,512]{1,0:T(8,128)(2,1)S(1)} %code.1.refs_0_), channel_id=1, source_target_pairs={{0,24},{1,25},{2,26},{3,27},{4,28},{5,29},{6,30},{7,31},{8,16},{9,... | collective-permute-start | bytes 294920 | tf_op jit(solution)/shard_map/ppermute | solution.py:40
  125.8 7.8 %collective-permute-start.41 = (bf16[96,512]{1,0:T(8,128)(2,1)S(1)}, bf16[96,512]{1,0:T(8,128)(2,1)S(1)}, u32[]{:S(2)}, u32[]{:S(2)}) collective-permute-start(bf16[96,512]{1,0:T(8,128)(2,1)S(1)} %code.1.refs_0_), channel_id=1, source_target_pairs={{0,16},{1,17},{2,18},{3,19},{4,20},{5,21},{6,22},{7,23},{8,24},{9,... | collective-permute-start | bytes 294920 | tf_op jit(solution)/shard_map/ppermute | solution.py:40
  125.8 7.8 %collective-permute-start.40 = (bf16[96,512]{1,0:T(8,128)(2,1)S(1)}, bf16[96,512]{1,0:T(8,128)(2,1)S(1)}, u32[]{:S(2)}, u32[]{:S(2)}) collective-permute-start(bf16[96,512]{1,0:T(8,128)(2,1)S(1)} %code.1.refs_0_), channel_id=1, source_target_pairs={{0,8},{1,9},{2,10},{3,11},{4,12},{5,13},{6,14},{7,15},{8,0},{9,1},... | collective-permute-start | bytes 294920 | tf_op jit(solution)/shard_map/ppermute | solution.py:40
  134.7 6.9 %collective-permute-start.45 = (bf16[128,512]{1,0:T(8,128)(2,1)S(1)}, bf16[128,512]{1,0:T(8,128)(2,1)S(1)}, u32[]{:S(2)}, u32[]{:S(2)}) collective-permute-start(bf16[128,512]{1,0:T(8,128)(2,1)S(1)} %finish.1.refs_0_), channel_id=1, source_target_pairs={{0,6},{1,7},{2,4},{3,5},{4,2},{5,3},{6,0},{7,1},{8,14},{9,15},{10,... | collective-permute-start | bytes 393224 | tf_op jit(solution)/shard_map/ppermute | solution.py:40
  136.4 7.0 %collective-permute-start.44 = (bf16[128,512]{1,0:T(8,128)(2,1)S(1)}, bf16[128,512]{1,0:T(8,128)(2,1)S(1)}, u32[]{:S(2)}, u32[]{:S(2)}) collective-permute-start(bf16[128,512]{1,0:T(8,128)(2,1)S(1)} %finish.1.refs_0_), channel_id=1, source_target_pairs={{0,4},{1,5},{2,6},{3,7},{4,0},{5,1},{6,2},{7,3},{8,12},{9,13},{10,... | collective-permute-start | bytes 393224 | tf_op jit(solution)/shard_map/ppermute | solution.py:40
  137.9 5.9 %collective-permute-start.43 = (bf16[128,512]{1,0:T(8,128)(2,1)S(1)}, bf16[128,512]{1,0:T(8,128)(2,1)S(1)}, u32[]{:S(2)}, u32[]{:S(2)}) collective-permute-start(bf16[128,512]{1,0:T(8,128)(2,1)S(1)} %finish.1.refs_0_), channel_id=1, source_target_pairs={{0,2},{1,3},{2,0},{3,1},{4,6},{5,7},{6,4},{7,5},{8,10},{9,11},{10,... | collective-permute-start | bytes 393224 | tf_op jit(solution)/shard_map/ppermute | solution.py:40
  138.2 5.7 %collective-permute-start.46 = (bf16[128,512]{1,0:T(8,128)(2,1)S(1)}, bf16[128,512]{1,0:T(8,128)(2,1)S(1)}, u32[]{:S(2)}, u32[]{:S(2)}) collective-permute-start(bf16[128,512]{1,0:T(8,128)(2,1)S(1)} %finish.1.refs_0_), channel_id=1, source_target_pairs={{0,1},{1,0},{2,3},{3,2},{4,5},{5,4},{6,7},{7,6},{8,9},{9,8},{10,11... | collective-permute-start | bytes 393224 | tf_op jit(solution)/shard_map/ppermute | solution.py:40
  141.6 2.4 %collective-permute-start.49 = (bf16[128,512]{1,0:T(8,128)(2,1)S(1)}, bf16[128,512]{1,0:T(8,128)(2,1)S(1)}, u32[]{:S(2)}, u32[]{:S(2)}) collective-permute-start(bf16[128,512]{1,0:T(8,128)(2,1)S(1)} %collective-permute-done.45.refs_3_), channel_id=1, source_target_pairs={{0,1},{1,0},{2,3},{3,2},{4,5},{5,4},{6,7},{7,6},{8,9},{9,8},{10,11... | collective-permute-start | bytes 393224 | tf_op jit(solution)/shard_map/ppermute | solution.py:40
  143.4 1.3 collective-permute-start.48
  143.7 1.3 collective-permute-start.47
  147.0 7.5 %collective-permute-start.50 = (bf16[256,256]{1,0:T(8,128)(2,1)S(1)}, bf16[256,256]{1,0:T(8,128)(2,1)S(1)}, u32[]{:S(2)}, u32[]{:S(2)}) collective-permute-start(bf16[256,256]{1,0:T(8,128)(2,1)S(1)} %get-tuple-element.172), channel_id=1, source_target_pairs={{0,8},{1,9},{2,10},{3,11},{4,12},{5,13},{6,14},{7,15},{8,0},{9,1},... | collective-permute-start | bytes 393224 | tf_op jit(solution)/shard_map/ppermute | solution.py:40
  147.0 12.9 %collective-permute-start.51 = (bf16[256,256]{1,0:T(8,128)(2,1)S(1)}, bf16[256,256]{1,0:T(8,128)(2,1)S(1)}, u32[]{:S(2)}, u32[]{:S(2)}) collective-permute-start(bf16[256,256]{1,0:T(8,128)(2,1)S(1)} %get-tuple-element.173), channel_id=1, source_target_pairs={{0,16},{1,17},{2,18},{3,19},{4,20},{5,21},{6,22},{7,23},{8,24},{9,... | collective-permute-start | bytes 393224 | tf_op jit(solution)/shard_map/ppermute | solution.py:40
  149.2 10.7 %collective-permute-start.52 = (bf16[256,256]{1,0:T(8,128)(2,1)S(1)}, bf16[256,256]{1,0:T(8,128)(2,1)S(1)}, u32[]{:S(2)}, u32[]{:S(2)}) collective-permute-start(bf16[256,256]{1,0:T(8,128)(2,1)S(1)} %get-tuple-element.174), channel_id=1, source_target_pairs={{0,24},{1,25},{2,26},{3,27},{4,28},{5,29},{6,30},{7,31},{8,16},{9,... | collective-permute-start | bytes 393224 | tf_op jit(solution)/shard_map/ppermute | solution.py:40

commit v6 on v5

--- a/solution.py
+++ b/solution.py
@@ -73,13 +73,14 @@
 
 def sends(place, axis, parts, few=False):
     size, here, toward = place.along(axis)
-    met = [parts[0]]
-    for step in range(1, size):
+    met = {0: parts[0]}
+    order = [*range(1, size)] if few else [*range(size - 1, 0, -1)]
+    for i, step in enumerate(order):
         part = parts[step]
-        if few and step > 2:
-            met[step - 2], part = lax.optimization_barrier((met[step - 2], part))
-        met.append(place.send(part, toward(step)))
-    return met
+        if few and i >= 2:
+            met[order[i - 2]], part = lax.optimization_barrier((met[order[i - 2]], part))
+        met[step] = place.send(part, toward(step))
+    return [met[step] for step in range(size)]
 
 
 def reduce_scatter(place, axis, value, few=False):
@@ -94,16 +95,24 @@
     return jnp.concatenate(ordered(parts, here), 0)
 
 
-def halve_kernel(place_ref, kept_ref, met_ref, *outs, axis):
+def halve_kernel(place_ref, kept_ref, met_ref, *outs):
     height = outs[0].shape[0]
     for step, out in enumerate(outs):
-        at = pl.ds(pl.multiple_of((place_ref[axis] ^ step) * height, height), height)
-        out[...] = kept_ref[at, :] + met_ref[at, :]
+        at = pl.ds(pl.multiple_of((place_ref[1] ^ step) * height, height), height)
+        total = kept_ref[at, :] + met_ref[at, :]
+        if step == 0:
+            out[...] = total
+        else:
+            encode(total, out)
+
+
+def plane_sum(met):
+    return tree_sum([met[0][...]] + [decode(ref, 1)[0] for ref in met[1:]])
 
 
 def plane_kernel(place_ref, *refs, n):
     met, outs, whole_ref = refs[:n], refs[n:-1], refs[-1]
-    whole_ref[...] = tree_sum([ref[...] for ref in met])
+    whole_ref[...] = plane_sum(met)
     height = outs[0].shape[0]
     for step, out in enumerate(outs):
         at = pl.ds(pl.multiple_of((place_ref[0] ^ step) * height, height), height)
@@ -116,7 +125,7 @@
 
 def code_kernel(place_ref, *refs, n):
     met, rows_ref, out_ref = refs[:n], refs[n], refs[n + 1]
-    total = tree_sum([ref[...] for ref in met])
+    total = plane_sum(met)
     coded = total.shape[0] + SCALE_ROWS
     encode(total, out_ref.at[:coded])
     out_ref[coded:] = rows_ref[...]
@@ -163,11 +172,12 @@
     half, batch = grams[0].shape
     kept, other = grams
     other = place.send(other, lambda z, a, b: (z, a, b ^ 1))
+    height = half // place.n
     parts = local(
-        functools.partial(halve_kernel, axis=1),
+        halve_kernel,
         place_array,
         (kept, other),
-        [((half // place.n, batch), F32)] * place.n,
+        [((height, batch), F32)] + [((height + SCALE_ROWS, batch), BF16)] * (place.n - 1),
         "halve",
     )
     return sends(place, "a", parts, few)
@@ -476,27 +486,33 @@
     n, k, z, a, b = place.n, place.k, place.z, place.a, place.b
     place_array = jnp.stack([z, a, b]).astype(jnp.int32)
     first = to_columns(place, h_first)
-    first, held = lax.optimization_barrier((first, fetch(weight)))
     first, second = lax.optimization_barrier((to_planes(place, first), to_columns(place, h_second)))
-    met, second = lax.optimization_barrier(
-        (met_rows(place, lay(place, place_array, first)), to_planes(place, second))
-    )
-
-    def projected(met, held, whole):
-        own = [jnp.concatenate(met, 0)] if whole else met
-        others = [place.send(part, lambda z, a, b: (z, a, b ^ 1)) for part in own]
-        return project(place, place_array, [met, others], held)
-
-    def second_projected(weight, *parts):
-        return projected(met_rows(place, lay(place, place_array, parts), True), fetch(weight), True)
+    first, late_weight = lax.optimization_barrier((lay(place, place_array, first), weight))
+    met_1, second, held = lax.optimization_barrier(
+        (met_rows(place, first), to_planes(place, second), fetch(late_weight))
+    )
 
     def sent(parts):
         return sends(place, "z", [parts[0], *parts])[1:]
 
-    own_1, parts_1 = projected(met, held, False)
-    second, own_1 = lax.optimization_barrier((second, own_1))
+    def swapped(part):
+        return place.send(part, lambda z, a, b: (z, a, b ^ 1))
+
+    own_1, parts_1 = project(place, place_array, [met_1, [swapped(part) for part in met_1]], held)
+    second = lay(place, place_array, second)
+    size, here, toward = place.along("a")
+    met_2 = [second] + [place.send(second, toward(step)) for step in range(1, size - 1)]
+    own_1, parts_1, met_2 = lax.optimization_barrier((own_1, parts_1, met_2))
     parts_1 = sent(parts_1)
-    own_2, parts_2 = in_one(place, second_projected, (weight, *second))
+
+    def second_projected(weight, *met):
+        last = place.send(met[0], toward(size - 1))
+        others = [swapped(jnp.concatenate(met, 0))]
+        last, others = lax.optimization_barrier((last, others))
+        others.append(swapped(last))
+        return project(place, place_array, [[*met, last], others], fetch(weight))
+
+    own_2, parts_2 = in_one(place, second_projected, (weight, *met_2))
     own_1, own_2 = lax.optimization_barrier((own_1, own_2))
     parts_2 = sent(parts_2)
     norm_1, packed_1, scale_1, *grams = normalize_parts(place, place_array, own_1, parts_1)

time: 162 us -> 152 us (0.938)
  starting transfers between devices: 60.9 us -> 56.4 us
  local copies, waits for them, and re-layouts: 6.09 us -> 1.9 us
  waiting for transfers between devices: 65 us -> 61.3 us
  other arithmetic: 0.2 us -> 2.17 us
    ppermute x53 -> x54, starting transfers between devices: 60.9 us -> 56.4 us  [send(): return lax.ppermute(value, ('dp', 'mp'), pairs)]
    unnamed x6, local copies, waits for them, and re-layouts: 4.17 us -> 0.01 us
    ppermute x53 -> x54, waiting for transfers between devices: 65 us -> 61.3 us  [send(): return lax.ppermute(value, ('dp', 'mp'), pairs)]
  transfers between devices with their start and end apart: 53 -> 54, of which waited for: 29 -> 25; matrix products, arithmetic and copies ran while one was open for 1% -> 2% of each run, Pallas kernels for 10% -> 13%
where the time goes in v6:
time: 152 us
  waiting for transfers between devices  61.3 us (40%)
  starting transfers between devices  56.4 us (37%)
  Pallas kernels  29 us (19%)
  other arithmetic  2.17 us (1%)
  local copies, waits for them, and re-layouts  1.9 us (1%)
    ppermute x54, waiting for transfers between devices, send(): return lax.ppermute(value, ('dp', 'mp'), pairs)  61.3 us
    ppermute x54, starting transfers between devices, send(): return lax.ppermute(value, ('dp', 'mp'), pairs)  56.4 us
    pallas_call x10, Pallas kernels, local(): pl.pallas_call(kernel, in_specs=[pl.BlockSpec(memory_space=pltpu.SMEM)] +...  10 us
    pallas_call x2, Pallas kernels, project(): pl.pallas_call(functools.partial(project_kernel, counts=counts, n=n, k=k)...  8.53 us
    pallas_call x2, Pallas kernels, normalize_parts(): pl.pallas_call(functools.partial(normalize_kernel, n=n, k=k, second=secon...  5.99 us
    pallas_call x2, Pallas kernels, fetch(): pl.pallas_call(fetch_kernel, in_specs=[pl.BlockSpec(memory_space=pl.ANY)]...  4.45 us
  transfers between devices with their start and end apart: 54, of which 25 were waited for; matrix products, arithmetic and copies ran while one was open for 2% of the time, Pallas kernels for 13%

profile of v6, /device:TPU:0, one launch (start us, length us, event | category | flops | bytes accessed | tf_op | source)
XLA Modules:
  0.0 151.7 jit_solution(2357308080308070183)
XLA Ops:
  0.7 0.9 dynamic-slice_bitcast_fusion.4
  1.6 3.0 %collective-permute-start.9 = (bf16[32,1024]{1,0:T(8,128)(2,1)S(1)}, bf16[32,1024]{1,0:T(8,128)(2,1)S(1)}, u32[]{:S(2)}, u32[]{:S(2)}) collective-permute-start(bf16[32,1024]{1,0:T(8,128)(2,1)S(1)} %get-tuple-element.187), channel_id=1, source_target_pairs={{0,2},{1,3},{2,0},{3,1},{4,6},{5,7},{6,4},{7,5},{8,10},{9,11},{10,... | collective-permute-start | bytes 196616 | tf_op jit(solution)/shard_map/ppermute | solution.py:40
  4.6 1.5 %collective-permute-start.8 = (bf16[32,1024]{1,0:T(8,128)(2,1)S(1)}, bf16[32,1024]{1,0:T(8,128)(2,1)S(1)}, u32[]{:S(2)}, u32[]{:S(2)}) collective-permute-start(bf16[32,1024]{1,0:T(8,128)(2,1)S(1)} %get-tuple-element.188), channel_id=1, source_target_pairs={{0,4},{1,5},{2,6},{3,7},{4,0},{5,1},{6,2},{7,3},{8,12},{9,13},{10,... | collective-permute-start | bytes 196616 | tf_op jit(solution)/shard_map/ppermute | solution.py:40
  6.1 1.0 dynamic-slice_bitcast_fusion
  7.1 3.0 %collective-permute-start.15 = (bf16[32,1024]{1,0:T(8,128)(2,1)S(1)}, bf16[32,1024]{1,0:T(8,128)(2,1)S(1)}, u32[]{:S(2)}, u32[]{:S(2)}) collective-permute-start(bf16[32,1024]{1,0:T(8,128)(2,1)S(1)} %get-tuple-element.183), channel_id=1, source_target_pairs={{0,6},{1,7},{2,4},{3,5},{4,2},{5,3},{6,0},{7,1},{8,14},{9,15},{10,... | collective-permute-start | bytes 196616 | tf_op jit(solution)/shard_map/ppermute | solution.py:40
  11.3 0.9 broadcast_select_fusion.10
  12.2 3.9 %collective-permute-start.12 = (bf16[32,1024]{1,0:T(8,128)(2,1)S(1)}, bf16[32,1024]{1,0:T(8,128)(2,1)S(1)}, u32[]{:S(2)}, u32[]{:S(2)}) collective-permute-start(bf16[32,1024]{1,0:T(8,128)(2,1)S(1)} %get-tuple-element.175), channel_id=1, source_target_pairs={{0,24},{1,25},{2,26},{3,27},{4,28},{5,29},{6,30},{7,31},{8,16},{9,... | collective-permute-start | bytes 196616 | tf_op jit(solution)/shard_map/ppermute | solution.py:40
  16.8 1.6 %collective-permute-done.12.refs_3_ = bf16[32,1024]{1,0:T(8,128)(2,1)S(1)} collective-permute-done((bf16[32,1024]{1,0:T(8,128)(2,1)S(1)}, bf16[32,1024]{1,0:T(8,128)(2,1)S(1)}, u32[]{:S(2)}, u32[]{:S(2)}) %collective-permute-start.12) | collective-permute-done | bytes 65568 | tf_op jit(solution)/shard_map/ppermute | solution.py:40
  18.4 2.1 %collective-permute-done.10.refs_1_ = bf16[32,1024]{1,0:T(8,128)(2,1)S(1)} collective-permute-done((bf16[32,1024]{1,0:T(8,128)(2,1)S(1)}, bf16[32,1024]{1,0:T(8,128)(2,1)S(1)}, u32[]{:S(2)}, u32[]{:S(2)}) %collective-permute-start.10) | collective-permute-done | bytes 65568 | tf_op jit(solution)/shard_map/ppermute | solution.py:40
  21.8 2.1 %collective-permute-start.18 = (bf16[128,1024]{1,0:T(8,128)(2,1)S(1)}, bf16[128,1024]{1,0:T(8,128)(2,1)S(1)}, u32[]{:S(2)}, u32[]{:S(2)}) collective-permute-start(bf16[128,1024]{1,0:T(8,128)(2,1)S(1)} %lay.2.refs_0_), channel_id=1, source_target_pairs={{0,6},{1,7},{2,4},{3,5},{4,2},{5,3},{6,0},{7,1},{8,14},{9,15},{10,... | collective-permute-start | bytes 786440 | tf_op jit(solution)/shard_map/ppermute | solution.py:40
  24.4 0.9 collective-permute-start.16
  25.4 1.7 %collective-permute-start.21 = (bf16[32,1024]{1,0:T(8,128)(2,1)S(1)}, bf16[32,1024]{1,0:T(8,128)(2,1)S(1)}, u32[]{:S(2)}, u32[]{:S(2)}) collective-permute-start(bf16[32,1024]{1,0:T(8,128)(2,1)S(1)} %get-tuple-element.179), channel_id=1, source_target_pairs={{0,24},{1,25},{2,26},{3,27},{4,28},{5,29},{6,30},{7,31},{8,16},{9,... | collective-permute-start | bytes 196616 | tf_op jit(solution)/shard_map/ppermute | solution.py:40
  27.5 4.1 %collective-permute-done.21.refs_3_ = bf16[32,1024]{1,0:T(8,128)(2,1)S(1)} collective-permute-done((bf16[32,1024]{1,0:T(8,128)(2,1)S(1)}, bf16[32,1024]{1,0:T(8,128)(2,1)S(1)}, u32[]{:S(2)}, u32[]{:S(2)}) %collective-permute-start.21) | collective-permute-done | bytes 65568 | tf_op jit(solution)/shard_map/ppermute | solution.py:40
  31.7 2.2 %fetch.3.refs_8_ = bf16[2048,1024]{1,0:T(8,128)(2,1)S(1)} custom-call(bf16[2048,1024]{1,0:T(8,128)(2,1)} %weight_ref), custom_call_target="tpu_custom_call" | custom-call | bytes 8388608 | tf_op jit(solution)/shard_map/fetch/pallas_call | solution.py:234
  33.9 3.6 %collective-permute-done.20.refs_2_ = bf16[32,1024]{1,0:T(8,128)(2,1)S(1)} collective-permute-done((bf16[32,1024]{1,0:T(8,128)(2,1)S(1)}, bf16[32,1024]{1,0:T(8,128)(2,1)S(1)}, u32[]{:S(2)}, u32[]{:S(2)}) %collective-permute-start.20) | collective-permute-done | bytes 65568 | tf_op jit(solution)/shard_map/ppermute | solution.py:40
  39.8 1.5 collective-permute-start.26
  41.3 3.9 %project.3 = (f32[512,256]{1,0:T(8,128)S(1)}, bf16[528,256]{1,0:T(8,128)(2,1)S(1)}, bf16[528,256]{1,0:T(8,128)(2,1)S(1)}, bf16[528,256]{1,0:T(8,128)(2,1)S(1)}) custom-call(s32[3]{0:T(128)S(1)} %pad_add_fusion.place_ref, bf16[128,1024]{1,0:T(8,128)(2,1)S(1)} %lay.2.refs_0_, bf16[128,1024]{1,0:T(8,128)(2,1)S(1)} %collective-permute-done.16.refs_1_, ...), custom_call_target="tpu_custom_call" | custom-call | flops 2147483648 | bytes 7864320 | tf_op jit(solution)/shard_map/project/pallas_call | solution.py:328
  45.2 2.3 %collective-permute-done.27 = bf16[128,1024]{1,0:T(8,128)(2,1)S(1)} collective-permute-done((bf16[128,1024]{1,0:T(8,128)(2,1)S(1)}, bf16[128,1024]{1,0:T(8,128)(2,1)S(1)}, u32[]{:S(2)}, u32[]{:S(2)}) %collective-permute-start.27) | collective-permute-done | bytes 262176 | tf_op jit(solution)/shard_map/ppermute | solution.py:40
  47.8 1.7 %collective-permute-start.31 = (bf16[528,256]{1,0:T(8,128)(2,1)S(1)}, bf16[528,256]{1,0:T(8,128)(2,1)S(1)}, u32[]{:S(2)}, u32[]{:S(2)}) collective-permute-start(bf16[528,256]{1,0:T(8,128)(2,1)S(1)} %get-tuple-element.138), channel_id=1, source_target_pairs={{0,8},{1,9},{2,10},{3,11},{4,12},{5,13},{6,14},{7,15},{8,0},{9,1},... | collective-permute-start | bytes 811016 | tf_op jit(solution)/shard_map/ppermute | solution.py:40
  49.5 1.1 collective-permute-start.32
  50.7 1.5 collective-permute-start.33
  52.2 17.8 %conditional.2 = ((f32[512,256]{1,0:T(8,128)S(1)}, bf16[528,256]{1,0:T(8,128)(2,1)}, bf16[528,256]{1,0:T(8,128)(2,1)}, bf16[528,256]{1,0:T(8,128)(2,1)})) conditional(s32[]{:T(128)} %convert_element_type.4, () %tuple.34, (bf16[128,1024]{1,0:T(8,128)(2,1)}, bf16[128,1024]{1,0:T(8,128)(2,1)}, bf16[128,1024]{1,0:T(8,128)(2,1)}, ...), branch_computations={%region_0.1_spmd, %region_1.2_spmd} | conditional | flops 2149842944 | bytes 26214612 | solution.py:201
  52.2 1.2 pad_maximum_fusion
  53.5 1.5 collective-permute-start.4
  55.0 8.1 %collective-permute-done.4.refs_3_ = bf16[128,1024]{1,0:T(8,128)(2,1)S(1)} collective-permute-done((bf16[128,1024]{1,0:T(8,128)(2,1)S(1)}, bf16[128,1024]{1,0:T(8,128)(2,1)S(1)}, u32[]{:S(2)}, u32[]{:S(2)}) %collective-permute-start.4) | collective-permute-done | bytes 262176 | tf_op jit(solution)/shard_map/cond/branch_1_fun/ppermute | solution.py:40
  63.1 2.3 %fetch.2.refs_6_ = bf16[2048,1024]{1,0:T(8,128)(2,1)S(1)} custom-call(bf16[2048,1024]{1,0:T(8,128)(2,1)} %get-tuple-element.22.weight_ref), custom_call_target="tpu_custom_call" | custom-call | bytes 8388608 | tf_op jit(solution)/shard_map/cond/branch_1_fun/fetch/pallas_call | solution.py:234
  65.4 4.6 %project.2 = (f32[512,256]{1,0:T(8,128)S(1)}, bf16[528,256]{1,0:T(8,128)(2,1)}, bf16[528,256]{1,0:T(8,128)(2,1)}, bf16[528,256]{1,0:T(8,128)(2,1)}) custom-call(s32[3]{0:T(128)S(1)} %get-tuple-element.16.place_ref, bf16[128,1024]{1,0:T(8,128)(2,1)S(1)} %copy-done.1, bf16[128,1024]{1,0:T(8,128)(2,1)S(1)} %copy-done.5, bf16[128,1024]{1,0:T(8,128)(2,1)S(1)} %copy-done.3, ...), custom_call_target="tpu_custom_call" | custom-call | flops 2147483648 | bytes 7864320 | tf_op jit(solution)/shard_map/cond/branch_1_fun/project/pallas_call | solution.py:328
  70.0 0.9 collective-permute-start.28
  70.9 2.0 %collective-permute-start.29 = (bf16[528,256]{1,0:T(8,128)(2,1)}, bf16[528,256]{1,0:T(8,128)(2,1)S(1)}, u32[]{:S(2)}, u32[]{:S(2)}) collective-permute-start(bf16[528,256]{1,0:T(8,128)(2,1)} %get-tuple-element.135), channel_id=1, source_target_pairs={{0,16},{1,17},{2,18},{3,19},{4,20},{5,21},{6,22},{7,23},{8,24},{9,... | collective-permute-start | bytes 811016 | tf_op jit(solution)/shard_map/ppermute | solution.py:40
  72.9 1.5 collective-permute-start.30
  74.4 3.4 %normalize.2 = (f32[512,256]{1,0:T(8,128)S(1)}, bf16[512,256]{1,0:T(8,128)(2,1)S(1)}, f32[1,256]{1,0:T(1,128)S(1)}, f32[256,512]{1,0:T(8,128)}, f32[256,512]{1,0:T(8,128)}) custom-call(s32[3]{0:T(128)S(1)} %pad_add_fusion.place_ref, f32[512,256]{1,0:T(8,128)S(1)} %get-tuple-element.137.refs_0_, bf16[528,256]{1,0:T(8,128)(2,1)S(1)} %collective-permute-done.31.refs_1_, ...), custom_call_target="tpu_custom_call" | custom-call | flops 134217728 | bytes 3145728 | tf_op jit(solution)/shard_map/normalize/pallas_call | solution.py:407
  77.8 14.3 %conditional.3 = ((f32[16,512]{1,0:T(8,128)S(1)}, f32[16,512]{1,0:T(8,128)S(1)}, f32[16,512]{1,0:T(8,128)S(1)}, f32[16,512]{1,0:T(8,128)S(1)})) conditional(s32[]{:T(128)} %convert_element_type.4, () %tuple.37, (f32[256,512]{1,0:T(8,128)}, s32[3]{0:T(128)S(1)}, f32[256,512]{1,0:T(8,128)}) %tuple.38), branch_computations={%region_2.3_spmd, %region_3.4_spmd} | conditional | bytes 3080360 | solution.py:201
  77.8 2.1 %collective-permute-done.met_ref = f32[256,512]{1,0:T(8,128)S(1)} collective-permute-done((f32[256,512]{1,0:T(8,128)}, f32[256,512]{1,0:T(8,128)S(1)}, u32[]{:S(2)}, u32[]{:S(2)}) %collective-permute-start) | collective-permute-done | bytes 524320 | tf_op jit(solution)/shard_map/cond/branch_1_fun/ppermute | solution.py:40
  79.9 1.3 halve.2
  81.3 1.6 %collective-permute-start.1 = (bf16[80,512]{1,0:T(8,128)(2,1)S(1)}, bf16[80,512]{1,0:T(8,128)(2,1)S(1)}, u32[]{:S(2)}, u32[]{:S(2)}) collective-permute-start(bf16[80,512]{1,0:T(8,128)(2,1)S(1)} %get-tuple-element.27), channel_id=1, source_target_pairs={{0,2},{1,3},{2,0},{3,1},{4,6},{5,7},{6,4},{7,5},{8,10},{9,11},{10,... | collective-permute-start | bytes 245768 | tf_op jit(solution)/shard_map/cond/branch_1_fun/ppermute | solution.py:40
  83.3 2.5 %collective-permute-done.1.refs_1_ = bf16[80,512]{1,0:T(8,128)(2,1)S(1)} collective-permute-done((bf16[80,512]{1,0:T(8,128)(2,1)S(1)}, bf16[80,512]{1,0:T(8,128)(2,1)S(1)}, u32[]{:S(2)}, u32[]{:S(2)}) %collective-permute-start.1) | collective-permute-done | bytes 81952 | tf_op jit(solution)/shard_map/cond/branch_1_fun/ppermute | solution.py:40
  85.8 1.4 collective-permute-start.3
  87.3 3.9 %collective-permute-done.3.refs_3_ = bf16[80,512]{1,0:T(8,128)(2,1)S(1)} collective-permute-done((bf16[80,512]{1,0:T(8,128)(2,1)S(1)}, bf16[80,512]{1,0:T(8,128)(2,1)S(1)}, u32[]{:S(2)}, u32[]{:S(2)}) %collective-permute-start.3) | collective-permute-done | bytes 81952 | tf_op jit(solution)/shard_map/cond/branch_1_fun/ppermute | solution.py:40
  91.2 0.9 plane.1
  92.1 1.1 collective-permute-start.34
  93.2 1.9 %collective-permute-start.35 = (f32[16,512]{1,0:T(8,128)S(1)}, f32[16,512]{1,0:T(8,128)S(1)}, u32[]{:S(2)}, u32[]{:S(2)}) collective-permute-start(f32[16,512]{1,0:T(8,128)S(1)} %get-tuple-element.145), channel_id=1, source_target_pairs={{0,16},{1,17},{2,18},{3,19},{4,20},{5,21},{6,22},{7,23},{8,24},{9,... | collective-permute-start | bytes 98312 | tf_op jit(solution)/shard_map/ppermute | solution.py:40
  95.0 1.5 collective-permute-start.36
  96.5 3.7 %collective-permute-done.35.refs_2_ = f32[16,512]{1,0:T(8,128)S(1)} collective-permute-done((f32[16,512]{1,0:T(8,128)S(1)}, f32[16,512]{1,0:T(8,128)S(1)}, u32[]{:S(2)}, u32[]{:S(2)}) %collective-permute-start.35) | collective-permute-done | bytes 32800 | tf_op jit(solution)/shard_map/ppermute | solution.py:40
  100.9 2.6 %normalize.3 = (f32[512,256]{1,0:T(8,128)S(1)}, bf16[512,256]{1,0:T(8,128)(2,1)S(1)}, f32[1,256]{1,0:T(1,128)S(1)}, f32[256,512]{1,0:T(8,128)S(1)}, f32[256,512]{1,0:T(8,128)S(1)}, /*index=5*/f32[1,256]{1,0:T(1,128)S(1)}) custom-call(s32[3]{0:T(128)S(1)} %pad_add_fusion.place_ref, f32[512,256]{1,0:T(8,128)S(1)} %get-tuple-element.147.refs_0_, ...), custom_call_target="tpu_custom_call" | custom-call | flops 134217728 | bytes 3145728 | tf_op jit(solution)/shard_map/normalize/pallas_call | solution.py:407
  103.6 1.9 %collective-permute-done.37.met_ref = f32[256,512]{1,0:T(8,128)S(1)} collective-permute-done((f32[256,512]{1,0:T(8,128)S(1)}, f32[256,512]{1,0:T(8,128)S(1)}, u32[]{:S(2)}, u32[]{:S(2)}) %collective-permute-start.37) | collective-permute-done | bytes 524320 | tf_op jit(solution)/shard_map/ppermute | solution.py:40
  106.3 1.6 %collective-permute-start.38 = (bf16[80,512]{1,0:T(8,128)(2,1)S(1)}, bf16[80,512]{1,0:T(8,128)(2,1)S(1)}, u32[]{:S(2)}, u32[]{:S(2)}) collective-permute-start(bf16[80,512]{1,0:T(8,128)(2,1)S(1)} %get-tuple-element.155), channel_id=1, source_target_pairs={{0,2},{1,3},{2,0},{3,1},{4,6},{5,7},{6,4},{7,5},{8,10},{9,11},{10,... | collective-permute-start | bytes 245768 | tf_op jit(solution)/shard_map/ppermute | solution.py:40
  108.4 1.5 collective-permute-start.40
  110.8 3.2 %collective-permute-done.39.refs_2_ = bf16[80,512]{1,0:T(8,128)(2,1)S(1)} collective-permute-done((bf16[80,512]{1,0:T(8,128)(2,1)S(1)}, bf16[80,512]{1,0:T(8,128)(2,1)S(1)}, u32[]{:S(2)}, u32[]{:S(2)}) %collective-permute-start.39) | collective-permute-done | bytes 81952 | tf_op jit(solution)/shard_map/ppermute | solution.py:40
  114.1 0.9 code.1.refs_0_
  115.0 1.5 %collective-permute-start.43 = (bf16[96,512]{1,0:T(8,128)(2,1)S(1)}, bf16[96,512]{1,0:T(8,128)(2,1)S(1)}, u32[]{:S(2)}, u32[]{:S(2)}) collective-permute-start(bf16[96,512]{1,0:T(8,128)(2,1)S(1)} %code.1.refs_0_), channel_id=1, source_target_pairs={{0,24},{1,25},{2,26},{3,27},{4,28},{5,29},{6,30},{7,31},{8,16},{9,... | collective-permute-start | bytes 294920 | tf_op jit(solution)/shard_map/ppermute | solution.py:40
  117.1 2.3 %collective-permute-start.41 = (bf16[96,512]{1,0:T(8,128)(2,1)S(1)}, bf16[96,512]{1,0:T(8,128)(2,1)S(1)}, u32[]{:S(2)}, u32[]{:S(2)}) collective-permute-start(bf16[96,512]{1,0:T(8,128)(2,1)S(1)} %code.1.refs_0_), channel_id=1, source_target_pairs={{0,8},{1,9},{2,10},{3,11},{4,12},{5,13},{6,14},{7,15},{8,0},{9,1},... | collective-permute-start | bytes 294920 | tf_op jit(solution)/shard_map/ppermute | solution.py:40
  119.4 2.6 %collective-permute-done.43.refs_3_ = bf16[96,512]{1,0:T(8,128)(2,1)S(1)} collective-permute-done((bf16[96,512]{1,0:T(8,128)(2,1)S(1)}, bf16[96,512]{1,0:T(8,128)(2,1)S(1)}, u32[]{:S(2)}, u32[]{:S(2)}) %collective-permute-start.43) | collective-permute-done | bytes 98336 | tf_op jit(solution)/shard_map/ppermute | solution.py:40
  122.0 3.0 %collective-permute-done.42.refs_2_ = bf16[96,512]{1,0:T(8,128)(2,1)S(1)} collective-permute-done((bf16[96,512]{1,0:T(8,128)(2,1)S(1)}, bf16[96,512]{1,0:T(8,128)(2,1)S(1)}, u32[]{:S(2)}, u32[]{:S(2)}) %collective-permute-start.42) | collective-permute-done | bytes 98336 | tf_op jit(solution)/shard_map/ppermute | solution.py:40
  125.0 1.0 finish.1.refs_0_
  126.0 1.8 %collective-permute-start.46 = (bf16[128,512]{1,0:T(8,128)(2,1)S(1)}, bf16[128,512]{1,0:T(8,128)(2,1)S(1)}, u32[]{:S(2)}, u32[]{:S(2)}) collective-permute-start(bf16[128,512]{1,0:T(8,128)(2,1)S(1)} %finish.1.refs_0_), channel_id=1, source_target_pairs={{0,6},{1,7},{2,4},{3,5},{4,2},{5,3},{6,0},{7,1},{8,14},{9,15},{10,... | collective-permute-start | bytes 393224 | tf_op jit(solution)/shard_map/ppermute | solution.py:40
  128.4 1.2 collective-permute-start.44
  129.6 3.3 %collective-permute-done.46.refs_3_ = bf16[128,512]{1,0:T(8,128)(2,1)S(1)} collective-permute-done((bf16[128,512]{1,0:T(8,128)(2,1)S(1)}, bf16[128,512]{1,0:T(8,128)(2,1)S(1)}, u32[]{:S(2)}, u32[]{:S(2)}) %collective-permute-start.46) | collective-permute-done | bytes 131104 | tf_op jit(solution)/shard_map/ppermute | solution.py:40
  132.9 1.0 collective-permute-done.45.refs_2_
  135.5 1.9 %gradient.1 = (bf16[256,256]{1,0:T(8,128)(2,1)S(1)}, bf16[256,256]{1,0:T(8,128)(2,1)S(1)}, bf16[256,256]{1,0:T(8,128)(2,1)S(1)}, bf16[256,256]{1,0:T(8,128)(2,1)S(1)}, f32[1,1]{1,0:T(1,128)}) custom-call(s32[3]{0:T(128)S(1)} %pad_add_fusion.place_ref, bf16[128,512]{1,0:T(8,128)(2,1)S(1)} %finish.1.refs_0_, ...), custom_call_target="tpu_custom_call" | custom-call | tf_op jit(solution)/shard_map/gradient/pallas_call | solution.py:160
  137.4 2.3 %collective-permute-start.52 = (bf16[256,256]{1,0:T(8,128)(2,1)S(1)}, bf16[256,256]{1,0:T(8,128)(2,1)S(1)}, u32[]{:S(2)}, u32[]{:S(2)}) collective-permute-start(bf16[256,256]{1,0:T(8,128)(2,1)S(1)} %get-tuple-element.170), channel_id=1, source_target_pairs={{0,16},{1,17},{2,18},{3,19},{4,20},{5,21},{6,22},{7,23},{8,24},{9,... | collective-permute-start | bytes 393224 | tf_op jit(solution)/shard_map/ppermute | solution.py:40
  139.7 2.1 %collective-permute-start.53 = (bf16[256,256]{1,0:T(8,128)(2,1)S(1)}, bf16[256,256]{1,0:T(8,128)(2,1)S(1)}, u32[]{:S(2)}, u32[]{:S(2)}) collective-permute-start(bf16[256,256]{1,0:T(8,128)(2,1)S(1)} %get-tuple-element.171), channel_id=1, source_target_pairs={{0,24},{1,25},{2,26},{3,27},{4,28},{5,29},{6,30},{7,31},{8,16},{9,... | collective-permute-start | bytes 393224 | tf_op jit(solution)/shard_map/ppermute | solution.py:40
  141.8 3.3 %collective-permute-done.51.refs_1_ = bf16[256,256]{1,0:T(8,128)(2,1)S(1)} collective-permute-done((bf16[256,256]{1,0:T(8,128)(2,1)S(1)}, bf16[256,256]{1,0:T(8,128)(2,1)S(1)}, u32[]{:S(2)}, u32[]{:S(2)}) %collective-permute-start.51) | collective-permute-done | bytes 131104 | tf_op jit(solution)/shard_map/ppermute | solution.py:40
  145.1 5.2 %collective-permute-done.52.refs_2_ = bf16[256,256]{1,0:T(8,128)(2,1)S(1)} collective-permute-done((bf16[256,256]{1,0:T(8,128)(2,1)S(1)}, bf16[256,256]{1,0:T(8,128)(2,1)S(1)}, u32[]{:S(2)}, u32[]{:S(2)}) %collective-permute-start.52) | collective-permute-done | bytes 131104 | tf_op jit(solution)/shard_map/ppermute | solution.py:40
  150.3 1.4 place.1
  (80 shorter events, 13.2 us)
Async XLA Ops:
  1.6 9.0 %collective-permute-start.9 = (bf16[32,1024]{1,0:T(8,128)(2,1)S(1)}, bf16[32,1024]{1,0:T(8,128)(2,1)S(1)}, u32[]{:S(2)}, u32[]{:S(2)}) collective-permute-start(bf16[32,1024]{1,0:T(8,128)(2,1)S(1)} %get-tuple-element.187), channel_id=1, source_target_pairs={{0,2},{1,3},{2,0},{3,1},{4,6},{5,7},{6,4},{7,5},{8,10},{9,11},{10,... | collective-permute-start | bytes 196616 | tf_op jit(solution)/shard_map/ppermute | solution.py:40
  4.6 6.1 %collective-permute-start.8 = (bf16[32,1024]{1,0:T(8,128)(2,1)S(1)}, bf16[32,1024]{1,0:T(8,128)(2,1)S(1)}, u32[]{:S(2)}, u32[]{:S(2)}) collective-permute-start(bf16[32,1024]{1,0:T(8,128)(2,1)S(1)} %get-tuple-element.188), channel_id=1, source_target_pairs={{0,4},{1,5},{2,6},{3,7},{4,0},{5,1},{6,2},{7,3},{8,12},{9,13},{10,... | collective-permute-start | bytes 196616 | tf_op jit(solution)/shard_map/ppermute | solution.py:40
  6.1 5.2 %collective-permute-start.7 = (bf16[32,1024]{1,0:T(8,128)(2,1)S(1)}, bf16[32,1024]{1,0:T(8,128)(2,1)S(1)}, u32[]{:S(2)}, u32[]{:S(2)}) collective-permute-start(bf16[32,1024]{1,0:T(8,128)(2,1)S(1)} %get-tuple-element.189), channel_id=1, source_target_pairs={{0,6},{1,7},{2,4},{3,5},{4,2},{5,3},{6,0},{7,1},{8,14},{9,15},{10,... | collective-permute-start | bytes 196616 | tf_op jit(solution)/shard_map/ppermute | solution.py:40
  7.1 9.0 %collective-permute-start.15 = (bf16[32,1024]{1,0:T(8,128)(2,1)S(1)}, bf16[32,1024]{1,0:T(8,128)(2,1)S(1)}, u32[]{:S(2)}, u32[]{:S(2)}) collective-permute-start(bf16[32,1024]{1,0:T(8,128)(2,1)S(1)} %get-tuple-element.183), channel_id=1, source_target_pairs={{0,6},{1,7},{2,4},{3,5},{4,2},{5,3},{6,0},{7,1},{8,14},{9,15},{10,... | collective-permute-start | bytes 196616 | tf_op jit(solution)/shard_map/ppermute | solution.py:40
  10.1 6.7 %collective-permute-start.14 = (bf16[32,1024]{1,0:T(8,128)(2,1)S(1)}, bf16[32,1024]{1,0:T(8,128)(2,1)S(1)}, u32[]{:S(2)}, u32[]{:S(2)}) collective-permute-start(bf16[32,1024]{1,0:T(8,128)(2,1)S(1)} %get-tuple-element.184), channel_id=1, source_target_pairs={{0,4},{1,5},{2,6},{3,7},{4,0},{5,1},{6,2},{7,3},{8,12},{9,13},{10,... | collective-permute-start | bytes 196616 | tf_op jit(solution)/shard_map/ppermute | solution.py:40
  10.6 6.2 %collective-permute-start.13 = (bf16[32,1024]{1,0:T(8,128)(2,1)S(1)}, bf16[32,1024]{1,0:T(8,128)(2,1)S(1)}, u32[]{:S(2)}, u32[]{:S(2)}) collective-permute-start(bf16[32,1024]{1,0:T(8,128)(2,1)S(1)} %get-tuple-element.185), channel_id=1, source_target_pairs={{0,2},{1,3},{2,0},{3,1},{4,6},{5,7},{6,4},{7,5},{8,10},{9,11},{10,... | collective-permute-start | bytes 196616 | tf_op jit(solution)/shard_map/ppermute | solution.py:40
  12.2 6.2 %collective-permute-start.12 = (bf16[32,1024]{1,0:T(8,128)(2,1)S(1)}, bf16[32,1024]{1,0:T(8,128)(2,1)S(1)}, u32[]{:S(2)}, u32[]{:S(2)}) collective-permute-start(bf16[32,1024]{1,0:T(8,128)(2,1)S(1)} %get-tuple-element.175), channel_id=1, source_target_pairs={{0,24},{1,25},{2,26},{3,27},{4,28},{5,29},{6,30},{7,31},{8,16},{9,... | collective-permute-start | bytes 196616 | tf_op jit(solution)/shard_map/ppermute | solution.py:40
  16.0 4.4 %collective-permute-start.10 = (bf16[32,1024]{1,0:T(8,128)(2,1)S(1)}, bf16[32,1024]{1,0:T(8,128)(2,1)S(1)}, u32[]{:S(2)}, u32[]{:S(2)}) collective-permute-start(bf16[32,1024]{1,0:T(8,128)(2,1)S(1)} %get-tuple-element.176), channel_id=1, source_target_pairs={{0,8},{1,9},{2,10},{3,11},{4,12},{5,13},{6,14},{7,15},{8,0},{9,1},... | collective-permute-start | bytes 196616 | tf_op jit(solution)/shard_map/ppermute | solution.py:40
  16.1 5.2 %collective-permute-start.11 = (bf16[32,1024]{1,0:T(8,128)(2,1)S(1)}, bf16[32,1024]{1,0:T(8,128)(2,1)S(1)}, u32[]{:S(2)}, u32[]{:S(2)}) collective-permute-start(bf16[32,1024]{1,0:T(8,128)(2,1)S(1)} %get-tuple-element.177), channel_id=1, source_target_pairs={{0,16},{1,17},{2,18},{3,19},{4,20},{5,21},{6,22},{7,23},{8,24},{9,... | collective-permute-start | bytes 196616 | tf_op jit(solution)/shard_map/ppermute | solution.py:40
  21.8 15.7 %collective-permute-start.18 = (bf16[128,1024]{1,0:T(8,128)(2,1)S(1)}, bf16[128,1024]{1,0:T(8,128)(2,1)S(1)}, u32[]{:S(2)}, u32[]{:S(2)}) collective-permute-start(bf16[128,1024]{1,0:T(8,128)(2,1)S(1)} %lay.2.refs_0_), channel_id=1, source_target_pairs={{0,6},{1,7},{2,4},{3,5},{4,2},{5,3},{6,0},{7,1},{8,14},{9,15},{10,... | collective-permute-start | bytes 786440 | tf_op jit(solution)/shard_map/ppermute | solution.py:40
  23.9 13.6 %collective-permute-start.17 = (bf16[128,1024]{1,0:T(8,128)(2,1)S(1)}, bf16[128,1024]{1,0:T(8,128)(2,1)S(1)}, u32[]{:S(2)}, u32[]{:S(2)}) collective-permute-start(bf16[128,1024]{1,0:T(8,128)(2,1)S(1)} %lay.2.refs_0_), channel_id=1, source_target_pairs={{0,4},{1,5},{2,6},{3,7},{4,0},{5,1},{6,2},{7,3},{8,12},{9,13},{10,... | collective-permute-start | bytes 786440 | tf_op jit(solution)/shard_map/ppermute | solution.py:40
  24.4 13.1 %collective-permute-start.16 = (bf16[128,1024]{1,0:T(8,128)(2,1)S(1)}, bf16[128,1024]{1,0:T(8,128)(2,1)S(1)}, u32[]{:S(2)}, u32[]{:S(2)}) collective-permute-start(bf16[128,1024]{1,0:T(8,128)(2,1)S(1)} %lay.2.refs_0_), channel_id=1, source_target_pairs={{0,2},{1,3},{2,0},{3,1},{4,6},{5,7},{6,4},{7,5},{8,10},{9,11},{10,... | collective-permute-start | bytes 786440 | tf_op jit(solution)/shard_map/ppermute | solution.py:40
  25.4 6.3 %collective-permute-start.21 = (bf16[32,1024]{1,0:T(8,128)(2,1)S(1)}, bf16[32,1024]{1,0:T(8,128)(2,1)S(1)}, u32[]{:S(2)}, u32[]{:S(2)}) collective-permute-start(bf16[32,1024]{1,0:T(8,128)(2,1)S(1)} %get-tuple-element.179), channel_id=1, source_target_pairs={{0,24},{1,25},{2,26},{3,27},{4,28},{5,29},{6,30},{7,31},{8,16},{9,... | collective-permute-start | bytes 196616 | tf_op jit(solution)/shard_map/ppermute | solution.py:40
  27.0 6.8 %collective-permute-start.19 = (bf16[32,1024]{1,0:T(8,128)(2,1)S(1)}, bf16[32,1024]{1,0:T(8,128)(2,1)S(1)}, u32[]{:S(2)}, u32[]{:S(2)}) collective-permute-start(bf16[32,1024]{1,0:T(8,128)(2,1)S(1)} %get-tuple-element.181), channel_id=1, source_target_pairs={{0,8},{1,9},{2,10},{3,11},{4,12},{5,13},{6,14},{7,15},{8,0},{9,1},... | collective-permute-start | bytes 196616 | tf_op jit(solution)/shard_map/ppermute | solution.py:40
  31.7 5.9 %collective-permute-start.20 = (bf16[32,1024]{1,0:T(8,128)(2,1)S(1)}, bf16[32,1024]{1,0:T(8,128)(2,1)S(1)}, u32[]{:S(2)}, u32[]{:S(2)}) collective-permute-start(bf16[32,1024]{1,0:T(8,128)(2,1)S(1)} %get-tuple-element.182), channel_id=1, source_target_pairs={{0,16},{1,17},{2,18},{3,19},{4,20},{5,21},{6,22},{7,23},{8,24},{9,... | collective-permute-start | bytes 196616 | tf_op jit(solution)/shard_map/ppermute | solution.py:40
  37.5 2.2 %collective-permute-start.22 = (bf16[128,1024]{1,0:T(8,128)(2,1)S(1)}, bf16[128,1024]{1,0:T(8,128)(2,1)S(1)}, u32[]{:S(2)}, u32[]{:S(2)}) collective-permute-start(bf16[128,1024]{1,0:T(8,128)(2,1)S(1)} %lay.2.refs_0_), channel_id=1, source_target_pairs={{0,1},{1,0},{2,3},{3,2},{4,5},{5,4},{6,7},{7,6},{8,9},{9,8},{10,11... | collective-permute-start | bytes 786440 | tf_op jit(solution)/shard_map/ppermute | solution.py:40
  37.6 3.7 %collective-permute-start.23 = (bf16[128,1024]{1,0:T(8,128)(2,1)S(1)}, bf16[128,1024]{1,0:T(8,128)(2,1)S(1)}, u32[]{:S(2)}, u32[]{:S(2)}) collective-permute-start(bf16[128,1024]{1,0:T(8,128)(2,1)S(1)} %collective-permute-done.16.refs_1_), channel_id=1, source_target_pairs={{0,1},{1,0},{2,3},{3,2},{4,5},{5,4},{6,7},{7,6},{8,9},{9,8},{10,11... | collective-permute-start | bytes 786440 | tf_op jit(solution)/shard_map/ppermute | solution.py:40
  38.1 3.2 %collective-permute-start.24 = (bf16[128,1024]{1,0:T(8,128)(2,1)S(1)}, bf16[128,1024]{1,0:T(8,128)(2,1)S(1)}, u32[]{:S(2)}, u32[]{:S(2)}) collective-permute-start(bf16[128,1024]{1,0:T(8,128)(2,1)S(1)} %collective-permute-done.17.refs_2_), channel_id=1, source_target_pairs={{0,1},{1,0},{2,3},{3,2},{4,5},{5,4},{6,7},{7,6},{8,9},{9,8},{10,11... | collective-permute-start | bytes 786440 | tf_op jit(solution)/shard_map/ppermute | solution.py:40
  38.2 3.1 %collective-permute-start.25 = (bf16[128,1024]{1,0:T(8,128)(2,1)S(1)}, bf16[128,1024]{1,0:T(8,128)(2,1)S(1)}, u32[]{:S(2)}, u32[]{:S(2)}) collective-permute-start(bf16[128,1024]{1,0:T(8,128)(2,1)S(1)} %collective-permute-done.18.refs_3_), channel_id=1, source_target_pairs={{0,1},{1,0},{2,3},{3,2},{4,5},{5,4},{6,7},{7,6},{8,9},{9,8},{10,11... | collective-permute-start | bytes 786440 | tf_op jit(solution)/shard_map/ppermute | solution.py:40
  39.2 6.0 %copy-start = (bf16[128,1024]{1,0:T(8,128)(2,1)}, bf16[128,1024]{1,0:T(8,128)(2,1)S(1)}, u32[]{:S(2)}) copy-start(bf16[128,1024]{1,0:T(8,128)(2,1)S(1)} %lay.3) | copy-start | bytes 786436
  39.2 8.4 %collective-permute-start.27 = (bf16[128,1024]{1,0:T(8,128)(2,1)S(1)}, bf16[128,1024]{1,0:T(8,128)(2,1)S(1)}, u32[]{:S(2)}, u32[]{:S(2)}) collective-permute-start(bf16[128,1024]{1,0:T(8,128)(2,1)S(1)} %lay.3), channel_id=1, source_target_pairs={{0,4},{1,5},{2,6},{3,7},{4,0},{5,1},{6,2},{7,3},{8,12},{9,13},{10,... | collective-permute-start | bytes 786440 | tf_op jit(solution)/shard_map/ppermute | solution.py:40
  39.8 8.0 %collective-permute-start.26 = (bf16[128,1024]{1,0:T(8,128)(2,1)S(1)}, bf16[128,1024]{1,0:T(8,128)(2,1)S(1)}, u32[]{:S(2)}, u32[]{:S(2)}) collective-permute-start(bf16[128,1024]{1,0:T(8,128)(2,1)S(1)} %lay.3), channel_id=1, source_target_pairs={{0,2},{1,3},{2,0},{3,1},{4,6},{5,7},{6,4},{7,5},{8,10},{9,11},{10,... | collective-permute-start | bytes 786440 | tf_op jit(solution)/shard_map/ppermute | solution.py:40
  47.6 3.1 %copy-start.2 = (bf16[128,1024]{1,0:T(8,128)(2,1)}, bf16[128,1024]{1,0:T(8,128)(2,1)S(1)}, u32[]{:S(2)}) copy-start(bf16[128,1024]{1,0:T(8,128)(2,1)S(1)} %collective-permute-done.27) | copy-start | bytes 786436
  47.8 2.9 %copy-start.4 = (bf16[128,1024]{1,0:T(8,128)(2,1)}, bf16[128,1024]{1,0:T(8,128)(2,1)S(1)}, u32[]{:S(2)}) copy-start(bf16[128,1024]{1,0:T(8,128)(2,1)S(1)} %collective-permute-done.26) | copy-start | bytes 786436
  47.8 25.1 %collective-permute-start.31 = (bf16[528,256]{1,0:T(8,128)(2,1)S(1)}, bf16[528,256]{1,0:T(8,128)(2,1)S(1)}, u32[]{:S(2)}, u32[]{:S(2)}) collective-permute-start(bf16[528,256]{1,0:T(8,128)(2,1)S(1)} %get-tuple-element.138), channel_id=1, source_target_pairs={{0,8},{1,9},{2,10},{3,11},{4,12},{5,13},{6,14},{7,15},{8,0},{9,1},... | collective-permute-start | bytes 811016 | tf_op jit(solution)/shard_map/ppermute | solution.py:40
  49.5 24.9 %collective-permute-start.32 = (bf16[528,256]{1,0:T(8,128)(2,1)S(1)}, bf16[528,256]{1,0:T(8,128)(2,1)S(1)}, u32[]{:S(2)}, u32[]{:S(2)}) collective-permute-start(bf16[528,256]{1,0:T(8,128)(2,1)S(1)} %get-tuple-element.139), channel_id=1, source_target_pairs={{0,16},{1,17},{2,18},{3,19},{4,20},{5,21},{6,22},{7,23},{8,24},{9,... | collective-permute-start | bytes 811016 | tf_op jit(solution)/shard_map/ppermute | solution.py:40
  50.7 23.7 %collective-permute-start.33 = (bf16[528,256]{1,0:T(8,128)(2,1)S(1)}, bf16[528,256]{1,0:T(8,128)(2,1)S(1)}, u32[]{:S(2)}, u32[]{:S(2)}) collective-permute-start(bf16[528,256]{1,0:T(8,128)(2,1)S(1)} %get-tuple-element.140), channel_id=1, source_target_pairs={{0,24},{1,25},{2,26},{3,27},{4,28},{5,29},{6,30},{7,31},{8,16},{9,... | collective-permute-start | bytes 811016 | tf_op jit(solution)/shard_map/ppermute | solution.py:40
  52.2 1.3 copy-start.1
  53.4 9.7 %collective-permute-start.5 = (bf16[384,1024]{1,0:T(8,128)(2,1)S(1)}, bf16[384,1024]{1,0:T(8,128)(2,1)S(1)}, u32[]{:S(2)}, u32[]{:S(2)}) collective-permute-start(bf16[384,1024]{1,0:T(8,128)(2,1)S(1)} %pad_maximum_fusion), channel_id=1, source_target_pairs={{0,1},{1,0},{2,3},{3,2},{4,5},{5,4},{6,7},{7,6},{8,9},{9,8},{10,11... | collective-permute-start | bytes 2359304 | tf_op jit(solution)/shard_map/cond/branch_1_fun/ppermute | solution.py:40
  53.5 9.6 %collective-permute-start.4 = (bf16[128,1024]{1,0:T(8,128)(2,1)S(1)}, bf16[128,1024]{1,0:T(8,128)(2,1)S(1)}, u32[]{:S(2)}, u32[]{:S(2)}) collective-permute-start(bf16[128,1024]{1,0:T(8,128)(2,1)S(1)} %copy-done.1), channel_id=1, source_target_pairs={{0,6},{1,7},{2,4},{3,5},{4,2},{5,3},{6,0},{7,1},{8,14},{9,15},{10,... | collective-permute-start | bytes 786440 | tf_op jit(solution)/shard_map/cond/branch_1_fun/ppermute | solution.py:40
  63.1 2.3 %collective-permute-start.6 = (bf16[128,1024]{1,0:T(8,128)(2,1)S(1)}, bf16[128,1024]{1,0:T(8,128)(2,1)S(1)}, u32[]{:S(2)}, u32[]{:S(2)}) collective-permute-start(bf16[128,1024]{1,0:T(8,128)(2,1)S(1)} %collective-permute-done.4.refs_3_), channel_id=1, source_target_pairs={{0,1},{1,0},{2,3},{3,2},{4,5},{5,4},{6,7},{7,6},{8,9},{9,8},{10,11... | collective-permute-start | bytes 786440 | tf_op jit(solution)/shard_map/cond/branch_1_fun/ppermute | solution.py:40
  63.1 2.3 %copy-start.3 = (bf16[128,1024]{1,0:T(8,128)(2,1)S(1)}, bf16[128,1024]{1,0:T(8,128)(2,1)}, u32[]{:S(2)}) copy-start(bf16[128,1024]{1,0:T(8,128)(2,1)} %get-tuple-element.19.refs_2_) | copy-start | bytes 786436 | tf_op jit(solution)/shard_map/cond
  63.1 2.3 %copy-start.5 = (bf16[128,1024]{1,0:T(8,128)(2,1)S(1)}, bf16[128,1024]{1,0:T(8,128)(2,1)}, u32[]{:S(2)}) copy-start(bf16[128,1024]{1,0:T(8,128)(2,1)} %get-tuple-element.18.refs_1_) | copy-start | bytes 786436 | tf_op jit(solution)/shard_map/cond
  70.0 25.0 %collective-permute-start.28 = (bf16[528,256]{1,0:T(8,128)(2,1)}, bf16[528,256]{1,0:T(8,128)(2,1)S(1)}, u32[]{:S(2)}, u32[]{:S(2)}) collective-permute-start(bf16[528,256]{1,0:T(8,128)(2,1)} %get-tuple-element.134), channel_id=1, source_target_pairs={{0,8},{1,9},{2,10},{3,11},{4,12},{5,13},{6,14},{7,15},{8,0},{9,1},... | collective-permute-start | bytes 811016 | tf_op jit(solution)/shard_map/ppermute | solution.py:40
  70.9 25.6 %collective-permute-start.29 = (bf16[528,256]{1,0:T(8,128)(2,1)}, bf16[528,256]{1,0:T(8,128)(2,1)S(1)}, u32[]{:S(2)}, u32[]{:S(2)}) collective-permute-start(bf16[528,256]{1,0:T(8,128)(2,1)} %get-tuple-element.135), channel_id=1, source_target_pairs={{0,16},{1,17},{2,18},{3,19},{4,20},{5,21},{6,22},{7,23},{8,24},{9,... | collective-permute-start | bytes 811016 | tf_op jit(solution)/shard_map/ppermute | solution.py:40
  72.9 23.6 %collective-permute-start.30 = (bf16[528,256]{1,0:T(8,128)(2,1)}, bf16[528,256]{1,0:T(8,128)(2,1)S(1)}, u32[]{:S(2)}, u32[]{:S(2)}) collective-permute-start(bf16[528,256]{1,0:T(8,128)(2,1)} %get-tuple-element.136), channel_id=1, source_target_pairs={{0,24},{1,25},{2,26},{3,27},{4,28},{5,29},{6,30},{7,31},{8,16},{9,... | collective-permute-start | bytes 811016 | tf_op jit(solution)/shard_map/ppermute | solution.py:40
  77.8 2.1 %collective-permute-start = (f32[256,512]{1,0:T(8,128)}, f32[256,512]{1,0:T(8,128)S(1)}, u32[]{:S(2)}, u32[]{:S(2)}) collective-permute-start(f32[256,512]{1,0:T(8,128)} %get-tuple-element.25), channel_id=1, source_target_pairs={{0,1},{1,0},{2,3},{3,2},{4,5},{5,4},{6,7},{7,6},{8,9},{9,8},{10,11... | collective-permute-start | bytes 1572872 | tf_op jit(solution)/shard_map/cond/branch_1_fun/ppermute | solution.py:40
  81.3 4.6 %collective-permute-start.1 = (bf16[80,512]{1,0:T(8,128)(2,1)S(1)}, bf16[80,512]{1,0:T(8,128)(2,1)S(1)}, u32[]{:S(2)}, u32[]{:S(2)}) collective-permute-start(bf16[80,512]{1,0:T(8,128)(2,1)S(1)} %get-tuple-element.27), channel_id=1, source_target_pairs={{0,2},{1,3},{2,0},{3,1},{4,6},{5,7},{6,4},{7,5},{8,10},{9,11},{10,... | collective-permute-start | bytes 245768 | tf_op jit(solution)/shard_map/cond/branch_1_fun/ppermute | solution.py:40
  82.8 4.4 %collective-permute-start.2 = (bf16[80,512]{1,0:T(8,128)(2,1)S(1)}, bf16[80,512]{1,0:T(8,128)(2,1)S(1)}, u32[]{:S(2)}, u32[]{:S(2)}) collective-permute-start(bf16[80,512]{1,0:T(8,128)(2,1)S(1)} %get-tuple-element.30), channel_id=1, source_target_pairs={{0,4},{1,5},{2,6},{3,7},{4,0},{5,1},{6,2},{7,3},{8,12},{9,13},{10,... | collective-permute-start | bytes 245768 | tf_op jit(solution)/shard_map/cond/branch_1_fun/ppermute | solution.py:40
  85.8 5.3 %collective-permute-start.3 = (bf16[80,512]{1,0:T(8,128)(2,1)S(1)}, bf16[80,512]{1,0:T(8,128)(2,1)S(1)}, u32[]{:S(2)}, u32[]{:S(2)}) collective-permute-start(bf16[80,512]{1,0:T(8,128)(2,1)S(1)} %get-tuple-element.31), channel_id=1, source_target_pairs={{0,6},{1,7},{2,4},{3,5},{4,2},{5,3},{6,0},{7,1},{8,14},{9,15},{10,... | collective-permute-start | bytes 245768 | tf_op jit(solution)/shard_map/cond/branch_1_fun/ppermute | solution.py:40
  92.1 4.5 %collective-permute-start.34 = (f32[16,512]{1,0:T(8,128)S(1)}, f32[16,512]{1,0:T(8,128)S(1)}, u32[]{:S(2)}, u32[]{:S(2)}) collective-permute-start(f32[16,512]{1,0:T(8,128)S(1)} %get-tuple-element.144), channel_id=1, source_target_pairs={{0,8},{1,9},{2,10},{3,11},{4,12},{5,13},{6,14},{7,15},{8,0},{9,1},... | collective-permute-start | bytes 98312 | tf_op jit(solution)/shard_map/ppermute | solution.py:40
  93.2 7.1 %collective-permute-start.35 = (f32[16,512]{1,0:T(8,128)S(1)}, f32[16,512]{1,0:T(8,128)S(1)}, u32[]{:S(2)}, u32[]{:S(2)}) collective-permute-start(f32[16,512]{1,0:T(8,128)S(1)} %get-tuple-element.145), channel_id=1, source_target_pairs={{0,16},{1,17},{2,18},{3,19},{4,20},{5,21},{6,22},{7,23},{8,24},{9,... | collective-permute-start | bytes 98312 | tf_op jit(solution)/shard_map/ppermute | solution.py:40
  95.0 5.8 %collective-permute-start.36 = (f32[16,512]{1,0:T(8,128)S(1)}, f32[16,512]{1,0:T(8,128)S(1)}, u32[]{:S(2)}, u32[]{:S(2)}) collective-permute-start(f32[16,512]{1,0:T(8,128)S(1)} %get-tuple-element.146), channel_id=1, source_target_pairs={{0,24},{1,25},{2,26},{3,27},{4,28},{5,29},{6,30},{7,31},{8,16},{9,... | collective-permute-start | bytes 98312 | tf_op jit(solution)/shard_map/ppermute | solution.py:40
  103.5 2.0 %collective-permute-start.37 = (f32[256,512]{1,0:T(8,128)S(1)}, f32[256,512]{1,0:T(8,128)S(1)}, u32[]{:S(2)}, u32[]{:S(2)}) collective-permute-start(f32[256,512]{1,0:T(8,128)S(1)} %get-tuple-element.153), channel_id=1, source_target_pairs={{0,1},{1,0},{2,3},{3,2},{4,5},{5,4},{6,7},{7,6},{8,9},{9,8},{10,11... | collective-permute-start | bytes 1572872 | tf_op jit(solution)/shard_map/ppermute | solution.py:40
  106.3 4.6 %collective-permute-start.38 = (bf16[80,512]{1,0:T(8,128)(2,1)S(1)}, bf16[80,512]{1,0:T(8,128)(2,1)S(1)}, u32[]{:S(2)}, u32[]{:S(2)}) collective-permute-start(bf16[80,512]{1,0:T(8,128)(2,1)S(1)} %get-tuple-element.155), channel_id=1, source_target_pairs={{0,2},{1,3},{2,0},{3,1},{4,6},{5,7},{6,4},{7,5},{8,10},{9,11},{10,... | collective-permute-start | bytes 245768 | tf_op jit(solution)/shard_map/ppermute | solution.py:40
  107.9 6.2 %collective-permute-start.39 = (bf16[80,512]{1,0:T(8,128)(2,1)S(1)}, bf16[80,512]{1,0:T(8,128)(2,1)S(1)}, u32[]{:S(2)}, u32[]{:S(2)}) collective-permute-start(bf16[80,512]{1,0:T(8,128)(2,1)S(1)} %get-tuple-element.156), channel_id=1, source_target_pairs={{0,4},{1,5},{2,6},{3,7},{4,0},{5,1},{6,2},{7,3},{8,12},{9,13},{10,... | collective-permute-start | bytes 245768 | tf_op jit(solution)/shard_map/ppermute | solution.py:40
  108.4 5.7 %collective-permute-start.40 = (bf16[80,512]{1,0:T(8,128)(2,1)S(1)}, bf16[80,512]{1,0:T(8,128)(2,1)S(1)}, u32[]{:S(2)}, u32[]{:S(2)}) collective-permute-start(bf16[80,512]{1,0:T(8,128)(2,1)S(1)} %get-tuple-element.157), channel_id=1, source_target_pairs={{0,6},{1,7},{2,4},{3,5},{4,2},{5,3},{6,0},{7,1},{8,14},{9,15},{10,... | collective-permute-start | bytes 245768 | tf_op jit(solution)/shard_map/ppermute | solution.py:40
  115.0 7.0 %collective-permute-start.43 = (bf16[96,512]{1,0:T(8,128)(2,1)S(1)}, bf16[96,512]{1,0:T(8,128)(2,1)S(1)}, u32[]{:S(2)}, u32[]{:S(2)}) collective-permute-start(bf16[96,512]{1,0:T(8,128)(2,1)S(1)} %code.1.refs_0_), channel_id=1, source_target_pairs={{0,24},{1,25},{2,26},{3,27},{4,28},{5,29},{6,30},{7,31},{8,16},{9,... | collective-permute-start | bytes 294920 | tf_op jit(solution)/shard_map/ppermute | solution.py:40
  116.5 8.5 %collective-permute-start.42 = (bf16[96,512]{1,0:T(8,128)(2,1)S(1)}, bf16[96,512]{1,0:T(8,128)(2,1)S(1)}, u32[]{:S(2)}, u32[]{:S(2)}) collective-permute-start(bf16[96,512]{1,0:T(8,128)(2,1)S(1)} %code.1.refs_0_), channel_id=1, source_target_pairs={{0,16},{1,17},{2,18},{3,19},{4,20},{5,21},{6,22},{7,23},{8,24},{9,... | collective-permute-start | bytes 294920 | tf_op jit(solution)/shard_map/ppermute | solution.py:40
  117.1 7.8 %collective-permute-start.41 = (bf16[96,512]{1,0:T(8,128)(2,1)S(1)}, bf16[96,512]{1,0:T(8,128)(2,1)S(1)}, u32[]{:S(2)}, u32[]{:S(2)}) collective-permute-start(bf16[96,512]{1,0:T(8,128)(2,1)S(1)} %code.1.refs_0_), channel_id=1, source_target_pairs={{0,8},{1,9},{2,10},{3,11},{4,12},{5,13},{6,14},{7,15},{8,0},{9,1},... | collective-permute-start | bytes 294920 | tf_op jit(solution)/shard_map/ppermute | solution.py:40
  126.0 6.9 %collective-permute-start.46 = (bf16[128,512]{1,0:T(8,128)(2,1)S(1)}, bf16[128,512]{1,0:T(8,128)(2,1)S(1)}, u32[]{:S(2)}, u32[]{:S(2)}) collective-permute-start(bf16[128,512]{1,0:T(8,128)(2,1)S(1)} %finish.1.refs_0_), channel_id=1, source_target_pairs={{0,6},{1,7},{2,4},{3,5},{4,2},{5,3},{6,0},{7,1},{8,14},{9,15},{10,... | collective-permute-start | bytes 393224 | tf_op jit(solution)/shard_map/ppermute | solution.py:40
  127.8 6.1 %collective-permute-start.45 = (bf16[128,512]{1,0:T(8,128)(2,1)S(1)}, bf16[128,512]{1,0:T(8,128)(2,1)S(1)}, u32[]{:S(2)}, u32[]{:S(2)}) collective-permute-start(bf16[128,512]{1,0:T(8,128)(2,1)S(1)} %finish.1.refs_0_), channel_id=1, source_target_pairs={{0,4},{1,5},{2,6},{3,7},{4,0},{5,1},{6,2},{7,3},{8,12},{9,13},{10,... | collective-permute-start | bytes 393224 | tf_op jit(solution)/shard_map/ppermute | solution.py:40
  128.4 5.6 %collective-permute-start.44 = (bf16[128,512]{1,0:T(8,128)(2,1)S(1)}, bf16[128,512]{1,0:T(8,128)(2,1)S(1)}, u32[]{:S(2)}, u32[]{:S(2)}) collective-permute-start(bf16[128,512]{1,0:T(8,128)(2,1)S(1)} %finish.1.refs_0_), channel_id=1, source_target_pairs={{0,2},{1,3},{2,0},{3,1},{4,6},{5,7},{6,4},{7,5},{8,10},{9,11},{10,... | collective-permute-start | bytes 393224 | tf_op jit(solution)/shard_map/ppermute | solution.py:40
  129.6 4.9 %collective-permute-start.47 = (bf16[128,512]{1,0:T(8,128)(2,1)S(1)}, bf16[128,512]{1,0:T(8,128)(2,1)S(1)}, u32[]{:S(2)}, u32[]{:S(2)}) collective-permute-start(bf16[128,512]{1,0:T(8,128)(2,1)S(1)} %finish.1.refs_0_), channel_id=1, source_target_pairs={{0,1},{1,0},{2,3},{3,2},{4,5},{5,4},{6,7},{7,6},{8,9},{9,8},{10,11... | collective-permute-start | bytes 393224 | tf_op jit(solution)/shard_map/ppermute | solution.py:40
  132.9 1.5 %collective-permute-start.50 = (bf16[128,512]{1,0:T(8,128)(2,1)S(1)}, bf16[128,512]{1,0:T(8,128)(2,1)S(1)}, u32[]{:S(2)}, u32[]{:S(2)}) collective-permute-start(bf16[128,512]{1,0:T(8,128)(2,1)S(1)} %collective-permute-done.46.refs_3_), channel_id=1, source_target_pairs={{0,1},{1,0},{2,3},{3,2},{4,5},{5,4},{6,7},{7,6},{8,9},{9,8},{10,11... | collective-permute-start | bytes 393224 | tf_op jit(solution)/shard_map/ppermute | solution.py:40
  133.9 1.3 collective-permute-start.49
  133.9 1.5 %collective-permute-start.48 = (bf16[128,512]{1,0:T(8,128)(2,1)S(1)}, bf16[128,512]{1,0:T(8,128)(2,1)S(1)}, u32[]{:S(2)}, u32[]{:S(2)}) collective-permute-start(bf16[128,512]{1,0:T(8,128)(2,1)S(1)} %collective-permute-done.44.refs_1_), channel_id=1, source_target_pairs={{0,1},{1,0},{2,3},{3,2},{4,5},{5,4},{6,7},{7,6},{8,9},{9,8},{10,11... | collective-permute-start | bytes 393224 | tf_op jit(solution)/shard_map/ppermute | solution.py:40
  137.4 7.7 %collective-permute-start.51 = (bf16[256,256]{1,0:T(8,128)(2,1)S(1)}, bf16[256,256]{1,0:T(8,128)(2,1)S(1)}, u32[]{:S(2)}, u32[]{:S(2)}) collective-permute-start(bf16[256,256]{1,0:T(8,128)(2,1)S(1)} %get-tuple-element.169), channel_id=1, source_target_pairs={{0,8},{1,9},{2,10},{3,11},{4,12},{5,13},{6,14},{7,15},{8,0},{9,1},... | collective-permute-start | bytes 393224 | tf_op jit(solution)/shard_map/ppermute | solution.py:40
  137.4 12.9 %collective-permute-start.52 = (bf16[256,256]{1,0:T(8,128)(2,1)S(1)}, bf16[256,256]{1,0:T(8,128)(2,1)S(1)}, u32[]{:S(2)}, u32[]{:S(2)}) collective-permute-start(bf16[256,256]{1,0:T(8,128)(2,1)S(1)} %get-tuple-element.170), channel_id=1, source_target_pairs={{0,16},{1,17},{2,18},{3,19},{4,20},{5,21},{6,22},{7,23},{8,24},{9,... | collective-permute-start | bytes 393224 | tf_op jit(solution)/shard_map/ppermute | solution.py:40
  139.7 10.6 %collective-permute-start.53 = (bf16[256,256]{1,0:T(8,128)(2,1)S(1)}, bf16[256,256]{1,0:T(8,128)(2,1)S(1)}, u32[]{:S(2)}, u32[]{:S(2)}) collective-permute-start(bf16[256,256]{1,0:T(8,128)(2,1)S(1)} %get-tuple-element.171), channel_id=1, source_target_pairs={{0,24},{1,25},{2,26},{3,27},{4,28},{5,29},{6,30},{7,31},{8,16},{9,... | collective-permute-start | bytes 393224 | tf_op jit(solution)/shard_map/ppermute | solution.py:40

commit v7 on v6

--- a/solution.py
+++ b/solution.py
@@ -277,7 +277,7 @@
     for count in counts:
         values.append(jnp.concatenate([ref[...] for ref in met[:count]], 0))
         met = met[count:]
-    for step in [*range(1, n), 0]:
+    for step in [*range(n - 1, 0, -1), 0]:
         at = pl.ds(pl.multiple_of((place_ref[0] ^ step) * columns, columns), columns)
         total = 0.0
         for i in range(k):
@@ -286,7 +286,7 @@
         if step == 0:
             own_ref[...] = total
         else:
-            encode(total, coded[step - 1])
+            encode(total, coded[n - 1 - step])
 
 
 def encode(total, coded_ref):
@@ -339,11 +339,11 @@
         ),
         name="project",
     )(place_array, *met, pltpu.with_memory_space_constraint(held, pltpu.VMEM))
-    return own, parts
+    return own, parts[::-1]
 
 
 def normalize_kernel(place_ref, *refs, n, k, second):
-    own_ref, parts = refs[0], refs[1:n]
+    own_ref, parts = refs[0], refs[n - 1 : 0 : -1]
     refs = refs[n:]
     if second:
         other_ref, refs = refs[0], refs[1:]
@@ -402,7 +402,7 @@
     ] + [jax.ShapeDtypeStruct((batch // k, batch), F32)] * k
     if second:
         out_shape.append(jax.ShapeDtypeStruct((1, columns), F32))
-    args = [own, *parts] + ([other] if second else [])
+    args = [own, *parts[::-1]] + ([other] if second else [])
     space = pl.BlockSpec(memory_space=pltpu.VMEM)
     return pl.pallas_call(
         functools.partial(normalize_kernel, n=n, k=k, second=second),
@@ -422,7 +422,7 @@
 def gradient_kernel(place_ref, *refs, n, k):
     grams, refs = refs[: n * k], refs[n * k :]
     packed, norms, scales, coeff_ref, refs = refs[0:2], refs[2:4], refs[4:6], refs[6], refs[7:]
-    outs, loss_ref = refs[:n], refs[n]
+    outs, loss_ref = [refs[0], *refs[n - 1 : 0 : -1]], refs[n]
     gram_ref, whole_ref = refs[n + 1 :]
     batch, columns = norms[0].shape
     height = grams[0].shape[0] // 2
@@ -474,7 +474,7 @@
 
 
 def place_kernel(place_ref, *refs, n):
-    parts, outs = refs[:n], refs[n:]
+    parts, outs = [refs[0], *refs[n - 1 : 0 : -1]], refs[n:]
     rows, columns = parts[0].shape[0] // len(outs), parts[0].shape[1]
     for step in range(n):
         at = pl.ds(pl.multiple_of((place_ref[0] ^ step) * columns, columns), columns)
@@ -485,8 +485,8 @@
 def with_kernels(place, h_first, h_second, weight):
     n, k, z, a, b = place.n, place.k, place.z, place.a, place.b
     place_array = jnp.stack([z, a, b]).astype(jnp.int32)
-    first = to_columns(place, h_first)
-    first, second = lax.optimization_barrier((to_planes(place, first), to_columns(place, h_second)))
+    first, second = lax.optimization_barrier((to_columns(place, h_first), h_second))
+    first, second = lax.optimization_barrier((to_planes(place, first), to_columns(place, second)))
     first, late_weight = lax.optimization_barrier((lay(place, place_array, first), weight))
     met_1, second, held = lax.optimization_barrier(
         (met_rows(place, first), to_planes(place, second), fetch(late_weight))
@@ -499,20 +499,21 @@
         return place.send(part, lambda z, a, b: (z, a, b ^ 1))
 
     own_1, parts_1 = project(place, place_array, [met_1, [swapped(part) for part in met_1]], held)
-    second = lay(place, place_array, second)
+    second, own_1 = lax.optimization_barrier((second, own_1))
+    parts_1 = sent(parts_1)
     size, here, toward = place.along("a")
-    met_2 = [second] + [place.send(second, toward(step)) for step in range(1, size - 1)]
-    own_1, parts_1, met_2 = lax.optimization_barrier((own_1, parts_1, met_2))
-    parts_1 = sent(parts_1)
-
-    def second_projected(weight, *met):
-        last = place.send(met[0], toward(size - 1))
+
+    def second_projected(weight, *parts):
+        values = lay(place, place_array, parts)
+        met = [values] + [place.send(values, toward(step)) for step in range(1, size - 1)]
+        values, met[1] = lax.optimization_barrier((values, met[1]))
+        last = place.send(values, toward(size - 1))
         others = [swapped(jnp.concatenate(met, 0))]
         last, others = lax.optimization_barrier((last, others))
         others.append(swapped(last))
         return project(place, place_array, [[*met, last], others], fetch(weight))
 
-    own_2, parts_2 = in_one(place, second_projected, (weight, *met_2))
+    own_2, parts_2 = in_one(place, second_projected, (weight, *second))
     own_1, own_2 = lax.optimization_barrier((own_1, own_2))
     parts_2 = sent(parts_2)
     norm_1, packed_1, scale_1, *grams = normalize_parts(place, place_array, own_1, parts_1)
@@ -542,7 +543,7 @@
     )
     grams = sends(place, "a", [part] * n)
     grams += [place.send(part, lambda z, a, b: (z, a, b ^ 1)) for part in grams]
-    *parts, loss = gradient(
+    first, *others, loss = gradient(
         place,
         place_array,
         grams,
@@ -554,7 +555,7 @@
     out_1, out_2 = local(
         functools.partial(place_kernel, n=n),
         place_array,
-        sends(place, "z", parts),
+        [first, *sends(place, "z", [first, *others[::-1]])[:0:-1]],
         [(h_first.shape, BF16)] * 2,
         "place",
     )

time: 152 us -> 159 us (1.046)
  waiting for transfers between devices: 61.3 us -> 68.1 us
  starting transfers between devices: 56.4 us -> 58.8 us
  other arithmetic: 2.17 us -> 0.18 us
    ppermute x54, waiting for transfers between devices: 61.3 us -> 68.1 us  [send(): return lax.ppermute(value, ('dp', 'mp'), pairs)]
    ppermute x54, starting transfers between devices: 56.4 us -> 58.8 us  [send(): return lax.ppermute(value, ('dp', 'mp'), pairs)]
  transfers between devices with their start and end apart: 54 -> 54, of which waited for: 25 -> 32; matrix products, arithmetic and copies ran while one was open for 2% -> 1% of each run, Pallas kernels for 13% -> 10%
where the time goes in v7:
time: 159 us
  waiting for transfers between devices  68.1 us (43%)
  starting transfers between devices  58.8 us (37%)
  Pallas kernels  29 us (18%)
  local copies, waits for them, and re-layouts  1.91 us (1%)
    ppermute x54, waiting for transfers between devices, send(): return lax.ppermute(value, ('dp', 'mp'), pairs)  68.1 us
    ppermute x54, starting transfers between devices, send(): return lax.ppermute(value, ('dp', 'mp'), pairs)  58.8 us
    pallas_call x10, Pallas kernels, local(): pl.pallas_call(kernel, in_specs=[pl.BlockSpec(memory_space=pltpu.SMEM)] +...  10 us
    pallas_call x2, Pallas kernels, project(): pl.pallas_call(functools.partial(project_kernel, counts=counts, n=n, k=k)...  8.49 us
    pallas_call x2, Pallas kernels, normalize_parts(): pl.pallas_call(functools.partial(normalize_kernel, n=n, k=k, second=secon...  6.03 us
    pallas_call x2, Pallas kernels, fetch(): pl.pallas_call(fetch_kernel, in_specs=[pl.BlockSpec(memory_space=pl.ANY)]...  4.39 us
  transfers between devices with their start and end apart: 54, of which 32 were waited for; matrix products, arithmetic and copies ran while one was open for 1% of the time, Pallas kernels for 10%

profile of v7, /device:TPU:0, one launch (start us, length us, event | category | flops | bytes accessed | tf_op | source)
XLA Modules:
  0.0 158.9 jit_solution(1341898776134653905)
XLA Ops:
  0.7 1.0 dynamic-slice_bitcast_fusion.4
  1.6 4.0 %collective-permute-start.11 = (bf16[32,1024]{1,0:T(8,128)(2,1)S(1)}, bf16[32,1024]{1,0:T(8,128)(2,1)S(1)}, u32[]{:S(2)}, u32[]{:S(2)}) collective-permute-start(bf16[32,1024]{1,0:T(8,128)(2,1)S(1)} %get-tuple-element.202), channel_id=1, source_target_pairs={{0,6},{1,7},{2,4},{3,5},{4,2},{5,3},{6,0},{7,1},{8,14},{9,15},{10,... | collective-permute-start | bytes 196616 | tf_op jit(solution)/shard_map/ppermute | solution.py:40
  6.2 1.6 %collective-permute-done.11 = bf16[32,1024]{1,0:T(8,128)(2,1)S(1)} collective-permute-done((bf16[32,1024]{1,0:T(8,128)(2,1)S(1)}, bf16[32,1024]{1,0:T(8,128)(2,1)S(1)}, u32[]{:S(2)}, u32[]{:S(2)}) %collective-permute-start.11) | collective-permute-done | bytes 65568 | tf_op jit(solution)/shard_map/ppermute | solution.py:40
  7.8 2.0 %collective-permute-done.10 = bf16[32,1024]{1,0:T(8,128)(2,1)S(1)} collective-permute-done((bf16[32,1024]{1,0:T(8,128)(2,1)S(1)}, bf16[32,1024]{1,0:T(8,128)(2,1)S(1)}, u32[]{:S(2)}, u32[]{:S(2)}) %collective-permute-start.10) | collective-permute-done | bytes 65568 | tf_op jit(solution)/shard_map/ppermute | solution.py:40
  10.4 3.7 %collective-permute-start.14 = (bf16[32,1024]{1,0:T(8,128)(2,1)S(1)}, bf16[32,1024]{1,0:T(8,128)(2,1)S(1)}, u32[]{:S(2)}, u32[]{:S(2)}) collective-permute-start(bf16[32,1024]{1,0:T(8,128)(2,1)S(1)} %get-tuple-element.198), channel_id=1, source_target_pairs={{0,24},{1,25},{2,26},{3,27},{4,28},{5,29},{6,30},{7,31},{8,16},{9,... | collective-permute-start | bytes 196616 | tf_op jit(solution)/shard_map/ppermute | solution.py:40
  14.1 0.8 collective-permute-start.13
  14.8 1.0 dynamic-slice_bitcast_fusion
  15.8 1.6 collective-permute-start.17
  17.8 1.6 collective-permute-start.15
  19.4 1.6 %collective-permute-done.17 = bf16[32,1024]{1,0:T(8,128)(2,1)S(1)} collective-permute-done((bf16[32,1024]{1,0:T(8,128)(2,1)S(1)}, bf16[32,1024]{1,0:T(8,128)(2,1)S(1)}, u32[]{:S(2)}, u32[]{:S(2)}) %collective-permute-start.17) | collective-permute-done | bytes 65568 | tf_op jit(solution)/shard_map/ppermute | solution.py:40
  22.6 3.2 %collective-permute-start.20 = (bf16[128,1024]{1,0:T(8,128)(2,1)S(1)}, bf16[128,1024]{1,0:T(8,128)(2,1)S(1)}, u32[]{:S(2)}, u32[]{:S(2)}) collective-permute-start(bf16[128,1024]{1,0:T(8,128)(2,1)S(1)} %lay.3.refs_0_), channel_id=1, source_target_pairs={{0,6},{1,7},{2,4},{3,5},{4,2},{5,3},{6,0},{7,1},{8,14},{9,15},{10,... | collective-permute-start | bytes 786440 | tf_op jit(solution)/shard_map/ppermute | solution.py:40
  26.5 3.8 %collective-permute-start.23 = (bf16[32,1024]{1,0:T(8,128)(2,1)S(1)}, bf16[32,1024]{1,0:T(8,128)(2,1)S(1)}, u32[]{:S(2)}, u32[]{:S(2)}) collective-permute-start(bf16[32,1024]{1,0:T(8,128)(2,1)S(1)} %get-tuple-element.190), channel_id=1, source_target_pairs={{0,24},{1,25},{2,26},{3,27},{4,28},{5,29},{6,30},{7,31},{8,16},{9,... | collective-permute-start | bytes 196616 | tf_op jit(solution)/shard_map/ppermute | solution.py:40
  30.3 2.8 %collective-permute-done.23 = bf16[32,1024]{1,0:T(8,128)(2,1)S(1)} collective-permute-done((bf16[32,1024]{1,0:T(8,128)(2,1)S(1)}, bf16[32,1024]{1,0:T(8,128)(2,1)S(1)}, u32[]{:S(2)}, u32[]{:S(2)}) %collective-permute-start.23) | collective-permute-done | bytes 65568 | tf_op jit(solution)/shard_map/ppermute | solution.py:40
  33.1 2.2 %fetch.3.refs_8_ = bf16[2048,1024]{1,0:T(8,128)(2,1)S(1)} custom-call(bf16[2048,1024]{1,0:T(8,128)(2,1)} %weight_ref), custom_call_target="tpu_custom_call" | custom-call | bytes 8388608 | tf_op jit(solution)/shard_map/fetch/pallas_call | solution.py:234
  35.3 3.6 %collective-permute-done.22 = bf16[32,1024]{1,0:T(8,128)(2,1)S(1)} collective-permute-done((bf16[32,1024]{1,0:T(8,128)(2,1)S(1)}, bf16[32,1024]{1,0:T(8,128)(2,1)S(1)}, u32[]{:S(2)}, u32[]{:S(2)}) %collective-permute-start.22) | collective-permute-done | bytes 65568 | tf_op jit(solution)/shard_map/ppermute | solution.py:40
  41.7 3.9 %project.3 = (f32[512,256]{1,0:T(8,128)S(1)}, bf16[528,256]{1,0:T(8,128)(2,1)S(1)}, bf16[528,256]{1,0:T(8,128)(2,1)S(1)}, bf16[528,256]{1,0:T(8,128)(2,1)S(1)}) custom-call(s32[3]{0:T(128)S(1)} %pad_add_fusion.place_ref, bf16[128,1024]{1,0:T(8,128)(2,1)S(1)} %lay.3.refs_0_, bf16[128,1024]{1,0:T(8,128)(2,1)S(1)} %collective-permute-done.18.refs_1_, ...), custom_call_target="tpu_custom_call" | custom-call | flops 2147483648 | bytes 7864320 | tf_op jit(solution)/shard_map/project/pallas_call | solution.py:328
  45.6 2.6 %collective-permute-start.31 = (bf16[528,256]{1,0:T(8,128)(2,1)S(1)}, bf16[528,256]{1,0:T(8,128)(2,1)S(1)}, u32[]{:S(2)}, u32[]{:S(2)}) collective-permute-start(bf16[528,256]{1,0:T(8,128)(2,1)S(1)} %get-tuple-element.153), channel_id=1, source_target_pairs={{0,24},{1,25},{2,26},{3,27},{4,28},{5,29},{6,30},{7,31},{8,16},{9,... | collective-permute-start | bytes 811016 | tf_op jit(solution)/shard_map/ppermute | solution.py:40
  48.2 1.8 %collective-permute-start.33 = (bf16[528,256]{1,0:T(8,128)(2,1)S(1)}, bf16[528,256]{1,0:T(8,128)(2,1)S(1)}, u32[]{:S(2)}, u32[]{:S(2)}) collective-permute-start(bf16[528,256]{1,0:T(8,128)(2,1)S(1)} %get-tuple-element.155), channel_id=1, source_target_pairs={{0,8},{1,9},{2,10},{3,11},{4,12},{5,13},{6,14},{7,15},{8,0},{9,1},... | collective-permute-start | bytes 811016 | tf_op jit(solution)/shard_map/ppermute | solution.py:40
  50.0 25.2 %conditional.2 = (f32[512,256]{1,0:T(8,128)S(1)}, bf16[528,256]{1,0:T(8,128)(2,1)}, bf16[528,256]{1,0:T(8,128)(2,1)}, bf16[528,256]{1,0:T(8,128)(2,1)}) conditional(s32[]{:T(128)} %convert_element_type.4, () %tuple.38, (s32[3]{0:T(128)S(1)}, bf16[32,1024]{1,0:T(8,128)(2,1)S(1)}, bf16[32,1024]{1,0:T(8,128)(2,1)S(1)}, bf16[32,1024]{1,0:T(8,128)(2,1)S(1)}, ...), branch_computations={%region_0.1_spmd, %region_1.2_spmd} | conditional | flops 2149842944 | bytes 25166056 | solution.py:201
  50.9 2.0 %collective-permute-start.5 = (bf16[128,1024]{1,0:T(8,128)(2,1)S(1)}, bf16[128,1024]{1,0:T(8,128)(2,1)S(1)}, u32[]{:S(2)}, u32[]{:S(2)}) collective-permute-start(bf16[128,1024]{1,0:T(8,128)(2,1)S(1)} %lay.2.refs_0_), channel_id=1, source_target_pairs={{0,4},{1,5},{2,6},{3,7},{4,0},{5,1},{6,2},{7,3},{8,12},{9,13},{10,... | collective-permute-start | bytes 786440 | tf_op jit(solution)/shard_map/cond/branch_1_fun/ppermute | solution.py:40
  52.9 5.3 %collective-permute-done.4.refs_1_ = bf16[128,1024]{1,0:T(8,128)(2,1)S(1)} collective-permute-done((bf16[128,1024]{1,0:T(8,128)(2,1)S(1)}, bf16[128,1024]{1,0:T(8,128)(2,1)S(1)}, u32[]{:S(2)}, u32[]{:S(2)}) %collective-permute-start.4) | collective-permute-done | bytes 262176 | tf_op jit(solution)/shard_map/cond/branch_1_fun/ppermute | solution.py:40
  58.8 1.6 %collective-permute-start.6 = (bf16[128,1024]{1,0:T(8,128)(2,1)S(1)}, bf16[128,1024]{1,0:T(8,128)(2,1)S(1)}, u32[]{:S(2)}, u32[]{:S(2)}) collective-permute-start(bf16[128,1024]{1,0:T(8,128)(2,1)S(1)} %lay.2.refs_0_), channel_id=1, source_target_pairs={{0,6},{1,7},{2,4},{3,5},{4,2},{5,3},{6,0},{7,1},{8,14},{9,15},{10,... | collective-permute-start | bytes 786440 | tf_op jit(solution)/shard_map/cond/branch_1_fun/ppermute | solution.py:40
  60.4 8.0 %collective-permute-done.6.refs_3_ = bf16[128,1024]{1,0:T(8,128)(2,1)S(1)} collective-permute-done((bf16[128,1024]{1,0:T(8,128)(2,1)S(1)}, bf16[128,1024]{1,0:T(8,128)(2,1)S(1)}, u32[]{:S(2)}, u32[]{:S(2)}) %collective-permute-start.6) | collective-permute-done | bytes 262176 | tf_op jit(solution)/shard_map/cond/branch_1_fun/ppermute | solution.py:40
  68.4 2.2 %fetch.2.refs_6_ = bf16[2048,1024]{1,0:T(8,128)(2,1)S(1)} custom-call(bf16[2048,1024]{1,0:T(8,128)(2,1)} %get-tuple-element.27.weight_ref), custom_call_target="tpu_custom_call" | custom-call | bytes 8388608 | tf_op jit(solution)/shard_map/cond/branch_1_fun/fetch/pallas_call | solution.py:234
  70.6 4.6 %project.2 = (f32[512,256]{1,0:T(8,128)S(1)}, bf16[528,256]{1,0:T(8,128)(2,1)}, bf16[528,256]{1,0:T(8,128)(2,1)}, bf16[528,256]{1,0:T(8,128)(2,1)}) custom-call(s32[3]{0:T(128)S(1)} %get-tuple-element.18.place_ref, bf16[128,1024]{1,0:T(8,128)(2,1)S(1)} %lay.2.refs_0_, bf16[128,1024]{1,0:T(8,128)(2,1)S(1)} %collective-permute-done.4.refs_1_, ...), custom_call_target="tpu_custom_call" | custom-call | flops 2147483648 | bytes 7864320 | tf_op jit(solution)/shard_map/cond/branch_1_fun/project/pallas_call | solution.py:328
  75.2 1.4 collective-permute-start.28
  76.6 2.6 %collective-permute-start.29 = (bf16[528,256]{1,0:T(8,128)(2,1)}, bf16[528,256]{1,0:T(8,128)(2,1)S(1)}, u32[]{:S(2)}, u32[]{:S(2)}) collective-permute-start(bf16[528,256]{1,0:T(8,128)(2,1)} %get-tuple-element.150), channel_id=1, source_target_pairs={{0,16},{1,17},{2,18},{3,19},{4,20},{5,21},{6,22},{7,23},{8,24},{9,... | collective-permute-start | bytes 811016 | tf_op jit(solution)/shard_map/ppermute | solution.py:40
  79.6 3.4 %normalize.2 = (f32[512,256]{1,0:T(8,128)S(1)}, bf16[512,256]{1,0:T(8,128)(2,1)S(1)}, f32[1,256]{1,0:T(1,128)S(1)}, f32[256,512]{1,0:T(8,128)}, f32[256,512]{1,0:T(8,128)}) custom-call(s32[3]{0:T(128)S(1)} %pad_add_fusion.place_ref, f32[512,256]{1,0:T(8,128)S(1)} %get-tuple-element.152.refs_0_, bf16[528,256]{1,0:T(8,128)(2,1)S(1)} %collective-permute-done.31.refs_1_, ...), custom_call_target="tpu_custom_call" | custom-call | flops 134217728 | bytes 3145728 | tf_op jit(solution)/shard_map/normalize/pallas_call | solution.py:407
  83.0 14.2 %conditional.3 = ((f32[16,512]{1,0:T(8,128)S(1)}, f32[16,512]{1,0:T(8,128)S(1)}, f32[16,512]{1,0:T(8,128)S(1)}, f32[16,512]{1,0:T(8,128)S(1)})) conditional(s32[]{:T(128)} %convert_element_type.4, () %tuple.41, (f32[256,512]{1,0:T(8,128)}, s32[3]{0:T(128)S(1)}, f32[256,512]{1,0:T(8,128)}) %tuple.42), branch_computations={%region_2.3_spmd, %region_3.4_spmd} | conditional | bytes 3080360 | solution.py:201
  83.0 2.1 %collective-permute-done.met_ref = f32[256,512]{1,0:T(8,128)S(1)} collective-permute-done((f32[256,512]{1,0:T(8,128)}, f32[256,512]{1,0:T(8,128)S(1)}, u32[]{:S(2)}, u32[]{:S(2)}) %collective-permute-start) | collective-permute-done | bytes 524320 | tf_op jit(solution)/shard_map/cond/branch_1_fun/ppermute | solution.py:40
  85.1 1.3 halve.2
  86.5 1.3 collective-permute-start.1
  87.8 0.8 collective-permute-start.2
  88.7 2.4 %collective-permute-done.1.refs_1_ = bf16[80,512]{1,0:T(8,128)(2,1)S(1)} collective-permute-done((bf16[80,512]{1,0:T(8,128)(2,1)S(1)}, bf16[80,512]{1,0:T(8,128)(2,1)S(1)}, u32[]{:S(2)}, u32[]{:S(2)}) %collective-permute-start.1) | collective-permute-done | bytes 81952 | tf_op jit(solution)/shard_map/cond/branch_1_fun/ppermute | solution.py:40
  91.0 1.5 collective-permute-start.3
  92.6 3.8 %collective-permute-done.3.refs_3_ = bf16[80,512]{1,0:T(8,128)(2,1)S(1)} collective-permute-done((bf16[80,512]{1,0:T(8,128)(2,1)S(1)}, bf16[80,512]{1,0:T(8,128)(2,1)S(1)}, u32[]{:S(2)}, u32[]{:S(2)}) %collective-permute-start.3) | collective-permute-done | bytes 81952 | tf_op jit(solution)/shard_map/cond/branch_1_fun/ppermute | solution.py:40
  96.4 0.9 plane.1
  97.8 3.5 %collective-permute-start.35 = (f32[16,512]{1,0:T(8,128)S(1)}, f32[16,512]{1,0:T(8,128)S(1)}, u32[]{:S(2)}, u32[]{:S(2)}) collective-permute-start(f32[16,512]{1,0:T(8,128)S(1)} %get-tuple-element.160), channel_id=1, source_target_pairs={{0,16},{1,17},{2,18},{3,19},{4,20},{5,21},{6,22},{7,23},{8,24},{9,... | collective-permute-start | bytes 98312 | tf_op jit(solution)/shard_map/ppermute | solution.py:40
  101.7 4.1 %collective-permute-done.35.refs_2_ = f32[16,512]{1,0:T(8,128)S(1)} collective-permute-done((f32[16,512]{1,0:T(8,128)S(1)}, f32[16,512]{1,0:T(8,128)S(1)}, u32[]{:S(2)}, u32[]{:S(2)}) %collective-permute-start.35) | collective-permute-done | bytes 32800 | tf_op jit(solution)/shard_map/ppermute | solution.py:40
  105.9 1.2 collective-permute-done.36.refs_3_
  107.1 2.6 %normalize.3 = (f32[512,256]{1,0:T(8,128)S(1)}, bf16[512,256]{1,0:T(8,128)(2,1)S(1)}, f32[1,256]{1,0:T(1,128)S(1)}, f32[256,512]{1,0:T(8,128)S(1)}, f32[256,512]{1,0:T(8,128)S(1)}, /*index=5*/f32[1,256]{1,0:T(1,128)S(1)}) custom-call(s32[3]{0:T(128)S(1)} %pad_add_fusion.place_ref, f32[512,256]{1,0:T(8,128)S(1)} %get-tuple-element.162.refs_0_, ...), custom_call_target="tpu_custom_call" | custom-call | flops 134217728 | bytes 3145728 | tf_op jit(solution)/shard_map/normalize/pallas_call | solution.py:407
  109.8 1.9 %collective-permute-done.37.met_ref = f32[256,512]{1,0:T(8,128)S(1)} collective-permute-done((f32[256,512]{1,0:T(8,128)S(1)}, f32[256,512]{1,0:T(8,128)S(1)}, u32[]{:S(2)}, u32[]{:S(2)}) %collective-permute-start.37) | collective-permute-done | bytes 524320 | tf_op jit(solution)/shard_map/ppermute | solution.py:40
  111.7 0.8 halve.3
  113.2 1.6 collective-permute-start.39
  114.7 1.4 collective-permute-start.40
  117.4 1.0 collective-permute-done.39.refs_2_
  118.5 1.6 %collective-permute-done.40.refs_3_ = bf16[80,512]{1,0:T(8,128)(2,1)S(1)} collective-permute-done((bf16[80,512]{1,0:T(8,128)(2,1)S(1)}, bf16[80,512]{1,0:T(8,128)(2,1)S(1)}, u32[]{:S(2)}, u32[]{:S(2)}) %collective-permute-start.40) | collective-permute-done | bytes 81952 | tf_op jit(solution)/shard_map/ppermute | solution.py:40
  120.1 0.9 code.1.refs_0_
  121.0 1.6 collective-permute-start.43
  122.6 2.9 %collective-permute-start.41 = (bf16[96,512]{1,0:T(8,128)(2,1)S(1)}, bf16[96,512]{1,0:T(8,128)(2,1)S(1)}, u32[]{:S(2)}, u32[]{:S(2)}) collective-permute-start(bf16[96,512]{1,0:T(8,128)(2,1)S(1)} %code.1.refs_0_), channel_id=1, source_target_pairs={{0,8},{1,9},{2,10},{3,11},{4,12},{5,13},{6,14},{7,15},{8,0},{9,1},... | collective-permute-start | bytes 294920 | tf_op jit(solution)/shard_map/ppermute | solution.py:40
  125.4 3.2 %collective-permute-done.43.refs_3_ = bf16[96,512]{1,0:T(8,128)(2,1)S(1)} collective-permute-done((bf16[96,512]{1,0:T(8,128)(2,1)S(1)}, bf16[96,512]{1,0:T(8,128)(2,1)S(1)}, u32[]{:S(2)}, u32[]{:S(2)}) %collective-permute-start.43) | collective-permute-done | bytes 98336 | tf_op jit(solution)/shard_map/ppermute | solution.py:40
  128.6 2.5 %collective-permute-done.42.refs_2_ = bf16[96,512]{1,0:T(8,128)(2,1)S(1)} collective-permute-done((bf16[96,512]{1,0:T(8,128)(2,1)S(1)}, bf16[96,512]{1,0:T(8,128)(2,1)S(1)}, u32[]{:S(2)}, u32[]{:S(2)}) %collective-permute-start.42) | collective-permute-done | bytes 98336 | tf_op jit(solution)/shard_map/ppermute | solution.py:40
  131.1 1.0 finish.1.refs_0_
  132.2 1.7 %collective-permute-start.46 = (bf16[128,512]{1,0:T(8,128)(2,1)S(1)}, bf16[128,512]{1,0:T(8,128)(2,1)S(1)}, u32[]{:S(2)}, u32[]{:S(2)}) collective-permute-start(bf16[128,512]{1,0:T(8,128)(2,1)S(1)} %finish.1.refs_0_), channel_id=1, source_target_pairs={{0,6},{1,7},{2,4},{3,5},{4,2},{5,3},{6,0},{7,1},{8,14},{9,15},{10,... | collective-permute-start | bytes 393224 | tf_op jit(solution)/shard_map/ppermute | solution.py:40
  133.8 1.5 collective-permute-start.45
  135.7 3.8 %collective-permute-done.46.refs_3_ = bf16[128,512]{1,0:T(8,128)(2,1)S(1)} collective-permute-done((bf16[128,512]{1,0:T(8,128)(2,1)S(1)}, bf16[128,512]{1,0:T(8,128)(2,1)S(1)}, u32[]{:S(2)}, u32[]{:S(2)}) %collective-permute-start.46) | collective-permute-done | bytes 131104 | tf_op jit(solution)/shard_map/ppermute | solution.py:40
  139.5 1.3 collective-permute-done.45.refs_2_
  141.4 0.8 collective-permute-done.49.refs_6_
  142.4 2.0 %gradient.1 = (bf16[256,256]{1,0:T(8,128)(2,1)S(1)}, bf16[256,256]{1,0:T(8,128)(2,1)S(1)}, bf16[256,256]{1,0:T(8,128)(2,1)S(1)}, bf16[256,256]{1,0:T(8,128)(2,1)S(1)}, f32[1,1]{1,0:T(1,128)}) custom-call(s32[3]{0:T(128)S(1)} %pad_add_fusion.place_ref, bf16[128,512]{1,0:T(8,128)(2,1)S(1)} %finish.1.refs_0_, ...), custom_call_target="tpu_custom_call" | custom-call | tf_op jit(solution)/shard_map/gradient/pallas_call | solution.py:160
  144.3 1.2 collective-permute-start.51
  145.5 3.2 %collective-permute-start.53 = (bf16[256,256]{1,0:T(8,128)(2,1)S(1)}, bf16[256,256]{1,0:T(8,128)(2,1)S(1)}, u32[]{:S(2)}, u32[]{:S(2)}) collective-permute-start(bf16[256,256]{1,0:T(8,128)(2,1)S(1)} %get-tuple-element.186), channel_id=1, source_target_pairs={{0,8},{1,9},{2,10},{3,11},{4,12},{5,13},{6,14},{7,15},{8,0},{9,1},... | collective-permute-start | bytes 393224 | tf_op jit(solution)/shard_map/ppermute | solution.py:40
  148.7 3.9 %collective-permute-done.51.refs_1_ = bf16[256,256]{1,0:T(8,128)(2,1)S(1)} collective-permute-done((bf16[256,256]{1,0:T(8,128)(2,1)S(1)}, bf16[256,256]{1,0:T(8,128)(2,1)S(1)}, u32[]{:S(2)}, u32[]{:S(2)}) %collective-permute-start.51) | collective-permute-done | bytes 131104 | tf_op jit(solution)/shard_map/ppermute | solution.py:40
  152.6 4.9 %collective-permute-done.52.refs_2_ = bf16[256,256]{1,0:T(8,128)(2,1)S(1)} collective-permute-done((bf16[256,256]{1,0:T(8,128)(2,1)S(1)}, bf16[256,256]{1,0:T(8,128)(2,1)S(1)}, u32[]{:S(2)}, u32[]{:S(2)}) %collective-permute-start.52) | collective-permute-done | bytes 131104 | tf_op jit(solution)/shard_map/ppermute | solution.py:40
  157.5 1.4 place.1
  (68 shorter events, 12.5 us)
Async XLA Ops:
  1.6 6.2 %collective-permute-start.11 = (bf16[32,1024]{1,0:T(8,128)(2,1)S(1)}, bf16[32,1024]{1,0:T(8,128)(2,1)S(1)}, u32[]{:S(2)}, u32[]{:S(2)}) collective-permute-start(bf16[32,1024]{1,0:T(8,128)(2,1)S(1)} %get-tuple-element.202), channel_id=1, source_target_pairs={{0,6},{1,7},{2,4},{3,5},{4,2},{5,3},{6,0},{7,1},{8,14},{9,15},{10,... | collective-permute-start | bytes 196616 | tf_op jit(solution)/shard_map/ppermute | solution.py:40
  5.6 4.3 %collective-permute-start.10 = (bf16[32,1024]{1,0:T(8,128)(2,1)S(1)}, bf16[32,1024]{1,0:T(8,128)(2,1)S(1)}, u32[]{:S(2)}, u32[]{:S(2)}) collective-permute-start(bf16[32,1024]{1,0:T(8,128)(2,1)S(1)} %get-tuple-element.203), channel_id=1, source_target_pairs={{0,4},{1,5},{2,6},{3,7},{4,0},{5,1},{6,2},{7,3},{8,12},{9,13},{10,... | collective-permute-start | bytes 196616 | tf_op jit(solution)/shard_map/ppermute | solution.py:40
  6.1 4.3 %collective-permute-start.9 = (bf16[32,1024]{1,0:T(8,128)(2,1)S(1)}, bf16[32,1024]{1,0:T(8,128)(2,1)S(1)}, u32[]{:S(2)}, u32[]{:S(2)}) collective-permute-start(bf16[32,1024]{1,0:T(8,128)(2,1)S(1)} %get-tuple-element.204), channel_id=1, source_target_pairs={{0,2},{1,3},{2,0},{3,1},{4,6},{5,7},{6,4},{7,5},{8,10},{9,11},{10,... | collective-permute-start | bytes 196616 | tf_op jit(solution)/shard_map/ppermute | solution.py:40
  10.4 7.4 %collective-permute-start.14 = (bf16[32,1024]{1,0:T(8,128)(2,1)S(1)}, bf16[32,1024]{1,0:T(8,128)(2,1)S(1)}, u32[]{:S(2)}, u32[]{:S(2)}) collective-permute-start(bf16[32,1024]{1,0:T(8,128)(2,1)S(1)} %get-tuple-element.198), channel_id=1, source_target_pairs={{0,24},{1,25},{2,26},{3,27},{4,28},{5,29},{6,30},{7,31},{8,16},{9,... | collective-permute-start | bytes 196616 | tf_op jit(solution)/shard_map/ppermute | solution.py:40
  14.1 5.4 %collective-permute-start.12 = (bf16[32,1024]{1,0:T(8,128)(2,1)S(1)}, bf16[32,1024]{1,0:T(8,128)(2,1)S(1)}, u32[]{:S(2)}, u32[]{:S(2)}) collective-permute-start(bf16[32,1024]{1,0:T(8,128)(2,1)S(1)} %get-tuple-element.199), channel_id=1, source_target_pairs={{0,8},{1,9},{2,10},{3,11},{4,12},{5,13},{6,14},{7,15},{8,0},{9,1},... | collective-permute-start | bytes 196616 | tf_op jit(solution)/shard_map/ppermute | solution.py:40
  14.1 5.4 %collective-permute-start.13 = (bf16[32,1024]{1,0:T(8,128)(2,1)S(1)}, bf16[32,1024]{1,0:T(8,128)(2,1)S(1)}, u32[]{:S(2)}, u32[]{:S(2)}) collective-permute-start(bf16[32,1024]{1,0:T(8,128)(2,1)S(1)} %get-tuple-element.200), channel_id=1, source_target_pairs={{0,16},{1,17},{2,18},{3,19},{4,20},{5,21},{6,22},{7,23},{8,24},{9,... | collective-permute-start | bytes 196616 | tf_op jit(solution)/shard_map/ppermute | solution.py:40
  15.8 5.2 %collective-permute-start.17 = (bf16[32,1024]{1,0:T(8,128)(2,1)S(1)}, bf16[32,1024]{1,0:T(8,128)(2,1)S(1)}, u32[]{:S(2)}, u32[]{:S(2)}) collective-permute-start(bf16[32,1024]{1,0:T(8,128)(2,1)S(1)} %get-tuple-element.194), channel_id=1, source_target_pairs={{0,6},{1,7},{2,4},{3,5},{4,2},{5,3},{6,0},{7,1},{8,14},{9,15},{10,... | collective-permute-start | bytes 196616 | tf_op jit(solution)/shard_map/ppermute | solution.py:40
  17.4 4.4 %collective-permute-start.16 = (bf16[32,1024]{1,0:T(8,128)(2,1)S(1)}, bf16[32,1024]{1,0:T(8,128)(2,1)S(1)}, u32[]{:S(2)}, u32[]{:S(2)}) collective-permute-start(bf16[32,1024]{1,0:T(8,128)(2,1)S(1)} %get-tuple-element.195), channel_id=1, source_target_pairs={{0,4},{1,5},{2,6},{3,7},{4,0},{5,1},{6,2},{7,3},{8,12},{9,13},{10,... | collective-permute-start | bytes 196616 | tf_op jit(solution)/shard_map/ppermute | solution.py:40
  17.8 4.3 %collective-permute-start.15 = (bf16[32,1024]{1,0:T(8,128)(2,1)S(1)}, bf16[32,1024]{1,0:T(8,128)(2,1)S(1)}, u32[]{:S(2)}, u32[]{:S(2)}) collective-permute-start(bf16[32,1024]{1,0:T(8,128)(2,1)S(1)} %get-tuple-element.196), channel_id=1, source_target_pairs={{0,2},{1,3},{2,0},{3,1},{4,6},{5,7},{6,4},{7,5},{8,10},{9,11},{10,... | collective-permute-start | bytes 196616 | tf_op jit(solution)/shard_map/ppermute | solution.py:40
  22.6 16.3 %collective-permute-start.20 = (bf16[128,1024]{1,0:T(8,128)(2,1)S(1)}, bf16[128,1024]{1,0:T(8,128)(2,1)S(1)}, u32[]{:S(2)}, u32[]{:S(2)}) collective-permute-start(bf16[128,1024]{1,0:T(8,128)(2,1)S(1)} %lay.3.refs_0_), channel_id=1, source_target_pairs={{0,6},{1,7},{2,4},{3,5},{4,2},{5,3},{6,0},{7,1},{8,14},{9,15},{10,... | collective-permute-start | bytes 786440 | tf_op jit(solution)/shard_map/ppermute | solution.py:40
  25.8 13.1 %collective-permute-start.19 = (bf16[128,1024]{1,0:T(8,128)(2,1)S(1)}, bf16[128,1024]{1,0:T(8,128)(2,1)S(1)}, u32[]{:S(2)}, u32[]{:S(2)}) collective-permute-start(bf16[128,1024]{1,0:T(8,128)(2,1)S(1)} %lay.3.refs_0_), channel_id=1, source_target_pairs={{0,4},{1,5},{2,6},{3,7},{4,0},{5,1},{6,2},{7,3},{8,12},{9,13},{10,... | collective-permute-start | bytes 786440 | tf_op jit(solution)/shard_map/ppermute | solution.py:40
  25.8 13.1 %collective-permute-start.18 = (bf16[128,1024]{1,0:T(8,128)(2,1)S(1)}, bf16[128,1024]{1,0:T(8,128)(2,1)S(1)}, u32[]{:S(2)}, u32[]{:S(2)}) collective-permute-start(bf16[128,1024]{1,0:T(8,128)(2,1)S(1)} %lay.3.refs_0_), channel_id=1, source_target_pairs={{0,2},{1,3},{2,0},{3,1},{4,6},{5,7},{6,4},{7,5},{8,10},{9,11},{10,... | collective-permute-start | bytes 786440 | tf_op jit(solution)/shard_map/ppermute | solution.py:40
  26.5 6.6 %collective-permute-start.23 = (bf16[32,1024]{1,0:T(8,128)(2,1)S(1)}, bf16[32,1024]{1,0:T(8,128)(2,1)S(1)}, u32[]{:S(2)}, u32[]{:S(2)}) collective-permute-start(bf16[32,1024]{1,0:T(8,128)(2,1)S(1)} %get-tuple-element.190), channel_id=1, source_target_pairs={{0,24},{1,25},{2,26},{3,27},{4,28},{5,29},{6,30},{7,31},{8,16},{9,... | collective-permute-start | bytes 196616 | tf_op jit(solution)/shard_map/ppermute | solution.py:40
  30.3 5.0 %collective-permute-start.21 = (bf16[32,1024]{1,0:T(8,128)(2,1)S(1)}, bf16[32,1024]{1,0:T(8,128)(2,1)S(1)}, u32[]{:S(2)}, u32[]{:S(2)}) collective-permute-start(bf16[32,1024]{1,0:T(8,128)(2,1)S(1)} %get-tuple-element.192), channel_id=1, source_target_pairs={{0,8},{1,9},{2,10},{3,11},{4,12},{5,13},{6,14},{7,15},{8,0},{9,1},... | collective-permute-start | bytes 196616 | tf_op jit(solution)/shard_map/ppermute | solution.py:40
  33.1 5.9 %collective-permute-start.22 = (bf16[32,1024]{1,0:T(8,128)(2,1)S(1)}, bf16[32,1024]{1,0:T(8,128)(2,1)S(1)}, u32[]{:S(2)}, u32[]{:S(2)}) collective-permute-start(bf16[32,1024]{1,0:T(8,128)(2,1)S(1)} %get-tuple-element.193), channel_id=1, source_target_pairs={{0,16},{1,17},{2,18},{3,19},{4,20},{5,21},{6,22},{7,23},{8,24},{9,... | collective-permute-start | bytes 196616 | tf_op jit(solution)/shard_map/ppermute | solution.py:40
  38.9 1.6 %collective-permute-start.24 = (bf16[128,1024]{1,0:T(8,128)(2,1)S(1)}, bf16[128,1024]{1,0:T(8,128)(2,1)S(1)}, u32[]{:S(2)}, u32[]{:S(2)}) collective-permute-start(bf16[128,1024]{1,0:T(8,128)(2,1)S(1)} %lay.3.refs_0_), channel_id=1, source_target_pairs={{0,1},{1,0},{2,3},{3,2},{4,5},{5,4},{6,7},{7,6},{8,9},{9,8},{10,11... | collective-permute-start | bytes 786440 | tf_op jit(solution)/shard_map/ppermute | solution.py:40
  39.0 1.9 %collective-permute-start.25 = (bf16[128,1024]{1,0:T(8,128)(2,1)S(1)}, bf16[128,1024]{1,0:T(8,128)(2,1)S(1)}, u32[]{:S(2)}, u32[]{:S(2)}) collective-permute-start(bf16[128,1024]{1,0:T(8,128)(2,1)S(1)} %collective-permute-done.18.refs_1_), channel_id=1, source_target_pairs={{0,1},{1,0},{2,3},{3,2},{4,5},{5,4},{6,7},{7,6},{8,9},{9,8},{10,11... | collective-permute-start | bytes 786440 | tf_op jit(solution)/shard_map/ppermute | solution.py:40
  39.5 1.8 %collective-permute-start.26 = (bf16[128,1024]{1,0:T(8,128)(2,1)S(1)}, bf16[128,1024]{1,0:T(8,128)(2,1)S(1)}, u32[]{:S(2)}, u32[]{:S(2)}) collective-permute-start(bf16[128,1024]{1,0:T(8,128)(2,1)S(1)} %collective-permute-done.19.refs_2_), channel_id=1, source_target_pairs={{0,1},{1,0},{2,3},{3,2},{4,5},{5,4},{6,7},{7,6},{8,9},{9,8},{10,11... | collective-permute-start | bytes 786440 | tf_op jit(solution)/shard_map/ppermute | solution.py:40
  39.6 2.1 %collective-permute-start.27 = (bf16[128,1024]{1,0:T(8,128)(2,1)S(1)}, bf16[128,1024]{1,0:T(8,128)(2,1)S(1)}, u32[]{:S(2)}, u32[]{:S(2)}) collective-permute-start(bf16[128,1024]{1,0:T(8,128)(2,1)S(1)} %collective-permute-done.20.refs_3_), channel_id=1, source_target_pairs={{0,1},{1,0},{2,3},{3,2},{4,5},{5,4},{6,7},{7,6},{8,9},{9,8},{10,11... | collective-permute-start | bytes 786440 | tf_op jit(solution)/shard_map/ppermute | solution.py:40
  45.6 33.7 %collective-permute-start.31 = (bf16[528,256]{1,0:T(8,128)(2,1)S(1)}, bf16[528,256]{1,0:T(8,128)(2,1)S(1)}, u32[]{:S(2)}, u32[]{:S(2)}) collective-permute-start(bf16[528,256]{1,0:T(8,128)(2,1)S(1)} %get-tuple-element.153), channel_id=1, source_target_pairs={{0,24},{1,25},{2,26},{3,27},{4,28},{5,29},{6,30},{7,31},{8,16},{9,... | collective-permute-start | bytes 811016 | tf_op jit(solution)/shard_map/ppermute | solution.py:40
  48.2 31.4 %collective-permute-start.32 = (bf16[528,256]{1,0:T(8,128)(2,1)S(1)}, bf16[528,256]{1,0:T(8,128)(2,1)S(1)}, u32[]{:S(2)}, u32[]{:S(2)}) collective-permute-start(bf16[528,256]{1,0:T(8,128)(2,1)S(1)} %get-tuple-element.154), channel_id=1, source_target_pairs={{0,16},{1,17},{2,18},{3,19},{4,20},{5,21},{6,22},{7,23},{8,24},{9,... | collective-permute-start | bytes 811016 | tf_op jit(solution)/shard_map/ppermute | solution.py:40
  48.2 31.4 %collective-permute-start.33 = (bf16[528,256]{1,0:T(8,128)(2,1)S(1)}, bf16[528,256]{1,0:T(8,128)(2,1)S(1)}, u32[]{:S(2)}, u32[]{:S(2)}) collective-permute-start(bf16[528,256]{1,0:T(8,128)(2,1)S(1)} %get-tuple-element.155), channel_id=1, source_target_pairs={{0,8},{1,9},{2,10},{3,11},{4,12},{5,13},{6,14},{7,15},{8,0},{9,1},... | collective-permute-start | bytes 811016 | tf_op jit(solution)/shard_map/ppermute | solution.py:40
  50.6 7.6 %collective-permute-start.4 = (bf16[128,1024]{1,0:T(8,128)(2,1)S(1)}, bf16[128,1024]{1,0:T(8,128)(2,1)S(1)}, u32[]{:S(2)}, u32[]{:S(2)}) collective-permute-start(bf16[128,1024]{1,0:T(8,128)(2,1)S(1)} %lay.2.refs_0_), channel_id=1, source_target_pairs={{0,2},{1,3},{2,0},{3,1},{4,6},{5,7},{6,4},{7,5},{8,10},{9,11},{10,... | collective-permute-start | bytes 786440 | tf_op jit(solution)/shard_map/cond/branch_1_fun/ppermute | solution.py:40
  50.9 7.8 %collective-permute-start.5 = (bf16[128,1024]{1,0:T(8,128)(2,1)S(1)}, bf16[128,1024]{1,0:T(8,128)(2,1)S(1)}, u32[]{:S(2)}, u32[]{:S(2)}) collective-permute-start(bf16[128,1024]{1,0:T(8,128)(2,1)S(1)} %lay.2.refs_0_), channel_id=1, source_target_pairs={{0,4},{1,5},{2,6},{3,7},{4,0},{5,1},{6,2},{7,3},{8,12},{9,13},{10,... | collective-permute-start | bytes 786440 | tf_op jit(solution)/shard_map/cond/branch_1_fun/ppermute | solution.py:40
  58.7 9.7 %collective-permute-start.7 = (bf16[384,1024]{1,0:T(8,128)(2,1)S(1)}, bf16[384,1024]{1,0:T(8,128)(2,1)S(1)}, u32[]{:S(2)}, u32[]{:S(2)}) collective-permute-start(bf16[384,1024]{1,0:T(8,128)(2,1)S(1)} %pad_maximum_fusion), channel_id=1, source_target_pairs={{0,1},{1,0},{2,3},{3,2},{4,5},{5,4},{6,7},{7,6},{8,9},{9,8},{10,11... | collective-permute-start | bytes 2359304 | tf_op jit(solution)/shard_map/cond/branch_1_fun/ppermute | solution.py:40
  58.8 9.6 %collective-permute-start.6 = (bf16[128,1024]{1,0:T(8,128)(2,1)S(1)}, bf16[128,1024]{1,0:T(8,128)(2,1)S(1)}, u32[]{:S(2)}, u32[]{:S(2)}) collective-permute-start(bf16[128,1024]{1,0:T(8,128)(2,1)S(1)} %lay.2.refs_0_), channel_id=1, source_target_pairs={{0,6},{1,7},{2,4},{3,5},{4,2},{5,3},{6,0},{7,1},{8,14},{9,15},{10,... | collective-permute-start | bytes 786440 | tf_op jit(solution)/shard_map/cond/branch_1_fun/ppermute | solution.py:40
  68.4 2.2 %collective-permute-start.8 = (bf16[128,1024]{1,0:T(8,128)(2,1)S(1)}, bf16[128,1024]{1,0:T(8,128)(2,1)S(1)}, u32[]{:S(2)}, u32[]{:S(2)}) collective-permute-start(bf16[128,1024]{1,0:T(8,128)(2,1)S(1)} %collective-permute-done.6.refs_3_), channel_id=1, source_target_pairs={{0,1},{1,0},{2,3},{3,2},{4,5},{5,4},{6,7},{7,6},{8,9},{9,8},{10,11... | collective-permute-start | bytes 786440 | tf_op jit(solution)/shard_map/cond/branch_1_fun/ppermute | solution.py:40
  75.2 26.2 %collective-permute-start.28 = (bf16[528,256]{1,0:T(8,128)(2,1)}, bf16[528,256]{1,0:T(8,128)(2,1)S(1)}, u32[]{:S(2)}, u32[]{:S(2)}) collective-permute-start(bf16[528,256]{1,0:T(8,128)(2,1)} %get-tuple-element.149), channel_id=1, source_target_pairs={{0,8},{1,9},{2,10},{3,11},{4,12},{5,13},{6,14},{7,15},{8,0},{9,1},... | collective-permute-start | bytes 811016 | tf_op jit(solution)/shard_map/ppermute | solution.py:40
  76.6 25.1 %collective-permute-start.29 = (bf16[528,256]{1,0:T(8,128)(2,1)}, bf16[528,256]{1,0:T(8,128)(2,1)S(1)}, u32[]{:S(2)}, u32[]{:S(2)}) collective-permute-start(bf16[528,256]{1,0:T(8,128)(2,1)} %get-tuple-element.150), channel_id=1, source_target_pairs={{0,16},{1,17},{2,18},{3,19},{4,20},{5,21},{6,22},{7,23},{8,24},{9,... | collective-permute-start | bytes 811016 | tf_op jit(solution)/shard_map/ppermute | solution.py:40
  79.3 22.5 %collective-permute-start.30 = (bf16[528,256]{1,0:T(8,128)(2,1)}, bf16[528,256]{1,0:T(8,128)(2,1)S(1)}, u32[]{:S(2)}, u32[]{:S(2)}) collective-permute-start(bf16[528,256]{1,0:T(8,128)(2,1)} %get-tuple-element.151), channel_id=1, source_target_pairs={{0,24},{1,25},{2,26},{3,27},{4,28},{5,29},{6,30},{7,31},{8,16},{9,... | collective-permute-start | bytes 811016 | tf_op jit(solution)/shard_map/ppermute | solution.py:40
  83.0 2.1 %collective-permute-start = (f32[256,512]{1,0:T(8,128)}, f32[256,512]{1,0:T(8,128)S(1)}, u32[]{:S(2)}, u32[]{:S(2)}) collective-permute-start(f32[256,512]{1,0:T(8,128)} %get-tuple-element.34), channel_id=1, source_target_pairs={{0,1},{1,0},{2,3},{3,2},{4,5},{5,4},{6,7},{7,6},{8,9},{9,8},{10,11... | collective-permute-start | bytes 1572872 | tf_op jit(solution)/shard_map/cond/branch_1_fun/ppermute | solution.py:40
  86.5 4.6 %collective-permute-start.1 = (bf16[80,512]{1,0:T(8,128)(2,1)S(1)}, bf16[80,512]{1,0:T(8,128)(2,1)S(1)}, u32[]{:S(2)}, u32[]{:S(2)}) collective-permute-start(bf16[80,512]{1,0:T(8,128)(2,1)S(1)} %get-tuple-element.36), channel_id=1, source_target_pairs={{0,2},{1,3},{2,0},{3,1},{4,6},{5,7},{6,4},{7,5},{8,10},{9,11},{10,... | collective-permute-start | bytes 245768 | tf_op jit(solution)/shard_map/cond/branch_1_fun/ppermute | solution.py:40
  87.8 4.8 %collective-permute-start.2 = (bf16[80,512]{1,0:T(8,128)(2,1)S(1)}, bf16[80,512]{1,0:T(8,128)(2,1)S(1)}, u32[]{:S(2)}, u32[]{:S(2)}) collective-permute-start(bf16[80,512]{1,0:T(8,128)(2,1)S(1)} %get-tuple-element.39), channel_id=1, source_target_pairs={{0,4},{1,5},{2,6},{3,7},{4,0},{5,1},{6,2},{7,3},{8,12},{9,13},{10,... | collective-permute-start | bytes 245768 | tf_op jit(solution)/shard_map/cond/branch_1_fun/ppermute | solution.py:40
  91.0 5.3 %collective-permute-start.3 = (bf16[80,512]{1,0:T(8,128)(2,1)S(1)}, bf16[80,512]{1,0:T(8,128)(2,1)S(1)}, u32[]{:S(2)}, u32[]{:S(2)}) collective-permute-start(bf16[80,512]{1,0:T(8,128)(2,1)S(1)} %get-tuple-element.40), channel_id=1, source_target_pairs={{0,6},{1,7},{2,4},{3,5},{4,2},{5,3},{6,0},{7,1},{8,14},{9,15},{10,... | collective-permute-start | bytes 245768 | tf_op jit(solution)/shard_map/cond/branch_1_fun/ppermute | solution.py:40
  97.3 4.5 %collective-permute-start.34 = (f32[16,512]{1,0:T(8,128)S(1)}, f32[16,512]{1,0:T(8,128)S(1)}, u32[]{:S(2)}, u32[]{:S(2)}) collective-permute-start(f32[16,512]{1,0:T(8,128)S(1)} %get-tuple-element.159), channel_id=1, source_target_pairs={{0,8},{1,9},{2,10},{3,11},{4,12},{5,13},{6,14},{7,15},{8,0},{9,1},... | collective-permute-start | bytes 98312 | tf_op jit(solution)/shard_map/ppermute | solution.py:40
  97.8 8.0 %collective-permute-start.35 = (f32[16,512]{1,0:T(8,128)S(1)}, f32[16,512]{1,0:T(8,128)S(1)}, u32[]{:S(2)}, u32[]{:S(2)}) collective-permute-start(f32[16,512]{1,0:T(8,128)S(1)} %get-tuple-element.160), channel_id=1, source_target_pairs={{0,16},{1,17},{2,18},{3,19},{4,20},{5,21},{6,22},{7,23},{8,24},{9,... | collective-permute-start | bytes 98312 | tf_op jit(solution)/shard_map/ppermute | solution.py:40
  101.4 5.7 %collective-permute-start.36 = (f32[16,512]{1,0:T(8,128)S(1)}, f32[16,512]{1,0:T(8,128)S(1)}, u32[]{:S(2)}, u32[]{:S(2)}) collective-permute-start(f32[16,512]{1,0:T(8,128)S(1)} %get-tuple-element.161), channel_id=1, source_target_pairs={{0,24},{1,25},{2,26},{3,27},{4,28},{5,29},{6,30},{7,31},{8,16},{9,... | collective-permute-start | bytes 98312 | tf_op jit(solution)/shard_map/ppermute | solution.py:40
  109.7 2.0 %collective-permute-start.37 = (f32[256,512]{1,0:T(8,128)S(1)}, f32[256,512]{1,0:T(8,128)S(1)}, u32[]{:S(2)}, u32[]{:S(2)}) collective-permute-start(f32[256,512]{1,0:T(8,128)S(1)} %get-tuple-element.168), channel_id=1, source_target_pairs={{0,1},{1,0},{2,3},{3,2},{4,5},{5,4},{6,7},{7,6},{8,9},{9,8},{10,11... | collective-permute-start | bytes 1572872 | tf_op jit(solution)/shard_map/ppermute | solution.py:40
  112.6 4.9 %collective-permute-start.38 = (bf16[80,512]{1,0:T(8,128)(2,1)S(1)}, bf16[80,512]{1,0:T(8,128)(2,1)S(1)}, u32[]{:S(2)}, u32[]{:S(2)}) collective-permute-start(bf16[80,512]{1,0:T(8,128)(2,1)S(1)} %get-tuple-element.170), channel_id=1, source_target_pairs={{0,2},{1,3},{2,0},{3,1},{4,6},{5,7},{6,4},{7,5},{8,10},{9,11},{10,... | collective-permute-start | bytes 245768 | tf_op jit(solution)/shard_map/ppermute | solution.py:40
  113.2 5.3 %collective-permute-start.39 = (bf16[80,512]{1,0:T(8,128)(2,1)S(1)}, bf16[80,512]{1,0:T(8,128)(2,1)S(1)}, u32[]{:S(2)}, u32[]{:S(2)}) collective-permute-start(bf16[80,512]{1,0:T(8,128)(2,1)S(1)} %get-tuple-element.171), channel_id=1, source_target_pairs={{0,4},{1,5},{2,6},{3,7},{4,0},{5,1},{6,2},{7,3},{8,12},{9,13},{10,... | collective-permute-start | bytes 245768 | tf_op jit(solution)/shard_map/ppermute | solution.py:40
  114.7 5.3 %collective-permute-start.40 = (bf16[80,512]{1,0:T(8,128)(2,1)S(1)}, bf16[80,512]{1,0:T(8,128)(2,1)S(1)}, u32[]{:S(2)}, u32[]{:S(2)}) collective-permute-start(bf16[80,512]{1,0:T(8,128)(2,1)S(1)} %get-tuple-element.172), channel_id=1, source_target_pairs={{0,6},{1,7},{2,4},{3,5},{4,2},{5,3},{6,0},{7,1},{8,14},{9,15},{10,... | collective-permute-start | bytes 245768 | tf_op jit(solution)/shard_map/ppermute | solution.py:40
  121.0 7.7 %collective-permute-start.43 = (bf16[96,512]{1,0:T(8,128)(2,1)S(1)}, bf16[96,512]{1,0:T(8,128)(2,1)S(1)}, u32[]{:S(2)}, u32[]{:S(2)}) collective-permute-start(bf16[96,512]{1,0:T(8,128)(2,1)S(1)} %code.1.refs_0_), channel_id=1, source_target_pairs={{0,24},{1,25},{2,26},{3,27},{4,28},{5,29},{6,30},{7,31},{8,16},{9,... | collective-permute-start | bytes 294920 | tf_op jit(solution)/shard_map/ppermute | solution.py:40
  122.5 8.6 %collective-permute-start.42 = (bf16[96,512]{1,0:T(8,128)(2,1)S(1)}, bf16[96,512]{1,0:T(8,128)(2,1)S(1)}, u32[]{:S(2)}, u32[]{:S(2)}) collective-permute-start(bf16[96,512]{1,0:T(8,128)(2,1)S(1)} %code.1.refs_0_), channel_id=1, source_target_pairs={{0,16},{1,17},{2,18},{3,19},{4,20},{5,21},{6,22},{7,23},{8,24},{9,... | collective-permute-start | bytes 294920 | tf_op jit(solution)/shard_map/ppermute | solution.py:40
  122.6 8.6 %collective-permute-start.41 = (bf16[96,512]{1,0:T(8,128)(2,1)S(1)}, bf16[96,512]{1,0:T(8,128)(2,1)S(1)}, u32[]{:S(2)}, u32[]{:S(2)}) collective-permute-start(bf16[96,512]{1,0:T(8,128)(2,1)S(1)} %code.1.refs_0_), channel_id=1, source_target_pairs={{0,8},{1,9},{2,10},{3,11},{4,12},{5,13},{6,14},{7,15},{8,0},{9,1},... | collective-permute-start | bytes 294920 | tf_op jit(solution)/shard_map/ppermute | solution.py:40
  132.2 7.4 %collective-permute-start.46 = (bf16[128,512]{1,0:T(8,128)(2,1)S(1)}, bf16[128,512]{1,0:T(8,128)(2,1)S(1)}, u32[]{:S(2)}, u32[]{:S(2)}) collective-permute-start(bf16[128,512]{1,0:T(8,128)(2,1)S(1)} %finish.1.refs_0_), channel_id=1, source_target_pairs={{0,6},{1,7},{2,4},{3,5},{4,2},{5,3},{6,0},{7,1},{8,14},{9,15},{10,... | collective-permute-start | bytes 393224 | tf_op jit(solution)/shard_map/ppermute | solution.py:40
  133.8 7.0 %collective-permute-start.45 = (bf16[128,512]{1,0:T(8,128)(2,1)S(1)}, bf16[128,512]{1,0:T(8,128)(2,1)S(1)}, u32[]{:S(2)}, u32[]{:S(2)}) collective-permute-start(bf16[128,512]{1,0:T(8,128)(2,1)S(1)} %finish.1.refs_0_), channel_id=1, source_target_pairs={{0,4},{1,5},{2,6},{3,7},{4,0},{5,1},{6,2},{7,3},{8,12},{9,13},{10,... | collective-permute-start | bytes 393224 | tf_op jit(solution)/shard_map/ppermute | solution.py:40
  135.4 5.5 %collective-permute-start.44 = (bf16[128,512]{1,0:T(8,128)(2,1)S(1)}, bf16[128,512]{1,0:T(8,128)(2,1)S(1)}, u32[]{:S(2)}, u32[]{:S(2)}) collective-permute-start(bf16[128,512]{1,0:T(8,128)(2,1)S(1)} %finish.1.refs_0_), channel_id=1, source_target_pairs={{0,2},{1,3},{2,0},{3,1},{4,6},{5,7},{6,4},{7,5},{8,10},{9,11},{10,... | collective-permute-start | bytes 393224 | tf_op jit(solution)/shard_map/ppermute | solution.py:40
  135.7 5.6 %collective-permute-start.47 = (bf16[128,512]{1,0:T(8,128)(2,1)S(1)}, bf16[128,512]{1,0:T(8,128)(2,1)S(1)}, u32[]{:S(2)}, u32[]{:S(2)}) collective-permute-start(bf16[128,512]{1,0:T(8,128)(2,1)S(1)} %finish.1.refs_0_), channel_id=1, source_target_pairs={{0,1},{1,0},{2,3},{3,2},{4,5},{5,4},{6,7},{7,6},{8,9},{9,8},{10,11... | collective-permute-start | bytes 393224 | tf_op jit(solution)/shard_map/ppermute | solution.py:40
  139.5 1.8 %collective-permute-start.50 = (bf16[128,512]{1,0:T(8,128)(2,1)S(1)}, bf16[128,512]{1,0:T(8,128)(2,1)S(1)}, u32[]{:S(2)}, u32[]{:S(2)}) collective-permute-start(bf16[128,512]{1,0:T(8,128)(2,1)S(1)} %collective-permute-done.46.refs_3_), channel_id=1, source_target_pairs={{0,1},{1,0},{2,3},{3,2},{4,5},{5,4},{6,7},{7,6},{8,9},{9,8},{10,11... | collective-permute-start | bytes 393224 | tf_op jit(solution)/shard_map/ppermute | solution.py:40
  140.8 1.3 collective-permute-start.49
  140.8 1.5 collective-permute-start.48
  144.3 8.3 %collective-permute-start.51 = (bf16[256,256]{1,0:T(8,128)(2,1)S(1)}, bf16[256,256]{1,0:T(8,128)(2,1)S(1)}, u32[]{:S(2)}, u32[]{:S(2)}) collective-permute-start(bf16[256,256]{1,0:T(8,128)(2,1)S(1)} %get-tuple-element.184), channel_id=1, source_target_pairs={{0,24},{1,25},{2,26},{3,27},{4,28},{5,29},{6,30},{7,31},{8,16},{9,... | collective-permute-start | bytes 393224 | tf_op jit(solution)/shard_map/ppermute | solution.py:40
  145.5 12.0 %collective-permute-start.52 = (bf16[256,256]{1,0:T(8,128)(2,1)S(1)}, bf16[256,256]{1,0:T(8,128)(2,1)S(1)}, u32[]{:S(2)}, u32[]{:S(2)}) collective-permute-start(bf16[256,256]{1,0:T(8,128)(2,1)S(1)} %get-tuple-element.185), channel_id=1, source_target_pairs={{0,16},{1,17},{2,18},{3,19},{4,20},{5,21},{6,22},{7,23},{8,24},{9,... | collective-permute-start | bytes 393224 | tf_op jit(solution)/shard_map/ppermute | solution.py:40
  145.5 12.0 %collective-permute-start.53 = (bf16[256,256]{1,0:T(8,128)(2,1)S(1)}, bf16[256,256]{1,0:T(8,128)(2,1)S(1)}, u32[]{:S(2)}, u32[]{:S(2)}) collective-permute-start(bf16[256,256]{1,0:T(8,128)(2,1)S(1)} %get-tuple-element.186), channel_id=1, source_target_pairs={{0,8},{1,9},{2,10},{3,11},{4,12},{5,13},{6,14},{7,15},{8,0},{9,1},... | collective-permute-start | bytes 393224 | tf_op jit(solution)/shard_map/ppermute | solution.py:40

commit v8 on v7

--- a/solution.py
+++ b/solution.py
@@ -499,21 +499,20 @@
         return place.send(part, lambda z, a, b: (z, a, b ^ 1))
 
     own_1, parts_1 = project(place, place_array, [met_1, [swapped(part) for part in met_1]], held)
-    second, own_1 = lax.optimization_barrier((second, own_1))
+    second = lay(place, place_array, second)
+    size, here, toward = place.along("a")
+    met_2 = [second] + [place.send(second, toward(step)) for step in range(1, size - 1)]
+    own_1, parts_1, late_weight = lax.optimization_barrier((own_1, parts_1, weight))
     parts_1 = sent(parts_1)
-    size, here, toward = place.along("a")
-
-    def second_projected(weight, *parts):
-        values = lay(place, place_array, parts)
-        met = [values] + [place.send(values, toward(step)) for step in range(1, size - 1)]
-        values, met[1] = lax.optimization_barrier((values, met[1]))
-        last = place.send(values, toward(size - 1))
+
+    def second_projected(weight, *met):
+        last = place.send(met[0], toward(size - 1))
         others = [swapped(jnp.concatenate(met, 0))]
         last, others = lax.optimization_barrier((last, others))
         others.append(swapped(last))
         return project(place, place_array, [[*met, last], others], fetch(weight))
 
-    own_2, parts_2 = in_one(place, second_projected, (weight, *second))
+    own_2, parts_2 = in_one(place, second_projected, (late_weight, *met_2))
     own_1, own_2 = lax.optimization_barrier((own_1, own_2))
     parts_2 = sent(parts_2)
     norm_1, packed_1, scale_1, *grams = normalize_parts(place, place_array, own_1, parts_1)

time: 159 us -> 154 us (0.969)
  waiting for transfers between devices: 68.1 us -> 61.7 us
    ppermute x54, waiting for transfers between devices: 68.1 us -> 61.7 us  [send(): return lax.ppermute(value, ('dp', 'mp'), pairs)]
  transfers between devices with their start and end apart: 54 -> 54, of which waited for: 32 -> 26; matrix products, arithmetic and copies ran while one was open for 1% -> 1% of each run, Pallas kernels for 10% -> 14%
where the time goes in v8:
time: 154 us; the launch traced here: 153 us
  waiting for transfers between devices  61.7 us (40%)
  starting transfers between devices  57.4 us (37%)
  Pallas kernels  30.2 us (20%)
  local copies, waits for them, and re-layouts  1.91 us (1%)
    ppermute x54, waiting for transfers between devices, send(): return lax.ppermute(value, ('dp', 'mp'), pairs)  61.7 us
    ppermute x54, starting transfers between devices, send(): return lax.ppermute(value, ('dp', 'mp'), pairs)  57.4 us
    pallas_call x10, Pallas kernels, local(): pl.pallas_call(kernel, in_specs=[pl.BlockSpec(memory_space=pltpu.SMEM)] +...  10.8 us
    pallas_call x2, Pallas kernels, project(): pl.pallas_call(functools.partial(project_kernel, counts=counts, n=n, k=k)...  9.07 us
    pallas_call x2, Pallas kernels, normalize_parts(): pl.pallas_call(functools.partial(normalize_kernel, n=n, k=k, second=secon...  6.02 us
    pallas_call x2, Pallas kernels, fetch(): pl.pallas_call(fetch_kernel, in_specs=[pl.BlockSpec(memory_space=pl.ANY)]...  4.39 us
  transfers between devices with their start and end apart: 54, of which 26 were waited for; matrix products, arithmetic and copies ran while one was open for 1% of the time, Pallas kernels for 14%

profile of v8, /device:TPU:0, one launch (start us, length us, event | category | flops | bytes accessed | tf_op | source)
XLA Modules:
  0.0 153.4 jit_solution(9256440493295479056)
XLA Ops:
  0.7 1.0 dynamic-slice_bitcast_fusion.4
  1.6 4.0 %collective-permute-start.9 = (bf16[32,1024]{1,0:T(8,128)(2,1)S(1)}, bf16[32,1024]{1,0:T(8,128)(2,1)S(1)}, u32[]{:S(2)}, u32[]{:S(2)}) collective-permute-start(bf16[32,1024]{1,0:T(8,128)(2,1)S(1)} %get-tuple-element.197), channel_id=1, source_target_pairs={{0,6},{1,7},{2,4},{3,5},{4,2},{5,3},{6,0},{7,1},{8,14},{9,15},{10,... | collective-permute-start | bytes 196616 | tf_op jit(solution)/shard_map/ppermute | solution.py:40
  6.2 1.6 %collective-permute-done.9 = bf16[32,1024]{1,0:T(8,128)(2,1)S(1)} collective-permute-done((bf16[32,1024]{1,0:T(8,128)(2,1)S(1)}, bf16[32,1024]{1,0:T(8,128)(2,1)S(1)}, u32[]{:S(2)}, u32[]{:S(2)}) %collective-permute-start.9) | collective-permute-done | bytes 65568 | tf_op jit(solution)/shard_map/ppermute | solution.py:40
  7.8 2.0 %collective-permute-done.8 = bf16[32,1024]{1,0:T(8,128)(2,1)S(1)} collective-permute-done((bf16[32,1024]{1,0:T(8,128)(2,1)S(1)}, bf16[32,1024]{1,0:T(8,128)(2,1)S(1)}, u32[]{:S(2)}, u32[]{:S(2)}) %collective-permute-start.8) | collective-permute-done | bytes 65568 | tf_op jit(solution)/shard_map/ppermute | solution.py:40
  10.4 3.7 %collective-permute-start.12 = (bf16[32,1024]{1,0:T(8,128)(2,1)S(1)}, bf16[32,1024]{1,0:T(8,128)(2,1)S(1)}, u32[]{:S(2)}, u32[]{:S(2)}) collective-permute-start(bf16[32,1024]{1,0:T(8,128)(2,1)S(1)} %get-tuple-element.193), channel_id=1, source_target_pairs={{0,24},{1,25},{2,26},{3,27},{4,28},{5,29},{6,30},{7,31},{8,16},{9,... | collective-permute-start | bytes 196616 | tf_op jit(solution)/shard_map/ppermute | solution.py:40
  14.1 0.8 collective-permute-start.11
  14.8 1.0 dynamic-slice_bitcast_fusion
  15.8 1.6 %collective-permute-start.15 = (bf16[32,1024]{1,0:T(8,128)(2,1)S(1)}, bf16[32,1024]{1,0:T(8,128)(2,1)S(1)}, u32[]{:S(2)}, u32[]{:S(2)}) collective-permute-start(bf16[32,1024]{1,0:T(8,128)(2,1)S(1)} %get-tuple-element.189), channel_id=1, source_target_pairs={{0,6},{1,7},{2,4},{3,5},{4,2},{5,3},{6,0},{7,1},{8,14},{9,15},{10,... | collective-permute-start | bytes 196616 | tf_op jit(solution)/shard_map/ppermute | solution.py:40
  17.8 1.6 %collective-permute-start.13 = (bf16[32,1024]{1,0:T(8,128)(2,1)S(1)}, bf16[32,1024]{1,0:T(8,128)(2,1)S(1)}, u32[]{:S(2)}, u32[]{:S(2)}) collective-permute-start(bf16[32,1024]{1,0:T(8,128)(2,1)S(1)} %get-tuple-element.191), channel_id=1, source_target_pairs={{0,2},{1,3},{2,0},{3,1},{4,6},{5,7},{6,4},{7,5},{8,10},{9,11},{10,... | collective-permute-start | bytes 196616 | tf_op jit(solution)/shard_map/ppermute | solution.py:40
  19.4 1.6 %collective-permute-done.15 = bf16[32,1024]{1,0:T(8,128)(2,1)S(1)} collective-permute-done((bf16[32,1024]{1,0:T(8,128)(2,1)S(1)}, bf16[32,1024]{1,0:T(8,128)(2,1)S(1)}, u32[]{:S(2)}, u32[]{:S(2)}) %collective-permute-start.15) | collective-permute-done | bytes 65568 | tf_op jit(solution)/shard_map/ppermute | solution.py:40
  21.0 0.7 collective-permute-done.14
  22.6 3.2 %collective-permute-start.18 = (bf16[128,1024]{1,0:T(8,128)(2,1)S(1)}, bf16[128,1024]{1,0:T(8,128)(2,1)S(1)}, u32[]{:S(2)}, u32[]{:S(2)}) collective-permute-start(bf16[128,1024]{1,0:T(8,128)(2,1)S(1)} %lay.2.refs_0_), channel_id=1, source_target_pairs={{0,6},{1,7},{2,4},{3,5},{4,2},{5,3},{6,0},{7,1},{8,14},{9,15},{10,... | collective-permute-start | bytes 786440 | tf_op jit(solution)/shard_map/ppermute | solution.py:40
  26.5 3.8 %collective-permute-start.21 = (bf16[32,1024]{1,0:T(8,128)(2,1)S(1)}, bf16[32,1024]{1,0:T(8,128)(2,1)S(1)}, u32[]{:S(2)}, u32[]{:S(2)}) collective-permute-start(bf16[32,1024]{1,0:T(8,128)(2,1)S(1)} %get-tuple-element.185), channel_id=1, source_target_pairs={{0,24},{1,25},{2,26},{3,27},{4,28},{5,29},{6,30},{7,31},{8,16},{9,... | collective-permute-start | bytes 196616 | tf_op jit(solution)/shard_map/ppermute | solution.py:40
  30.3 2.8 %collective-permute-done.21.refs_3_ = bf16[32,1024]{1,0:T(8,128)(2,1)S(1)} collective-permute-done((bf16[32,1024]{1,0:T(8,128)(2,1)S(1)}, bf16[32,1024]{1,0:T(8,128)(2,1)S(1)}, u32[]{:S(2)}, u32[]{:S(2)}) %collective-permute-start.21) | collective-permute-done | bytes 65568 | tf_op jit(solution)/shard_map/ppermute | solution.py:40
  33.1 2.2 %fetch.3.refs_8_ = bf16[2048,1024]{1,0:T(8,128)(2,1)S(1)} custom-call(bf16[2048,1024]{1,0:T(8,128)(2,1)} %weight_ref), custom_call_target="tpu_custom_call" | custom-call | bytes 8388608 | tf_op jit(solution)/shard_map/fetch/pallas_call | solution.py:234
  35.3 3.6 %collective-permute-done.20.refs_2_ = bf16[32,1024]{1,0:T(8,128)(2,1)S(1)} collective-permute-done((bf16[32,1024]{1,0:T(8,128)(2,1)S(1)}, bf16[32,1024]{1,0:T(8,128)(2,1)S(1)}, u32[]{:S(2)}, u32[]{:S(2)}) %collective-permute-start.20) | collective-permute-done | bytes 65568 | tf_op jit(solution)/shard_map/ppermute | solution.py:40
  40.0 1.3 lay.3
  41.7 1.9 %collective-permute-start.26 = (bf16[128,1024]{1,0:T(8,128)(2,1)}, bf16[128,1024]{1,0:T(8,128)(2,1)}, u32[]{:S(2)}, u32[]{:S(2)}) collective-permute-start(bf16[128,1024]{1,0:T(8,128)(2,1)} %lay.3), channel_id=1, source_target_pairs={{0,2},{1,3},{2,0},{3,1},{4,6},{5,7},{6,4},{7,5},{8,10},{9,11},{10,... | collective-permute-start | bytes 786440 | tf_op jit(solution)/shard_map/ppermute | solution.py:40
  43.5 3.9 %project.3 = (f32[512,256]{1,0:T(8,128)S(1)}, bf16[528,256]{1,0:T(8,128)(2,1)S(1)}, bf16[528,256]{1,0:T(8,128)(2,1)S(1)}, bf16[528,256]{1,0:T(8,128)(2,1)S(1)}) custom-call(s32[3]{0:T(128)S(1)} %pad_add_fusion.place_ref, bf16[128,1024]{1,0:T(8,128)(2,1)S(1)} %lay.2.refs_0_, bf16[128,1024]{1,0:T(8,128)(2,1)S(1)} %collective-permute-done.16.refs_1_, ...), custom_call_target="tpu_custom_call" | custom-call | flops 2147483648 | bytes 7864320 | tf_op jit(solution)/shard_map/project/pallas_call | solution.py:328
  47.5 3.8 %collective-permute-start.31 = (bf16[528,256]{1,0:T(8,128)(2,1)S(1)}, bf16[528,256]{1,0:T(8,128)(2,1)S(1)}, u32[]{:S(2)}, u32[]{:S(2)}) collective-permute-start(bf16[528,256]{1,0:T(8,128)(2,1)S(1)} %get-tuple-element.148), channel_id=1, source_target_pairs={{0,24},{1,25},{2,26},{3,27},{4,28},{5,29},{6,30},{7,31},{8,16},{9,... | collective-permute-start | bytes 811016 | tf_op jit(solution)/shard_map/ppermute | solution.py:40
  51.2 0.7 collective-permute-start.33
  51.9 18.5 %conditional.2 = (f32[512,256]{1,0:T(8,128)S(1)}, bf16[528,256]{1,0:T(8,128)(2,1)}, bf16[528,256]{1,0:T(8,128)(2,1)}, bf16[528,256]{1,0:T(8,128)(2,1)}) conditional(s32[]{:T(128)} %convert_element_type.4, () %tuple.37, (bf16[128,1024]{1,0:T(8,128)(2,1)}, bf16[128,1024]{1,0:T(8,128)(2,1)}, bf16[128,1024]{1,0:T(8,128)(2,1)}, ...), branch_computations={%region_0.1_spmd, %region_1.2_spmd} | conditional | flops 2149842944 | bytes 23068824 | solution.py:201
  51.9 1.2 pad_maximum_fusion
  53.2 1.3 collective-permute-start.4
  54.5 8.5 %collective-permute-done.4.refs_3_ = bf16[128,1024]{1,0:T(8,128)(2,1)S(1)} collective-permute-done((bf16[128,1024]{1,0:T(8,128)(2,1)}, bf16[128,1024]{1,0:T(8,128)(2,1)S(1)}, u32[]{:S(2)}, u32[]{:S(2)}) %collective-permute-start.4) | collective-permute-done | bytes 262176 | tf_op jit(solution)/shard_map/cond/branch_1_fun/ppermute | solution.py:40
  63.0 2.2 %fetch.2.refs_6_ = bf16[2048,1024]{1,0:T(8,128)(2,1)S(1)} custom-call(bf16[2048,1024]{1,0:T(8,128)(2,1)} %get-tuple-element.22.weight_ref), custom_call_target="tpu_custom_call" | custom-call | bytes 8388608 | tf_op jit(solution)/shard_map/cond/branch_1_fun/fetch/pallas_call | solution.py:234
  65.2 5.2 %project.2 = (f32[512,256]{1,0:T(8,128)S(1)}, bf16[528,256]{1,0:T(8,128)(2,1)}, bf16[528,256]{1,0:T(8,128)(2,1)}, bf16[528,256]{1,0:T(8,128)(2,1)}) custom-call(s32[3]{0:T(128)S(1)} %get-tuple-element.16.place_ref, bf16[128,1024]{1,0:T(8,128)(2,1)} %get-tuple-element.17.refs_0_, bf16[128,1024]{1,0:T(8,128)(2,1)} %get-tuple-element.18.refs_1_, ...), custom_call_target="tpu_custom_call" | custom-call | flops 2147483648 | bytes 7864320 | tf_op jit(solution)/shard_map/cond/branch_1_fun/project/pallas_call | solution.py:328
  70.4 1.4 collective-permute-start.28
  71.8 2.9 %collective-permute-start.29 = (bf16[528,256]{1,0:T(8,128)(2,1)}, bf16[528,256]{1,0:T(8,128)(2,1)S(1)}, u32[]{:S(2)}, u32[]{:S(2)}) collective-permute-start(bf16[528,256]{1,0:T(8,128)(2,1)} %get-tuple-element.145), channel_id=1, source_target_pairs={{0,16},{1,17},{2,18},{3,19},{4,20},{5,21},{6,22},{7,23},{8,24},{9,... | collective-permute-start | bytes 811016 | tf_op jit(solution)/shard_map/ppermute | solution.py:40
  74.8 3.4 %normalize.2 = (f32[512,256]{1,0:T(8,128)S(1)}, bf16[512,256]{1,0:T(8,128)(2,1)S(1)}, f32[1,256]{1,0:T(1,128)S(1)}, f32[256,512]{1,0:T(8,128)}, f32[256,512]{1,0:T(8,128)}) custom-call(s32[3]{0:T(128)S(1)} %pad_add_fusion.place_ref, f32[512,256]{1,0:T(8,128)S(1)} %get-tuple-element.147.refs_0_, bf16[528,256]{1,0:T(8,128)(2,1)S(1)} %collective-permute-done.31.refs_1_, ...), custom_call_target="tpu_custom_call" | custom-call | flops 134217728 | bytes 3145728 | tf_op jit(solution)/shard_map/normalize/pallas_call | solution.py:407
  78.2 14.3 %conditional.3 = ((f32[16,512]{1,0:T(8,128)S(1)}, f32[16,512]{1,0:T(8,128)S(1)}, f32[16,512]{1,0:T(8,128)S(1)}, f32[16,512]{1,0:T(8,128)S(1)})) conditional(s32[]{:T(128)} %convert_element_type.4, () %tuple.40, (f32[256,512]{1,0:T(8,128)}, s32[3]{0:T(128)S(1)}, f32[256,512]{1,0:T(8,128)}) %tuple.41), branch_computations={%region_2.3_spmd, %region_3.4_spmd} | conditional | bytes 3080360 | solution.py:201
  78.2 2.1 %collective-permute-done.met_ref = f32[256,512]{1,0:T(8,128)S(1)} collective-permute-done((f32[256,512]{1,0:T(8,128)}, f32[256,512]{1,0:T(8,128)S(1)}, u32[]{:S(2)}, u32[]{:S(2)}) %collective-permute-start) | collective-permute-done | bytes 524320 | tf_op jit(solution)/shard_map/cond/branch_1_fun/ppermute | solution.py:40
  80.3 1.3 halve.2
  81.9 1.7 %collective-permute-start.2 = (bf16[80,512]{1,0:T(8,128)(2,1)S(1)}, bf16[80,512]{1,0:T(8,128)(2,1)S(1)}, u32[]{:S(2)}, u32[]{:S(2)}) collective-permute-start(bf16[80,512]{1,0:T(8,128)(2,1)S(1)} %get-tuple-element.34), channel_id=1, source_target_pairs={{0,4},{1,5},{2,6},{3,7},{4,0},{5,1},{6,2},{7,3},{8,12},{9,13},{10,... | collective-permute-start | bytes 245768 | tf_op jit(solution)/shard_map/cond/branch_1_fun/ppermute | solution.py:40
  83.5 2.7 %collective-permute-done.1.refs_1_ = bf16[80,512]{1,0:T(8,128)(2,1)S(1)} collective-permute-done((bf16[80,512]{1,0:T(8,128)(2,1)S(1)}, bf16[80,512]{1,0:T(8,128)(2,1)S(1)}, u32[]{:S(2)}, u32[]{:S(2)}) %collective-permute-start.1) | collective-permute-done | bytes 81952 | tf_op jit(solution)/shard_map/cond/branch_1_fun/ppermute | solution.py:40
  86.2 1.3 collective-permute-start.3
  87.5 4.1 %collective-permute-done.3.refs_3_ = bf16[80,512]{1,0:T(8,128)(2,1)S(1)} collective-permute-done((bf16[80,512]{1,0:T(8,128)(2,1)S(1)}, bf16[80,512]{1,0:T(8,128)(2,1)S(1)}, u32[]{:S(2)}, u32[]{:S(2)}) %collective-permute-start.3) | collective-permute-done | bytes 81952 | tf_op jit(solution)/shard_map/cond/branch_1_fun/ppermute | solution.py:40
  91.5 0.9 plane.1
  93.0 3.8 %collective-permute-start.35 = (f32[16,512]{1,0:T(8,128)S(1)}, f32[16,512]{1,0:T(8,128)S(1)}, u32[]{:S(2)}, u32[]{:S(2)}) collective-permute-start(f32[16,512]{1,0:T(8,128)S(1)} %get-tuple-element.155), channel_id=1, source_target_pairs={{0,16},{1,17},{2,18},{3,19},{4,20},{5,21},{6,22},{7,23},{8,24},{9,... | collective-permute-start | bytes 98312 | tf_op jit(solution)/shard_map/ppermute | solution.py:40
  96.9 4.4 %collective-permute-done.35.refs_2_ = f32[16,512]{1,0:T(8,128)S(1)} collective-permute-done((f32[16,512]{1,0:T(8,128)S(1)}, f32[16,512]{1,0:T(8,128)S(1)}, u32[]{:S(2)}, u32[]{:S(2)}) %collective-permute-start.35) | collective-permute-done | bytes 32800 | tf_op jit(solution)/shard_map/ppermute | solution.py:40
  101.3 1.2 collective-permute-done.36.refs_3_
  102.5 2.6 %normalize.3 = (f32[512,256]{1,0:T(8,128)S(1)}, bf16[512,256]{1,0:T(8,128)(2,1)S(1)}, f32[1,256]{1,0:T(1,128)S(1)}, f32[256,512]{1,0:T(8,128)S(1)}, f32[256,512]{1,0:T(8,128)S(1)}, /*index=5*/f32[1,256]{1,0:T(1,128)S(1)}) custom-call(s32[3]{0:T(128)S(1)} %pad_add_fusion.place_ref, f32[512,256]{1,0:T(8,128)S(1)} %get-tuple-element.157.refs_0_, ...), custom_call_target="tpu_custom_call" | custom-call | flops 134217728 | bytes 3145728 | tf_op jit(solution)/shard_map/normalize/pallas_call | solution.py:407
  105.2 1.9 %collective-permute-done.37.met_ref = f32[256,512]{1,0:T(8,128)S(1)} collective-permute-done((f32[256,512]{1,0:T(8,128)S(1)}, f32[256,512]{1,0:T(8,128)S(1)}, u32[]{:S(2)}, u32[]{:S(2)}) %collective-permute-start.37) | collective-permute-done | bytes 524320 | tf_op jit(solution)/shard_map/ppermute | solution.py:40
  107.1 0.8 halve.3
  108.8 2.7 %collective-permute-start.40 = (bf16[80,512]{1,0:T(8,128)(2,1)S(1)}, bf16[80,512]{1,0:T(8,128)(2,1)S(1)}, u32[]{:S(2)}, u32[]{:S(2)}) collective-permute-start(bf16[80,512]{1,0:T(8,128)(2,1)S(1)} %get-tuple-element.167), channel_id=1, source_target_pairs={{0,6},{1,7},{2,4},{3,5},{4,2},{5,3},{6,0},{7,1},{8,14},{9,15},{10,... | collective-permute-start | bytes 245768 | tf_op jit(solution)/shard_map/ppermute | solution.py:40
  112.1 1.0 collective-permute-done.38.refs_1_
  113.1 1.4 collective-permute-done.39.refs_2_
  114.5 0.9 code.1.refs_0_
  115.4 1.4 collective-permute-start.43
  116.8 3.1 %collective-permute-start.41 = (bf16[96,512]{1,0:T(8,128)(2,1)S(1)}, bf16[96,512]{1,0:T(8,128)(2,1)S(1)}, u32[]{:S(2)}, u32[]{:S(2)}) collective-permute-start(bf16[96,512]{1,0:T(8,128)(2,1)S(1)} %code.1.refs_0_), channel_id=1, source_target_pairs={{0,8},{1,9},{2,10},{3,11},{4,12},{5,13},{6,14},{7,15},{8,0},{9,1},... | collective-permute-start | bytes 294920 | tf_op jit(solution)/shard_map/ppermute | solution.py:40
  119.9 2.7 %collective-permute-done.43.refs_3_ = bf16[96,512]{1,0:T(8,128)(2,1)S(1)} collective-permute-done((bf16[96,512]{1,0:T(8,128)(2,1)S(1)}, bf16[96,512]{1,0:T(8,128)(2,1)S(1)}, u32[]{:S(2)}, u32[]{:S(2)}) %collective-permute-start.43) | collective-permute-done | bytes 98336 | tf_op jit(solution)/shard_map/ppermute | solution.py:40
  122.5 2.8 %collective-permute-done.42.refs_2_ = bf16[96,512]{1,0:T(8,128)(2,1)S(1)} collective-permute-done((bf16[96,512]{1,0:T(8,128)(2,1)S(1)}, bf16[96,512]{1,0:T(8,128)(2,1)S(1)}, u32[]{:S(2)}, u32[]{:S(2)}) %collective-permute-start.42) | collective-permute-done | bytes 98336 | tf_op jit(solution)/shard_map/ppermute | solution.py:40
  125.4 1.0 finish.1.refs_0_
  126.4 2.6 %collective-permute-start.46 = (bf16[128,512]{1,0:T(8,128)(2,1)S(1)}, bf16[128,512]{1,0:T(8,128)(2,1)S(1)}, u32[]{:S(2)}, u32[]{:S(2)}) collective-permute-start(bf16[128,512]{1,0:T(8,128)(2,1)S(1)} %finish.1.refs_0_), channel_id=1, source_target_pairs={{0,6},{1,7},{2,4},{3,5},{4,2},{5,3},{6,0},{7,1},{8,14},{9,15},{10,... | collective-permute-start | bytes 393224 | tf_op jit(solution)/shard_map/ppermute | solution.py:40
  130.0 3.0 %collective-permute-done.46.refs_3_ = bf16[128,512]{1,0:T(8,128)(2,1)S(1)} collective-permute-done((bf16[128,512]{1,0:T(8,128)(2,1)S(1)}, bf16[128,512]{1,0:T(8,128)(2,1)S(1)}, u32[]{:S(2)}, u32[]{:S(2)}) %collective-permute-start.46) | collective-permute-done | bytes 131104 | tf_op jit(solution)/shard_map/ppermute | solution.py:40
  133.0 1.9 %collective-permute-done.45.refs_2_ = bf16[128,512]{1,0:T(8,128)(2,1)S(1)} collective-permute-done((bf16[128,512]{1,0:T(8,128)(2,1)S(1)}, bf16[128,512]{1,0:T(8,128)(2,1)S(1)}, u32[]{:S(2)}, u32[]{:S(2)}) %collective-permute-start.45) | collective-permute-done | bytes 131104 | tf_op jit(solution)/shard_map/ppermute | solution.py:40
  134.9 0.8 collective-permute-done.44.refs_1_
  136.2 0.8 collective-permute-done.48.refs_5_
  137.1 2.0 %gradient.1 = (bf16[256,256]{1,0:T(8,128)(2,1)S(1)}, bf16[256,256]{1,0:T(8,128)(2,1)S(1)}, bf16[256,256]{1,0:T(8,128)(2,1)S(1)}, bf16[256,256]{1,0:T(8,128)(2,1)S(1)}, f32[1,1]{1,0:T(1,128)}) custom-call(s32[3]{0:T(128)S(1)} %pad_add_fusion.place_ref, bf16[128,512]{1,0:T(8,128)(2,1)S(1)} %finish.1.refs_0_, ...), custom_call_target="tpu_custom_call" | custom-call | tf_op jit(solution)/shard_map/gradient/pallas_call | solution.py:160
  139.0 1.7 %collective-permute-start.51 = (bf16[256,256]{1,0:T(8,128)(2,1)S(1)}, bf16[256,256]{1,0:T(8,128)(2,1)S(1)}, u32[]{:S(2)}, u32[]{:S(2)}) collective-permute-start(bf16[256,256]{1,0:T(8,128)(2,1)S(1)} %get-tuple-element.179), channel_id=1, source_target_pairs={{0,24},{1,25},{2,26},{3,27},{4,28},{5,29},{6,30},{7,31},{8,16},{9,... | collective-permute-start | bytes 393224 | tf_op jit(solution)/shard_map/ppermute | solution.py:40
  140.7 2.7 %collective-permute-start.53 = (bf16[256,256]{1,0:T(8,128)(2,1)S(1)}, bf16[256,256]{1,0:T(8,128)(2,1)S(1)}, u32[]{:S(2)}, u32[]{:S(2)}) collective-permute-start(bf16[256,256]{1,0:T(8,128)(2,1)S(1)} %get-tuple-element.181), channel_id=1, source_target_pairs={{0,8},{1,9},{2,10},{3,11},{4,12},{5,13},{6,14},{7,15},{8,0},{9,1},... | collective-permute-start | bytes 393224 | tf_op jit(solution)/shard_map/ppermute | solution.py:40
  143.4 3.9 %collective-permute-done.51.refs_1_ = bf16[256,256]{1,0:T(8,128)(2,1)S(1)} collective-permute-done((bf16[256,256]{1,0:T(8,128)(2,1)S(1)}, bf16[256,256]{1,0:T(8,128)(2,1)S(1)}, u32[]{:S(2)}, u32[]{:S(2)}) %collective-permute-start.51) | collective-permute-done | bytes 131104 | tf_op jit(solution)/shard_map/ppermute | solution.py:40
  147.3 4.7 %collective-permute-done.52.refs_2_ = bf16[256,256]{1,0:T(8,128)(2,1)S(1)} collective-permute-done((bf16[256,256]{1,0:T(8,128)(2,1)S(1)}, bf16[256,256]{1,0:T(8,128)(2,1)S(1)}, u32[]{:S(2)}, u32[]{:S(2)}) %collective-permute-start.52) | collective-permute-done | bytes 131104 | tf_op jit(solution)/shard_map/ppermute | solution.py:40
  152.0 1.4 place.1
  (68 shorter events, 8.8 us)
Async XLA Ops:
  1.6 6.2 %collective-permute-start.9 = (bf16[32,1024]{1,0:T(8,128)(2,1)S(1)}, bf16[32,1024]{1,0:T(8,128)(2,1)S(1)}, u32[]{:S(2)}, u32[]{:S(2)}) collective-permute-start(bf16[32,1024]{1,0:T(8,128)(2,1)S(1)} %get-tuple-element.197), channel_id=1, source_target_pairs={{0,6},{1,7},{2,4},{3,5},{4,2},{5,3},{6,0},{7,1},{8,14},{9,15},{10,... | collective-permute-start | bytes 196616 | tf_op jit(solution)/shard_map/ppermute | solution.py:40
  5.6 4.3 %collective-permute-start.8 = (bf16[32,1024]{1,0:T(8,128)(2,1)S(1)}, bf16[32,1024]{1,0:T(8,128)(2,1)S(1)}, u32[]{:S(2)}, u32[]{:S(2)}) collective-permute-start(bf16[32,1024]{1,0:T(8,128)(2,1)S(1)} %get-tuple-element.198), channel_id=1, source_target_pairs={{0,4},{1,5},{2,6},{3,7},{4,0},{5,1},{6,2},{7,3},{8,12},{9,13},{10,... | collective-permute-start | bytes 196616 | tf_op jit(solution)/shard_map/ppermute | solution.py:40
  6.1 4.3 %collective-permute-start.7 = (bf16[32,1024]{1,0:T(8,128)(2,1)S(1)}, bf16[32,1024]{1,0:T(8,128)(2,1)S(1)}, u32[]{:S(2)}, u32[]{:S(2)}) collective-permute-start(bf16[32,1024]{1,0:T(8,128)(2,1)S(1)} %get-tuple-element.199), channel_id=1, source_target_pairs={{0,2},{1,3},{2,0},{3,1},{4,6},{5,7},{6,4},{7,5},{8,10},{9,11},{10,... | collective-permute-start | bytes 196616 | tf_op jit(solution)/shard_map/ppermute | solution.py:40
  10.4 7.4 %collective-permute-start.12 = (bf16[32,1024]{1,0:T(8,128)(2,1)S(1)}, bf16[32,1024]{1,0:T(8,128)(2,1)S(1)}, u32[]{:S(2)}, u32[]{:S(2)}) collective-permute-start(bf16[32,1024]{1,0:T(8,128)(2,1)S(1)} %get-tuple-element.193), channel_id=1, source_target_pairs={{0,24},{1,25},{2,26},{3,27},{4,28},{5,29},{6,30},{7,31},{8,16},{9,... | collective-permute-start | bytes 196616 | tf_op jit(solution)/shard_map/ppermute | solution.py:40
  14.1 5.4 %collective-permute-start.10 = (bf16[32,1024]{1,0:T(8,128)(2,1)S(1)}, bf16[32,1024]{1,0:T(8,128)(2,1)S(1)}, u32[]{:S(2)}, u32[]{:S(2)}) collective-permute-start(bf16[32,1024]{1,0:T(8,128)(2,1)S(1)} %get-tuple-element.194), channel_id=1, source_target_pairs={{0,8},{1,9},{2,10},{3,11},{4,12},{5,13},{6,14},{7,15},{8,0},{9,1},... | collective-permute-start | bytes 196616 | tf_op jit(solution)/shard_map/ppermute | solution.py:40
  14.1 5.4 %collective-permute-start.11 = (bf16[32,1024]{1,0:T(8,128)(2,1)S(1)}, bf16[32,1024]{1,0:T(8,128)(2,1)S(1)}, u32[]{:S(2)}, u32[]{:S(2)}) collective-permute-start(bf16[32,1024]{1,0:T(8,128)(2,1)S(1)} %get-tuple-element.195), channel_id=1, source_target_pairs={{0,16},{1,17},{2,18},{3,19},{4,20},{5,21},{6,22},{7,23},{8,24},{9,... | collective-permute-start | bytes 196616 | tf_op jit(solution)/shard_map/ppermute | solution.py:40
  15.8 5.2 %collective-permute-start.15 = (bf16[32,1024]{1,0:T(8,128)(2,1)S(1)}, bf16[32,1024]{1,0:T(8,128)(2,1)S(1)}, u32[]{:S(2)}, u32[]{:S(2)}) collective-permute-start(bf16[32,1024]{1,0:T(8,128)(2,1)S(1)} %get-tuple-element.189), channel_id=1, source_target_pairs={{0,6},{1,7},{2,4},{3,5},{4,2},{5,3},{6,0},{7,1},{8,14},{9,15},{10,... | collective-permute-start | bytes 196616 | tf_op jit(solution)/shard_map/ppermute | solution.py:40
  17.4 4.4 %collective-permute-start.14 = (bf16[32,1024]{1,0:T(8,128)(2,1)S(1)}, bf16[32,1024]{1,0:T(8,128)(2,1)S(1)}, u32[]{:S(2)}, u32[]{:S(2)}) collective-permute-start(bf16[32,1024]{1,0:T(8,128)(2,1)S(1)} %get-tuple-element.190), channel_id=1, source_target_pairs={{0,4},{1,5},{2,6},{3,7},{4,0},{5,1},{6,2},{7,3},{8,12},{9,13},{10,... | collective-permute-start | bytes 196616 | tf_op jit(solution)/shard_map/ppermute | solution.py:40
  17.8 4.3 %collective-permute-start.13 = (bf16[32,1024]{1,0:T(8,128)(2,1)S(1)}, bf16[32,1024]{1,0:T(8,128)(2,1)S(1)}, u32[]{:S(2)}, u32[]{:S(2)}) collective-permute-start(bf16[32,1024]{1,0:T(8,128)(2,1)S(1)} %get-tuple-element.191), channel_id=1, source_target_pairs={{0,2},{1,3},{2,0},{3,1},{4,6},{5,7},{6,4},{7,5},{8,10},{9,11},{10,... | collective-permute-start | bytes 196616 | tf_op jit(solution)/shard_map/ppermute | solution.py:40
  22.6 16.3 %collective-permute-start.18 = (bf16[128,1024]{1,0:T(8,128)(2,1)S(1)}, bf16[128,1024]{1,0:T(8,128)(2,1)S(1)}, u32[]{:S(2)}, u32[]{:S(2)}) collective-permute-start(bf16[128,1024]{1,0:T(8,128)(2,1)S(1)} %lay.2.refs_0_), channel_id=1, source_target_pairs={{0,6},{1,7},{2,4},{3,5},{4,2},{5,3},{6,0},{7,1},{8,14},{9,15},{10,... | collective-permute-start | bytes 786440 | tf_op jit(solution)/shard_map/ppermute | solution.py:40
  25.8 13.1 %collective-permute-start.17 = (bf16[128,1024]{1,0:T(8,128)(2,1)S(1)}, bf16[128,1024]{1,0:T(8,128)(2,1)S(1)}, u32[]{:S(2)}, u32[]{:S(2)}) collective-permute-start(bf16[128,1024]{1,0:T(8,128)(2,1)S(1)} %lay.2.refs_0_), channel_id=1, source_target_pairs={{0,4},{1,5},{2,6},{3,7},{4,0},{5,1},{6,2},{7,3},{8,12},{9,13},{10,... | collective-permute-start | bytes 786440 | tf_op jit(solution)/shard_map/ppermute | solution.py:40
  25.8 13.1 %collective-permute-start.16 = (bf16[128,1024]{1,0:T(8,128)(2,1)S(1)}, bf16[128,1024]{1,0:T(8,128)(2,1)S(1)}, u32[]{:S(2)}, u32[]{:S(2)}) collective-permute-start(bf16[128,1024]{1,0:T(8,128)(2,1)S(1)} %lay.2.refs_0_), channel_id=1, source_target_pairs={{0,2},{1,3},{2,0},{3,1},{4,6},{5,7},{6,4},{7,5},{8,10},{9,11},{10,... | collective-permute-start | bytes 786440 | tf_op jit(solution)/shard_map/ppermute | solution.py:40
  26.5 6.6 %collective-permute-start.21 = (bf16[32,1024]{1,0:T(8,128)(2,1)S(1)}, bf16[32,1024]{1,0:T(8,128)(2,1)S(1)}, u32[]{:S(2)}, u32[]{:S(2)}) collective-permute-start(bf16[32,1024]{1,0:T(8,128)(2,1)S(1)} %get-tuple-element.185), channel_id=1, source_target_pairs={{0,24},{1,25},{2,26},{3,27},{4,28},{5,29},{6,30},{7,31},{8,16},{9,... | collective-permute-start | bytes 196616 | tf_op jit(solution)/shard_map/ppermute | solution.py:40
  30.3 5.0 %collective-permute-start.19 = (bf16[32,1024]{1,0:T(8,128)(2,1)S(1)}, bf16[32,1024]{1,0:T(8,128)(2,1)S(1)}, u32[]{:S(2)}, u32[]{:S(2)}) collective-permute-start(bf16[32,1024]{1,0:T(8,128)(2,1)S(1)} %get-tuple-element.187), channel_id=1, source_target_pairs={{0,8},{1,9},{2,10},{3,11},{4,12},{5,13},{6,14},{7,15},{8,0},{9,1},... | collective-permute-start | bytes 196616 | tf_op jit(solution)/shard_map/ppermute | solution.py:40
  33.1 5.9 %collective-permute-start.20 = (bf16[32,1024]{1,0:T(8,128)(2,1)S(1)}, bf16[32,1024]{1,0:T(8,128)(2,1)S(1)}, u32[]{:S(2)}, u32[]{:S(2)}) collective-permute-start(bf16[32,1024]{1,0:T(8,128)(2,1)S(1)} %get-tuple-element.188), channel_id=1, source_target_pairs={{0,16},{1,17},{2,18},{3,19},{4,20},{5,21},{6,22},{7,23},{8,24},{9,... | collective-permute-start | bytes 196616 | tf_op jit(solution)/shard_map/ppermute | solution.py:40
  38.9 2.7 %collective-permute-start.22 = (bf16[128,1024]{1,0:T(8,128)(2,1)S(1)}, bf16[128,1024]{1,0:T(8,128)(2,1)S(1)}, u32[]{:S(2)}, u32[]{:S(2)}) collective-permute-start(bf16[128,1024]{1,0:T(8,128)(2,1)S(1)} %lay.2.refs_0_), channel_id=1, source_target_pairs={{0,1},{1,0},{2,3},{3,2},{4,5},{5,4},{6,7},{7,6},{8,9},{9,8},{10,11... | collective-permute-start | bytes 786440 | tf_op jit(solution)/shard_map/ppermute | solution.py:40
  39.0 4.5 %collective-permute-start.23 = (bf16[128,1024]{1,0:T(8,128)(2,1)S(1)}, bf16[128,1024]{1,0:T(8,128)(2,1)S(1)}, u32[]{:S(2)}, u32[]{:S(2)}) collective-permute-start(bf16[128,1024]{1,0:T(8,128)(2,1)S(1)} %collective-permute-done.16.refs_1_), channel_id=1, source_target_pairs={{0,1},{1,0},{2,3},{3,2},{4,5},{5,4},{6,7},{7,6},{8,9},{9,8},{10,11... | collective-permute-start | bytes 786440 | tf_op jit(solution)/shard_map/ppermute | solution.py:40
  39.5 4.0 %collective-permute-start.24 = (bf16[128,1024]{1,0:T(8,128)(2,1)S(1)}, bf16[128,1024]{1,0:T(8,128)(2,1)S(1)}, u32[]{:S(2)}, u32[]{:S(2)}) collective-permute-start(bf16[128,1024]{1,0:T(8,128)(2,1)S(1)} %collective-permute-done.17.refs_2_), channel_id=1, source_target_pairs={{0,1},{1,0},{2,3},{3,2},{4,5},{5,4},{6,7},{7,6},{8,9},{9,8},{10,11... | collective-permute-start | bytes 786440 | tf_op jit(solution)/shard_map/ppermute | solution.py:40
  39.6 4.0 %collective-permute-start.25 = (bf16[128,1024]{1,0:T(8,128)(2,1)S(1)}, bf16[128,1024]{1,0:T(8,128)(2,1)S(1)}, u32[]{:S(2)}, u32[]{:S(2)}) collective-permute-start(bf16[128,1024]{1,0:T(8,128)(2,1)S(1)} %collective-permute-done.18.refs_3_), channel_id=1, source_target_pairs={{0,1},{1,0},{2,3},{3,2},{4,5},{5,4},{6,7},{7,6},{8,9},{9,8},{10,11... | collective-permute-start | bytes 786440 | tf_op jit(solution)/shard_map/ppermute | solution.py:40
  41.3 10.6 %collective-permute-start.27 = (bf16[128,1024]{1,0:T(8,128)(2,1)}, bf16[128,1024]{1,0:T(8,128)(2,1)}, u32[]{:S(2)}, u32[]{:S(2)}) collective-permute-start(bf16[128,1024]{1,0:T(8,128)(2,1)} %lay.3), channel_id=1, source_target_pairs={{0,4},{1,5},{2,6},{3,7},{4,0},{5,1},{6,2},{7,3},{8,12},{9,13},{10,... | collective-permute-start | bytes 786440 | tf_op jit(solution)/shard_map/ppermute | solution.py:40
  41.7 10.3 %collective-permute-start.26 = (bf16[128,1024]{1,0:T(8,128)(2,1)}, bf16[128,1024]{1,0:T(8,128)(2,1)}, u32[]{:S(2)}, u32[]{:S(2)}) collective-permute-start(bf16[128,1024]{1,0:T(8,128)(2,1)} %lay.3), channel_id=1, source_target_pairs={{0,2},{1,3},{2,0},{3,1},{4,6},{5,7},{6,4},{7,5},{8,10},{9,11},{10,... | collective-permute-start | bytes 786440 | tf_op jit(solution)/shard_map/ppermute | solution.py:40
  47.5 27.2 %collective-permute-start.31 = (bf16[528,256]{1,0:T(8,128)(2,1)S(1)}, bf16[528,256]{1,0:T(8,128)(2,1)S(1)}, u32[]{:S(2)}, u32[]{:S(2)}) collective-permute-start(bf16[528,256]{1,0:T(8,128)(2,1)S(1)} %get-tuple-element.148), channel_id=1, source_target_pairs={{0,24},{1,25},{2,26},{3,27},{4,28},{5,29},{6,30},{7,31},{8,16},{9,... | collective-permute-start | bytes 811016 | tf_op jit(solution)/shard_map/ppermute | solution.py:40
  51.2 23.5 %collective-permute-start.32 = (bf16[528,256]{1,0:T(8,128)(2,1)S(1)}, bf16[528,256]{1,0:T(8,128)(2,1)S(1)}, u32[]{:S(2)}, u32[]{:S(2)}) collective-permute-start(bf16[528,256]{1,0:T(8,128)(2,1)S(1)} %get-tuple-element.149), channel_id=1, source_target_pairs={{0,16},{1,17},{2,18},{3,19},{4,20},{5,21},{6,22},{7,23},{8,24},{9,... | collective-permute-start | bytes 811016 | tf_op jit(solution)/shard_map/ppermute | solution.py:40
  51.2 23.5 %collective-permute-start.33 = (bf16[528,256]{1,0:T(8,128)(2,1)S(1)}, bf16[528,256]{1,0:T(8,128)(2,1)S(1)}, u32[]{:S(2)}, u32[]{:S(2)}) collective-permute-start(bf16[528,256]{1,0:T(8,128)(2,1)S(1)} %get-tuple-element.150), channel_id=1, source_target_pairs={{0,8},{1,9},{2,10},{3,11},{4,12},{5,13},{6,14},{7,15},{8,0},{9,1},... | collective-permute-start | bytes 811016 | tf_op jit(solution)/shard_map/ppermute | solution.py:40
  53.1 9.9 %collective-permute-start.5 = (bf16[384,1024]{1,0:T(8,128)(2,1)S(1)}, bf16[384,1024]{1,0:T(8,128)(2,1)S(1)}, u32[]{:S(2)}, u32[]{:S(2)}) collective-permute-start(bf16[384,1024]{1,0:T(8,128)(2,1)S(1)} %pad_maximum_fusion), channel_id=1, source_target_pairs={{0,1},{1,0},{2,3},{3,2},{4,5},{5,4},{6,7},{7,6},{8,9},{9,8},{10,11... | collective-permute-start | bytes 2359304 | tf_op jit(solution)/shard_map/cond/branch_1_fun/ppermute | solution.py:40
  53.2 9.8 %collective-permute-start.4 = (bf16[128,1024]{1,0:T(8,128)(2,1)}, bf16[128,1024]{1,0:T(8,128)(2,1)S(1)}, u32[]{:S(2)}, u32[]{:S(2)}) collective-permute-start(bf16[128,1024]{1,0:T(8,128)(2,1)} %get-tuple-element.17.refs_0_), channel_id=1, source_target_pairs={{0,6},{1,7},{2,4},{3,5},{4,2},{5,3},{6,0},{7,1},{8,14},{9,15},{10,... | collective-permute-start | bytes 786440 | tf_op jit(solution)/shard_map/cond/branch_1_fun/ppermute | solution.py:40
  63.0 2.2 %collective-permute-start.6 = (bf16[128,1024]{1,0:T(8,128)(2,1)S(1)}, bf16[128,1024]{1,0:T(8,128)(2,1)S(1)}, u32[]{:S(2)}, u32[]{:S(2)}) collective-permute-start(bf16[128,1024]{1,0:T(8,128)(2,1)S(1)} %collective-permute-done.4.refs_3_), channel_id=1, source_target_pairs={{0,1},{1,0},{2,3},{3,2},{4,5},{5,4},{6,7},{7,6},{8,9},{9,8},{10,11... | collective-permute-start | bytes 786440 | tf_op jit(solution)/shard_map/cond/branch_1_fun/ppermute | solution.py:40
  70.4 26.4 %collective-permute-start.28 = (bf16[528,256]{1,0:T(8,128)(2,1)}, bf16[528,256]{1,0:T(8,128)(2,1)S(1)}, u32[]{:S(2)}, u32[]{:S(2)}) collective-permute-start(bf16[528,256]{1,0:T(8,128)(2,1)} %get-tuple-element.144), channel_id=1, source_target_pairs={{0,8},{1,9},{2,10},{3,11},{4,12},{5,13},{6,14},{7,15},{8,0},{9,1},... | collective-permute-start | bytes 811016 | tf_op jit(solution)/shard_map/ppermute | solution.py:40
  71.8 25.1 %collective-permute-start.29 = (bf16[528,256]{1,0:T(8,128)(2,1)}, bf16[528,256]{1,0:T(8,128)(2,1)S(1)}, u32[]{:S(2)}, u32[]{:S(2)}) collective-permute-start(bf16[528,256]{1,0:T(8,128)(2,1)} %get-tuple-element.145), channel_id=1, source_target_pairs={{0,16},{1,17},{2,18},{3,19},{4,20},{5,21},{6,22},{7,23},{8,24},{9,... | collective-permute-start | bytes 811016 | tf_op jit(solution)/shard_map/ppermute | solution.py:40
  74.7 22.2 %collective-permute-start.30 = (bf16[528,256]{1,0:T(8,128)(2,1)}, bf16[528,256]{1,0:T(8,128)(2,1)S(1)}, u32[]{:S(2)}, u32[]{:S(2)}) collective-permute-start(bf16[528,256]{1,0:T(8,128)(2,1)} %get-tuple-element.146), channel_id=1, source_target_pairs={{0,24},{1,25},{2,26},{3,27},{4,28},{5,29},{6,30},{7,31},{8,16},{9,... | collective-permute-start | bytes 811016 | tf_op jit(solution)/shard_map/ppermute | solution.py:40
  78.2 2.1 %collective-permute-start = (f32[256,512]{1,0:T(8,128)}, f32[256,512]{1,0:T(8,128)S(1)}, u32[]{:S(2)}, u32[]{:S(2)}) collective-permute-start(f32[256,512]{1,0:T(8,128)} %get-tuple-element.29), channel_id=1, source_target_pairs={{0,1},{1,0},{2,3},{3,2},{4,5},{5,4},{6,7},{7,6},{8,9},{9,8},{10,11... | collective-permute-start | bytes 1572872 | tf_op jit(solution)/shard_map/cond/branch_1_fun/ppermute | solution.py:40
  81.6 4.6 %collective-permute-start.1 = (bf16[80,512]{1,0:T(8,128)(2,1)S(1)}, bf16[80,512]{1,0:T(8,128)(2,1)S(1)}, u32[]{:S(2)}, u32[]{:S(2)}) collective-permute-start(bf16[80,512]{1,0:T(8,128)(2,1)S(1)} %get-tuple-element.31), channel_id=1, source_target_pairs={{0,2},{1,3},{2,0},{3,1},{4,6},{5,7},{6,4},{7,5},{8,10},{9,11},{10,... | collective-permute-start | bytes 245768 | tf_op jit(solution)/shard_map/cond/branch_1_fun/ppermute | solution.py:40
  81.9 5.6 %collective-permute-start.2 = (bf16[80,512]{1,0:T(8,128)(2,1)S(1)}, bf16[80,512]{1,0:T(8,128)(2,1)S(1)}, u32[]{:S(2)}, u32[]{:S(2)}) collective-permute-start(bf16[80,512]{1,0:T(8,128)(2,1)S(1)} %get-tuple-element.34), channel_id=1, source_target_pairs={{0,4},{1,5},{2,6},{3,7},{4,0},{5,1},{6,2},{7,3},{8,12},{9,13},{10,... | collective-permute-start | bytes 245768 | tf_op jit(solution)/shard_map/cond/branch_1_fun/ppermute | solution.py:40
  86.2 5.3 %collective-permute-start.3 = (bf16[80,512]{1,0:T(8,128)(2,1)S(1)}, bf16[80,512]{1,0:T(8,128)(2,1)S(1)}, u32[]{:S(2)}, u32[]{:S(2)}) collective-permute-start(bf16[80,512]{1,0:T(8,128)(2,1)S(1)} %get-tuple-element.35), channel_id=1, source_target_pairs={{0,6},{1,7},{2,4},{3,5},{4,2},{5,3},{6,0},{7,1},{8,14},{9,15},{10,... | collective-permute-start | bytes 245768 | tf_op jit(solution)/shard_map/cond/branch_1_fun/ppermute | solution.py:40
  92.4 4.5 %collective-permute-start.34 = (f32[16,512]{1,0:T(8,128)S(1)}, f32[16,512]{1,0:T(8,128)S(1)}, u32[]{:S(2)}, u32[]{:S(2)}) collective-permute-start(f32[16,512]{1,0:T(8,128)S(1)} %get-tuple-element.154), channel_id=1, source_target_pairs={{0,8},{1,9},{2,10},{3,11},{4,12},{5,13},{6,14},{7,15},{8,0},{9,1},... | collective-permute-start | bytes 98312 | tf_op jit(solution)/shard_map/ppermute | solution.py:40
  93.0 8.3 %collective-permute-start.35 = (f32[16,512]{1,0:T(8,128)S(1)}, f32[16,512]{1,0:T(8,128)S(1)}, u32[]{:S(2)}, u32[]{:S(2)}) collective-permute-start(f32[16,512]{1,0:T(8,128)S(1)} %get-tuple-element.155), channel_id=1, source_target_pairs={{0,16},{1,17},{2,18},{3,19},{4,20},{5,21},{6,22},{7,23},{8,24},{9,... | collective-permute-start | bytes 98312 | tf_op jit(solution)/shard_map/ppermute | solution.py:40
  96.8 5.7 %collective-permute-start.36 = (f32[16,512]{1,0:T(8,128)S(1)}, f32[16,512]{1,0:T(8,128)S(1)}, u32[]{:S(2)}, u32[]{:S(2)}) collective-permute-start(f32[16,512]{1,0:T(8,128)S(1)} %get-tuple-element.156), channel_id=1, source_target_pairs={{0,24},{1,25},{2,26},{3,27},{4,28},{5,29},{6,30},{7,31},{8,16},{9,... | collective-permute-start | bytes 98312 | tf_op jit(solution)/shard_map/ppermute | solution.py:40
  105.1 2.0 %collective-permute-start.37 = (f32[256,512]{1,0:T(8,128)S(1)}, f32[256,512]{1,0:T(8,128)S(1)}, u32[]{:S(2)}, u32[]{:S(2)}) collective-permute-start(f32[256,512]{1,0:T(8,128)S(1)} %get-tuple-element.163), channel_id=1, source_target_pairs={{0,1},{1,0},{2,3},{3,2},{4,5},{5,4},{6,7},{7,6},{8,9},{9,8},{10,11... | collective-permute-start | bytes 1572872 | tf_op jit(solution)/shard_map/ppermute | solution.py:40
  108.0 5.1 %collective-permute-start.38 = (bf16[80,512]{1,0:T(8,128)(2,1)S(1)}, bf16[80,512]{1,0:T(8,128)(2,1)S(1)}, u32[]{:S(2)}, u32[]{:S(2)}) collective-permute-start(bf16[80,512]{1,0:T(8,128)(2,1)S(1)} %get-tuple-element.165), channel_id=1, source_target_pairs={{0,2},{1,3},{2,0},{3,1},{4,6},{5,7},{6,4},{7,5},{8,10},{9,11},{10,... | collective-permute-start | bytes 245768 | tf_op jit(solution)/shard_map/ppermute | solution.py:40
  108.3 6.2 %collective-permute-start.39 = (bf16[80,512]{1,0:T(8,128)(2,1)S(1)}, bf16[80,512]{1,0:T(8,128)(2,1)S(1)}, u32[]{:S(2)}, u32[]{:S(2)}) collective-permute-start(bf16[80,512]{1,0:T(8,128)(2,1)S(1)} %get-tuple-element.166), channel_id=1, source_target_pairs={{0,4},{1,5},{2,6},{3,7},{4,0},{5,1},{6,2},{7,3},{8,12},{9,13},{10,... | collective-permute-start | bytes 245768 | tf_op jit(solution)/shard_map/ppermute | solution.py:40
  108.8 5.7 %collective-permute-start.40 = (bf16[80,512]{1,0:T(8,128)(2,1)S(1)}, bf16[80,512]{1,0:T(8,128)(2,1)S(1)}, u32[]{:S(2)}, u32[]{:S(2)}) collective-permute-start(bf16[80,512]{1,0:T(8,128)(2,1)S(1)} %get-tuple-element.167), channel_id=1, source_target_pairs={{0,6},{1,7},{2,4},{3,5},{4,2},{5,3},{6,0},{7,1},{8,14},{9,15},{10,... | collective-permute-start | bytes 245768 | tf_op jit(solution)/shard_map/ppermute | solution.py:40
  115.4 7.1 %collective-permute-start.43 = (bf16[96,512]{1,0:T(8,128)(2,1)S(1)}, bf16[96,512]{1,0:T(8,128)(2,1)S(1)}, u32[]{:S(2)}, u32[]{:S(2)}) collective-permute-start(bf16[96,512]{1,0:T(8,128)(2,1)S(1)} %code.1.refs_0_), channel_id=1, source_target_pairs={{0,24},{1,25},{2,26},{3,27},{4,28},{5,29},{6,30},{7,31},{8,16},{9,... | collective-permute-start | bytes 294920 | tf_op jit(solution)/shard_map/ppermute | solution.py:40
  116.8 8.6 %collective-permute-start.42 = (bf16[96,512]{1,0:T(8,128)(2,1)S(1)}, bf16[96,512]{1,0:T(8,128)(2,1)S(1)}, u32[]{:S(2)}, u32[]{:S(2)}) collective-permute-start(bf16[96,512]{1,0:T(8,128)(2,1)S(1)} %code.1.refs_0_), channel_id=1, source_target_pairs={{0,16},{1,17},{2,18},{3,19},{4,20},{5,21},{6,22},{7,23},{8,24},{9,... | collective-permute-start | bytes 294920 | tf_op jit(solution)/shard_map/ppermute | solution.py:40
  116.8 8.6 %collective-permute-start.41 = (bf16[96,512]{1,0:T(8,128)(2,1)S(1)}, bf16[96,512]{1,0:T(8,128)(2,1)S(1)}, u32[]{:S(2)}, u32[]{:S(2)}) collective-permute-start(bf16[96,512]{1,0:T(8,128)(2,1)S(1)} %code.1.refs_0_), channel_id=1, source_target_pairs={{0,8},{1,9},{2,10},{3,11},{4,12},{5,13},{6,14},{7,15},{8,0},{9,1},... | collective-permute-start | bytes 294920 | tf_op jit(solution)/shard_map/ppermute | solution.py:40
  126.4 6.5 %collective-permute-start.46 = (bf16[128,512]{1,0:T(8,128)(2,1)S(1)}, bf16[128,512]{1,0:T(8,128)(2,1)S(1)}, u32[]{:S(2)}, u32[]{:S(2)}) collective-permute-start(bf16[128,512]{1,0:T(8,128)(2,1)S(1)} %finish.1.refs_0_), channel_id=1, source_target_pairs={{0,6},{1,7},{2,4},{3,5},{4,2},{5,3},{6,0},{7,1},{8,14},{9,15},{10,... | collective-permute-start | bytes 393224 | tf_op jit(solution)/shard_map/ppermute | solution.py:40
  129.0 5.9 %collective-permute-start.45 = (bf16[128,512]{1,0:T(8,128)(2,1)S(1)}, bf16[128,512]{1,0:T(8,128)(2,1)S(1)}, u32[]{:S(2)}, u32[]{:S(2)}) collective-permute-start(bf16[128,512]{1,0:T(8,128)(2,1)S(1)} %finish.1.refs_0_), channel_id=1, source_target_pairs={{0,4},{1,5},{2,6},{3,7},{4,0},{5,1},{6,2},{7,3},{8,12},{9,13},{10,... | collective-permute-start | bytes 393224 | tf_op jit(solution)/shard_map/ppermute | solution.py:40
  129.5 6.2 %collective-permute-start.44 = (bf16[128,512]{1,0:T(8,128)(2,1)S(1)}, bf16[128,512]{1,0:T(8,128)(2,1)S(1)}, u32[]{:S(2)}, u32[]{:S(2)}) collective-permute-start(bf16[128,512]{1,0:T(8,128)(2,1)S(1)} %finish.1.refs_0_), channel_id=1, source_target_pairs={{0,2},{1,3},{2,0},{3,1},{4,6},{5,7},{6,4},{7,5},{8,10},{9,11},{10,... | collective-permute-start | bytes 393224 | tf_op jit(solution)/shard_map/ppermute | solution.py:40
  130.0 5.7 %collective-permute-start.47 = (bf16[128,512]{1,0:T(8,128)(2,1)S(1)}, bf16[128,512]{1,0:T(8,128)(2,1)S(1)}, u32[]{:S(2)}, u32[]{:S(2)}) collective-permute-start(bf16[128,512]{1,0:T(8,128)(2,1)S(1)} %finish.1.refs_0_), channel_id=1, source_target_pairs={{0,1},{1,0},{2,3},{3,2},{4,5},{5,4},{6,7},{7,6},{8,9},{9,8},{10,11... | collective-permute-start | bytes 393224 | tf_op jit(solution)/shard_map/ppermute | solution.py:40
  133.0 2.8 %collective-permute-start.50 = (bf16[128,512]{1,0:T(8,128)(2,1)S(1)}, bf16[128,512]{1,0:T(8,128)(2,1)S(1)}, u32[]{:S(2)}, u32[]{:S(2)}) collective-permute-start(bf16[128,512]{1,0:T(8,128)(2,1)S(1)} %collective-permute-done.46.refs_3_), channel_id=1, source_target_pairs={{0,1},{1,0},{2,3},{3,2},{4,5},{5,4},{6,7},{7,6},{8,9},{9,8},{10,11... | collective-permute-start | bytes 393224 | tf_op jit(solution)/shard_map/ppermute | solution.py:40
  134.9 1.3 collective-permute-start.49
  135.7 1.3 collective-permute-start.48
  139.0 8.3 %collective-permute-start.51 = (bf16[256,256]{1,0:T(8,128)(2,1)S(1)}, bf16[256,256]{1,0:T(8,128)(2,1)S(1)}, u32[]{:S(2)}, u32[]{:S(2)}) collective-permute-start(bf16[256,256]{1,0:T(8,128)(2,1)S(1)} %get-tuple-element.179), channel_id=1, source_target_pairs={{0,24},{1,25},{2,26},{3,27},{4,28},{5,29},{6,30},{7,31},{8,16},{9,... | collective-permute-start | bytes 393224 | tf_op jit(solution)/shard_map/ppermute | solution.py:40
  140.7 11.3 %collective-permute-start.52 = (bf16[256,256]{1,0:T(8,128)(2,1)S(1)}, bf16[256,256]{1,0:T(8,128)(2,1)S(1)}, u32[]{:S(2)}, u32[]{:S(2)}) collective-permute-start(bf16[256,256]{1,0:T(8,128)(2,1)S(1)} %get-tuple-element.180), channel_id=1, source_target_pairs={{0,16},{1,17},{2,18},{3,19},{4,20},{5,21},{6,22},{7,23},{8,24},{9,... | collective-permute-start | bytes 393224 | tf_op jit(solution)/shard_map/ppermute | solution.py:40
  140.7 11.3 %collective-permute-start.53 = (bf16[256,256]{1,0:T(8,128)(2,1)S(1)}, bf16[256,256]{1,0:T(8,128)(2,1)S(1)}, u32[]{:S(2)}, u32[]{:S(2)}) collective-permute-start(bf16[256,256]{1,0:T(8,128)(2,1)S(1)} %get-tuple-element.181), channel_id=1, source_target_pairs={{0,8},{1,9},{2,10},{3,11},{4,12},{5,13},{6,14},{7,15},{8,0},{9,1},... | collective-permute-start | bytes 393224 | tf_op jit(solution)/shard_map/ppermute | solution.py:40

commit v9 on v8

--- a/solution.py
+++ b/solution.py
@@ -95,11 +95,23 @@
     return jnp.concatenate(ordered(parts, here), 0)
 
 
-def halve_kernel(place_ref, kept_ref, met_ref, *outs):
-    height = outs[0].shape[0]
-    for step, out in enumerate(outs):
-        at = pl.ds(pl.multiple_of((place_ref[1] ^ step) * height, height), height)
-        total = kept_ref[at, :] + met_ref[at, :]
+def gram_kernel(place_ref, own_ref, other_ref, *refs, n):
+    share_ref = None
+    if len(refs) > n:
+        share_ref, refs = refs[0], refs[1:]
+    height = refs[0].shape[0]
+    dims = (((1,), (1,)), ((), ()))
+    for step, out in enumerate(refs):
+        at = place_ref[2] * (n * height) + (place_ref[1] ^ step) * height
+        at = pl.ds(pl.multiple_of(at, height), height)
+        total = 0.0
+        for ref in (own_ref, other_ref):
+            total += lax.dot_general(ref[at, :], ref[...], dims, preferred_element_type=F32)
+        if share_ref is not None:
+            row = lax.broadcasted_iota(jnp.int32, total.shape, 0)
+            column = lax.broadcasted_iota(jnp.int32, total.shape, 1)
+            first = (row == height - 1) & (column == 0) & ((place_ref[1] ^ step) == n - 1)
+            total = jnp.where(first, share_ref[...], total)
         if step == 0:
             out[...] = total
         else:
@@ -141,7 +153,7 @@
         out_ref[at, :] = refs[step][coded:]
         met += decode(refs[step].at[:coded], 1)
     total = tree_sum(met)
-    last = (place_ref[1] == n - 1) & (place_ref[2] == k - 1)
+    last = place_ref[1] == n - 1
     edge = total[-8:, :128]
     row = lax.broadcasted_iota(jnp.int32, edge.shape, 0)
     column = lax.broadcasted_iota(jnp.int32, edge.shape, 1)
@@ -155,12 +167,12 @@
     out_ref[height:] = jnp.concatenate([total[:-8], edge], 0).astype(BF16)
 
 
-def local(kernel, place_array, args, shapes, name, **more):
+def local(kernel, place_array, args, shapes, name, out=None, **more):
     space = pl.BlockSpec(memory_space=pltpu.VMEM)
     return pl.pallas_call(
         kernel,
         in_specs=[pl.BlockSpec(memory_space=pltpu.SMEM)] + [space] * len(args),
-        out_specs=[space] * len(shapes),
+        out_specs=[out or space] * len(shapes),
         out_shape=[jax.ShapeDtypeStruct(shape, dtype) for shape, dtype in shapes],
         compiler_params=pltpu.CompilerParams(vmem_limit_bytes=VMEM_BYTES // 2),
         name=name,
@@ -168,23 +180,22 @@
     )(place_array, *args)
 
 
-def plane_rows(place, place_array, grams, few=False):
-    half, batch = grams[0].shape
-    kept, other = grams
-    other = place.send(other, lambda z, a, b: (z, a, b ^ 1))
-    height = half // place.n
+def plane_rows(place, place_array, packed, few=False, share=()):
+    batch = packed.shape[0]
+    height = batch // (place.n * place.k)
+    other = place.send(packed, lambda z, a, b: (z, a, b ^ 1))
     parts = local(
-        halve_kernel,
-        place_array,
-        (kept, other),
+        functools.partial(gram_kernel, n=place.n),
+        place_array,
+        (packed, other, *share),
         [((height, batch), F32)] + [((height + SCALE_ROWS, batch), BF16)] * (place.n - 1),
-        "halve",
+        "gram",
     )
     return sends(place, "a", parts, few)
 
 
-def first_rows(place, place_array, grams):
-    parts = plane_rows(place, place_array, grams, True)
+def first_rows(place, place_array, packed):
+    parts = plane_rows(place, place_array, packed, True)
     height, batch = parts[0].shape
     return local(
         functools.partial(plane_kernel, n=place.n),
@@ -342,13 +353,12 @@
     return own, parts[::-1]
 
 
-def normalize_kernel(place_ref, *refs, n, k, second):
+def normalize_kernel(place_ref, *refs, n, second):
     own_ref, parts = refs[0], refs[n - 1 : 0 : -1]
     refs = refs[n:]
     if second:
         other_ref, refs = refs[0], refs[1:]
     norm_ref, packed_ref, scale_ref = refs[:3]
-    grams = refs[3 : 3 + k]
     batch, columns = own_ref.shape
     height = batch // n
     met = [[own_ref[i * height : (i + 1) * height] for i in range(n)]]
@@ -368,27 +378,11 @@
             at = pl.multiple_of(plane * rows + (place_ref[1] ^ step) * few, few)
             norm_ref[pl.ds(at, few), :] = normed[first : first + few]
             packed_ref[pl.ds(at, few), :] = normed[first : first + few].astype(BF16)
-    dims = (((1,), (1,)), ((), ()))
-    packed = packed_ref[...]
-    size = batch // k
-    for i in range(k):
-        at = pl.multiple_of((place_ref[2] ^ i) * size, size)
-        gram = lax.dot_general(packed_ref[pl.ds(at, size), :], packed, dims, preferred_element_type=F32)
-        grams[i][...] = gram
     if second:
-        coeff_ref = refs[3 + k]
+        coeff_ref, share_ref = refs[3:]
         diag = jnp.sum(norm_ref[...] * other_ref[...], 0, keepdims=True) / batch
         coeff_ref[...] = 2.0 * ((1.0 - off_weight) * diag - 1.0)
-        share = jnp.sum((1.0 - diag) ** 2 - off_weight * diag * diag, 1, keepdims=True)
-        for i in range(k):
-
-            @pl.when((place_ref[2] ^ i) == k - 1)
-            def _():
-                row = grams[i][size - 8 :, :128]
-                first = (lax.broadcasted_iota(jnp.int32, row.shape, 0) == 7) & (
-                    lax.broadcasted_iota(jnp.int32, row.shape, 1) == 0
-                )
-                grams[i][size - 8 :, :128] = jnp.where(first, share, row)
+        share_ref[...] = jnp.sum((1.0 - diag) ** 2 - off_weight * diag * diag, 1, keepdims=True)
 
 
 def normalize_parts(place, place_array, own, parts, other=None):
@@ -399,20 +393,20 @@
         jax.ShapeDtypeStruct((batch, columns), F32),
         jax.ShapeDtypeStruct((batch, columns), BF16),
         jax.ShapeDtypeStruct((1, columns), F32),
-    ] + [jax.ShapeDtypeStruct((batch // k, batch), F32)] * k
+    ]
     if second:
-        out_shape.append(jax.ShapeDtypeStruct((1, columns), F32))
+        out_shape += [jax.ShapeDtypeStruct((1, columns), F32), jax.ShapeDtypeStruct((1, 1), F32)]
     args = [own, *parts[::-1]] + ([other] if second else [])
     space = pl.BlockSpec(memory_space=pltpu.VMEM)
     return pl.pallas_call(
-        functools.partial(normalize_kernel, n=n, k=k, second=second),
+        functools.partial(normalize_kernel, n=n, second=second),
         in_specs=[pl.BlockSpec(memory_space=pltpu.SMEM)] + [space] * len(args),
         out_specs=[space] * len(out_shape),
         out_shape=out_shape,
         compiler_params=pltpu.CompilerParams(vmem_limit_bytes=VMEM_BYTES // 2),
         cost_estimate=pl.CostEstimate(
-            flops=2 * batch * batch * columns,
-            bytes_accessed=16 * batch * columns + 4 * batch * batch,
+            flops=40 * batch * columns,
+            bytes_accessed=16 * batch * columns,
             transcendentals=0,
         ),
         name="normalize",
@@ -432,14 +426,15 @@
             to = pl.ds(pl.multiple_of(at, height), height)
             for view in range(2):
                 gram_ref[view, to, :] = grams[i * n + step][view * height : (view + 1) * height, :]
-    edge = batch - 128
-    tail = gram_ref[1, edge:, :128].astype(F32)
-    row = lax.broadcasted_iota(jnp.int32, tail.shape, 0)
-    column = lax.broadcasted_iota(jnp.int32, tail.shape, 1)
-    taken = (row == 127) & (column < 3)
-    mirror = gram_ref[1, :128, edge:].astype(F32).T
-    share = jnp.sum(jnp.where(taken, tail, 0.0), keepdims=True)
-    gram_ref[1, edge:, :128] = jnp.where(taken, mirror, tail).astype(BF16)
+    share = 0.0
+    for edge in (batch // 2 - 128, batch - 128):
+        tail = gram_ref[1, edge : edge + 128, :128].astype(F32)
+        row = lax.broadcasted_iota(jnp.int32, tail.shape, 0)
+        column = lax.broadcasted_iota(jnp.int32, tail.shape, 1)
+        taken = (row == 127) & (column < 3)
+        mirror = gram_ref[1, :128, edge : edge + 128].astype(F32).T
+        share += jnp.sum(jnp.where(taken, tail, 0.0), keepdims=True)
+        gram_ref[1, edge : edge + 128, :128] = jnp.where(taken, mirror, tail).astype(BF16)
     factor = 2.0 * off_weight / batch
     rows = batch // n
     for view in (1, 0):
@@ -474,22 +469,31 @@
 
 
 def place_kernel(place_ref, *refs, n):
-    parts, outs = [refs[0], *refs[n - 1 : 0 : -1]], refs[n:]
+    parts, outs, done = [refs[0], *refs[n - 1 : 0 : -1]], refs[n:-1], refs[-1]
     rows, columns = parts[0].shape[0] // len(outs), parts[0].shape[1]
+    copies = []
     for step in range(n):
         at = pl.ds(pl.multiple_of((place_ref[0] ^ step) * columns, columns), columns)
         for i, out in enumerate(outs):
-            out[:, at] = parts[step][i * rows : (i + 1) * rows, :]
+            part = parts[step].at[i * rows : (i + 1) * rows]
+            copies.append(pltpu.make_async_copy(part, out.at[:, at], done.at[step, i]))
+            copies[-1].start()
+    for copy in copies:
+        copy.wait()
 
 
 def with_kernels(place, h_first, h_second, weight):
     n, k, z, a, b = place.n, place.k, place.z, place.a, place.b
     place_array = jnp.stack([z, a, b]).astype(jnp.int32)
     first, second = lax.optimization_barrier((to_columns(place, h_first), h_second))
-    first, second = lax.optimization_barrier((to_planes(place, first), to_columns(place, second)))
+    first, second = to_planes(place, first), to_columns(place, second)
     first, late_weight = lax.optimization_barrier((lay(place, place_array, first), weight))
     met_1, second, held = lax.optimization_barrier(
-        (met_rows(place, first), to_planes(place, second), fetch(late_weight))
+        (
+            met_rows(place, first),
+            lay(place, place_array, to_planes(place, second)),
+            fetch(late_weight),
+        )
     )
 
     def sent(parts):
@@ -499,7 +503,6 @@
         return place.send(part, lambda z, a, b: (z, a, b ^ 1))
 
     own_1, parts_1 = project(place, place_array, [met_1, [swapped(part) for part in met_1]], held)
-    second = lay(place, place_array, second)
     size, here, toward = place.along("a")
     met_2 = [second] + [place.send(second, toward(step)) for step in range(1, size - 1)]
     own_1, parts_1, late_weight = lax.optimization_barrier((own_1, parts_1, weight))
@@ -515,16 +518,16 @@
     own_2, parts_2 = in_one(place, second_projected, (late_weight, *met_2))
     own_1, own_2 = lax.optimization_barrier((own_1, own_2))
     parts_2 = sent(parts_2)
-    norm_1, packed_1, scale_1, *grams = normalize_parts(place, place_array, own_1, parts_1)
-    met_1 = in_one(place, lambda *grams: first_rows(place, place_array, grams), grams)
+    norm_1, packed_1, scale_1 = normalize_parts(place, place_array, own_1, parts_1)
+    met_1 = in_one(place, lambda packed: first_rows(place, place_array, packed), (packed_1,))
     met_1 = sends(place, "z", met_1)
     own_2, parts_2, met_1 = lax.optimization_barrier((own_2, parts_2, met_1))
-    norm_2, packed_2, scale_2, *grams, coeff = normalize_parts(
+    norm_2, packed_2, scale_2, coeff, share = normalize_parts(
         place, place_array, own_2, parts_2, norm_1
     )
     height, batch = met_1[0].shape
     (rows_1,) = local(rows_kernel, place_array, met_1, [((height, batch), BF16)], "rows")
-    met_2 = plane_rows(place, place_array, grams)
+    met_2 = plane_rows(place, place_array, packed_2, share=(share,))
     rows = met_2[0].shape[0]
     (part,) = local(
         functools.partial(code_kernel, n=n),
@@ -557,6 +560,8 @@
         [first, *sends(place, "z", [first, *others[::-1]])[:0:-1]],
         [(h_first.shape, BF16)] * 2,
         "place",
+        pl.BlockSpec(memory_space=pltpu.HBM),
+        scratch_shapes=[pltpu.SemaphoreType.DMA((n, 2))],
     )
     return (out_1, out_2, loss.reshape(()))
 

time: 154 us -> 155 us (level)
  waiting for transfers between devices: 61.7 us -> 59.6 us
  Pallas kernels: 30.2 us -> 32 us
    ppermute x54, waiting for transfers between devices: 61.7 us -> 59.6 us  [send(): return lax.ppermute(value, ('dp', 'mp'), pairs)]
    pallas_call x10, Pallas kernels: 10.8 us -> 12.7 us  [local(): pl.pallas_call(kernel, in_specs=[pl.BlockSpec(memory_space=pltpu.SMEM)] +...]
  transfers between devices with their start and end apart: 54 -> 54, of which waited for: 26 -> 25; matrix products, arithmetic and copies ran while one was open for 1% -> 2% of each run, Pallas kernels for 14% -> 14%
where the time goes in v9:
time: 155 us; the launch traced here: 154 us
  waiting for transfers between devices  59.6 us (38%)
  starting transfers between devices  57.6 us (37%)
  Pallas kernels  32 us (21%)
  other arithmetic  2.13 us (1%)
  local copies, waits for them, and re-layouts  1.88 us (1%)
    ppermute x54, waiting for transfers between devices, send(): return lax.ppermute(value, ('dp', 'mp'), pairs)  59.6 us
    ppermute x54, starting transfers between devices, send(): return lax.ppermute(value, ('dp', 'mp'), pairs)  57.6 us
    pallas_call x10, Pallas kernels, local(): pl.pallas_call(kernel, in_specs=[pl.BlockSpec(memory_space=pltpu.SMEM)] +...  12.7 us
    pallas_call x2, Pallas kernels, project(): pl.pallas_call(functools.partial(project_kernel, counts=counts, n=n, k=k)...  9.09 us
    pallas_call x2, Pallas kernels, normalize_parts(): pl.pallas_call(functools.partial(normalize_kernel, n=n, second=second), i...  5.77 us
    pallas_call x2, Pallas kernels, fetch(): pl.pallas_call(fetch_kernel, in_specs=[pl.BlockSpec(memory_space=pl.ANY)]...  4.39 us
  transfers between devices with their start and end apart: 54, of which 25 were waited for; matrix products, arithmetic and copies ran while one was open for 2% of the time, Pallas kernels for 14%

profile of v9, /device:TPU:0, one launch (start us, length us, event | category | flops | bytes accessed | tf_op | source)
XLA Modules:
  0.0 154.3 jit_solution(14980088393237075154)
XLA Ops:
  0.7 1.0 dynamic-slice_bitcast_fusion.3
  1.6 4.0 %collective-permute-start.9 = (bf16[32,1024]{1,0:T(8,128)(2,1)S(1)}, bf16[32,1024]{1,0:T(8,128)(2,1)S(1)}, u32[]{:S(2)}, u32[]{:S(2)}) collective-permute-start(bf16[32,1024]{1,0:T(8,128)(2,1)S(1)} %get-tuple-element.165), channel_id=1, source_target_pairs={{0,6},{1,7},{2,4},{3,5},{4,2},{5,3},{6,0},{7,1},{8,14},{9,15},{10,... | collective-permute-start | bytes 196616 | tf_op jit(solution)/shard_map/ppermute | solution.py:40
  6.2 1.6 %collective-permute-done.9 = bf16[32,1024]{1,0:T(8,128)(2,1)S(1)} collective-permute-done((bf16[32,1024]{1,0:T(8,128)(2,1)S(1)}, bf16[32,1024]{1,0:T(8,128)(2,1)S(1)}, u32[]{:S(2)}, u32[]{:S(2)}) %collective-permute-start.9) | collective-permute-done | bytes 65568 | tf_op jit(solution)/shard_map/ppermute | solution.py:40
  7.8 2.0 %collective-permute-done.8 = bf16[32,1024]{1,0:T(8,128)(2,1)S(1)} collective-permute-done((bf16[32,1024]{1,0:T(8,128)(2,1)S(1)}, bf16[32,1024]{1,0:T(8,128)(2,1)S(1)}, u32[]{:S(2)}, u32[]{:S(2)}) %collective-permute-start.8) | collective-permute-done | bytes 65568 | tf_op jit(solution)/shard_map/ppermute | solution.py:40
  10.4 3.7 %collective-permute-start.12 = (bf16[32,1024]{1,0:T(8,128)(2,1)S(1)}, bf16[32,1024]{1,0:T(8,128)(2,1)S(1)}, u32[]{:S(2)}, u32[]{:S(2)}) collective-permute-start(bf16[32,1024]{1,0:T(8,128)(2,1)S(1)} %get-tuple-element.161), channel_id=1, source_target_pairs={{0,24},{1,25},{2,26},{3,27},{4,28},{5,29},{6,30},{7,31},{8,16},{9,... | collective-permute-start | bytes 196616 | tf_op jit(solution)/shard_map/ppermute | solution.py:40
  14.1 0.8 collective-permute-start.11
  14.8 0.9 dynamic-slice_bitcast_fusion
  16.3 1.6 %collective-permute-start.17 = (bf16[32,1024]{1,0:T(8,128)(2,1)S(1)}, bf16[32,1024]{1,0:T(8,128)(2,1)S(1)}, u32[]{:S(2)}, u32[]{:S(2)}) collective-permute-start(bf16[32,1024]{1,0:T(8,128)(2,1)S(1)} %get-tuple-element.159), channel_id=1, source_target_pairs={{0,4},{1,5},{2,6},{3,7},{4,0},{5,1},{6,2},{7,3},{8,12},{9,13},{10,... | collective-permute-start | bytes 196616 | tf_op jit(solution)/shard_map/ppermute | solution.py:40
  17.9 1.4 collective-permute-start.16
  20.0 1.6 %collective-permute-start.15 = (bf16[128,1024]{1,0:T(8,128)(2,1)S(1)}, bf16[128,1024]{1,0:T(8,128)(2,1)S(1)}, u32[]{:S(2)}, u32[]{:S(2)}) collective-permute-start(bf16[128,1024]{1,0:T(8,128)(2,1)S(1)} %lay.2.refs_0_), channel_id=1, source_target_pairs={{0,6},{1,7},{2,4},{3,5},{4,2},{5,3},{6,0},{7,1},{8,14},{9,15},{10,... | collective-permute-start | bytes 786440 | tf_op jit(solution)/shard_map/ppermute | solution.py:40
  22.0 1.6 %collective-permute-start.13 = (bf16[128,1024]{1,0:T(8,128)(2,1)S(1)}, bf16[128,1024]{1,0:T(8,128)(2,1)S(1)}, u32[]{:S(2)}, u32[]{:S(2)}) collective-permute-start(bf16[128,1024]{1,0:T(8,128)(2,1)S(1)} %lay.2.refs_0_), channel_id=1, source_target_pairs={{0,2},{1,3},{2,0},{3,1},{4,6},{5,7},{6,4},{7,5},{8,10},{9,11},{10,... | collective-permute-start | bytes 786440 | tf_op jit(solution)/shard_map/ppermute | solution.py:40
  23.9 0.9 broadcast_select_fusion.6
  24.7 3.7 %collective-permute-start.21 = (bf16[32,1024]{1,0:T(8,128)(2,1)S(1)}, bf16[32,1024]{1,0:T(8,128)(2,1)S(1)}, u32[]{:S(2)}, u32[]{:S(2)}) collective-permute-start(bf16[32,1024]{1,0:T(8,128)(2,1)S(1)} %get-tuple-element.154), channel_id=1, source_target_pairs={{0,24},{1,25},{2,26},{3,27},{4,28},{5,29},{6,30},{7,31},{8,16},{9,... | collective-permute-start | bytes 196616 | tf_op jit(solution)/shard_map/ppermute | solution.py:40
  28.5 3.1 %collective-permute-done.21.refs_3_ = bf16[32,1024]{1,0:T(8,128)(2,1)S(1)} collective-permute-done((bf16[32,1024]{1,0:T(8,128)(2,1)S(1)}, bf16[32,1024]{1,0:T(8,128)(2,1)S(1)}, u32[]{:S(2)}, u32[]{:S(2)}) %collective-permute-start.21) | collective-permute-done | bytes 65568 | tf_op jit(solution)/shard_map/ppermute | solution.py:40
  31.6 2.2 %fetch.3.refs_8_ = bf16[2048,1024]{1,0:T(8,128)(2,1)S(1)} custom-call(bf16[2048,1024]{1,0:T(8,128)(2,1)} %weight_ref), custom_call_target="tpu_custom_call" | custom-call | bytes 8388608 | tf_op jit(solution)/shard_map/fetch/pallas_call | solution.py:245
  33.8 3.6 %collective-permute-done.20.refs_2_ = bf16[32,1024]{1,0:T(8,128)(2,1)S(1)} collective-permute-done((bf16[32,1024]{1,0:T(8,128)(2,1)S(1)}, bf16[32,1024]{1,0:T(8,128)(2,1)S(1)}, u32[]{:S(2)}, u32[]{:S(2)}) %collective-permute-start.20) | collective-permute-done | bytes 65568 | tf_op jit(solution)/shard_map/ppermute | solution.py:40
  37.4 1.3 lay.3
  40.3 2.8 %collective-permute-start.26 = (bf16[128,1024]{1,0:T(8,128)(2,1)}, bf16[128,1024]{1,0:T(8,128)(2,1)}, u32[]{:S(2)}, u32[]{:S(2)}) collective-permute-start(bf16[128,1024]{1,0:T(8,128)(2,1)} %lay.3), channel_id=1, source_target_pairs={{0,2},{1,3},{2,0},{3,1},{4,6},{5,7},{6,4},{7,5},{8,10},{9,11},{10,... | collective-permute-start | bytes 786440 | tf_op jit(solution)/shard_map/ppermute | solution.py:40
  43.0 3.9 %project.3 = (f32[512,256]{1,0:T(8,128)S(1)}, bf16[528,256]{1,0:T(8,128)(2,1)S(1)}, bf16[528,256]{1,0:T(8,128)(2,1)S(1)}, bf16[528,256]{1,0:T(8,128)(2,1)S(1)}) custom-call(s32[3]{0:T(128)S(1)} %pad_add_fusion.place_ref, bf16[128,1024]{1,0:T(8,128)(2,1)S(1)} %lay.2.refs_0_, bf16[128,1024]{1,0:T(8,128)(2,1)S(1)} %collective-permute-done.13.refs_1_, ...), custom_call_target="tpu_custom_call" | custom-call | flops 2147483648 | bytes 7864320 | tf_op jit(solution)/shard_map/project/pallas_call | solution.py:339
  47.0 3.9 %collective-permute-start.31 = (bf16[528,256]{1,0:T(8,128)(2,1)S(1)}, bf16[528,256]{1,0:T(8,128)(2,1)S(1)}, u32[]{:S(2)}, u32[]{:S(2)}) collective-permute-start(bf16[528,256]{1,0:T(8,128)(2,1)S(1)} %get-tuple-element.120), channel_id=1, source_target_pairs={{0,24},{1,25},{2,26},{3,27},{4,28},{5,29},{6,30},{7,31},{8,16},{9,... | collective-permute-start | bytes 811016 | tf_op jit(solution)/shard_map/ppermute | solution.py:40
  51.5 18.5 %conditional.2 = (f32[512,256]{1,0:T(8,128)S(1)}, bf16[528,256]{1,0:T(8,128)(2,1)}, bf16[528,256]{1,0:T(8,128)(2,1)}, bf16[528,256]{1,0:T(8,128)(2,1)}) conditional(s32[]{:T(128)} %convert_element_type.4, () %tuple.35, (bf16[128,1024]{1,0:T(8,128)(2,1)}, bf16[128,1024]{1,0:T(8,128)(2,1)}, bf16[128,1024]{1,0:T(8,128)(2,1)}, ...), branch_computations={%region_0.1_spmd, %region_1.2_spmd} | conditional | flops 2149842944 | bytes 23068824 | solution.py:212
  51.5 1.2 pad_maximum_fusion
  52.7 1.1 collective-permute-start.4
  53.8 8.7 %collective-permute-done.4.refs_3_ = bf16[128,1024]{1,0:T(8,128)(2,1)S(1)} collective-permute-done((bf16[128,1024]{1,0:T(8,128)(2,1)}, bf16[128,1024]{1,0:T(8,128)(2,1)S(1)}, u32[]{:S(2)}, u32[]{:S(2)}) %collective-permute-start.4) | collective-permute-done | bytes 262176 | tf_op jit(solution)/shard_map/cond/branch_1_fun/ppermute | solution.py:40
  62.6 2.2 %fetch.2.refs_6_ = bf16[2048,1024]{1,0:T(8,128)(2,1)S(1)} custom-call(bf16[2048,1024]{1,0:T(8,128)(2,1)} %get-tuple-element.20.weight_ref), custom_call_target="tpu_custom_call" | custom-call | bytes 8388608 | tf_op jit(solution)/shard_map/cond/branch_1_fun/fetch/pallas_call | solution.py:245
  64.8 5.2 %project.2 = (f32[512,256]{1,0:T(8,128)S(1)}, bf16[528,256]{1,0:T(8,128)(2,1)}, bf16[528,256]{1,0:T(8,128)(2,1)}, bf16[528,256]{1,0:T(8,128)(2,1)}) custom-call(s32[3]{0:T(128)S(1)} %get-tuple-element.14.place_ref, bf16[128,1024]{1,0:T(8,128)(2,1)} %get-tuple-element.15.refs_0_, bf16[128,1024]{1,0:T(8,128)(2,1)} %get-tuple-element.16.refs_1_, ...), custom_call_target="tpu_custom_call" | custom-call | flops 2147483648 | bytes 7864320 | tf_op jit(solution)/shard_map/cond/branch_1_fun/project/pallas_call | solution.py:339
  70.0 1.4 collective-permute-start.28
  71.4 2.9 %collective-permute-start.29 = (bf16[528,256]{1,0:T(8,128)(2,1)}, bf16[528,256]{1,0:T(8,128)(2,1)S(1)}, u32[]{:S(2)}, u32[]{:S(2)}) collective-permute-start(bf16[528,256]{1,0:T(8,128)(2,1)} %get-tuple-element.117), channel_id=1, source_target_pairs={{0,16},{1,17},{2,18},{3,19},{4,20},{5,21},{6,22},{7,23},{8,24},{9,... | collective-permute-start | bytes 811016 | tf_op jit(solution)/shard_map/ppermute | solution.py:40
  74.4 2.8 %normalize.2 = (f32[512,256]{1,0:T(8,128)S(1)}, bf16[512,256]{1,0:T(8,128)(2,1)}, f32[1,256]{1,0:T(1,128)S(1)}) custom-call(s32[3]{0:T(128)S(1)} %pad_add_fusion.place_ref, f32[512,256]{1,0:T(8,128)S(1)} %get-tuple-element.119.refs_0_, bf16[528,256]{1,0:T(8,128)(2,1)S(1)} %collective-permute-done.31.refs_1_, ...), custom_call_target="tpu_custom_call" | custom-call | flops 5242880 | bytes 2097152 | tf_op jit(solution)/shard_map/normalize/pallas_call | solution.py:401
  77.2 14.3 %conditional.3 = ((f32[16,512]{1,0:T(8,128)S(1)}, f32[16,512]{1,0:T(8,128)S(1)}, f32[16,512]{1,0:T(8,128)S(1)}, f32[16,512]{1,0:T(8,128)S(1)})) conditional(s32[]{:T(128)} %convert_element_type.4, () %tuple.38, (bf16[512,256]{1,0:T(8,128)(2,1)}, s32[3]{0:T(128)S(1)}) %tuple.39), branch_computations={%region_2.3_spmd, %region_3.4_spmd} | conditional | bytes 2031784 | solution.py:212
  77.2 1.7 %collective-permute-done.other_ref = bf16[512,256]{1,0:T(8,128)(2,1)S(1)} collective-permute-done((bf16[512,256]{1,0:T(8,128)(2,1)}, bf16[512,256]{1,0:T(8,128)(2,1)S(1)}, u32[]{:S(2)}, u32[]{:S(2)}) %collective-permute-start) | collective-permute-done | bytes 262176 | tf_op jit(solution)/shard_map/cond/branch_1_fun/ppermute | solution.py:40
  78.9 1.8 %gram.2 = (f32[64,512]{1,0:T(8,128)S(1)}, bf16[80,512]{1,0:T(8,128)(2,1)S(1)}, bf16[80,512]{1,0:T(8,128)(2,1)S(1)}, bf16[80,512]{1,0:T(8,128)(2,1)S(1)}) custom-call(s32[3]{0:T(128)S(1)} %get-tuple-element.25.place_ref, bf16[512,256]{1,0:T(8,128)(2,1)} %get-tuple-element.26.own_ref, bf16[512,256]{1,0:T(8,128)(2,1)S(1)} %collective-permute-done.other_ref), custom_call_target="tpu_custom_call" | custom-call | tf_op jit(solution)/shard_map/cond/branch_1_fun/gram/pallas_call | solution.py:172
  80.8 1.6 %collective-permute-start.2 = (bf16[80,512]{1,0:T(8,128)(2,1)S(1)}, bf16[80,512]{1,0:T(8,128)(2,1)S(1)}, u32[]{:S(2)}, u32[]{:S(2)}) collective-permute-start(bf16[80,512]{1,0:T(8,128)(2,1)S(1)} %get-tuple-element.31), channel_id=1, source_target_pairs={{0,4},{1,5},{2,6},{3,7},{4,0},{5,1},{6,2},{7,3},{8,12},{9,13},{10,... | collective-permute-start | bytes 245768 | tf_op jit(solution)/shard_map/cond/branch_1_fun/ppermute | solution.py:40
  82.4 2.9 %collective-permute-done.1.refs_1_ = bf16[80,512]{1,0:T(8,128)(2,1)S(1)} collective-permute-done((bf16[80,512]{1,0:T(8,128)(2,1)S(1)}, bf16[80,512]{1,0:T(8,128)(2,1)S(1)}, u32[]{:S(2)}, u32[]{:S(2)}) %collective-permute-start.1) | collective-permute-done | bytes 81952 | tf_op jit(solution)/shard_map/cond/branch_1_fun/ppermute | solution.py:40
  85.3 1.1 collective-permute-start.3
  86.3 4.3 %collective-permute-done.3.refs_3_ = bf16[80,512]{1,0:T(8,128)(2,1)S(1)} collective-permute-done((bf16[80,512]{1,0:T(8,128)(2,1)S(1)}, bf16[80,512]{1,0:T(8,128)(2,1)S(1)}, u32[]{:S(2)}, u32[]{:S(2)}) %collective-permute-start.3) | collective-permute-done | bytes 81952 | tf_op jit(solution)/shard_map/cond/branch_1_fun/ppermute | solution.py:40
  90.6 0.9 plane.1
  92.1 3.8 %collective-permute-start.35 = (f32[16,512]{1,0:T(8,128)S(1)}, f32[16,512]{1,0:T(8,128)S(1)}, u32[]{:S(2)}, u32[]{:S(2)}) collective-permute-start(f32[16,512]{1,0:T(8,128)S(1)} %get-tuple-element.126), channel_id=1, source_target_pairs={{0,16},{1,17},{2,18},{3,19},{4,20},{5,21},{6,22},{7,23},{8,24},{9,... | collective-permute-start | bytes 98312 | tf_op jit(solution)/shard_map/ppermute | solution.py:40
  96.0 4.9 %collective-permute-done.35.refs_2_ = f32[16,512]{1,0:T(8,128)S(1)} collective-permute-done((f32[16,512]{1,0:T(8,128)S(1)}, f32[16,512]{1,0:T(8,128)S(1)}, u32[]{:S(2)}, u32[]{:S(2)}) %collective-permute-start.35) | collective-permute-done | bytes 32800 | tf_op jit(solution)/shard_map/ppermute | solution.py:40
  100.9 0.7 collective-permute-done.36.refs_3_
  101.6 2.9 %normalize.3 = (f32[512,256]{1,0:T(8,128)S(1)}, bf16[512,256]{1,0:T(8,128)(2,1)S(1)}, f32[1,256]{1,0:T(1,128)S(1)}, f32[1,256]{1,0:T(1,128)S(1)}, f32[1,1]{1,0:T(1,128)}) custom-call(s32[3]{0:T(128)S(1)} %pad_add_fusion.place_ref, f32[512,256]{1,0:T(8,128)S(1)} %get-tuple-element.128.refs_0_, bf16[528,256]{1,0:T(8,128)(2,1)S(1)} %collective-permute-done.30.refs_1_, ...), custom_call_target="tpu_custom_call" | custom-call | flops 5242880 | bytes 2097152 | tf_op jit(solution)/shard_map/normalize/pallas_call | solution.py:401
  104.6 1.5 collective-permute-done.37.other_ref
  106.1 2.0 %gram.3 = (f32[64,512]{1,0:T(8,128)S(1)}, bf16[80,512]{1,0:T(8,128)(2,1)S(1)}, bf16[80,512]{1,0:T(8,128)(2,1)S(1)}, bf16[80,512]{1,0:T(8,128)(2,1)S(1)}) custom-call(s32[3]{0:T(128)S(1)} %pad_add_fusion.place_ref, bf16[512,256]{1,0:T(8,128)(2,1)S(1)} %get-tuple-element.133.own_ref.refs_9_, bf16[512,256]{1,0:T(8,128)(2,1)S(1)} %collective-permute-done.37.other_ref, ...), custom_call_target="tpu_custom_call" | custom-call | tf_op jit(solution)/shard_map/gram/pallas_call | solution.py:172
  108.5 1.3 collective-permute-start.39
  109.8 1.9 %collective-permute-start.40 = (bf16[80,512]{1,0:T(8,128)(2,1)S(1)}, bf16[80,512]{1,0:T(8,128)(2,1)S(1)}, u32[]{:S(2)}, u32[]{:S(2)}) collective-permute-start(bf16[80,512]{1,0:T(8,128)(2,1)S(1)} %get-tuple-element.138), channel_id=1, source_target_pairs={{0,6},{1,7},{2,4},{3,5},{4,2},{5,3},{6,0},{7,1},{8,14},{9,15},{10,... | collective-permute-start | bytes 245768 | tf_op jit(solution)/shard_map/ppermute | solution.py:40
  112.3 1.0 collective-permute-done.38.refs_1_
  113.3 1.9 %collective-permute-done.40.refs_3_ = bf16[80,512]{1,0:T(8,128)(2,1)S(1)} collective-permute-done((bf16[80,512]{1,0:T(8,128)(2,1)S(1)}, bf16[80,512]{1,0:T(8,128)(2,1)S(1)}, u32[]{:S(2)}, u32[]{:S(2)}) %collective-permute-start.40) | collective-permute-done | bytes 81952 | tf_op jit(solution)/shard_map/ppermute | solution.py:40
  115.2 0.9 code.1.refs_0_
  116.1 2.0 %collective-permute-start.43 = (bf16[96,512]{1,0:T(8,128)(2,1)S(1)}, bf16[96,512]{1,0:T(8,128)(2,1)S(1)}, u32[]{:S(2)}, u32[]{:S(2)}) collective-permute-start(bf16[96,512]{1,0:T(8,128)(2,1)S(1)} %code.1.refs_0_), channel_id=1, source_target_pairs={{0,24},{1,25},{2,26},{3,27},{4,28},{5,29},{6,30},{7,31},{8,16},{9,... | collective-permute-start | bytes 294920 | tf_op jit(solution)/shard_map/ppermute | solution.py:40
  118.1 2.4 %collective-permute-start.41 = (bf16[96,512]{1,0:T(8,128)(2,1)S(1)}, bf16[96,512]{1,0:T(8,128)(2,1)S(1)}, u32[]{:S(2)}, u32[]{:S(2)}) collective-permute-start(bf16[96,512]{1,0:T(8,128)(2,1)S(1)} %code.1.refs_0_), channel_id=1, source_target_pairs={{0,8},{1,9},{2,10},{3,11},{4,12},{5,13},{6,14},{7,15},{8,0},{9,1},... | collective-permute-start | bytes 294920 | tf_op jit(solution)/shard_map/ppermute | solution.py:40
  120.6 2.8 %collective-permute-done.43.refs_3_ = bf16[96,512]{1,0:T(8,128)(2,1)S(1)} collective-permute-done((bf16[96,512]{1,0:T(8,128)(2,1)S(1)}, bf16[96,512]{1,0:T(8,128)(2,1)S(1)}, u32[]{:S(2)}, u32[]{:S(2)}) %collective-permute-start.43) | collective-permute-done | bytes 98336 | tf_op jit(solution)/shard_map/ppermute | solution.py:40
  123.3 3.1 %collective-permute-done.42.refs_2_ = bf16[96,512]{1,0:T(8,128)(2,1)S(1)} collective-permute-done((bf16[96,512]{1,0:T(8,128)(2,1)S(1)}, bf16[96,512]{1,0:T(8,128)(2,1)S(1)}, u32[]{:S(2)}, u32[]{:S(2)}) %collective-permute-start.42) | collective-permute-done | bytes 98336 | tf_op jit(solution)/shard_map/ppermute | solution.py:40
  126.4 1.0 finish.1.refs_0_
  127.4 1.9 %collective-permute-start.46 = (bf16[128,512]{1,0:T(8,128)(2,1)S(1)}, bf16[128,512]{1,0:T(8,128)(2,1)S(1)}, u32[]{:S(2)}, u32[]{:S(2)}) collective-permute-start(bf16[128,512]{1,0:T(8,128)(2,1)S(1)} %finish.1.refs_0_), channel_id=1, source_target_pairs={{0,6},{1,7},{2,4},{3,5},{4,2},{5,3},{6,0},{7,1},{8,14},{9,15},{10,... | collective-permute-start | bytes 393224 | tf_op jit(solution)/shard_map/ppermute | solution.py:40
  130.0 1.0 collective-permute-start.44
  131.0 3.7 %collective-permute-done.46.refs_3_ = bf16[128,512]{1,0:T(8,128)(2,1)S(1)} collective-permute-done((bf16[128,512]{1,0:T(8,128)(2,1)S(1)}, bf16[128,512]{1,0:T(8,128)(2,1)S(1)}, u32[]{:S(2)}, u32[]{:S(2)}) %collective-permute-start.46) | collective-permute-done | bytes 131104 | tf_op jit(solution)/shard_map/ppermute | solution.py:40
  134.8 1.0 collective-permute-done.45.refs_2_
  136.2 0.8 collective-permute-done.49.refs_6_
  137.3 2.3 %gradient.1 = (bf16[256,256]{1,0:T(8,128)(2,1)S(1)}, bf16[256,256]{1,0:T(8,128)(2,1)S(1)}, bf16[256,256]{1,0:T(8,128)(2,1)S(1)}, bf16[256,256]{1,0:T(8,128)(2,1)S(1)}, f32[1,1]{1,0:T(1,128)}) custom-call(s32[3]{0:T(128)S(1)} %pad_add_fusion.place_ref, bf16[128,512]{1,0:T(8,128)(2,1)S(1)} %finish.1.refs_0_, ...), custom_call_target="tpu_custom_call" | custom-call | tf_op jit(solution)/shard_map/gradient/pallas_call | solution.py:172
  139.5 2.1 %collective-permute-start.51 = (bf16[256,256]{1,0:T(8,128)(2,1)S(1)}, bf16[256,256]{1,0:T(8,128)(2,1)S(1)}, u32[]{:S(2)}, u32[]{:S(2)}) collective-permute-start(bf16[256,256]{1,0:T(8,128)(2,1)S(1)} %get-tuple-element.148), channel_id=1, source_target_pairs={{0,24},{1,25},{2,26},{3,27},{4,28},{5,29},{6,30},{7,31},{8,16},{9,... | collective-permute-start | bytes 393224 | tf_op jit(solution)/shard_map/ppermute | solution.py:40
  141.6 2.3 %collective-permute-start.53 = (bf16[256,256]{1,0:T(8,128)(2,1)S(1)}, bf16[256,256]{1,0:T(8,128)(2,1)S(1)}, u32[]{:S(2)}, u32[]{:S(2)}) collective-permute-start(bf16[256,256]{1,0:T(8,128)(2,1)S(1)} %get-tuple-element.150), channel_id=1, source_target_pairs={{0,8},{1,9},{2,10},{3,11},{4,12},{5,13},{6,14},{7,15},{8,0},{9,1},... | collective-permute-start | bytes 393224 | tf_op jit(solution)/shard_map/ppermute | solution.py:40
  143.9 3.9 %collective-permute-done.51.refs_1_ = bf16[256,256]{1,0:T(8,128)(2,1)S(1)} collective-permute-done((bf16[256,256]{1,0:T(8,128)(2,1)S(1)}, bf16[256,256]{1,0:T(8,128)(2,1)S(1)}, u32[]{:S(2)}, u32[]{:S(2)}) %collective-permute-start.51) | collective-permute-done | bytes 131104 | tf_op jit(solution)/shard_map/ppermute | solution.py:40
  147.8 4.9 %collective-permute-done.52.refs_2_ = bf16[256,256]{1,0:T(8,128)(2,1)S(1)} collective-permute-done((bf16[256,256]{1,0:T(8,128)(2,1)S(1)}, bf16[256,256]{1,0:T(8,128)(2,1)S(1)}, u32[]{:S(2)}, u32[]{:S(2)}) %collective-permute-start.52) | collective-permute-done | bytes 131104 | tf_op jit(solution)/shard_map/ppermute | solution.py:40
  152.7 1.4 place.1
  (68 shorter events, 8.5 us)
Async XLA Ops:
  1.6 6.2 %collective-permute-start.9 = (bf16[32,1024]{1,0:T(8,128)(2,1)S(1)}, bf16[32,1024]{1,0:T(8,128)(2,1)S(1)}, u32[]{:S(2)}, u32[]{:S(2)}) collective-permute-start(bf16[32,1024]{1,0:T(8,128)(2,1)S(1)} %get-tuple-element.165), channel_id=1, source_target_pairs={{0,6},{1,7},{2,4},{3,5},{4,2},{5,3},{6,0},{7,1},{8,14},{9,15},{10,... | collective-permute-start | bytes 196616 | tf_op jit(solution)/shard_map/ppermute | solution.py:40
  5.6 4.3 %collective-permute-start.8 = (bf16[32,1024]{1,0:T(8,128)(2,1)S(1)}, bf16[32,1024]{1,0:T(8,128)(2,1)S(1)}, u32[]{:S(2)}, u32[]{:S(2)}) collective-permute-start(bf16[32,1024]{1,0:T(8,128)(2,1)S(1)} %get-tuple-element.166), channel_id=1, source_target_pairs={{0,4},{1,5},{2,6},{3,7},{4,0},{5,1},{6,2},{7,3},{8,12},{9,13},{10,... | collective-permute-start | bytes 196616 | tf_op jit(solution)/shard_map/ppermute | solution.py:40
  6.1 4.3 %collective-permute-start.7 = (bf16[32,1024]{1,0:T(8,128)(2,1)S(1)}, bf16[32,1024]{1,0:T(8,128)(2,1)S(1)}, u32[]{:S(2)}, u32[]{:S(2)}) collective-permute-start(bf16[32,1024]{1,0:T(8,128)(2,1)S(1)} %get-tuple-element.167), channel_id=1, source_target_pairs={{0,2},{1,3},{2,0},{3,1},{4,6},{5,7},{6,4},{7,5},{8,10},{9,11},{10,... | collective-permute-start | bytes 196616 | tf_op jit(solution)/shard_map/ppermute | solution.py:40
  10.4 7.5 %collective-permute-start.12 = (bf16[32,1024]{1,0:T(8,128)(2,1)S(1)}, bf16[32,1024]{1,0:T(8,128)(2,1)S(1)}, u32[]{:S(2)}, u32[]{:S(2)}) collective-permute-start(bf16[32,1024]{1,0:T(8,128)(2,1)S(1)} %get-tuple-element.161), channel_id=1, source_target_pairs={{0,24},{1,25},{2,26},{3,27},{4,28},{5,29},{6,30},{7,31},{8,16},{9,... | collective-permute-start | bytes 196616 | tf_op jit(solution)/shard_map/ppermute | solution.py:40
  14.1 5.3 %collective-permute-start.10 = (bf16[32,1024]{1,0:T(8,128)(2,1)S(1)}, bf16[32,1024]{1,0:T(8,128)(2,1)S(1)}, u32[]{:S(2)}, u32[]{:S(2)}) collective-permute-start(bf16[32,1024]{1,0:T(8,128)(2,1)S(1)} %get-tuple-element.162), channel_id=1, source_target_pairs={{0,8},{1,9},{2,10},{3,11},{4,12},{5,13},{6,14},{7,15},{8,0},{9,1},... | collective-permute-start | bytes 196616 | tf_op jit(solution)/shard_map/ppermute | solution.py:40
  14.1 5.3 %collective-permute-start.11 = (bf16[32,1024]{1,0:T(8,128)(2,1)S(1)}, bf16[32,1024]{1,0:T(8,128)(2,1)S(1)}, u32[]{:S(2)}, u32[]{:S(2)}) collective-permute-start(bf16[32,1024]{1,0:T(8,128)(2,1)S(1)} %get-tuple-element.163), channel_id=1, source_target_pairs={{0,16},{1,17},{2,18},{3,19},{4,20},{5,21},{6,22},{7,23},{8,24},{9,... | collective-permute-start | bytes 196616 | tf_op jit(solution)/shard_map/ppermute | solution.py:40
  15.8 6.2 %collective-permute-start.18 = (bf16[32,1024]{1,0:T(8,128)(2,1)S(1)}, bf16[32,1024]{1,0:T(8,128)(2,1)S(1)}, u32[]{:S(2)}, u32[]{:S(2)}) collective-permute-start(bf16[32,1024]{1,0:T(8,128)(2,1)S(1)} %get-tuple-element.158), channel_id=1, source_target_pairs={{0,2},{1,3},{2,0},{3,1},{4,6},{5,7},{6,4},{7,5},{8,10},{9,11},{10,... | collective-permute-start | bytes 196616 | tf_op jit(solution)/shard_map/ppermute | solution.py:40
  16.3 7.2 %collective-permute-start.17 = (bf16[32,1024]{1,0:T(8,128)(2,1)S(1)}, bf16[32,1024]{1,0:T(8,128)(2,1)S(1)}, u32[]{:S(2)}, u32[]{:S(2)}) collective-permute-start(bf16[32,1024]{1,0:T(8,128)(2,1)S(1)} %get-tuple-element.159), channel_id=1, source_target_pairs={{0,4},{1,5},{2,6},{3,7},{4,0},{5,1},{6,2},{7,3},{8,12},{9,13},{10,... | collective-permute-start | bytes 196616 | tf_op jit(solution)/shard_map/ppermute | solution.py:40
  17.9 6.0 %collective-permute-start.16 = (bf16[32,1024]{1,0:T(8,128)(2,1)S(1)}, bf16[32,1024]{1,0:T(8,128)(2,1)S(1)}, u32[]{:S(2)}, u32[]{:S(2)}) collective-permute-start(bf16[32,1024]{1,0:T(8,128)(2,1)S(1)} %get-tuple-element.160), channel_id=1, source_target_pairs={{0,6},{1,7},{2,4},{3,5},{4,2},{5,3},{6,0},{7,1},{8,14},{9,15},{10,... | collective-permute-start | bytes 196616 | tf_op jit(solution)/shard_map/ppermute | solution.py:40
  20.0 18.7 %collective-permute-start.15 = (bf16[128,1024]{1,0:T(8,128)(2,1)S(1)}, bf16[128,1024]{1,0:T(8,128)(2,1)S(1)}, u32[]{:S(2)}, u32[]{:S(2)}) collective-permute-start(bf16[128,1024]{1,0:T(8,128)(2,1)S(1)} %lay.2.refs_0_), channel_id=1, source_target_pairs={{0,6},{1,7},{2,4},{3,5},{4,2},{5,3},{6,0},{7,1},{8,14},{9,15},{10,... | collective-permute-start | bytes 786440 | tf_op jit(solution)/shard_map/ppermute | solution.py:40
  21.5 17.1 %collective-permute-start.14 = (bf16[128,1024]{1,0:T(8,128)(2,1)S(1)}, bf16[128,1024]{1,0:T(8,128)(2,1)S(1)}, u32[]{:S(2)}, u32[]{:S(2)}) collective-permute-start(bf16[128,1024]{1,0:T(8,128)(2,1)S(1)} %lay.2.refs_0_), channel_id=1, source_target_pairs={{0,4},{1,5},{2,6},{3,7},{4,0},{5,1},{6,2},{7,3},{8,12},{9,13},{10,... | collective-permute-start | bytes 786440 | tf_op jit(solution)/shard_map/ppermute | solution.py:40
  22.0 16.7 %collective-permute-start.13 = (bf16[128,1024]{1,0:T(8,128)(2,1)S(1)}, bf16[128,1024]{1,0:T(8,128)(2,1)S(1)}, u32[]{:S(2)}, u32[]{:S(2)}) collective-permute-start(bf16[128,1024]{1,0:T(8,128)(2,1)S(1)} %lay.2.refs_0_), channel_id=1, source_target_pairs={{0,2},{1,3},{2,0},{3,1},{4,6},{5,7},{6,4},{7,5},{8,10},{9,11},{10,... | collective-permute-start | bytes 786440 | tf_op jit(solution)/shard_map/ppermute | solution.py:40
  24.7 6.8 %collective-permute-start.21 = (bf16[32,1024]{1,0:T(8,128)(2,1)S(1)}, bf16[32,1024]{1,0:T(8,128)(2,1)S(1)}, u32[]{:S(2)}, u32[]{:S(2)}) collective-permute-start(bf16[32,1024]{1,0:T(8,128)(2,1)S(1)} %get-tuple-element.154), channel_id=1, source_target_pairs={{0,24},{1,25},{2,26},{3,27},{4,28},{5,29},{6,30},{7,31},{8,16},{9,... | collective-permute-start | bytes 196616 | tf_op jit(solution)/shard_map/ppermute | solution.py:40
  28.5 5.3 %collective-permute-start.19 = (bf16[32,1024]{1,0:T(8,128)(2,1)S(1)}, bf16[32,1024]{1,0:T(8,128)(2,1)S(1)}, u32[]{:S(2)}, u32[]{:S(2)}) collective-permute-start(bf16[32,1024]{1,0:T(8,128)(2,1)S(1)} %get-tuple-element.156), channel_id=1, source_target_pairs={{0,8},{1,9},{2,10},{3,11},{4,12},{5,13},{6,14},{7,15},{8,0},{9,1},... | collective-permute-start | bytes 196616 | tf_op jit(solution)/shard_map/ppermute | solution.py:40
  31.5 5.9 %collective-permute-start.20 = (bf16[32,1024]{1,0:T(8,128)(2,1)S(1)}, bf16[32,1024]{1,0:T(8,128)(2,1)S(1)}, u32[]{:S(2)}, u32[]{:S(2)}) collective-permute-start(bf16[32,1024]{1,0:T(8,128)(2,1)S(1)} %get-tuple-element.157), channel_id=1, source_target_pairs={{0,16},{1,17},{2,18},{3,19},{4,20},{5,21},{6,22},{7,23},{8,24},{9,... | collective-permute-start | bytes 196616 | tf_op jit(solution)/shard_map/ppermute | solution.py:40
  38.7 1.6 %collective-permute-start.22 = (bf16[128,1024]{1,0:T(8,128)(2,1)S(1)}, bf16[128,1024]{1,0:T(8,128)(2,1)S(1)}, u32[]{:S(2)}, u32[]{:S(2)}) collective-permute-start(bf16[128,1024]{1,0:T(8,128)(2,1)S(1)} %lay.2.refs_0_), channel_id=1, source_target_pairs={{0,1},{1,0},{2,3},{3,2},{4,5},{5,4},{6,7},{7,6},{8,9},{9,8},{10,11... | collective-permute-start | bytes 786440 | tf_op jit(solution)/shard_map/ppermute | solution.py:40
  38.7 4.3 %collective-permute-start.23 = (bf16[128,1024]{1,0:T(8,128)(2,1)S(1)}, bf16[128,1024]{1,0:T(8,128)(2,1)S(1)}, u32[]{:S(2)}, u32[]{:S(2)}) collective-permute-start(bf16[128,1024]{1,0:T(8,128)(2,1)S(1)} %collective-permute-done.13.refs_1_), channel_id=1, source_target_pairs={{0,1},{1,0},{2,3},{3,2},{4,5},{5,4},{6,7},{7,6},{8,9},{9,8},{10,11... | collective-permute-start | bytes 786440 | tf_op jit(solution)/shard_map/ppermute | solution.py:40
  39.2 3.8 %collective-permute-start.24 = (bf16[128,1024]{1,0:T(8,128)(2,1)S(1)}, bf16[128,1024]{1,0:T(8,128)(2,1)S(1)}, u32[]{:S(2)}, u32[]{:S(2)}) collective-permute-start(bf16[128,1024]{1,0:T(8,128)(2,1)S(1)} %collective-permute-done.14.refs_2_), channel_id=1, source_target_pairs={{0,1},{1,0},{2,3},{3,2},{4,5},{5,4},{6,7},{7,6},{8,9},{9,8},{10,11... | collective-permute-start | bytes 786440 | tf_op jit(solution)/shard_map/ppermute | solution.py:40
  39.3 3.7 %collective-permute-start.25 = (bf16[128,1024]{1,0:T(8,128)(2,1)S(1)}, bf16[128,1024]{1,0:T(8,128)(2,1)S(1)}, u32[]{:S(2)}, u32[]{:S(2)}) collective-permute-start(bf16[128,1024]{1,0:T(8,128)(2,1)S(1)} %collective-permute-done.15.refs_3_), channel_id=1, source_target_pairs={{0,1},{1,0},{2,3},{3,2},{4,5},{5,4},{6,7},{7,6},{8,9},{9,8},{10,11... | collective-permute-start | bytes 786440 | tf_op jit(solution)/shard_map/ppermute | solution.py:40
  39.8 11.7 %collective-permute-start.27 = (bf16[128,1024]{1,0:T(8,128)(2,1)}, bf16[128,1024]{1,0:T(8,128)(2,1)}, u32[]{:S(2)}, u32[]{:S(2)}) collective-permute-start(bf16[128,1024]{1,0:T(8,128)(2,1)} %lay.3), channel_id=1, source_target_pairs={{0,4},{1,5},{2,6},{3,7},{4,0},{5,1},{6,2},{7,3},{8,12},{9,13},{10,... | collective-permute-start | bytes 786440 | tf_op jit(solution)/shard_map/ppermute | solution.py:40
  40.3 11.2 %collective-permute-start.26 = (bf16[128,1024]{1,0:T(8,128)(2,1)}, bf16[128,1024]{1,0:T(8,128)(2,1)}, u32[]{:S(2)}, u32[]{:S(2)}) collective-permute-start(bf16[128,1024]{1,0:T(8,128)(2,1)} %lay.3), channel_id=1, source_target_pairs={{0,2},{1,3},{2,0},{3,1},{4,6},{5,7},{6,4},{7,5},{8,10},{9,11},{10,... | collective-permute-start | bytes 786440 | tf_op jit(solution)/shard_map/ppermute | solution.py:40
  47.0 27.3 %collective-permute-start.31 = (bf16[528,256]{1,0:T(8,128)(2,1)S(1)}, bf16[528,256]{1,0:T(8,128)(2,1)S(1)}, u32[]{:S(2)}, u32[]{:S(2)}) collective-permute-start(bf16[528,256]{1,0:T(8,128)(2,1)S(1)} %get-tuple-element.120), channel_id=1, source_target_pairs={{0,24},{1,25},{2,26},{3,27},{4,28},{5,29},{6,30},{7,31},{8,16},{9,... | collective-permute-start | bytes 811016 | tf_op jit(solution)/shard_map/ppermute | solution.py:40
  50.8 23.5 %collective-permute-start.32 = (bf16[528,256]{1,0:T(8,128)(2,1)S(1)}, bf16[528,256]{1,0:T(8,128)(2,1)S(1)}, u32[]{:S(2)}, u32[]{:S(2)}) collective-permute-start(bf16[528,256]{1,0:T(8,128)(2,1)S(1)} %get-tuple-element.121), channel_id=1, source_target_pairs={{0,16},{1,17},{2,18},{3,19},{4,20},{5,21},{6,22},{7,23},{8,24},{9,... | collective-permute-start | bytes 811016 | tf_op jit(solution)/shard_map/ppermute | solution.py:40
  50.8 23.5 %collective-permute-start.33 = (bf16[528,256]{1,0:T(8,128)(2,1)S(1)}, bf16[528,256]{1,0:T(8,128)(2,1)S(1)}, u32[]{:S(2)}, u32[]{:S(2)}) collective-permute-start(bf16[528,256]{1,0:T(8,128)(2,1)S(1)} %get-tuple-element.122), channel_id=1, source_target_pairs={{0,8},{1,9},{2,10},{3,11},{4,12},{5,13},{6,14},{7,15},{8,0},{9,1},... | collective-permute-start | bytes 811016 | tf_op jit(solution)/shard_map/ppermute | solution.py:40
  52.6 9.9 %collective-permute-start.5 = (bf16[384,1024]{1,0:T(8,128)(2,1)S(1)}, bf16[384,1024]{1,0:T(8,128)(2,1)S(1)}, u32[]{:S(2)}, u32[]{:S(2)}) collective-permute-start(bf16[384,1024]{1,0:T(8,128)(2,1)S(1)} %pad_maximum_fusion), channel_id=1, source_target_pairs={{0,1},{1,0},{2,3},{3,2},{4,5},{5,4},{6,7},{7,6},{8,9},{9,8},{10,11... | collective-permute-start | bytes 2359304 | tf_op jit(solution)/shard_map/cond/branch_1_fun/ppermute | solution.py:40
  52.7 9.8 %collective-permute-start.4 = (bf16[128,1024]{1,0:T(8,128)(2,1)}, bf16[128,1024]{1,0:T(8,128)(2,1)S(1)}, u32[]{:S(2)}, u32[]{:S(2)}) collective-permute-start(bf16[128,1024]{1,0:T(8,128)(2,1)} %get-tuple-element.15.refs_0_), channel_id=1, source_target_pairs={{0,6},{1,7},{2,4},{3,5},{4,2},{5,3},{6,0},{7,1},{8,14},{9,15},{10,... | collective-permute-start | bytes 786440 | tf_op jit(solution)/shard_map/cond/branch_1_fun/ppermute | solution.py:40
  62.6 2.2 %collective-permute-start.6 = (bf16[128,1024]{1,0:T(8,128)(2,1)S(1)}, bf16[128,1024]{1,0:T(8,128)(2,1)S(1)}, u32[]{:S(2)}, u32[]{:S(2)}) collective-permute-start(bf16[128,1024]{1,0:T(8,128)(2,1)S(1)} %collective-permute-done.4.refs_3_), channel_id=1, source_target_pairs={{0,1},{1,0},{2,3},{3,2},{4,5},{5,4},{6,7},{7,6},{8,9},{9,8},{10,11... | collective-permute-start | bytes 786440 | tf_op jit(solution)/shard_map/cond/branch_1_fun/ppermute | solution.py:40
  70.0 26.0 %collective-permute-start.28 = (bf16[528,256]{1,0:T(8,128)(2,1)}, bf16[528,256]{1,0:T(8,128)(2,1)S(1)}, u32[]{:S(2)}, u32[]{:S(2)}) collective-permute-start(bf16[528,256]{1,0:T(8,128)(2,1)} %get-tuple-element.116), channel_id=1, source_target_pairs={{0,8},{1,9},{2,10},{3,11},{4,12},{5,13},{6,14},{7,15},{8,0},{9,1},... | collective-permute-start | bytes 811016 | tf_op jit(solution)/shard_map/ppermute | solution.py:40
  71.4 24.6 %collective-permute-start.29 = (bf16[528,256]{1,0:T(8,128)(2,1)}, bf16[528,256]{1,0:T(8,128)(2,1)S(1)}, u32[]{:S(2)}, u32[]{:S(2)}) collective-permute-start(bf16[528,256]{1,0:T(8,128)(2,1)} %get-tuple-element.117), channel_id=1, source_target_pairs={{0,16},{1,17},{2,18},{3,19},{4,20},{5,21},{6,22},{7,23},{8,24},{9,... | collective-permute-start | bytes 811016 | tf_op jit(solution)/shard_map/ppermute | solution.py:40
  74.3 21.7 %collective-permute-start.30 = (bf16[528,256]{1,0:T(8,128)(2,1)}, bf16[528,256]{1,0:T(8,128)(2,1)S(1)}, u32[]{:S(2)}, u32[]{:S(2)}) collective-permute-start(bf16[528,256]{1,0:T(8,128)(2,1)} %get-tuple-element.118), channel_id=1, source_target_pairs={{0,24},{1,25},{2,26},{3,27},{4,28},{5,29},{6,30},{7,31},{8,16},{9,... | collective-permute-start | bytes 811016 | tf_op jit(solution)/shard_map/ppermute | solution.py:40
  77.2 1.7 %collective-permute-start = (bf16[512,256]{1,0:T(8,128)(2,1)}, bf16[512,256]{1,0:T(8,128)(2,1)S(1)}, u32[]{:S(2)}, u32[]{:S(2)}) collective-permute-start(bf16[512,256]{1,0:T(8,128)(2,1)} %get-tuple-element.26.own_ref), channel_id=1, source_target_pairs={{0,1},{1,0},{2,3},{3,2},{4,5},{5,4},{6,7},{7,6},{8,9},{9,8},{10,11... | collective-permute-start | bytes 786440 | tf_op jit(solution)/shard_map/cond/branch_1_fun/ppermute | solution.py:40
  80.7 4.5 %collective-permute-start.1 = (bf16[80,512]{1,0:T(8,128)(2,1)S(1)}, bf16[80,512]{1,0:T(8,128)(2,1)S(1)}, u32[]{:S(2)}, u32[]{:S(2)}) collective-permute-start(bf16[80,512]{1,0:T(8,128)(2,1)S(1)} %get-tuple-element.28), channel_id=1, source_target_pairs={{0,2},{1,3},{2,0},{3,1},{4,6},{5,7},{6,4},{7,5},{8,10},{9,11},{10,... | collective-permute-start | bytes 245768 | tf_op jit(solution)/shard_map/cond/branch_1_fun/ppermute | solution.py:40
  80.8 5.5 %collective-permute-start.2 = (bf16[80,512]{1,0:T(8,128)(2,1)S(1)}, bf16[80,512]{1,0:T(8,128)(2,1)S(1)}, u32[]{:S(2)}, u32[]{:S(2)}) collective-permute-start(bf16[80,512]{1,0:T(8,128)(2,1)S(1)} %get-tuple-element.31), channel_id=1, source_target_pairs={{0,4},{1,5},{2,6},{3,7},{4,0},{5,1},{6,2},{7,3},{8,12},{9,13},{10,... | collective-permute-start | bytes 245768 | tf_op jit(solution)/shard_map/cond/branch_1_fun/ppermute | solution.py:40
  85.3 5.3 %collective-permute-start.3 = (bf16[80,512]{1,0:T(8,128)(2,1)S(1)}, bf16[80,512]{1,0:T(8,128)(2,1)S(1)}, u32[]{:S(2)}, u32[]{:S(2)}) collective-permute-start(bf16[80,512]{1,0:T(8,128)(2,1)S(1)} %get-tuple-element.32), channel_id=1, source_target_pairs={{0,6},{1,7},{2,4},{3,5},{4,2},{5,3},{6,0},{7,1},{8,14},{9,15},{10,... | collective-permute-start | bytes 245768 | tf_op jit(solution)/shard_map/cond/branch_1_fun/ppermute | solution.py:40
  91.5 4.5 %collective-permute-start.34 = (f32[16,512]{1,0:T(8,128)S(1)}, f32[16,512]{1,0:T(8,128)S(1)}, u32[]{:S(2)}, u32[]{:S(2)}) collective-permute-start(f32[16,512]{1,0:T(8,128)S(1)} %get-tuple-element.125), channel_id=1, source_target_pairs={{0,8},{1,9},{2,10},{3,11},{4,12},{5,13},{6,14},{7,15},{8,0},{9,1},... | collective-permute-start | bytes 98312 | tf_op jit(solution)/shard_map/ppermute | solution.py:40
  92.1 8.8 %collective-permute-start.35 = (f32[16,512]{1,0:T(8,128)S(1)}, f32[16,512]{1,0:T(8,128)S(1)}, u32[]{:S(2)}, u32[]{:S(2)}) collective-permute-start(f32[16,512]{1,0:T(8,128)S(1)} %get-tuple-element.126), channel_id=1, source_target_pairs={{0,16},{1,17},{2,18},{3,19},{4,20},{5,21},{6,22},{7,23},{8,24},{9,... | collective-permute-start | bytes 98312 | tf_op jit(solution)/shard_map/ppermute | solution.py:40
  95.9 5.7 %collective-permute-start.36 = (f32[16,512]{1,0:T(8,128)S(1)}, f32[16,512]{1,0:T(8,128)S(1)}, u32[]{:S(2)}, u32[]{:S(2)}) collective-permute-start(f32[16,512]{1,0:T(8,128)S(1)} %get-tuple-element.127), channel_id=1, source_target_pairs={{0,24},{1,25},{2,26},{3,27},{4,28},{5,29},{6,30},{7,31},{8,16},{9,... | collective-permute-start | bytes 98312 | tf_op jit(solution)/shard_map/ppermute | solution.py:40
  104.6 1.5 collective-permute-start.37
  108.2 5.1 %collective-permute-start.38 = (bf16[80,512]{1,0:T(8,128)(2,1)S(1)}, bf16[80,512]{1,0:T(8,128)(2,1)S(1)}, u32[]{:S(2)}, u32[]{:S(2)}) collective-permute-start(bf16[80,512]{1,0:T(8,128)(2,1)S(1)} %get-tuple-element.136), channel_id=1, source_target_pairs={{0,2},{1,3},{2,0},{3,1},{4,6},{5,7},{6,4},{7,5},{8,10},{9,11},{10,... | collective-permute-start | bytes 245768 | tf_op jit(solution)/shard_map/ppermute | solution.py:40
  108.5 4.8 %collective-permute-start.39 = (bf16[80,512]{1,0:T(8,128)(2,1)S(1)}, bf16[80,512]{1,0:T(8,128)(2,1)S(1)}, u32[]{:S(2)}, u32[]{:S(2)}) collective-permute-start(bf16[80,512]{1,0:T(8,128)(2,1)S(1)} %get-tuple-element.137), channel_id=1, source_target_pairs={{0,4},{1,5},{2,6},{3,7},{4,0},{5,1},{6,2},{7,3},{8,12},{9,13},{10,... | collective-permute-start | bytes 245768 | tf_op jit(solution)/shard_map/ppermute | solution.py:40
  109.8 5.3 %collective-permute-start.40 = (bf16[80,512]{1,0:T(8,128)(2,1)S(1)}, bf16[80,512]{1,0:T(8,128)(2,1)S(1)}, u32[]{:S(2)}, u32[]{:S(2)}) collective-permute-start(bf16[80,512]{1,0:T(8,128)(2,1)S(1)} %get-tuple-element.138), channel_id=1, source_target_pairs={{0,6},{1,7},{2,4},{3,5},{4,2},{5,3},{6,0},{7,1},{8,14},{9,15},{10,... | collective-permute-start | bytes 245768 | tf_op jit(solution)/shard_map/ppermute | solution.py:40
  116.1 7.2 %collective-permute-start.43 = (bf16[96,512]{1,0:T(8,128)(2,1)S(1)}, bf16[96,512]{1,0:T(8,128)(2,1)S(1)}, u32[]{:S(2)}, u32[]{:S(2)}) collective-permute-start(bf16[96,512]{1,0:T(8,128)(2,1)S(1)} %code.1.refs_0_), channel_id=1, source_target_pairs={{0,24},{1,25},{2,26},{3,27},{4,28},{5,29},{6,30},{7,31},{8,16},{9,... | collective-permute-start | bytes 294920 | tf_op jit(solution)/shard_map/ppermute | solution.py:40
  118.1 8.3 %collective-permute-start.42 = (bf16[96,512]{1,0:T(8,128)(2,1)S(1)}, bf16[96,512]{1,0:T(8,128)(2,1)S(1)}, u32[]{:S(2)}, u32[]{:S(2)}) collective-permute-start(bf16[96,512]{1,0:T(8,128)(2,1)S(1)} %code.1.refs_0_), channel_id=1, source_target_pairs={{0,16},{1,17},{2,18},{3,19},{4,20},{5,21},{6,22},{7,23},{8,24},{9,... | collective-permute-start | bytes 294920 | tf_op jit(solution)/shard_map/ppermute | solution.py:40
  118.1 8.3 %collective-permute-start.41 = (bf16[96,512]{1,0:T(8,128)(2,1)S(1)}, bf16[96,512]{1,0:T(8,128)(2,1)S(1)}, u32[]{:S(2)}, u32[]{:S(2)}) collective-permute-start(bf16[96,512]{1,0:T(8,128)(2,1)S(1)} %code.1.refs_0_), channel_id=1, source_target_pairs={{0,8},{1,9},{2,10},{3,11},{4,12},{5,13},{6,14},{7,15},{8,0},{9,1},... | collective-permute-start | bytes 294920 | tf_op jit(solution)/shard_map/ppermute | solution.py:40
  127.4 7.3 %collective-permute-start.46 = (bf16[128,512]{1,0:T(8,128)(2,1)S(1)}, bf16[128,512]{1,0:T(8,128)(2,1)S(1)}, u32[]{:S(2)}, u32[]{:S(2)}) collective-permute-start(bf16[128,512]{1,0:T(8,128)(2,1)S(1)} %finish.1.refs_0_), channel_id=1, source_target_pairs={{0,6},{1,7},{2,4},{3,5},{4,2},{5,3},{6,0},{7,1},{8,14},{9,15},{10,... | collective-permute-start | bytes 393224 | tf_op jit(solution)/shard_map/ppermute | solution.py:40
  129.3 6.4 %collective-permute-start.45 = (bf16[128,512]{1,0:T(8,128)(2,1)S(1)}, bf16[128,512]{1,0:T(8,128)(2,1)S(1)}, u32[]{:S(2)}, u32[]{:S(2)}) collective-permute-start(bf16[128,512]{1,0:T(8,128)(2,1)S(1)} %finish.1.refs_0_), channel_id=1, source_target_pairs={{0,4},{1,5},{2,6},{3,7},{4,0},{5,1},{6,2},{7,3},{8,12},{9,13},{10,... | collective-permute-start | bytes 393224 | tf_op jit(solution)/shard_map/ppermute | solution.py:40
  130.0 6.0 %collective-permute-start.44 = (bf16[128,512]{1,0:T(8,128)(2,1)S(1)}, bf16[128,512]{1,0:T(8,128)(2,1)S(1)}, u32[]{:S(2)}, u32[]{:S(2)}) collective-permute-start(bf16[128,512]{1,0:T(8,128)(2,1)S(1)} %finish.1.refs_0_), channel_id=1, source_target_pairs={{0,2},{1,3},{2,0},{3,1},{4,6},{5,7},{6,4},{7,5},{8,10},{9,11},{10,... | collective-permute-start | bytes 393224 | tf_op jit(solution)/shard_map/ppermute | solution.py:40
  131.0 5.2 %collective-permute-start.47 = (bf16[128,512]{1,0:T(8,128)(2,1)S(1)}, bf16[128,512]{1,0:T(8,128)(2,1)S(1)}, u32[]{:S(2)}, u32[]{:S(2)}) collective-permute-start(bf16[128,512]{1,0:T(8,128)(2,1)S(1)} %finish.1.refs_0_), channel_id=1, source_target_pairs={{0,1},{1,0},{2,3},{3,2},{4,5},{5,4},{6,7},{7,6},{8,9},{9,8},{10,11... | collective-permute-start | bytes 393224 | tf_op jit(solution)/shard_map/ppermute | solution.py:40
  134.8 1.5 collective-permute-start.50
  135.7 1.3 collective-permute-start.49
  135.9 1.3 collective-permute-start.48
  139.5 8.3 %collective-permute-start.51 = (bf16[256,256]{1,0:T(8,128)(2,1)S(1)}, bf16[256,256]{1,0:T(8,128)(2,1)S(1)}, u32[]{:S(2)}, u32[]{:S(2)}) collective-permute-start(bf16[256,256]{1,0:T(8,128)(2,1)S(1)} %get-tuple-element.148), channel_id=1, source_target_pairs={{0,24},{1,25},{2,26},{3,27},{4,28},{5,29},{6,30},{7,31},{8,16},{9,... | collective-permute-start | bytes 393224 | tf_op jit(solution)/shard_map/ppermute | solution.py:40
  141.6 11.1 %collective-permute-start.52 = (bf16[256,256]{1,0:T(8,128)(2,1)S(1)}, bf16[256,256]{1,0:T(8,128)(2,1)S(1)}, u32[]{:S(2)}, u32[]{:S(2)}) collective-permute-start(bf16[256,256]{1,0:T(8,128)(2,1)S(1)} %get-tuple-element.149), channel_id=1, source_target_pairs={{0,16},{1,17},{2,18},{3,19},{4,20},{5,21},{6,22},{7,23},{8,24},{9,... | collective-permute-start | bytes 393224 | tf_op jit(solution)/shard_map/ppermute | solution.py:40
  141.6 11.1 %collective-permute-start.53 = (bf16[256,256]{1,0:T(8,128)(2,1)S(1)}, bf16[256,256]{1,0:T(8,128)(2,1)S(1)}, u32[]{:S(2)}, u32[]{:S(2)}) collective-permute-start(bf16[256,256]{1,0:T(8,128)(2,1)S(1)} %get-tuple-element.150), channel_id=1, source_target_pairs={{0,8},{1,9},{2,10},{3,11},{4,12},{5,13},{6,14},{7,15},{8,0},{9,1},... | collective-permute-start | bytes 393224 | tf_op jit(solution)/shard_map/ppermute | solution.py:40

commit v10 on v8

--- a/solution.py
+++ b/solution.py
@@ -95,11 +95,22 @@
     return jnp.concatenate(ordered(parts, here), 0)
 
 
-def halve_kernel(place_ref, kept_ref, met_ref, *outs):
-    height = outs[0].shape[0]
+BLOCKS = 4
+KEPT = 3
+
+
+def halve_kernel(place_ref, kept_ref, met_ref, *outs, n):
+    height = kept_ref.shape[0] // n
+    width = kept_ref.shape[1] // BLOCKS
     for step, out in enumerate(outs):
-        at = pl.ds(pl.multiple_of((place_ref[1] ^ step) * height, height), height)
-        total = kept_ref[at, :] + met_ref[at, :]
+        block = place_ref[1] ^ step
+        at = pl.ds(pl.multiple_of(block * height, height), height)
+        block = (place_ref[2] * n + block) // (2 * n // BLOCKS)
+        total = []
+        for i in range(KEPT):
+            cut = pl.ds(pl.multiple_of(lax.rem(block + i, BLOCKS) * width, width), width)
+            total.append(kept_ref[at, cut] + met_ref[at, cut])
+        total = jnp.concatenate(total, 1)
         if step == 0:
             out[...] = total
         else:
@@ -142,7 +153,8 @@
         met += decode(refs[step].at[:coded], 1)
     total = tree_sum(met)
     last = (place_ref[1] == n - 1) & (place_ref[2] == k - 1)
-    edge = total[-8:, :128]
+    start = 2 * (total.shape[1] // KEPT)
+    edge = total[-8:, start:]
     row = lax.broadcasted_iota(jnp.int32, edge.shape, 0)
     column = lax.broadcasted_iota(jnp.int32, edge.shape, 1)
     taken = (row == 7) & last
@@ -151,7 +163,7 @@
     middle = (whole - high).astype(BF16).astype(F32)
     three = jnp.where(column == 0, high, jnp.where(column == 1, middle, whole - high - middle))
     edge = jnp.where(taken & (column < 3), three, edge)
-    edge = jnp.concatenate([edge, total[-8:, 128:]], 1)
+    edge = jnp.concatenate([total[-8:, :start], edge], 1)
     out_ref[height:] = jnp.concatenate([total[:-8], edge], 0).astype(BF16)
 
 
@@ -172,9 +184,9 @@
     half, batch = grams[0].shape
     kept, other = grams
     other = place.send(other, lambda z, a, b: (z, a, b ^ 1))
-    height = half // place.n
+    height, batch = half // place.n, batch * KEPT // BLOCKS
     parts = local(
-        halve_kernel,
+        functools.partial(halve_kernel, n=place.n),
         place_array,
         (kept, other),
         [((height, batch), F32)] + [((height + SCALE_ROWS, batch), BF16)] * (place.n - 1),
@@ -384,11 +396,12 @@
 
             @pl.when((place_ref[2] ^ i) == k - 1)
             def _():
-                row = grams[i][size - 8 :, :128]
+                at = batch // BLOCKS
+                row = grams[i][size - 8 :, at : at + 128]
                 first = (lax.broadcasted_iota(jnp.int32, row.shape, 0) == 7) & (
                     lax.broadcasted_iota(jnp.int32, row.shape, 1) == 0
                 )
-                grams[i][size - 8 :, :128] = jnp.where(first, share, row)
+                grams[i][size - 8 :, at : at + 128] = jnp.where(first, share, row)
 
 
 def normalize_parts(place, place_array, own, parts, other=None):
@@ -426,20 +439,30 @@
     gram_ref, whole_ref = refs[n + 1 :]
     batch, columns = norms[0].shape
     height = grams[0].shape[0] // 2
+    width = batch // BLOCKS
     for i in range(k):
         for step in range(n):
-            at = ((place_ref[2] ^ i) * n + (place_ref[1] ^ step)) * height
-            to = pl.ds(pl.multiple_of(at, height), height)
-            for view in range(2):
-                gram_ref[view, to, :] = grams[i * n + step][view * height : (view + 1) * height, :]
-    edge = batch - 128
-    tail = gram_ref[1, edge:, :128].astype(F32)
+            block = (place_ref[2] ^ i) * n + (place_ref[1] ^ step)
+            at = pl.ds(pl.multiple_of(block * height, height), height)
+            block = block // (2 * n // BLOCKS)
+            for j in range(KEPT):
+                to = pl.ds(pl.multiple_of(lax.rem(block + j, BLOCKS) * width, width), width)
+                for view in range(2):
+                    gram_ref[view, at, to] = grams[i * n + step][
+                        view * height : (view + 1) * height, j * width : (j + 1) * width
+                    ]
+    blocks = [slice(i * width, (i + 1) * width) for i in range(BLOCKS)]
+    for view in range(2):
+        for i in range(BLOCKS):
+            other = gram_ref[view, blocks[i - 1], blocks[i]].astype(F32).T
+            gram_ref[view, blocks[i], blocks[i - 1]] = other.astype(BF16)
+    tail = gram_ref[1, blocks[3], blocks[1]].astype(F32)
     row = lax.broadcasted_iota(jnp.int32, tail.shape, 0)
     column = lax.broadcasted_iota(jnp.int32, tail.shape, 1)
-    taken = (row == 127) & (column < 3)
-    mirror = gram_ref[1, :128, edge:].astype(F32).T
+    taken = (row == width - 1) & (column < 3)
+    mirror = gram_ref[1, blocks[1], blocks[3]].astype(F32).T
     share = jnp.sum(jnp.where(taken, tail, 0.0), keepdims=True)
-    gram_ref[1, edge:, :128] = jnp.where(taken, mirror, tail).astype(BF16)
+    gram_ref[1, blocks[3], blocks[1]] = jnp.where(taken, mirror, tail).astype(BF16)
     factor = 2.0 * off_weight / batch
     rows = batch // n
     for view in (1, 0):
@@ -485,8 +508,8 @@
 def with_kernels(place, h_first, h_second, weight):
     n, k, z, a, b = place.n, place.k, place.z, place.a, place.b
     place_array = jnp.stack([z, a, b]).astype(jnp.int32)
-    first, second = lax.optimization_barrier((to_columns(place, h_first), h_second))
-    first, second = lax.optimization_barrier((to_planes(place, first), to_columns(place, second)))
+    first = to_columns(place, h_first)
+    first, second = lax.optimization_barrier((to_planes(place, first), to_columns(place, h_second)))
     first, late_weight = lax.optimization_barrier((lay(place, place_array, first), weight))
     met_1, second, held = lax.optimization_barrier(
         (met_rows(place, first), to_planes(place, second), fetch(late_weight))

time: 154 us -> 147 us (0.955)
  waiting for transfers between devices: 61.7 us -> 55.8 us
    ppermute x54, waiting for transfers between devices: 61.7 us -> 55.8 us  [send(): return lax.ppermute(value, ('dp', 'mp'), pairs)]
  transfers between devices with their start and end apart: 54 -> 54, of which waited for: 26 -> 25; matrix products, arithmetic and copies ran while one was open for 1% -> 2% of each run, Pallas kernels for 14% -> 14%
where the time goes in v10:
time: 147 us
  starting transfers between devices  56.2 us (38%)
  waiting for transfers between devices  55.8 us (38%)
  Pallas kernels  30.1 us (20%)
  other arithmetic  2.13 us (1%)
  local copies, waits for them, and re-layouts  1.88 us (1%)
    ppermute x54, starting transfers between devices, send(): return lax.ppermute(value, ('dp', 'mp'), pairs)  56.2 us
    ppermute x54, waiting for transfers between devices, send(): return lax.ppermute(value, ('dp', 'mp'), pairs)  55.8 us
    pallas_call x10, Pallas kernels, local(): pl.pallas_call(kernel, in_specs=[pl.BlockSpec(memory_space=pltpu.SMEM)] +...  10.7 us
    pallas_call x2, Pallas kernels, project(): pl.pallas_call(functools.partial(project_kernel, counts=counts, n=n, k=k)...  9.07 us
    pallas_call x2, Pallas kernels, normalize_parts(): pl.pallas_call(functools.partial(normalize_kernel, n=n, k=k, second=secon...  6.01 us
    pallas_call x2, Pallas kernels, fetch(): pl.pallas_call(fetch_kernel, in_specs=[pl.BlockSpec(memory_space=pl.ANY)]...  4.39 us
  transfers between devices with their start and end apart: 54, of which 25 were waited for; matrix products, arithmetic and copies ran while one was open for 2% of the time, Pallas kernels for 14%

profile of v10, /device:TPU:0, one launch (start us, length us, event | category | flops | bytes accessed | tf_op | source)
XLA Modules:
  0.0 147.1 jit_solution(1591903938762327356)
XLA Ops:
  0.7 0.9 dynamic-slice_bitcast_fusion.4
  1.6 3.0 %collective-permute-start.9 = (bf16[32,1024]{1,0:T(8,128)(2,1)S(1)}, bf16[32,1024]{1,0:T(8,128)(2,1)S(1)}, u32[]{:S(2)}, u32[]{:S(2)}) collective-permute-start(bf16[32,1024]{1,0:T(8,128)(2,1)S(1)} %get-tuple-element.187), channel_id=1, source_target_pairs={{0,2},{1,3},{2,0},{3,1},{4,6},{5,7},{6,4},{7,5},{8,10},{9,11},{10,... | collective-permute-start | bytes 196616 | tf_op jit(solution)/shard_map/ppermute | solution.py:40
  4.6 1.5 %collective-permute-start.8 = (bf16[32,1024]{1,0:T(8,128)(2,1)S(1)}, bf16[32,1024]{1,0:T(8,128)(2,1)S(1)}, u32[]{:S(2)}, u32[]{:S(2)}) collective-permute-start(bf16[32,1024]{1,0:T(8,128)(2,1)S(1)} %get-tuple-element.188), channel_id=1, source_target_pairs={{0,4},{1,5},{2,6},{3,7},{4,0},{5,1},{6,2},{7,3},{8,12},{9,13},{10,... | collective-permute-start | bytes 196616 | tf_op jit(solution)/shard_map/ppermute | solution.py:40
  6.1 1.0 dynamic-slice_bitcast_fusion
  7.1 3.0 %collective-permute-start.15 = (bf16[32,1024]{1,0:T(8,128)(2,1)S(1)}, bf16[32,1024]{1,0:T(8,128)(2,1)S(1)}, u32[]{:S(2)}, u32[]{:S(2)}) collective-permute-start(bf16[32,1024]{1,0:T(8,128)(2,1)S(1)} %get-tuple-element.183), channel_id=1, source_target_pairs={{0,6},{1,7},{2,4},{3,5},{4,2},{5,3},{6,0},{7,1},{8,14},{9,15},{10,... | collective-permute-start | bytes 196616 | tf_op jit(solution)/shard_map/ppermute | solution.py:40
  11.3 0.9 broadcast_select_fusion.10
  12.2 3.9 %collective-permute-start.12 = (bf16[32,1024]{1,0:T(8,128)(2,1)S(1)}, bf16[32,1024]{1,0:T(8,128)(2,1)S(1)}, u32[]{:S(2)}, u32[]{:S(2)}) collective-permute-start(bf16[32,1024]{1,0:T(8,128)(2,1)S(1)} %get-tuple-element.175), channel_id=1, source_target_pairs={{0,24},{1,25},{2,26},{3,27},{4,28},{5,29},{6,30},{7,31},{8,16},{9,... | collective-permute-start | bytes 196616 | tf_op jit(solution)/shard_map/ppermute | solution.py:40
  16.8 1.6 %collective-permute-done.12.refs_3_ = bf16[32,1024]{1,0:T(8,128)(2,1)S(1)} collective-permute-done((bf16[32,1024]{1,0:T(8,128)(2,1)S(1)}, bf16[32,1024]{1,0:T(8,128)(2,1)S(1)}, u32[]{:S(2)}, u32[]{:S(2)}) %collective-permute-start.12) | collective-permute-done | bytes 65568 | tf_op jit(solution)/shard_map/ppermute | solution.py:40
  18.4 2.1 %collective-permute-done.10.refs_1_ = bf16[32,1024]{1,0:T(8,128)(2,1)S(1)} collective-permute-done((bf16[32,1024]{1,0:T(8,128)(2,1)S(1)}, bf16[32,1024]{1,0:T(8,128)(2,1)S(1)}, u32[]{:S(2)}, u32[]{:S(2)}) %collective-permute-start.10) | collective-permute-done | bytes 65568 | tf_op jit(solution)/shard_map/ppermute | solution.py:40
  21.8 2.1 %collective-permute-start.18 = (bf16[128,1024]{1,0:T(8,128)(2,1)S(1)}, bf16[128,1024]{1,0:T(8,128)(2,1)S(1)}, u32[]{:S(2)}, u32[]{:S(2)}) collective-permute-start(bf16[128,1024]{1,0:T(8,128)(2,1)S(1)} %lay.2.refs_0_), channel_id=1, source_target_pairs={{0,6},{1,7},{2,4},{3,5},{4,2},{5,3},{6,0},{7,1},{8,14},{9,15},{10,... | collective-permute-start | bytes 786440 | tf_op jit(solution)/shard_map/ppermute | solution.py:40
  24.4 0.9 collective-permute-start.16
  25.4 1.7 %collective-permute-start.21 = (bf16[32,1024]{1,0:T(8,128)(2,1)S(1)}, bf16[32,1024]{1,0:T(8,128)(2,1)S(1)}, u32[]{:S(2)}, u32[]{:S(2)}) collective-permute-start(bf16[32,1024]{1,0:T(8,128)(2,1)S(1)} %get-tuple-element.179), channel_id=1, source_target_pairs={{0,24},{1,25},{2,26},{3,27},{4,28},{5,29},{6,30},{7,31},{8,16},{9,... | collective-permute-start | bytes 196616 | tf_op jit(solution)/shard_map/ppermute | solution.py:40
  27.5 4.1 %collective-permute-done.21.refs_3_ = bf16[32,1024]{1,0:T(8,128)(2,1)S(1)} collective-permute-done((bf16[32,1024]{1,0:T(8,128)(2,1)S(1)}, bf16[32,1024]{1,0:T(8,128)(2,1)S(1)}, u32[]{:S(2)}, u32[]{:S(2)}) %collective-permute-start.21) | collective-permute-done | bytes 65568 | tf_op jit(solution)/shard_map/ppermute | solution.py:40
  31.7 2.2 %fetch.3.refs_8_ = bf16[2048,1024]{1,0:T(8,128)(2,1)S(1)} custom-call(bf16[2048,1024]{1,0:T(8,128)(2,1)} %weight_ref), custom_call_target="tpu_custom_call" | custom-call | bytes 8388608 | tf_op jit(solution)/shard_map/fetch/pallas_call | solution.py:246
  33.9 3.6 %collective-permute-done.20.refs_2_ = bf16[32,1024]{1,0:T(8,128)(2,1)S(1)} collective-permute-done((bf16[32,1024]{1,0:T(8,128)(2,1)S(1)}, bf16[32,1024]{1,0:T(8,128)(2,1)S(1)}, u32[]{:S(2)}, u32[]{:S(2)}) %collective-permute-start.20) | collective-permute-done | bytes 65568 | tf_op jit(solution)/shard_map/ppermute | solution.py:40
  38.6 1.3 lay.3
  40.4 1.5 %collective-permute-start.26 = (bf16[128,1024]{1,0:T(8,128)(2,1)}, bf16[128,1024]{1,0:T(8,128)(2,1)}, u32[]{:S(2)}, u32[]{:S(2)}) collective-permute-start(bf16[128,1024]{1,0:T(8,128)(2,1)} %lay.3), channel_id=1, source_target_pairs={{0,2},{1,3},{2,0},{3,1},{4,6},{5,7},{6,4},{7,5},{8,10},{9,11},{10,... | collective-permute-start | bytes 786440 | tf_op jit(solution)/shard_map/ppermute | solution.py:40
  41.9 3.9 %project.3 = (f32[512,256]{1,0:T(8,128)S(1)}, bf16[528,256]{1,0:T(8,128)(2,1)S(1)}, bf16[528,256]{1,0:T(8,128)(2,1)S(1)}, bf16[528,256]{1,0:T(8,128)(2,1)S(1)}) custom-call(s32[3]{0:T(128)S(1)} %pad_add_fusion.place_ref, bf16[128,1024]{1,0:T(8,128)(2,1)S(1)} %lay.2.refs_0_, bf16[128,1024]{1,0:T(8,128)(2,1)S(1)} %collective-permute-done.16.refs_1_, ...), custom_call_target="tpu_custom_call" | custom-call | flops 2147483648 | bytes 7864320 | tf_op jit(solution)/shard_map/project/pallas_call | solution.py:340
  45.8 2.4 %collective-permute-start.31 = (bf16[528,256]{1,0:T(8,128)(2,1)S(1)}, bf16[528,256]{1,0:T(8,128)(2,1)S(1)}, u32[]{:S(2)}, u32[]{:S(2)}) collective-permute-start(bf16[528,256]{1,0:T(8,128)(2,1)S(1)} %get-tuple-element.138), channel_id=1, source_target_pairs={{0,24},{1,25},{2,26},{3,27},{4,28},{5,29},{6,30},{7,31},{8,16},{9,... | collective-permute-start | bytes 811016 | tf_op jit(solution)/shard_map/ppermute | solution.py:40
  48.2 0.9 collective-permute-start.32
  49.1 1.2 collective-permute-start.33
  50.3 18.5 %conditional.2 = (f32[512,256]{1,0:T(8,128)S(1)}, bf16[528,256]{1,0:T(8,128)(2,1)}, bf16[528,256]{1,0:T(8,128)(2,1)}, bf16[528,256]{1,0:T(8,128)(2,1)}) conditional(s32[]{:T(128)} %convert_element_type.4, () %tuple.35, (bf16[128,1024]{1,0:T(8,128)(2,1)}, bf16[128,1024]{1,0:T(8,128)(2,1)}, bf16[128,1024]{1,0:T(8,128)(2,1)}, ...), branch_computations={%region_0.1_spmd, %region_1.2_spmd} | conditional | flops 2149842944 | bytes 23068824 | solution.py:213
  50.3 1.2 pad_maximum_fusion
  51.5 1.6 %collective-permute-start.4 = (bf16[128,1024]{1,0:T(8,128)(2,1)}, bf16[128,1024]{1,0:T(8,128)(2,1)S(1)}, u32[]{:S(2)}, u32[]{:S(2)}) collective-permute-start(bf16[128,1024]{1,0:T(8,128)(2,1)} %get-tuple-element.17.refs_0_), channel_id=1, source_target_pairs={{0,6},{1,7},{2,4},{3,5},{4,2},{5,3},{6,0},{7,1},{8,14},{9,15},{10,... | collective-permute-start | bytes 786440 | tf_op jit(solution)/shard_map/cond/branch_1_fun/ppermute | solution.py:40
  53.1 8.3 %collective-permute-done.4.refs_3_ = bf16[128,1024]{1,0:T(8,128)(2,1)S(1)} collective-permute-done((bf16[128,1024]{1,0:T(8,128)(2,1)}, bf16[128,1024]{1,0:T(8,128)(2,1)S(1)}, u32[]{:S(2)}, u32[]{:S(2)}) %collective-permute-start.4) | collective-permute-done | bytes 262176 | tf_op jit(solution)/shard_map/cond/branch_1_fun/ppermute | solution.py:40
  61.4 2.2 %fetch.2.refs_6_ = bf16[2048,1024]{1,0:T(8,128)(2,1)S(1)} custom-call(bf16[2048,1024]{1,0:T(8,128)(2,1)} %get-tuple-element.22.weight_ref), custom_call_target="tpu_custom_call" | custom-call | bytes 8388608 | tf_op jit(solution)/shard_map/cond/branch_1_fun/fetch/pallas_call | solution.py:246
  63.6 5.2 %project.2 = (f32[512,256]{1,0:T(8,128)S(1)}, bf16[528,256]{1,0:T(8,128)(2,1)}, bf16[528,256]{1,0:T(8,128)(2,1)}, bf16[528,256]{1,0:T(8,128)(2,1)}) custom-call(s32[3]{0:T(128)S(1)} %get-tuple-element.16.place_ref, bf16[128,1024]{1,0:T(8,128)(2,1)} %get-tuple-element.17.refs_0_, bf16[128,1024]{1,0:T(8,128)(2,1)} %get-tuple-element.18.refs_1_, ...), custom_call_target="tpu_custom_call" | custom-call | flops 2147483648 | bytes 7864320 | tf_op jit(solution)/shard_map/cond/branch_1_fun/project/pallas_call | solution.py:340
  68.8 0.9 collective-permute-start.28
  69.6 2.0 %collective-permute-start.29 = (bf16[528,256]{1,0:T(8,128)(2,1)}, bf16[528,256]{1,0:T(8,128)(2,1)S(1)}, u32[]{:S(2)}, u32[]{:S(2)}) collective-permute-start(bf16[528,256]{1,0:T(8,128)(2,1)} %get-tuple-element.135), channel_id=1, source_target_pairs={{0,16},{1,17},{2,18},{3,19},{4,20},{5,21},{6,22},{7,23},{8,24},{9,... | collective-permute-start | bytes 811016 | tf_op jit(solution)/shard_map/ppermute | solution.py:40
  71.6 1.5 %collective-permute-start.30 = (bf16[528,256]{1,0:T(8,128)(2,1)}, bf16[528,256]{1,0:T(8,128)(2,1)S(1)}, u32[]{:S(2)}, u32[]{:S(2)}) collective-permute-start(bf16[528,256]{1,0:T(8,128)(2,1)} %get-tuple-element.136), channel_id=1, source_target_pairs={{0,24},{1,25},{2,26},{3,27},{4,28},{5,29},{6,30},{7,31},{8,16},{9,... | collective-permute-start | bytes 811016 | tf_op jit(solution)/shard_map/ppermute | solution.py:40
  73.2 3.4 %normalize.2 = (f32[512,256]{1,0:T(8,128)S(1)}, bf16[512,256]{1,0:T(8,128)(2,1)S(1)}, f32[1,256]{1,0:T(1,128)S(1)}, f32[256,512]{1,0:T(8,128)}, f32[256,512]{1,0:T(8,128)}) custom-call(s32[3]{0:T(128)S(1)} %pad_add_fusion.place_ref, f32[512,256]{1,0:T(8,128)S(1)} %get-tuple-element.137.refs_0_, bf16[528,256]{1,0:T(8,128)(2,1)S(1)} %collective-permute-done.31.refs_1_, ...), custom_call_target="tpu_custom_call" | custom-call | flops 134217728 | bytes 3145728 | tf_op jit(solution)/shard_map/normalize/pallas_call | solution.py:420
  76.5 13.6 %conditional.3 = ((f32[16,384]{1,0:T(8,128)S(1)}, f32[16,384]{1,0:T(8,128)S(1)}, f32[16,384]{1,0:T(8,128)S(1)}, f32[16,384]{1,0:T(8,128)S(1)})) conditional(s32[]{:T(128)} %convert_element_type.4, () %tuple.38, (f32[256,512]{1,0:T(8,128)}, s32[3]{0:T(128)S(1)}, f32[256,512]{1,0:T(8,128)}) %tuple.39), branch_computations={%region_2.3_spmd, %region_3.4_spmd} | conditional | bytes 2834600 | solution.py:213
  76.6 2.1 %collective-permute-done.met_ref = f32[256,512]{1,0:T(8,128)S(1)} collective-permute-done((f32[256,512]{1,0:T(8,128)}, f32[256,512]{1,0:T(8,128)S(1)}, u32[]{:S(2)}, u32[]{:S(2)}) %collective-permute-start) | collective-permute-done | bytes 524320 | tf_op jit(solution)/shard_map/cond/branch_1_fun/ppermute | solution.py:40
  78.7 1.3 halve.2
  80.6 1.5 %collective-permute-start.2 = (bf16[80,384]{1,0:T(8,128)(2,1)S(1)}, bf16[80,384]{1,0:T(8,128)(2,1)S(1)}, u32[]{:S(2)}, u32[]{:S(2)}) collective-permute-start(bf16[80,384]{1,0:T(8,128)(2,1)S(1)} %get-tuple-element.34), channel_id=1, source_target_pairs={{0,4},{1,5},{2,6},{3,7},{4,0},{5,1},{6,2},{7,3},{8,12},{9,13},{10,... | collective-permute-start | bytes 184328 | tf_op jit(solution)/shard_map/cond/branch_1_fun/ppermute | solution.py:40
  82.1 2.2 %collective-permute-done.1.refs_1_ = bf16[80,384]{1,0:T(8,128)(2,1)S(1)} collective-permute-done((bf16[80,384]{1,0:T(8,128)(2,1)S(1)}, bf16[80,384]{1,0:T(8,128)(2,1)S(1)}, u32[]{:S(2)}, u32[]{:S(2)}) %collective-permute-start.1) | collective-permute-done | bytes 61472 | tf_op jit(solution)/shard_map/cond/branch_1_fun/ppermute | solution.py:40
  84.3 1.5 %collective-permute-start.3 = (bf16[80,384]{1,0:T(8,128)(2,1)S(1)}, bf16[80,384]{1,0:T(8,128)(2,1)S(1)}, u32[]{:S(2)}, u32[]{:S(2)}) collective-permute-start(bf16[80,384]{1,0:T(8,128)(2,1)S(1)} %get-tuple-element.35), channel_id=1, source_target_pairs={{0,6},{1,7},{2,4},{3,5},{4,2},{5,3},{6,0},{7,1},{8,14},{9,15},{10,... | collective-permute-start | bytes 184328 | tf_op jit(solution)/shard_map/cond/branch_1_fun/ppermute | solution.py:40
  85.8 3.6 %collective-permute-done.3.refs_3_ = bf16[80,384]{1,0:T(8,128)(2,1)S(1)} collective-permute-done((bf16[80,384]{1,0:T(8,128)(2,1)S(1)}, bf16[80,384]{1,0:T(8,128)(2,1)S(1)}, u32[]{:S(2)}, u32[]{:S(2)}) %collective-permute-start.3) | collective-permute-done | bytes 61472 | tf_op jit(solution)/shard_map/cond/branch_1_fun/ppermute | solution.py:40
  89.4 0.8 plane.1
  90.3 2.9 %collective-permute-start.35 = (f32[16,384]{1,0:T(8,128)S(1)}, f32[16,384]{1,0:T(8,128)S(1)}, u32[]{:S(2)}, u32[]{:S(2)}) collective-permute-start(f32[16,384]{1,0:T(8,128)S(1)} %get-tuple-element.145), channel_id=1, source_target_pairs={{0,16},{1,17},{2,18},{3,19},{4,20},{5,21},{6,22},{7,23},{8,24},{9,... | collective-permute-start | bytes 73736 | tf_op jit(solution)/shard_map/ppermute | solution.py:40
  93.1 1.5 %collective-permute-start.36 = (f32[16,384]{1,0:T(8,128)S(1)}, f32[16,384]{1,0:T(8,128)S(1)}, u32[]{:S(2)}, u32[]{:S(2)}) collective-permute-start(f32[16,384]{1,0:T(8,128)S(1)} %get-tuple-element.146), channel_id=1, source_target_pairs={{0,24},{1,25},{2,26},{3,27},{4,28},{5,29},{6,30},{7,31},{8,16},{9,... | collective-permute-start | bytes 73736 | tf_op jit(solution)/shard_map/ppermute | solution.py:40
  94.7 3.7 %collective-permute-done.35.refs_2_ = f32[16,384]{1,0:T(8,128)S(1)} collective-permute-done((f32[16,384]{1,0:T(8,128)S(1)}, f32[16,384]{1,0:T(8,128)S(1)}, u32[]{:S(2)}, u32[]{:S(2)}) %collective-permute-start.35) | collective-permute-done | bytes 24608 | tf_op jit(solution)/shard_map/ppermute | solution.py:40
  98.9 2.6 %normalize.3 = (f32[512,256]{1,0:T(8,128)S(1)}, bf16[512,256]{1,0:T(8,128)(2,1)S(1)}, f32[1,256]{1,0:T(1,128)S(1)}, f32[256,512]{1,0:T(8,128)S(1)}, f32[256,512]{1,0:T(8,128)S(1)}, /*index=5*/f32[1,256]{1,0:T(1,128)S(1)}) custom-call(s32[3]{0:T(128)S(1)} %pad_add_fusion.place_ref, f32[512,256]{1,0:T(8,128)S(1)} %get-tuple-element.147.refs_0_, ...), custom_call_target="tpu_custom_call" | custom-call | flops 134217728 | bytes 3145728 | tf_op jit(solution)/shard_map/normalize/pallas_call | solution.py:420
  101.6 1.9 %collective-permute-done.37.met_ref = f32[256,512]{1,0:T(8,128)S(1)} collective-permute-done((f32[256,512]{1,0:T(8,128)S(1)}, f32[256,512]{1,0:T(8,128)S(1)}, u32[]{:S(2)}, u32[]{:S(2)}) %collective-permute-start.37) | collective-permute-done | bytes 524320 | tf_op jit(solution)/shard_map/ppermute | solution.py:40
  103.5 0.8 halve.3
  105.6 2.3 %collective-permute-start.40 = (bf16[80,384]{1,0:T(8,128)(2,1)S(1)}, bf16[80,384]{1,0:T(8,128)(2,1)S(1)}, u32[]{:S(2)}, u32[]{:S(2)}) collective-permute-start(bf16[80,384]{1,0:T(8,128)(2,1)S(1)} %get-tuple-element.157), channel_id=1, source_target_pairs={{0,6},{1,7},{2,4},{3,5},{4,2},{5,3},{6,0},{7,1},{8,14},{9,15},{10,... | collective-permute-start | bytes 184328 | tf_op jit(solution)/shard_map/ppermute | solution.py:40
  108.6 1.2 collective-permute-done.39.refs_2_
  109.8 0.9 collective-permute-done.40.refs_3_
  110.7 0.8 code.1.refs_0_
  111.5 2.3 %collective-permute-start.43 = (bf16[96,384]{1,0:T(8,128)(2,1)S(1)}, bf16[96,384]{1,0:T(8,128)(2,1)S(1)}, u32[]{:S(2)}, u32[]{:S(2)}) collective-permute-start(bf16[96,384]{1,0:T(8,128)(2,1)S(1)} %code.1.refs_0_), channel_id=1, source_target_pairs={{0,24},{1,25},{2,26},{3,27},{4,28},{5,29},{6,30},{7,31},{8,16},{9,... | collective-permute-start | bytes 221192 | tf_op jit(solution)/shard_map/ppermute | solution.py:40
  113.9 2.1 %collective-permute-start.41 = (bf16[96,384]{1,0:T(8,128)(2,1)S(1)}, bf16[96,384]{1,0:T(8,128)(2,1)S(1)}, u32[]{:S(2)}, u32[]{:S(2)}) collective-permute-start(bf16[96,384]{1,0:T(8,128)(2,1)S(1)} %code.1.refs_0_), channel_id=1, source_target_pairs={{0,8},{1,9},{2,10},{3,11},{4,12},{5,13},{6,14},{7,15},{8,0},{9,1},... | collective-permute-start | bytes 221192 | tf_op jit(solution)/shard_map/ppermute | solution.py:40
  116.0 2.4 %collective-permute-done.43.refs_3_ = bf16[96,384]{1,0:T(8,128)(2,1)S(1)} collective-permute-done((bf16[96,384]{1,0:T(8,128)(2,1)S(1)}, bf16[96,384]{1,0:T(8,128)(2,1)S(1)}, u32[]{:S(2)}, u32[]{:S(2)}) %collective-permute-start.43) | collective-permute-done | bytes 73760 | tf_op jit(solution)/shard_map/ppermute | solution.py:40
  118.4 1.7 %collective-permute-done.42.refs_2_ = bf16[96,384]{1,0:T(8,128)(2,1)S(1)} collective-permute-done((bf16[96,384]{1,0:T(8,128)(2,1)S(1)}, bf16[96,384]{1,0:T(8,128)(2,1)S(1)}, u32[]{:S(2)}, u32[]{:S(2)}) %collective-permute-start.42) | collective-permute-done | bytes 73760 | tf_op jit(solution)/shard_map/ppermute | solution.py:40
  120.0 0.9 finish.1.refs_0_
  121.0 2.2 %collective-permute-start.46 = (bf16[128,384]{1,0:T(8,128)(2,1)S(1)}, bf16[128,384]{1,0:T(8,128)(2,1)S(1)}, u32[]{:S(2)}, u32[]{:S(2)}) collective-permute-start(bf16[128,384]{1,0:T(8,128)(2,1)S(1)} %finish.1.refs_0_), channel_id=1, source_target_pairs={{0,6},{1,7},{2,4},{3,5},{4,2},{5,3},{6,0},{7,1},{8,14},{9,15},{10,... | collective-permute-start | bytes 294920 | tf_op jit(solution)/shard_map/ppermute | solution.py:40
  124.5 2.9 %collective-permute-done.46.refs_3_ = bf16[128,384]{1,0:T(8,128)(2,1)S(1)} collective-permute-done((bf16[128,384]{1,0:T(8,128)(2,1)S(1)}, bf16[128,384]{1,0:T(8,128)(2,1)S(1)}, u32[]{:S(2)}, u32[]{:S(2)}) %collective-permute-start.46) | collective-permute-done | bytes 98336 | tf_op jit(solution)/shard_map/ppermute | solution.py:40
  127.4 0.7 collective-permute-done.45.refs_2_
  128.7 0.7 collective-permute-done.49.refs_6_
  129.7 2.2 %gradient.1 = (bf16[256,256]{1,0:T(8,128)(2,1)S(1)}, bf16[256,256]{1,0:T(8,128)(2,1)S(1)}, bf16[256,256]{1,0:T(8,128)(2,1)S(1)}, bf16[256,256]{1,0:T(8,128)(2,1)S(1)}, f32[1,1]{1,0:T(1,128)}) custom-call(s32[3]{0:T(128)S(1)} %pad_add_fusion.place_ref, bf16[128,384]{1,0:T(8,128)(2,1)S(1)} %finish.1.refs_0_, ...), custom_call_target="tpu_custom_call" | custom-call | tf_op jit(solution)/shard_map/gradient/pallas_call | solution.py:172
  132.0 1.8 %collective-permute-start.51 = (bf16[256,256]{1,0:T(8,128)(2,1)S(1)}, bf16[256,256]{1,0:T(8,128)(2,1)S(1)}, u32[]{:S(2)}, u32[]{:S(2)}) collective-permute-start(bf16[256,256]{1,0:T(8,128)(2,1)S(1)} %get-tuple-element.169), channel_id=1, source_target_pairs={{0,24},{1,25},{2,26},{3,27},{4,28},{5,29},{6,30},{7,31},{8,16},{9,... | collective-permute-start | bytes 393224 | tf_op jit(solution)/shard_map/ppermute | solution.py:40
  133.8 2.6 %collective-permute-start.53 = (bf16[256,256]{1,0:T(8,128)(2,1)S(1)}, bf16[256,256]{1,0:T(8,128)(2,1)S(1)}, u32[]{:S(2)}, u32[]{:S(2)}) collective-permute-start(bf16[256,256]{1,0:T(8,128)(2,1)S(1)} %get-tuple-element.171), channel_id=1, source_target_pairs={{0,8},{1,9},{2,10},{3,11},{4,12},{5,13},{6,14},{7,15},{8,0},{9,1},... | collective-permute-start | bytes 393224 | tf_op jit(solution)/shard_map/ppermute | solution.py:40
  136.3 3.9 %collective-permute-done.51.refs_1_ = bf16[256,256]{1,0:T(8,128)(2,1)S(1)} collective-permute-done((bf16[256,256]{1,0:T(8,128)(2,1)S(1)}, bf16[256,256]{1,0:T(8,128)(2,1)S(1)}, u32[]{:S(2)}, u32[]{:S(2)}) %collective-permute-start.51) | collective-permute-done | bytes 131104 | tf_op jit(solution)/shard_map/ppermute | solution.py:40
  140.2 5.4 %collective-permute-done.52.refs_2_ = bf16[256,256]{1,0:T(8,128)(2,1)S(1)} collective-permute-done((bf16[256,256]{1,0:T(8,128)(2,1)S(1)}, bf16[256,256]{1,0:T(8,128)(2,1)S(1)}, u32[]{:S(2)}, u32[]{:S(2)}) %collective-permute-start.52) | collective-permute-done | bytes 131104 | tf_op jit(solution)/shard_map/ppermute | solution.py:40
  145.7 1.4 place.1
  (68 shorter events, 11.7 us)
Async XLA Ops:
  1.6 9.0 %collective-permute-start.9 = (bf16[32,1024]{1,0:T(8,128)(2,1)S(1)}, bf16[32,1024]{1,0:T(8,128)(2,1)S(1)}, u32[]{:S(2)}, u32[]{:S(2)}) collective-permute-start(bf16[32,1024]{1,0:T(8,128)(2,1)S(1)} %get-tuple-element.187), channel_id=1, source_target_pairs={{0,2},{1,3},{2,0},{3,1},{4,6},{5,7},{6,4},{7,5},{8,10},{9,11},{10,... | collective-permute-start | bytes 196616 | tf_op jit(solution)/shard_map/ppermute | solution.py:40
  4.6 6.1 %collective-permute-start.8 = (bf16[32,1024]{1,0:T(8,128)(2,1)S(1)}, bf16[32,1024]{1,0:T(8,128)(2,1)S(1)}, u32[]{:S(2)}, u32[]{:S(2)}) collective-permute-start(bf16[32,1024]{1,0:T(8,128)(2,1)S(1)} %get-tuple-element.188), channel_id=1, source_target_pairs={{0,4},{1,5},{2,6},{3,7},{4,0},{5,1},{6,2},{7,3},{8,12},{9,13},{10,... | collective-permute-start | bytes 196616 | tf_op jit(solution)/shard_map/ppermute | solution.py:40
  6.1 5.2 %collective-permute-start.7 = (bf16[32,1024]{1,0:T(8,128)(2,1)S(1)}, bf16[32,1024]{1,0:T(8,128)(2,1)S(1)}, u32[]{:S(2)}, u32[]{:S(2)}) collective-permute-start(bf16[32,1024]{1,0:T(8,128)(2,1)S(1)} %get-tuple-element.189), channel_id=1, source_target_pairs={{0,6},{1,7},{2,4},{3,5},{4,2},{5,3},{6,0},{7,1},{8,14},{9,15},{10,... | collective-permute-start | bytes 196616 | tf_op jit(solution)/shard_map/ppermute | solution.py:40
  7.1 9.0 %collective-permute-start.15 = (bf16[32,1024]{1,0:T(8,128)(2,1)S(1)}, bf16[32,1024]{1,0:T(8,128)(2,1)S(1)}, u32[]{:S(2)}, u32[]{:S(2)}) collective-permute-start(bf16[32,1024]{1,0:T(8,128)(2,1)S(1)} %get-tuple-element.183), channel_id=1, source_target_pairs={{0,6},{1,7},{2,4},{3,5},{4,2},{5,3},{6,0},{7,1},{8,14},{9,15},{10,... | collective-permute-start | bytes 196616 | tf_op jit(solution)/shard_map/ppermute | solution.py:40
  10.1 6.7 %collective-permute-start.14 = (bf16[32,1024]{1,0:T(8,128)(2,1)S(1)}, bf16[32,1024]{1,0:T(8,128)(2,1)S(1)}, u32[]{:S(2)}, u32[]{:S(2)}) collective-permute-start(bf16[32,1024]{1,0:T(8,128)(2,1)S(1)} %get-tuple-element.184), channel_id=1, source_target_pairs={{0,4},{1,5},{2,6},{3,7},{4,0},{5,1},{6,2},{7,3},{8,12},{9,13},{10,... | collective-permute-start | bytes 196616 | tf_op jit(solution)/shard_map/ppermute | solution.py:40
  10.6 6.2 %collective-permute-start.13 = (bf16[32,1024]{1,0:T(8,128)(2,1)S(1)}, bf16[32,1024]{1,0:T(8,128)(2,1)S(1)}, u32[]{:S(2)}, u32[]{:S(2)}) collective-permute-start(bf16[32,1024]{1,0:T(8,128)(2,1)S(1)} %get-tuple-element.185), channel_id=1, source_target_pairs={{0,2},{1,3},{2,0},{3,1},{4,6},{5,7},{6,4},{7,5},{8,10},{9,11},{10,... | collective-permute-start | bytes 196616 | tf_op jit(solution)/shard_map/ppermute | solution.py:40
  12.2 6.2 %collective-permute-start.12 = (bf16[32,1024]{1,0:T(8,128)(2,1)S(1)}, bf16[32,1024]{1,0:T(8,128)(2,1)S(1)}, u32[]{:S(2)}, u32[]{:S(2)}) collective-permute-start(bf16[32,1024]{1,0:T(8,128)(2,1)S(1)} %get-tuple-element.175), channel_id=1, source_target_pairs={{0,24},{1,25},{2,26},{3,27},{4,28},{5,29},{6,30},{7,31},{8,16},{9,... | collective-permute-start | bytes 196616 | tf_op jit(solution)/shard_map/ppermute | solution.py:40
  16.0 4.4 %collective-permute-start.10 = (bf16[32,1024]{1,0:T(8,128)(2,1)S(1)}, bf16[32,1024]{1,0:T(8,128)(2,1)S(1)}, u32[]{:S(2)}, u32[]{:S(2)}) collective-permute-start(bf16[32,1024]{1,0:T(8,128)(2,1)S(1)} %get-tuple-element.176), channel_id=1, source_target_pairs={{0,8},{1,9},{2,10},{3,11},{4,12},{5,13},{6,14},{7,15},{8,0},{9,1},... | collective-permute-start | bytes 196616 | tf_op jit(solution)/shard_map/ppermute | solution.py:40
  16.1 5.2 %collective-permute-start.11 = (bf16[32,1024]{1,0:T(8,128)(2,1)S(1)}, bf16[32,1024]{1,0:T(8,128)(2,1)S(1)}, u32[]{:S(2)}, u32[]{:S(2)}) collective-permute-start(bf16[32,1024]{1,0:T(8,128)(2,1)S(1)} %get-tuple-element.177), channel_id=1, source_target_pairs={{0,16},{1,17},{2,18},{3,19},{4,20},{5,21},{6,22},{7,23},{8,24},{9,... | collective-permute-start | bytes 196616 | tf_op jit(solution)/shard_map/ppermute | solution.py:40
  21.8 15.7 %collective-permute-start.18 = (bf16[128,1024]{1,0:T(8,128)(2,1)S(1)}, bf16[128,1024]{1,0:T(8,128)(2,1)S(1)}, u32[]{:S(2)}, u32[]{:S(2)}) collective-permute-start(bf16[128,1024]{1,0:T(8,128)(2,1)S(1)} %lay.2.refs_0_), channel_id=1, source_target_pairs={{0,6},{1,7},{2,4},{3,5},{4,2},{5,3},{6,0},{7,1},{8,14},{9,15},{10,... | collective-permute-start | bytes 786440 | tf_op jit(solution)/shard_map/ppermute | solution.py:40
  23.9 13.6 %collective-permute-start.17 = (bf16[128,1024]{1,0:T(8,128)(2,1)S(1)}, bf16[128,1024]{1,0:T(8,128)(2,1)S(1)}, u32[]{:S(2)}, u32[]{:S(2)}) collective-permute-start(bf16[128,1024]{1,0:T(8,128)(2,1)S(1)} %lay.2.refs_0_), channel_id=1, source_target_pairs={{0,4},{1,5},{2,6},{3,7},{4,0},{5,1},{6,2},{7,3},{8,12},{9,13},{10,... | collective-permute-start | bytes 786440 | tf_op jit(solution)/shard_map/ppermute | solution.py:40
  24.4 13.1 %collective-permute-start.16 = (bf16[128,1024]{1,0:T(8,128)(2,1)S(1)}, bf16[128,1024]{1,0:T(8,128)(2,1)S(1)}, u32[]{:S(2)}, u32[]{:S(2)}) collective-permute-start(bf16[128,1024]{1,0:T(8,128)(2,1)S(1)} %lay.2.refs_0_), channel_id=1, source_target_pairs={{0,2},{1,3},{2,0},{3,1},{4,6},{5,7},{6,4},{7,5},{8,10},{9,11},{10,... | collective-permute-start | bytes 786440 | tf_op jit(solution)/shard_map/ppermute | solution.py:40
  25.4 6.3 %collective-permute-start.21 = (bf16[32,1024]{1,0:T(8,128)(2,1)S(1)}, bf16[32,1024]{1,0:T(8,128)(2,1)S(1)}, u32[]{:S(2)}, u32[]{:S(2)}) collective-permute-start(bf16[32,1024]{1,0:T(8,128)(2,1)S(1)} %get-tuple-element.179), channel_id=1, source_target_pairs={{0,24},{1,25},{2,26},{3,27},{4,28},{5,29},{6,30},{7,31},{8,16},{9,... | collective-permute-start | bytes 196616 | tf_op jit(solution)/shard_map/ppermute | solution.py:40
  27.0 6.8 %collective-permute-start.19 = (bf16[32,1024]{1,0:T(8,128)(2,1)S(1)}, bf16[32,1024]{1,0:T(8,128)(2,1)S(1)}, u32[]{:S(2)}, u32[]{:S(2)}) collective-permute-start(bf16[32,1024]{1,0:T(8,128)(2,1)S(1)} %get-tuple-element.181), channel_id=1, source_target_pairs={{0,8},{1,9},{2,10},{3,11},{4,12},{5,13},{6,14},{7,15},{8,0},{9,1},... | collective-permute-start | bytes 196616 | tf_op jit(solution)/shard_map/ppermute | solution.py:40
  31.7 5.9 %collective-permute-start.20 = (bf16[32,1024]{1,0:T(8,128)(2,1)S(1)}, bf16[32,1024]{1,0:T(8,128)(2,1)S(1)}, u32[]{:S(2)}, u32[]{:S(2)}) collective-permute-start(bf16[32,1024]{1,0:T(8,128)(2,1)S(1)} %get-tuple-element.182), channel_id=1, source_target_pairs={{0,16},{1,17},{2,18},{3,19},{4,20},{5,21},{6,22},{7,23},{8,24},{9,... | collective-permute-start | bytes 196616 | tf_op jit(solution)/shard_map/ppermute | solution.py:40
  37.5 2.9 %collective-permute-start.22 = (bf16[128,1024]{1,0:T(8,128)(2,1)S(1)}, bf16[128,1024]{1,0:T(8,128)(2,1)S(1)}, u32[]{:S(2)}, u32[]{:S(2)}) collective-permute-start(bf16[128,1024]{1,0:T(8,128)(2,1)S(1)} %lay.2.refs_0_), channel_id=1, source_target_pairs={{0,1},{1,0},{2,3},{3,2},{4,5},{5,4},{6,7},{7,6},{8,9},{9,8},{10,11... | collective-permute-start | bytes 786440 | tf_op jit(solution)/shard_map/ppermute | solution.py:40
  37.6 4.3 %collective-permute-start.23 = (bf16[128,1024]{1,0:T(8,128)(2,1)S(1)}, bf16[128,1024]{1,0:T(8,128)(2,1)S(1)}, u32[]{:S(2)}, u32[]{:S(2)}) collective-permute-start(bf16[128,1024]{1,0:T(8,128)(2,1)S(1)} %collective-permute-done.16.refs_1_), channel_id=1, source_target_pairs={{0,1},{1,0},{2,3},{3,2},{4,5},{5,4},{6,7},{7,6},{8,9},{9,8},{10,11... | collective-permute-start | bytes 786440 | tf_op jit(solution)/shard_map/ppermute | solution.py:40
  38.1 3.8 %collective-permute-start.24 = (bf16[128,1024]{1,0:T(8,128)(2,1)S(1)}, bf16[128,1024]{1,0:T(8,128)(2,1)S(1)}, u32[]{:S(2)}, u32[]{:S(2)}) collective-permute-start(bf16[128,1024]{1,0:T(8,128)(2,1)S(1)} %collective-permute-done.17.refs_2_), channel_id=1, source_target_pairs={{0,1},{1,0},{2,3},{3,2},{4,5},{5,4},{6,7},{7,6},{8,9},{9,8},{10,11... | collective-permute-start | bytes 786440 | tf_op jit(solution)/shard_map/ppermute | solution.py:40
  38.2 3.7 %collective-permute-start.25 = (bf16[128,1024]{1,0:T(8,128)(2,1)S(1)}, bf16[128,1024]{1,0:T(8,128)(2,1)S(1)}, u32[]{:S(2)}, u32[]{:S(2)}) collective-permute-start(bf16[128,1024]{1,0:T(8,128)(2,1)S(1)} %collective-permute-done.18.refs_3_), channel_id=1, source_target_pairs={{0,1},{1,0},{2,3},{3,2},{4,5},{5,4},{6,7},{7,6},{8,9},{9,8},{10,11... | collective-permute-start | bytes 786440 | tf_op jit(solution)/shard_map/ppermute | solution.py:40
  39.9 10.4 %collective-permute-start.27 = (bf16[128,1024]{1,0:T(8,128)(2,1)}, bf16[128,1024]{1,0:T(8,128)(2,1)}, u32[]{:S(2)}, u32[]{:S(2)}) collective-permute-start(bf16[128,1024]{1,0:T(8,128)(2,1)} %lay.3), channel_id=1, source_target_pairs={{0,4},{1,5},{2,6},{3,7},{4,0},{5,1},{6,2},{7,3},{8,12},{9,13},{10,... | collective-permute-start | bytes 786440 | tf_op jit(solution)/shard_map/ppermute | solution.py:40
  40.4 9.9 %collective-permute-start.26 = (bf16[128,1024]{1,0:T(8,128)(2,1)}, bf16[128,1024]{1,0:T(8,128)(2,1)}, u32[]{:S(2)}, u32[]{:S(2)}) collective-permute-start(bf16[128,1024]{1,0:T(8,128)(2,1)} %lay.3), channel_id=1, source_target_pairs={{0,2},{1,3},{2,0},{3,1},{4,6},{5,7},{6,4},{7,5},{8,10},{9,11},{10,... | collective-permute-start | bytes 786440 | tf_op jit(solution)/shard_map/ppermute | solution.py:40
  45.8 25.8 %collective-permute-start.31 = (bf16[528,256]{1,0:T(8,128)(2,1)S(1)}, bf16[528,256]{1,0:T(8,128)(2,1)S(1)}, u32[]{:S(2)}, u32[]{:S(2)}) collective-permute-start(bf16[528,256]{1,0:T(8,128)(2,1)S(1)} %get-tuple-element.138), channel_id=1, source_target_pairs={{0,24},{1,25},{2,26},{3,27},{4,28},{5,29},{6,30},{7,31},{8,16},{9,... | collective-permute-start | bytes 811016 | tf_op jit(solution)/shard_map/ppermute | solution.py:40
  48.2 24.9 %collective-permute-start.32 = (bf16[528,256]{1,0:T(8,128)(2,1)S(1)}, bf16[528,256]{1,0:T(8,128)(2,1)S(1)}, u32[]{:S(2)}, u32[]{:S(2)}) collective-permute-start(bf16[528,256]{1,0:T(8,128)(2,1)S(1)} %get-tuple-element.139), channel_id=1, source_target_pairs={{0,16},{1,17},{2,18},{3,19},{4,20},{5,21},{6,22},{7,23},{8,24},{9,... | collective-permute-start | bytes 811016 | tf_op jit(solution)/shard_map/ppermute | solution.py:40
  49.1 24.0 %collective-permute-start.33 = (bf16[528,256]{1,0:T(8,128)(2,1)S(1)}, bf16[528,256]{1,0:T(8,128)(2,1)S(1)}, u32[]{:S(2)}, u32[]{:S(2)}) collective-permute-start(bf16[528,256]{1,0:T(8,128)(2,1)S(1)} %get-tuple-element.140), channel_id=1, source_target_pairs={{0,8},{1,9},{2,10},{3,11},{4,12},{5,13},{6,14},{7,15},{8,0},{9,1},... | collective-permute-start | bytes 811016 | tf_op jit(solution)/shard_map/ppermute | solution.py:40
  51.4 9.9 %collective-permute-start.5 = (bf16[384,1024]{1,0:T(8,128)(2,1)S(1)}, bf16[384,1024]{1,0:T(8,128)(2,1)S(1)}, u32[]{:S(2)}, u32[]{:S(2)}) collective-permute-start(bf16[384,1024]{1,0:T(8,128)(2,1)S(1)} %pad_maximum_fusion), channel_id=1, source_target_pairs={{0,1},{1,0},{2,3},{3,2},{4,5},{5,4},{6,7},{7,6},{8,9},{9,8},{10,11... | collective-permute-start | bytes 2359304 | tf_op jit(solution)/shard_map/cond/branch_1_fun/ppermute | solution.py:40
  51.5 9.8 %collective-permute-start.4 = (bf16[128,1024]{1,0:T(8,128)(2,1)}, bf16[128,1024]{1,0:T(8,128)(2,1)S(1)}, u32[]{:S(2)}, u32[]{:S(2)}) collective-permute-start(bf16[128,1024]{1,0:T(8,128)(2,1)} %get-tuple-element.17.refs_0_), channel_id=1, source_target_pairs={{0,6},{1,7},{2,4},{3,5},{4,2},{5,3},{6,0},{7,1},{8,14},{9,15},{10,... | collective-permute-start | bytes 786440 | tf_op jit(solution)/shard_map/cond/branch_1_fun/ppermute | solution.py:40
  61.4 2.2 %collective-permute-start.6 = (bf16[128,1024]{1,0:T(8,128)(2,1)S(1)}, bf16[128,1024]{1,0:T(8,128)(2,1)S(1)}, u32[]{:S(2)}, u32[]{:S(2)}) collective-permute-start(bf16[128,1024]{1,0:T(8,128)(2,1)S(1)} %collective-permute-done.4.refs_3_), channel_id=1, source_target_pairs={{0,1},{1,0},{2,3},{3,2},{4,5},{5,4},{6,7},{7,6},{8,9},{9,8},{10,11... | collective-permute-start | bytes 786440 | tf_op jit(solution)/shard_map/cond/branch_1_fun/ppermute | solution.py:40
  68.8 24.4 %collective-permute-start.28 = (bf16[528,256]{1,0:T(8,128)(2,1)}, bf16[528,256]{1,0:T(8,128)(2,1)S(1)}, u32[]{:S(2)}, u32[]{:S(2)}) collective-permute-start(bf16[528,256]{1,0:T(8,128)(2,1)} %get-tuple-element.134), channel_id=1, source_target_pairs={{0,8},{1,9},{2,10},{3,11},{4,12},{5,13},{6,14},{7,15},{8,0},{9,1},... | collective-permute-start | bytes 811016 | tf_op jit(solution)/shard_map/ppermute | solution.py:40
  69.6 25.0 %collective-permute-start.29 = (bf16[528,256]{1,0:T(8,128)(2,1)}, bf16[528,256]{1,0:T(8,128)(2,1)S(1)}, u32[]{:S(2)}, u32[]{:S(2)}) collective-permute-start(bf16[528,256]{1,0:T(8,128)(2,1)} %get-tuple-element.135), channel_id=1, source_target_pairs={{0,16},{1,17},{2,18},{3,19},{4,20},{5,21},{6,22},{7,23},{8,24},{9,... | collective-permute-start | bytes 811016 | tf_op jit(solution)/shard_map/ppermute | solution.py:40
  71.6 23.0 %collective-permute-start.30 = (bf16[528,256]{1,0:T(8,128)(2,1)}, bf16[528,256]{1,0:T(8,128)(2,1)S(1)}, u32[]{:S(2)}, u32[]{:S(2)}) collective-permute-start(bf16[528,256]{1,0:T(8,128)(2,1)} %get-tuple-element.136), channel_id=1, source_target_pairs={{0,24},{1,25},{2,26},{3,27},{4,28},{5,29},{6,30},{7,31},{8,16},{9,... | collective-permute-start | bytes 811016 | tf_op jit(solution)/shard_map/ppermute | solution.py:40
  76.5 2.1 %collective-permute-start = (f32[256,512]{1,0:T(8,128)}, f32[256,512]{1,0:T(8,128)S(1)}, u32[]{:S(2)}, u32[]{:S(2)}) collective-permute-start(f32[256,512]{1,0:T(8,128)} %get-tuple-element.29), channel_id=1, source_target_pairs={{0,1},{1,0},{2,3},{3,2},{4,5},{5,4},{6,7},{7,6},{8,9},{9,8},{10,11... | collective-permute-start | bytes 1572872 | tf_op jit(solution)/shard_map/cond/branch_1_fun/ppermute | solution.py:40
  80.0 4.3 %collective-permute-start.1 = (bf16[80,384]{1,0:T(8,128)(2,1)S(1)}, bf16[80,384]{1,0:T(8,128)(2,1)S(1)}, u32[]{:S(2)}, u32[]{:S(2)}) collective-permute-start(bf16[80,384]{1,0:T(8,128)(2,1)S(1)} %get-tuple-element.31), channel_id=1, source_target_pairs={{0,2},{1,3},{2,0},{3,1},{4,6},{5,7},{6,4},{7,5},{8,10},{9,11},{10,... | collective-permute-start | bytes 184328 | tf_op jit(solution)/shard_map/cond/branch_1_fun/ppermute | solution.py:40
  80.6 5.2 %collective-permute-start.2 = (bf16[80,384]{1,0:T(8,128)(2,1)S(1)}, bf16[80,384]{1,0:T(8,128)(2,1)S(1)}, u32[]{:S(2)}, u32[]{:S(2)}) collective-permute-start(bf16[80,384]{1,0:T(8,128)(2,1)S(1)} %get-tuple-element.34), channel_id=1, source_target_pairs={{0,4},{1,5},{2,6},{3,7},{4,0},{5,1},{6,2},{7,3},{8,12},{9,13},{10,... | collective-permute-start | bytes 184328 | tf_op jit(solution)/shard_map/cond/branch_1_fun/ppermute | solution.py:40
  84.3 5.1 %collective-permute-start.3 = (bf16[80,384]{1,0:T(8,128)(2,1)S(1)}, bf16[80,384]{1,0:T(8,128)(2,1)S(1)}, u32[]{:S(2)}, u32[]{:S(2)}) collective-permute-start(bf16[80,384]{1,0:T(8,128)(2,1)S(1)} %get-tuple-element.35), channel_id=1, source_target_pairs={{0,6},{1,7},{2,4},{3,5},{4,2},{5,3},{6,0},{7,1},{8,14},{9,15},{10,... | collective-permute-start | bytes 184328 | tf_op jit(solution)/shard_map/cond/branch_1_fun/ppermute | solution.py:40
  90.2 4.5 %collective-permute-start.34 = (f32[16,384]{1,0:T(8,128)S(1)}, f32[16,384]{1,0:T(8,128)S(1)}, u32[]{:S(2)}, u32[]{:S(2)}) collective-permute-start(f32[16,384]{1,0:T(8,128)S(1)} %get-tuple-element.144), channel_id=1, source_target_pairs={{0,8},{1,9},{2,10},{3,11},{4,12},{5,13},{6,14},{7,15},{8,0},{9,1},... | collective-permute-start | bytes 73736 | tf_op jit(solution)/shard_map/ppermute | solution.py:40
  90.3 8.1 %collective-permute-start.35 = (f32[16,384]{1,0:T(8,128)S(1)}, f32[16,384]{1,0:T(8,128)S(1)}, u32[]{:S(2)}, u32[]{:S(2)}) collective-permute-start(f32[16,384]{1,0:T(8,128)S(1)} %get-tuple-element.145), channel_id=1, source_target_pairs={{0,16},{1,17},{2,18},{3,19},{4,20},{5,21},{6,22},{7,23},{8,24},{9,... | collective-permute-start | bytes 73736 | tf_op jit(solution)/shard_map/ppermute | solution.py:40
  93.1 5.7 %collective-permute-start.36 = (f32[16,384]{1,0:T(8,128)S(1)}, f32[16,384]{1,0:T(8,128)S(1)}, u32[]{:S(2)}, u32[]{:S(2)}) collective-permute-start(f32[16,384]{1,0:T(8,128)S(1)} %get-tuple-element.146), channel_id=1, source_target_pairs={{0,24},{1,25},{2,26},{3,27},{4,28},{5,29},{6,30},{7,31},{8,16},{9,... | collective-permute-start | bytes 73736 | tf_op jit(solution)/shard_map/ppermute | solution.py:40
  101.5 2.0 %collective-permute-start.37 = (f32[256,512]{1,0:T(8,128)S(1)}, f32[256,512]{1,0:T(8,128)S(1)}, u32[]{:S(2)}, u32[]{:S(2)}) collective-permute-start(f32[256,512]{1,0:T(8,128)S(1)} %get-tuple-element.153), channel_id=1, source_target_pairs={{0,1},{1,0},{2,3},{3,2},{4,5},{5,4},{6,7},{7,6},{8,9},{9,8},{10,11... | collective-permute-start | bytes 1572872 | tf_op jit(solution)/shard_map/ppermute | solution.py:40
  104.3 4.4 %collective-permute-start.38 = (bf16[80,384]{1,0:T(8,128)(2,1)S(1)}, bf16[80,384]{1,0:T(8,128)(2,1)S(1)}, u32[]{:S(2)}, u32[]{:S(2)}) collective-permute-start(bf16[80,384]{1,0:T(8,128)(2,1)S(1)} %get-tuple-element.155), channel_id=1, source_target_pairs={{0,2},{1,3},{2,0},{3,1},{4,6},{5,7},{6,4},{7,5},{8,10},{9,11},{10,... | collective-permute-start | bytes 184328 | tf_op jit(solution)/shard_map/ppermute | solution.py:40
  104.9 4.9 %collective-permute-start.39 = (bf16[80,384]{1,0:T(8,128)(2,1)S(1)}, bf16[80,384]{1,0:T(8,128)(2,1)S(1)}, u32[]{:S(2)}, u32[]{:S(2)}) collective-permute-start(bf16[80,384]{1,0:T(8,128)(2,1)S(1)} %get-tuple-element.156), channel_id=1, source_target_pairs={{0,4},{1,5},{2,6},{3,7},{4,0},{5,1},{6,2},{7,3},{8,12},{9,13},{10,... | collective-permute-start | bytes 184328 | tf_op jit(solution)/shard_map/ppermute | solution.py:40
  105.6 5.1 %collective-permute-start.40 = (bf16[80,384]{1,0:T(8,128)(2,1)S(1)}, bf16[80,384]{1,0:T(8,128)(2,1)S(1)}, u32[]{:S(2)}, u32[]{:S(2)}) collective-permute-start(bf16[80,384]{1,0:T(8,128)(2,1)S(1)} %get-tuple-element.157), channel_id=1, source_target_pairs={{0,6},{1,7},{2,4},{3,5},{4,2},{5,3},{6,0},{7,1},{8,14},{9,15},{10,... | collective-permute-start | bytes 184328 | tf_op jit(solution)/shard_map/ppermute | solution.py:40
  111.5 6.8 %collective-permute-start.43 = (bf16[96,384]{1,0:T(8,128)(2,1)S(1)}, bf16[96,384]{1,0:T(8,128)(2,1)S(1)}, u32[]{:S(2)}, u32[]{:S(2)}) collective-permute-start(bf16[96,384]{1,0:T(8,128)(2,1)S(1)} %code.1.refs_0_), channel_id=1, source_target_pairs={{0,24},{1,25},{2,26},{3,27},{4,28},{5,29},{6,30},{7,31},{8,16},{9,... | collective-permute-start | bytes 221192 | tf_op jit(solution)/shard_map/ppermute | solution.py:40
  113.8 6.2 %collective-permute-start.42 = (bf16[96,384]{1,0:T(8,128)(2,1)S(1)}, bf16[96,384]{1,0:T(8,128)(2,1)S(1)}, u32[]{:S(2)}, u32[]{:S(2)}) collective-permute-start(bf16[96,384]{1,0:T(8,128)(2,1)S(1)} %code.1.refs_0_), channel_id=1, source_target_pairs={{0,16},{1,17},{2,18},{3,19},{4,20},{5,21},{6,22},{7,23},{8,24},{9,... | collective-permute-start | bytes 221192 | tf_op jit(solution)/shard_map/ppermute | solution.py:40
  113.9 6.2 %collective-permute-start.41 = (bf16[96,384]{1,0:T(8,128)(2,1)S(1)}, bf16[96,384]{1,0:T(8,128)(2,1)S(1)}, u32[]{:S(2)}, u32[]{:S(2)}) collective-permute-start(bf16[96,384]{1,0:T(8,128)(2,1)S(1)} %code.1.refs_0_), channel_id=1, source_target_pairs={{0,8},{1,9},{2,10},{3,11},{4,12},{5,13},{6,14},{7,15},{8,0},{9,1},... | collective-permute-start | bytes 221192 | tf_op jit(solution)/shard_map/ppermute | solution.py:40
  121.0 6.4 %collective-permute-start.46 = (bf16[128,384]{1,0:T(8,128)(2,1)S(1)}, bf16[128,384]{1,0:T(8,128)(2,1)S(1)}, u32[]{:S(2)}, u32[]{:S(2)}) collective-permute-start(bf16[128,384]{1,0:T(8,128)(2,1)S(1)} %finish.1.refs_0_), channel_id=1, source_target_pairs={{0,6},{1,7},{2,4},{3,5},{4,2},{5,3},{6,0},{7,1},{8,14},{9,15},{10,... | collective-permute-start | bytes 294920 | tf_op jit(solution)/shard_map/ppermute | solution.py:40
  123.2 4.9 %collective-permute-start.45 = (bf16[128,384]{1,0:T(8,128)(2,1)S(1)}, bf16[128,384]{1,0:T(8,128)(2,1)S(1)}, u32[]{:S(2)}, u32[]{:S(2)}) collective-permute-start(bf16[128,384]{1,0:T(8,128)(2,1)S(1)} %finish.1.refs_0_), channel_id=1, source_target_pairs={{0,4},{1,5},{2,6},{3,7},{4,0},{5,1},{6,2},{7,3},{8,12},{9,13},{10,... | collective-permute-start | bytes 294920 | tf_op jit(solution)/shard_map/ppermute | solution.py:40
  123.8 4.6 %collective-permute-start.44 = (bf16[128,384]{1,0:T(8,128)(2,1)S(1)}, bf16[128,384]{1,0:T(8,128)(2,1)S(1)}, u32[]{:S(2)}, u32[]{:S(2)}) collective-permute-start(bf16[128,384]{1,0:T(8,128)(2,1)S(1)} %finish.1.refs_0_), channel_id=1, source_target_pairs={{0,2},{1,3},{2,0},{3,1},{4,6},{5,7},{6,4},{7,5},{8,10},{9,11},{10,... | collective-permute-start | bytes 294920 | tf_op jit(solution)/shard_map/ppermute | solution.py:40
  124.5 4.1 %collective-permute-start.47 = (bf16[128,384]{1,0:T(8,128)(2,1)S(1)}, bf16[128,384]{1,0:T(8,128)(2,1)S(1)}, u32[]{:S(2)}, u32[]{:S(2)}) collective-permute-start(bf16[128,384]{1,0:T(8,128)(2,1)S(1)} %finish.1.refs_0_), channel_id=1, source_target_pairs={{0,1},{1,0},{2,3},{3,2},{4,5},{5,4},{6,7},{7,6},{8,9},{9,8},{10,11... | collective-permute-start | bytes 294920 | tf_op jit(solution)/shard_map/ppermute | solution.py:40
  127.4 1.3 collective-permute-start.50
  128.1 1.3 collective-permute-start.49
  128.4 1.3 collective-permute-start.48
  132.0 8.3 %collective-permute-start.51 = (bf16[256,256]{1,0:T(8,128)(2,1)S(1)}, bf16[256,256]{1,0:T(8,128)(2,1)S(1)}, u32[]{:S(2)}, u32[]{:S(2)}) collective-permute-start(bf16[256,256]{1,0:T(8,128)(2,1)S(1)} %get-tuple-element.169), channel_id=1, source_target_pairs={{0,24},{1,25},{2,26},{3,27},{4,28},{5,29},{6,30},{7,31},{8,16},{9,... | collective-permute-start | bytes 393224 | tf_op jit(solution)/shard_map/ppermute | solution.py:40
  133.8 11.9 %collective-permute-start.52 = (bf16[256,256]{1,0:T(8,128)(2,1)S(1)}, bf16[256,256]{1,0:T(8,128)(2,1)S(1)}, u32[]{:S(2)}, u32[]{:S(2)}) collective-permute-start(bf16[256,256]{1,0:T(8,128)(2,1)S(1)} %get-tuple-element.170), channel_id=1, source_target_pairs={{0,16},{1,17},{2,18},{3,19},{4,20},{5,21},{6,22},{7,23},{8,24},{9,... | collective-permute-start | bytes 393224 | tf_op jit(solution)/shard_map/ppermute | solution.py:40
  133.8 11.9 %collective-permute-start.53 = (bf16[256,256]{1,0:T(8,128)(2,1)S(1)}, bf16[256,256]{1,0:T(8,128)(2,1)S(1)}, u32[]{:S(2)}, u32[]{:S(2)}) collective-permute-start(bf16[256,256]{1,0:T(8,128)(2,1)S(1)} %get-tuple-element.171), channel_id=1, source_target_pairs={{0,8},{1,9},{2,10},{3,11},{4,12},{5,13},{6,14},{7,15},{8,0},{9,1},... | collective-permute-start | bytes 393224 | tf_op jit(solution)/shard_map/ppermute | solution.py:40

commit v11 on v10

--- a/solution.py
+++ b/solution.py
@@ -354,7 +354,7 @@
     return own, parts[::-1]
 
 
-def normalize_kernel(place_ref, *refs, n, k, second):
+def normalize_kernel(place_ref, *refs, n, k, order, second):
     own_ref, parts = refs[0], refs[n - 1 : 0 : -1]
     refs = refs[n:]
     if second:
@@ -377,7 +377,7 @@
         normed = (block - mean) * scale
         for first in range(0, height, few):
             step, plane = divmod((i * height + first) // few, n)
-            at = pl.multiple_of(plane * rows + (place_ref[1] ^ step) * few, few)
+            at = pl.multiple_of(plane * rows + (place_ref[1] ^ order[step]) * few, few)
             norm_ref[pl.ds(at, few), :] = normed[first : first + few]
             packed_ref[pl.ds(at, few), :] = normed[first : first + few].astype(BF16)
     dims = (((1,), (1,)), ((), ()))
@@ -404,7 +404,7 @@
                 grams[i][size - 8 :, at : at + 128] = jnp.where(first, share, row)
 
 
-def normalize_parts(place, place_array, own, parts, other=None):
+def normalize_parts(place, place_array, own, parts, order, other=None):
     n, k = place.n, place.k
     batch, columns = own.shape
     second = other is not None
@@ -418,7 +418,7 @@
     args = [own, *parts[::-1]] + ([other] if second else [])
     space = pl.BlockSpec(memory_space=pltpu.VMEM)
     return pl.pallas_call(
-        functools.partial(normalize_kernel, n=n, k=k, second=second),
+        functools.partial(normalize_kernel, n=n, k=k, order=order, second=second),
         in_specs=[pl.BlockSpec(memory_space=pltpu.SMEM)] + [space] * len(args),
         out_specs=[space] * len(out_shape),
         out_shape=out_shape,
@@ -524,26 +524,29 @@
     own_1, parts_1 = project(place, place_array, [met_1, [swapped(part) for part in met_1]], held)
     second = lay(place, place_array, second)
     size, here, toward = place.along("a")
-    met_2 = [second] + [place.send(second, toward(step)) for step in range(1, size - 1)]
+    order_2 = [0, size - 1, *range(1, size - 1)]
+    last = place.send(second, toward(size - 1))
     own_1, parts_1, late_weight = lax.optimization_barrier((own_1, parts_1, weight))
     parts_1 = sent(parts_1)
 
-    def second_projected(weight, *met):
-        last = place.send(met[0], toward(size - 1))
-        others = [swapped(jnp.concatenate(met, 0))]
-        last, others = lax.optimization_barrier((last, others))
-        others.append(swapped(last))
-        return project(place, place_array, [[*met, last], others], fetch(weight))
-
-    own_2, parts_2 = in_one(place, second_projected, (late_weight, *met_2))
+    def second_projected(weight, values, last):
+        met = [place.send(values, toward(step)) for step in range(1, size - 1)]
+        values, met[0] = lax.optimization_barrier((values, met[0]))
+        early = swapped(jnp.concatenate([values, last], 0))
+        late = swapped(jnp.concatenate(met, 0))
+        return project(place, place_array, [[values, last, *met], [early, late]], fetch(weight))
+
+    own_2, parts_2 = in_one(place, second_projected, (late_weight, second, last))
     own_1, own_2 = lax.optimization_barrier((own_1, own_2))
     parts_2 = sent(parts_2)
-    norm_1, packed_1, scale_1, *grams = normalize_parts(place, place_array, own_1, parts_1)
+    norm_1, packed_1, scale_1, *grams = normalize_parts(
+        place, place_array, own_1, parts_1, [*range(n)]
+    )
     met_1 = in_one(place, lambda *grams: first_rows(place, place_array, grams), grams)
     met_1 = sends(place, "z", met_1)
     own_2, parts_2, met_1 = lax.optimization_barrier((own_2, parts_2, met_1))
     norm_2, packed_2, scale_2, *grams, coeff = normalize_parts(
-        place, place_array, own_2, parts_2, norm_1
+        place, place_array, own_2, parts_2, order_2, norm_1
     )
     height, batch = met_1[0].shape
     (rows_1,) = local(rows_kernel, place_array, met_1, [((height, batch), BF16)], "rows")

time: 147 us -> 146 us (level)
  waiting for transfers between devices: 55.8 us -> 54.3 us
    ppermute x54, waiting for transfers between devices: 55.8 us -> 54.3 us  [send(): return lax.ppermute(value, ('dp', 'mp'), pairs)]
where the time goes in v11:
time: 146 us; the launch traced here: 145 us
  starting transfers between devices  56.9 us (39%)
  waiting for transfers between devices  54.3 us (37%)
  Pallas kernels  29.3 us (20%)
  other arithmetic  2.02 us (1%)
  local copies, waits for them, and re-layouts  1.88 us (1%)
    ppermute x54, starting transfers between devices, send(): return lax.ppermute(value, ('dp', 'mp'), pairs)  56.9 us
    ppermute x54, waiting for transfers between devices, send(): return lax.ppermute(value, ('dp', 'mp'), pairs)  54.3 us
    pallas_call x10, Pallas kernels, local(): pl.pallas_call(kernel, in_specs=[pl.BlockSpec(memory_space=pltpu.SMEM)] +...  9.98 us
    pallas_call x2, Pallas kernels, project(): pl.pallas_call(functools.partial(project_kernel, counts=counts, n=n, k=k)...  8.94 us
    pallas_call x2, Pallas kernels, normalize_parts(): pl.pallas_call(functools.partial(normalize_kernel, n=n, k=k, order=order,...  6 us
    pallas_call x2, Pallas kernels, fetch(): pl.pallas_call(fetch_kernel, in_specs=[pl.BlockSpec(memory_space=pl.ANY)]...  4.39 us
  transfers between devices with their start and end apart: 54, of which 25 were waited for; matrix products, arithmetic and copies ran while one was open for 2% of the time, Pallas kernels for 14%

profile of v11, /device:TPU:0, one launch (start us, length us, event | category | flops | bytes accessed | tf_op | source)
XLA Modules:
  0.0 145.2 jit_solution(3084581369904217007)
XLA Ops:
  0.7 0.9 dynamic-slice_bitcast_fusion.4
  1.6 3.0 %collective-permute-start.10 = (bf16[32,1024]{1,0:T(8,128)(2,1)S(1)}, bf16[32,1024]{1,0:T(8,128)(2,1)S(1)}, u32[]{:S(2)}, u32[]{:S(2)}) collective-permute-start(bf16[32,1024]{1,0:T(8,128)(2,1)S(1)} %get-tuple-element.184), channel_id=1, source_target_pairs={{0,2},{1,3},{2,0},{3,1},{4,6},{5,7},{6,4},{7,5},{8,10},{9,11},{10,... | collective-permute-start | bytes 196616 | tf_op jit(solution)/shard_map/ppermute | solution.py:40
  4.6 1.5 %collective-permute-start.9 = (bf16[32,1024]{1,0:T(8,128)(2,1)S(1)}, bf16[32,1024]{1,0:T(8,128)(2,1)S(1)}, u32[]{:S(2)}, u32[]{:S(2)}) collective-permute-start(bf16[32,1024]{1,0:T(8,128)(2,1)S(1)} %get-tuple-element.185), channel_id=1, source_target_pairs={{0,4},{1,5},{2,6},{3,7},{4,0},{5,1},{6,2},{7,3},{8,12},{9,13},{10,... | collective-permute-start | bytes 196616 | tf_op jit(solution)/shard_map/ppermute | solution.py:40
  6.1 1.0 dynamic-slice_bitcast_fusion
  7.1 3.0 %collective-permute-start.16 = (bf16[32,1024]{1,0:T(8,128)(2,1)S(1)}, bf16[32,1024]{1,0:T(8,128)(2,1)S(1)}, u32[]{:S(2)}, u32[]{:S(2)}) collective-permute-start(bf16[32,1024]{1,0:T(8,128)(2,1)S(1)} %get-tuple-element.180), channel_id=1, source_target_pairs={{0,6},{1,7},{2,4},{3,5},{4,2},{5,3},{6,0},{7,1},{8,14},{9,15},{10,... | collective-permute-start | bytes 196616 | tf_op jit(solution)/shard_map/ppermute | solution.py:40
  11.3 0.9 broadcast_select_fusion.10
  12.2 3.9 %collective-permute-start.13 = (bf16[32,1024]{1,0:T(8,128)(2,1)S(1)}, bf16[32,1024]{1,0:T(8,128)(2,1)S(1)}, u32[]{:S(2)}, u32[]{:S(2)}) collective-permute-start(bf16[32,1024]{1,0:T(8,128)(2,1)S(1)} %get-tuple-element.172), channel_id=1, source_target_pairs={{0,24},{1,25},{2,26},{3,27},{4,28},{5,29},{6,30},{7,31},{8,16},{9,... | collective-permute-start | bytes 196616 | tf_op jit(solution)/shard_map/ppermute | solution.py:40
  16.8 1.6 %collective-permute-done.13.refs_3_ = bf16[32,1024]{1,0:T(8,128)(2,1)S(1)} collective-permute-done((bf16[32,1024]{1,0:T(8,128)(2,1)S(1)}, bf16[32,1024]{1,0:T(8,128)(2,1)S(1)}, u32[]{:S(2)}, u32[]{:S(2)}) %collective-permute-start.13) | collective-permute-done | bytes 65568 | tf_op jit(solution)/shard_map/ppermute | solution.py:40
  18.4 2.1 %collective-permute-done.11.refs_1_ = bf16[32,1024]{1,0:T(8,128)(2,1)S(1)} collective-permute-done((bf16[32,1024]{1,0:T(8,128)(2,1)S(1)}, bf16[32,1024]{1,0:T(8,128)(2,1)S(1)}, u32[]{:S(2)}, u32[]{:S(2)}) %collective-permute-start.11) | collective-permute-done | bytes 65568 | tf_op jit(solution)/shard_map/ppermute | solution.py:40
  21.8 2.1 %collective-permute-start.19 = (bf16[128,1024]{1,0:T(8,128)(2,1)S(1)}, bf16[128,1024]{1,0:T(8,128)(2,1)S(1)}, u32[]{:S(2)}, u32[]{:S(2)}) collective-permute-start(bf16[128,1024]{1,0:T(8,128)(2,1)S(1)} %lay.2.refs_0_), channel_id=1, source_target_pairs={{0,6},{1,7},{2,4},{3,5},{4,2},{5,3},{6,0},{7,1},{8,14},{9,15},{10,... | collective-permute-start | bytes 786440 | tf_op jit(solution)/shard_map/ppermute | solution.py:40
  24.4 0.9 collective-permute-start.17
  25.4 1.7 %collective-permute-start.22 = (bf16[32,1024]{1,0:T(8,128)(2,1)S(1)}, bf16[32,1024]{1,0:T(8,128)(2,1)S(1)}, u32[]{:S(2)}, u32[]{:S(2)}) collective-permute-start(bf16[32,1024]{1,0:T(8,128)(2,1)S(1)} %get-tuple-element.176), channel_id=1, source_target_pairs={{0,24},{1,25},{2,26},{3,27},{4,28},{5,29},{6,30},{7,31},{8,16},{9,... | collective-permute-start | bytes 196616 | tf_op jit(solution)/shard_map/ppermute | solution.py:40
  27.5 4.1 %collective-permute-done.22.refs_3_ = bf16[32,1024]{1,0:T(8,128)(2,1)S(1)} collective-permute-done((bf16[32,1024]{1,0:T(8,128)(2,1)S(1)}, bf16[32,1024]{1,0:T(8,128)(2,1)S(1)}, u32[]{:S(2)}, u32[]{:S(2)}) %collective-permute-start.22) | collective-permute-done | bytes 65568 | tf_op jit(solution)/shard_map/ppermute | solution.py:40
  31.7 2.2 %fetch.3.refs_8_ = bf16[2048,1024]{1,0:T(8,128)(2,1)S(1)} custom-call(bf16[2048,1024]{1,0:T(8,128)(2,1)} %weight_ref), custom_call_target="tpu_custom_call" | custom-call | bytes 8388608 | tf_op jit(solution)/shard_map/fetch/pallas_call | solution.py:246
  33.9 3.6 %collective-permute-done.21.refs_2_ = bf16[32,1024]{1,0:T(8,128)(2,1)S(1)} collective-permute-done((bf16[32,1024]{1,0:T(8,128)(2,1)S(1)}, bf16[32,1024]{1,0:T(8,128)(2,1)S(1)}, u32[]{:S(2)}, u32[]{:S(2)}) %collective-permute-start.21) | collective-permute-done | bytes 65568 | tf_op jit(solution)/shard_map/ppermute | solution.py:40
  39.2 1.5 %collective-permute-start.27 = (bf16[128,1024]{1,0:T(8,128)(2,1)S(1)}, bf16[128,1024]{1,0:T(8,128)(2,1)}, u32[]{:S(2)}, u32[]{:S(2)}) collective-permute-start(bf16[128,1024]{1,0:T(8,128)(2,1)S(1)} %lay.3), channel_id=1, source_target_pairs={{0,6},{1,7},{2,4},{3,5},{4,2},{5,3},{6,0},{7,1},{8,14},{9,15},{10,... | collective-permute-start | bytes 786440 | tf_op jit(solution)/shard_map/ppermute | solution.py:40
  40.7 3.9 %project.3 = (f32[512,256]{1,0:T(8,128)S(1)}, bf16[528,256]{1,0:T(8,128)(2,1)S(1)}, bf16[528,256]{1,0:T(8,128)(2,1)S(1)}, bf16[528,256]{1,0:T(8,128)(2,1)S(1)}) custom-call(s32[3]{0:T(128)S(1)} %pad_add_fusion.place_ref, bf16[128,1024]{1,0:T(8,128)(2,1)S(1)} %lay.2.refs_0_, bf16[128,1024]{1,0:T(8,128)(2,1)S(1)} %collective-permute-done.17.refs_1_, ...), custom_call_target="tpu_custom_call" | custom-call | flops 2147483648 | bytes 7864320 | tf_op jit(solution)/shard_map/project/pallas_call | solution.py:340
  44.7 2.4 %collective-permute-start.31 = (bf16[528,256]{1,0:T(8,128)(2,1)S(1)}, bf16[528,256]{1,0:T(8,128)(2,1)S(1)}, u32[]{:S(2)}, u32[]{:S(2)}) collective-permute-start(bf16[528,256]{1,0:T(8,128)(2,1)S(1)} %get-tuple-element.135), channel_id=1, source_target_pairs={{0,24},{1,25},{2,26},{3,27},{4,28},{5,29},{6,30},{7,31},{8,16},{9,... | collective-permute-start | bytes 811016 | tf_op jit(solution)/shard_map/ppermute | solution.py:40
  47.0 0.9 collective-permute-start.32
  47.9 1.2 collective-permute-start.33
  49.1 16.4 %conditional.2 = (f32[512,256]{1,0:T(8,128)S(1)}, bf16[528,256]{1,0:T(8,128)(2,1)}, bf16[528,256]{1,0:T(8,128)(2,1)}, bf16[528,256]{1,0:T(8,128)(2,1)}) conditional(s32[]{:T(128)} %convert_element_type.4, () %tuple.35, (bf16[128,1024]{1,0:T(8,128)(2,1)S(1)}, bf16[128,1024]{1,0:T(8,128)(2,1)}, bf16[2048,1024]{1,0:T(8,128)(2,1)}, s32[3]{0:T(128)S(1)}) %tuple.36), branch_computations={%region_0.1_spmd, %region_1.2_spmd} | conditional | flops 2149580800 | bytes 24641728 | solution.py:213
  49.6 1.5 %collective-permute-start.5 = (bf16[128,1024]{1,0:T(8,128)(2,1)S(1)}, bf16[128,1024]{1,0:T(8,128)(2,1)S(1)}, u32[]{:S(2)}, u32[]{:S(2)}) collective-permute-start(bf16[128,1024]{1,0:T(8,128)(2,1)S(1)} %get-tuple-element.16.refs_0_), channel_id=1, source_target_pairs={{0,4},{1,5},{2,6},{3,7},{4,0},{5,1},{6,2},{7,3},{8,12},{9,13},{10,... | collective-permute-start | bytes 786440 | tf_op jit(solution)/shard_map/cond/branch_1_fun/ppermute | solution.py:40
  51.2 5.1 %collective-permute-done.4.refs_2_ = bf16[128,1024]{1,0:T(8,128)(2,1)S(1)} collective-permute-done((bf16[128,1024]{1,0:T(8,128)(2,1)S(1)}, bf16[128,1024]{1,0:T(8,128)(2,1)S(1)}, u32[]{:S(2)}, u32[]{:S(2)}) %collective-permute-start.4) | collective-permute-done | bytes 262176 | tf_op jit(solution)/shard_map/cond/branch_1_fun/ppermute | solution.py:40
  56.6 1.0 pad_maximum_fusion
  58.2 2.2 %fetch.2.refs_6_ = bf16[2048,1024]{1,0:T(8,128)(2,1)S(1)} custom-call(bf16[2048,1024]{1,0:T(8,128)(2,1)} %get-tuple-element.19.weight_ref), custom_call_target="tpu_custom_call" | custom-call | bytes 8388608 | tf_op jit(solution)/shard_map/cond/branch_1_fun/fetch/pallas_call | solution.py:246
  60.4 5.0 %project.2 = (f32[512,256]{1,0:T(8,128)S(1)}, bf16[528,256]{1,0:T(8,128)(2,1)}, bf16[528,256]{1,0:T(8,128)(2,1)}, bf16[528,256]{1,0:T(8,128)(2,1)}) custom-call(s32[3]{0:T(128)S(1)} %get-tuple-element.14.place_ref, bf16[128,1024]{1,0:T(8,128)(2,1)S(1)} %get-tuple-element.16.refs_0_, bf16[128,1024]{1,0:T(8,128)(2,1)} %get-tuple-element.17.refs_1_, ...), custom_call_target="tpu_custom_call" | custom-call | flops 2147483648 | bytes 7864320 | tf_op jit(solution)/shard_map/cond/branch_1_fun/project/pallas_call | solution.py:340
  65.5 1.4 collective-permute-start.28
  66.9 1.4 collective-permute-start.29
  68.3 1.5 %collective-permute-start.30 = (bf16[528,256]{1,0:T(8,128)(2,1)}, bf16[528,256]{1,0:T(8,128)(2,1)S(1)}, u32[]{:S(2)}, u32[]{:S(2)}) collective-permute-start(bf16[528,256]{1,0:T(8,128)(2,1)} %get-tuple-element.133), channel_id=1, source_target_pairs={{0,24},{1,25},{2,26},{3,27},{4,28},{5,29},{6,30},{7,31},{8,16},{9,... | collective-permute-start | bytes 811016 | tf_op jit(solution)/shard_map/ppermute | solution.py:40
  69.9 2.4 %collective-permute-done.32.refs_2_ = bf16[528,256]{1,0:T(8,128)(2,1)S(1)} collective-permute-done((bf16[528,256]{1,0:T(8,128)(2,1)S(1)}, bf16[528,256]{1,0:T(8,128)(2,1)S(1)}, u32[]{:S(2)}, u32[]{:S(2)}) %collective-permute-start.32) | collective-permute-done | bytes 270368 | tf_op jit(solution)/shard_map/ppermute | solution.py:40
  72.3 3.4 %normalize.2 = (f32[512,256]{1,0:T(8,128)S(1)}, bf16[512,256]{1,0:T(8,128)(2,1)S(1)}, f32[1,256]{1,0:T(1,128)S(1)}, f32[256,512]{1,0:T(8,128)}, f32[256,512]{1,0:T(8,128)}) custom-call(s32[3]{0:T(128)S(1)} %pad_add_fusion.place_ref, f32[512,256]{1,0:T(8,128)S(1)} %get-tuple-element.134.refs_0_, bf16[528,256]{1,0:T(8,128)(2,1)S(1)} %collective-permute-done.31.refs_1_, ...), custom_call_target="tpu_custom_call" | custom-call | flops 134217728 | bytes 3145728 | tf_op jit(solution)/shard_map/normalize/pallas_call | solution.py:420
  75.7 13.6 %conditional.3 = ((f32[16,384]{1,0:T(8,128)S(1)}, f32[16,384]{1,0:T(8,128)S(1)}, f32[16,384]{1,0:T(8,128)S(1)}, f32[16,384]{1,0:T(8,128)S(1)})) conditional(s32[]{:T(128)} %convert_element_type.4, () %tuple.38, (f32[256,512]{1,0:T(8,128)}, s32[3]{0:T(128)S(1)}, f32[256,512]{1,0:T(8,128)}) %tuple.39), branch_computations={%region_2.3_spmd, %region_3.4_spmd} | conditional | bytes 2834600 | solution.py:213
  75.7 2.1 %collective-permute-done.met_ref = f32[256,512]{1,0:T(8,128)S(1)} collective-permute-done((f32[256,512]{1,0:T(8,128)}, f32[256,512]{1,0:T(8,128)S(1)}, u32[]{:S(2)}, u32[]{:S(2)}) %collective-permute-start) | collective-permute-done | bytes 524320 | tf_op jit(solution)/shard_map/cond/branch_1_fun/ppermute | solution.py:40
  77.8 1.3 halve.2
  79.7 1.4 collective-permute-start.2
  81.1 2.3 %collective-permute-done.1.refs_1_ = bf16[80,384]{1,0:T(8,128)(2,1)S(1)} collective-permute-done((bf16[80,384]{1,0:T(8,128)(2,1)S(1)}, bf16[80,384]{1,0:T(8,128)(2,1)S(1)}, u32[]{:S(2)}, u32[]{:S(2)}) %collective-permute-start.1) | collective-permute-done | bytes 61472 | tf_op jit(solution)/shard_map/cond/branch_1_fun/ppermute | solution.py:40
  83.4 1.4 collective-permute-start.3
  84.8 3.7 %collective-permute-done.3.refs_3_ = bf16[80,384]{1,0:T(8,128)(2,1)S(1)} collective-permute-done((bf16[80,384]{1,0:T(8,128)(2,1)S(1)}, bf16[80,384]{1,0:T(8,128)(2,1)S(1)}, u32[]{:S(2)}, u32[]{:S(2)}) %collective-permute-start.3) | collective-permute-done | bytes 61472 | tf_op jit(solution)/shard_map/cond/branch_1_fun/ppermute | solution.py:40
  88.5 0.8 plane.1
  89.4 1.9 %collective-permute-start.35 = (f32[16,384]{1,0:T(8,128)S(1)}, f32[16,384]{1,0:T(8,128)S(1)}, u32[]{:S(2)}, u32[]{:S(2)}) collective-permute-start(f32[16,384]{1,0:T(8,128)S(1)} %get-tuple-element.142), channel_id=1, source_target_pairs={{0,16},{1,17},{2,18},{3,19},{4,20},{5,21},{6,22},{7,23},{8,24},{9,... | collective-permute-start | bytes 73736 | tf_op jit(solution)/shard_map/ppermute | solution.py:40
  91.3 2.5 %collective-permute-start.36 = (f32[16,384]{1,0:T(8,128)S(1)}, f32[16,384]{1,0:T(8,128)S(1)}, u32[]{:S(2)}, u32[]{:S(2)}) collective-permute-start(f32[16,384]{1,0:T(8,128)S(1)} %get-tuple-element.143), channel_id=1, source_target_pairs={{0,24},{1,25},{2,26},{3,27},{4,28},{5,29},{6,30},{7,31},{8,16},{9,... | collective-permute-start | bytes 73736 | tf_op jit(solution)/shard_map/ppermute | solution.py:40
  93.8 2.5 %collective-permute-done.35.refs_2_ = f32[16,384]{1,0:T(8,128)S(1)} collective-permute-done((f32[16,384]{1,0:T(8,128)S(1)}, f32[16,384]{1,0:T(8,128)S(1)}, u32[]{:S(2)}, u32[]{:S(2)}) %collective-permute-start.35) | collective-permute-done | bytes 24608 | tf_op jit(solution)/shard_map/ppermute | solution.py:40
  96.9 2.6 %normalize.3 = (f32[512,256]{1,0:T(8,128)S(1)}, bf16[512,256]{1,0:T(8,128)(2,1)S(1)}, f32[1,256]{1,0:T(1,128)S(1)}, f32[256,512]{1,0:T(8,128)S(1)}, f32[256,512]{1,0:T(8,128)S(1)}, /*index=5*/f32[1,256]{1,0:T(1,128)S(1)}) custom-call(s32[3]{0:T(128)S(1)} %pad_add_fusion.place_ref, f32[512,256]{1,0:T(8,128)S(1)} %get-tuple-element.144.refs_0_, ...), custom_call_target="tpu_custom_call" | custom-call | flops 134217728 | bytes 3145728 | tf_op jit(solution)/shard_map/normalize/pallas_call | solution.py:420
  99.6 1.9 %collective-permute-done.37.met_ref = f32[256,512]{1,0:T(8,128)S(1)} collective-permute-done((f32[256,512]{1,0:T(8,128)S(1)}, f32[256,512]{1,0:T(8,128)S(1)}, u32[]{:S(2)}, u32[]{:S(2)}) %collective-permute-start.37) | collective-permute-done | bytes 524320 | tf_op jit(solution)/shard_map/ppermute | solution.py:40
  101.5 0.8 halve.3
  102.6 1.4 collective-permute-start.39
  104.0 1.9 %collective-permute-start.40 = (bf16[80,384]{1,0:T(8,128)(2,1)S(1)}, bf16[80,384]{1,0:T(8,128)(2,1)S(1)}, u32[]{:S(2)}, u32[]{:S(2)}) collective-permute-start(bf16[80,384]{1,0:T(8,128)(2,1)S(1)} %get-tuple-element.154), channel_id=1, source_target_pairs={{0,6},{1,7},{2,4},{3,5},{4,2},{5,3},{6,0},{7,1},{8,14},{9,15},{10,... | collective-permute-start | bytes 184328 | tf_op jit(solution)/shard_map/ppermute | solution.py:40
  106.9 2.2 %collective-permute-done.40.refs_3_ = bf16[80,384]{1,0:T(8,128)(2,1)S(1)} collective-permute-done((bf16[80,384]{1,0:T(8,128)(2,1)S(1)}, bf16[80,384]{1,0:T(8,128)(2,1)S(1)}, u32[]{:S(2)}, u32[]{:S(2)}) %collective-permute-start.40) | collective-permute-done | bytes 61472 | tf_op jit(solution)/shard_map/ppermute | solution.py:40
  109.1 0.8 code.1.refs_0_
  109.9 2.9 %collective-permute-start.43 = (bf16[96,384]{1,0:T(8,128)(2,1)S(1)}, bf16[96,384]{1,0:T(8,128)(2,1)S(1)}, u32[]{:S(2)}, u32[]{:S(2)}) collective-permute-start(bf16[96,384]{1,0:T(8,128)(2,1)S(1)} %code.1.refs_0_), channel_id=1, source_target_pairs={{0,24},{1,25},{2,26},{3,27},{4,28},{5,29},{6,30},{7,31},{8,16},{9,... | collective-permute-start | bytes 221192 | tf_op jit(solution)/shard_map/ppermute | solution.py:40
  112.9 1.5 %collective-permute-start.41 = (bf16[96,384]{1,0:T(8,128)(2,1)S(1)}, bf16[96,384]{1,0:T(8,128)(2,1)S(1)}, u32[]{:S(2)}, u32[]{:S(2)}) collective-permute-start(bf16[96,384]{1,0:T(8,128)(2,1)S(1)} %code.1.refs_0_), channel_id=1, source_target_pairs={{0,8},{1,9},{2,10},{3,11},{4,12},{5,13},{6,14},{7,15},{8,0},{9,1},... | collective-permute-start | bytes 221192 | tf_op jit(solution)/shard_map/ppermute | solution.py:40
  114.4 2.3 %collective-permute-done.43.refs_3_ = bf16[96,384]{1,0:T(8,128)(2,1)S(1)} collective-permute-done((bf16[96,384]{1,0:T(8,128)(2,1)S(1)}, bf16[96,384]{1,0:T(8,128)(2,1)S(1)}, u32[]{:S(2)}, u32[]{:S(2)}) %collective-permute-start.43) | collective-permute-done | bytes 73760 | tf_op jit(solution)/shard_map/ppermute | solution.py:40
  116.7 1.8 %collective-permute-done.42.refs_2_ = bf16[96,384]{1,0:T(8,128)(2,1)S(1)} collective-permute-done((bf16[96,384]{1,0:T(8,128)(2,1)S(1)}, bf16[96,384]{1,0:T(8,128)(2,1)S(1)}, u32[]{:S(2)}, u32[]{:S(2)}) %collective-permute-start.42) | collective-permute-done | bytes 73760 | tf_op jit(solution)/shard_map/ppermute | solution.py:40
  118.5 0.9 finish.1.refs_0_
  119.5 1.9 %collective-permute-start.46 = (bf16[128,384]{1,0:T(8,128)(2,1)S(1)}, bf16[128,384]{1,0:T(8,128)(2,1)S(1)}, u32[]{:S(2)}, u32[]{:S(2)}) collective-permute-start(bf16[128,384]{1,0:T(8,128)(2,1)S(1)} %finish.1.refs_0_), channel_id=1, source_target_pairs={{0,6},{1,7},{2,4},{3,5},{4,2},{5,3},{6,0},{7,1},{8,14},{9,15},{10,... | collective-permute-start | bytes 294920 | tf_op jit(solution)/shard_map/ppermute | solution.py:40
  121.6 1.4 collective-permute-start.44
  123.0 2.2 %collective-permute-done.46.refs_3_ = bf16[128,384]{1,0:T(8,128)(2,1)S(1)} collective-permute-done((bf16[128,384]{1,0:T(8,128)(2,1)S(1)}, bf16[128,384]{1,0:T(8,128)(2,1)S(1)}, u32[]{:S(2)}, u32[]{:S(2)}) %collective-permute-start.46) | collective-permute-done | bytes 98336 | tf_op jit(solution)/shard_map/ppermute | solution.py:40
  125.2 1.0 collective-permute-done.45.refs_2_
  127.7 2.3 %gradient.1 = (bf16[256,256]{1,0:T(8,128)(2,1)S(1)}, bf16[256,256]{1,0:T(8,128)(2,1)S(1)}, bf16[256,256]{1,0:T(8,128)(2,1)S(1)}, bf16[256,256]{1,0:T(8,128)(2,1)S(1)}, f32[1,1]{1,0:T(1,128)}) custom-call(s32[3]{0:T(128)S(1)} %pad_add_fusion.place_ref, bf16[128,384]{1,0:T(8,128)(2,1)S(1)} %finish.1.refs_0_, ...), custom_call_target="tpu_custom_call" | custom-call | tf_op jit(solution)/shard_map/gradient/pallas_call | solution.py:172
  130.0 1.9 %collective-permute-start.51 = (bf16[256,256]{1,0:T(8,128)(2,1)S(1)}, bf16[256,256]{1,0:T(8,128)(2,1)S(1)}, u32[]{:S(2)}, u32[]{:S(2)}) collective-permute-start(bf16[256,256]{1,0:T(8,128)(2,1)S(1)} %get-tuple-element.166), channel_id=1, source_target_pairs={{0,24},{1,25},{2,26},{3,27},{4,28},{5,29},{6,30},{7,31},{8,16},{9,... | collective-permute-start | bytes 393224 | tf_op jit(solution)/shard_map/ppermute | solution.py:40
  131.9 2.5 %collective-permute-start.53 = (bf16[256,256]{1,0:T(8,128)(2,1)S(1)}, bf16[256,256]{1,0:T(8,128)(2,1)S(1)}, u32[]{:S(2)}, u32[]{:S(2)}) collective-permute-start(bf16[256,256]{1,0:T(8,128)(2,1)S(1)} %get-tuple-element.168), channel_id=1, source_target_pairs={{0,8},{1,9},{2,10},{3,11},{4,12},{5,13},{6,14},{7,15},{8,0},{9,1},... | collective-permute-start | bytes 393224 | tf_op jit(solution)/shard_map/ppermute | solution.py:40
  134.4 3.9 %collective-permute-done.51.refs_1_ = bf16[256,256]{1,0:T(8,128)(2,1)S(1)} collective-permute-done((bf16[256,256]{1,0:T(8,128)(2,1)S(1)}, bf16[256,256]{1,0:T(8,128)(2,1)S(1)}, u32[]{:S(2)}, u32[]{:S(2)}) %collective-permute-start.51) | collective-permute-done | bytes 131104 | tf_op jit(solution)/shard_map/ppermute | solution.py:40
  138.2 5.6 %collective-permute-done.52.refs_2_ = bf16[256,256]{1,0:T(8,128)(2,1)S(1)} collective-permute-done((bf16[256,256]{1,0:T(8,128)(2,1)S(1)}, bf16[256,256]{1,0:T(8,128)(2,1)S(1)}, u32[]{:S(2)}, u32[]{:S(2)}) %collective-permute-start.52) | collective-permute-done | bytes 131104 | tf_op jit(solution)/shard_map/ppermute | solution.py:40
  143.8 1.4 place.1
  (69 shorter events, 11.9 us)
Async XLA Ops:
  1.6 9.0 %collective-permute-start.10 = (bf16[32,1024]{1,0:T(8,128)(2,1)S(1)}, bf16[32,1024]{1,0:T(8,128)(2,1)S(1)}, u32[]{:S(2)}, u32[]{:S(2)}) collective-permute-start(bf16[32,1024]{1,0:T(8,128)(2,1)S(1)} %get-tuple-element.184), channel_id=1, source_target_pairs={{0,2},{1,3},{2,0},{3,1},{4,6},{5,7},{6,4},{7,5},{8,10},{9,11},{10,... | collective-permute-start | bytes 196616 | tf_op jit(solution)/shard_map/ppermute | solution.py:40
  4.6 6.1 %collective-permute-start.9 = (bf16[32,1024]{1,0:T(8,128)(2,1)S(1)}, bf16[32,1024]{1,0:T(8,128)(2,1)S(1)}, u32[]{:S(2)}, u32[]{:S(2)}) collective-permute-start(bf16[32,1024]{1,0:T(8,128)(2,1)S(1)} %get-tuple-element.185), channel_id=1, source_target_pairs={{0,4},{1,5},{2,6},{3,7},{4,0},{5,1},{6,2},{7,3},{8,12},{9,13},{10,... | collective-permute-start | bytes 196616 | tf_op jit(solution)/shard_map/ppermute | solution.py:40
  6.1 5.2 %collective-permute-start.8 = (bf16[32,1024]{1,0:T(8,128)(2,1)S(1)}, bf16[32,1024]{1,0:T(8,128)(2,1)S(1)}, u32[]{:S(2)}, u32[]{:S(2)}) collective-permute-start(bf16[32,1024]{1,0:T(8,128)(2,1)S(1)} %get-tuple-element.186), channel_id=1, source_target_pairs={{0,6},{1,7},{2,4},{3,5},{4,2},{5,3},{6,0},{7,1},{8,14},{9,15},{10,... | collective-permute-start | bytes 196616 | tf_op jit(solution)/shard_map/ppermute | solution.py:40
  7.1 9.0 %collective-permute-start.16 = (bf16[32,1024]{1,0:T(8,128)(2,1)S(1)}, bf16[32,1024]{1,0:T(8,128)(2,1)S(1)}, u32[]{:S(2)}, u32[]{:S(2)}) collective-permute-start(bf16[32,1024]{1,0:T(8,128)(2,1)S(1)} %get-tuple-element.180), channel_id=1, source_target_pairs={{0,6},{1,7},{2,4},{3,5},{4,2},{5,3},{6,0},{7,1},{8,14},{9,15},{10,... | collective-permute-start | bytes 196616 | tf_op jit(solution)/shard_map/ppermute | solution.py:40
  10.1 6.7 %collective-permute-start.15 = (bf16[32,1024]{1,0:T(8,128)(2,1)S(1)}, bf16[32,1024]{1,0:T(8,128)(2,1)S(1)}, u32[]{:S(2)}, u32[]{:S(2)}) collective-permute-start(bf16[32,1024]{1,0:T(8,128)(2,1)S(1)} %get-tuple-element.181), channel_id=1, source_target_pairs={{0,4},{1,5},{2,6},{3,7},{4,0},{5,1},{6,2},{7,3},{8,12},{9,13},{10,... | collective-permute-start | bytes 196616 | tf_op jit(solution)/shard_map/ppermute | solution.py:40
  10.6 6.2 %collective-permute-start.14 = (bf16[32,1024]{1,0:T(8,128)(2,1)S(1)}, bf16[32,1024]{1,0:T(8,128)(2,1)S(1)}, u32[]{:S(2)}, u32[]{:S(2)}) collective-permute-start(bf16[32,1024]{1,0:T(8,128)(2,1)S(1)} %get-tuple-element.182), channel_id=1, source_target_pairs={{0,2},{1,3},{2,0},{3,1},{4,6},{5,7},{6,4},{7,5},{8,10},{9,11},{10,... | collective-permute-start | bytes 196616 | tf_op jit(solution)/shard_map/ppermute | solution.py:40
  12.2 6.2 %collective-permute-start.13 = (bf16[32,1024]{1,0:T(8,128)(2,1)S(1)}, bf16[32,1024]{1,0:T(8,128)(2,1)S(1)}, u32[]{:S(2)}, u32[]{:S(2)}) collective-permute-start(bf16[32,1024]{1,0:T(8,128)(2,1)S(1)} %get-tuple-element.172), channel_id=1, source_target_pairs={{0,24},{1,25},{2,26},{3,27},{4,28},{5,29},{6,30},{7,31},{8,16},{9,... | collective-permute-start | bytes 196616 | tf_op jit(solution)/shard_map/ppermute | solution.py:40
  16.0 4.4 %collective-permute-start.11 = (bf16[32,1024]{1,0:T(8,128)(2,1)S(1)}, bf16[32,1024]{1,0:T(8,128)(2,1)S(1)}, u32[]{:S(2)}, u32[]{:S(2)}) collective-permute-start(bf16[32,1024]{1,0:T(8,128)(2,1)S(1)} %get-tuple-element.173), channel_id=1, source_target_pairs={{0,8},{1,9},{2,10},{3,11},{4,12},{5,13},{6,14},{7,15},{8,0},{9,1},... | collective-permute-start | bytes 196616 | tf_op jit(solution)/shard_map/ppermute | solution.py:40
  16.1 5.2 %collective-permute-start.12 = (bf16[32,1024]{1,0:T(8,128)(2,1)S(1)}, bf16[32,1024]{1,0:T(8,128)(2,1)S(1)}, u32[]{:S(2)}, u32[]{:S(2)}) collective-permute-start(bf16[32,1024]{1,0:T(8,128)(2,1)S(1)} %get-tuple-element.174), channel_id=1, source_target_pairs={{0,16},{1,17},{2,18},{3,19},{4,20},{5,21},{6,22},{7,23},{8,24},{9,... | collective-permute-start | bytes 196616 | tf_op jit(solution)/shard_map/ppermute | solution.py:40
  21.8 15.7 %collective-permute-start.19 = (bf16[128,1024]{1,0:T(8,128)(2,1)S(1)}, bf16[128,1024]{1,0:T(8,128)(2,1)S(1)}, u32[]{:S(2)}, u32[]{:S(2)}) collective-permute-start(bf16[128,1024]{1,0:T(8,128)(2,1)S(1)} %lay.2.refs_0_), channel_id=1, source_target_pairs={{0,6},{1,7},{2,4},{3,5},{4,2},{5,3},{6,0},{7,1},{8,14},{9,15},{10,... | collective-permute-start | bytes 786440 | tf_op jit(solution)/shard_map/ppermute | solution.py:40
  23.9 13.6 %collective-permute-start.18 = (bf16[128,1024]{1,0:T(8,128)(2,1)S(1)}, bf16[128,1024]{1,0:T(8,128)(2,1)S(1)}, u32[]{:S(2)}, u32[]{:S(2)}) collective-permute-start(bf16[128,1024]{1,0:T(8,128)(2,1)S(1)} %lay.2.refs_0_), channel_id=1, source_target_pairs={{0,4},{1,5},{2,6},{3,7},{4,0},{5,1},{6,2},{7,3},{8,12},{9,13},{10,... | collective-permute-start | bytes 786440 | tf_op jit(solution)/shard_map/ppermute | solution.py:40
  24.4 13.1 %collective-permute-start.17 = (bf16[128,1024]{1,0:T(8,128)(2,1)S(1)}, bf16[128,1024]{1,0:T(8,128)(2,1)S(1)}, u32[]{:S(2)}, u32[]{:S(2)}) collective-permute-start(bf16[128,1024]{1,0:T(8,128)(2,1)S(1)} %lay.2.refs_0_), channel_id=1, source_target_pairs={{0,2},{1,3},{2,0},{3,1},{4,6},{5,7},{6,4},{7,5},{8,10},{9,11},{10,... | collective-permute-start | bytes 786440 | tf_op jit(solution)/shard_map/ppermute | solution.py:40
  25.4 6.3 %collective-permute-start.22 = (bf16[32,1024]{1,0:T(8,128)(2,1)S(1)}, bf16[32,1024]{1,0:T(8,128)(2,1)S(1)}, u32[]{:S(2)}, u32[]{:S(2)}) collective-permute-start(bf16[32,1024]{1,0:T(8,128)(2,1)S(1)} %get-tuple-element.176), channel_id=1, source_target_pairs={{0,24},{1,25},{2,26},{3,27},{4,28},{5,29},{6,30},{7,31},{8,16},{9,... | collective-permute-start | bytes 196616 | tf_op jit(solution)/shard_map/ppermute | solution.py:40
  27.0 6.8 %collective-permute-start.20 = (bf16[32,1024]{1,0:T(8,128)(2,1)S(1)}, bf16[32,1024]{1,0:T(8,128)(2,1)S(1)}, u32[]{:S(2)}, u32[]{:S(2)}) collective-permute-start(bf16[32,1024]{1,0:T(8,128)(2,1)S(1)} %get-tuple-element.178), channel_id=1, source_target_pairs={{0,8},{1,9},{2,10},{3,11},{4,12},{5,13},{6,14},{7,15},{8,0},{9,1},... | collective-permute-start | bytes 196616 | tf_op jit(solution)/shard_map/ppermute | solution.py:40
  31.7 5.9 %collective-permute-start.21 = (bf16[32,1024]{1,0:T(8,128)(2,1)S(1)}, bf16[32,1024]{1,0:T(8,128)(2,1)S(1)}, u32[]{:S(2)}, u32[]{:S(2)}) collective-permute-start(bf16[32,1024]{1,0:T(8,128)(2,1)S(1)} %get-tuple-element.179), channel_id=1, source_target_pairs={{0,16},{1,17},{2,18},{3,19},{4,20},{5,21},{6,22},{7,23},{8,24},{9,... | collective-permute-start | bytes 196616 | tf_op jit(solution)/shard_map/ppermute | solution.py:40
  37.5 3.2 %collective-permute-start.23 = (bf16[128,1024]{1,0:T(8,128)(2,1)S(1)}, bf16[128,1024]{1,0:T(8,128)(2,1)S(1)}, u32[]{:S(2)}, u32[]{:S(2)}) collective-permute-start(bf16[128,1024]{1,0:T(8,128)(2,1)S(1)} %lay.2.refs_0_), channel_id=1, source_target_pairs={{0,1},{1,0},{2,3},{3,2},{4,5},{5,4},{6,7},{7,6},{8,9},{9,8},{10,11... | collective-permute-start | bytes 786440 | tf_op jit(solution)/shard_map/ppermute | solution.py:40
  37.6 3.1 %collective-permute-start.24 = (bf16[128,1024]{1,0:T(8,128)(2,1)S(1)}, bf16[128,1024]{1,0:T(8,128)(2,1)S(1)}, u32[]{:S(2)}, u32[]{:S(2)}) collective-permute-start(bf16[128,1024]{1,0:T(8,128)(2,1)S(1)} %collective-permute-done.17.refs_1_), channel_id=1, source_target_pairs={{0,1},{1,0},{2,3},{3,2},{4,5},{5,4},{6,7},{7,6},{8,9},{9,8},{10,11... | collective-permute-start | bytes 786440 | tf_op jit(solution)/shard_map/ppermute | solution.py:40
  38.1 2.6 %collective-permute-start.25 = (bf16[128,1024]{1,0:T(8,128)(2,1)S(1)}, bf16[128,1024]{1,0:T(8,128)(2,1)S(1)}, u32[]{:S(2)}, u32[]{:S(2)}) collective-permute-start(bf16[128,1024]{1,0:T(8,128)(2,1)S(1)} %collective-permute-done.18.refs_2_), channel_id=1, source_target_pairs={{0,1},{1,0},{2,3},{3,2},{4,5},{5,4},{6,7},{7,6},{8,9},{9,8},{10,11... | collective-permute-start | bytes 786440 | tf_op jit(solution)/shard_map/ppermute | solution.py:40
  38.2 2.5 %collective-permute-start.26 = (bf16[128,1024]{1,0:T(8,128)(2,1)S(1)}, bf16[128,1024]{1,0:T(8,128)(2,1)S(1)}, u32[]{:S(2)}, u32[]{:S(2)}) collective-permute-start(bf16[128,1024]{1,0:T(8,128)(2,1)S(1)} %collective-permute-done.19.refs_3_), channel_id=1, source_target_pairs={{0,1},{1,0},{2,3},{3,2},{4,5},{5,4},{6,7},{7,6},{8,9},{9,8},{10,11... | collective-permute-start | bytes 786440 | tf_op jit(solution)/shard_map/ppermute | solution.py:40
  39.2 9.9 %collective-permute-start.27 = (bf16[128,1024]{1,0:T(8,128)(2,1)S(1)}, bf16[128,1024]{1,0:T(8,128)(2,1)}, u32[]{:S(2)}, u32[]{:S(2)}) collective-permute-start(bf16[128,1024]{1,0:T(8,128)(2,1)S(1)} %lay.3), channel_id=1, source_target_pairs={{0,6},{1,7},{2,4},{3,5},{4,2},{5,3},{6,0},{7,1},{8,14},{9,15},{10,... | collective-permute-start | bytes 786440 | tf_op jit(solution)/shard_map/ppermute | solution.py:40
  44.7 23.7 %collective-permute-start.31 = (bf16[528,256]{1,0:T(8,128)(2,1)S(1)}, bf16[528,256]{1,0:T(8,128)(2,1)S(1)}, u32[]{:S(2)}, u32[]{:S(2)}) collective-permute-start(bf16[528,256]{1,0:T(8,128)(2,1)S(1)} %get-tuple-element.135), channel_id=1, source_target_pairs={{0,24},{1,25},{2,26},{3,27},{4,28},{5,29},{6,30},{7,31},{8,16},{9,... | collective-permute-start | bytes 811016 | tf_op jit(solution)/shard_map/ppermute | solution.py:40
  47.0 25.3 %collective-permute-start.32 = (bf16[528,256]{1,0:T(8,128)(2,1)S(1)}, bf16[528,256]{1,0:T(8,128)(2,1)S(1)}, u32[]{:S(2)}, u32[]{:S(2)}) collective-permute-start(bf16[528,256]{1,0:T(8,128)(2,1)S(1)} %get-tuple-element.136), channel_id=1, source_target_pairs={{0,16},{1,17},{2,18},{3,19},{4,20},{5,21},{6,22},{7,23},{8,24},{9,... | collective-permute-start | bytes 811016 | tf_op jit(solution)/shard_map/ppermute | solution.py:40
  47.9 24.4 %collective-permute-start.33 = (bf16[528,256]{1,0:T(8,128)(2,1)S(1)}, bf16[528,256]{1,0:T(8,128)(2,1)S(1)}, u32[]{:S(2)}, u32[]{:S(2)}) collective-permute-start(bf16[528,256]{1,0:T(8,128)(2,1)S(1)} %get-tuple-element.137), channel_id=1, source_target_pairs={{0,8},{1,9},{2,10},{3,11},{4,12},{5,13},{6,14},{7,15},{8,0},{9,1},... | collective-permute-start | bytes 811016 | tf_op jit(solution)/shard_map/ppermute | solution.py:40
  49.1 7.2 %collective-permute-start.4 = (bf16[128,1024]{1,0:T(8,128)(2,1)S(1)}, bf16[128,1024]{1,0:T(8,128)(2,1)S(1)}, u32[]{:S(2)}, u32[]{:S(2)}) collective-permute-start(bf16[128,1024]{1,0:T(8,128)(2,1)S(1)} %get-tuple-element.16.refs_0_), channel_id=1, source_target_pairs={{0,2},{1,3},{2,0},{3,1},{4,6},{5,7},{6,4},{7,5},{8,10},{9,11},{10,... | collective-permute-start | bytes 786440 | tf_op jit(solution)/shard_map/cond/branch_1_fun/ppermute | solution.py:40
  49.6 6.9 %collective-permute-start.5 = (bf16[128,1024]{1,0:T(8,128)(2,1)S(1)}, bf16[128,1024]{1,0:T(8,128)(2,1)S(1)}, u32[]{:S(2)}, u32[]{:S(2)}) collective-permute-start(bf16[128,1024]{1,0:T(8,128)(2,1)S(1)} %get-tuple-element.16.refs_0_), channel_id=1, source_target_pairs={{0,4},{1,5},{2,6},{3,7},{4,0},{5,1},{6,2},{7,3},{8,12},{9,13},{10,... | collective-permute-start | bytes 786440 | tf_op jit(solution)/shard_map/cond/branch_1_fun/ppermute | solution.py:40
  56.6 3.9 %collective-permute-start.7 = (bf16[256,1024]{1,0:T(8,128)(2,1)S(1)}, bf16[256,1024]{1,0:T(8,128)(2,1)S(1)}, u32[]{:S(2)}, u32[]{:S(2)}) collective-permute-start(bf16[256,1024]{1,0:T(8,128)(2,1)S(1)} %pad_maximum_fusion.1), channel_id=1, source_target_pairs={{0,1},{1,0},{2,3},{3,2},{4,5},{5,4},{6,7},{7,6},{8,9},{9,8},{10,11... | collective-permute-start | bytes 1572872 | tf_op jit(solution)/shard_map/cond/branch_1_fun/ppermute | solution.py:40
  57.7 2.8 %collective-permute-start.6 = (bf16[256,1024]{1,0:T(8,128)(2,1)S(1)}, bf16[256,1024]{1,0:T(8,128)(2,1)S(1)}, u32[]{:S(2)}, u32[]{:S(2)}) collective-permute-start(bf16[256,1024]{1,0:T(8,128)(2,1)S(1)} %pad_maximum_fusion), channel_id=1, source_target_pairs={{0,1},{1,0},{2,3},{3,2},{4,5},{5,4},{6,7},{7,6},{8,9},{9,8},{10,11... | collective-permute-start | bytes 1572872 | tf_op jit(solution)/shard_map/cond/branch_1_fun/ppermute | solution.py:40
  65.5 25.8 %collective-permute-start.28 = (bf16[528,256]{1,0:T(8,128)(2,1)}, bf16[528,256]{1,0:T(8,128)(2,1)S(1)}, u32[]{:S(2)}, u32[]{:S(2)}) collective-permute-start(bf16[528,256]{1,0:T(8,128)(2,1)} %get-tuple-element.131), channel_id=1, source_target_pairs={{0,8},{1,9},{2,10},{3,11},{4,12},{5,13},{6,14},{7,15},{8,0},{9,1},... | collective-permute-start | bytes 811016 | tf_op jit(solution)/shard_map/ppermute | solution.py:40
  66.9 26.9 %collective-permute-start.29 = (bf16[528,256]{1,0:T(8,128)(2,1)}, bf16[528,256]{1,0:T(8,128)(2,1)S(1)}, u32[]{:S(2)}, u32[]{:S(2)}) collective-permute-start(bf16[528,256]{1,0:T(8,128)(2,1)} %get-tuple-element.132), channel_id=1, source_target_pairs={{0,16},{1,17},{2,18},{3,19},{4,20},{5,21},{6,22},{7,23},{8,24},{9,... | collective-permute-start | bytes 811016 | tf_op jit(solution)/shard_map/ppermute | solution.py:40
  68.3 25.5 %collective-permute-start.30 = (bf16[528,256]{1,0:T(8,128)(2,1)}, bf16[528,256]{1,0:T(8,128)(2,1)S(1)}, u32[]{:S(2)}, u32[]{:S(2)}) collective-permute-start(bf16[528,256]{1,0:T(8,128)(2,1)} %get-tuple-element.133), channel_id=1, source_target_pairs={{0,24},{1,25},{2,26},{3,27},{4,28},{5,29},{6,30},{7,31},{8,16},{9,... | collective-permute-start | bytes 811016 | tf_op jit(solution)/shard_map/ppermute | solution.py:40
  75.7 2.1 %collective-permute-start = (f32[256,512]{1,0:T(8,128)}, f32[256,512]{1,0:T(8,128)S(1)}, u32[]{:S(2)}, u32[]{:S(2)}) collective-permute-start(f32[256,512]{1,0:T(8,128)} %get-tuple-element.26), channel_id=1, source_target_pairs={{0,1},{1,0},{2,3},{3,2},{4,5},{5,4},{6,7},{7,6},{8,9},{9,8},{10,11... | collective-permute-start | bytes 1572872 | tf_op jit(solution)/shard_map/cond/branch_1_fun/ppermute | solution.py:40
  79.1 4.3 %collective-permute-start.1 = (bf16[80,384]{1,0:T(8,128)(2,1)S(1)}, bf16[80,384]{1,0:T(8,128)(2,1)S(1)}, u32[]{:S(2)}, u32[]{:S(2)}) collective-permute-start(bf16[80,384]{1,0:T(8,128)(2,1)S(1)} %get-tuple-element.28), channel_id=1, source_target_pairs={{0,2},{1,3},{2,0},{3,1},{4,6},{5,7},{6,4},{7,5},{8,10},{9,11},{10,... | collective-permute-start | bytes 184328 | tf_op jit(solution)/shard_map/cond/branch_1_fun/ppermute | solution.py:40
  79.7 5.1 %collective-permute-start.2 = (bf16[80,384]{1,0:T(8,128)(2,1)S(1)}, bf16[80,384]{1,0:T(8,128)(2,1)S(1)}, u32[]{:S(2)}, u32[]{:S(2)}) collective-permute-start(bf16[80,384]{1,0:T(8,128)(2,1)S(1)} %get-tuple-element.31), channel_id=1, source_target_pairs={{0,4},{1,5},{2,6},{3,7},{4,0},{5,1},{6,2},{7,3},{8,12},{9,13},{10,... | collective-permute-start | bytes 184328 | tf_op jit(solution)/shard_map/cond/branch_1_fun/ppermute | solution.py:40
  83.4 5.1 %collective-permute-start.3 = (bf16[80,384]{1,0:T(8,128)(2,1)S(1)}, bf16[80,384]{1,0:T(8,128)(2,1)S(1)}, u32[]{:S(2)}, u32[]{:S(2)}) collective-permute-start(bf16[80,384]{1,0:T(8,128)(2,1)S(1)} %get-tuple-element.32), channel_id=1, source_target_pairs={{0,6},{1,7},{2,4},{3,5},{4,2},{5,3},{6,0},{7,1},{8,14},{9,15},{10,... | collective-permute-start | bytes 184328 | tf_op jit(solution)/shard_map/cond/branch_1_fun/ppermute | solution.py:40
  89.3 4.5 %collective-permute-start.34 = (f32[16,384]{1,0:T(8,128)S(1)}, f32[16,384]{1,0:T(8,128)S(1)}, u32[]{:S(2)}, u32[]{:S(2)}) collective-permute-start(f32[16,384]{1,0:T(8,128)S(1)} %get-tuple-element.141), channel_id=1, source_target_pairs={{0,8},{1,9},{2,10},{3,11},{4,12},{5,13},{6,14},{7,15},{8,0},{9,1},... | collective-permute-start | bytes 73736 | tf_op jit(solution)/shard_map/ppermute | solution.py:40
  89.4 6.9 %collective-permute-start.35 = (f32[16,384]{1,0:T(8,128)S(1)}, f32[16,384]{1,0:T(8,128)S(1)}, u32[]{:S(2)}, u32[]{:S(2)}) collective-permute-start(f32[16,384]{1,0:T(8,128)S(1)} %get-tuple-element.142), channel_id=1, source_target_pairs={{0,16},{1,17},{2,18},{3,19},{4,20},{5,21},{6,22},{7,23},{8,24},{9,... | collective-permute-start | bytes 73736 | tf_op jit(solution)/shard_map/ppermute | solution.py:40
  91.3 5.6 %collective-permute-start.36 = (f32[16,384]{1,0:T(8,128)S(1)}, f32[16,384]{1,0:T(8,128)S(1)}, u32[]{:S(2)}, u32[]{:S(2)}) collective-permute-start(f32[16,384]{1,0:T(8,128)S(1)} %get-tuple-element.143), channel_id=1, source_target_pairs={{0,24},{1,25},{2,26},{3,27},{4,28},{5,29},{6,30},{7,31},{8,16},{9,... | collective-permute-start | bytes 73736 | tf_op jit(solution)/shard_map/ppermute | solution.py:40
  99.5 2.0 %collective-permute-start.37 = (f32[256,512]{1,0:T(8,128)S(1)}, f32[256,512]{1,0:T(8,128)S(1)}, u32[]{:S(2)}, u32[]{:S(2)}) collective-permute-start(f32[256,512]{1,0:T(8,128)S(1)} %get-tuple-element.150), channel_id=1, source_target_pairs={{0,1},{1,0},{2,3},{3,2},{4,5},{5,4},{6,7},{7,6},{8,9},{9,8},{10,11... | collective-permute-start | bytes 1572872 | tf_op jit(solution)/shard_map/ppermute | solution.py:40
  102.3 4.6 %collective-permute-start.38 = (bf16[80,384]{1,0:T(8,128)(2,1)S(1)}, bf16[80,384]{1,0:T(8,128)(2,1)S(1)}, u32[]{:S(2)}, u32[]{:S(2)}) collective-permute-start(bf16[80,384]{1,0:T(8,128)(2,1)S(1)} %get-tuple-element.152), channel_id=1, source_target_pairs={{0,2},{1,3},{2,0},{3,1},{4,6},{5,7},{6,4},{7,5},{8,10},{9,11},{10,... | collective-permute-start | bytes 184328 | tf_op jit(solution)/shard_map/ppermute | solution.py:40
  102.6 4.3 %collective-permute-start.39 = (bf16[80,384]{1,0:T(8,128)(2,1)S(1)}, bf16[80,384]{1,0:T(8,128)(2,1)S(1)}, u32[]{:S(2)}, u32[]{:S(2)}) collective-permute-start(bf16[80,384]{1,0:T(8,128)(2,1)S(1)} %get-tuple-element.153), channel_id=1, source_target_pairs={{0,4},{1,5},{2,6},{3,7},{4,0},{5,1},{6,2},{7,3},{8,12},{9,13},{10,... | collective-permute-start | bytes 184328 | tf_op jit(solution)/shard_map/ppermute | solution.py:40
  104.0 5.1 %collective-permute-start.40 = (bf16[80,384]{1,0:T(8,128)(2,1)S(1)}, bf16[80,384]{1,0:T(8,128)(2,1)S(1)}, u32[]{:S(2)}, u32[]{:S(2)}) collective-permute-start(bf16[80,384]{1,0:T(8,128)(2,1)S(1)} %get-tuple-element.154), channel_id=1, source_target_pairs={{0,6},{1,7},{2,4},{3,5},{4,2},{5,3},{6,0},{7,1},{8,14},{9,15},{10,... | collective-permute-start | bytes 184328 | tf_op jit(solution)/shard_map/ppermute | solution.py:40
  109.9 6.8 %collective-permute-start.43 = (bf16[96,384]{1,0:T(8,128)(2,1)S(1)}, bf16[96,384]{1,0:T(8,128)(2,1)S(1)}, u32[]{:S(2)}, u32[]{:S(2)}) collective-permute-start(bf16[96,384]{1,0:T(8,128)(2,1)S(1)} %code.1.refs_0_), channel_id=1, source_target_pairs={{0,24},{1,25},{2,26},{3,27},{4,28},{5,29},{6,30},{7,31},{8,16},{9,... | collective-permute-start | bytes 221192 | tf_op jit(solution)/shard_map/ppermute | solution.py:40
  112.9 5.7 %collective-permute-start.42 = (bf16[96,384]{1,0:T(8,128)(2,1)S(1)}, bf16[96,384]{1,0:T(8,128)(2,1)S(1)}, u32[]{:S(2)}, u32[]{:S(2)}) collective-permute-start(bf16[96,384]{1,0:T(8,128)(2,1)S(1)} %code.1.refs_0_), channel_id=1, source_target_pairs={{0,16},{1,17},{2,18},{3,19},{4,20},{5,21},{6,22},{7,23},{8,24},{9,... | collective-permute-start | bytes 221192 | tf_op jit(solution)/shard_map/ppermute | solution.py:40
  112.9 5.7 %collective-permute-start.41 = (bf16[96,384]{1,0:T(8,128)(2,1)S(1)}, bf16[96,384]{1,0:T(8,128)(2,1)S(1)}, u32[]{:S(2)}, u32[]{:S(2)}) collective-permute-start(bf16[96,384]{1,0:T(8,128)(2,1)S(1)} %code.1.refs_0_), channel_id=1, source_target_pairs={{0,8},{1,9},{2,10},{3,11},{4,12},{5,13},{6,14},{7,15},{8,0},{9,1},... | collective-permute-start | bytes 221192 | tf_op jit(solution)/shard_map/ppermute | solution.py:40
  119.5 5.8 %collective-permute-start.46 = (bf16[128,384]{1,0:T(8,128)(2,1)S(1)}, bf16[128,384]{1,0:T(8,128)(2,1)S(1)}, u32[]{:S(2)}, u32[]{:S(2)}) collective-permute-start(bf16[128,384]{1,0:T(8,128)(2,1)S(1)} %finish.1.refs_0_), channel_id=1, source_target_pairs={{0,6},{1,7},{2,4},{3,5},{4,2},{5,3},{6,0},{7,1},{8,14},{9,15},{10,... | collective-permute-start | bytes 294920 | tf_op jit(solution)/shard_map/ppermute | solution.py:40
  121.4 4.9 %collective-permute-start.45 = (bf16[128,384]{1,0:T(8,128)(2,1)S(1)}, bf16[128,384]{1,0:T(8,128)(2,1)S(1)}, u32[]{:S(2)}, u32[]{:S(2)}) collective-permute-start(bf16[128,384]{1,0:T(8,128)(2,1)S(1)} %finish.1.refs_0_), channel_id=1, source_target_pairs={{0,4},{1,5},{2,6},{3,7},{4,0},{5,1},{6,2},{7,3},{8,12},{9,13},{10,... | collective-permute-start | bytes 294920 | tf_op jit(solution)/shard_map/ppermute | solution.py:40
  121.6 4.7 %collective-permute-start.44 = (bf16[128,384]{1,0:T(8,128)(2,1)S(1)}, bf16[128,384]{1,0:T(8,128)(2,1)S(1)}, u32[]{:S(2)}, u32[]{:S(2)}) collective-permute-start(bf16[128,384]{1,0:T(8,128)(2,1)S(1)} %finish.1.refs_0_), channel_id=1, source_target_pairs={{0,2},{1,3},{2,0},{3,1},{4,6},{5,7},{6,4},{7,5},{8,10},{9,11},{10,... | collective-permute-start | bytes 294920 | tf_op jit(solution)/shard_map/ppermute | solution.py:40
  123.0 3.8 %collective-permute-start.47 = (bf16[128,384]{1,0:T(8,128)(2,1)S(1)}, bf16[128,384]{1,0:T(8,128)(2,1)S(1)}, u32[]{:S(2)}, u32[]{:S(2)}) collective-permute-start(bf16[128,384]{1,0:T(8,128)(2,1)S(1)} %finish.1.refs_0_), channel_id=1, source_target_pairs={{0,1},{1,0},{2,3},{3,2},{4,5},{5,4},{6,7},{7,6},{8,9},{9,8},{10,11... | collective-permute-start | bytes 294920 | tf_op jit(solution)/shard_map/ppermute | solution.py:40
  125.2 1.5 %collective-permute-start.50 = (bf16[128,384]{1,0:T(8,128)(2,1)S(1)}, bf16[128,384]{1,0:T(8,128)(2,1)S(1)}, u32[]{:S(2)}, u32[]{:S(2)}) collective-permute-start(bf16[128,384]{1,0:T(8,128)(2,1)S(1)} %collective-permute-done.46.refs_3_), channel_id=1, source_target_pairs={{0,1},{1,0},{2,3},{3,2},{4,5},{5,4},{6,7},{7,6},{8,9},{9,8},{10,11... | collective-permute-start | bytes 294920 | tf_op jit(solution)/shard_map/ppermute | solution.py:40
  126.3 1.3 collective-permute-start.49
  126.3 1.5 %collective-permute-start.48 = (bf16[128,384]{1,0:T(8,128)(2,1)S(1)}, bf16[128,384]{1,0:T(8,128)(2,1)S(1)}, u32[]{:S(2)}, u32[]{:S(2)}) collective-permute-start(bf16[128,384]{1,0:T(8,128)(2,1)S(1)} %collective-permute-done.44.refs_1_), channel_id=1, source_target_pairs={{0,1},{1,0},{2,3},{3,2},{4,5},{5,4},{6,7},{7,6},{8,9},{9,8},{10,11... | collective-permute-start | bytes 294920 | tf_op jit(solution)/shard_map/ppermute | solution.py:40
  130.0 8.3 %collective-permute-start.51 = (bf16[256,256]{1,0:T(8,128)(2,1)S(1)}, bf16[256,256]{1,0:T(8,128)(2,1)S(1)}, u32[]{:S(2)}, u32[]{:S(2)}) collective-permute-start(bf16[256,256]{1,0:T(8,128)(2,1)S(1)} %get-tuple-element.166), channel_id=1, source_target_pairs={{0,24},{1,25},{2,26},{3,27},{4,28},{5,29},{6,30},{7,31},{8,16},{9,... | collective-permute-start | bytes 393224 | tf_op jit(solution)/shard_map/ppermute | solution.py:40
  131.9 12.0 %collective-permute-start.52 = (bf16[256,256]{1,0:T(8,128)(2,1)S(1)}, bf16[256,256]{1,0:T(8,128)(2,1)S(1)}, u32[]{:S(2)}, u32[]{:S(2)}) collective-permute-start(bf16[256,256]{1,0:T(8,128)(2,1)S(1)} %get-tuple-element.167), channel_id=1, source_target_pairs={{0,16},{1,17},{2,18},{3,19},{4,20},{5,21},{6,22},{7,23},{8,24},{9,... | collective-permute-start | bytes 393224 | tf_op jit(solution)/shard_map/ppermute | solution.py:40
  131.9 12.0 %collective-permute-start.53 = (bf16[256,256]{1,0:T(8,128)(2,1)S(1)}, bf16[256,256]{1,0:T(8,128)(2,1)S(1)}, u32[]{:S(2)}, u32[]{:S(2)}) collective-permute-start(bf16[256,256]{1,0:T(8,128)(2,1)S(1)} %get-tuple-element.168), channel_id=1, source_target_pairs={{0,8},{1,9},{2,10},{3,11},{4,12},{5,13},{6,14},{7,15},{8,0},{9,1},... | collective-permute-start | bytes 393224 | tf_op jit(solution)/shard_map/ppermute | solution.py:40

commit v12 on v11

--- a/solution.py
+++ b/solution.py
@@ -508,12 +508,12 @@
 def with_kernels(place, h_first, h_second, weight):
     n, k, z, a, b = place.n, place.k, place.z, place.a, place.b
     place_array = jnp.stack([z, a, b]).astype(jnp.int32)
-    first = to_columns(place, h_first)
-    first, second = lax.optimization_barrier((to_planes(place, first), to_columns(place, h_second)))
+    size, here, toward = place.along("a")
+    first, second = lax.optimization_barrier((to_columns(place, h_first), h_second))
+    first, second = to_planes(place, first), to_columns(place, second)
     first, late_weight = lax.optimization_barrier((lay(place, place_array, first), weight))
-    met_1, second, held = lax.optimization_barrier(
-        (met_rows(place, first), to_planes(place, second), fetch(late_weight))
-    )
+    met_1, second = met_rows(place, first), to_planes(place, second)
+    met_1, second, held = lax.optimization_barrier((met_1, second, fetch(late_weight)))
 
     def sent(parts):
         return sends(place, "z", [parts[0], *parts])[1:]
@@ -521,22 +521,22 @@
     def swapped(part):
         return place.send(part, lambda z, a, b: (z, a, b ^ 1))
 
-    own_1, parts_1 = project(place, place_array, [met_1, [swapped(part) for part in met_1]], held)
-    second = lay(place, place_array, second)
-    size, here, toward = place.along("a")
-    order_2 = [0, size - 1, *range(1, size - 1)]
-    last = place.send(second, toward(size - 1))
+    others_1 = [swapped(part) for part in met_1]
+    own_1, parts_1 = project(place, place_array, [met_1, others_1], held)
     own_1, parts_1, late_weight = lax.optimization_barrier((own_1, parts_1, weight))
     parts_1 = sent(parts_1)
-
-    def second_projected(weight, values, last):
-        met = [place.send(values, toward(step)) for step in range(1, size - 1)]
-        values, met[0] = lax.optimization_barrier((values, met[0]))
+    order_2 = [0, size - 1, *range(1, size - 1)]
+
+    def second_projected(weight, *parts):
+        values = lay(place, place_array, parts)
+        last, met = [place.send(values, toward(step)) for step in (size - 1, 1)]
+        again, met = lax.optimization_barrier((values, met))
+        met = [met] + [place.send(again, toward(step)) for step in range(2, size - 1)]
         early = swapped(jnp.concatenate([values, last], 0))
         late = swapped(jnp.concatenate(met, 0))
         return project(place, place_array, [[values, last, *met], [early, late]], fetch(weight))
 
-    own_2, parts_2 = in_one(place, second_projected, (late_weight, second, last))
+    own_2, parts_2 = in_one(place, second_projected, (late_weight, *second))
     own_1, own_2 = lax.optimization_barrier((own_1, own_2))
     parts_2 = sent(parts_2)
     norm_1, packed_1, scale_1, *grams = normalize_parts(

time: 146 us -> 155 us (1.062)
  waiting for transfers between devices: 54.3 us -> 63.4 us
  starting transfers between devices: 56.9 us -> 58.8 us
    ppermute x54, waiting for transfers between devices: 54.3 us -> 63.4 us  [send(): return lax.ppermute(value, ('dp', 'mp'), pairs)]
    ppermute x54, starting transfers between devices: 56.9 us -> 58.8 us  [send(): return lax.ppermute(value, ('dp', 'mp'), pairs)]
  transfers between devices with their start and end apart: 54 -> 54, of which waited for: 25 -> 31; matrix products, arithmetic and copies ran while one was open for 2% -> 1% of each run, Pallas kernels for 14% -> 10%
where the time goes in v12:
time: 155 us
  waiting for transfers between devices  63.4 us (41%)
  starting transfers between devices  58.8 us (38%)
  Pallas kernels  28.9 us (19%)
  local copies, waits for them, and re-layouts  1.88 us (1%)
    ppermute x54, waiting for transfers between devices, send(): return lax.ppermute(value, ('dp', 'mp'), pairs)  63.4 us
    ppermute x54, starting transfers between devices, send(): return lax.ppermute(value, ('dp', 'mp'), pairs)  58.8 us
    pallas_call x10, Pallas kernels, local(): pl.pallas_call(kernel, in_specs=[pl.BlockSpec(memory_space=pltpu.SMEM)] +...  9.97 us
    pallas_call x2, Pallas kernels, project(): pl.pallas_call(functools.partial(project_kernel, counts=counts, n=n, k=k)...  8.5 us
    pallas_call x2, Pallas kernels, normalize_parts(): pl.pallas_call(functools.partial(normalize_kernel, n=n, k=k, order=order,...  6.02 us
    pallas_call x2, Pallas kernels, fetch(): pl.pallas_call(fetch_kernel, in_specs=[pl.BlockSpec(memory_space=pl.ANY)]...  4.39 us
  transfers between devices with their start and end apart: 54, of which 31 were waited for; matrix products, arithmetic and copies ran while one was open for 1% of the time, Pallas kernels for 10%

profile of v12, /device:TPU:0, one launch (start us, length us, event | category | flops | bytes accessed | tf_op | source)
XLA Modules:
  0.0 154.8 jit_solution(17377781512970382999)
XLA Ops:
  0.7 1.0 dynamic-slice_bitcast_fusion.3
  1.6 4.0 %collective-permute-start.11 = (bf16[32,1024]{1,0:T(8,128)(2,1)S(1)}, bf16[32,1024]{1,0:T(8,128)(2,1)S(1)}, u32[]{:S(2)}, u32[]{:S(2)}) collective-permute-start(bf16[32,1024]{1,0:T(8,128)(2,1)S(1)} %get-tuple-element.183), channel_id=1, source_target_pairs={{0,6},{1,7},{2,4},{3,5},{4,2},{5,3},{6,0},{7,1},{8,14},{9,15},{10,... | collective-permute-start | bytes 196616 | tf_op jit(solution)/shard_map/ppermute | solution.py:40
  6.2 1.6 %collective-permute-done.11 = bf16[32,1024]{1,0:T(8,128)(2,1)S(1)} collective-permute-done((bf16[32,1024]{1,0:T(8,128)(2,1)S(1)}, bf16[32,1024]{1,0:T(8,128)(2,1)S(1)}, u32[]{:S(2)}, u32[]{:S(2)}) %collective-permute-start.11) | collective-permute-done | bytes 65568 | tf_op jit(solution)/shard_map/ppermute | solution.py:40
  7.8 2.0 %collective-permute-done.10 = bf16[32,1024]{1,0:T(8,128)(2,1)S(1)} collective-permute-done((bf16[32,1024]{1,0:T(8,128)(2,1)S(1)}, bf16[32,1024]{1,0:T(8,128)(2,1)S(1)}, u32[]{:S(2)}, u32[]{:S(2)}) %collective-permute-start.10) | collective-permute-done | bytes 65568 | tf_op jit(solution)/shard_map/ppermute | solution.py:40
  10.4 3.7 %collective-permute-start.14 = (bf16[32,1024]{1,0:T(8,128)(2,1)S(1)}, bf16[32,1024]{1,0:T(8,128)(2,1)S(1)}, u32[]{:S(2)}, u32[]{:S(2)}) collective-permute-start(bf16[32,1024]{1,0:T(8,128)(2,1)S(1)} %get-tuple-element.179), channel_id=1, source_target_pairs={{0,24},{1,25},{2,26},{3,27},{4,28},{5,29},{6,30},{7,31},{8,16},{9,... | collective-permute-start | bytes 196616 | tf_op jit(solution)/shard_map/ppermute | solution.py:40
  14.1 0.8 collective-permute-start.13
  14.8 0.9 dynamic-slice_bitcast_fusion
  16.3 1.6 %collective-permute-start.19 = (bf16[32,1024]{1,0:T(8,128)(2,1)S(1)}, bf16[32,1024]{1,0:T(8,128)(2,1)S(1)}, u32[]{:S(2)}, u32[]{:S(2)}) collective-permute-start(bf16[32,1024]{1,0:T(8,128)(2,1)S(1)} %get-tuple-element.177), channel_id=1, source_target_pairs={{0,4},{1,5},{2,6},{3,7},{4,0},{5,1},{6,2},{7,3},{8,12},{9,13},{10,... | collective-permute-start | bytes 196616 | tf_op jit(solution)/shard_map/ppermute | solution.py:40
  17.9 1.4 collective-permute-start.18
  20.0 1.6 %collective-permute-start.17 = (bf16[128,1024]{1,0:T(8,128)(2,1)S(1)}, bf16[128,1024]{1,0:T(8,128)(2,1)S(1)}, u32[]{:S(2)}, u32[]{:S(2)}) collective-permute-start(bf16[128,1024]{1,0:T(8,128)(2,1)S(1)} %lay.3.refs_0_), channel_id=1, source_target_pairs={{0,6},{1,7},{2,4},{3,5},{4,2},{5,3},{6,0},{7,1},{8,14},{9,15},{10,... | collective-permute-start | bytes 786440 | tf_op jit(solution)/shard_map/ppermute | solution.py:40
  22.0 1.6 %collective-permute-start.15 = (bf16[128,1024]{1,0:T(8,128)(2,1)S(1)}, bf16[128,1024]{1,0:T(8,128)(2,1)S(1)}, u32[]{:S(2)}, u32[]{:S(2)}) collective-permute-start(bf16[128,1024]{1,0:T(8,128)(2,1)S(1)} %lay.3.refs_0_), channel_id=1, source_target_pairs={{0,2},{1,3},{2,0},{3,1},{4,6},{5,7},{6,4},{7,5},{8,10},{9,11},{10,... | collective-permute-start | bytes 786440 | tf_op jit(solution)/shard_map/ppermute | solution.py:40
  23.9 0.9 broadcast_select_fusion.6
  24.7 3.7 %collective-permute-start.23 = (bf16[32,1024]{1,0:T(8,128)(2,1)S(1)}, bf16[32,1024]{1,0:T(8,128)(2,1)S(1)}, u32[]{:S(2)}, u32[]{:S(2)}) collective-permute-start(bf16[32,1024]{1,0:T(8,128)(2,1)S(1)} %get-tuple-element.172), channel_id=1, source_target_pairs={{0,24},{1,25},{2,26},{3,27},{4,28},{5,29},{6,30},{7,31},{8,16},{9,... | collective-permute-start | bytes 196616 | tf_op jit(solution)/shard_map/ppermute | solution.py:40
  28.5 3.1 %collective-permute-done.23 = bf16[32,1024]{1,0:T(8,128)(2,1)S(1)} collective-permute-done((bf16[32,1024]{1,0:T(8,128)(2,1)S(1)}, bf16[32,1024]{1,0:T(8,128)(2,1)S(1)}, u32[]{:S(2)}, u32[]{:S(2)}) %collective-permute-start.23) | collective-permute-done | bytes 65568 | tf_op jit(solution)/shard_map/ppermute | solution.py:40
  31.6 2.2 %fetch.3.refs_8_ = bf16[2048,1024]{1,0:T(8,128)(2,1)S(1)} custom-call(bf16[2048,1024]{1,0:T(8,128)(2,1)} %weight_ref), custom_call_target="tpu_custom_call" | custom-call | bytes 8388608 | tf_op jit(solution)/shard_map/fetch/pallas_call | solution.py:246
  33.8 3.6 %collective-permute-done.22 = bf16[32,1024]{1,0:T(8,128)(2,1)S(1)} collective-permute-done((bf16[32,1024]{1,0:T(8,128)(2,1)S(1)}, bf16[32,1024]{1,0:T(8,128)(2,1)S(1)}, u32[]{:S(2)}, u32[]{:S(2)}) %collective-permute-start.22) | collective-permute-done | bytes 65568 | tf_op jit(solution)/shard_map/ppermute | solution.py:40
  40.1 3.9 %project.3 = (f32[512,256]{1,0:T(8,128)S(1)}, bf16[528,256]{1,0:T(8,128)(2,1)S(1)}, bf16[528,256]{1,0:T(8,128)(2,1)S(1)}, bf16[528,256]{1,0:T(8,128)(2,1)S(1)}) custom-call(s32[3]{0:T(128)S(1)} %pad_add_fusion.place_ref, bf16[128,1024]{1,0:T(8,128)(2,1)S(1)} %lay.3.refs_0_, bf16[128,1024]{1,0:T(8,128)(2,1)S(1)} %collective-permute-done.15.refs_1_, ...), custom_call_target="tpu_custom_call" | custom-call | flops 2147483648 | bytes 7864320 | tf_op jit(solution)/shard_map/project/pallas_call | solution.py:340
  44.0 2.4 %collective-permute-start.31 = (bf16[528,256]{1,0:T(8,128)(2,1)S(1)}, bf16[528,256]{1,0:T(8,128)(2,1)S(1)}, u32[]{:S(2)}, u32[]{:S(2)}) collective-permute-start(bf16[528,256]{1,0:T(8,128)(2,1)S(1)} %get-tuple-element.135), channel_id=1, source_target_pairs={{0,24},{1,25},{2,26},{3,27},{4,28},{5,29},{6,30},{7,31},{8,16},{9,... | collective-permute-start | bytes 811016 | tf_op jit(solution)/shard_map/ppermute | solution.py:40
  46.4 2.1 %collective-permute-start.33 = (bf16[528,256]{1,0:T(8,128)(2,1)S(1)}, bf16[528,256]{1,0:T(8,128)(2,1)S(1)}, u32[]{:S(2)}, u32[]{:S(2)}) collective-permute-start(bf16[528,256]{1,0:T(8,128)(2,1)S(1)} %get-tuple-element.137), channel_id=1, source_target_pairs={{0,8},{1,9},{2,10},{3,11},{4,12},{5,13},{6,14},{7,15},{8,0},{9,1},... | collective-permute-start | bytes 811016 | tf_op jit(solution)/shard_map/ppermute | solution.py:40
  48.5 27.3 %conditional.2 = (f32[512,256]{1,0:T(8,128)S(1)}, bf16[528,256]{1,0:T(8,128)(2,1)}, bf16[528,256]{1,0:T(8,128)(2,1)}, bf16[528,256]{1,0:T(8,128)(2,1)}) conditional(s32[]{:T(128)} %convert_element_type.4, () %tuple.35, (s32[3]{0:T(128)S(1)}, bf16[32,1024]{1,0:T(8,128)(2,1)S(1)}, bf16[32,1024]{1,0:T(8,128)(2,1)S(1)}, bf16[32,1024]{1,0:T(8,128)(2,1)S(1)}, ...), branch_computations={%region_0.1_spmd, %region_1.2_spmd} | conditional | flops 2149580800 | bytes 25690344 | solution.py:213
  49.1 1.7 %collective-permute-start.5 = (bf16[128,1024]{1,0:T(8,128)(2,1)S(1)}, bf16[128,1024]{1,0:T(8,128)(2,1)S(1)}, u32[]{:S(2)}, u32[]{:S(2)}) collective-permute-start(bf16[128,1024]{1,0:T(8,128)(2,1)S(1)} %lay.2.refs_0_), channel_id=1, source_target_pairs={{0,2},{1,3},{2,0},{3,1},{4,6},{5,7},{6,4},{7,5},{8,10},{9,11},{10,... | collective-permute-start | bytes 786440 | tf_op jit(solution)/shard_map/cond/branch_1_fun/ppermute | solution.py:40
  50.8 1.2 collective-permute-start.4
  52.0 6.4 %collective-permute-done.5.refs_2_ = bf16[128,1024]{1,0:T(8,128)(2,1)S(1)} collective-permute-done((bf16[128,1024]{1,0:T(8,128)(2,1)S(1)}, bf16[128,1024]{1,0:T(8,128)(2,1)S(1)}, u32[]{:S(2)}, u32[]{:S(2)}) %collective-permute-start.5) | collective-permute-done | bytes 262176 | tf_op jit(solution)/shard_map/cond/branch_1_fun/ppermute | solution.py:40
  58.4 1.3 collective-permute-start.6
  59.6 4.0 %collective-permute-done.4.refs_1_ = bf16[128,1024]{1,0:T(8,128)(2,1)S(1)} collective-permute-done((bf16[128,1024]{1,0:T(8,128)(2,1)S(1)}, bf16[128,1024]{1,0:T(8,128)(2,1)S(1)}, u32[]{:S(2)}, u32[]{:S(2)}) %collective-permute-start.4) | collective-permute-done | bytes 262176 | tf_op jit(solution)/shard_map/cond/branch_1_fun/ppermute | solution.py:40
  63.8 5.0 %collective-permute-done.6.refs_3_ = bf16[128,1024]{1,0:T(8,128)(2,1)S(1)} collective-permute-done((bf16[128,1024]{1,0:T(8,128)(2,1)S(1)}, bf16[128,1024]{1,0:T(8,128)(2,1)S(1)}, u32[]{:S(2)}, u32[]{:S(2)}) %collective-permute-start.6) | collective-permute-done | bytes 262176 | tf_op jit(solution)/shard_map/cond/branch_1_fun/ppermute | solution.py:40
  68.9 2.2 %fetch.2.refs_6_ = bf16[2048,1024]{1,0:T(8,128)(2,1)S(1)} custom-call(bf16[2048,1024]{1,0:T(8,128)(2,1)} %get-tuple-element.25.weight_ref), custom_call_target="tpu_custom_call" | custom-call | bytes 8388608 | tf_op jit(solution)/shard_map/cond/branch_1_fun/fetch/pallas_call | solution.py:246
  71.2 4.6 %project.2 = (f32[512,256]{1,0:T(8,128)S(1)}, bf16[528,256]{1,0:T(8,128)(2,1)}, bf16[528,256]{1,0:T(8,128)(2,1)}, bf16[528,256]{1,0:T(8,128)(2,1)}) custom-call(s32[3]{0:T(128)S(1)} %get-tuple-element.18.place_ref, bf16[128,1024]{1,0:T(8,128)(2,1)S(1)} %lay.2.refs_0_, bf16[128,1024]{1,0:T(8,128)(2,1)S(1)} %collective-permute-done.4.refs_1_, ...), custom_call_target="tpu_custom_call" | custom-call | flops 2147483648 | bytes 7864320 | tf_op jit(solution)/shard_map/cond/branch_1_fun/project/pallas_call | solution.py:340
  75.8 1.4 collective-permute-start.28
  77.2 2.3 %collective-permute-start.29 = (bf16[528,256]{1,0:T(8,128)(2,1)}, bf16[528,256]{1,0:T(8,128)(2,1)S(1)}, u32[]{:S(2)}, u32[]{:S(2)}) collective-permute-start(bf16[528,256]{1,0:T(8,128)(2,1)} %get-tuple-element.132), channel_id=1, source_target_pairs={{0,16},{1,17},{2,18},{3,19},{4,20},{5,21},{6,22},{7,23},{8,24},{9,... | collective-permute-start | bytes 811016 | tf_op jit(solution)/shard_map/ppermute | solution.py:40
  80.2 3.4 %normalize.2 = (f32[512,256]{1,0:T(8,128)S(1)}, bf16[512,256]{1,0:T(8,128)(2,1)S(1)}, f32[1,256]{1,0:T(1,128)S(1)}, f32[256,512]{1,0:T(8,128)}, f32[256,512]{1,0:T(8,128)}) custom-call(s32[3]{0:T(128)S(1)} %pad_add_fusion.place_ref, f32[512,256]{1,0:T(8,128)S(1)} %get-tuple-element.134.refs_0_, bf16[528,256]{1,0:T(8,128)(2,1)S(1)} %collective-permute-done.31.refs_1_, ...), custom_call_target="tpu_custom_call" | custom-call | flops 134217728 | bytes 3145728 | tf_op jit(solution)/shard_map/normalize/pallas_call | solution.py:420
  83.6 13.6 %conditional.3 = ((f32[16,384]{1,0:T(8,128)S(1)}, f32[16,384]{1,0:T(8,128)S(1)}, f32[16,384]{1,0:T(8,128)S(1)}, f32[16,384]{1,0:T(8,128)S(1)})) conditional(s32[]{:T(128)} %convert_element_type.4, () %tuple.38, (f32[256,512]{1,0:T(8,128)}, s32[3]{0:T(128)S(1)}, f32[256,512]{1,0:T(8,128)}) %tuple.39), branch_computations={%region_2.3_spmd, %region_3.4_spmd} | conditional | bytes 2834600 | solution.py:213
  83.6 2.1 %collective-permute-done.met_ref = f32[256,512]{1,0:T(8,128)S(1)} collective-permute-done((f32[256,512]{1,0:T(8,128)}, f32[256,512]{1,0:T(8,128)S(1)}, u32[]{:S(2)}, u32[]{:S(2)}) %collective-permute-start) | collective-permute-done | bytes 524320 | tf_op jit(solution)/shard_map/cond/branch_1_fun/ppermute | solution.py:40
  85.7 1.3 halve.2
  87.0 1.5 collective-permute-start.1
  88.5 0.8 collective-permute-start.2
  89.3 2.0 %collective-permute-done.1.refs_1_ = bf16[80,384]{1,0:T(8,128)(2,1)S(1)} collective-permute-done((bf16[80,384]{1,0:T(8,128)(2,1)S(1)}, bf16[80,384]{1,0:T(8,128)(2,1)S(1)}, u32[]{:S(2)}, u32[]{:S(2)}) %collective-permute-start.1) | collective-permute-done | bytes 61472 | tf_op jit(solution)/shard_map/cond/branch_1_fun/ppermute | solution.py:40
  91.3 1.6 %collective-permute-start.3 = (bf16[80,384]{1,0:T(8,128)(2,1)S(1)}, bf16[80,384]{1,0:T(8,128)(2,1)S(1)}, u32[]{:S(2)}, u32[]{:S(2)}) collective-permute-start(bf16[80,384]{1,0:T(8,128)(2,1)S(1)} %get-tuple-element.38), channel_id=1, source_target_pairs={{0,6},{1,7},{2,4},{3,5},{4,2},{5,3},{6,0},{7,1},{8,14},{9,15},{10,... | collective-permute-start | bytes 184328 | tf_op jit(solution)/shard_map/cond/branch_1_fun/ppermute | solution.py:40
  92.9 3.5 %collective-permute-done.3.refs_3_ = bf16[80,384]{1,0:T(8,128)(2,1)S(1)} collective-permute-done((bf16[80,384]{1,0:T(8,128)(2,1)S(1)}, bf16[80,384]{1,0:T(8,128)(2,1)S(1)}, u32[]{:S(2)}, u32[]{:S(2)}) %collective-permute-start.3) | collective-permute-done | bytes 61472 | tf_op jit(solution)/shard_map/cond/branch_1_fun/ppermute | solution.py:40
  96.4 0.8 plane.1
  97.8 3.2 %collective-permute-start.35 = (f32[16,384]{1,0:T(8,128)S(1)}, f32[16,384]{1,0:T(8,128)S(1)}, u32[]{:S(2)}, u32[]{:S(2)}) collective-permute-start(f32[16,384]{1,0:T(8,128)S(1)} %get-tuple-element.142), channel_id=1, source_target_pairs={{0,16},{1,17},{2,18},{3,19},{4,20},{5,21},{6,22},{7,23},{8,24},{9,... | collective-permute-start | bytes 73736 | tf_op jit(solution)/shard_map/ppermute | solution.py:40
  101.7 4.2 %collective-permute-done.35.refs_2_ = f32[16,384]{1,0:T(8,128)S(1)} collective-permute-done((f32[16,384]{1,0:T(8,128)S(1)}, f32[16,384]{1,0:T(8,128)S(1)}, u32[]{:S(2)}, u32[]{:S(2)}) %collective-permute-start.35) | collective-permute-done | bytes 24608 | tf_op jit(solution)/shard_map/ppermute | solution.py:40
  105.9 0.8 collective-permute-done.36.refs_3_
  106.6 2.6 %normalize.3 = (f32[512,256]{1,0:T(8,128)S(1)}, bf16[512,256]{1,0:T(8,128)(2,1)S(1)}, f32[1,256]{1,0:T(1,128)S(1)}, f32[256,512]{1,0:T(8,128)S(1)}, f32[256,512]{1,0:T(8,128)S(1)}, /*index=5*/f32[1,256]{1,0:T(1,128)S(1)}) custom-call(s32[3]{0:T(128)S(1)} %pad_add_fusion.place_ref, f32[512,256]{1,0:T(8,128)S(1)} %get-tuple-element.144.refs_0_, ...), custom_call_target="tpu_custom_call" | custom-call | flops 134217728 | bytes 3145728 | tf_op jit(solution)/shard_map/normalize/pallas_call | solution.py:420
  109.3 1.9 %collective-permute-done.37.met_ref = f32[256,512]{1,0:T(8,128)S(1)} collective-permute-done((f32[256,512]{1,0:T(8,128)S(1)}, f32[256,512]{1,0:T(8,128)S(1)}, u32[]{:S(2)}, u32[]{:S(2)}) %collective-permute-start.37) | collective-permute-done | bytes 524320 | tf_op jit(solution)/shard_map/ppermute | solution.py:40
  111.2 0.8 halve.3
  112.0 1.5 collective-permute-start.38
  113.6 2.0 %collective-permute-start.40 = (bf16[80,384]{1,0:T(8,128)(2,1)S(1)}, bf16[80,384]{1,0:T(8,128)(2,1)S(1)}, u32[]{:S(2)}, u32[]{:S(2)}) collective-permute-start(bf16[80,384]{1,0:T(8,128)(2,1)S(1)} %get-tuple-element.154), channel_id=1, source_target_pairs={{0,6},{1,7},{2,4},{3,5},{4,2},{5,3},{6,0},{7,1},{8,14},{9,15},{10,... | collective-permute-start | bytes 184328 | tf_op jit(solution)/shard_map/ppermute | solution.py:40
  116.3 2.6 %collective-permute-done.39.refs_2_ = bf16[80,384]{1,0:T(8,128)(2,1)S(1)} collective-permute-done((bf16[80,384]{1,0:T(8,128)(2,1)S(1)}, bf16[80,384]{1,0:T(8,128)(2,1)S(1)}, u32[]{:S(2)}, u32[]{:S(2)}) %collective-permute-start.39) | collective-permute-done | bytes 61472 | tf_op jit(solution)/shard_map/ppermute | solution.py:40
  118.9 0.8 code.1.refs_0_
  119.7 1.9 %collective-permute-start.43 = (bf16[96,384]{1,0:T(8,128)(2,1)S(1)}, bf16[96,384]{1,0:T(8,128)(2,1)S(1)}, u32[]{:S(2)}, u32[]{:S(2)}) collective-permute-start(bf16[96,384]{1,0:T(8,128)(2,1)S(1)} %code.1.refs_0_), channel_id=1, source_target_pairs={{0,24},{1,25},{2,26},{3,27},{4,28},{5,29},{6,30},{7,31},{8,16},{9,... | collective-permute-start | bytes 221192 | tf_op jit(solution)/shard_map/ppermute | solution.py:40
  121.6 2.5 %collective-permute-start.41 = (bf16[96,384]{1,0:T(8,128)(2,1)S(1)}, bf16[96,384]{1,0:T(8,128)(2,1)S(1)}, u32[]{:S(2)}, u32[]{:S(2)}) collective-permute-start(bf16[96,384]{1,0:T(8,128)(2,1)S(1)} %code.1.refs_0_), channel_id=1, source_target_pairs={{0,8},{1,9},{2,10},{3,11},{4,12},{5,13},{6,14},{7,15},{8,0},{9,1},... | collective-permute-start | bytes 221192 | tf_op jit(solution)/shard_map/ppermute | solution.py:40
  124.2 2.0 %collective-permute-done.43.refs_3_ = bf16[96,384]{1,0:T(8,128)(2,1)S(1)} collective-permute-done((bf16[96,384]{1,0:T(8,128)(2,1)S(1)}, bf16[96,384]{1,0:T(8,128)(2,1)S(1)}, u32[]{:S(2)}, u32[]{:S(2)}) %collective-permute-start.43) | collective-permute-done | bytes 73760 | tf_op jit(solution)/shard_map/ppermute | solution.py:40
  126.2 2.1 %collective-permute-done.42.refs_2_ = bf16[96,384]{1,0:T(8,128)(2,1)S(1)} collective-permute-done((bf16[96,384]{1,0:T(8,128)(2,1)S(1)}, bf16[96,384]{1,0:T(8,128)(2,1)S(1)}, u32[]{:S(2)}, u32[]{:S(2)}) %collective-permute-start.42) | collective-permute-done | bytes 73760 | tf_op jit(solution)/shard_map/ppermute | solution.py:40
  128.2 0.9 finish.1.refs_0_
  129.2 1.8 %collective-permute-start.46 = (bf16[128,384]{1,0:T(8,128)(2,1)S(1)}, bf16[128,384]{1,0:T(8,128)(2,1)S(1)}, u32[]{:S(2)}, u32[]{:S(2)}) collective-permute-start(bf16[128,384]{1,0:T(8,128)(2,1)S(1)} %finish.1.refs_0_), channel_id=1, source_target_pairs={{0,6},{1,7},{2,4},{3,5},{4,2},{5,3},{6,0},{7,1},{8,14},{9,15},{10,... | collective-permute-start | bytes 294920 | tf_op jit(solution)/shard_map/ppermute | solution.py:40
  131.3 1.4 collective-permute-start.44
  132.7 3.0 %collective-permute-done.46.refs_3_ = bf16[128,384]{1,0:T(8,128)(2,1)S(1)} collective-permute-done((bf16[128,384]{1,0:T(8,128)(2,1)S(1)}, bf16[128,384]{1,0:T(8,128)(2,1)S(1)}, u32[]{:S(2)}, u32[]{:S(2)}) %collective-permute-start.46) | collective-permute-done | bytes 98336 | tf_op jit(solution)/shard_map/ppermute | solution.py:40
  137.9 2.2 %gradient.1 = (bf16[256,256]{1,0:T(8,128)(2,1)S(1)}, bf16[256,256]{1,0:T(8,128)(2,1)S(1)}, bf16[256,256]{1,0:T(8,128)(2,1)S(1)}, bf16[256,256]{1,0:T(8,128)(2,1)S(1)}, f32[1,1]{1,0:T(1,128)}) custom-call(s32[3]{0:T(128)S(1)} %pad_add_fusion.place_ref, bf16[128,384]{1,0:T(8,128)(2,1)S(1)} %finish.1.refs_0_, ...), custom_call_target="tpu_custom_call" | custom-call | tf_op jit(solution)/shard_map/gradient/pallas_call | solution.py:172
  140.1 1.7 %collective-permute-start.51 = (bf16[256,256]{1,0:T(8,128)(2,1)S(1)}, bf16[256,256]{1,0:T(8,128)(2,1)S(1)}, u32[]{:S(2)}, u32[]{:S(2)}) collective-permute-start(bf16[256,256]{1,0:T(8,128)(2,1)S(1)} %get-tuple-element.166), channel_id=1, source_target_pairs={{0,24},{1,25},{2,26},{3,27},{4,28},{5,29},{6,30},{7,31},{8,16},{9,... | collective-permute-start | bytes 393224 | tf_op jit(solution)/shard_map/ppermute | solution.py:40
  141.8 2.7 %collective-permute-start.53 = (bf16[256,256]{1,0:T(8,128)(2,1)S(1)}, bf16[256,256]{1,0:T(8,128)(2,1)S(1)}, u32[]{:S(2)}, u32[]{:S(2)}) collective-permute-start(bf16[256,256]{1,0:T(8,128)(2,1)S(1)} %get-tuple-element.168), channel_id=1, source_target_pairs={{0,8},{1,9},{2,10},{3,11},{4,12},{5,13},{6,14},{7,15},{8,0},{9,1},... | collective-permute-start | bytes 393224 | tf_op jit(solution)/shard_map/ppermute | solution.py:40
  144.5 3.9 %collective-permute-done.51.refs_1_ = bf16[256,256]{1,0:T(8,128)(2,1)S(1)} collective-permute-done((bf16[256,256]{1,0:T(8,128)(2,1)S(1)}, bf16[256,256]{1,0:T(8,128)(2,1)S(1)}, u32[]{:S(2)}, u32[]{:S(2)}) %collective-permute-start.51) | collective-permute-done | bytes 131104 | tf_op jit(solution)/shard_map/ppermute | solution.py:40
  148.4 5.0 %collective-permute-done.52.refs_2_ = bf16[256,256]{1,0:T(8,128)(2,1)S(1)} collective-permute-done((bf16[256,256]{1,0:T(8,128)(2,1)S(1)}, bf16[256,256]{1,0:T(8,128)(2,1)S(1)}, u32[]{:S(2)}, u32[]{:S(2)}) %collective-permute-start.52) | collective-permute-done | bytes 131104 | tf_op jit(solution)/shard_map/ppermute | solution.py:40
  153.4 1.4 place.1
  (69 shorter events, 11.9 us)
Async XLA Ops:
  1.6 6.2 %collective-permute-start.11 = (bf16[32,1024]{1,0:T(8,128)(2,1)S(1)}, bf16[32,1024]{1,0:T(8,128)(2,1)S(1)}, u32[]{:S(2)}, u32[]{:S(2)}) collective-permute-start(bf16[32,1024]{1,0:T(8,128)(2,1)S(1)} %get-tuple-element.183), channel_id=1, source_target_pairs={{0,6},{1,7},{2,4},{3,5},{4,2},{5,3},{6,0},{7,1},{8,14},{9,15},{10,... | collective-permute-start | bytes 196616 | tf_op jit(solution)/shard_map/ppermute | solution.py:40
  5.6 4.3 %collective-permute-start.10 = (bf16[32,1024]{1,0:T(8,128)(2,1)S(1)}, bf16[32,1024]{1,0:T(8,128)(2,1)S(1)}, u32[]{:S(2)}, u32[]{:S(2)}) collective-permute-start(bf16[32,1024]{1,0:T(8,128)(2,1)S(1)} %get-tuple-element.184), channel_id=1, source_target_pairs={{0,4},{1,5},{2,6},{3,7},{4,0},{5,1},{6,2},{7,3},{8,12},{9,13},{10,... | collective-permute-start | bytes 196616 | tf_op jit(solution)/shard_map/ppermute | solution.py:40
  6.1 4.3 %collective-permute-start.9 = (bf16[32,1024]{1,0:T(8,128)(2,1)S(1)}, bf16[32,1024]{1,0:T(8,128)(2,1)S(1)}, u32[]{:S(2)}, u32[]{:S(2)}) collective-permute-start(bf16[32,1024]{1,0:T(8,128)(2,1)S(1)} %get-tuple-element.185), channel_id=1, source_target_pairs={{0,2},{1,3},{2,0},{3,1},{4,6},{5,7},{6,4},{7,5},{8,10},{9,11},{10,... | collective-permute-start | bytes 196616 | tf_op jit(solution)/shard_map/ppermute | solution.py:40
  10.4 7.5 %collective-permute-start.14 = (bf16[32,1024]{1,0:T(8,128)(2,1)S(1)}, bf16[32,1024]{1,0:T(8,128)(2,1)S(1)}, u32[]{:S(2)}, u32[]{:S(2)}) collective-permute-start(bf16[32,1024]{1,0:T(8,128)(2,1)S(1)} %get-tuple-element.179), channel_id=1, source_target_pairs={{0,24},{1,25},{2,26},{3,27},{4,28},{5,29},{6,30},{7,31},{8,16},{9,... | collective-permute-start | bytes 196616 | tf_op jit(solution)/shard_map/ppermute | solution.py:40
  14.1 5.3 %collective-permute-start.12 = (bf16[32,1024]{1,0:T(8,128)(2,1)S(1)}, bf16[32,1024]{1,0:T(8,128)(2,1)S(1)}, u32[]{:S(2)}, u32[]{:S(2)}) collective-permute-start(bf16[32,1024]{1,0:T(8,128)(2,1)S(1)} %get-tuple-element.180), channel_id=1, source_target_pairs={{0,8},{1,9},{2,10},{3,11},{4,12},{5,13},{6,14},{7,15},{8,0},{9,1},... | collective-permute-start | bytes 196616 | tf_op jit(solution)/shard_map/ppermute | solution.py:40
  14.1 5.3 %collective-permute-start.13 = (bf16[32,1024]{1,0:T(8,128)(2,1)S(1)}, bf16[32,1024]{1,0:T(8,128)(2,1)S(1)}, u32[]{:S(2)}, u32[]{:S(2)}) collective-permute-start(bf16[32,1024]{1,0:T(8,128)(2,1)S(1)} %get-tuple-element.181), channel_id=1, source_target_pairs={{0,16},{1,17},{2,18},{3,19},{4,20},{5,21},{6,22},{7,23},{8,24},{9,... | collective-permute-start | bytes 196616 | tf_op jit(solution)/shard_map/ppermute | solution.py:40
  15.8 6.2 %collective-permute-start.20 = (bf16[32,1024]{1,0:T(8,128)(2,1)S(1)}, bf16[32,1024]{1,0:T(8,128)(2,1)S(1)}, u32[]{:S(2)}, u32[]{:S(2)}) collective-permute-start(bf16[32,1024]{1,0:T(8,128)(2,1)S(1)} %get-tuple-element.176), channel_id=1, source_target_pairs={{0,2},{1,3},{2,0},{3,1},{4,6},{5,7},{6,4},{7,5},{8,10},{9,11},{10,... | collective-permute-start | bytes 196616 | tf_op jit(solution)/shard_map/ppermute | solution.py:40
  16.3 7.2 %collective-permute-start.19 = (bf16[32,1024]{1,0:T(8,128)(2,1)S(1)}, bf16[32,1024]{1,0:T(8,128)(2,1)S(1)}, u32[]{:S(2)}, u32[]{:S(2)}) collective-permute-start(bf16[32,1024]{1,0:T(8,128)(2,1)S(1)} %get-tuple-element.177), channel_id=1, source_target_pairs={{0,4},{1,5},{2,6},{3,7},{4,0},{5,1},{6,2},{7,3},{8,12},{9,13},{10,... | collective-permute-start | bytes 196616 | tf_op jit(solution)/shard_map/ppermute | solution.py:40
  17.9 6.0 %collective-permute-start.18 = (bf16[32,1024]{1,0:T(8,128)(2,1)S(1)}, bf16[32,1024]{1,0:T(8,128)(2,1)S(1)}, u32[]{:S(2)}, u32[]{:S(2)}) collective-permute-start(bf16[32,1024]{1,0:T(8,128)(2,1)S(1)} %get-tuple-element.178), channel_id=1, source_target_pairs={{0,6},{1,7},{2,4},{3,5},{4,2},{5,3},{6,0},{7,1},{8,14},{9,15},{10,... | collective-permute-start | bytes 196616 | tf_op jit(solution)/shard_map/ppermute | solution.py:40
  20.0 17.4 %collective-permute-start.17 = (bf16[128,1024]{1,0:T(8,128)(2,1)S(1)}, bf16[128,1024]{1,0:T(8,128)(2,1)S(1)}, u32[]{:S(2)}, u32[]{:S(2)}) collective-permute-start(bf16[128,1024]{1,0:T(8,128)(2,1)S(1)} %lay.3.refs_0_), channel_id=1, source_target_pairs={{0,6},{1,7},{2,4},{3,5},{4,2},{5,3},{6,0},{7,1},{8,14},{9,15},{10,... | collective-permute-start | bytes 786440 | tf_op jit(solution)/shard_map/ppermute | solution.py:40
  21.5 15.9 %collective-permute-start.16 = (bf16[128,1024]{1,0:T(8,128)(2,1)S(1)}, bf16[128,1024]{1,0:T(8,128)(2,1)S(1)}, u32[]{:S(2)}, u32[]{:S(2)}) collective-permute-start(bf16[128,1024]{1,0:T(8,128)(2,1)S(1)} %lay.3.refs_0_), channel_id=1, source_target_pairs={{0,4},{1,5},{2,6},{3,7},{4,0},{5,1},{6,2},{7,3},{8,12},{9,13},{10,... | collective-permute-start | bytes 786440 | tf_op jit(solution)/shard_map/ppermute | solution.py:40
  22.0 15.4 %collective-permute-start.15 = (bf16[128,1024]{1,0:T(8,128)(2,1)S(1)}, bf16[128,1024]{1,0:T(8,128)(2,1)S(1)}, u32[]{:S(2)}, u32[]{:S(2)}) collective-permute-start(bf16[128,1024]{1,0:T(8,128)(2,1)S(1)} %lay.3.refs_0_), channel_id=1, source_target_pairs={{0,2},{1,3},{2,0},{3,1},{4,6},{5,7},{6,4},{7,5},{8,10},{9,11},{10,... | collective-permute-start | bytes 786440 | tf_op jit(solution)/shard_map/ppermute | solution.py:40
  24.7 6.8 %collective-permute-start.23 = (bf16[32,1024]{1,0:T(8,128)(2,1)S(1)}, bf16[32,1024]{1,0:T(8,128)(2,1)S(1)}, u32[]{:S(2)}, u32[]{:S(2)}) collective-permute-start(bf16[32,1024]{1,0:T(8,128)(2,1)S(1)} %get-tuple-element.172), channel_id=1, source_target_pairs={{0,24},{1,25},{2,26},{3,27},{4,28},{5,29},{6,30},{7,31},{8,16},{9,... | collective-permute-start | bytes 196616 | tf_op jit(solution)/shard_map/ppermute | solution.py:40
  28.5 5.3 %collective-permute-start.21 = (bf16[32,1024]{1,0:T(8,128)(2,1)S(1)}, bf16[32,1024]{1,0:T(8,128)(2,1)S(1)}, u32[]{:S(2)}, u32[]{:S(2)}) collective-permute-start(bf16[32,1024]{1,0:T(8,128)(2,1)S(1)} %get-tuple-element.174), channel_id=1, source_target_pairs={{0,8},{1,9},{2,10},{3,11},{4,12},{5,13},{6,14},{7,15},{8,0},{9,1},... | collective-permute-start | bytes 196616 | tf_op jit(solution)/shard_map/ppermute | solution.py:40
  31.5 5.9 %collective-permute-start.22 = (bf16[32,1024]{1,0:T(8,128)(2,1)S(1)}, bf16[32,1024]{1,0:T(8,128)(2,1)S(1)}, u32[]{:S(2)}, u32[]{:S(2)}) collective-permute-start(bf16[32,1024]{1,0:T(8,128)(2,1)S(1)} %get-tuple-element.175), channel_id=1, source_target_pairs={{0,16},{1,17},{2,18},{3,19},{4,20},{5,21},{6,22},{7,23},{8,24},{9,... | collective-permute-start | bytes 196616 | tf_op jit(solution)/shard_map/ppermute | solution.py:40
  37.4 1.6 %collective-permute-start.24 = (bf16[128,1024]{1,0:T(8,128)(2,1)S(1)}, bf16[128,1024]{1,0:T(8,128)(2,1)S(1)}, u32[]{:S(2)}, u32[]{:S(2)}) collective-permute-start(bf16[128,1024]{1,0:T(8,128)(2,1)S(1)} %lay.3.refs_0_), channel_id=1, source_target_pairs={{0,1},{1,0},{2,3},{3,2},{4,5},{5,4},{6,7},{7,6},{8,9},{9,8},{10,11... | collective-permute-start | bytes 786440 | tf_op jit(solution)/shard_map/ppermute | solution.py:40
  37.5 1.9 %collective-permute-start.25 = (bf16[128,1024]{1,0:T(8,128)(2,1)S(1)}, bf16[128,1024]{1,0:T(8,128)(2,1)S(1)}, u32[]{:S(2)}, u32[]{:S(2)}) collective-permute-start(bf16[128,1024]{1,0:T(8,128)(2,1)S(1)} %collective-permute-done.15.refs_1_), channel_id=1, source_target_pairs={{0,1},{1,0},{2,3},{3,2},{4,5},{5,4},{6,7},{7,6},{8,9},{9,8},{10,11... | collective-permute-start | bytes 786440 | tf_op jit(solution)/shard_map/ppermute | solution.py:40
  38.0 1.8 %collective-permute-start.26 = (bf16[128,1024]{1,0:T(8,128)(2,1)S(1)}, bf16[128,1024]{1,0:T(8,128)(2,1)S(1)}, u32[]{:S(2)}, u32[]{:S(2)}) collective-permute-start(bf16[128,1024]{1,0:T(8,128)(2,1)S(1)} %collective-permute-done.16.refs_2_), channel_id=1, source_target_pairs={{0,1},{1,0},{2,3},{3,2},{4,5},{5,4},{6,7},{7,6},{8,9},{9,8},{10,11... | collective-permute-start | bytes 786440 | tf_op jit(solution)/shard_map/ppermute | solution.py:40
  38.1 2.1 %collective-permute-start.27 = (bf16[128,1024]{1,0:T(8,128)(2,1)S(1)}, bf16[128,1024]{1,0:T(8,128)(2,1)S(1)}, u32[]{:S(2)}, u32[]{:S(2)}) collective-permute-start(bf16[128,1024]{1,0:T(8,128)(2,1)S(1)} %collective-permute-done.17.refs_3_), channel_id=1, source_target_pairs={{0,1},{1,0},{2,3},{3,2},{4,5},{5,4},{6,7},{7,6},{8,9},{9,8},{10,11... | collective-permute-start | bytes 786440 | tf_op jit(solution)/shard_map/ppermute | solution.py:40
  44.0 35.5 %collective-permute-start.31 = (bf16[528,256]{1,0:T(8,128)(2,1)S(1)}, bf16[528,256]{1,0:T(8,128)(2,1)S(1)}, u32[]{:S(2)}, u32[]{:S(2)}) collective-permute-start(bf16[528,256]{1,0:T(8,128)(2,1)S(1)} %get-tuple-element.135), channel_id=1, source_target_pairs={{0,24},{1,25},{2,26},{3,27},{4,28},{5,29},{6,30},{7,31},{8,16},{9,... | collective-permute-start | bytes 811016 | tf_op jit(solution)/shard_map/ppermute | solution.py:40
  46.4 33.8 %collective-permute-start.32 = (bf16[528,256]{1,0:T(8,128)(2,1)S(1)}, bf16[528,256]{1,0:T(8,128)(2,1)S(1)}, u32[]{:S(2)}, u32[]{:S(2)}) collective-permute-start(bf16[528,256]{1,0:T(8,128)(2,1)S(1)} %get-tuple-element.136), channel_id=1, source_target_pairs={{0,16},{1,17},{2,18},{3,19},{4,20},{5,21},{6,22},{7,23},{8,24},{9,... | collective-permute-start | bytes 811016 | tf_op jit(solution)/shard_map/ppermute | solution.py:40
  46.4 33.8 %collective-permute-start.33 = (bf16[528,256]{1,0:T(8,128)(2,1)S(1)}, bf16[528,256]{1,0:T(8,128)(2,1)S(1)}, u32[]{:S(2)}, u32[]{:S(2)}) collective-permute-start(bf16[528,256]{1,0:T(8,128)(2,1)S(1)} %get-tuple-element.137), channel_id=1, source_target_pairs={{0,8},{1,9},{2,10},{3,11},{4,12},{5,13},{6,14},{7,15},{8,0},{9,1},... | collective-permute-start | bytes 811016 | tf_op jit(solution)/shard_map/ppermute | solution.py:40
  49.1 9.3 %collective-permute-start.5 = (bf16[128,1024]{1,0:T(8,128)(2,1)S(1)}, bf16[128,1024]{1,0:T(8,128)(2,1)S(1)}, u32[]{:S(2)}, u32[]{:S(2)}) collective-permute-start(bf16[128,1024]{1,0:T(8,128)(2,1)S(1)} %lay.2.refs_0_), channel_id=1, source_target_pairs={{0,2},{1,3},{2,0},{3,1},{4,6},{5,7},{6,4},{7,5},{8,10},{9,11},{10,... | collective-permute-start | bytes 786440 | tf_op jit(solution)/shard_map/cond/branch_1_fun/ppermute | solution.py:40
  50.8 12.9 %collective-permute-start.4 = (bf16[128,1024]{1,0:T(8,128)(2,1)S(1)}, bf16[128,1024]{1,0:T(8,128)(2,1)S(1)}, u32[]{:S(2)}, u32[]{:S(2)}) collective-permute-start(bf16[128,1024]{1,0:T(8,128)(2,1)S(1)} %lay.2.refs_0_), channel_id=1, source_target_pairs={{0,6},{1,7},{2,4},{3,5},{4,2},{5,3},{6,0},{7,1},{8,14},{9,15},{10,... | collective-permute-start | bytes 786440 | tf_op jit(solution)/shard_map/cond/branch_1_fun/ppermute | solution.py:40
  58.4 10.5 %collective-permute-start.6 = (bf16[128,1024]{1,0:T(8,128)(2,1)S(1)}, bf16[128,1024]{1,0:T(8,128)(2,1)S(1)}, u32[]{:S(2)}, u32[]{:S(2)}) collective-permute-start(bf16[128,1024]{1,0:T(8,128)(2,1)S(1)} %lay.2.refs_0_), channel_id=1, source_target_pairs={{0,4},{1,5},{2,6},{3,7},{4,0},{5,1},{6,2},{7,3},{8,12},{9,13},{10,... | collective-permute-start | bytes 786440 | tf_op jit(solution)/shard_map/cond/branch_1_fun/ppermute | solution.py:40
  63.7 7.4 %collective-permute-start.7 = (bf16[256,1024]{1,0:T(8,128)(2,1)S(1)}, bf16[256,1024]{1,0:T(8,128)(2,1)S(1)}, u32[]{:S(2)}, u32[]{:S(2)}) collective-permute-start(bf16[256,1024]{1,0:T(8,128)(2,1)S(1)} %pad_maximum_fusion), channel_id=1, source_target_pairs={{0,1},{1,0},{2,3},{3,2},{4,5},{5,4},{6,7},{7,6},{8,9},{9,8},{10,11... | collective-permute-start | bytes 1572872 | tf_op jit(solution)/shard_map/cond/branch_1_fun/ppermute | solution.py:40
  68.9 2.3 %collective-permute-start.8 = (bf16[256,1024]{1,0:T(8,128)(2,1)S(1)}, bf16[256,1024]{1,0:T(8,128)(2,1)S(1)}, u32[]{:S(2)}, u32[]{:S(2)}) collective-permute-start(bf16[256,1024]{1,0:T(8,128)(2,1)S(1)} %pad_maximum_fusion.1), channel_id=1, source_target_pairs={{0,1},{1,0},{2,3},{3,2},{4,5},{5,4},{6,7},{7,6},{8,9},{9,8},{10,11... | collective-permute-start | bytes 1572872 | tf_op jit(solution)/shard_map/cond/branch_1_fun/ppermute | solution.py:40
  75.8 25.2 %collective-permute-start.28 = (bf16[528,256]{1,0:T(8,128)(2,1)}, bf16[528,256]{1,0:T(8,128)(2,1)S(1)}, u32[]{:S(2)}, u32[]{:S(2)}) collective-permute-start(bf16[528,256]{1,0:T(8,128)(2,1)} %get-tuple-element.131), channel_id=1, source_target_pairs={{0,8},{1,9},{2,10},{3,11},{4,12},{5,13},{6,14},{7,15},{8,0},{9,1},... | collective-permute-start | bytes 811016 | tf_op jit(solution)/shard_map/ppermute | solution.py:40
  77.2 24.5 %collective-permute-start.29 = (bf16[528,256]{1,0:T(8,128)(2,1)}, bf16[528,256]{1,0:T(8,128)(2,1)S(1)}, u32[]{:S(2)}, u32[]{:S(2)}) collective-permute-start(bf16[528,256]{1,0:T(8,128)(2,1)} %get-tuple-element.132), channel_id=1, source_target_pairs={{0,16},{1,17},{2,18},{3,19},{4,20},{5,21},{6,22},{7,23},{8,24},{9,... | collective-permute-start | bytes 811016 | tf_op jit(solution)/shard_map/ppermute | solution.py:40
  79.5 22.2 %collective-permute-start.30 = (bf16[528,256]{1,0:T(8,128)(2,1)}, bf16[528,256]{1,0:T(8,128)(2,1)S(1)}, u32[]{:S(2)}, u32[]{:S(2)}) collective-permute-start(bf16[528,256]{1,0:T(8,128)(2,1)} %get-tuple-element.133), channel_id=1, source_target_pairs={{0,24},{1,25},{2,26},{3,27},{4,28},{5,29},{6,30},{7,31},{8,16},{9,... | collective-permute-start | bytes 811016 | tf_op jit(solution)/shard_map/ppermute | solution.py:40
  83.6 2.1 %collective-permute-start = (f32[256,512]{1,0:T(8,128)}, f32[256,512]{1,0:T(8,128)S(1)}, u32[]{:S(2)}, u32[]{:S(2)}) collective-permute-start(f32[256,512]{1,0:T(8,128)} %get-tuple-element.32), channel_id=1, source_target_pairs={{0,1},{1,0},{2,3},{3,2},{4,5},{5,4},{6,7},{7,6},{8,9},{9,8},{10,11... | collective-permute-start | bytes 1572872 | tf_op jit(solution)/shard_map/cond/branch_1_fun/ppermute | solution.py:40
  87.0 4.3 %collective-permute-start.1 = (bf16[80,384]{1,0:T(8,128)(2,1)S(1)}, bf16[80,384]{1,0:T(8,128)(2,1)S(1)}, u32[]{:S(2)}, u32[]{:S(2)}) collective-permute-start(bf16[80,384]{1,0:T(8,128)(2,1)S(1)} %get-tuple-element.34), channel_id=1, source_target_pairs={{0,2},{1,3},{2,0},{3,1},{4,6},{5,7},{6,4},{7,5},{8,10},{9,11},{10,... | collective-permute-start | bytes 184328 | tf_op jit(solution)/shard_map/cond/branch_1_fun/ppermute | solution.py:40
  88.5 4.4 %collective-permute-start.2 = (bf16[80,384]{1,0:T(8,128)(2,1)S(1)}, bf16[80,384]{1,0:T(8,128)(2,1)S(1)}, u32[]{:S(2)}, u32[]{:S(2)}) collective-permute-start(bf16[80,384]{1,0:T(8,128)(2,1)S(1)} %get-tuple-element.37), channel_id=1, source_target_pairs={{0,4},{1,5},{2,6},{3,7},{4,0},{5,1},{6,2},{7,3},{8,12},{9,13},{10,... | collective-permute-start | bytes 184328 | tf_op jit(solution)/shard_map/cond/branch_1_fun/ppermute | solution.py:40
  91.3 5.1 %collective-permute-start.3 = (bf16[80,384]{1,0:T(8,128)(2,1)S(1)}, bf16[80,384]{1,0:T(8,128)(2,1)S(1)}, u32[]{:S(2)}, u32[]{:S(2)}) collective-permute-start(bf16[80,384]{1,0:T(8,128)(2,1)S(1)} %get-tuple-element.38), channel_id=1, source_target_pairs={{0,6},{1,7},{2,4},{3,5},{4,2},{5,3},{6,0},{7,1},{8,14},{9,15},{10,... | collective-permute-start | bytes 184328 | tf_op jit(solution)/shard_map/cond/branch_1_fun/ppermute | solution.py:40
  97.2 4.5 %collective-permute-start.34 = (f32[16,384]{1,0:T(8,128)S(1)}, f32[16,384]{1,0:T(8,128)S(1)}, u32[]{:S(2)}, u32[]{:S(2)}) collective-permute-start(f32[16,384]{1,0:T(8,128)S(1)} %get-tuple-element.141), channel_id=1, source_target_pairs={{0,8},{1,9},{2,10},{3,11},{4,12},{5,13},{6,14},{7,15},{8,0},{9,1},... | collective-permute-start | bytes 73736 | tf_op jit(solution)/shard_map/ppermute | solution.py:40
  97.8 8.1 %collective-permute-start.35 = (f32[16,384]{1,0:T(8,128)S(1)}, f32[16,384]{1,0:T(8,128)S(1)}, u32[]{:S(2)}, u32[]{:S(2)}) collective-permute-start(f32[16,384]{1,0:T(8,128)S(1)} %get-tuple-element.142), channel_id=1, source_target_pairs={{0,16},{1,17},{2,18},{3,19},{4,20},{5,21},{6,22},{7,23},{8,24},{9,... | collective-permute-start | bytes 73736 | tf_op jit(solution)/shard_map/ppermute | solution.py:40
  101.0 5.6 %collective-permute-start.36 = (f32[16,384]{1,0:T(8,128)S(1)}, f32[16,384]{1,0:T(8,128)S(1)}, u32[]{:S(2)}, u32[]{:S(2)}) collective-permute-start(f32[16,384]{1,0:T(8,128)S(1)} %get-tuple-element.143), channel_id=1, source_target_pairs={{0,24},{1,25},{2,26},{3,27},{4,28},{5,29},{6,30},{7,31},{8,16},{9,... | collective-permute-start | bytes 73736 | tf_op jit(solution)/shard_map/ppermute | solution.py:40
  109.3 2.0 %collective-permute-start.37 = (f32[256,512]{1,0:T(8,128)S(1)}, f32[256,512]{1,0:T(8,128)S(1)}, u32[]{:S(2)}, u32[]{:S(2)}) collective-permute-start(f32[256,512]{1,0:T(8,128)S(1)} %get-tuple-element.150), channel_id=1, source_target_pairs={{0,1},{1,0},{2,3},{3,2},{4,5},{5,4},{6,7},{7,6},{8,9},{9,8},{10,11... | collective-permute-start | bytes 1572872 | tf_op jit(solution)/shard_map/ppermute | solution.py:40
  112.0 4.3 %collective-permute-start.38 = (bf16[80,384]{1,0:T(8,128)(2,1)S(1)}, bf16[80,384]{1,0:T(8,128)(2,1)S(1)}, u32[]{:S(2)}, u32[]{:S(2)}) collective-permute-start(bf16[80,384]{1,0:T(8,128)(2,1)S(1)} %get-tuple-element.152), channel_id=1, source_target_pairs={{0,2},{1,3},{2,0},{3,1},{4,6},{5,7},{6,4},{7,5},{8,10},{9,11},{10,... | collective-permute-start | bytes 184328 | tf_op jit(solution)/shard_map/ppermute | solution.py:40
  113.6 5.3 %collective-permute-start.39 = (bf16[80,384]{1,0:T(8,128)(2,1)S(1)}, bf16[80,384]{1,0:T(8,128)(2,1)S(1)}, u32[]{:S(2)}, u32[]{:S(2)}) collective-permute-start(bf16[80,384]{1,0:T(8,128)(2,1)S(1)} %get-tuple-element.153), channel_id=1, source_target_pairs={{0,4},{1,5},{2,6},{3,7},{4,0},{5,1},{6,2},{7,3},{8,12},{9,13},{10,... | collective-permute-start | bytes 184328 | tf_op jit(solution)/shard_map/ppermute | solution.py:40
  113.6 5.3 %collective-permute-start.40 = (bf16[80,384]{1,0:T(8,128)(2,1)S(1)}, bf16[80,384]{1,0:T(8,128)(2,1)S(1)}, u32[]{:S(2)}, u32[]{:S(2)}) collective-permute-start(bf16[80,384]{1,0:T(8,128)(2,1)S(1)} %get-tuple-element.154), channel_id=1, source_target_pairs={{0,6},{1,7},{2,4},{3,5},{4,2},{5,3},{6,0},{7,1},{8,14},{9,15},{10,... | collective-permute-start | bytes 184328 | tf_op jit(solution)/shard_map/ppermute | solution.py:40
  119.7 6.5 %collective-permute-start.43 = (bf16[96,384]{1,0:T(8,128)(2,1)S(1)}, bf16[96,384]{1,0:T(8,128)(2,1)S(1)}, u32[]{:S(2)}, u32[]{:S(2)}) collective-permute-start(bf16[96,384]{1,0:T(8,128)(2,1)S(1)} %code.1.refs_0_), channel_id=1, source_target_pairs={{0,24},{1,25},{2,26},{3,27},{4,28},{5,29},{6,30},{7,31},{8,16},{9,... | collective-permute-start | bytes 221192 | tf_op jit(solution)/shard_map/ppermute | solution.py:40
  121.6 6.6 %collective-permute-start.42 = (bf16[96,384]{1,0:T(8,128)(2,1)S(1)}, bf16[96,384]{1,0:T(8,128)(2,1)S(1)}, u32[]{:S(2)}, u32[]{:S(2)}) collective-permute-start(bf16[96,384]{1,0:T(8,128)(2,1)S(1)} %code.1.refs_0_), channel_id=1, source_target_pairs={{0,16},{1,17},{2,18},{3,19},{4,20},{5,21},{6,22},{7,23},{8,24},{9,... | collective-permute-start | bytes 221192 | tf_op jit(solution)/shard_map/ppermute | solution.py:40
  121.6 6.6 %collective-permute-start.41 = (bf16[96,384]{1,0:T(8,128)(2,1)S(1)}, bf16[96,384]{1,0:T(8,128)(2,1)S(1)}, u32[]{:S(2)}, u32[]{:S(2)}) collective-permute-start(bf16[96,384]{1,0:T(8,128)(2,1)S(1)} %code.1.refs_0_), channel_id=1, source_target_pairs={{0,8},{1,9},{2,10},{3,11},{4,12},{5,13},{6,14},{7,15},{8,0},{9,1},... | collective-permute-start | bytes 221192 | tf_op jit(solution)/shard_map/ppermute | solution.py:40
  129.2 6.5 %collective-permute-start.46 = (bf16[128,384]{1,0:T(8,128)(2,1)S(1)}, bf16[128,384]{1,0:T(8,128)(2,1)S(1)}, u32[]{:S(2)}, u32[]{:S(2)}) collective-permute-start(bf16[128,384]{1,0:T(8,128)(2,1)S(1)} %finish.1.refs_0_), channel_id=1, source_target_pairs={{0,6},{1,7},{2,4},{3,5},{4,2},{5,3},{6,0},{7,1},{8,14},{9,15},{10,... | collective-permute-start | bytes 294920 | tf_op jit(solution)/shard_map/ppermute | solution.py:40
  131.0 5.4 %collective-permute-start.45 = (bf16[128,384]{1,0:T(8,128)(2,1)S(1)}, bf16[128,384]{1,0:T(8,128)(2,1)S(1)}, u32[]{:S(2)}, u32[]{:S(2)}) collective-permute-start(bf16[128,384]{1,0:T(8,128)(2,1)S(1)} %finish.1.refs_0_), channel_id=1, source_target_pairs={{0,4},{1,5},{2,6},{3,7},{4,0},{5,1},{6,2},{7,3},{8,12},{9,13},{10,... | collective-permute-start | bytes 294920 | tf_op jit(solution)/shard_map/ppermute | solution.py:40
  131.3 5.3 %collective-permute-start.44 = (bf16[128,384]{1,0:T(8,128)(2,1)S(1)}, bf16[128,384]{1,0:T(8,128)(2,1)S(1)}, u32[]{:S(2)}, u32[]{:S(2)}) collective-permute-start(bf16[128,384]{1,0:T(8,128)(2,1)S(1)} %finish.1.refs_0_), channel_id=1, source_target_pairs={{0,2},{1,3},{2,0},{3,1},{4,6},{5,7},{6,4},{7,5},{8,10},{9,11},{10,... | collective-permute-start | bytes 294920 | tf_op jit(solution)/shard_map/ppermute | solution.py:40
  132.7 4.1 %collective-permute-start.47 = (bf16[128,384]{1,0:T(8,128)(2,1)S(1)}, bf16[128,384]{1,0:T(8,128)(2,1)S(1)}, u32[]{:S(2)}, u32[]{:S(2)}) collective-permute-start(bf16[128,384]{1,0:T(8,128)(2,1)S(1)} %finish.1.refs_0_), channel_id=1, source_target_pairs={{0,1},{1,0},{2,3},{3,2},{4,5},{5,4},{6,7},{7,6},{8,9},{9,8},{10,11... | collective-permute-start | bytes 294920 | tf_op jit(solution)/shard_map/ppermute | solution.py:40
  135.7 1.3 collective-permute-start.50
  136.3 1.3 collective-permute-start.49
  136.6 1.3 collective-permute-start.48
  140.1 8.3 %collective-permute-start.51 = (bf16[256,256]{1,0:T(8,128)(2,1)S(1)}, bf16[256,256]{1,0:T(8,128)(2,1)S(1)}, u32[]{:S(2)}, u32[]{:S(2)}) collective-permute-start(bf16[256,256]{1,0:T(8,128)(2,1)S(1)} %get-tuple-element.166), channel_id=1, source_target_pairs={{0,24},{1,25},{2,26},{3,27},{4,28},{5,29},{6,30},{7,31},{8,16},{9,... | collective-permute-start | bytes 393224 | tf_op jit(solution)/shard_map/ppermute | solution.py:40
  141.8 11.7 %collective-permute-start.52 = (bf16[256,256]{1,0:T(8,128)(2,1)S(1)}, bf16[256,256]{1,0:T(8,128)(2,1)S(1)}, u32[]{:S(2)}, u32[]{:S(2)}) collective-permute-start(bf16[256,256]{1,0:T(8,128)(2,1)S(1)} %get-tuple-element.167), channel_id=1, source_target_pairs={{0,16},{1,17},{2,18},{3,19},{4,20},{5,21},{6,22},{7,23},{8,24},{9,... | collective-permute-start | bytes 393224 | tf_op jit(solution)/shard_map/ppermute | solution.py:40
  141.8 11.7 %collective-permute-start.53 = (bf16[256,256]{1,0:T(8,128)(2,1)S(1)}, bf16[256,256]{1,0:T(8,128)(2,1)S(1)}, u32[]{:S(2)}, u32[]{:S(2)}) collective-permute-start(bf16[256,256]{1,0:T(8,128)(2,1)S(1)} %get-tuple-element.168), channel_id=1, source_target_pairs={{0,8},{1,9},{2,10},{3,11},{4,12},{5,13},{6,14},{7,15},{8,0},{9,1},... | collective-permute-start | bytes 393224 | tf_op jit(solution)/shard_map/ppermute | solution.py:40

commit v13 on v11

--- a/solution.py
+++ b/solution.py
@@ -435,8 +435,8 @@
 def gradient_kernel(place_ref, *refs, n, k):
     grams, refs = refs[: n * k], refs[n * k :]
     packed, norms, scales, coeff_ref, refs = refs[0:2], refs[2:4], refs[4:6], refs[6], refs[7:]
-    outs, loss_ref = [refs[0], *refs[n - 1 : 0 : -1]], refs[n]
-    gram_ref, whole_ref = refs[n + 1 :]
+    outs = [refs[0], *refs[n - 1 : 0 : -1]]
+    share_ref, gram_ref, whole_ref = refs[n:]
     batch, columns = norms[0].shape
     height = grams[0].shape[0] // 2
     width = batch // BLOCKS
@@ -477,8 +477,13 @@
         for step in range(n):
             at = pl.multiple_of((place_ref[0] ^ step) * rows, rows)
             outs[step][view * rows : (view + 1) * rows, :] = whole_ref[view, pl.ds(at, rows), :]
+    share_ref[...] = share
+
+
+def loss_kernel(place_ref, gram_ref, share_ref, loss_ref):
+    batch = gram_ref.shape[1]
     frob = jnp.sum(gram_ref[0].astype(F32) * gram_ref[1].astype(F32), keepdims=True)
-    loss_ref[...] = (share + off_weight * (frob / (batch * batch))) / D
+    loss_ref[...] = (share_ref[...] + off_weight * (frob / (batch * batch))) / D
 
 
 def gradient(place, place_array, grams, packed, norms, scales, coeff):
@@ -487,12 +492,10 @@
         functools.partial(gradient_kernel, n=place.n, k=place.k),
         place_array,
         (*grams, *packed, *norms, *scales, coeff),
-        [((2 * batch // place.n, columns), BF16)] * place.n + [((1, 1), F32)],
+        [((2 * batch // place.n, columns), BF16)] * place.n
+        + [((1, 1), F32), ((2, batch, batch), BF16)],
         "gradient",
-        scratch_shapes=[
-            pltpu.VMEM((2, batch, batch), BF16),
-            pltpu.VMEM((2, batch, columns), BF16),
-        ],
+        scratch_shapes=[pltpu.VMEM((2, batch, columns), BF16)],
     )
 
 
@@ -508,8 +511,8 @@
 def with_kernels(place, h_first, h_second, weight):
     n, k, z, a, b = place.n, place.k, place.z, place.a, place.b
     place_array = jnp.stack([z, a, b]).astype(jnp.int32)
-    first = to_columns(place, h_first)
-    first, second = lax.optimization_barrier((to_planes(place, first), to_columns(place, h_second)))
+    first, second = lax.optimization_barrier((to_columns(place, h_first), h_second))
+    first, second = to_planes(place, first), to_columns(place, second)
     first, late_weight = lax.optimization_barrier((lay(place, place_array, first), weight))
     met_1, second, held = lax.optimization_barrier(
         (met_rows(place, first), to_planes(place, second), fetch(late_weight))
@@ -568,7 +571,7 @@
     )
     grams = sends(place, "a", [part] * n)
     grams += [place.send(part, lambda z, a, b: (z, a, b ^ 1)) for part in grams]
-    first, *others, loss = gradient(
+    first, *others, share, grams = gradient(
         place,
         place_array,
         grams,
@@ -584,6 +587,7 @@
         [(h_first.shape, BF16)] * 2,
         "place",
     )
+    (loss,) = local(loss_kernel, place_array, (grams, share), [((1, 1), F32)], "loss")
     return (out_1, out_2, loss.reshape(()))
 
 

time: 146 us -> 148 us (1.014)
  Pallas kernels: 29.3 us -> 31.9 us
    pallas_call x10 -> x11, Pallas kernels: 9.98 us -> 12.5 us  [local(): pl.pallas_call(kernel, in_specs=[pl.BlockSpec(memory_space=pltpu.SMEM)] +...]
  transfers between devices with their start and end apart: 54 -> 54, of which waited for: 25 -> 27; matrix products, arithmetic and copies ran while one was open for 2% -> 2% of each run, Pallas kernels for 14% -> 16%
where the time goes in v13:
time: 148 us
  starting transfers between devices  56.5 us (38%)
  waiting for transfers between devices  54.7 us (37%)
  Pallas kernels  31.9 us (22%)
  other arithmetic  2.07 us (1%)
  local copies, waits for them, and re-layouts  1.88 us (1%)
    ppermute x54, starting transfers between devices, send(): return lax.ppermute(value, ('dp', 'mp'), pairs)  56.5 us
    ppermute x54, waiting for transfers between devices, send(): return lax.ppermute(value, ('dp', 'mp'), pairs)  54.7 us
    pallas_call x11, Pallas kernels, local(): pl.pallas_call(kernel, in_specs=[pl.BlockSpec(memory_space=pltpu.SMEM)] +...  12.5 us
    pallas_call x2, Pallas kernels, project(): pl.pallas_call(functools.partial(project_kernel, counts=counts, n=n, k=k)...  9 us
    pallas_call x2, Pallas kernels, normalize_parts(): pl.pallas_call(functools.partial(normalize_kernel, n=n, k=k, order=order,...  6 us
    pallas_call x2, Pallas kernels, fetch(): pl.pallas_call(fetch_kernel, in_specs=[pl.BlockSpec(memory_space=pl.ANY)]...  4.39 us
  transfers between devices with their start and end apart: 54, of which 27 were waited for; matrix products, arithmetic and copies ran while one was open for 2% of the time, Pallas kernels for 16%

profile of v13, /device:TPU:0, one launch (start us, length us, event | category | flops | bytes accessed | tf_op | source)
XLA Modules:
  0.0 148.0 jit_solution(7793246482736303535)
XLA Ops:
  0.7 1.0 dynamic-slice_bitcast_fusion.3
  1.6 4.0 %collective-permute-start.10 = (bf16[32,1024]{1,0:T(8,128)(2,1)S(1)}, bf16[32,1024]{1,0:T(8,128)(2,1)S(1)}, u32[]{:S(2)}, u32[]{:S(2)}) collective-permute-start(bf16[32,1024]{1,0:T(8,128)(2,1)S(1)} %get-tuple-element.179), channel_id=1, source_target_pairs={{0,6},{1,7},{2,4},{3,5},{4,2},{5,3},{6,0},{7,1},{8,14},{9,15},{10,... | collective-permute-start | bytes 196616 | tf_op jit(solution)/shard_map/ppermute | solution.py:40
  6.2 1.6 %collective-permute-done.10 = bf16[32,1024]{1,0:T(8,128)(2,1)S(1)} collective-permute-done((bf16[32,1024]{1,0:T(8,128)(2,1)S(1)}, bf16[32,1024]{1,0:T(8,128)(2,1)S(1)}, u32[]{:S(2)}, u32[]{:S(2)}) %collective-permute-start.10) | collective-permute-done | bytes 65568 | tf_op jit(solution)/shard_map/ppermute | solution.py:40
  7.8 2.0 %collective-permute-done.9 = bf16[32,1024]{1,0:T(8,128)(2,1)S(1)} collective-permute-done((bf16[32,1024]{1,0:T(8,128)(2,1)S(1)}, bf16[32,1024]{1,0:T(8,128)(2,1)S(1)}, u32[]{:S(2)}, u32[]{:S(2)}) %collective-permute-start.9) | collective-permute-done | bytes 65568 | tf_op jit(solution)/shard_map/ppermute | solution.py:40
  10.4 3.7 %collective-permute-start.13 = (bf16[32,1024]{1,0:T(8,128)(2,1)S(1)}, bf16[32,1024]{1,0:T(8,128)(2,1)S(1)}, u32[]{:S(2)}, u32[]{:S(2)}) collective-permute-start(bf16[32,1024]{1,0:T(8,128)(2,1)S(1)} %get-tuple-element.175), channel_id=1, source_target_pairs={{0,24},{1,25},{2,26},{3,27},{4,28},{5,29},{6,30},{7,31},{8,16},{9,... | collective-permute-start | bytes 196616 | tf_op jit(solution)/shard_map/ppermute | solution.py:40
  14.1 0.8 collective-permute-start.12
  14.8 0.9 dynamic-slice_bitcast_fusion
  16.3 1.6 %collective-permute-start.18 = (bf16[32,1024]{1,0:T(8,128)(2,1)S(1)}, bf16[32,1024]{1,0:T(8,128)(2,1)S(1)}, u32[]{:S(2)}, u32[]{:S(2)}) collective-permute-start(bf16[32,1024]{1,0:T(8,128)(2,1)S(1)} %get-tuple-element.173), channel_id=1, source_target_pairs={{0,4},{1,5},{2,6},{3,7},{4,0},{5,1},{6,2},{7,3},{8,12},{9,13},{10,... | collective-permute-start | bytes 196616 | tf_op jit(solution)/shard_map/ppermute | solution.py:40
  17.9 1.4 collective-permute-start.17
  20.0 1.6 %collective-permute-start.16 = (bf16[128,1024]{1,0:T(8,128)(2,1)S(1)}, bf16[128,1024]{1,0:T(8,128)(2,1)S(1)}, u32[]{:S(2)}, u32[]{:S(2)}) collective-permute-start(bf16[128,1024]{1,0:T(8,128)(2,1)S(1)} %lay.2.refs_0_), channel_id=1, source_target_pairs={{0,6},{1,7},{2,4},{3,5},{4,2},{5,3},{6,0},{7,1},{8,14},{9,15},{10,... | collective-permute-start | bytes 786440 | tf_op jit(solution)/shard_map/ppermute | solution.py:40
  22.0 1.6 %collective-permute-start.14 = (bf16[128,1024]{1,0:T(8,128)(2,1)S(1)}, bf16[128,1024]{1,0:T(8,128)(2,1)S(1)}, u32[]{:S(2)}, u32[]{:S(2)}) collective-permute-start(bf16[128,1024]{1,0:T(8,128)(2,1)S(1)} %lay.2.refs_0_), channel_id=1, source_target_pairs={{0,2},{1,3},{2,0},{3,1},{4,6},{5,7},{6,4},{7,5},{8,10},{9,11},{10,... | collective-permute-start | bytes 786440 | tf_op jit(solution)/shard_map/ppermute | solution.py:40
  23.9 0.9 broadcast_select_fusion.6
  24.7 3.7 %collective-permute-start.22 = (bf16[32,1024]{1,0:T(8,128)(2,1)S(1)}, bf16[32,1024]{1,0:T(8,128)(2,1)S(1)}, u32[]{:S(2)}, u32[]{:S(2)}) collective-permute-start(bf16[32,1024]{1,0:T(8,128)(2,1)S(1)} %get-tuple-element.168), channel_id=1, source_target_pairs={{0,24},{1,25},{2,26},{3,27},{4,28},{5,29},{6,30},{7,31},{8,16},{9,... | collective-permute-start | bytes 196616 | tf_op jit(solution)/shard_map/ppermute | solution.py:40
  28.5 3.1 %collective-permute-done.22.refs_3_ = bf16[32,1024]{1,0:T(8,128)(2,1)S(1)} collective-permute-done((bf16[32,1024]{1,0:T(8,128)(2,1)S(1)}, bf16[32,1024]{1,0:T(8,128)(2,1)S(1)}, u32[]{:S(2)}, u32[]{:S(2)}) %collective-permute-start.22) | collective-permute-done | bytes 65568 | tf_op jit(solution)/shard_map/ppermute | solution.py:40
  31.6 2.2 %fetch.3.refs_8_ = bf16[2048,1024]{1,0:T(8,128)(2,1)S(1)} custom-call(bf16[2048,1024]{1,0:T(8,128)(2,1)} %weight_ref), custom_call_target="tpu_custom_call" | custom-call | bytes 8388608 | tf_op jit(solution)/shard_map/fetch/pallas_call | solution.py:246
  33.8 3.6 %collective-permute-done.21.refs_2_ = bf16[32,1024]{1,0:T(8,128)(2,1)S(1)} collective-permute-done((bf16[32,1024]{1,0:T(8,128)(2,1)S(1)}, bf16[32,1024]{1,0:T(8,128)(2,1)S(1)}, u32[]{:S(2)}, u32[]{:S(2)}) %collective-permute-start.21) | collective-permute-done | bytes 65568 | tf_op jit(solution)/shard_map/ppermute | solution.py:40
  38.5 1.3 lay.3
  39.8 2.7 %collective-permute-start.27 = (bf16[128,1024]{1,0:T(8,128)(2,1)}, bf16[128,1024]{1,0:T(8,128)(2,1)}, u32[]{:S(2)}, u32[]{:S(2)}) collective-permute-start(bf16[128,1024]{1,0:T(8,128)(2,1)} %lay.3), channel_id=1, source_target_pairs={{0,6},{1,7},{2,4},{3,5},{4,2},{5,3},{6,0},{7,1},{8,14},{9,15},{10,... | collective-permute-start | bytes 786440 | tf_op jit(solution)/shard_map/ppermute | solution.py:40
  42.5 3.9 %project.3 = (f32[512,256]{1,0:T(8,128)S(1)}, bf16[528,256]{1,0:T(8,128)(2,1)S(1)}, bf16[528,256]{1,0:T(8,128)(2,1)S(1)}, bf16[528,256]{1,0:T(8,128)(2,1)S(1)}) custom-call(s32[3]{0:T(128)S(1)} %pad_add_fusion.place_ref, bf16[128,1024]{1,0:T(8,128)(2,1)S(1)} %lay.2.refs_0_, bf16[128,1024]{1,0:T(8,128)(2,1)S(1)} %collective-permute-done.14.refs_1_, ...), custom_call_target="tpu_custom_call" | custom-call | flops 2147483648 | bytes 7864320 | tf_op jit(solution)/shard_map/project/pallas_call | solution.py:340
  46.4 3.9 %collective-permute-start.31 = (bf16[528,256]{1,0:T(8,128)(2,1)S(1)}, bf16[528,256]{1,0:T(8,128)(2,1)S(1)}, u32[]{:S(2)}, u32[]{:S(2)}) collective-permute-start(bf16[528,256]{1,0:T(8,128)(2,1)S(1)} %get-tuple-element.130), channel_id=1, source_target_pairs={{0,24},{1,25},{2,26},{3,27},{4,28},{5,29},{6,30},{7,31},{8,16},{9,... | collective-permute-start | bytes 811016 | tf_op jit(solution)/shard_map/ppermute | solution.py:40
  50.9 16.7 %conditional.2 = (f32[512,256]{1,0:T(8,128)S(1)}, bf16[528,256]{1,0:T(8,128)(2,1)}, bf16[528,256]{1,0:T(8,128)(2,1)}, bf16[528,256]{1,0:T(8,128)(2,1)}) conditional(s32[]{:T(128)} %convert_element_type.4, () %tuple.35, (bf16[128,1024]{1,0:T(8,128)(2,1)}, bf16[128,1024]{1,0:T(8,128)(2,1)}, bf16[2048,1024]{1,0:T(8,128)(2,1)}, s32[3]{0:T(128)S(1)}) %tuple.36), branch_computations={%region_0.1_spmd, %region_1.2_spmd} | conditional | flops 2149580800 | bytes 24641728 | solution.py:213
  50.9 1.6 %collective-permute-start.5 = (bf16[128,1024]{1,0:T(8,128)(2,1)}, bf16[128,1024]{1,0:T(8,128)(2,1)S(1)}, u32[]{:S(2)}, u32[]{:S(2)}) collective-permute-start(bf16[128,1024]{1,0:T(8,128)(2,1)} %get-tuple-element.16.refs_0_), channel_id=1, source_target_pairs={{0,4},{1,5},{2,6},{3,7},{4,0},{5,1},{6,2},{7,3},{8,12},{9,13},{10,... | collective-permute-start | bytes 786440 | tf_op jit(solution)/shard_map/cond/branch_1_fun/ppermute | solution.py:40
  52.5 6.1 %collective-permute-done.4.refs_2_ = bf16[128,1024]{1,0:T(8,128)(2,1)S(1)} collective-permute-done((bf16[128,1024]{1,0:T(8,128)(2,1)}, bf16[128,1024]{1,0:T(8,128)(2,1)S(1)}, u32[]{:S(2)}, u32[]{:S(2)}) %collective-permute-start.4) | collective-permute-done | bytes 262176 | tf_op jit(solution)/shard_map/cond/branch_1_fun/ppermute | solution.py:40
  58.7 1.1 pad_maximum_fusion
  60.3 2.2 %fetch.2.refs_6_ = bf16[2048,1024]{1,0:T(8,128)(2,1)S(1)} custom-call(bf16[2048,1024]{1,0:T(8,128)(2,1)} %get-tuple-element.19.weight_ref), custom_call_target="tpu_custom_call" | custom-call | bytes 8388608 | tf_op jit(solution)/shard_map/cond/branch_1_fun/fetch/pallas_call | solution.py:246
  62.6 5.1 %project.2 = (f32[512,256]{1,0:T(8,128)S(1)}, bf16[528,256]{1,0:T(8,128)(2,1)}, bf16[528,256]{1,0:T(8,128)(2,1)}, bf16[528,256]{1,0:T(8,128)(2,1)}) custom-call(s32[3]{0:T(128)S(1)} %get-tuple-element.14.place_ref, bf16[128,1024]{1,0:T(8,128)(2,1)} %get-tuple-element.16.refs_0_, bf16[128,1024]{1,0:T(8,128)(2,1)} %get-tuple-element.17.refs_1_, ...), custom_call_target="tpu_custom_call" | custom-call | flops 2147483648 | bytes 7864320 | tf_op jit(solution)/shard_map/cond/branch_1_fun/project/pallas_call | solution.py:340
  67.7 1.4 collective-permute-start.28
  69.1 2.6 %collective-permute-start.29 = (bf16[528,256]{1,0:T(8,128)(2,1)}, bf16[528,256]{1,0:T(8,128)(2,1)S(1)}, u32[]{:S(2)}, u32[]{:S(2)}) collective-permute-start(bf16[528,256]{1,0:T(8,128)(2,1)} %get-tuple-element.127), channel_id=1, source_target_pairs={{0,16},{1,17},{2,18},{3,19},{4,20},{5,21},{6,22},{7,23},{8,24},{9,... | collective-permute-start | bytes 811016 | tf_op jit(solution)/shard_map/ppermute | solution.py:40
  72.1 1.4 collective-permute-done.32.refs_2_
  73.4 3.4 %normalize.2 = (f32[512,256]{1,0:T(8,128)S(1)}, bf16[512,256]{1,0:T(8,128)(2,1)S(1)}, f32[1,256]{1,0:T(1,128)S(1)}, f32[256,512]{1,0:T(8,128)}, f32[256,512]{1,0:T(8,128)}) custom-call(s32[3]{0:T(128)S(1)} %pad_add_fusion.place_ref, f32[512,256]{1,0:T(8,128)S(1)} %get-tuple-element.129.refs_0_, bf16[528,256]{1,0:T(8,128)(2,1)S(1)} %collective-permute-done.31.refs_1_, ...), custom_call_target="tpu_custom_call" | custom-call | flops 134217728 | bytes 3145728 | tf_op jit(solution)/shard_map/normalize/pallas_call | solution.py:420
  76.8 13.6 %conditional.3 = ((f32[16,384]{1,0:T(8,128)S(1)}, f32[16,384]{1,0:T(8,128)S(1)}, f32[16,384]{1,0:T(8,128)S(1)}, f32[16,384]{1,0:T(8,128)S(1)})) conditional(s32[]{:T(128)} %convert_element_type.4, () %tuple.38, (f32[256,512]{1,0:T(8,128)}, s32[3]{0:T(128)S(1)}, f32[256,512]{1,0:T(8,128)}) %tuple.39), branch_computations={%region_2.3_spmd, %region_3.4_spmd} | conditional | bytes 2834600 | solution.py:213
  76.8 2.1 %collective-permute-done.met_ref = f32[256,512]{1,0:T(8,128)S(1)} collective-permute-done((f32[256,512]{1,0:T(8,128)}, f32[256,512]{1,0:T(8,128)S(1)}, u32[]{:S(2)}, u32[]{:S(2)}) %collective-permute-start) | collective-permute-done | bytes 524320 | tf_op jit(solution)/shard_map/cond/branch_1_fun/ppermute | solution.py:40
  78.9 1.3 halve.2
  81.2 3.4 %collective-permute-done.1.refs_1_ = bf16[80,384]{1,0:T(8,128)(2,1)S(1)} collective-permute-done((bf16[80,384]{1,0:T(8,128)(2,1)S(1)}, bf16[80,384]{1,0:T(8,128)(2,1)S(1)}, u32[]{:S(2)}, u32[]{:S(2)}) %collective-permute-start.1) | collective-permute-done | bytes 61472 | tf_op jit(solution)/shard_map/cond/branch_1_fun/ppermute | solution.py:40
  84.9 4.8 %collective-permute-done.3.refs_3_ = bf16[80,384]{1,0:T(8,128)(2,1)S(1)} collective-permute-done((bf16[80,384]{1,0:T(8,128)(2,1)S(1)}, bf16[80,384]{1,0:T(8,128)(2,1)S(1)}, u32[]{:S(2)}, u32[]{:S(2)}) %collective-permute-start.3) | collective-permute-done | bytes 61472 | tf_op jit(solution)/shard_map/cond/branch_1_fun/ppermute | solution.py:40
  89.7 0.8 plane.1
  90.5 2.6 %collective-permute-start.35 = (f32[16,384]{1,0:T(8,128)S(1)}, f32[16,384]{1,0:T(8,128)S(1)}, u32[]{:S(2)}, u32[]{:S(2)}) collective-permute-start(f32[16,384]{1,0:T(8,128)S(1)} %get-tuple-element.137), channel_id=1, source_target_pairs={{0,16},{1,17},{2,18},{3,19},{4,20},{5,21},{6,22},{7,23},{8,24},{9,... | collective-permute-start | bytes 73736 | tf_op jit(solution)/shard_map/ppermute | solution.py:40
  93.2 1.7 %collective-permute-start.36 = (f32[16,384]{1,0:T(8,128)S(1)}, f32[16,384]{1,0:T(8,128)S(1)}, u32[]{:S(2)}, u32[]{:S(2)}) collective-permute-start(f32[16,384]{1,0:T(8,128)S(1)} %get-tuple-element.138), channel_id=1, source_target_pairs={{0,24},{1,25},{2,26},{3,27},{4,28},{5,29},{6,30},{7,31},{8,16},{9,... | collective-permute-start | bytes 73736 | tf_op jit(solution)/shard_map/ppermute | solution.py:40
  94.9 2.8 %collective-permute-done.35.refs_2_ = f32[16,384]{1,0:T(8,128)S(1)} collective-permute-done((f32[16,384]{1,0:T(8,128)S(1)}, f32[16,384]{1,0:T(8,128)S(1)}, u32[]{:S(2)}, u32[]{:S(2)}) %collective-permute-start.35) | collective-permute-done | bytes 24608 | tf_op jit(solution)/shard_map/ppermute | solution.py:40
  97.7 1.1 collective-permute-done.36.refs_3_
  98.8 2.6 %normalize.3 = (f32[512,256]{1,0:T(8,128)S(1)}, bf16[512,256]{1,0:T(8,128)(2,1)S(1)}, f32[1,256]{1,0:T(1,128)S(1)}, f32[256,512]{1,0:T(8,128)S(1)}, f32[256,512]{1,0:T(8,128)S(1)}, /*index=5*/f32[1,256]{1,0:T(1,128)S(1)}) custom-call(s32[3]{0:T(128)S(1)} %pad_add_fusion.place_ref, f32[512,256]{1,0:T(8,128)S(1)} %get-tuple-element.139.refs_0_, ...), custom_call_target="tpu_custom_call" | custom-call | flops 134217728 | bytes 3145728 | tf_op jit(solution)/shard_map/normalize/pallas_call | solution.py:420
  101.5 1.9 %collective-permute-done.37.met_ref = f32[256,512]{1,0:T(8,128)S(1)} collective-permute-done((f32[256,512]{1,0:T(8,128)S(1)}, f32[256,512]{1,0:T(8,128)S(1)}, u32[]{:S(2)}, u32[]{:S(2)}) %collective-permute-start.37) | collective-permute-done | bytes 524320 | tf_op jit(solution)/shard_map/ppermute | solution.py:40
  103.4 0.8 halve.3
  104.2 1.8 %collective-permute-start.38 = (bf16[80,384]{1,0:T(8,128)(2,1)S(1)}, bf16[80,384]{1,0:T(8,128)(2,1)S(1)}, u32[]{:S(2)}, u32[]{:S(2)}) collective-permute-start(bf16[80,384]{1,0:T(8,128)(2,1)S(1)} %get-tuple-element.147), channel_id=1, source_target_pairs={{0,2},{1,3},{2,0},{3,1},{4,6},{5,7},{6,4},{7,5},{8,10},{9,11},{10,... | collective-permute-start | bytes 184328 | tf_op jit(solution)/shard_map/ppermute | solution.py:40
  106.4 1.4 collective-permute-start.40
  108.5 2.3 %collective-permute-done.39.refs_2_ = bf16[80,384]{1,0:T(8,128)(2,1)S(1)} collective-permute-done((bf16[80,384]{1,0:T(8,128)(2,1)S(1)}, bf16[80,384]{1,0:T(8,128)(2,1)S(1)}, u32[]{:S(2)}, u32[]{:S(2)}) %collective-permute-start.39) | collective-permute-done | bytes 61472 | tf_op jit(solution)/shard_map/ppermute | solution.py:40
  111.5 0.8 code.1.refs_0_
  112.3 1.2 collective-permute-start.43
  113.5 3.3 %collective-permute-start.41 = (bf16[96,384]{1,0:T(8,128)(2,1)S(1)}, bf16[96,384]{1,0:T(8,128)(2,1)S(1)}, u32[]{:S(2)}, u32[]{:S(2)}) collective-permute-start(bf16[96,384]{1,0:T(8,128)(2,1)S(1)} %code.1.refs_0_), channel_id=1, source_target_pairs={{0,8},{1,9},{2,10},{3,11},{4,12},{5,13},{6,14},{7,15},{8,0},{9,1},... | collective-permute-start | bytes 221192 | tf_op jit(solution)/shard_map/ppermute | solution.py:40
  116.8 2.1 %collective-permute-done.43.refs_3_ = bf16[96,384]{1,0:T(8,128)(2,1)S(1)} collective-permute-done((bf16[96,384]{1,0:T(8,128)(2,1)S(1)}, bf16[96,384]{1,0:T(8,128)(2,1)S(1)}, u32[]{:S(2)}, u32[]{:S(2)}) %collective-permute-start.43) | collective-permute-done | bytes 73760 | tf_op jit(solution)/shard_map/ppermute | solution.py:40
  118.9 1.4 collective-permute-done.42.refs_2_
  120.2 0.9 finish.1.refs_0_
  121.2 1.9 %collective-permute-start.46 = (bf16[128,384]{1,0:T(8,128)(2,1)S(1)}, bf16[128,384]{1,0:T(8,128)(2,1)S(1)}, u32[]{:S(2)}, u32[]{:S(2)}) collective-permute-start(bf16[128,384]{1,0:T(8,128)(2,1)S(1)} %finish.1.refs_0_), channel_id=1, source_target_pairs={{0,6},{1,7},{2,4},{3,5},{4,2},{5,3},{6,0},{7,1},{8,14},{9,15},{10,... | collective-permute-start | bytes 294920 | tf_op jit(solution)/shard_map/ppermute | solution.py:40
  123.1 1.2 collective-permute-start.45
  124.7 2.7 %collective-permute-done.46.refs_3_ = bf16[128,384]{1,0:T(8,128)(2,1)S(1)} collective-permute-done((bf16[128,384]{1,0:T(8,128)(2,1)S(1)}, bf16[128,384]{1,0:T(8,128)(2,1)S(1)}, u32[]{:S(2)}, u32[]{:S(2)}) %collective-permute-start.46) | collective-permute-done | bytes 98336 | tf_op jit(solution)/shard_map/ppermute | solution.py:40
  128.1 0.8 collective-permute-done.44.refs_1_
  129.4 0.8 collective-permute-done.48.refs_5_
  130.2 2.0 %gradient.1 = (bf16[256,256]{1,0:T(8,128)(2,1)S(1)}, bf16[256,256]{1,0:T(8,128)(2,1)S(1)}, bf16[256,256]{1,0:T(8,128)(2,1)S(1)}, bf16[256,256]{1,0:T(8,128)(2,1)...) custom-call(s32[3]{0:T(128)S(1)} %pad_add_fusion.place_ref, bf16[128,384]{1,0:T(8,128)(2,1)S(1)} %finish.1.refs_0_, ...), custom_call_target="tpu_custom_call" | custom-call | tf_op jit(solution)/shard_map/gradient/pallas_call | solution.py:172
  132.2 1.8 %collective-permute-start.51 = (bf16[256,256]{1,0:T(8,128)(2,1)S(1)}, bf16[256,256]{1,0:T(8,128)(2,1)S(1)}, u32[]{:S(2)}, u32[]{:S(2)}) collective-permute-start(bf16[256,256]{1,0:T(8,128)(2,1)S(1)} %get-tuple-element.161), channel_id=1, source_target_pairs={{0,24},{1,25},{2,26},{3,27},{4,28},{5,29},{6,30},{7,31},{8,16},{9,... | collective-permute-start | bytes 393224 | tf_op jit(solution)/shard_map/ppermute | solution.py:40
  134.6 2.0 %collective-permute-start.53 = (bf16[256,256]{1,0:T(8,128)(2,1)S(1)}, bf16[256,256]{1,0:T(8,128)(2,1)S(1)}, u32[]{:S(2)}, u32[]{:S(2)}) collective-permute-start(bf16[256,256]{1,0:T(8,128)(2,1)S(1)} %get-tuple-element.163), channel_id=1, source_target_pairs={{0,8},{1,9},{2,10},{3,11},{4,12},{5,13},{6,14},{7,15},{8,0},{9,1},... | collective-permute-start | bytes 393224 | tf_op jit(solution)/shard_map/ppermute | solution.py:40
  136.6 2.1 %loss.1 = f32[1,1]{1,0:T(1,128)} custom-call(s32[3]{0:T(128)S(1)} %pad_add_fusion.place_ref, bf16[2,512,512]{2,1,0:T(8,128)(2,1)S(1)} %get-tuple-element.166.gram_ref, f32[1,1]{1,0:T(1,128)} %get-tuple-element.167.share_ref), custom_call_target="tpu_custom_call" | custom-call | tf_op jit(solution)/shard_map/loss/pallas_call | solution.py:172
  138.7 1.8 %collective-permute-done.51.refs_1_ = bf16[256,256]{1,0:T(8,128)(2,1)S(1)} collective-permute-done((bf16[256,256]{1,0:T(8,128)(2,1)S(1)}, bf16[256,256]{1,0:T(8,128)(2,1)S(1)}, u32[]{:S(2)}, u32[]{:S(2)}) %collective-permute-start.51) | collective-permute-done | bytes 131104 | tf_op jit(solution)/shard_map/ppermute | solution.py:40
  140.5 6.1 %collective-permute-done.52.refs_2_ = bf16[256,256]{1,0:T(8,128)(2,1)S(1)} collective-permute-done((bf16[256,256]{1,0:T(8,128)(2,1)S(1)}, bf16[256,256]{1,0:T(8,128)(2,1)S(1)}, u32[]{:S(2)}, u32[]{:S(2)}) %collective-permute-start.52) | collective-permute-done | bytes 131104 | tf_op jit(solution)/shard_map/ppermute | solution.py:40
  146.6 1.4 place.1
  (70 shorter events, 11.2 us)
Async XLA Ops:
  1.6 6.2 %collective-permute-start.10 = (bf16[32,1024]{1,0:T(8,128)(2,1)S(1)}, bf16[32,1024]{1,0:T(8,128)(2,1)S(1)}, u32[]{:S(2)}, u32[]{:S(2)}) collective-permute-start(bf16[32,1024]{1,0:T(8,128)(2,1)S(1)} %get-tuple-element.179), channel_id=1, source_target_pairs={{0,6},{1,7},{2,4},{3,5},{4,2},{5,3},{6,0},{7,1},{8,14},{9,15},{10,... | collective-permute-start | bytes 196616 | tf_op jit(solution)/shard_map/ppermute | solution.py:40
  5.6 4.3 %collective-permute-start.9 = (bf16[32,1024]{1,0:T(8,128)(2,1)S(1)}, bf16[32,1024]{1,0:T(8,128)(2,1)S(1)}, u32[]{:S(2)}, u32[]{:S(2)}) collective-permute-start(bf16[32,1024]{1,0:T(8,128)(2,1)S(1)} %get-tuple-element.180), channel_id=1, source_target_pairs={{0,4},{1,5},{2,6},{3,7},{4,0},{5,1},{6,2},{7,3},{8,12},{9,13},{10,... | collective-permute-start | bytes 196616 | tf_op jit(solution)/shard_map/ppermute | solution.py:40
  6.1 4.3 %collective-permute-start.8 = (bf16[32,1024]{1,0:T(8,128)(2,1)S(1)}, bf16[32,1024]{1,0:T(8,128)(2,1)S(1)}, u32[]{:S(2)}, u32[]{:S(2)}) collective-permute-start(bf16[32,1024]{1,0:T(8,128)(2,1)S(1)} %get-tuple-element.181), channel_id=1, source_target_pairs={{0,2},{1,3},{2,0},{3,1},{4,6},{5,7},{6,4},{7,5},{8,10},{9,11},{10,... | collective-permute-start | bytes 196616 | tf_op jit(solution)/shard_map/ppermute | solution.py:40
  10.4 7.5 %collective-permute-start.13 = (bf16[32,1024]{1,0:T(8,128)(2,1)S(1)}, bf16[32,1024]{1,0:T(8,128)(2,1)S(1)}, u32[]{:S(2)}, u32[]{:S(2)}) collective-permute-start(bf16[32,1024]{1,0:T(8,128)(2,1)S(1)} %get-tuple-element.175), channel_id=1, source_target_pairs={{0,24},{1,25},{2,26},{3,27},{4,28},{5,29},{6,30},{7,31},{8,16},{9,... | collective-permute-start | bytes 196616 | tf_op jit(solution)/shard_map/ppermute | solution.py:40
  14.1 5.3 %collective-permute-start.11 = (bf16[32,1024]{1,0:T(8,128)(2,1)S(1)}, bf16[32,1024]{1,0:T(8,128)(2,1)S(1)}, u32[]{:S(2)}, u32[]{:S(2)}) collective-permute-start(bf16[32,1024]{1,0:T(8,128)(2,1)S(1)} %get-tuple-element.176), channel_id=1, source_target_pairs={{0,8},{1,9},{2,10},{3,11},{4,12},{5,13},{6,14},{7,15},{8,0},{9,1},... | collective-permute-start | bytes 196616 | tf_op jit(solution)/shard_map/ppermute | solution.py:40
  14.1 5.3 %collective-permute-start.12 = (bf16[32,1024]{1,0:T(8,128)(2,1)S(1)}, bf16[32,1024]{1,0:T(8,128)(2,1)S(1)}, u32[]{:S(2)}, u32[]{:S(2)}) collective-permute-start(bf16[32,1024]{1,0:T(8,128)(2,1)S(1)} %get-tuple-element.177), channel_id=1, source_target_pairs={{0,16},{1,17},{2,18},{3,19},{4,20},{5,21},{6,22},{7,23},{8,24},{9,... | collective-permute-start | bytes 196616 | tf_op jit(solution)/shard_map/ppermute | solution.py:40
  15.8 6.2 %collective-permute-start.19 = (bf16[32,1024]{1,0:T(8,128)(2,1)S(1)}, bf16[32,1024]{1,0:T(8,128)(2,1)S(1)}, u32[]{:S(2)}, u32[]{:S(2)}) collective-permute-start(bf16[32,1024]{1,0:T(8,128)(2,1)S(1)} %get-tuple-element.172), channel_id=1, source_target_pairs={{0,2},{1,3},{2,0},{3,1},{4,6},{5,7},{6,4},{7,5},{8,10},{9,11},{10,... | collective-permute-start | bytes 196616 | tf_op jit(solution)/shard_map/ppermute | solution.py:40
  16.3 7.2 %collective-permute-start.18 = (bf16[32,1024]{1,0:T(8,128)(2,1)S(1)}, bf16[32,1024]{1,0:T(8,128)(2,1)S(1)}, u32[]{:S(2)}, u32[]{:S(2)}) collective-permute-start(bf16[32,1024]{1,0:T(8,128)(2,1)S(1)} %get-tuple-element.173), channel_id=1, source_target_pairs={{0,4},{1,5},{2,6},{3,7},{4,0},{5,1},{6,2},{7,3},{8,12},{9,13},{10,... | collective-permute-start | bytes 196616 | tf_op jit(solution)/shard_map/ppermute | solution.py:40
  17.9 6.0 %collective-permute-start.17 = (bf16[32,1024]{1,0:T(8,128)(2,1)S(1)}, bf16[32,1024]{1,0:T(8,128)(2,1)S(1)}, u32[]{:S(2)}, u32[]{:S(2)}) collective-permute-start(bf16[32,1024]{1,0:T(8,128)(2,1)S(1)} %get-tuple-element.174), channel_id=1, source_target_pairs={{0,6},{1,7},{2,4},{3,5},{4,2},{5,3},{6,0},{7,1},{8,14},{9,15},{10,... | collective-permute-start | bytes 196616 | tf_op jit(solution)/shard_map/ppermute | solution.py:40
  20.0 17.4 %collective-permute-start.16 = (bf16[128,1024]{1,0:T(8,128)(2,1)S(1)}, bf16[128,1024]{1,0:T(8,128)(2,1)S(1)}, u32[]{:S(2)}, u32[]{:S(2)}) collective-permute-start(bf16[128,1024]{1,0:T(8,128)(2,1)S(1)} %lay.2.refs_0_), channel_id=1, source_target_pairs={{0,6},{1,7},{2,4},{3,5},{4,2},{5,3},{6,0},{7,1},{8,14},{9,15},{10,... | collective-permute-start | bytes 786440 | tf_op jit(solution)/shard_map/ppermute | solution.py:40
  21.5 15.9 %collective-permute-start.15 = (bf16[128,1024]{1,0:T(8,128)(2,1)S(1)}, bf16[128,1024]{1,0:T(8,128)(2,1)S(1)}, u32[]{:S(2)}, u32[]{:S(2)}) collective-permute-start(bf16[128,1024]{1,0:T(8,128)(2,1)S(1)} %lay.2.refs_0_), channel_id=1, source_target_pairs={{0,4},{1,5},{2,6},{3,7},{4,0},{5,1},{6,2},{7,3},{8,12},{9,13},{10,... | collective-permute-start | bytes 786440 | tf_op jit(solution)/shard_map/ppermute | solution.py:40
  22.0 15.4 %collective-permute-start.14 = (bf16[128,1024]{1,0:T(8,128)(2,1)S(1)}, bf16[128,1024]{1,0:T(8,128)(2,1)S(1)}, u32[]{:S(2)}, u32[]{:S(2)}) collective-permute-start(bf16[128,1024]{1,0:T(8,128)(2,1)S(1)} %lay.2.refs_0_), channel_id=1, source_target_pairs={{0,2},{1,3},{2,0},{3,1},{4,6},{5,7},{6,4},{7,5},{8,10},{9,11},{10,... | collective-permute-start | bytes 786440 | tf_op jit(solution)/shard_map/ppermute | solution.py:40
  24.7 6.8 %collective-permute-start.22 = (bf16[32,1024]{1,0:T(8,128)(2,1)S(1)}, bf16[32,1024]{1,0:T(8,128)(2,1)S(1)}, u32[]{:S(2)}, u32[]{:S(2)}) collective-permute-start(bf16[32,1024]{1,0:T(8,128)(2,1)S(1)} %get-tuple-element.168), channel_id=1, source_target_pairs={{0,24},{1,25},{2,26},{3,27},{4,28},{5,29},{6,30},{7,31},{8,16},{9,... | collective-permute-start | bytes 196616 | tf_op jit(solution)/shard_map/ppermute | solution.py:40
  28.5 5.3 %collective-permute-start.20 = (bf16[32,1024]{1,0:T(8,128)(2,1)S(1)}, bf16[32,1024]{1,0:T(8,128)(2,1)S(1)}, u32[]{:S(2)}, u32[]{:S(2)}) collective-permute-start(bf16[32,1024]{1,0:T(8,128)(2,1)S(1)} %get-tuple-element.170), channel_id=1, source_target_pairs={{0,8},{1,9},{2,10},{3,11},{4,12},{5,13},{6,14},{7,15},{8,0},{9,1},... | collective-permute-start | bytes 196616 | tf_op jit(solution)/shard_map/ppermute | solution.py:40
  31.5 5.9 %collective-permute-start.21 = (bf16[32,1024]{1,0:T(8,128)(2,1)S(1)}, bf16[32,1024]{1,0:T(8,128)(2,1)S(1)}, u32[]{:S(2)}, u32[]{:S(2)}) collective-permute-start(bf16[32,1024]{1,0:T(8,128)(2,1)S(1)} %get-tuple-element.171), channel_id=1, source_target_pairs={{0,16},{1,17},{2,18},{3,19},{4,20},{5,21},{6,22},{7,23},{8,24},{9,... | collective-permute-start | bytes 196616 | tf_op jit(solution)/shard_map/ppermute | solution.py:40
  37.4 5.1 %collective-permute-start.23 = (bf16[128,1024]{1,0:T(8,128)(2,1)S(1)}, bf16[128,1024]{1,0:T(8,128)(2,1)S(1)}, u32[]{:S(2)}, u32[]{:S(2)}) collective-permute-start(bf16[128,1024]{1,0:T(8,128)(2,1)S(1)} %lay.2.refs_0_), channel_id=1, source_target_pairs={{0,1},{1,0},{2,3},{3,2},{4,5},{5,4},{6,7},{7,6},{8,9},{9,8},{10,11... | collective-permute-start | bytes 786440 | tf_op jit(solution)/shard_map/ppermute | solution.py:40
  37.5 5.0 %collective-permute-start.24 = (bf16[128,1024]{1,0:T(8,128)(2,1)S(1)}, bf16[128,1024]{1,0:T(8,128)(2,1)S(1)}, u32[]{:S(2)}, u32[]{:S(2)}) collective-permute-start(bf16[128,1024]{1,0:T(8,128)(2,1)S(1)} %collective-permute-done.14.refs_1_), channel_id=1, source_target_pairs={{0,1},{1,0},{2,3},{3,2},{4,5},{5,4},{6,7},{7,6},{8,9},{9,8},{10,11... | collective-permute-start | bytes 786440 | tf_op jit(solution)/shard_map/ppermute | solution.py:40
  38.0 4.5 %collective-permute-start.25 = (bf16[128,1024]{1,0:T(8,128)(2,1)S(1)}, bf16[128,1024]{1,0:T(8,128)(2,1)S(1)}, u32[]{:S(2)}, u32[]{:S(2)}) collective-permute-start(bf16[128,1024]{1,0:T(8,128)(2,1)S(1)} %collective-permute-done.15.refs_2_), channel_id=1, source_target_pairs={{0,1},{1,0},{2,3},{3,2},{4,5},{5,4},{6,7},{7,6},{8,9},{9,8},{10,11... | collective-permute-start | bytes 786440 | tf_op jit(solution)/shard_map/ppermute | solution.py:40
  38.1 4.4 %collective-permute-start.26 = (bf16[128,1024]{1,0:T(8,128)(2,1)S(1)}, bf16[128,1024]{1,0:T(8,128)(2,1)S(1)}, u32[]{:S(2)}, u32[]{:S(2)}) collective-permute-start(bf16[128,1024]{1,0:T(8,128)(2,1)S(1)} %collective-permute-done.16.refs_3_), channel_id=1, source_target_pairs={{0,1},{1,0},{2,3},{3,2},{4,5},{5,4},{6,7},{7,6},{8,9},{9,8},{10,11... | collective-permute-start | bytes 786440 | tf_op jit(solution)/shard_map/ppermute | solution.py:40
  39.8 11.2 %collective-permute-start.27 = (bf16[128,1024]{1,0:T(8,128)(2,1)}, bf16[128,1024]{1,0:T(8,128)(2,1)}, u32[]{:S(2)}, u32[]{:S(2)}) collective-permute-start(bf16[128,1024]{1,0:T(8,128)(2,1)} %lay.3), channel_id=1, source_target_pairs={{0,6},{1,7},{2,4},{3,5},{4,2},{5,3},{6,0},{7,1},{8,14},{9,15},{10,... | collective-permute-start | bytes 786440 | tf_op jit(solution)/shard_map/ppermute | solution.py:40
  46.4 25.3 %collective-permute-start.31 = (bf16[528,256]{1,0:T(8,128)(2,1)S(1)}, bf16[528,256]{1,0:T(8,128)(2,1)S(1)}, u32[]{:S(2)}, u32[]{:S(2)}) collective-permute-start(bf16[528,256]{1,0:T(8,128)(2,1)S(1)} %get-tuple-element.130), channel_id=1, source_target_pairs={{0,24},{1,25},{2,26},{3,27},{4,28},{5,29},{6,30},{7,31},{8,16},{9,... | collective-permute-start | bytes 811016 | tf_op jit(solution)/shard_map/ppermute | solution.py:40
  50.3 23.2 %collective-permute-start.32 = (bf16[528,256]{1,0:T(8,128)(2,1)S(1)}, bf16[528,256]{1,0:T(8,128)(2,1)S(1)}, u32[]{:S(2)}, u32[]{:S(2)}) collective-permute-start(bf16[528,256]{1,0:T(8,128)(2,1)S(1)} %get-tuple-element.131), channel_id=1, source_target_pairs={{0,16},{1,17},{2,18},{3,19},{4,20},{5,21},{6,22},{7,23},{8,24},{9,... | collective-permute-start | bytes 811016 | tf_op jit(solution)/shard_map/ppermute | solution.py:40
  50.3 23.2 %collective-permute-start.33 = (bf16[528,256]{1,0:T(8,128)(2,1)S(1)}, bf16[528,256]{1,0:T(8,128)(2,1)S(1)}, u32[]{:S(2)}, u32[]{:S(2)}) collective-permute-start(bf16[528,256]{1,0:T(8,128)(2,1)S(1)} %get-tuple-element.132), channel_id=1, source_target_pairs={{0,8},{1,9},{2,10},{3,11},{4,12},{5,13},{6,14},{7,15},{8,0},{9,1},... | collective-permute-start | bytes 811016 | tf_op jit(solution)/shard_map/ppermute | solution.py:40
  50.9 7.7 %collective-permute-start.4 = (bf16[128,1024]{1,0:T(8,128)(2,1)}, bf16[128,1024]{1,0:T(8,128)(2,1)S(1)}, u32[]{:S(2)}, u32[]{:S(2)}) collective-permute-start(bf16[128,1024]{1,0:T(8,128)(2,1)} %get-tuple-element.16.refs_0_), channel_id=1, source_target_pairs={{0,2},{1,3},{2,0},{3,1},{4,6},{5,7},{6,4},{7,5},{8,10},{9,11},{10,... | collective-permute-start | bytes 786440 | tf_op jit(solution)/shard_map/cond/branch_1_fun/ppermute | solution.py:40
  50.9 7.7 %collective-permute-start.5 = (bf16[128,1024]{1,0:T(8,128)(2,1)}, bf16[128,1024]{1,0:T(8,128)(2,1)S(1)}, u32[]{:S(2)}, u32[]{:S(2)}) collective-permute-start(bf16[128,1024]{1,0:T(8,128)(2,1)} %get-tuple-element.16.refs_0_), channel_id=1, source_target_pairs={{0,4},{1,5},{2,6},{3,7},{4,0},{5,1},{6,2},{7,3},{8,12},{9,13},{10,... | collective-permute-start | bytes 786440 | tf_op jit(solution)/shard_map/cond/branch_1_fun/ppermute | solution.py:40
  58.6 3.9 %collective-permute-start.7 = (bf16[256,1024]{1,0:T(8,128)(2,1)S(1)}, bf16[256,1024]{1,0:T(8,128)(2,1)S(1)}, u32[]{:S(2)}, u32[]{:S(2)}) collective-permute-start(bf16[256,1024]{1,0:T(8,128)(2,1)S(1)} %pad_maximum_fusion.1), channel_id=1, source_target_pairs={{0,1},{1,0},{2,3},{3,2},{4,5},{5,4},{6,7},{7,6},{8,9},{9,8},{10,11... | collective-permute-start | bytes 1572872 | tf_op jit(solution)/shard_map/cond/branch_1_fun/ppermute | solution.py:40
  59.8 2.8 %collective-permute-start.6 = (bf16[256,1024]{1,0:T(8,128)(2,1)S(1)}, bf16[256,1024]{1,0:T(8,128)(2,1)S(1)}, u32[]{:S(2)}, u32[]{:S(2)}) collective-permute-start(bf16[256,1024]{1,0:T(8,128)(2,1)S(1)} %pad_maximum_fusion), channel_id=1, source_target_pairs={{0,1},{1,0},{2,3},{3,2},{4,5},{5,4},{6,7},{7,6},{8,9},{9,8},{10,11... | collective-permute-start | bytes 1572872 | tf_op jit(solution)/shard_map/cond/branch_1_fun/ppermute | solution.py:40
  67.7 25.5 %collective-permute-start.28 = (bf16[528,256]{1,0:T(8,128)(2,1)}, bf16[528,256]{1,0:T(8,128)(2,1)S(1)}, u32[]{:S(2)}, u32[]{:S(2)}) collective-permute-start(bf16[528,256]{1,0:T(8,128)(2,1)} %get-tuple-element.126), channel_id=1, source_target_pairs={{0,8},{1,9},{2,10},{3,11},{4,12},{5,13},{6,14},{7,15},{8,0},{9,1},... | collective-permute-start | bytes 811016 | tf_op jit(solution)/shard_map/ppermute | solution.py:40
  69.1 25.9 %collective-permute-start.29 = (bf16[528,256]{1,0:T(8,128)(2,1)}, bf16[528,256]{1,0:T(8,128)(2,1)S(1)}, u32[]{:S(2)}, u32[]{:S(2)}) collective-permute-start(bf16[528,256]{1,0:T(8,128)(2,1)} %get-tuple-element.127), channel_id=1, source_target_pairs={{0,16},{1,17},{2,18},{3,19},{4,20},{5,21},{6,22},{7,23},{8,24},{9,... | collective-permute-start | bytes 811016 | tf_op jit(solution)/shard_map/ppermute | solution.py:40
  71.7 23.2 %collective-permute-start.30 = (bf16[528,256]{1,0:T(8,128)(2,1)}, bf16[528,256]{1,0:T(8,128)(2,1)S(1)}, u32[]{:S(2)}, u32[]{:S(2)}) collective-permute-start(bf16[528,256]{1,0:T(8,128)(2,1)} %get-tuple-element.128), channel_id=1, source_target_pairs={{0,24},{1,25},{2,26},{3,27},{4,28},{5,29},{6,30},{7,31},{8,16},{9,... | collective-permute-start | bytes 811016 | tf_op jit(solution)/shard_map/ppermute | solution.py:40
  76.8 2.1 %collective-permute-start = (f32[256,512]{1,0:T(8,128)}, f32[256,512]{1,0:T(8,128)S(1)}, u32[]{:S(2)}, u32[]{:S(2)}) collective-permute-start(f32[256,512]{1,0:T(8,128)} %get-tuple-element.26), channel_id=1, source_target_pairs={{0,1},{1,0},{2,3},{3,2},{4,5},{5,4},{6,7},{7,6},{8,9},{9,8},{10,11... | collective-permute-start | bytes 1572872 | tf_op jit(solution)/shard_map/cond/branch_1_fun/ppermute | solution.py:40
  80.3 4.3 %collective-permute-start.1 = (bf16[80,384]{1,0:T(8,128)(2,1)S(1)}, bf16[80,384]{1,0:T(8,128)(2,1)S(1)}, u32[]{:S(2)}, u32[]{:S(2)}) collective-permute-start(bf16[80,384]{1,0:T(8,128)(2,1)S(1)} %get-tuple-element.28), channel_id=1, source_target_pairs={{0,2},{1,3},{2,0},{3,1},{4,6},{5,7},{6,4},{7,5},{8,10},{9,11},{10,... | collective-permute-start | bytes 184328 | tf_op jit(solution)/shard_map/cond/branch_1_fun/ppermute | solution.py:40
  80.7 4.2 %collective-permute-start.2 = (bf16[80,384]{1,0:T(8,128)(2,1)S(1)}, bf16[80,384]{1,0:T(8,128)(2,1)S(1)}, u32[]{:S(2)}, u32[]{:S(2)}) collective-permute-start(bf16[80,384]{1,0:T(8,128)(2,1)S(1)} %get-tuple-element.31), channel_id=1, source_target_pairs={{0,4},{1,5},{2,6},{3,7},{4,0},{5,1},{6,2},{7,3},{8,12},{9,13},{10,... | collective-permute-start | bytes 184328 | tf_op jit(solution)/shard_map/cond/branch_1_fun/ppermute | solution.py:40
  84.5 5.1 %collective-permute-start.3 = (bf16[80,384]{1,0:T(8,128)(2,1)S(1)}, bf16[80,384]{1,0:T(8,128)(2,1)S(1)}, u32[]{:S(2)}, u32[]{:S(2)}) collective-permute-start(bf16[80,384]{1,0:T(8,128)(2,1)S(1)} %get-tuple-element.32), channel_id=1, source_target_pairs={{0,6},{1,7},{2,4},{3,5},{4,2},{5,3},{6,0},{7,1},{8,14},{9,15},{10,... | collective-permute-start | bytes 184328 | tf_op jit(solution)/shard_map/cond/branch_1_fun/ppermute | solution.py:40
  90.5 4.5 %collective-permute-start.34 = (f32[16,384]{1,0:T(8,128)S(1)}, f32[16,384]{1,0:T(8,128)S(1)}, u32[]{:S(2)}, u32[]{:S(2)}) collective-permute-start(f32[16,384]{1,0:T(8,128)S(1)} %get-tuple-element.136), channel_id=1, source_target_pairs={{0,8},{1,9},{2,10},{3,11},{4,12},{5,13},{6,14},{7,15},{8,0},{9,1},... | collective-permute-start | bytes 73736 | tf_op jit(solution)/shard_map/ppermute | solution.py:40
  90.5 7.2 %collective-permute-start.35 = (f32[16,384]{1,0:T(8,128)S(1)}, f32[16,384]{1,0:T(8,128)S(1)}, u32[]{:S(2)}, u32[]{:S(2)}) collective-permute-start(f32[16,384]{1,0:T(8,128)S(1)} %get-tuple-element.137), channel_id=1, source_target_pairs={{0,16},{1,17},{2,18},{3,19},{4,20},{5,21},{6,22},{7,23},{8,24},{9,... | collective-permute-start | bytes 73736 | tf_op jit(solution)/shard_map/ppermute | solution.py:40
  93.2 5.6 %collective-permute-start.36 = (f32[16,384]{1,0:T(8,128)S(1)}, f32[16,384]{1,0:T(8,128)S(1)}, u32[]{:S(2)}, u32[]{:S(2)}) collective-permute-start(f32[16,384]{1,0:T(8,128)S(1)} %get-tuple-element.138), channel_id=1, source_target_pairs={{0,24},{1,25},{2,26},{3,27},{4,28},{5,29},{6,30},{7,31},{8,16},{9,... | collective-permute-start | bytes 73736 | tf_op jit(solution)/shard_map/ppermute | solution.py:40
  101.4 2.0 %collective-permute-start.37 = (f32[256,512]{1,0:T(8,128)S(1)}, f32[256,512]{1,0:T(8,128)S(1)}, u32[]{:S(2)}, u32[]{:S(2)}) collective-permute-start(f32[256,512]{1,0:T(8,128)S(1)} %get-tuple-element.145), channel_id=1, source_target_pairs={{0,1},{1,0},{2,3},{3,2},{4,5},{5,4},{6,7},{7,6},{8,9},{9,8},{10,11... | collective-permute-start | bytes 1572872 | tf_op jit(solution)/shard_map/ppermute | solution.py:40
  104.2 4.3 %collective-permute-start.38 = (bf16[80,384]{1,0:T(8,128)(2,1)S(1)}, bf16[80,384]{1,0:T(8,128)(2,1)S(1)}, u32[]{:S(2)}, u32[]{:S(2)}) collective-permute-start(bf16[80,384]{1,0:T(8,128)(2,1)S(1)} %get-tuple-element.147), channel_id=1, source_target_pairs={{0,2},{1,3},{2,0},{3,1},{4,6},{5,7},{6,4},{7,5},{8,10},{9,11},{10,... | collective-permute-start | bytes 184328 | tf_op jit(solution)/shard_map/ppermute | solution.py:40
  106.0 4.8 %collective-permute-start.39 = (bf16[80,384]{1,0:T(8,128)(2,1)S(1)}, bf16[80,384]{1,0:T(8,128)(2,1)S(1)}, u32[]{:S(2)}, u32[]{:S(2)}) collective-permute-start(bf16[80,384]{1,0:T(8,128)(2,1)S(1)} %get-tuple-element.148), channel_id=1, source_target_pairs={{0,4},{1,5},{2,6},{3,7},{4,0},{5,1},{6,2},{7,3},{8,12},{9,13},{10,... | collective-permute-start | bytes 184328 | tf_op jit(solution)/shard_map/ppermute | solution.py:40
  106.4 5.1 %collective-permute-start.40 = (bf16[80,384]{1,0:T(8,128)(2,1)S(1)}, bf16[80,384]{1,0:T(8,128)(2,1)S(1)}, u32[]{:S(2)}, u32[]{:S(2)}) collective-permute-start(bf16[80,384]{1,0:T(8,128)(2,1)S(1)} %get-tuple-element.149), channel_id=1, source_target_pairs={{0,6},{1,7},{2,4},{3,5},{4,2},{5,3},{6,0},{7,1},{8,14},{9,15},{10,... | collective-permute-start | bytes 184328 | tf_op jit(solution)/shard_map/ppermute | solution.py:40
  112.3 6.5 %collective-permute-start.43 = (bf16[96,384]{1,0:T(8,128)(2,1)S(1)}, bf16[96,384]{1,0:T(8,128)(2,1)S(1)}, u32[]{:S(2)}, u32[]{:S(2)}) collective-permute-start(bf16[96,384]{1,0:T(8,128)(2,1)S(1)} %code.1.refs_0_), channel_id=1, source_target_pairs={{0,24},{1,25},{2,26},{3,27},{4,28},{5,29},{6,30},{7,31},{8,16},{9,... | collective-permute-start | bytes 221192 | tf_op jit(solution)/shard_map/ppermute | solution.py:40
  113.5 6.8 %collective-permute-start.42 = (bf16[96,384]{1,0:T(8,128)(2,1)S(1)}, bf16[96,384]{1,0:T(8,128)(2,1)S(1)}, u32[]{:S(2)}, u32[]{:S(2)}) collective-permute-start(bf16[96,384]{1,0:T(8,128)(2,1)S(1)} %code.1.refs_0_), channel_id=1, source_target_pairs={{0,16},{1,17},{2,18},{3,19},{4,20},{5,21},{6,22},{7,23},{8,24},{9,... | collective-permute-start | bytes 221192 | tf_op jit(solution)/shard_map/ppermute | solution.py:40
  113.5 6.8 %collective-permute-start.41 = (bf16[96,384]{1,0:T(8,128)(2,1)S(1)}, bf16[96,384]{1,0:T(8,128)(2,1)S(1)}, u32[]{:S(2)}, u32[]{:S(2)}) collective-permute-start(bf16[96,384]{1,0:T(8,128)(2,1)S(1)} %code.1.refs_0_), channel_id=1, source_target_pairs={{0,8},{1,9},{2,10},{3,11},{4,12},{5,13},{6,14},{7,15},{8,0},{9,1},... | collective-permute-start | bytes 221192 | tf_op jit(solution)/shard_map/ppermute | solution.py:40
  121.2 6.3 %collective-permute-start.46 = (bf16[128,384]{1,0:T(8,128)(2,1)S(1)}, bf16[128,384]{1,0:T(8,128)(2,1)S(1)}, u32[]{:S(2)}, u32[]{:S(2)}) collective-permute-start(bf16[128,384]{1,0:T(8,128)(2,1)S(1)} %finish.1.refs_0_), channel_id=1, source_target_pairs={{0,6},{1,7},{2,4},{3,5},{4,2},{5,3},{6,0},{7,1},{8,14},{9,15},{10,... | collective-permute-start | bytes 294920 | tf_op jit(solution)/shard_map/ppermute | solution.py:40
  123.1 5.0 %collective-permute-start.45 = (bf16[128,384]{1,0:T(8,128)(2,1)S(1)}, bf16[128,384]{1,0:T(8,128)(2,1)S(1)}, u32[]{:S(2)}, u32[]{:S(2)}) collective-permute-start(bf16[128,384]{1,0:T(8,128)(2,1)S(1)} %finish.1.refs_0_), channel_id=1, source_target_pairs={{0,4},{1,5},{2,6},{3,7},{4,0},{5,1},{6,2},{7,3},{8,12},{9,13},{10,... | collective-permute-start | bytes 294920 | tf_op jit(solution)/shard_map/ppermute | solution.py:40
  124.3 4.6 %collective-permute-start.44 = (bf16[128,384]{1,0:T(8,128)(2,1)S(1)}, bf16[128,384]{1,0:T(8,128)(2,1)S(1)}, u32[]{:S(2)}, u32[]{:S(2)}) collective-permute-start(bf16[128,384]{1,0:T(8,128)(2,1)S(1)} %finish.1.refs_0_), channel_id=1, source_target_pairs={{0,2},{1,3},{2,0},{3,1},{4,6},{5,7},{6,4},{7,5},{8,10},{9,11},{10,... | collective-permute-start | bytes 294920 | tf_op jit(solution)/shard_map/ppermute | solution.py:40
  124.7 4.2 %collective-permute-start.47 = (bf16[128,384]{1,0:T(8,128)(2,1)S(1)}, bf16[128,384]{1,0:T(8,128)(2,1)S(1)}, u32[]{:S(2)}, u32[]{:S(2)}) collective-permute-start(bf16[128,384]{1,0:T(8,128)(2,1)S(1)} %finish.1.refs_0_), channel_id=1, source_target_pairs={{0,1},{1,0},{2,3},{3,2},{4,5},{5,4},{6,7},{7,6},{8,9},{9,8},{10,11... | collective-permute-start | bytes 294920 | tf_op jit(solution)/shard_map/ppermute | solution.py:40
  127.5 1.5 collective-permute-start.50
  128.1 1.3 collective-permute-start.49
  128.9 1.3 collective-permute-start.48
  132.2 8.3 %collective-permute-start.51 = (bf16[256,256]{1,0:T(8,128)(2,1)S(1)}, bf16[256,256]{1,0:T(8,128)(2,1)S(1)}, u32[]{:S(2)}, u32[]{:S(2)}) collective-permute-start(bf16[256,256]{1,0:T(8,128)(2,1)S(1)} %get-tuple-element.161), channel_id=1, source_target_pairs={{0,24},{1,25},{2,26},{3,27},{4,28},{5,29},{6,30},{7,31},{8,16},{9,... | collective-permute-start | bytes 393224 | tf_op jit(solution)/shard_map/ppermute | solution.py:40
  134.0 12.5 %collective-permute-start.52 = (bf16[256,256]{1,0:T(8,128)(2,1)S(1)}, bf16[256,256]{1,0:T(8,128)(2,1)S(1)}, u32[]{:S(2)}, u32[]{:S(2)}) collective-permute-start(bf16[256,256]{1,0:T(8,128)(2,1)S(1)} %get-tuple-element.162), channel_id=1, source_target_pairs={{0,16},{1,17},{2,18},{3,19},{4,20},{5,21},{6,22},{7,23},{8,24},{9,... | collective-permute-start | bytes 393224 | tf_op jit(solution)/shard_map/ppermute | solution.py:40
  134.6 12.0 %collective-permute-start.53 = (bf16[256,256]{1,0:T(8,128)(2,1)S(1)}, bf16[256,256]{1,0:T(8,128)(2,1)S(1)}, u32[]{:S(2)}, u32[]{:S(2)}) collective-permute-start(bf16[256,256]{1,0:T(8,128)(2,1)S(1)} %get-tuple-element.163), channel_id=1, source_target_pairs={{0,8},{1,9},{2,10},{3,11},{4,12},{5,13},{6,14},{7,15},{8,0},{9,1},... | collective-permute-start | bytes 393224 | tf_op jit(solution)/shard_map/ppermute | solution.py:40

commit v14 on v13

--- a/solution.py
+++ b/solution.py
@@ -97,6 +97,20 @@
 
 BLOCKS = 4
 KEPT = 3
+
+
+def folded(values):
+    width = values.shape[1] // KEPT
+    return jnp.concatenate([values[:, i * width : (i + 1) * width] for i in range(KEPT)], 0)
+
+
+def unfolded(values):
+    height = values.shape[0] // KEPT
+    return jnp.concatenate([values[i * height : (i + 1) * height] for i in range(KEPT)], 1)
+
+
+def folded_shape(rows, columns):
+    return (rows * KEPT + SCALE_ROWS, columns // KEPT)
 
 
 def halve_kernel(place_ref, kept_ref, met_ref, *outs, n):
@@ -114,11 +128,11 @@
         if step == 0:
             out[...] = total
         else:
-            encode(total, out)
+            encode(folded(total), out)
 
 
 def plane_sum(met):
-    return tree_sum([met[0][...]] + [decode(ref, 1)[0] for ref in met[1:]])
+    return tree_sum([met[0][...]] + [unfolded(decode(ref, 1)[0]) for ref in met[1:]])
 
 
 def plane_kernel(place_ref, *refs, n):
@@ -127,31 +141,34 @@
     height = outs[0].shape[0]
     for step, out in enumerate(outs):
         at = pl.ds(pl.multiple_of((place_ref[0] ^ step) * height, height), height)
-        out[...] = whole_ref[at, :]
+        if step == 0:
+            out[...] = whole_ref[at, :]
+        else:
+            encode(folded(whole_ref[at, :]), out)
 
 
 def rows_kernel(place_ref, *refs):
-    refs[-1][...] = tree_sum([ref[...] for ref in refs[:-1]]).astype(BF16)
+    refs[-1][...] = plane_sum(refs[:-1]).astype(BF16)
 
 
 def code_kernel(place_ref, *refs, n):
     met, rows_ref, out_ref = refs[:n], refs[n], refs[n + 1]
-    total = plane_sum(met)
+    total = folded(plane_sum(met))
     coded = total.shape[0] + SCALE_ROWS
     encode(total, out_ref.at[:coded])
-    out_ref[coded:] = rows_ref[...]
+    out_ref[coded:] = folded(rows_ref[...])
 
 
 def finish_kernel(place_ref, *refs, n, k):
     out_ref = refs[-1]
     height = out_ref.shape[0] // 2
-    coded, few = height + SCALE_ROWS, height // n
+    coded, few = height * KEPT + SCALE_ROWS, height // n
     met = []
     for step in range(n):
         at = pl.ds(pl.multiple_of((place_ref[0] ^ step) * few, few), few)
-        out_ref[at, :] = refs[step][coded:]
+        out_ref[at, :] = unfolded(refs[step][coded:])
         met += decode(refs[step].at[:coded], 1)
-    total = tree_sum(met)
+    total = unfolded(tree_sum(met))
     last = (place_ref[1] == n - 1) & (place_ref[2] == k - 1)
     start = 2 * (total.shape[1] // KEPT)
     edge = total[-8:, start:]
@@ -189,7 +206,7 @@
         functools.partial(halve_kernel, n=place.n),
         place_array,
         (kept, other),
-        [((height, batch), F32)] + [((height + SCALE_ROWS, batch), BF16)] * (place.n - 1),
+        [((height, batch), F32)] + [(folded_shape(height, batch), BF16)] * (place.n - 1),
         "halve",
     )
     return sends(place, "a", parts, few)
@@ -198,11 +215,12 @@
 def first_rows(place, place_array, grams):
     parts = plane_rows(place, place_array, grams, True)
     height, batch = parts[0].shape
+    few = height // place.n
     return local(
         functools.partial(plane_kernel, n=place.n),
         place_array,
         parts,
-        [((height // place.n, batch), F32)] * place.n,
+        [((few, batch), F32)] + [(folded_shape(few, batch), BF16)] * (place.n - 1),
         "plane",
         scratch_shapes=[pltpu.VMEM((height, batch), F32)],
     )
@@ -511,8 +529,8 @@
 def with_kernels(place, h_first, h_second, weight):
     n, k, z, a, b = place.n, place.k, place.z, place.a, place.b
     place_array = jnp.stack([z, a, b]).astype(jnp.int32)
-    first, second = lax.optimization_barrier((to_columns(place, h_first), h_second))
-    first, second = to_planes(place, first), to_columns(place, second)
+    first = to_columns(place, h_first)
+    first, second = lax.optimization_barrier((to_planes(place, first), to_columns(place, h_second)))
     first, late_weight = lax.optimization_barrier((lay(place, place_array, first), weight))
     met_1, second, held = lax.optimization_barrier(
         (met_rows(place, first), to_planes(place, second), fetch(late_weight))
@@ -559,7 +577,7 @@
         functools.partial(code_kernel, n=n),
         place_array,
         (*met_2, rows_1),
-        [((rows + SCALE_ROWS + height, batch), BF16)],
+        [((folded_shape(rows, batch)[0] + height * KEPT, batch // KEPT), BF16)],
         "code",
     )
     (part,) = local(

time: 148 us -> 146 us (0.986)
  starting transfers between devices: 56.5 us -> 54 us
    ppermute x54, starting transfers between devices: 56.5 us -> 54 us  [send(): return lax.ppermute(value, ('dp', 'mp'), pairs)]
where the time goes in v14:
time: 146 us; the launch traced here: 145 us
  waiting for transfers between devices  54.1 us (37%)
  starting transfers between devices  54 us (37%)
  Pallas kernels  32.1 us (22%)
  other arithmetic  2.07 us (1%)
  local copies, waits for them, and re-layouts  1.88 us (1%)
    ppermute x54, waiting for transfers between devices, send(): return lax.ppermute(value, ('dp', 'mp'), pairs)  54.1 us
    ppermute x54, starting transfers between devices, send(): return lax.ppermute(value, ('dp', 'mp'), pairs)  54 us
    pallas_call x11, Pallas kernels, local(): pl.pallas_call(kernel, in_specs=[pl.BlockSpec(memory_space=pltpu.SMEM)] +...  12.7 us
    pallas_call x2, Pallas kernels, project(): pl.pallas_call(functools.partial(project_kernel, counts=counts, n=n, k=k)...  9.01 us
    pallas_call x2, Pallas kernels, normalize_parts(): pl.pallas_call(functools.partial(normalize_kernel, n=n, k=k, order=order,...  6.02 us
    pallas_call x2, Pallas kernels, fetch(): pl.pallas_call(fetch_kernel, in_specs=[pl.BlockSpec(memory_space=pl.ANY)]...  4.39 us
  transfers between devices with their start and end apart: 54, of which 27 were waited for; matrix products, arithmetic and copies ran while one was open for 2% of the time, Pallas kernels for 16%

profile of v14, /device:TPU:0, one launch (start us, length us, event | category | flops | bytes accessed | tf_op | source)
XLA Modules:
  0.0 145.1 jit_solution(6349582676855712721)
XLA Ops:
  0.7 0.9 dynamic-slice_bitcast_fusion.4
  1.6 3.0 %collective-permute-start.10 = (bf16[32,1024]{1,0:T(8,128)(2,1)S(1)}, bf16[32,1024]{1,0:T(8,128)(2,1)S(1)}, u32[]{:S(2)}, u32[]{:S(2)}) collective-permute-start(bf16[32,1024]{1,0:T(8,128)(2,1)S(1)} %get-tuple-element.186), channel_id=1, source_target_pairs={{0,2},{1,3},{2,0},{3,1},{4,6},{5,7},{6,4},{7,5},{8,10},{9,11},{10,... | collective-permute-start | bytes 196616 | tf_op jit(solution)/shard_map/ppermute | solution.py:40
  4.6 1.5 %collective-permute-start.9 = (bf16[32,1024]{1,0:T(8,128)(2,1)S(1)}, bf16[32,1024]{1,0:T(8,128)(2,1)S(1)}, u32[]{:S(2)}, u32[]{:S(2)}) collective-permute-start(bf16[32,1024]{1,0:T(8,128)(2,1)S(1)} %get-tuple-element.187), channel_id=1, source_target_pairs={{0,4},{1,5},{2,6},{3,7},{4,0},{5,1},{6,2},{7,3},{8,12},{9,13},{10,... | collective-permute-start | bytes 196616 | tf_op jit(solution)/shard_map/ppermute | solution.py:40
  6.1 1.0 dynamic-slice_bitcast_fusion
  7.1 3.0 %collective-permute-start.16 = (bf16[32,1024]{1,0:T(8,128)(2,1)S(1)}, bf16[32,1024]{1,0:T(8,128)(2,1)S(1)}, u32[]{:S(2)}, u32[]{:S(2)}) collective-permute-start(bf16[32,1024]{1,0:T(8,128)(2,1)S(1)} %get-tuple-element.182), channel_id=1, source_target_pairs={{0,6},{1,7},{2,4},{3,5},{4,2},{5,3},{6,0},{7,1},{8,14},{9,15},{10,... | collective-permute-start | bytes 196616 | tf_op jit(solution)/shard_map/ppermute | solution.py:40
  11.3 0.9 broadcast_select_fusion.10
  12.2 3.9 %collective-permute-start.13 = (bf16[32,1024]{1,0:T(8,128)(2,1)S(1)}, bf16[32,1024]{1,0:T(8,128)(2,1)S(1)}, u32[]{:S(2)}, u32[]{:S(2)}) collective-permute-start(bf16[32,1024]{1,0:T(8,128)(2,1)S(1)} %get-tuple-element.174), channel_id=1, source_target_pairs={{0,24},{1,25},{2,26},{3,27},{4,28},{5,29},{6,30},{7,31},{8,16},{9,... | collective-permute-start | bytes 196616 | tf_op jit(solution)/shard_map/ppermute | solution.py:40
  16.8 1.6 %collective-permute-done.13.refs_3_ = bf16[32,1024]{1,0:T(8,128)(2,1)S(1)} collective-permute-done((bf16[32,1024]{1,0:T(8,128)(2,1)S(1)}, bf16[32,1024]{1,0:T(8,128)(2,1)S(1)}, u32[]{:S(2)}, u32[]{:S(2)}) %collective-permute-start.13) | collective-permute-done | bytes 65568 | tf_op jit(solution)/shard_map/ppermute | solution.py:40
  18.4 2.1 %collective-permute-done.11.refs_1_ = bf16[32,1024]{1,0:T(8,128)(2,1)S(1)} collective-permute-done((bf16[32,1024]{1,0:T(8,128)(2,1)S(1)}, bf16[32,1024]{1,0:T(8,128)(2,1)S(1)}, u32[]{:S(2)}, u32[]{:S(2)}) %collective-permute-start.11) | collective-permute-done | bytes 65568 | tf_op jit(solution)/shard_map/ppermute | solution.py:40
  21.8 2.1 %collective-permute-start.19 = (bf16[128,1024]{1,0:T(8,128)(2,1)S(1)}, bf16[128,1024]{1,0:T(8,128)(2,1)S(1)}, u32[]{:S(2)}, u32[]{:S(2)}) collective-permute-start(bf16[128,1024]{1,0:T(8,128)(2,1)S(1)} %lay.2.refs_0_), channel_id=1, source_target_pairs={{0,6},{1,7},{2,4},{3,5},{4,2},{5,3},{6,0},{7,1},{8,14},{9,15},{10,... | collective-permute-start | bytes 786440 | tf_op jit(solution)/shard_map/ppermute | solution.py:40
  24.4 0.9 collective-permute-start.17
  25.4 1.7 %collective-permute-start.22 = (bf16[32,1024]{1,0:T(8,128)(2,1)S(1)}, bf16[32,1024]{1,0:T(8,128)(2,1)S(1)}, u32[]{:S(2)}, u32[]{:S(2)}) collective-permute-start(bf16[32,1024]{1,0:T(8,128)(2,1)S(1)} %get-tuple-element.178), channel_id=1, source_target_pairs={{0,24},{1,25},{2,26},{3,27},{4,28},{5,29},{6,30},{7,31},{8,16},{9,... | collective-permute-start | bytes 196616 | tf_op jit(solution)/shard_map/ppermute | solution.py:40
  27.5 4.1 %collective-permute-done.22.refs_3_ = bf16[32,1024]{1,0:T(8,128)(2,1)S(1)} collective-permute-done((bf16[32,1024]{1,0:T(8,128)(2,1)S(1)}, bf16[32,1024]{1,0:T(8,128)(2,1)S(1)}, u32[]{:S(2)}, u32[]{:S(2)}) %collective-permute-start.22) | collective-permute-done | bytes 65568 | tf_op jit(solution)/shard_map/ppermute | solution.py:40
  31.7 2.2 %fetch.3.refs_8_ = bf16[2048,1024]{1,0:T(8,128)(2,1)S(1)} custom-call(bf16[2048,1024]{1,0:T(8,128)(2,1)} %weight_ref), custom_call_target="tpu_custom_call" | custom-call | bytes 8388608 | tf_op jit(solution)/shard_map/fetch/pallas_call | solution.py:264
  33.9 3.6 %collective-permute-done.21.refs_2_ = bf16[32,1024]{1,0:T(8,128)(2,1)S(1)} collective-permute-done((bf16[32,1024]{1,0:T(8,128)(2,1)S(1)}, bf16[32,1024]{1,0:T(8,128)(2,1)S(1)}, u32[]{:S(2)}, u32[]{:S(2)}) %collective-permute-start.21) | collective-permute-done | bytes 65568 | tf_op jit(solution)/shard_map/ppermute | solution.py:40
  38.6 1.3 lay.3
  39.9 1.4 collective-permute-start.27
  41.4 3.9 %project.3 = (f32[512,256]{1,0:T(8,128)S(1)}, bf16[528,256]{1,0:T(8,128)(2,1)S(1)}, bf16[528,256]{1,0:T(8,128)(2,1)S(1)}, bf16[528,256]{1,0:T(8,128)(2,1)S(1)}) custom-call(s32[3]{0:T(128)S(1)} %pad_add_fusion.place_ref, bf16[128,1024]{1,0:T(8,128)(2,1)S(1)} %lay.2.refs_0_, bf16[128,1024]{1,0:T(8,128)(2,1)S(1)} %collective-permute-done.17.refs_1_, ...), custom_call_target="tpu_custom_call" | custom-call | flops 2147483648 | bytes 7864320 | tf_op jit(solution)/shard_map/project/pallas_call | solution.py:358
  45.3 2.4 %collective-permute-start.31 = (bf16[528,256]{1,0:T(8,128)(2,1)S(1)}, bf16[528,256]{1,0:T(8,128)(2,1)S(1)}, u32[]{:S(2)}, u32[]{:S(2)}) collective-permute-start(bf16[528,256]{1,0:T(8,128)(2,1)S(1)} %get-tuple-element.136), channel_id=1, source_target_pairs={{0,24},{1,25},{2,26},{3,27},{4,28},{5,29},{6,30},{7,31},{8,16},{9,... | collective-permute-start | bytes 811016 | tf_op jit(solution)/shard_map/ppermute | solution.py:40
  47.7 0.9 collective-permute-start.32
  48.5 1.2 collective-permute-start.33
  49.7 16.7 %conditional.2 = (f32[512,256]{1,0:T(8,128)S(1)}, bf16[528,256]{1,0:T(8,128)(2,1)}, bf16[528,256]{1,0:T(8,128)(2,1)}, bf16[528,256]{1,0:T(8,128)(2,1)}) conditional(s32[]{:T(128)} %convert_element_type.4, () %tuple.35, (bf16[128,1024]{1,0:T(8,128)(2,1)}, bf16[128,1024]{1,0:T(8,128)(2,1)}, bf16[2048,1024]{1,0:T(8,128)(2,1)}, s32[3]{0:T(128)S(1)}) %tuple.36), branch_computations={%region_0.1_spmd, %region_1.2_spmd} | conditional | flops 2149580800 | bytes 24641728 | solution.py:231
  50.3 1.5 %collective-permute-start.5 = (bf16[128,1024]{1,0:T(8,128)(2,1)}, bf16[128,1024]{1,0:T(8,128)(2,1)S(1)}, u32[]{:S(2)}, u32[]{:S(2)}) collective-permute-start(bf16[128,1024]{1,0:T(8,128)(2,1)} %get-tuple-element.16.refs_0_), channel_id=1, source_target_pairs={{0,4},{1,5},{2,6},{3,7},{4,0},{5,1},{6,2},{7,3},{8,12},{9,13},{10,... | collective-permute-start | bytes 786440 | tf_op jit(solution)/shard_map/cond/branch_1_fun/ppermute | solution.py:40
  51.8 5.3 %collective-permute-done.4.refs_2_ = bf16[128,1024]{1,0:T(8,128)(2,1)S(1)} collective-permute-done((bf16[128,1024]{1,0:T(8,128)(2,1)}, bf16[128,1024]{1,0:T(8,128)(2,1)S(1)}, u32[]{:S(2)}, u32[]{:S(2)}) %collective-permute-start.4) | collective-permute-done | bytes 262176 | tf_op jit(solution)/shard_map/cond/branch_1_fun/ppermute | solution.py:40
  57.5 1.1 pad_maximum_fusion
  59.1 2.2 %fetch.2.refs_6_ = bf16[2048,1024]{1,0:T(8,128)(2,1)S(1)} custom-call(bf16[2048,1024]{1,0:T(8,128)(2,1)} %get-tuple-element.19.weight_ref), custom_call_target="tpu_custom_call" | custom-call | bytes 8388608 | tf_op jit(solution)/shard_map/cond/branch_1_fun/fetch/pallas_call | solution.py:264
  61.3 5.1 %project.2 = (f32[512,256]{1,0:T(8,128)S(1)}, bf16[528,256]{1,0:T(8,128)(2,1)}, bf16[528,256]{1,0:T(8,128)(2,1)}, bf16[528,256]{1,0:T(8,128)(2,1)}) custom-call(s32[3]{0:T(128)S(1)} %get-tuple-element.14.place_ref, bf16[128,1024]{1,0:T(8,128)(2,1)} %get-tuple-element.16.refs_0_, bf16[128,1024]{1,0:T(8,128)(2,1)} %get-tuple-element.17.refs_1_, ...), custom_call_target="tpu_custom_call" | custom-call | flops 2147483648 | bytes 7864320 | tf_op jit(solution)/shard_map/cond/branch_1_fun/project/pallas_call | solution.py:358
  66.4 1.6 %collective-permute-start.28 = (bf16[528,256]{1,0:T(8,128)(2,1)}, bf16[528,256]{1,0:T(8,128)(2,1)S(1)}, u32[]{:S(2)}, u32[]{:S(2)}) collective-permute-start(bf16[528,256]{1,0:T(8,128)(2,1)} %get-tuple-element.132), channel_id=1, source_target_pairs={{0,8},{1,9},{2,10},{3,11},{4,12},{5,13},{6,14},{7,15},{8,0},{9,1},... | collective-permute-start | bytes 811016 | tf_op jit(solution)/shard_map/ppermute | solution.py:40
  68.1 1.2 collective-permute-start.29
  69.3 1.5 %collective-permute-start.30 = (bf16[528,256]{1,0:T(8,128)(2,1)}, bf16[528,256]{1,0:T(8,128)(2,1)S(1)}, u32[]{:S(2)}, u32[]{:S(2)}) collective-permute-start(bf16[528,256]{1,0:T(8,128)(2,1)} %get-tuple-element.134), channel_id=1, source_target_pairs={{0,24},{1,25},{2,26},{3,27},{4,28},{5,29},{6,30},{7,31},{8,16},{9,... | collective-permute-start | bytes 811016 | tf_op jit(solution)/shard_map/ppermute | solution.py:40
  70.8 1.9 %collective-permute-done.32.refs_2_ = bf16[528,256]{1,0:T(8,128)(2,1)S(1)} collective-permute-done((bf16[528,256]{1,0:T(8,128)(2,1)S(1)}, bf16[528,256]{1,0:T(8,128)(2,1)S(1)}, u32[]{:S(2)}, u32[]{:S(2)}) %collective-permute-start.32) | collective-permute-done | bytes 270368 | tf_op jit(solution)/shard_map/ppermute | solution.py:40
  72.7 3.4 %normalize.2 = (f32[512,256]{1,0:T(8,128)S(1)}, bf16[512,256]{1,0:T(8,128)(2,1)S(1)}, f32[1,256]{1,0:T(1,128)S(1)}, f32[256,512]{1,0:T(8,128)}, f32[256,512]{1,0:T(8,128)}) custom-call(s32[3]{0:T(128)S(1)} %pad_add_fusion.place_ref, f32[512,256]{1,0:T(8,128)S(1)} %get-tuple-element.135.refs_0_, bf16[528,256]{1,0:T(8,128)(2,1)S(1)} %collective-permute-done.31.refs_1_, ...), custom_call_target="tpu_custom_call" | custom-call | flops 134217728 | bytes 3145728 | tf_op jit(solution)/shard_map/normalize/pallas_call | solution.py:438
  76.1 13.5 %conditional.3 = ((f32[16,384]{1,0:T(8,128)S(1)}, bf16[64,128]{1,0:T(8,128)(2,1)S(1)}, bf16[64,128]{1,0:T(8,128)(2,1)S(1)}, bf16[64,128]{1,0:T(8,128)(2,1)S(1)})) conditional(s32[]{:T(128)} %convert_element_type.4, () %tuple.38, (f32[256,512]{1,0:T(8,128)}, s32[3]{0:T(128)S(1)}, f32[256,512]{1,0:T(8,128)}) %tuple.39), branch_computations={%region_2.3_spmd, %region_3.4_spmd} | conditional | bytes 2736296 | solution.py:231
  76.1 2.1 %collective-permute-done.met_ref = f32[256,512]{1,0:T(8,128)S(1)} collective-permute-done((f32[256,512]{1,0:T(8,128)}, f32[256,512]{1,0:T(8,128)S(1)}, u32[]{:S(2)}, u32[]{:S(2)}) %collective-permute-start) | collective-permute-done | bytes 524320 | tf_op jit(solution)/shard_map/cond/branch_1_fun/ppermute | solution.py:40
  78.3 1.3 halve.2
  80.4 3.4 %collective-permute-done.1.refs_1_ = bf16[208,128]{1,0:T(8,128)(2,1)S(1)} collective-permute-done((bf16[208,128]{1,0:T(8,128)(2,1)S(1)}, bf16[208,128]{1,0:T(8,128)(2,1)S(1)}, u32[]{:S(2)}, u32[]{:S(2)}) %collective-permute-start.1) | collective-permute-done | bytes 53280 | tf_op jit(solution)/shard_map/cond/branch_1_fun/ppermute | solution.py:40
  84.1 4.7 %collective-permute-done.3.refs_3_ = bf16[208,128]{1,0:T(8,128)(2,1)S(1)} collective-permute-done((bf16[208,128]{1,0:T(8,128)(2,1)S(1)}, bf16[208,128]{1,0:T(8,128)(2,1)S(1)}, u32[]{:S(2)}, u32[]{:S(2)}) %collective-permute-start.3) | collective-permute-done | bytes 53280 | tf_op jit(solution)/shard_map/cond/branch_1_fun/ppermute | solution.py:40
  88.8 0.8 plane.1
  89.7 1.9 %collective-permute-start.35 = (bf16[64,128]{1,0:T(8,128)(2,1)S(1)}, bf16[64,128]{1,0:T(8,128)(2,1)S(1)}, u32[]{:S(2)}, u32[]{:S(2)}) collective-permute-start(bf16[64,128]{1,0:T(8,128)(2,1)S(1)} %get-tuple-element.143), channel_id=1, source_target_pairs={{0,16},{1,17},{2,18},{3,19},{4,20},{5,21},{6,22},{7,23},{8,24},{9,... | collective-permute-start | bytes 49160 | tf_op jit(solution)/shard_map/ppermute | solution.py:40
  91.7 2.5 %collective-permute-start.36 = (bf16[64,128]{1,0:T(8,128)(2,1)S(1)}, bf16[64,128]{1,0:T(8,128)(2,1)S(1)}, u32[]{:S(2)}, u32[]{:S(2)}) collective-permute-start(bf16[64,128]{1,0:T(8,128)(2,1)S(1)} %get-tuple-element.144), channel_id=1, source_target_pairs={{0,24},{1,25},{2,26},{3,27},{4,28},{5,29},{6,30},{7,31},{8,16},{9,... | collective-permute-start | bytes 49160 | tf_op jit(solution)/shard_map/ppermute | solution.py:40
  94.1 2.2 %collective-permute-done.35.refs_2_ = bf16[64,128]{1,0:T(8,128)(2,1)S(1)} collective-permute-done((bf16[64,128]{1,0:T(8,128)(2,1)S(1)}, bf16[64,128]{1,0:T(8,128)(2,1)S(1)}, u32[]{:S(2)}, u32[]{:S(2)}) %collective-permute-start.35) | collective-permute-done | bytes 16416 | tf_op jit(solution)/shard_map/ppermute | solution.py:40
  96.4 0.8 collective-permute-done.36.refs_3_
  97.2 2.6 %normalize.3 = (f32[512,256]{1,0:T(8,128)S(1)}, bf16[512,256]{1,0:T(8,128)(2,1)S(1)}, f32[1,256]{1,0:T(1,128)S(1)}, f32[256,512]{1,0:T(8,128)S(1)}, f32[256,512]{1,0:T(8,128)S(1)}, /*index=5*/f32[1,256]{1,0:T(1,128)S(1)}) custom-call(s32[3]{0:T(128)S(1)} %pad_add_fusion.place_ref, f32[512,256]{1,0:T(8,128)S(1)} %get-tuple-element.145.refs_0_, ...), custom_call_target="tpu_custom_call" | custom-call | flops 134217728 | bytes 3145728 | tf_op jit(solution)/shard_map/normalize/pallas_call | solution.py:438
  99.9 1.9 %collective-permute-done.37.met_ref = f32[256,512]{1,0:T(8,128)S(1)} collective-permute-done((f32[256,512]{1,0:T(8,128)S(1)}, f32[256,512]{1,0:T(8,128)S(1)}, u32[]{:S(2)}, u32[]{:S(2)}) %collective-permute-start.37) | collective-permute-done | bytes 524320 | tf_op jit(solution)/shard_map/ppermute | solution.py:40
  101.8 0.8 halve.3
  103.7 2.4 %collective-permute-start.40 = (bf16[208,128]{1,0:T(8,128)(2,1)S(1)}, bf16[208,128]{1,0:T(8,128)(2,1)S(1)}, u32[]{:S(2)}, u32[]{:S(2)}) collective-permute-start(bf16[208,128]{1,0:T(8,128)(2,1)S(1)} %get-tuple-element.155), channel_id=1, source_target_pairs={{0,6},{1,7},{2,4},{3,5},{4,2},{5,3},{6,0},{7,1},{8,14},{9,15},{10,... | collective-permute-start | bytes 159752 | tf_op jit(solution)/shard_map/ppermute | solution.py:40
  106.8 1.1 collective-permute-done.39.refs_2_
  107.9 0.8 collective-permute-done.40.refs_3_
  108.8 0.8 code.1.refs_0_
  109.6 2.2 %collective-permute-start.43 = (bf16[256,128]{1,0:T(8,128)(2,1)S(1)}, bf16[256,128]{1,0:T(8,128)(2,1)S(1)}, u32[]{:S(2)}, u32[]{:S(2)}) collective-permute-start(bf16[256,128]{1,0:T(8,128)(2,1)S(1)} %code.1.refs_0_), channel_id=1, source_target_pairs={{0,24},{1,25},{2,26},{3,27},{4,28},{5,29},{6,30},{7,31},{8,16},{9,... | collective-permute-start | bytes 196616 | tf_op jit(solution)/shard_map/ppermute | solution.py:40
  111.8 2.3 %collective-permute-start.41 = (bf16[256,128]{1,0:T(8,128)(2,1)S(1)}, bf16[256,128]{1,0:T(8,128)(2,1)S(1)}, u32[]{:S(2)}, u32[]{:S(2)}) collective-permute-start(bf16[256,128]{1,0:T(8,128)(2,1)S(1)} %code.1.refs_0_), channel_id=1, source_target_pairs={{0,8},{1,9},{2,10},{3,11},{4,12},{5,13},{6,14},{7,15},{8,0},{9,1},... | collective-permute-start | bytes 196616 | tf_op jit(solution)/shard_map/ppermute | solution.py:40
  114.1 2.2 %collective-permute-done.43.refs_3_ = bf16[256,128]{1,0:T(8,128)(2,1)S(1)} collective-permute-done((bf16[256,128]{1,0:T(8,128)(2,1)S(1)}, bf16[256,128]{1,0:T(8,128)(2,1)S(1)}, u32[]{:S(2)}, u32[]{:S(2)}) %collective-permute-start.43) | collective-permute-done | bytes 65568 | tf_op jit(solution)/shard_map/ppermute | solution.py:40
  116.3 1.4 collective-permute-done.42.refs_2_
  117.7 1.0 finish.1.refs_0_
  118.7 2.6 %collective-permute-start.46 = (bf16[128,384]{1,0:T(8,128)(2,1)S(1)}, bf16[128,384]{1,0:T(8,128)(2,1)S(1)}, u32[]{:S(2)}, u32[]{:S(2)}) collective-permute-start(bf16[128,384]{1,0:T(8,128)(2,1)S(1)} %finish.1.refs_0_), channel_id=1, source_target_pairs={{0,6},{1,7},{2,4},{3,5},{4,2},{5,3},{6,0},{7,1},{8,14},{9,15},{10,... | collective-permute-start | bytes 294920 | tf_op jit(solution)/shard_map/ppermute | solution.py:40
  122.2 2.6 %collective-permute-done.46.refs_3_ = bf16[128,384]{1,0:T(8,128)(2,1)S(1)} collective-permute-done((bf16[128,384]{1,0:T(8,128)(2,1)S(1)}, bf16[128,384]{1,0:T(8,128)(2,1)S(1)}, u32[]{:S(2)}, u32[]{:S(2)}) %collective-permute-start.46) | collective-permute-done | bytes 98336 | tf_op jit(solution)/shard_map/ppermute | solution.py:40
  124.8 1.1 collective-permute-done.45.refs_2_
  127.5 2.0 %gradient.1 = (bf16[256,256]{1,0:T(8,128)(2,1)S(1)}, bf16[256,256]{1,0:T(8,128)(2,1)S(1)}, bf16[256,256]{1,0:T(8,128)(2,1)S(1)}, bf16[256,256]{1,0:T(8,128)(2,1)...) custom-call(s32[3]{0:T(128)S(1)} %pad_add_fusion.place_ref, bf16[128,384]{1,0:T(8,128)(2,1)S(1)} %finish.1.refs_0_, ...), custom_call_target="tpu_custom_call" | custom-call | tf_op jit(solution)/shard_map/gradient/pallas_call | solution.py:189
  129.5 1.7 %collective-permute-start.51 = (bf16[256,256]{1,0:T(8,128)(2,1)S(1)}, bf16[256,256]{1,0:T(8,128)(2,1)S(1)}, u32[]{:S(2)}, u32[]{:S(2)}) collective-permute-start(bf16[256,256]{1,0:T(8,128)(2,1)S(1)} %get-tuple-element.167), channel_id=1, source_target_pairs={{0,24},{1,25},{2,26},{3,27},{4,28},{5,29},{6,30},{7,31},{8,16},{9,... | collective-permute-start | bytes 393224 | tf_op jit(solution)/shard_map/ppermute | solution.py:40
  131.7 2.2 %collective-permute-start.53 = (bf16[256,256]{1,0:T(8,128)(2,1)S(1)}, bf16[256,256]{1,0:T(8,128)(2,1)S(1)}, u32[]{:S(2)}, u32[]{:S(2)}) collective-permute-start(bf16[256,256]{1,0:T(8,128)(2,1)S(1)} %get-tuple-element.169), channel_id=1, source_target_pairs={{0,8},{1,9},{2,10},{3,11},{4,12},{5,13},{6,14},{7,15},{8,0},{9,1},... | collective-permute-start | bytes 393224 | tf_op jit(solution)/shard_map/ppermute | solution.py:40
  133.9 2.1 %loss.1 = f32[1,1]{1,0:T(1,128)} custom-call(s32[3]{0:T(128)S(1)} %pad_add_fusion.place_ref, bf16[2,512,512]{2,1,0:T(8,128)(2,1)S(1)} %get-tuple-element.172.gram_ref, f32[1,1]{1,0:T(1,128)} %get-tuple-element.173.share_ref), custom_call_target="tpu_custom_call" | custom-call | tf_op jit(solution)/shard_map/loss/pallas_call | solution.py:189
  136.0 1.8 %collective-permute-done.51.refs_1_ = bf16[256,256]{1,0:T(8,128)(2,1)S(1)} collective-permute-done((bf16[256,256]{1,0:T(8,128)(2,1)S(1)}, bf16[256,256]{1,0:T(8,128)(2,1)S(1)}, u32[]{:S(2)}, u32[]{:S(2)}) %collective-permute-start.51) | collective-permute-done | bytes 131104 | tf_op jit(solution)/shard_map/ppermute | solution.py:40
  137.8 5.9 %collective-permute-done.52.refs_2_ = bf16[256,256]{1,0:T(8,128)(2,1)S(1)} collective-permute-done((bf16[256,256]{1,0:T(8,128)(2,1)S(1)}, bf16[256,256]{1,0:T(8,128)(2,1)S(1)}, u32[]{:S(2)}, u32[]{:S(2)}) %collective-permute-start.52) | collective-permute-done | bytes 131104 | tf_op jit(solution)/shard_map/ppermute | solution.py:40
  143.7 1.4 place.1
  (70 shorter events, 13.1 us)
Async XLA Ops:
  1.6 9.0 %collective-permute-start.10 = (bf16[32,1024]{1,0:T(8,128)(2,1)S(1)}, bf16[32,1024]{1,0:T(8,128)(2,1)S(1)}, u32[]{:S(2)}, u32[]{:S(2)}) collective-permute-start(bf16[32,1024]{1,0:T(8,128)(2,1)S(1)} %get-tuple-element.186), channel_id=1, source_target_pairs={{0,2},{1,3},{2,0},{3,1},{4,6},{5,7},{6,4},{7,5},{8,10},{9,11},{10,... | collective-permute-start | bytes 196616 | tf_op jit(solution)/shard_map/ppermute | solution.py:40
  4.6 6.1 %collective-permute-start.9 = (bf16[32,1024]{1,0:T(8,128)(2,1)S(1)}, bf16[32,1024]{1,0:T(8,128)(2,1)S(1)}, u32[]{:S(2)}, u32[]{:S(2)}) collective-permute-start(bf16[32,1024]{1,0:T(8,128)(2,1)S(1)} %get-tuple-element.187), channel_id=1, source_target_pairs={{0,4},{1,5},{2,6},{3,7},{4,0},{5,1},{6,2},{7,3},{8,12},{9,13},{10,... | collective-permute-start | bytes 196616 | tf_op jit(solution)/shard_map/ppermute | solution.py:40
  6.1 5.2 %collective-permute-start.8 = (bf16[32,1024]{1,0:T(8,128)(2,1)S(1)}, bf16[32,1024]{1,0:T(8,128)(2,1)S(1)}, u32[]{:S(2)}, u32[]{:S(2)}) collective-permute-start(bf16[32,1024]{1,0:T(8,128)(2,1)S(1)} %get-tuple-element.188), channel_id=1, source_target_pairs={{0,6},{1,7},{2,4},{3,5},{4,2},{5,3},{6,0},{7,1},{8,14},{9,15},{10,... | collective-permute-start | bytes 196616 | tf_op jit(solution)/shard_map/ppermute | solution.py:40
  7.1 9.0 %collective-permute-start.16 = (bf16[32,1024]{1,0:T(8,128)(2,1)S(1)}, bf16[32,1024]{1,0:T(8,128)(2,1)S(1)}, u32[]{:S(2)}, u32[]{:S(2)}) collective-permute-start(bf16[32,1024]{1,0:T(8,128)(2,1)S(1)} %get-tuple-element.182), channel_id=1, source_target_pairs={{0,6},{1,7},{2,4},{3,5},{4,2},{5,3},{6,0},{7,1},{8,14},{9,15},{10,... | collective-permute-start | bytes 196616 | tf_op jit(solution)/shard_map/ppermute | solution.py:40
  10.1 6.7 %collective-permute-start.15 = (bf16[32,1024]{1,0:T(8,128)(2,1)S(1)}, bf16[32,1024]{1,0:T(8,128)(2,1)S(1)}, u32[]{:S(2)}, u32[]{:S(2)}) collective-permute-start(bf16[32,1024]{1,0:T(8,128)(2,1)S(1)} %get-tuple-element.183), channel_id=1, source_target_pairs={{0,4},{1,5},{2,6},{3,7},{4,0},{5,1},{6,2},{7,3},{8,12},{9,13},{10,... | collective-permute-start | bytes 196616 | tf_op jit(solution)/shard_map/ppermute | solution.py:40
  10.6 6.2 %collective-permute-start.14 = (bf16[32,1024]{1,0:T(8,128)(2,1)S(1)}, bf16[32,1024]{1,0:T(8,128)(2,1)S(1)}, u32[]{:S(2)}, u32[]{:S(2)}) collective-permute-start(bf16[32,1024]{1,0:T(8,128)(2,1)S(1)} %get-tuple-element.184), channel_id=1, source_target_pairs={{0,2},{1,3},{2,0},{3,1},{4,6},{5,7},{6,4},{7,5},{8,10},{9,11},{10,... | collective-permute-start | bytes 196616 | tf_op jit(solution)/shard_map/ppermute | solution.py:40
  12.2 6.2 %collective-permute-start.13 = (bf16[32,1024]{1,0:T(8,128)(2,1)S(1)}, bf16[32,1024]{1,0:T(8,128)(2,1)S(1)}, u32[]{:S(2)}, u32[]{:S(2)}) collective-permute-start(bf16[32,1024]{1,0:T(8,128)(2,1)S(1)} %get-tuple-element.174), channel_id=1, source_target_pairs={{0,24},{1,25},{2,26},{3,27},{4,28},{5,29},{6,30},{7,31},{8,16},{9,... | collective-permute-start | bytes 196616 | tf_op jit(solution)/shard_map/ppermute | solution.py:40
  16.1 4.4 %collective-permute-start.11 = (bf16[32,1024]{1,0:T(8,128)(2,1)S(1)}, bf16[32,1024]{1,0:T(8,128)(2,1)S(1)}, u32[]{:S(2)}, u32[]{:S(2)}) collective-permute-start(bf16[32,1024]{1,0:T(8,128)(2,1)S(1)} %get-tuple-element.175), channel_id=1, source_target_pairs={{0,8},{1,9},{2,10},{3,11},{4,12},{5,13},{6,14},{7,15},{8,0},{9,1},... | collective-permute-start | bytes 196616 | tf_op jit(solution)/shard_map/ppermute | solution.py:40
  16.1 5.2 %collective-permute-start.12 = (bf16[32,1024]{1,0:T(8,128)(2,1)S(1)}, bf16[32,1024]{1,0:T(8,128)(2,1)S(1)}, u32[]{:S(2)}, u32[]{:S(2)}) collective-permute-start(bf16[32,1024]{1,0:T(8,128)(2,1)S(1)} %get-tuple-element.176), channel_id=1, source_target_pairs={{0,16},{1,17},{2,18},{3,19},{4,20},{5,21},{6,22},{7,23},{8,24},{9,... | collective-permute-start | bytes 196616 | tf_op jit(solution)/shard_map/ppermute | solution.py:40
  21.8 15.7 %collective-permute-start.19 = (bf16[128,1024]{1,0:T(8,128)(2,1)S(1)}, bf16[128,1024]{1,0:T(8,128)(2,1)S(1)}, u32[]{:S(2)}, u32[]{:S(2)}) collective-permute-start(bf16[128,1024]{1,0:T(8,128)(2,1)S(1)} %lay.2.refs_0_), channel_id=1, source_target_pairs={{0,6},{1,7},{2,4},{3,5},{4,2},{5,3},{6,0},{7,1},{8,14},{9,15},{10,... | collective-permute-start | bytes 786440 | tf_op jit(solution)/shard_map/ppermute | solution.py:40
  23.9 13.6 %collective-permute-start.18 = (bf16[128,1024]{1,0:T(8,128)(2,1)S(1)}, bf16[128,1024]{1,0:T(8,128)(2,1)S(1)}, u32[]{:S(2)}, u32[]{:S(2)}) collective-permute-start(bf16[128,1024]{1,0:T(8,128)(2,1)S(1)} %lay.2.refs_0_), channel_id=1, source_target_pairs={{0,4},{1,5},{2,6},{3,7},{4,0},{5,1},{6,2},{7,3},{8,12},{9,13},{10,... | collective-permute-start | bytes 786440 | tf_op jit(solution)/shard_map/ppermute | solution.py:40
  24.4 13.1 %collective-permute-start.17 = (bf16[128,1024]{1,0:T(8,128)(2,1)S(1)}, bf16[128,1024]{1,0:T(8,128)(2,1)S(1)}, u32[]{:S(2)}, u32[]{:S(2)}) collective-permute-start(bf16[128,1024]{1,0:T(8,128)(2,1)S(1)} %lay.2.refs_0_), channel_id=1, source_target_pairs={{0,2},{1,3},{2,0},{3,1},{4,6},{5,7},{6,4},{7,5},{8,10},{9,11},{10,... | collective-permute-start | bytes 786440 | tf_op jit(solution)/shard_map/ppermute | solution.py:40
  25.4 6.3 %collective-permute-start.22 = (bf16[32,1024]{1,0:T(8,128)(2,1)S(1)}, bf16[32,1024]{1,0:T(8,128)(2,1)S(1)}, u32[]{:S(2)}, u32[]{:S(2)}) collective-permute-start(bf16[32,1024]{1,0:T(8,128)(2,1)S(1)} %get-tuple-element.178), channel_id=1, source_target_pairs={{0,24},{1,25},{2,26},{3,27},{4,28},{5,29},{6,30},{7,31},{8,16},{9,... | collective-permute-start | bytes 196616 | tf_op jit(solution)/shard_map/ppermute | solution.py:40
  27.0 6.8 %collective-permute-start.20 = (bf16[32,1024]{1,0:T(8,128)(2,1)S(1)}, bf16[32,1024]{1,0:T(8,128)(2,1)S(1)}, u32[]{:S(2)}, u32[]{:S(2)}) collective-permute-start(bf16[32,1024]{1,0:T(8,128)(2,1)S(1)} %get-tuple-element.180), channel_id=1, source_target_pairs={{0,8},{1,9},{2,10},{3,11},{4,12},{5,13},{6,14},{7,15},{8,0},{9,1},... | collective-permute-start | bytes 196616 | tf_op jit(solution)/shard_map/ppermute | solution.py:40
  31.7 5.9 %collective-permute-start.21 = (bf16[32,1024]{1,0:T(8,128)(2,1)S(1)}, bf16[32,1024]{1,0:T(8,128)(2,1)S(1)}, u32[]{:S(2)}, u32[]{:S(2)}) collective-permute-start(bf16[32,1024]{1,0:T(8,128)(2,1)S(1)} %get-tuple-element.181), channel_id=1, source_target_pairs={{0,16},{1,17},{2,18},{3,19},{4,20},{5,21},{6,22},{7,23},{8,24},{9,... | collective-permute-start | bytes 196616 | tf_op jit(solution)/shard_map/ppermute | solution.py:40
  37.5 3.8 %collective-permute-start.23 = (bf16[128,1024]{1,0:T(8,128)(2,1)S(1)}, bf16[128,1024]{1,0:T(8,128)(2,1)S(1)}, u32[]{:S(2)}, u32[]{:S(2)}) collective-permute-start(bf16[128,1024]{1,0:T(8,128)(2,1)S(1)} %lay.2.refs_0_), channel_id=1, source_target_pairs={{0,1},{1,0},{2,3},{3,2},{4,5},{5,4},{6,7},{7,6},{8,9},{9,8},{10,11... | collective-permute-start | bytes 786440 | tf_op jit(solution)/shard_map/ppermute | solution.py:40
  37.6 3.7 %collective-permute-start.24 = (bf16[128,1024]{1,0:T(8,128)(2,1)S(1)}, bf16[128,1024]{1,0:T(8,128)(2,1)S(1)}, u32[]{:S(2)}, u32[]{:S(2)}) collective-permute-start(bf16[128,1024]{1,0:T(8,128)(2,1)S(1)} %collective-permute-done.17.refs_1_), channel_id=1, source_target_pairs={{0,1},{1,0},{2,3},{3,2},{4,5},{5,4},{6,7},{7,6},{8,9},{9,8},{10,11... | collective-permute-start | bytes 786440 | tf_op jit(solution)/shard_map/ppermute | solution.py:40
  38.1 3.2 %collective-permute-start.25 = (bf16[128,1024]{1,0:T(8,128)(2,1)S(1)}, bf16[128,1024]{1,0:T(8,128)(2,1)S(1)}, u32[]{:S(2)}, u32[]{:S(2)}) collective-permute-start(bf16[128,1024]{1,0:T(8,128)(2,1)S(1)} %collective-permute-done.18.refs_2_), channel_id=1, source_target_pairs={{0,1},{1,0},{2,3},{3,2},{4,5},{5,4},{6,7},{7,6},{8,9},{9,8},{10,11... | collective-permute-start | bytes 786440 | tf_op jit(solution)/shard_map/ppermute | solution.py:40
  38.2 3.1 %collective-permute-start.26 = (bf16[128,1024]{1,0:T(8,128)(2,1)S(1)}, bf16[128,1024]{1,0:T(8,128)(2,1)S(1)}, u32[]{:S(2)}, u32[]{:S(2)}) collective-permute-start(bf16[128,1024]{1,0:T(8,128)(2,1)S(1)} %collective-permute-done.19.refs_3_), channel_id=1, source_target_pairs={{0,1},{1,0},{2,3},{3,2},{4,5},{5,4},{6,7},{7,6},{8,9},{9,8},{10,11... | collective-permute-start | bytes 786440 | tf_op jit(solution)/shard_map/ppermute | solution.py:40
  39.9 9.8 %collective-permute-start.27 = (bf16[128,1024]{1,0:T(8,128)(2,1)}, bf16[128,1024]{1,0:T(8,128)(2,1)}, u32[]{:S(2)}, u32[]{:S(2)}) collective-permute-start(bf16[128,1024]{1,0:T(8,128)(2,1)} %lay.3), channel_id=1, source_target_pairs={{0,6},{1,7},{2,4},{3,5},{4,2},{5,3},{6,0},{7,1},{8,14},{9,15},{10,... | collective-permute-start | bytes 786440 | tf_op jit(solution)/shard_map/ppermute | solution.py:40
  45.3 24.1 %collective-permute-start.31 = (bf16[528,256]{1,0:T(8,128)(2,1)S(1)}, bf16[528,256]{1,0:T(8,128)(2,1)S(1)}, u32[]{:S(2)}, u32[]{:S(2)}) collective-permute-start(bf16[528,256]{1,0:T(8,128)(2,1)S(1)} %get-tuple-element.136), channel_id=1, source_target_pairs={{0,24},{1,25},{2,26},{3,27},{4,28},{5,29},{6,30},{7,31},{8,16},{9,... | collective-permute-start | bytes 811016 | tf_op jit(solution)/shard_map/ppermute | solution.py:40
  47.7 25.1 %collective-permute-start.32 = (bf16[528,256]{1,0:T(8,128)(2,1)S(1)}, bf16[528,256]{1,0:T(8,128)(2,1)S(1)}, u32[]{:S(2)}, u32[]{:S(2)}) collective-permute-start(bf16[528,256]{1,0:T(8,128)(2,1)S(1)} %get-tuple-element.137), channel_id=1, source_target_pairs={{0,16},{1,17},{2,18},{3,19},{4,20},{5,21},{6,22},{7,23},{8,24},{9,... | collective-permute-start | bytes 811016 | tf_op jit(solution)/shard_map/ppermute | solution.py:40
  48.5 24.2 %collective-permute-start.33 = (bf16[528,256]{1,0:T(8,128)(2,1)S(1)}, bf16[528,256]{1,0:T(8,128)(2,1)S(1)}, u32[]{:S(2)}, u32[]{:S(2)}) collective-permute-start(bf16[528,256]{1,0:T(8,128)(2,1)S(1)} %get-tuple-element.138), channel_id=1, source_target_pairs={{0,8},{1,9},{2,10},{3,11},{4,12},{5,13},{6,14},{7,15},{8,0},{9,1},... | collective-permute-start | bytes 811016 | tf_op jit(solution)/shard_map/ppermute | solution.py:40
  49.7 7.4 %collective-permute-start.4 = (bf16[128,1024]{1,0:T(8,128)(2,1)}, bf16[128,1024]{1,0:T(8,128)(2,1)S(1)}, u32[]{:S(2)}, u32[]{:S(2)}) collective-permute-start(bf16[128,1024]{1,0:T(8,128)(2,1)} %get-tuple-element.16.refs_0_), channel_id=1, source_target_pairs={{0,2},{1,3},{2,0},{3,1},{4,6},{5,7},{6,4},{7,5},{8,10},{9,11},{10,... | collective-permute-start | bytes 786440 | tf_op jit(solution)/shard_map/cond/branch_1_fun/ppermute | solution.py:40
  50.3 7.1 %collective-permute-start.5 = (bf16[128,1024]{1,0:T(8,128)(2,1)}, bf16[128,1024]{1,0:T(8,128)(2,1)S(1)}, u32[]{:S(2)}, u32[]{:S(2)}) collective-permute-start(bf16[128,1024]{1,0:T(8,128)(2,1)} %get-tuple-element.16.refs_0_), channel_id=1, source_target_pairs={{0,4},{1,5},{2,6},{3,7},{4,0},{5,1},{6,2},{7,3},{8,12},{9,13},{10,... | collective-permute-start | bytes 786440 | tf_op jit(solution)/shard_map/cond/branch_1_fun/ppermute | solution.py:40
  57.4 3.9 %collective-permute-start.7 = (bf16[256,1024]{1,0:T(8,128)(2,1)S(1)}, bf16[256,1024]{1,0:T(8,128)(2,1)S(1)}, u32[]{:S(2)}, u32[]{:S(2)}) collective-permute-start(bf16[256,1024]{1,0:T(8,128)(2,1)S(1)} %pad_maximum_fusion.1), channel_id=1, source_target_pairs={{0,1},{1,0},{2,3},{3,2},{4,5},{5,4},{6,7},{7,6},{8,9},{9,8},{10,11... | collective-permute-start | bytes 1572872 | tf_op jit(solution)/shard_map/cond/branch_1_fun/ppermute | solution.py:40
  58.6 2.8 %collective-permute-start.6 = (bf16[256,1024]{1,0:T(8,128)(2,1)S(1)}, bf16[256,1024]{1,0:T(8,128)(2,1)S(1)}, u32[]{:S(2)}, u32[]{:S(2)}) collective-permute-start(bf16[256,1024]{1,0:T(8,128)(2,1)S(1)} %pad_maximum_fusion), channel_id=1, source_target_pairs={{0,1},{1,0},{2,3},{3,2},{4,5},{5,4},{6,7},{7,6},{8,9},{9,8},{10,11... | collective-permute-start | bytes 1572872 | tf_op jit(solution)/shard_map/cond/branch_1_fun/ppermute | solution.py:40
  66.4 25.2 %collective-permute-start.28 = (bf16[528,256]{1,0:T(8,128)(2,1)}, bf16[528,256]{1,0:T(8,128)(2,1)S(1)}, u32[]{:S(2)}, u32[]{:S(2)}) collective-permute-start(bf16[528,256]{1,0:T(8,128)(2,1)} %get-tuple-element.132), channel_id=1, source_target_pairs={{0,8},{1,9},{2,10},{3,11},{4,12},{5,13},{6,14},{7,15},{8,0},{9,1},... | collective-permute-start | bytes 811016 | tf_op jit(solution)/shard_map/ppermute | solution.py:40
  68.1 26.0 %collective-permute-start.29 = (bf16[528,256]{1,0:T(8,128)(2,1)}, bf16[528,256]{1,0:T(8,128)(2,1)S(1)}, u32[]{:S(2)}, u32[]{:S(2)}) collective-permute-start(bf16[528,256]{1,0:T(8,128)(2,1)} %get-tuple-element.133), channel_id=1, source_target_pairs={{0,16},{1,17},{2,18},{3,19},{4,20},{5,21},{6,22},{7,23},{8,24},{9,... | collective-permute-start | bytes 811016 | tf_op jit(solution)/shard_map/ppermute | solution.py:40
  69.3 24.8 %collective-permute-start.30 = (bf16[528,256]{1,0:T(8,128)(2,1)}, bf16[528,256]{1,0:T(8,128)(2,1)S(1)}, u32[]{:S(2)}, u32[]{:S(2)}) collective-permute-start(bf16[528,256]{1,0:T(8,128)(2,1)} %get-tuple-element.134), channel_id=1, source_target_pairs={{0,24},{1,25},{2,26},{3,27},{4,28},{5,29},{6,30},{7,31},{8,16},{9,... | collective-permute-start | bytes 811016 | tf_op jit(solution)/shard_map/ppermute | solution.py:40
  76.1 2.1 %collective-permute-start = (f32[256,512]{1,0:T(8,128)}, f32[256,512]{1,0:T(8,128)S(1)}, u32[]{:S(2)}, u32[]{:S(2)}) collective-permute-start(f32[256,512]{1,0:T(8,128)} %get-tuple-element.26), channel_id=1, source_target_pairs={{0,1},{1,0},{2,3},{3,2},{4,5},{5,4},{6,7},{7,6},{8,9},{9,8},{10,11... | collective-permute-start | bytes 1572872 | tf_op jit(solution)/shard_map/cond/branch_1_fun/ppermute | solution.py:40
  79.6 4.2 %collective-permute-start.1 = (bf16[208,128]{1,0:T(8,128)(2,1)S(1)}, bf16[208,128]{1,0:T(8,128)(2,1)S(1)}, u32[]{:S(2)}, u32[]{:S(2)}) collective-permute-start(bf16[208,128]{1,0:T(8,128)(2,1)S(1)} %get-tuple-element.28), channel_id=1, source_target_pairs={{0,2},{1,3},{2,0},{3,1},{4,6},{5,7},{6,4},{7,5},{8,10},{9,11},{10,... | collective-permute-start | bytes 159752 | tf_op jit(solution)/shard_map/cond/branch_1_fun/ppermute | solution.py:40
  80.0 4.1 %collective-permute-start.2 = (bf16[208,128]{1,0:T(8,128)(2,1)S(1)}, bf16[208,128]{1,0:T(8,128)(2,1)S(1)}, u32[]{:S(2)}, u32[]{:S(2)}) collective-permute-start(bf16[208,128]{1,0:T(8,128)(2,1)S(1)} %get-tuple-element.31), channel_id=1, source_target_pairs={{0,4},{1,5},{2,6},{3,7},{4,0},{5,1},{6,2},{7,3},{8,12},{9,13},{10,... | collective-permute-start | bytes 159752 | tf_op jit(solution)/shard_map/cond/branch_1_fun/ppermute | solution.py:40
  83.8 5.0 %collective-permute-start.3 = (bf16[208,128]{1,0:T(8,128)(2,1)S(1)}, bf16[208,128]{1,0:T(8,128)(2,1)S(1)}, u32[]{:S(2)}, u32[]{:S(2)}) collective-permute-start(bf16[208,128]{1,0:T(8,128)(2,1)S(1)} %get-tuple-element.32), channel_id=1, source_target_pairs={{0,6},{1,7},{2,4},{3,5},{4,2},{5,3},{6,0},{7,1},{8,14},{9,15},{10,... | collective-permute-start | bytes 159752 | tf_op jit(solution)/shard_map/cond/branch_1_fun/ppermute | solution.py:40
  89.7 4.5 %collective-permute-start.34 = (bf16[64,128]{1,0:T(8,128)(2,1)S(1)}, bf16[64,128]{1,0:T(8,128)(2,1)S(1)}, u32[]{:S(2)}, u32[]{:S(2)}) collective-permute-start(bf16[64,128]{1,0:T(8,128)(2,1)S(1)} %get-tuple-element.142), channel_id=1, source_target_pairs={{0,8},{1,9},{2,10},{3,11},{4,12},{5,13},{6,14},{7,15},{8,0},{9,1},... | collective-permute-start | bytes 49160 | tf_op jit(solution)/shard_map/ppermute | solution.py:40
  89.7 6.6 %collective-permute-start.35 = (bf16[64,128]{1,0:T(8,128)(2,1)S(1)}, bf16[64,128]{1,0:T(8,128)(2,1)S(1)}, u32[]{:S(2)}, u32[]{:S(2)}) collective-permute-start(bf16[64,128]{1,0:T(8,128)(2,1)S(1)} %get-tuple-element.143), channel_id=1, source_target_pairs={{0,16},{1,17},{2,18},{3,19},{4,20},{5,21},{6,22},{7,23},{8,24},{9,... | collective-permute-start | bytes 49160 | tf_op jit(solution)/shard_map/ppermute | solution.py:40
  91.7 5.5 %collective-permute-start.36 = (bf16[64,128]{1,0:T(8,128)(2,1)S(1)}, bf16[64,128]{1,0:T(8,128)(2,1)S(1)}, u32[]{:S(2)}, u32[]{:S(2)}) collective-permute-start(bf16[64,128]{1,0:T(8,128)(2,1)S(1)} %get-tuple-element.144), channel_id=1, source_target_pairs={{0,24},{1,25},{2,26},{3,27},{4,28},{5,29},{6,30},{7,31},{8,16},{9,... | collective-permute-start | bytes 49160 | tf_op jit(solution)/shard_map/ppermute | solution.py:40
  99.8 2.0 %collective-permute-start.37 = (f32[256,512]{1,0:T(8,128)S(1)}, f32[256,512]{1,0:T(8,128)S(1)}, u32[]{:S(2)}, u32[]{:S(2)}) collective-permute-start(f32[256,512]{1,0:T(8,128)S(1)} %get-tuple-element.151), channel_id=1, source_target_pairs={{0,1},{1,0},{2,3},{3,2},{4,5},{5,4},{6,7},{7,6},{8,9},{9,8},{10,11... | collective-permute-start | bytes 1572872 | tf_op jit(solution)/shard_map/ppermute | solution.py:40
  102.6 4.2 %collective-permute-start.38 = (bf16[208,128]{1,0:T(8,128)(2,1)S(1)}, bf16[208,128]{1,0:T(8,128)(2,1)S(1)}, u32[]{:S(2)}, u32[]{:S(2)}) collective-permute-start(bf16[208,128]{1,0:T(8,128)(2,1)S(1)} %get-tuple-element.153), channel_id=1, source_target_pairs={{0,2},{1,3},{2,0},{3,1},{4,6},{5,7},{6,4},{7,5},{8,10},{9,11},{10,... | collective-permute-start | bytes 159752 | tf_op jit(solution)/shard_map/ppermute | solution.py:40
  103.2 4.7 %collective-permute-start.39 = (bf16[208,128]{1,0:T(8,128)(2,1)S(1)}, bf16[208,128]{1,0:T(8,128)(2,1)S(1)}, u32[]{:S(2)}, u32[]{:S(2)}) collective-permute-start(bf16[208,128]{1,0:T(8,128)(2,1)S(1)} %get-tuple-element.154), channel_id=1, source_target_pairs={{0,4},{1,5},{2,6},{3,7},{4,0},{5,1},{6,2},{7,3},{8,12},{9,13},{10,... | collective-permute-start | bytes 159752 | tf_op jit(solution)/shard_map/ppermute | solution.py:40
  103.7 5.0 %collective-permute-start.40 = (bf16[208,128]{1,0:T(8,128)(2,1)S(1)}, bf16[208,128]{1,0:T(8,128)(2,1)S(1)}, u32[]{:S(2)}, u32[]{:S(2)}) collective-permute-start(bf16[208,128]{1,0:T(8,128)(2,1)S(1)} %get-tuple-element.155), channel_id=1, source_target_pairs={{0,6},{1,7},{2,4},{3,5},{4,2},{5,3},{6,0},{7,1},{8,14},{9,15},{10,... | collective-permute-start | bytes 159752 | tf_op jit(solution)/shard_map/ppermute | solution.py:40
  109.6 6.7 %collective-permute-start.43 = (bf16[256,128]{1,0:T(8,128)(2,1)S(1)}, bf16[256,128]{1,0:T(8,128)(2,1)S(1)}, u32[]{:S(2)}, u32[]{:S(2)}) collective-permute-start(bf16[256,128]{1,0:T(8,128)(2,1)S(1)} %code.1.refs_0_), channel_id=1, source_target_pairs={{0,24},{1,25},{2,26},{3,27},{4,28},{5,29},{6,30},{7,31},{8,16},{9,... | collective-permute-start | bytes 196616 | tf_op jit(solution)/shard_map/ppermute | solution.py:40
  111.8 5.9 %collective-permute-start.42 = (bf16[256,128]{1,0:T(8,128)(2,1)S(1)}, bf16[256,128]{1,0:T(8,128)(2,1)S(1)}, u32[]{:S(2)}, u32[]{:S(2)}) collective-permute-start(bf16[256,128]{1,0:T(8,128)(2,1)S(1)} %code.1.refs_0_), channel_id=1, source_target_pairs={{0,16},{1,17},{2,18},{3,19},{4,20},{5,21},{6,22},{7,23},{8,24},{9,... | collective-permute-start | bytes 196616 | tf_op jit(solution)/shard_map/ppermute | solution.py:40
  111.8 5.9 %collective-permute-start.41 = (bf16[256,128]{1,0:T(8,128)(2,1)S(1)}, bf16[256,128]{1,0:T(8,128)(2,1)S(1)}, u32[]{:S(2)}, u32[]{:S(2)}) collective-permute-start(bf16[256,128]{1,0:T(8,128)(2,1)S(1)} %code.1.refs_0_), channel_id=1, source_target_pairs={{0,8},{1,9},{2,10},{3,11},{4,12},{5,13},{6,14},{7,15},{8,0},{9,1},... | collective-permute-start | bytes 196616 | tf_op jit(solution)/shard_map/ppermute | solution.py:40
  118.7 6.1 %collective-permute-start.46 = (bf16[128,384]{1,0:T(8,128)(2,1)S(1)}, bf16[128,384]{1,0:T(8,128)(2,1)S(1)}, u32[]{:S(2)}, u32[]{:S(2)}) collective-permute-start(bf16[128,384]{1,0:T(8,128)(2,1)S(1)} %finish.1.refs_0_), channel_id=1, source_target_pairs={{0,6},{1,7},{2,4},{3,5},{4,2},{5,3},{6,0},{7,1},{8,14},{9,15},{10,... | collective-permute-start | bytes 294920 | tf_op jit(solution)/shard_map/ppermute | solution.py:40
  121.3 4.6 %collective-permute-start.45 = (bf16[128,384]{1,0:T(8,128)(2,1)S(1)}, bf16[128,384]{1,0:T(8,128)(2,1)S(1)}, u32[]{:S(2)}, u32[]{:S(2)}) collective-permute-start(bf16[128,384]{1,0:T(8,128)(2,1)S(1)} %finish.1.refs_0_), channel_id=1, source_target_pairs={{0,4},{1,5},{2,6},{3,7},{4,0},{5,1},{6,2},{7,3},{8,12},{9,13},{10,... | collective-permute-start | bytes 294920 | tf_op jit(solution)/shard_map/ppermute | solution.py:40
  121.6 4.6 %collective-permute-start.44 = (bf16[128,384]{1,0:T(8,128)(2,1)S(1)}, bf16[128,384]{1,0:T(8,128)(2,1)S(1)}, u32[]{:S(2)}, u32[]{:S(2)}) collective-permute-start(bf16[128,384]{1,0:T(8,128)(2,1)S(1)} %finish.1.refs_0_), channel_id=1, source_target_pairs={{0,2},{1,3},{2,0},{3,1},{4,6},{5,7},{6,4},{7,5},{8,10},{9,11},{10,... | collective-permute-start | bytes 294920 | tf_op jit(solution)/shard_map/ppermute | solution.py:40
  122.2 4.2 %collective-permute-start.47 = (bf16[128,384]{1,0:T(8,128)(2,1)S(1)}, bf16[128,384]{1,0:T(8,128)(2,1)S(1)}, u32[]{:S(2)}, u32[]{:S(2)}) collective-permute-start(bf16[128,384]{1,0:T(8,128)(2,1)S(1)} %finish.1.refs_0_), channel_id=1, source_target_pairs={{0,1},{1,0},{2,3},{3,2},{4,5},{5,4},{6,7},{7,6},{8,9},{9,8},{10,11... | collective-permute-start | bytes 294920 | tf_op jit(solution)/shard_map/ppermute | solution.py:40
  124.8 1.6 %collective-permute-start.50 = (bf16[128,384]{1,0:T(8,128)(2,1)S(1)}, bf16[128,384]{1,0:T(8,128)(2,1)S(1)}, u32[]{:S(2)}, u32[]{:S(2)}) collective-permute-start(bf16[128,384]{1,0:T(8,128)(2,1)S(1)} %collective-permute-done.46.refs_3_), channel_id=1, source_target_pairs={{0,1},{1,0},{2,3},{3,2},{4,5},{5,4},{6,7},{7,6},{8,9},{9,8},{10,11... | collective-permute-start | bytes 294920 | tf_op jit(solution)/shard_map/ppermute | solution.py:40
  125.9 1.3 collective-permute-start.49
  126.2 1.3 collective-permute-start.48
  129.5 8.3 %collective-permute-start.51 = (bf16[256,256]{1,0:T(8,128)(2,1)S(1)}, bf16[256,256]{1,0:T(8,128)(2,1)S(1)}, u32[]{:S(2)}, u32[]{:S(2)}) collective-permute-start(bf16[256,256]{1,0:T(8,128)(2,1)S(1)} %get-tuple-element.167), channel_id=1, source_target_pairs={{0,24},{1,25},{2,26},{3,27},{4,28},{5,29},{6,30},{7,31},{8,16},{9,... | collective-permute-start | bytes 393224 | tf_op jit(solution)/shard_map/ppermute | solution.py:40
  131.2 12.5 %collective-permute-start.52 = (bf16[256,256]{1,0:T(8,128)(2,1)S(1)}, bf16[256,256]{1,0:T(8,128)(2,1)S(1)}, u32[]{:S(2)}, u32[]{:S(2)}) collective-permute-start(bf16[256,256]{1,0:T(8,128)(2,1)S(1)} %get-tuple-element.168), channel_id=1, source_target_pairs={{0,16},{1,17},{2,18},{3,19},{4,20},{5,21},{6,22},{7,23},{8,24},{9,... | collective-permute-start | bytes 393224 | tf_op jit(solution)/shard_map/ppermute | solution.py:40
  131.7 12.0 %collective-permute-start.53 = (bf16[256,256]{1,0:T(8,128)(2,1)S(1)}, bf16[256,256]{1,0:T(8,128)(2,1)S(1)}, u32[]{:S(2)}, u32[]{:S(2)}) collective-permute-start(bf16[256,256]{1,0:T(8,128)(2,1)S(1)} %get-tuple-element.169), channel_id=1, source_target_pairs={{0,8},{1,9},{2,10},{3,11},{4,12},{5,13},{6,14},{7,15},{8,0},{9,1},... | collective-permute-start | bytes 393224 | tf_op jit(solution)/shard_map/ppermute | solution.py:40

commit v15 on v14

--- a/solution.py
+++ b/solution.py
@@ -184,13 +184,14 @@
     out_ref[height:] = jnp.concatenate([total[:-8], edge], 0).astype(BF16)
 
 
-def local(kernel, place_array, args, shapes, name, **more):
+def local(kernel, place_array, args, shapes, name, pinned=False, **more):
+    kind = pltpu.VMEM if pinned else jax.ShapeDtypeStruct
     space = pl.BlockSpec(memory_space=pltpu.VMEM)
     return pl.pallas_call(
         kernel,
         in_specs=[pl.BlockSpec(memory_space=pltpu.SMEM)] + [space] * len(args),
         out_specs=[space] * len(shapes),
-        out_shape=[jax.ShapeDtypeStruct(shape, dtype) for shape, dtype in shapes],
+        out_shape=[kind(shape, dtype) for shape, dtype in shapes],
         compiler_params=pltpu.CompilerParams(vmem_limit_bytes=VMEM_BYTES // 2),
         name=name,
         **more,
@@ -246,7 +247,7 @@
 
 
 def lay_kernel(place_ref, *refs, n):
-    parts, outs = refs[:n], refs[n:]
+    parts, outs = [refs[0], *refs[n - 1 : 0 : -1]], refs[n:]
     few = parts[0].shape[0] // len(outs)
     for step in range(n):
         at = pl.ds(pl.multiple_of((place_ref[0] ^ step) * few, few), few)
@@ -278,8 +279,26 @@
     return exchange(place, "a", view.reshape(place.n, rows // place.n, width))
 
 
-def to_planes(place, parts):
-    return sends(place, "z", ordered(parts, place.a ^ place.z))
+def turn_kernel(place_ref, *refs, n):
+    turned = ordered([ref[...] for ref in refs[:n]], place_ref[1] ^ place_ref[0])
+    for ref, part in zip(refs[n:], [turned[0], *turned[:0:-1]]):
+        ref[...] = part
+
+
+def to_planes(place, place_array, parts, kernel):
+    if kernel:
+        parts = local(
+            functools.partial(turn_kernel, n=place.n),
+            place_array,
+            parts,
+            [(parts[0].shape, BF16)] * place.n,
+            "turn",
+            pinned=True,
+        )
+        parts = [parts[0], *parts[:0:-1]]
+    else:
+        parts = ordered(parts, place.a ^ place.z)
+    return sends(place, "z", parts)
 
 
 def lay(place, place_array, parts):
@@ -287,9 +306,10 @@
     (laid,) = local(
         functools.partial(lay_kernel, n=place.n),
         place_array,
-        parts,
+        [parts[0], *parts[:0:-1]],
         [((rows * place.n, width), BF16)],
         "lay",
+        pinned=True,
     )
     return laid
 
@@ -530,10 +550,10 @@
     n, k, z, a, b = place.n, place.k, place.z, place.a, place.b
     place_array = jnp.stack([z, a, b]).astype(jnp.int32)
     first = to_columns(place, h_first)
-    first, second = lax.optimization_barrier((to_planes(place, first), to_columns(place, h_second)))
+    first, second = lax.optimization_barrier((to_planes(place, place_array, first, True), to_columns(place, h_second)))
     first, late_weight = lax.optimization_barrier((lay(place, place_array, first), weight))
     met_1, second, held = lax.optimization_barrier(
-        (met_rows(place, first), to_planes(place, second), fetch(late_weight))
+        (met_rows(place, first), to_planes(place, place_array, second, False), fetch(late_weight))
     )
 
     def sent(parts):

time: 146 us -> 145 us (level)
  starting transfers between devices: 54 us -> 56.4 us
  waiting for transfers between devices: 54.1 us -> 52.1 us
    ppermute x54, starting transfers between devices: 54 us -> 56.4 us  [send(): return lax.ppermute(value, ('dp', 'mp'), pairs)]
    ppermute x54, waiting for transfers between devices: 54.1 us -> 52.1 us  [send(): return lax.ppermute(value, ('dp', 'mp'), pairs)]
    pallas_call x11 -> x12, Pallas kernels: 12.7 us -> 12.6 us  [local(): pl.pallas_call(kernel, in_specs=[pl.BlockSpec(memory_space=pltpu.SMEM)] +...]
  transfers between devices with their start and end apart: 54 -> 54, of which waited for: 27 -> 24; matrix products, arithmetic and copies ran while one was open for 2% -> 1% of each run, Pallas kernels for 16% -> 16%
where the time goes in v15:
time: 145 us; the launch traced here: 144 us
  starting transfers between devices  56.4 us (39%)
  waiting for transfers between devices  52.1 us (36%)
  Pallas kernels  31.9 us (22%)
  local copies, waits for them, and re-layouts  1.91 us (1%)
    ppermute x54, starting transfers between devices, send(): return lax.ppermute(value, ('dp', 'mp'), pairs)  56.4 us
    ppermute x54, waiting for transfers between devices, send(): return lax.ppermute(value, ('dp', 'mp'), pairs)  52.1 us
    pallas_call x12, Pallas kernels, local(): pl.pallas_call(kernel, in_specs=[pl.BlockSpec(memory_space=pltpu.SMEM)] +...  12.6 us
    pallas_call x2, Pallas kernels, project(): pl.pallas_call(functools.partial(project_kernel, counts=counts, n=n, k=k)...  8.91 us
    pallas_call x2, Pallas kernels, normalize_parts(): pl.pallas_call(functools.partial(normalize_kernel, n=n, k=k, order=order,...  6.01 us
    pallas_call x2, Pallas kernels, fetch(): pl.pallas_call(fetch_kernel, in_specs=[pl.BlockSpec(memory_space=pl.ANY)]...  4.39 us
  transfers between devices with their start and end apart: 54, of which 24 were waited for; matrix products, arithmetic and copies ran while one was open for 1% of the time, Pallas kernels for 16%

profile of v15, /device:TPU:0, one launch (start us, length us, event | category | flops | bytes accessed | tf_op | source)
XLA Modules:
  0.0 144.4 jit_solution(16764720629023103199)
XLA Ops:
  0.7 1.0 dynamic-slice_bitcast_fusion.4
  1.6 4.0 %collective-permute-start.10 = (bf16[32,1024]{1,0:T(8,128)(2,1)S(1)}, bf16[32,1024]{1,0:T(8,128)(2,1)S(1)}, u32[]{:S(2)}, u32[]{:S(2)}) collective-permute-start(bf16[32,1024]{1,0:T(8,128)(2,1)S(1)} %get-tuple-element.190), channel_id=1, source_target_pairs={{0,6},{1,7},{2,4},{3,5},{4,2},{5,3},{6,0},{7,1},{8,14},{9,15},{10,... | collective-permute-start | bytes 196616 | tf_op jit(solution)/shard_map/ppermute | solution.py:40
  6.2 1.0 dynamic-slice_bitcast_fusion
  7.2 2.9 %collective-permute-start.16 = (bf16[32,1024]{1,0:T(8,128)(2,1)S(1)}, bf16[32,1024]{1,0:T(8,128)(2,1)S(1)}, u32[]{:S(2)}, u32[]{:S(2)}) collective-permute-start(bf16[32,1024]{1,0:T(8,128)(2,1)S(1)} %get-tuple-element.186), channel_id=1, source_target_pairs={{0,6},{1,7},{2,4},{3,5},{4,2},{5,3},{6,0},{7,1},{8,14},{9,15},{10,... | collective-permute-start | bytes 196616 | tf_op jit(solution)/shard_map/ppermute | solution.py:40
  11.4 2.0 %collective-permute-start.11 = (bf16[32,1024]{1,0:T(8,128)(2,1)S(1)}, bf16[32,1024]{1,0:T(8,128)(2,1)S(1)}, u32[]{:S(2)}, u32[]{:S(2)}) collective-permute-start(bf16[32,1024]{1,0:T(8,128)(2,1)S(1)} %get-tuple-element.110), channel_id=1, source_target_pairs={{0,8},{1,9},{2,10},{3,11},{4,12},{5,13},{6,14},{7,15},{8,0},{9,1},... | collective-permute-start | bytes 196616 | tf_op jit(solution)/shard_map/ppermute | solution.py:40
  13.5 2.6 %collective-permute-start.12 = (bf16[32,1024]{1,0:T(8,128)(2,1)S(1)}, bf16[32,1024]{1,0:T(8,128)(2,1)S(1)}, u32[]{:S(2)}, u32[]{:S(2)}) collective-permute-start(bf16[32,1024]{1,0:T(8,128)(2,1)S(1)} %get-tuple-element.111), channel_id=1, source_target_pairs={{0,16},{1,17},{2,18},{3,19},{4,20},{5,21},{6,22},{7,23},{8,24},{9,... | collective-permute-start | bytes 196616 | tf_op jit(solution)/shard_map/ppermute | solution.py:40
  16.6 3.4 %collective-permute-done.12.refs_2_ = bf16[32,1024]{1,0:T(8,128)(2,1)S(1)} collective-permute-done((bf16[32,1024]{1,0:T(8,128)(2,1)S(1)}, bf16[32,1024]{1,0:T(8,128)(2,1)S(1)}, u32[]{:S(2)}, u32[]{:S(2)}) %collective-permute-start.12) | collective-permute-done | bytes 65568 | tf_op jit(solution)/shard_map/ppermute | solution.py:40
  20.0 2.1 %collective-permute-done.13.refs_1_ = bf16[32,1024]{1,0:T(8,128)(2,1)S(1)} collective-permute-done((bf16[32,1024]{1,0:T(8,128)(2,1)S(1)}, bf16[32,1024]{1,0:T(8,128)(2,1)S(1)}, u32[]{:S(2)}, u32[]{:S(2)}) %collective-permute-start.13) | collective-permute-done | bytes 65568 | tf_op jit(solution)/shard_map/ppermute | solution.py:40
  22.7 2.5 %collective-permute-start.19 = (bf16[128,1024]{1,0:T(8,128)(2,1)S(1)}, bf16[128,1024]{1,0:T(8,128)(2,1)S(1)}, u32[]{:S(2)}, u32[]{:S(2)}) collective-permute-start(bf16[128,1024]{1,0:T(8,128)(2,1)S(1)} %lay.2.refs_0_), channel_id=1, source_target_pairs={{0,6},{1,7},{2,4},{3,5},{4,2},{5,3},{6,0},{7,1},{8,14},{9,15},{10,... | collective-permute-start | bytes 786440 | tf_op jit(solution)/shard_map/ppermute | solution.py:40
  26.3 0.9 collective-permute-start.22
  27.2 5.4 %collective-permute-done.22.refs_1_ = bf16[32,1024]{1,0:T(8,128)(2,1)S(1)} collective-permute-done((bf16[32,1024]{1,0:T(8,128)(2,1)S(1)}, bf16[32,1024]{1,0:T(8,128)(2,1)S(1)}, u32[]{:S(2)}, u32[]{:S(2)}) %collective-permute-start.22) | collective-permute-done | bytes 65568 | tf_op jit(solution)/shard_map/ppermute | solution.py:40
  32.5 2.2 %fetch.3.refs_8_ = bf16[2048,1024]{1,0:T(8,128)(2,1)S(1)} custom-call(bf16[2048,1024]{1,0:T(8,128)(2,1)} %weight_ref), custom_call_target="tpu_custom_call" | custom-call | bytes 8388608 | tf_op jit(solution)/shard_map/fetch/pallas_call | solution.py:265
  34.7 2.9 %collective-permute-done.21.refs_2_ = bf16[32,1024]{1,0:T(8,128)(2,1)S(1)} collective-permute-done((bf16[32,1024]{1,0:T(8,128)(2,1)S(1)}, bf16[32,1024]{1,0:T(8,128)(2,1)S(1)}, u32[]{:S(2)}, u32[]{:S(2)}) %collective-permute-start.21) | collective-permute-done | bytes 65568 | tf_op jit(solution)/shard_map/ppermute | solution.py:40
  39.3 2.5 %collective-permute-start.27 = (bf16[128,1024]{1,0:T(8,128)(2,1)S(1)}, bf16[128,1024]{1,0:T(8,128)(2,1)}, u32[]{:S(2)}, u32[]{:S(2)}) collective-permute-start(bf16[128,1024]{1,0:T(8,128)(2,1)S(1)} %lay.3), channel_id=1, source_target_pairs={{0,6},{1,7},{2,4},{3,5},{4,2},{5,3},{6,0},{7,1},{8,14},{9,15},{10,... | collective-permute-start | bytes 786440 | tf_op jit(solution)/shard_map/ppermute | solution.py:40
  41.9 3.9 %project.3 = (f32[512,256]{1,0:T(8,128)S(1)}, bf16[528,256]{1,0:T(8,128)(2,1)S(1)}, bf16[528,256]{1,0:T(8,128)(2,1)S(1)}, bf16[528,256]{1,0:T(8,128)(2,1)S(1)}) custom-call(s32[3]{0:T(128)S(1)} %pad_add_fusion.place_ref, bf16[128,1024]{1,0:T(8,128)(2,1)S(1)} %lay.2.refs_0_, bf16[128,1024]{1,0:T(8,128)(2,1)S(1)} %collective-permute-done.17.refs_1_, ...), custom_call_target="tpu_custom_call" | custom-call | flops 2147483648 | bytes 7864320 | tf_op jit(solution)/shard_map/project/pallas_call | solution.py:378
  45.8 1.7 %collective-permute-start.31 = (bf16[528,256]{1,0:T(8,128)(2,1)S(1)}, bf16[528,256]{1,0:T(8,128)(2,1)S(1)}, u32[]{:S(2)}, u32[]{:S(2)}) collective-permute-start(bf16[528,256]{1,0:T(8,128)(2,1)S(1)} %get-tuple-element.144), channel_id=1, source_target_pairs={{0,24},{1,25},{2,26},{3,27},{4,28},{5,29},{6,30},{7,31},{8,16},{9,... | collective-permute-start | bytes 811016 | tf_op jit(solution)/shard_map/ppermute | solution.py:40
  47.5 2.8 %collective-permute-start.33 = (bf16[528,256]{1,0:T(8,128)(2,1)S(1)}, bf16[528,256]{1,0:T(8,128)(2,1)S(1)}, u32[]{:S(2)}, u32[]{:S(2)}) collective-permute-start(bf16[528,256]{1,0:T(8,128)(2,1)S(1)} %get-tuple-element.146), channel_id=1, source_target_pairs={{0,8},{1,9},{2,10},{3,11},{4,12},{5,13},{6,14},{7,15},{8,0},{9,1},... | collective-permute-start | bytes 811016 | tf_op jit(solution)/shard_map/ppermute | solution.py:40
  50.2 16.4 %conditional.2 = (f32[512,256]{1,0:T(8,128)S(1)}, bf16[528,256]{1,0:T(8,128)(2,1)}, bf16[528,256]{1,0:T(8,128)(2,1)}, bf16[528,256]{1,0:T(8,128)(2,1)}) conditional(s32[]{:T(128)} %convert_element_type.4, () %tuple.35, (bf16[128,1024]{1,0:T(8,128)(2,1)S(1)}, bf16[128,1024]{1,0:T(8,128)(2,1)}, bf16[2048,1024]{1,0:T(8,128)(2,1)}, s32[3]{0:T(128)S(1)}) %tuple.36), branch_computations={%region_0.1_spmd, %region_1.2_spmd} | conditional | flops 2149580800 | bytes 24641728 | solution.py:232
  50.8 1.0 collective-permute-start.5
  51.8 5.6 %collective-permute-done.4.refs_2_ = bf16[128,1024]{1,0:T(8,128)(2,1)S(1)} collective-permute-done((bf16[128,1024]{1,0:T(8,128)(2,1)S(1)}, bf16[128,1024]{1,0:T(8,128)(2,1)S(1)}, u32[]{:S(2)}, u32[]{:S(2)}) %collective-permute-start.4) | collective-permute-done | bytes 262176 | tf_op jit(solution)/shard_map/cond/branch_1_fun/ppermute | solution.py:40
  57.8 1.0 pad_maximum_fusion
  59.4 2.2 %fetch.2.refs_6_ = bf16[2048,1024]{1,0:T(8,128)(2,1)S(1)} custom-call(bf16[2048,1024]{1,0:T(8,128)(2,1)} %get-tuple-element.19.weight_ref), custom_call_target="tpu_custom_call" | custom-call | bytes 8388608 | tf_op jit(solution)/shard_map/cond/branch_1_fun/fetch/pallas_call | solution.py:265
  61.6 5.0 %project.2 = (f32[512,256]{1,0:T(8,128)S(1)}, bf16[528,256]{1,0:T(8,128)(2,1)}, bf16[528,256]{1,0:T(8,128)(2,1)}, bf16[528,256]{1,0:T(8,128)(2,1)}) custom-call(s32[3]{0:T(128)S(1)} %get-tuple-element.14.place_ref, bf16[128,1024]{1,0:T(8,128)(2,1)S(1)} %get-tuple-element.16.refs_0_, bf16[128,1024]{1,0:T(8,128)(2,1)} %get-tuple-element.17.refs_1_, ...), custom_call_target="tpu_custom_call" | custom-call | flops 2147483648 | bytes 7864320 | tf_op jit(solution)/shard_map/cond/branch_1_fun/project/pallas_call | solution.py:378
  66.9 1.8 %collective-permute-start.29 = (bf16[528,256]{1,0:T(8,128)(2,1)}, bf16[528,256]{1,0:T(8,128)(2,1)S(1)}, u32[]{:S(2)}, u32[]{:S(2)}) collective-permute-start(bf16[528,256]{1,0:T(8,128)(2,1)} %get-tuple-element.141), channel_id=1, source_target_pairs={{0,16},{1,17},{2,18},{3,19},{4,20},{5,21},{6,22},{7,23},{8,24},{9,... | collective-permute-start | bytes 811016 | tf_op jit(solution)/shard_map/ppermute | solution.py:40
  68.7 2.3 %collective-permute-start.30 = (bf16[528,256]{1,0:T(8,128)(2,1)}, bf16[528,256]{1,0:T(8,128)(2,1)S(1)}, u32[]{:S(2)}, u32[]{:S(2)}) collective-permute-start(bf16[528,256]{1,0:T(8,128)(2,1)} %get-tuple-element.142), channel_id=1, source_target_pairs={{0,24},{1,25},{2,26},{3,27},{4,28},{5,29},{6,30},{7,31},{8,16},{9,... | collective-permute-start | bytes 811016 | tf_op jit(solution)/shard_map/ppermute | solution.py:40
  71.0 3.4 %normalize.2 = (f32[512,256]{1,0:T(8,128)S(1)}, bf16[512,256]{1,0:T(8,128)(2,1)S(1)}, f32[1,256]{1,0:T(1,128)S(1)}, f32[256,512]{1,0:T(8,128)}, f32[256,512]{1,0:T(8,128)}) custom-call(s32[3]{0:T(128)S(1)} %pad_add_fusion.place_ref, f32[512,256]{1,0:T(8,128)S(1)} %get-tuple-element.143.refs_0_, bf16[528,256]{1,0:T(8,128)(2,1)S(1)} %collective-permute-done.31.refs_1_, ...), custom_call_target="tpu_custom_call" | custom-call | flops 134217728 | bytes 3145728 | tf_op jit(solution)/shard_map/normalize/pallas_call | solution.py:458
  74.4 13.5 %conditional.3 = ((f32[16,384]{1,0:T(8,128)S(1)}, bf16[64,128]{1,0:T(8,128)(2,1)S(1)}, bf16[64,128]{1,0:T(8,128)(2,1)S(1)}, bf16[64,128]{1,0:T(8,128)(2,1)S(1)})) conditional(s32[]{:T(128)} %convert_element_type.4, () %tuple.38, (f32[256,512]{1,0:T(8,128)}, s32[3]{0:T(128)S(1)}, f32[256,512]{1,0:T(8,128)}) %tuple.39), branch_computations={%region_2.3_spmd, %region_3.4_spmd} | conditional | bytes 2736296 | solution.py:232
  74.4 2.1 %collective-permute-done.met_ref = f32[256,512]{1,0:T(8,128)S(1)} collective-permute-done((f32[256,512]{1,0:T(8,128)}, f32[256,512]{1,0:T(8,128)S(1)}, u32[]{:S(2)}, u32[]{:S(2)}) %collective-permute-start) | collective-permute-done | bytes 524320 | tf_op jit(solution)/shard_map/cond/branch_1_fun/ppermute | solution.py:40
  76.5 1.3 halve.2
  77.9 1.6 %collective-permute-start.1 = (bf16[208,128]{1,0:T(8,128)(2,1)S(1)}, bf16[208,128]{1,0:T(8,128)(2,1)S(1)}, u32[]{:S(2)}, u32[]{:S(2)}) collective-permute-start(bf16[208,128]{1,0:T(8,128)(2,1)S(1)} %get-tuple-element.28), channel_id=1, source_target_pairs={{0,2},{1,3},{2,0},{3,1},{4,6},{5,7},{6,4},{7,5},{8,10},{9,11},{10,... | collective-permute-start | bytes 159752 | tf_op jit(solution)/shard_map/cond/branch_1_fun/ppermute | solution.py:40
  79.9 2.1 %collective-permute-done.1.refs_1_ = bf16[208,128]{1,0:T(8,128)(2,1)S(1)} collective-permute-done((bf16[208,128]{1,0:T(8,128)(2,1)S(1)}, bf16[208,128]{1,0:T(8,128)(2,1)S(1)}, u32[]{:S(2)}, u32[]{:S(2)}) %collective-permute-start.1) | collective-permute-done | bytes 53280 | tf_op jit(solution)/shard_map/cond/branch_1_fun/ppermute | solution.py:40
  82.1 1.4 collective-permute-start.3
  83.5 3.5 %collective-permute-done.3.refs_3_ = bf16[208,128]{1,0:T(8,128)(2,1)S(1)} collective-permute-done((bf16[208,128]{1,0:T(8,128)(2,1)S(1)}, bf16[208,128]{1,0:T(8,128)(2,1)S(1)}, u32[]{:S(2)}, u32[]{:S(2)}) %collective-permute-start.3) | collective-permute-done | bytes 53280 | tf_op jit(solution)/shard_map/cond/branch_1_fun/ppermute | solution.py:40
  87.1 0.8 plane.1
  88.0 2.4 %collective-permute-start.35 = (bf16[64,128]{1,0:T(8,128)(2,1)S(1)}, bf16[64,128]{1,0:T(8,128)(2,1)S(1)}, u32[]{:S(2)}, u32[]{:S(2)}) collective-permute-start(bf16[64,128]{1,0:T(8,128)(2,1)S(1)} %get-tuple-element.151), channel_id=1, source_target_pairs={{0,16},{1,17},{2,18},{3,19},{4,20},{5,21},{6,22},{7,23},{8,24},{9,... | collective-permute-start | bytes 49160 | tf_op jit(solution)/shard_map/ppermute | solution.py:40
  90.4 2.0 %collective-permute-start.36 = (bf16[64,128]{1,0:T(8,128)(2,1)S(1)}, bf16[64,128]{1,0:T(8,128)(2,1)S(1)}, u32[]{:S(2)}, u32[]{:S(2)}) collective-permute-start(bf16[64,128]{1,0:T(8,128)(2,1)S(1)} %get-tuple-element.152), channel_id=1, source_target_pairs={{0,24},{1,25},{2,26},{3,27},{4,28},{5,29},{6,30},{7,31},{8,16},{9,... | collective-permute-start | bytes 49160 | tf_op jit(solution)/shard_map/ppermute | solution.py:40
  92.4 2.2 %collective-permute-done.35.refs_2_ = bf16[64,128]{1,0:T(8,128)(2,1)S(1)} collective-permute-done((bf16[64,128]{1,0:T(8,128)(2,1)S(1)}, bf16[64,128]{1,0:T(8,128)(2,1)S(1)}, u32[]{:S(2)}, u32[]{:S(2)}) %collective-permute-start.35) | collective-permute-done | bytes 16416 | tf_op jit(solution)/shard_map/ppermute | solution.py:40
  94.6 1.3 collective-permute-done.36.refs_3_
  95.9 2.6 %normalize.3 = (f32[512,256]{1,0:T(8,128)S(1)}, bf16[512,256]{1,0:T(8,128)(2,1)S(1)}, f32[1,256]{1,0:T(1,128)S(1)}, f32[256,512]{1,0:T(8,128)S(1)}, f32[256,512]{1,0:T(8,128)S(1)}, /*index=5*/f32[1,256]{1,0:T(1,128)S(1)}) custom-call(s32[3]{0:T(128)S(1)} %pad_add_fusion.place_ref, f32[512,256]{1,0:T(8,128)S(1)} %get-tuple-element.153.refs_0_, ...), custom_call_target="tpu_custom_call" | custom-call | flops 134217728 | bytes 3145728 | tf_op jit(solution)/shard_map/normalize/pallas_call | solution.py:458
  98.6 1.9 %collective-permute-done.37.met_ref = f32[256,512]{1,0:T(8,128)S(1)} collective-permute-done((f32[256,512]{1,0:T(8,128)S(1)}, f32[256,512]{1,0:T(8,128)S(1)}, u32[]{:S(2)}, u32[]{:S(2)}) %collective-permute-start.37) | collective-permute-done | bytes 524320 | tf_op jit(solution)/shard_map/ppermute | solution.py:40
  100.5 0.8 halve.3
  101.3 1.3 collective-permute-start.38
  103.2 1.7 %collective-permute-start.40 = (bf16[208,128]{1,0:T(8,128)(2,1)S(1)}, bf16[208,128]{1,0:T(8,128)(2,1)S(1)}, u32[]{:S(2)}, u32[]{:S(2)}) collective-permute-start(bf16[208,128]{1,0:T(8,128)(2,1)S(1)} %get-tuple-element.163), channel_id=1, source_target_pairs={{0,6},{1,7},{2,4},{3,5},{4,2},{5,3},{6,0},{7,1},{8,14},{9,15},{10,... | collective-permute-start | bytes 159752 | tf_op jit(solution)/shard_map/ppermute | solution.py:40
  105.5 1.8 %collective-permute-done.39.refs_2_ = bf16[208,128]{1,0:T(8,128)(2,1)S(1)} collective-permute-done((bf16[208,128]{1,0:T(8,128)(2,1)S(1)}, bf16[208,128]{1,0:T(8,128)(2,1)S(1)}, u32[]{:S(2)}, u32[]{:S(2)}) %collective-permute-start.39) | collective-permute-done | bytes 53280 | tf_op jit(solution)/shard_map/ppermute | solution.py:40
  107.3 0.9 collective-permute-done.40.refs_3_
  108.2 0.8 code.1.refs_0_
  109.1 2.3 %collective-permute-start.43 = (bf16[256,128]{1,0:T(8,128)(2,1)S(1)}, bf16[256,128]{1,0:T(8,128)(2,1)S(1)}, u32[]{:S(2)}, u32[]{:S(2)}) collective-permute-start(bf16[256,128]{1,0:T(8,128)(2,1)S(1)} %code.1.refs_0_), channel_id=1, source_target_pairs={{0,24},{1,25},{2,26},{3,27},{4,28},{5,29},{6,30},{7,31},{8,16},{9,... | collective-permute-start | bytes 196616 | tf_op jit(solution)/shard_map/ppermute | solution.py:40
  111.4 2.1 %collective-permute-start.41 = (bf16[256,128]{1,0:T(8,128)(2,1)S(1)}, bf16[256,128]{1,0:T(8,128)(2,1)S(1)}, u32[]{:S(2)}, u32[]{:S(2)}) collective-permute-start(bf16[256,128]{1,0:T(8,128)(2,1)S(1)} %code.1.refs_0_), channel_id=1, source_target_pairs={{0,8},{1,9},{2,10},{3,11},{4,12},{5,13},{6,14},{7,15},{8,0},{9,1},... | collective-permute-start | bytes 196616 | tf_op jit(solution)/shard_map/ppermute | solution.py:40
  113.5 2.3 %collective-permute-done.43.refs_3_ = bf16[256,128]{1,0:T(8,128)(2,1)S(1)} collective-permute-done((bf16[256,128]{1,0:T(8,128)(2,1)S(1)}, bf16[256,128]{1,0:T(8,128)(2,1)S(1)}, u32[]{:S(2)}, u32[]{:S(2)}) %collective-permute-start.43) | collective-permute-done | bytes 65568 | tf_op jit(solution)/shard_map/ppermute | solution.py:40
  115.8 1.3 collective-permute-done.42.refs_2_
  117.1 1.0 finish.1.refs_0_
  118.1 1.5 %collective-permute-start.46 = (bf16[128,384]{1,0:T(8,128)(2,1)S(1)}, bf16[128,384]{1,0:T(8,128)(2,1)S(1)}, u32[]{:S(2)}, u32[]{:S(2)}) collective-permute-start(bf16[128,384]{1,0:T(8,128)(2,1)S(1)} %finish.1.refs_0_), channel_id=1, source_target_pairs={{0,6},{1,7},{2,4},{3,5},{4,2},{5,3},{6,0},{7,1},{8,14},{9,15},{10,... | collective-permute-start | bytes 294920 | tf_op jit(solution)/shard_map/ppermute | solution.py:40
  119.6 1.2 collective-permute-start.45
  121.7 2.1 %collective-permute-done.46.refs_3_ = bf16[128,384]{1,0:T(8,128)(2,1)S(1)} collective-permute-done((bf16[128,384]{1,0:T(8,128)(2,1)S(1)}, bf16[128,384]{1,0:T(8,128)(2,1)S(1)}, u32[]{:S(2)}, u32[]{:S(2)}) %collective-permute-start.46) | collective-permute-done | bytes 98336 | tf_op jit(solution)/shard_map/ppermute | solution.py:40
  123.7 1.0 collective-permute-done.45.refs_2_
  124.7 0.8 collective-permute-done.44.refs_1_
  126.0 0.8 collective-permute-done.48.refs_5_
  126.8 2.0 %gradient.1 = (bf16[256,256]{1,0:T(8,128)(2,1)S(1)}, bf16[256,256]{1,0:T(8,128)(2,1)S(1)}, bf16[256,256]{1,0:T(8,128)(2,1)S(1)}, bf16[256,256]{1,0:T(8,128)(2,1)...) custom-call(s32[3]{0:T(128)S(1)} %pad_add_fusion.place_ref, bf16[128,384]{1,0:T(8,128)(2,1)S(1)} %finish.1.refs_0_, ...), custom_call_target="tpu_custom_call" | custom-call | tf_op jit(solution)/shard_map/gradient/pallas_call | solution.py:190
  128.8 1.8 %collective-permute-start.51 = (bf16[256,256]{1,0:T(8,128)(2,1)S(1)}, bf16[256,256]{1,0:T(8,128)(2,1)S(1)}, u32[]{:S(2)}, u32[]{:S(2)}) collective-permute-start(bf16[256,256]{1,0:T(8,128)(2,1)S(1)} %get-tuple-element.175), channel_id=1, source_target_pairs={{0,24},{1,25},{2,26},{3,27},{4,28},{5,29},{6,30},{7,31},{8,16},{9,... | collective-permute-start | bytes 393224 | tf_op jit(solution)/shard_map/ppermute | solution.py:40
  131.0 2.2 %collective-permute-start.53 = (bf16[256,256]{1,0:T(8,128)(2,1)S(1)}, bf16[256,256]{1,0:T(8,128)(2,1)S(1)}, u32[]{:S(2)}, u32[]{:S(2)}) collective-permute-start(bf16[256,256]{1,0:T(8,128)(2,1)S(1)} %get-tuple-element.177), channel_id=1, source_target_pairs={{0,8},{1,9},{2,10},{3,11},{4,12},{5,13},{6,14},{7,15},{8,0},{9,1},... | collective-permute-start | bytes 393224 | tf_op jit(solution)/shard_map/ppermute | solution.py:40
  133.2 2.1 %loss.1 = f32[1,1]{1,0:T(1,128)} custom-call(s32[3]{0:T(128)S(1)} %pad_add_fusion.place_ref, bf16[2,512,512]{2,1,0:T(8,128)(2,1)S(1)} %get-tuple-element.180.gram_ref, f32[1,1]{1,0:T(1,128)} %get-tuple-element.181.share_ref), custom_call_target="tpu_custom_call" | custom-call | tf_op jit(solution)/shard_map/loss/pallas_call | solution.py:190
  135.3 1.8 %collective-permute-done.51.refs_1_ = bf16[256,256]{1,0:T(8,128)(2,1)S(1)} collective-permute-done((bf16[256,256]{1,0:T(8,128)(2,1)S(1)}, bf16[256,256]{1,0:T(8,128)(2,1)S(1)}, u32[]{:S(2)}, u32[]{:S(2)}) %collective-permute-start.51) | collective-permute-done | bytes 131104 | tf_op jit(solution)/shard_map/ppermute | solution.py:40
  137.1 5.9 %collective-permute-done.52.refs_2_ = bf16[256,256]{1,0:T(8,128)(2,1)S(1)} collective-permute-done((bf16[256,256]{1,0:T(8,128)(2,1)S(1)}, bf16[256,256]{1,0:T(8,128)(2,1)S(1)}, u32[]{:S(2)}, u32[]{:S(2)}) %collective-permute-start.52) | collective-permute-done | bytes 131104 | tf_op jit(solution)/shard_map/ppermute | solution.py:40
  143.0 1.4 place.1
  (70 shorter events, 11.2 us)
Async XLA Ops:
  1.6 9.1 %collective-permute-start.10 = (bf16[32,1024]{1,0:T(8,128)(2,1)S(1)}, bf16[32,1024]{1,0:T(8,128)(2,1)S(1)}, u32[]{:S(2)}, u32[]{:S(2)}) collective-permute-start(bf16[32,1024]{1,0:T(8,128)(2,1)S(1)} %get-tuple-element.190), channel_id=1, source_target_pairs={{0,6},{1,7},{2,4},{3,5},{4,2},{5,3},{6,0},{7,1},{8,14},{9,15},{10,... | collective-permute-start | bytes 196616 | tf_op jit(solution)/shard_map/ppermute | solution.py:40
  5.6 5.2 %collective-permute-start.9 = (bf16[32,1024]{1,0:T(8,128)(2,1)S(1)}, bf16[32,1024]{1,0:T(8,128)(2,1)S(1)}, u32[]{:S(2)}, u32[]{:S(2)}) collective-permute-start(bf16[32,1024]{1,0:T(8,128)(2,1)S(1)} %get-tuple-element.191), channel_id=1, source_target_pairs={{0,4},{1,5},{2,6},{3,7},{4,0},{5,1},{6,2},{7,3},{8,12},{9,13},{10,... | collective-permute-start | bytes 196616 | tf_op jit(solution)/shard_map/ppermute | solution.py:40
  6.1 4.7 %collective-permute-start.8 = (bf16[32,1024]{1,0:T(8,128)(2,1)S(1)}, bf16[32,1024]{1,0:T(8,128)(2,1)S(1)}, u32[]{:S(2)}, u32[]{:S(2)}) collective-permute-start(bf16[32,1024]{1,0:T(8,128)(2,1)S(1)} %get-tuple-element.192), channel_id=1, source_target_pairs={{0,2},{1,3},{2,0},{3,1},{4,6},{5,7},{6,4},{7,5},{8,10},{9,11},{10,... | collective-permute-start | bytes 196616 | tf_op jit(solution)/shard_map/ppermute | solution.py:40
  7.2 8.9 %collective-permute-start.16 = (bf16[32,1024]{1,0:T(8,128)(2,1)S(1)}, bf16[32,1024]{1,0:T(8,128)(2,1)S(1)}, u32[]{:S(2)}, u32[]{:S(2)}) collective-permute-start(bf16[32,1024]{1,0:T(8,128)(2,1)S(1)} %get-tuple-element.186), channel_id=1, source_target_pairs={{0,6},{1,7},{2,4},{3,5},{4,2},{5,3},{6,0},{7,1},{8,14},{9,15},{10,... | collective-permute-start | bytes 196616 | tf_op jit(solution)/shard_map/ppermute | solution.py:40
  10.1 6.5 %collective-permute-start.15 = (bf16[32,1024]{1,0:T(8,128)(2,1)S(1)}, bf16[32,1024]{1,0:T(8,128)(2,1)S(1)}, u32[]{:S(2)}, u32[]{:S(2)}) collective-permute-start(bf16[32,1024]{1,0:T(8,128)(2,1)S(1)} %get-tuple-element.187), channel_id=1, source_target_pairs={{0,4},{1,5},{2,6},{3,7},{4,0},{5,1},{6,2},{7,3},{8,12},{9,13},{10,... | collective-permute-start | bytes 196616 | tf_op jit(solution)/shard_map/ppermute | solution.py:40
  10.7 5.9 %collective-permute-start.14 = (bf16[32,1024]{1,0:T(8,128)(2,1)S(1)}, bf16[32,1024]{1,0:T(8,128)(2,1)S(1)}, u32[]{:S(2)}, u32[]{:S(2)}) collective-permute-start(bf16[32,1024]{1,0:T(8,128)(2,1)S(1)} %get-tuple-element.188), channel_id=1, source_target_pairs={{0,2},{1,3},{2,0},{3,1},{4,6},{5,7},{6,4},{7,5},{8,10},{9,11},{10,... | collective-permute-start | bytes 196616 | tf_op jit(solution)/shard_map/ppermute | solution.py:40
  11.4 5.2 %collective-permute-start.11 = (bf16[32,1024]{1,0:T(8,128)(2,1)S(1)}, bf16[32,1024]{1,0:T(8,128)(2,1)S(1)}, u32[]{:S(2)}, u32[]{:S(2)}) collective-permute-start(bf16[32,1024]{1,0:T(8,128)(2,1)S(1)} %get-tuple-element.110), channel_id=1, source_target_pairs={{0,8},{1,9},{2,10},{3,11},{4,12},{5,13},{6,14},{7,15},{8,0},{9,1},... | collective-permute-start | bytes 196616 | tf_op jit(solution)/shard_map/ppermute | solution.py:40
  13.5 6.6 %collective-permute-start.12 = (bf16[32,1024]{1,0:T(8,128)(2,1)S(1)}, bf16[32,1024]{1,0:T(8,128)(2,1)S(1)}, u32[]{:S(2)}, u32[]{:S(2)}) collective-permute-start(bf16[32,1024]{1,0:T(8,128)(2,1)S(1)} %get-tuple-element.111), channel_id=1, source_target_pairs={{0,16},{1,17},{2,18},{3,19},{4,20},{5,21},{6,22},{7,23},{8,24},{9,... | collective-permute-start | bytes 196616 | tf_op jit(solution)/shard_map/ppermute | solution.py:40
  16.1 6.1 %collective-permute-start.13 = (bf16[32,1024]{1,0:T(8,128)(2,1)S(1)}, bf16[32,1024]{1,0:T(8,128)(2,1)S(1)}, u32[]{:S(2)}, u32[]{:S(2)}) collective-permute-start(bf16[32,1024]{1,0:T(8,128)(2,1)S(1)} %get-tuple-element.112), channel_id=1, source_target_pairs={{0,24},{1,25},{2,26},{3,27},{4,28},{5,29},{6,30},{7,31},{8,16},{9,... | collective-permute-start | bytes 196616 | tf_op jit(solution)/shard_map/ppermute | solution.py:40
  22.7 15.0 %collective-permute-start.19 = (bf16[128,1024]{1,0:T(8,128)(2,1)S(1)}, bf16[128,1024]{1,0:T(8,128)(2,1)S(1)}, u32[]{:S(2)}, u32[]{:S(2)}) collective-permute-start(bf16[128,1024]{1,0:T(8,128)(2,1)S(1)} %lay.2.refs_0_), channel_id=1, source_target_pairs={{0,6},{1,7},{2,4},{3,5},{4,2},{5,3},{6,0},{7,1},{8,14},{9,15},{10,... | collective-permute-start | bytes 786440 | tf_op jit(solution)/shard_map/ppermute | solution.py:40
  25.2 12.5 %collective-permute-start.18 = (bf16[128,1024]{1,0:T(8,128)(2,1)S(1)}, bf16[128,1024]{1,0:T(8,128)(2,1)S(1)}, u32[]{:S(2)}, u32[]{:S(2)}) collective-permute-start(bf16[128,1024]{1,0:T(8,128)(2,1)S(1)} %lay.2.refs_0_), channel_id=1, source_target_pairs={{0,4},{1,5},{2,6},{3,7},{4,0},{5,1},{6,2},{7,3},{8,12},{9,13},{10,... | collective-permute-start | bytes 786440 | tf_op jit(solution)/shard_map/ppermute | solution.py:40
  25.7 12.0 %collective-permute-start.17 = (bf16[128,1024]{1,0:T(8,128)(2,1)S(1)}, bf16[128,1024]{1,0:T(8,128)(2,1)S(1)}, u32[]{:S(2)}, u32[]{:S(2)}) collective-permute-start(bf16[128,1024]{1,0:T(8,128)(2,1)S(1)} %lay.2.refs_0_), channel_id=1, source_target_pairs={{0,2},{1,3},{2,0},{3,1},{4,6},{5,7},{6,4},{7,5},{8,10},{9,11},{10,... | collective-permute-start | bytes 786440 | tf_op jit(solution)/shard_map/ppermute | solution.py:40
  26.3 6.2 %collective-permute-start.22 = (bf16[32,1024]{1,0:T(8,128)(2,1)S(1)}, bf16[32,1024]{1,0:T(8,128)(2,1)S(1)}, u32[]{:S(2)}, u32[]{:S(2)}) collective-permute-start(bf16[32,1024]{1,0:T(8,128)(2,1)S(1)} %get-tuple-element.182), channel_id=1, source_target_pairs={{0,24},{1,25},{2,26},{3,27},{4,28},{5,29},{6,30},{7,31},{8,16},{9,... | collective-permute-start | bytes 196616 | tf_op jit(solution)/shard_map/ppermute | solution.py:40
  27.1 7.6 %collective-permute-start.20 = (bf16[32,1024]{1,0:T(8,128)(2,1)S(1)}, bf16[32,1024]{1,0:T(8,128)(2,1)S(1)}, u32[]{:S(2)}, u32[]{:S(2)}) collective-permute-start(bf16[32,1024]{1,0:T(8,128)(2,1)S(1)} %get-tuple-element.183), channel_id=1, source_target_pairs={{0,8},{1,9},{2,10},{3,11},{4,12},{5,13},{6,14},{7,15},{8,0},{9,1},... | collective-permute-start | bytes 196616 | tf_op jit(solution)/shard_map/ppermute | solution.py:40
  32.5 5.2 %collective-permute-start.21 = (bf16[32,1024]{1,0:T(8,128)(2,1)S(1)}, bf16[32,1024]{1,0:T(8,128)(2,1)S(1)}, u32[]{:S(2)}, u32[]{:S(2)}) collective-permute-start(bf16[32,1024]{1,0:T(8,128)(2,1)S(1)} %get-tuple-element.184), channel_id=1, source_target_pairs={{0,16},{1,17},{2,18},{3,19},{4,20},{5,21},{6,22},{7,23},{8,24},{9,... | collective-permute-start | bytes 196616 | tf_op jit(solution)/shard_map/ppermute | solution.py:40
  37.7 4.2 %collective-permute-start.23 = (bf16[128,1024]{1,0:T(8,128)(2,1)S(1)}, bf16[128,1024]{1,0:T(8,128)(2,1)S(1)}, u32[]{:S(2)}, u32[]{:S(2)}) collective-permute-start(bf16[128,1024]{1,0:T(8,128)(2,1)S(1)} %lay.2.refs_0_), channel_id=1, source_target_pairs={{0,1},{1,0},{2,3},{3,2},{4,5},{5,4},{6,7},{7,6},{8,9},{9,8},{10,11... | collective-permute-start | bytes 786440 | tf_op jit(solution)/shard_map/ppermute | solution.py:40
  37.8 4.1 %collective-permute-start.24 = (bf16[128,1024]{1,0:T(8,128)(2,1)S(1)}, bf16[128,1024]{1,0:T(8,128)(2,1)S(1)}, u32[]{:S(2)}, u32[]{:S(2)}) collective-permute-start(bf16[128,1024]{1,0:T(8,128)(2,1)S(1)} %collective-permute-done.17.refs_1_), channel_id=1, source_target_pairs={{0,1},{1,0},{2,3},{3,2},{4,5},{5,4},{6,7},{7,6},{8,9},{9,8},{10,11... | collective-permute-start | bytes 786440 | tf_op jit(solution)/shard_map/ppermute | solution.py:40
  38.3 3.6 %collective-permute-start.25 = (bf16[128,1024]{1,0:T(8,128)(2,1)S(1)}, bf16[128,1024]{1,0:T(8,128)(2,1)S(1)}, u32[]{:S(2)}, u32[]{:S(2)}) collective-permute-start(bf16[128,1024]{1,0:T(8,128)(2,1)S(1)} %collective-permute-done.18.refs_2_), channel_id=1, source_target_pairs={{0,1},{1,0},{2,3},{3,2},{4,5},{5,4},{6,7},{7,6},{8,9},{9,8},{10,11... | collective-permute-start | bytes 786440 | tf_op jit(solution)/shard_map/ppermute | solution.py:40
  38.3 3.5 %collective-permute-start.26 = (bf16[128,1024]{1,0:T(8,128)(2,1)S(1)}, bf16[128,1024]{1,0:T(8,128)(2,1)S(1)}, u32[]{:S(2)}, u32[]{:S(2)}) collective-permute-start(bf16[128,1024]{1,0:T(8,128)(2,1)S(1)} %collective-permute-done.19.refs_3_), channel_id=1, source_target_pairs={{0,1},{1,0},{2,3},{3,2},{4,5},{5,4},{6,7},{7,6},{8,9},{9,8},{10,11... | collective-permute-start | bytes 786440 | tf_op jit(solution)/shard_map/ppermute | solution.py:40
  39.3 10.9 %collective-permute-start.27 = (bf16[128,1024]{1,0:T(8,128)(2,1)S(1)}, bf16[128,1024]{1,0:T(8,128)(2,1)}, u32[]{:S(2)}, u32[]{:S(2)}) collective-permute-start(bf16[128,1024]{1,0:T(8,128)(2,1)S(1)} %lay.3), channel_id=1, source_target_pairs={{0,6},{1,7},{2,4},{3,5},{4,2},{5,3},{6,0},{7,1},{8,14},{9,15},{10,... | collective-permute-start | bytes 786440 | tf_op jit(solution)/shard_map/ppermute | solution.py:40
  45.8 23.0 %collective-permute-start.31 = (bf16[528,256]{1,0:T(8,128)(2,1)S(1)}, bf16[528,256]{1,0:T(8,128)(2,1)S(1)}, u32[]{:S(2)}, u32[]{:S(2)}) collective-permute-start(bf16[528,256]{1,0:T(8,128)(2,1)S(1)} %get-tuple-element.144), channel_id=1, source_target_pairs={{0,24},{1,25},{2,26},{3,27},{4,28},{5,29},{6,30},{7,31},{8,16},{9,... | collective-permute-start | bytes 811016 | tf_op jit(solution)/shard_map/ppermute | solution.py:40
  47.4 23.6 %collective-permute-start.32 = (bf16[528,256]{1,0:T(8,128)(2,1)S(1)}, bf16[528,256]{1,0:T(8,128)(2,1)S(1)}, u32[]{:S(2)}, u32[]{:S(2)}) collective-permute-start(bf16[528,256]{1,0:T(8,128)(2,1)S(1)} %get-tuple-element.145), channel_id=1, source_target_pairs={{0,16},{1,17},{2,18},{3,19},{4,20},{5,21},{6,22},{7,23},{8,24},{9,... | collective-permute-start | bytes 811016 | tf_op jit(solution)/shard_map/ppermute | solution.py:40
  47.5 23.6 %collective-permute-start.33 = (bf16[528,256]{1,0:T(8,128)(2,1)S(1)}, bf16[528,256]{1,0:T(8,128)(2,1)S(1)}, u32[]{:S(2)}, u32[]{:S(2)}) collective-permute-start(bf16[528,256]{1,0:T(8,128)(2,1)S(1)} %get-tuple-element.146), channel_id=1, source_target_pairs={{0,8},{1,9},{2,10},{3,11},{4,12},{5,13},{6,14},{7,15},{8,0},{9,1},... | collective-permute-start | bytes 811016 | tf_op jit(solution)/shard_map/ppermute | solution.py:40
  50.2 7.2 %collective-permute-start.4 = (bf16[128,1024]{1,0:T(8,128)(2,1)S(1)}, bf16[128,1024]{1,0:T(8,128)(2,1)S(1)}, u32[]{:S(2)}, u32[]{:S(2)}) collective-permute-start(bf16[128,1024]{1,0:T(8,128)(2,1)S(1)} %get-tuple-element.16.refs_0_), channel_id=1, source_target_pairs={{0,2},{1,3},{2,0},{3,1},{4,6},{5,7},{6,4},{7,5},{8,10},{9,11},{10,... | collective-permute-start | bytes 786440 | tf_op jit(solution)/shard_map/cond/branch_1_fun/ppermute | solution.py:40
  50.8 6.9 %collective-permute-start.5 = (bf16[128,1024]{1,0:T(8,128)(2,1)S(1)}, bf16[128,1024]{1,0:T(8,128)(2,1)S(1)}, u32[]{:S(2)}, u32[]{:S(2)}) collective-permute-start(bf16[128,1024]{1,0:T(8,128)(2,1)S(1)} %get-tuple-element.16.refs_0_), channel_id=1, source_target_pairs={{0,4},{1,5},{2,6},{3,7},{4,0},{5,1},{6,2},{7,3},{8,12},{9,13},{10,... | collective-permute-start | bytes 786440 | tf_op jit(solution)/shard_map/cond/branch_1_fun/ppermute | solution.py:40
  57.7 3.9 %collective-permute-start.7 = (bf16[256,1024]{1,0:T(8,128)(2,1)S(1)}, bf16[256,1024]{1,0:T(8,128)(2,1)S(1)}, u32[]{:S(2)}, u32[]{:S(2)}) collective-permute-start(bf16[256,1024]{1,0:T(8,128)(2,1)S(1)} %pad_maximum_fusion.1), channel_id=1, source_target_pairs={{0,1},{1,0},{2,3},{3,2},{4,5},{5,4},{6,7},{7,6},{8,9},{9,8},{10,11... | collective-permute-start | bytes 1572872 | tf_op jit(solution)/shard_map/cond/branch_1_fun/ppermute | solution.py:40
  58.8 2.8 %collective-permute-start.6 = (bf16[256,1024]{1,0:T(8,128)(2,1)S(1)}, bf16[256,1024]{1,0:T(8,128)(2,1)S(1)}, u32[]{:S(2)}, u32[]{:S(2)}) collective-permute-start(bf16[256,1024]{1,0:T(8,128)(2,1)S(1)} %pad_maximum_fusion), channel_id=1, source_target_pairs={{0,1},{1,0},{2,3},{3,2},{4,5},{5,4},{6,7},{7,6},{8,9},{9,8},{10,11... | collective-permute-start | bytes 1572872 | tf_op jit(solution)/shard_map/cond/branch_1_fun/ppermute | solution.py:40
  66.6 23.8 %collective-permute-start.28 = (bf16[528,256]{1,0:T(8,128)(2,1)}, bf16[528,256]{1,0:T(8,128)(2,1)S(1)}, u32[]{:S(2)}, u32[]{:S(2)}) collective-permute-start(bf16[528,256]{1,0:T(8,128)(2,1)} %get-tuple-element.140), channel_id=1, source_target_pairs={{0,8},{1,9},{2,10},{3,11},{4,12},{5,13},{6,14},{7,15},{8,0},{9,1},... | collective-permute-start | bytes 811016 | tf_op jit(solution)/shard_map/ppermute | solution.py:40
  66.9 25.5 %collective-permute-start.29 = (bf16[528,256]{1,0:T(8,128)(2,1)}, bf16[528,256]{1,0:T(8,128)(2,1)S(1)}, u32[]{:S(2)}, u32[]{:S(2)}) collective-permute-start(bf16[528,256]{1,0:T(8,128)(2,1)} %get-tuple-element.141), channel_id=1, source_target_pairs={{0,16},{1,17},{2,18},{3,19},{4,20},{5,21},{6,22},{7,23},{8,24},{9,... | collective-permute-start | bytes 811016 | tf_op jit(solution)/shard_map/ppermute | solution.py:40
  68.7 23.7 %collective-permute-start.30 = (bf16[528,256]{1,0:T(8,128)(2,1)}, bf16[528,256]{1,0:T(8,128)(2,1)S(1)}, u32[]{:S(2)}, u32[]{:S(2)}) collective-permute-start(bf16[528,256]{1,0:T(8,128)(2,1)} %get-tuple-element.142), channel_id=1, source_target_pairs={{0,24},{1,25},{2,26},{3,27},{4,28},{5,29},{6,30},{7,31},{8,16},{9,... | collective-permute-start | bytes 811016 | tf_op jit(solution)/shard_map/ppermute | solution.py:40
  74.4 2.1 %collective-permute-start = (f32[256,512]{1,0:T(8,128)}, f32[256,512]{1,0:T(8,128)S(1)}, u32[]{:S(2)}, u32[]{:S(2)}) collective-permute-start(f32[256,512]{1,0:T(8,128)} %get-tuple-element.26), channel_id=1, source_target_pairs={{0,1},{1,0},{2,3},{3,2},{4,5},{5,4},{6,7},{7,6},{8,9},{9,8},{10,11... | collective-permute-start | bytes 1572872 | tf_op jit(solution)/shard_map/cond/branch_1_fun/ppermute | solution.py:40
  77.9 4.2 %collective-permute-start.1 = (bf16[208,128]{1,0:T(8,128)(2,1)S(1)}, bf16[208,128]{1,0:T(8,128)(2,1)S(1)}, u32[]{:S(2)}, u32[]{:S(2)}) collective-permute-start(bf16[208,128]{1,0:T(8,128)(2,1)S(1)} %get-tuple-element.28), channel_id=1, source_target_pairs={{0,2},{1,3},{2,0},{3,1},{4,6},{5,7},{6,4},{7,5},{8,10},{9,11},{10,... | collective-permute-start | bytes 159752 | tf_op jit(solution)/shard_map/cond/branch_1_fun/ppermute | solution.py:40
  79.4 4.1 %collective-permute-start.2 = (bf16[208,128]{1,0:T(8,128)(2,1)S(1)}, bf16[208,128]{1,0:T(8,128)(2,1)S(1)}, u32[]{:S(2)}, u32[]{:S(2)}) collective-permute-start(bf16[208,128]{1,0:T(8,128)(2,1)S(1)} %get-tuple-element.31), channel_id=1, source_target_pairs={{0,4},{1,5},{2,6},{3,7},{4,0},{5,1},{6,2},{7,3},{8,12},{9,13},{10,... | collective-permute-start | bytes 159752 | tf_op jit(solution)/shard_map/cond/branch_1_fun/ppermute | solution.py:40
  82.1 5.0 %collective-permute-start.3 = (bf16[208,128]{1,0:T(8,128)(2,1)S(1)}, bf16[208,128]{1,0:T(8,128)(2,1)S(1)}, u32[]{:S(2)}, u32[]{:S(2)}) collective-permute-start(bf16[208,128]{1,0:T(8,128)(2,1)S(1)} %get-tuple-element.32), channel_id=1, source_target_pairs={{0,6},{1,7},{2,4},{3,5},{4,2},{5,3},{6,0},{7,1},{8,14},{9,15},{10,... | collective-permute-start | bytes 159752 | tf_op jit(solution)/shard_map/cond/branch_1_fun/ppermute | solution.py:40
  87.9 4.5 %collective-permute-start.34 = (bf16[64,128]{1,0:T(8,128)(2,1)S(1)}, bf16[64,128]{1,0:T(8,128)(2,1)S(1)}, u32[]{:S(2)}, u32[]{:S(2)}) collective-permute-start(bf16[64,128]{1,0:T(8,128)(2,1)S(1)} %get-tuple-element.150), channel_id=1, source_target_pairs={{0,8},{1,9},{2,10},{3,11},{4,12},{5,13},{6,14},{7,15},{8,0},{9,1},... | collective-permute-start | bytes 49160 | tf_op jit(solution)/shard_map/ppermute | solution.py:40
  88.0 6.6 %collective-permute-start.35 = (bf16[64,128]{1,0:T(8,128)(2,1)S(1)}, bf16[64,128]{1,0:T(8,128)(2,1)S(1)}, u32[]{:S(2)}, u32[]{:S(2)}) collective-permute-start(bf16[64,128]{1,0:T(8,128)(2,1)S(1)} %get-tuple-element.151), channel_id=1, source_target_pairs={{0,16},{1,17},{2,18},{3,19},{4,20},{5,21},{6,22},{7,23},{8,24},{9,... | collective-permute-start | bytes 49160 | tf_op jit(solution)/shard_map/ppermute | solution.py:40
  90.4 5.5 %collective-permute-start.36 = (bf16[64,128]{1,0:T(8,128)(2,1)S(1)}, bf16[64,128]{1,0:T(8,128)(2,1)S(1)}, u32[]{:S(2)}, u32[]{:S(2)}) collective-permute-start(bf16[64,128]{1,0:T(8,128)(2,1)S(1)} %get-tuple-element.152), channel_id=1, source_target_pairs={{0,24},{1,25},{2,26},{3,27},{4,28},{5,29},{6,30},{7,31},{8,16},{9,... | collective-permute-start | bytes 49160 | tf_op jit(solution)/shard_map/ppermute | solution.py:40
  98.5 2.0 %collective-permute-start.37 = (f32[256,512]{1,0:T(8,128)S(1)}, f32[256,512]{1,0:T(8,128)S(1)}, u32[]{:S(2)}, u32[]{:S(2)}) collective-permute-start(f32[256,512]{1,0:T(8,128)S(1)} %get-tuple-element.159), channel_id=1, source_target_pairs={{0,1},{1,0},{2,3},{3,2},{4,5},{5,4},{6,7},{7,6},{8,9},{9,8},{10,11... | collective-permute-start | bytes 1572872 | tf_op jit(solution)/shard_map/ppermute | solution.py:40
  101.3 4.2 %collective-permute-start.38 = (bf16[208,128]{1,0:T(8,128)(2,1)S(1)}, bf16[208,128]{1,0:T(8,128)(2,1)S(1)}, u32[]{:S(2)}, u32[]{:S(2)}) collective-permute-start(bf16[208,128]{1,0:T(8,128)(2,1)S(1)} %get-tuple-element.161), channel_id=1, source_target_pairs={{0,2},{1,3},{2,0},{3,1},{4,6},{5,7},{6,4},{7,5},{8,10},{9,11},{10,... | collective-permute-start | bytes 159752 | tf_op jit(solution)/shard_map/ppermute | solution.py:40
  102.6 4.7 %collective-permute-start.39 = (bf16[208,128]{1,0:T(8,128)(2,1)S(1)}, bf16[208,128]{1,0:T(8,128)(2,1)S(1)}, u32[]{:S(2)}, u32[]{:S(2)}) collective-permute-start(bf16[208,128]{1,0:T(8,128)(2,1)S(1)} %get-tuple-element.162), channel_id=1, source_target_pairs={{0,4},{1,5},{2,6},{3,7},{4,0},{5,1},{6,2},{7,3},{8,12},{9,13},{10,... | collective-permute-start | bytes 159752 | tf_op jit(solution)/shard_map/ppermute | solution.py:40
  103.2 5.0 %collective-permute-start.40 = (bf16[208,128]{1,0:T(8,128)(2,1)S(1)}, bf16[208,128]{1,0:T(8,128)(2,1)S(1)}, u32[]{:S(2)}, u32[]{:S(2)}) collective-permute-start(bf16[208,128]{1,0:T(8,128)(2,1)S(1)} %get-tuple-element.163), channel_id=1, source_target_pairs={{0,6},{1,7},{2,4},{3,5},{4,2},{5,3},{6,0},{7,1},{8,14},{9,15},{10,... | collective-permute-start | bytes 159752 | tf_op jit(solution)/shard_map/ppermute | solution.py:40
  109.1 6.7 %collective-permute-start.43 = (bf16[256,128]{1,0:T(8,128)(2,1)S(1)}, bf16[256,128]{1,0:T(8,128)(2,1)S(1)}, u32[]{:S(2)}, u32[]{:S(2)}) collective-permute-start(bf16[256,128]{1,0:T(8,128)(2,1)S(1)} %code.1.refs_0_), channel_id=1, source_target_pairs={{0,24},{1,25},{2,26},{3,27},{4,28},{5,29},{6,30},{7,31},{8,16},{9,... | collective-permute-start | bytes 196616 | tf_op jit(solution)/shard_map/ppermute | solution.py:40
  111.4 5.7 %collective-permute-start.42 = (bf16[256,128]{1,0:T(8,128)(2,1)S(1)}, bf16[256,128]{1,0:T(8,128)(2,1)S(1)}, u32[]{:S(2)}, u32[]{:S(2)}) collective-permute-start(bf16[256,128]{1,0:T(8,128)(2,1)S(1)} %code.1.refs_0_), channel_id=1, source_target_pairs={{0,16},{1,17},{2,18},{3,19},{4,20},{5,21},{6,22},{7,23},{8,24},{9,... | collective-permute-start | bytes 196616 | tf_op jit(solution)/shard_map/ppermute | solution.py:40
  111.4 5.7 %collective-permute-start.41 = (bf16[256,128]{1,0:T(8,128)(2,1)S(1)}, bf16[256,128]{1,0:T(8,128)(2,1)S(1)}, u32[]{:S(2)}, u32[]{:S(2)}) collective-permute-start(bf16[256,128]{1,0:T(8,128)(2,1)S(1)} %code.1.refs_0_), channel_id=1, source_target_pairs={{0,8},{1,9},{2,10},{3,11},{4,12},{5,13},{6,14},{7,15},{8,0},{9,1},... | collective-permute-start | bytes 196616 | tf_op jit(solution)/shard_map/ppermute | solution.py:40
  118.1 5.6 %collective-permute-start.46 = (bf16[128,384]{1,0:T(8,128)(2,1)S(1)}, bf16[128,384]{1,0:T(8,128)(2,1)S(1)}, u32[]{:S(2)}, u32[]{:S(2)}) collective-permute-start(bf16[128,384]{1,0:T(8,128)(2,1)S(1)} %finish.1.refs_0_), channel_id=1, source_target_pairs={{0,6},{1,7},{2,4},{3,5},{4,2},{5,3},{6,0},{7,1},{8,14},{9,15},{10,... | collective-permute-start | bytes 294920 | tf_op jit(solution)/shard_map/ppermute | solution.py:40
  119.6 5.1 %collective-permute-start.45 = (bf16[128,384]{1,0:T(8,128)(2,1)S(1)}, bf16[128,384]{1,0:T(8,128)(2,1)S(1)}, u32[]{:S(2)}, u32[]{:S(2)}) collective-permute-start(bf16[128,384]{1,0:T(8,128)(2,1)S(1)} %finish.1.refs_0_), channel_id=1, source_target_pairs={{0,4},{1,5},{2,6},{3,7},{4,0},{5,1},{6,2},{7,3},{8,12},{9,13},{10,... | collective-permute-start | bytes 294920 | tf_op jit(solution)/shard_map/ppermute | solution.py:40
  120.9 4.6 %collective-permute-start.44 = (bf16[128,384]{1,0:T(8,128)(2,1)S(1)}, bf16[128,384]{1,0:T(8,128)(2,1)S(1)}, u32[]{:S(2)}, u32[]{:S(2)}) collective-permute-start(bf16[128,384]{1,0:T(8,128)(2,1)S(1)} %finish.1.refs_0_), channel_id=1, source_target_pairs={{0,2},{1,3},{2,0},{3,1},{4,6},{5,7},{6,4},{7,5},{8,10},{9,11},{10,... | collective-permute-start | bytes 294920 | tf_op jit(solution)/shard_map/ppermute | solution.py:40
  121.6 3.9 %collective-permute-start.47 = (bf16[128,384]{1,0:T(8,128)(2,1)S(1)}, bf16[128,384]{1,0:T(8,128)(2,1)S(1)}, u32[]{:S(2)}, u32[]{:S(2)}) collective-permute-start(bf16[128,384]{1,0:T(8,128)(2,1)S(1)} %finish.1.refs_0_), channel_id=1, source_target_pairs={{0,1},{1,0},{2,3},{3,2},{4,5},{5,4},{6,7},{7,6},{8,9},{9,8},{10,11... | collective-permute-start | bytes 294920 | tf_op jit(solution)/shard_map/ppermute | solution.py:40
  123.7 1.8 %collective-permute-start.50 = (bf16[128,384]{1,0:T(8,128)(2,1)S(1)}, bf16[128,384]{1,0:T(8,128)(2,1)S(1)}, u32[]{:S(2)}, u32[]{:S(2)}) collective-permute-start(bf16[128,384]{1,0:T(8,128)(2,1)S(1)} %collective-permute-done.46.refs_3_), channel_id=1, source_target_pairs={{0,1},{1,0},{2,3},{3,2},{4,5},{5,4},{6,7},{7,6},{8,9},{9,8},{10,11... | collective-permute-start | bytes 294920 | tf_op jit(solution)/shard_map/ppermute | solution.py:40
  124.7 1.3 collective-permute-start.49
  125.5 1.3 collective-permute-start.48
  128.8 8.3 %collective-permute-start.51 = (bf16[256,256]{1,0:T(8,128)(2,1)S(1)}, bf16[256,256]{1,0:T(8,128)(2,1)S(1)}, u32[]{:S(2)}, u32[]{:S(2)}) collective-permute-start(bf16[256,256]{1,0:T(8,128)(2,1)S(1)} %get-tuple-element.175), channel_id=1, source_target_pairs={{0,24},{1,25},{2,26},{3,27},{4,28},{5,29},{6,30},{7,31},{8,16},{9,... | collective-permute-start | bytes 393224 | tf_op jit(solution)/shard_map/ppermute | solution.py:40
  130.6 12.4 %collective-permute-start.52 = (bf16[256,256]{1,0:T(8,128)(2,1)S(1)}, bf16[256,256]{1,0:T(8,128)(2,1)S(1)}, u32[]{:S(2)}, u32[]{:S(2)}) collective-permute-start(bf16[256,256]{1,0:T(8,128)(2,1)S(1)} %get-tuple-element.176), channel_id=1, source_target_pairs={{0,16},{1,17},{2,18},{3,19},{4,20},{5,21},{6,22},{7,23},{8,24},{9,... | collective-permute-start | bytes 393224 | tf_op jit(solution)/shard_map/ppermute | solution.py:40
  131.0 12.0 %collective-permute-start.53 = (bf16[256,256]{1,0:T(8,128)(2,1)S(1)}, bf16[256,256]{1,0:T(8,128)(2,1)S(1)}, u32[]{:S(2)}, u32[]{:S(2)}) collective-permute-start(bf16[256,256]{1,0:T(8,128)(2,1)S(1)} %get-tuple-element.177), channel_id=1, source_target_pairs={{0,8},{1,9},{2,10},{3,11},{4,12},{5,13},{6,14},{7,15},{8,0},{9,1},... | collective-permute-start | bytes 393224 | tf_op jit(solution)/shard_map/ppermute | solution.py:40

commit v16 on v15

--- a/solution.py
+++ b/solution.py
@@ -74,7 +74,7 @@
 def sends(place, axis, parts, few=False):
     size, here, toward = place.along(axis)
     met = {0: parts[0]}
-    order = [*range(1, size)] if few else [*range(size - 1, 0, -1)]
+    order = [size - 1, *range(1, size - 1)] if few else [*range(size - 1, 0, -1)]
     for i, step in enumerate(order):
         part = parts[step]
         if few and i >= 2:

time: 145 us -> 145 us (level)
  transfers between devices with their start and end apart: 54 -> 54, of which waited for: 24 -> 23; matrix products, arithmetic and copies ran while one was open for 1% -> 1% of each run, Pallas kernels for 16% -> 16%
where the time goes in v16:
time: 145 us
  starting transfers between devices  57.1 us (39%)
  waiting for transfers between devices  51.7 us (36%)
  Pallas kernels  31.9 us (22%)
  local copies, waits for them, and re-layouts  1.91 us (1%)
    ppermute x54, starting transfers between devices, send(): return lax.ppermute(value, ('dp', 'mp'), pairs)  57.1 us
    ppermute x54, waiting for transfers between devices, send(): return lax.ppermute(value, ('dp', 'mp'), pairs)  51.7 us
    pallas_call x12, Pallas kernels, local(): pl.pallas_call(kernel, in_specs=[pl.BlockSpec(memory_space=pltpu.SMEM)] +...  12.6 us
    pallas_call x2, Pallas kernels, project(): pl.pallas_call(functools.partial(project_kernel, counts=counts, n=n, k=k)...  8.91 us
    pallas_call x2, Pallas kernels, normalize_parts(): pl.pallas_call(functools.partial(normalize_kernel, n=n, k=k, order=order,...  6.01 us
    pallas_call x2, Pallas kernels, fetch(): pl.pallas_call(fetch_kernel, in_specs=[pl.BlockSpec(memory_space=pl.ANY)]...  4.39 us
  transfers between devices with their start and end apart: 54, of which 23 were waited for; matrix products, arithmetic and copies ran while one was open for 1% of the time, Pallas kernels for 16%

profile of v16, /device:TPU:0, one launch (start us, length us, event | category | flops | bytes accessed | tf_op | source)
XLA Modules:
  0.0 144.7 jit_solution(3724185989323948073)
XLA Ops:
  0.7 1.0 dynamic-slice_bitcast_fusion.4
  1.6 4.0 %collective-permute-start.10 = (bf16[32,1024]{1,0:T(8,128)(2,1)S(1)}, bf16[32,1024]{1,0:T(8,128)(2,1)S(1)}, u32[]{:S(2)}, u32[]{:S(2)}) collective-permute-start(bf16[32,1024]{1,0:T(8,128)(2,1)S(1)} %get-tuple-element.190), channel_id=1, source_target_pairs={{0,6},{1,7},{2,4},{3,5},{4,2},{5,3},{6,0},{7,1},{8,14},{9,15},{10,... | collective-permute-start | bytes 196616 | tf_op jit(solution)/shard_map/ppermute | solution.py:40
  6.2 1.0 dynamic-slice_bitcast_fusion
  7.2 2.9 %collective-permute-start.16 = (bf16[32,1024]{1,0:T(8,128)(2,1)S(1)}, bf16[32,1024]{1,0:T(8,128)(2,1)S(1)}, u32[]{:S(2)}, u32[]{:S(2)}) collective-permute-start(bf16[32,1024]{1,0:T(8,128)(2,1)S(1)} %get-tuple-element.186), channel_id=1, source_target_pairs={{0,6},{1,7},{2,4},{3,5},{4,2},{5,3},{6,0},{7,1},{8,14},{9,15},{10,... | collective-permute-start | bytes 196616 | tf_op jit(solution)/shard_map/ppermute | solution.py:40
  11.4 2.0 %collective-permute-start.11 = (bf16[32,1024]{1,0:T(8,128)(2,1)S(1)}, bf16[32,1024]{1,0:T(8,128)(2,1)S(1)}, u32[]{:S(2)}, u32[]{:S(2)}) collective-permute-start(bf16[32,1024]{1,0:T(8,128)(2,1)S(1)} %get-tuple-element.110), channel_id=1, source_target_pairs={{0,8},{1,9},{2,10},{3,11},{4,12},{5,13},{6,14},{7,15},{8,0},{9,1},... | collective-permute-start | bytes 196616 | tf_op jit(solution)/shard_map/ppermute | solution.py:40
  13.5 2.6 %collective-permute-start.12 = (bf16[32,1024]{1,0:T(8,128)(2,1)S(1)}, bf16[32,1024]{1,0:T(8,128)(2,1)S(1)}, u32[]{:S(2)}, u32[]{:S(2)}) collective-permute-start(bf16[32,1024]{1,0:T(8,128)(2,1)S(1)} %get-tuple-element.111), channel_id=1, source_target_pairs={{0,16},{1,17},{2,18},{3,19},{4,20},{5,21},{6,22},{7,23},{8,24},{9,... | collective-permute-start | bytes 196616 | tf_op jit(solution)/shard_map/ppermute | solution.py:40
  16.6 3.4 %collective-permute-done.12.refs_2_ = bf16[32,1024]{1,0:T(8,128)(2,1)S(1)} collective-permute-done((bf16[32,1024]{1,0:T(8,128)(2,1)S(1)}, bf16[32,1024]{1,0:T(8,128)(2,1)S(1)}, u32[]{:S(2)}, u32[]{:S(2)}) %collective-permute-start.12) | collective-permute-done | bytes 65568 | tf_op jit(solution)/shard_map/ppermute | solution.py:40
  20.0 2.1 %collective-permute-done.13.refs_1_ = bf16[32,1024]{1,0:T(8,128)(2,1)S(1)} collective-permute-done((bf16[32,1024]{1,0:T(8,128)(2,1)S(1)}, bf16[32,1024]{1,0:T(8,128)(2,1)S(1)}, u32[]{:S(2)}, u32[]{:S(2)}) %collective-permute-start.13) | collective-permute-done | bytes 65568 | tf_op jit(solution)/shard_map/ppermute | solution.py:40
  22.7 2.5 %collective-permute-start.19 = (bf16[128,1024]{1,0:T(8,128)(2,1)S(1)}, bf16[128,1024]{1,0:T(8,128)(2,1)S(1)}, u32[]{:S(2)}, u32[]{:S(2)}) collective-permute-start(bf16[128,1024]{1,0:T(8,128)(2,1)S(1)} %lay.2.refs_0_), channel_id=1, source_target_pairs={{0,6},{1,7},{2,4},{3,5},{4,2},{5,3},{6,0},{7,1},{8,14},{9,15},{10,... | collective-permute-start | bytes 786440 | tf_op jit(solution)/shard_map/ppermute | solution.py:40
  26.3 0.9 collective-permute-start.22
  27.2 5.4 %collective-permute-done.22.refs_1_ = bf16[32,1024]{1,0:T(8,128)(2,1)S(1)} collective-permute-done((bf16[32,1024]{1,0:T(8,128)(2,1)S(1)}, bf16[32,1024]{1,0:T(8,128)(2,1)S(1)}, u32[]{:S(2)}, u32[]{:S(2)}) %collective-permute-start.22) | collective-permute-done | bytes 65568 | tf_op jit(solution)/shard_map/ppermute | solution.py:40
  32.5 2.2 %fetch.3.refs_8_ = bf16[2048,1024]{1,0:T(8,128)(2,1)S(1)} custom-call(bf16[2048,1024]{1,0:T(8,128)(2,1)} %weight_ref), custom_call_target="tpu_custom_call" | custom-call | bytes 8388608 | tf_op jit(solution)/shard_map/fetch/pallas_call | solution.py:265
  34.7 2.9 %collective-permute-done.21.refs_2_ = bf16[32,1024]{1,0:T(8,128)(2,1)S(1)} collective-permute-done((bf16[32,1024]{1,0:T(8,128)(2,1)S(1)}, bf16[32,1024]{1,0:T(8,128)(2,1)S(1)}, u32[]{:S(2)}, u32[]{:S(2)}) %collective-permute-start.21) | collective-permute-done | bytes 65568 | tf_op jit(solution)/shard_map/ppermute | solution.py:40
  39.3 2.5 %collective-permute-start.27 = (bf16[128,1024]{1,0:T(8,128)(2,1)S(1)}, bf16[128,1024]{1,0:T(8,128)(2,1)}, u32[]{:S(2)}, u32[]{:S(2)}) collective-permute-start(bf16[128,1024]{1,0:T(8,128)(2,1)S(1)} %lay.3), channel_id=1, source_target_pairs={{0,6},{1,7},{2,4},{3,5},{4,2},{5,3},{6,0},{7,1},{8,14},{9,15},{10,... | collective-permute-start | bytes 786440 | tf_op jit(solution)/shard_map/ppermute | solution.py:40
  41.9 3.9 %project.3 = (f32[512,256]{1,0:T(8,128)S(1)}, bf16[528,256]{1,0:T(8,128)(2,1)S(1)}, bf16[528,256]{1,0:T(8,128)(2,1)S(1)}, bf16[528,256]{1,0:T(8,128)(2,1)S(1)}) custom-call(s32[3]{0:T(128)S(1)} %pad_add_fusion.place_ref, bf16[128,1024]{1,0:T(8,128)(2,1)S(1)} %lay.2.refs_0_, bf16[128,1024]{1,0:T(8,128)(2,1)S(1)} %collective-permute-done.17.refs_1_, ...), custom_call_target="tpu_custom_call" | custom-call | flops 2147483648 | bytes 7864320 | tf_op jit(solution)/shard_map/project/pallas_call | solution.py:378
  45.8 1.7 %collective-permute-start.31 = (bf16[528,256]{1,0:T(8,128)(2,1)S(1)}, bf16[528,256]{1,0:T(8,128)(2,1)S(1)}, u32[]{:S(2)}, u32[]{:S(2)}) collective-permute-start(bf16[528,256]{1,0:T(8,128)(2,1)S(1)} %get-tuple-element.144), channel_id=1, source_target_pairs={{0,24},{1,25},{2,26},{3,27},{4,28},{5,29},{6,30},{7,31},{8,16},{9,... | collective-permute-start | bytes 811016 | tf_op jit(solution)/shard_map/ppermute | solution.py:40
  47.5 2.8 %collective-permute-start.33 = (bf16[528,256]{1,0:T(8,128)(2,1)S(1)}, bf16[528,256]{1,0:T(8,128)(2,1)S(1)}, u32[]{:S(2)}, u32[]{:S(2)}) collective-permute-start(bf16[528,256]{1,0:T(8,128)(2,1)S(1)} %get-tuple-element.146), channel_id=1, source_target_pairs={{0,8},{1,9},{2,10},{3,11},{4,12},{5,13},{6,14},{7,15},{8,0},{9,1},... | collective-permute-start | bytes 811016 | tf_op jit(solution)/shard_map/ppermute | solution.py:40
  50.2 16.4 %conditional.2 = (f32[512,256]{1,0:T(8,128)S(1)}, bf16[528,256]{1,0:T(8,128)(2,1)}, bf16[528,256]{1,0:T(8,128)(2,1)}, bf16[528,256]{1,0:T(8,128)(2,1)}) conditional(s32[]{:T(128)} %convert_element_type.4, () %tuple.35, (bf16[128,1024]{1,0:T(8,128)(2,1)S(1)}, bf16[128,1024]{1,0:T(8,128)(2,1)}, bf16[2048,1024]{1,0:T(8,128)(2,1)}, s32[3]{0:T(128)S(1)}) %tuple.36), branch_computations={%region_0.1_spmd, %region_1.2_spmd} | conditional | flops 2149580800 | bytes 24641728 | solution.py:232
  50.8 1.0 collective-permute-start.5
  51.8 5.6 %collective-permute-done.4.refs_2_ = bf16[128,1024]{1,0:T(8,128)(2,1)S(1)} collective-permute-done((bf16[128,1024]{1,0:T(8,128)(2,1)S(1)}, bf16[128,1024]{1,0:T(8,128)(2,1)S(1)}, u32[]{:S(2)}, u32[]{:S(2)}) %collective-permute-start.4) | collective-permute-done | bytes 262176 | tf_op jit(solution)/shard_map/cond/branch_1_fun/ppermute | solution.py:40
  57.8 1.0 pad_maximum_fusion
  59.4 2.2 %fetch.2.refs_6_ = bf16[2048,1024]{1,0:T(8,128)(2,1)S(1)} custom-call(bf16[2048,1024]{1,0:T(8,128)(2,1)} %get-tuple-element.19.weight_ref), custom_call_target="tpu_custom_call" | custom-call | bytes 8388608 | tf_op jit(solution)/shard_map/cond/branch_1_fun/fetch/pallas_call | solution.py:265
  61.6 5.0 %project.2 = (f32[512,256]{1,0:T(8,128)S(1)}, bf16[528,256]{1,0:T(8,128)(2,1)}, bf16[528,256]{1,0:T(8,128)(2,1)}, bf16[528,256]{1,0:T(8,128)(2,1)}) custom-call(s32[3]{0:T(128)S(1)} %get-tuple-element.14.place_ref, bf16[128,1024]{1,0:T(8,128)(2,1)S(1)} %get-tuple-element.16.refs_0_, bf16[128,1024]{1,0:T(8,128)(2,1)} %get-tuple-element.17.refs_1_, ...), custom_call_target="tpu_custom_call" | custom-call | flops 2147483648 | bytes 7864320 | tf_op jit(solution)/shard_map/cond/branch_1_fun/project/pallas_call | solution.py:378
  66.9 1.8 %collective-permute-start.29 = (bf16[528,256]{1,0:T(8,128)(2,1)}, bf16[528,256]{1,0:T(8,128)(2,1)S(1)}, u32[]{:S(2)}, u32[]{:S(2)}) collective-permute-start(bf16[528,256]{1,0:T(8,128)(2,1)} %get-tuple-element.141), channel_id=1, source_target_pairs={{0,16},{1,17},{2,18},{3,19},{4,20},{5,21},{6,22},{7,23},{8,24},{9,... | collective-permute-start | bytes 811016 | tf_op jit(solution)/shard_map/ppermute | solution.py:40
  68.7 2.3 %collective-permute-start.30 = (bf16[528,256]{1,0:T(8,128)(2,1)}, bf16[528,256]{1,0:T(8,128)(2,1)S(1)}, u32[]{:S(2)}, u32[]{:S(2)}) collective-permute-start(bf16[528,256]{1,0:T(8,128)(2,1)} %get-tuple-element.142), channel_id=1, source_target_pairs={{0,24},{1,25},{2,26},{3,27},{4,28},{5,29},{6,30},{7,31},{8,16},{9,... | collective-permute-start | bytes 811016 | tf_op jit(solution)/shard_map/ppermute | solution.py:40
  71.0 3.4 %normalize.2 = (f32[512,256]{1,0:T(8,128)S(1)}, bf16[512,256]{1,0:T(8,128)(2,1)S(1)}, f32[1,256]{1,0:T(1,128)S(1)}, f32[256,512]{1,0:T(8,128)}, f32[256,512]{1,0:T(8,128)}) custom-call(s32[3]{0:T(128)S(1)} %pad_add_fusion.place_ref, f32[512,256]{1,0:T(8,128)S(1)} %get-tuple-element.143.refs_0_, bf16[528,256]{1,0:T(8,128)(2,1)S(1)} %collective-permute-done.31.refs_1_, ...), custom_call_target="tpu_custom_call" | custom-call | flops 134217728 | bytes 3145728 | tf_op jit(solution)/shard_map/normalize/pallas_call | solution.py:458
  74.4 13.8 %conditional.3 = ((f32[16,384]{1,0:T(8,128)S(1)}, bf16[64,128]{1,0:T(8,128)(2,1)S(1)}, bf16[64,128]{1,0:T(8,128)(2,1)S(1)}, bf16[64,128]{1,0:T(8,128)(2,1)S(1)})) conditional(s32[]{:T(128)} %convert_element_type.4, () %tuple.38, (f32[256,512]{1,0:T(8,128)}, s32[3]{0:T(128)S(1)}, f32[256,512]{1,0:T(8,128)}) %tuple.39), branch_computations={%region_2.3_spmd, %region_3.4_spmd} | conditional | bytes 2736296 | solution.py:232
  74.4 2.1 %collective-permute-done.met_ref = f32[256,512]{1,0:T(8,128)S(1)} collective-permute-done((f32[256,512]{1,0:T(8,128)}, f32[256,512]{1,0:T(8,128)S(1)}, u32[]{:S(2)}, u32[]{:S(2)}) %collective-permute-start) | collective-permute-done | bytes 524320 | tf_op jit(solution)/shard_map/cond/branch_1_fun/ppermute | solution.py:40
  76.5 1.3 halve.2
  77.9 1.5 %collective-permute-start.2 = (bf16[208,128]{1,0:T(8,128)(2,1)S(1)}, bf16[208,128]{1,0:T(8,128)(2,1)S(1)}, u32[]{:S(2)}, u32[]{:S(2)}) collective-permute-start(bf16[208,128]{1,0:T(8,128)(2,1)S(1)} %get-tuple-element.29), channel_id=1, source_target_pairs={{0,6},{1,7},{2,4},{3,5},{4,2},{5,3},{6,0},{7,1},{8,14},{9,15},{10,... | collective-permute-start | bytes 159752 | tf_op jit(solution)/shard_map/cond/branch_1_fun/ppermute | solution.py:40
  79.4 1.4 collective-permute-start.1
  80.7 2.5 %collective-permute-done.2.refs_3_ = bf16[208,128]{1,0:T(8,128)(2,1)S(1)} collective-permute-done((bf16[208,128]{1,0:T(8,128)(2,1)S(1)}, bf16[208,128]{1,0:T(8,128)(2,1)S(1)}, u32[]{:S(2)}, u32[]{:S(2)}) %collective-permute-start.2) | collective-permute-done | bytes 53280 | tf_op jit(solution)/shard_map/cond/branch_1_fun/ppermute | solution.py:40
  83.2 1.4 collective-permute-start.3
  84.6 2.8 %collective-permute-done.3.refs_2_ = bf16[208,128]{1,0:T(8,128)(2,1)S(1)} collective-permute-done((bf16[208,128]{1,0:T(8,128)(2,1)S(1)}, bf16[208,128]{1,0:T(8,128)(2,1)S(1)}, u32[]{:S(2)}, u32[]{:S(2)}) %collective-permute-start.3) | collective-permute-done | bytes 53280 | tf_op jit(solution)/shard_map/cond/branch_1_fun/ppermute | solution.py:40
  87.4 0.8 plane.1
  88.3 2.5 %collective-permute-start.35 = (bf16[64,128]{1,0:T(8,128)(2,1)S(1)}, bf16[64,128]{1,0:T(8,128)(2,1)S(1)}, u32[]{:S(2)}, u32[]{:S(2)}) collective-permute-start(bf16[64,128]{1,0:T(8,128)(2,1)S(1)} %get-tuple-element.151), channel_id=1, source_target_pairs={{0,16},{1,17},{2,18},{3,19},{4,20},{5,21},{6,22},{7,23},{8,24},{9,... | collective-permute-start | bytes 49160 | tf_op jit(solution)/shard_map/ppermute | solution.py:40
  90.8 1.8 %collective-permute-start.36 = (bf16[64,128]{1,0:T(8,128)(2,1)S(1)}, bf16[64,128]{1,0:T(8,128)(2,1)S(1)}, u32[]{:S(2)}, u32[]{:S(2)}) collective-permute-start(bf16[64,128]{1,0:T(8,128)(2,1)S(1)} %get-tuple-element.152), channel_id=1, source_target_pairs={{0,24},{1,25},{2,26},{3,27},{4,28},{5,29},{6,30},{7,31},{8,16},{9,... | collective-permute-start | bytes 49160 | tf_op jit(solution)/shard_map/ppermute | solution.py:40
  92.7 1.9 %collective-permute-done.35.refs_2_ = bf16[64,128]{1,0:T(8,128)(2,1)S(1)} collective-permute-done((bf16[64,128]{1,0:T(8,128)(2,1)S(1)}, bf16[64,128]{1,0:T(8,128)(2,1)S(1)}, u32[]{:S(2)}, u32[]{:S(2)}) %collective-permute-start.35) | collective-permute-done | bytes 16416 | tf_op jit(solution)/shard_map/ppermute | solution.py:40
  94.6 1.8 %collective-permute-done.36.refs_3_ = bf16[64,128]{1,0:T(8,128)(2,1)S(1)} collective-permute-done((bf16[64,128]{1,0:T(8,128)(2,1)S(1)}, bf16[64,128]{1,0:T(8,128)(2,1)S(1)}, u32[]{:S(2)}, u32[]{:S(2)}) %collective-permute-start.36) | collective-permute-done | bytes 16416 | tf_op jit(solution)/shard_map/ppermute | solution.py:40
  96.4 2.6 %normalize.3 = (f32[512,256]{1,0:T(8,128)S(1)}, bf16[512,256]{1,0:T(8,128)(2,1)S(1)}, f32[1,256]{1,0:T(1,128)S(1)}, f32[256,512]{1,0:T(8,128)S(1)}, f32[256,512]{1,0:T(8,128)S(1)}, /*index=5*/f32[1,256]{1,0:T(1,128)S(1)}) custom-call(s32[3]{0:T(128)S(1)} %pad_add_fusion.place_ref, f32[512,256]{1,0:T(8,128)S(1)} %get-tuple-element.153.refs_0_, ...), custom_call_target="tpu_custom_call" | custom-call | flops 134217728 | bytes 3145728 | tf_op jit(solution)/shard_map/normalize/pallas_call | solution.py:458
  99.1 1.9 %collective-permute-done.37.met_ref = f32[256,512]{1,0:T(8,128)S(1)} collective-permute-done((f32[256,512]{1,0:T(8,128)S(1)}, f32[256,512]{1,0:T(8,128)S(1)}, u32[]{:S(2)}, u32[]{:S(2)}) %collective-permute-start.37) | collective-permute-done | bytes 524320 | tf_op jit(solution)/shard_map/ppermute | solution.py:40
  101.0 0.8 halve.3
  101.8 1.2 collective-permute-start.38
  103.5 1.8 %collective-permute-start.40 = (bf16[208,128]{1,0:T(8,128)(2,1)S(1)}, bf16[208,128]{1,0:T(8,128)(2,1)S(1)}, u32[]{:S(2)}, u32[]{:S(2)}) collective-permute-start(bf16[208,128]{1,0:T(8,128)(2,1)S(1)} %get-tuple-element.163), channel_id=1, source_target_pairs={{0,6},{1,7},{2,4},{3,5},{4,2},{5,3},{6,0},{7,1},{8,14},{9,15},{10,... | collective-permute-start | bytes 159752 | tf_op jit(solution)/shard_map/ppermute | solution.py:40
  106.0 1.7 %collective-permute-done.39.refs_2_ = bf16[208,128]{1,0:T(8,128)(2,1)S(1)} collective-permute-done((bf16[208,128]{1,0:T(8,128)(2,1)S(1)}, bf16[208,128]{1,0:T(8,128)(2,1)S(1)}, u32[]{:S(2)}, u32[]{:S(2)}) %collective-permute-start.39) | collective-permute-done | bytes 53280 | tf_op jit(solution)/shard_map/ppermute | solution.py:40
  107.7 0.9 collective-permute-done.40.refs_3_
  108.5 0.8 code.1.refs_0_
  109.4 2.3 %collective-permute-start.43 = (bf16[256,128]{1,0:T(8,128)(2,1)S(1)}, bf16[256,128]{1,0:T(8,128)(2,1)S(1)}, u32[]{:S(2)}, u32[]{:S(2)}) collective-permute-start(bf16[256,128]{1,0:T(8,128)(2,1)S(1)} %code.1.refs_0_), channel_id=1, source_target_pairs={{0,24},{1,25},{2,26},{3,27},{4,28},{5,29},{6,30},{7,31},{8,16},{9,... | collective-permute-start | bytes 196616 | tf_op jit(solution)/shard_map/ppermute | solution.py:40
  111.7 2.2 %collective-permute-start.41 = (bf16[256,128]{1,0:T(8,128)(2,1)S(1)}, bf16[256,128]{1,0:T(8,128)(2,1)S(1)}, u32[]{:S(2)}, u32[]{:S(2)}) collective-permute-start(bf16[256,128]{1,0:T(8,128)(2,1)S(1)} %code.1.refs_0_), channel_id=1, source_target_pairs={{0,8},{1,9},{2,10},{3,11},{4,12},{5,13},{6,14},{7,15},{8,0},{9,1},... | collective-permute-start | bytes 196616 | tf_op jit(solution)/shard_map/ppermute | solution.py:40
  113.8 2.3 %collective-permute-done.43.refs_3_ = bf16[256,128]{1,0:T(8,128)(2,1)S(1)} collective-permute-done((bf16[256,128]{1,0:T(8,128)(2,1)S(1)}, bf16[256,128]{1,0:T(8,128)(2,1)S(1)}, u32[]{:S(2)}, u32[]{:S(2)}) %collective-permute-start.43) | collective-permute-done | bytes 65568 | tf_op jit(solution)/shard_map/ppermute | solution.py:40
  116.1 1.3 collective-permute-done.42.refs_2_
  117.4 1.0 finish.1.refs_0_
  118.4 1.5 %collective-permute-start.46 = (bf16[128,384]{1,0:T(8,128)(2,1)S(1)}, bf16[128,384]{1,0:T(8,128)(2,1)S(1)}, u32[]{:S(2)}, u32[]{:S(2)}) collective-permute-start(bf16[128,384]{1,0:T(8,128)(2,1)S(1)} %finish.1.refs_0_), channel_id=1, source_target_pairs={{0,6},{1,7},{2,4},{3,5},{4,2},{5,3},{6,0},{7,1},{8,14},{9,15},{10,... | collective-permute-start | bytes 294920 | tf_op jit(solution)/shard_map/ppermute | solution.py:40
  119.9 1.3 collective-permute-start.45
  122.0 2.1 %collective-permute-done.46.refs_3_ = bf16[128,384]{1,0:T(8,128)(2,1)S(1)} collective-permute-done((bf16[128,384]{1,0:T(8,128)(2,1)S(1)}, bf16[128,384]{1,0:T(8,128)(2,1)S(1)}, u32[]{:S(2)}, u32[]{:S(2)}) %collective-permute-start.46) | collective-permute-done | bytes 98336 | tf_op jit(solution)/shard_map/ppermute | solution.py:40
  124.0 1.0 collective-permute-done.45.refs_2_
  126.3 0.8 collective-permute-done.48.refs_5_
  127.1 2.0 %gradient.1 = (bf16[256,256]{1,0:T(8,128)(2,1)S(1)}, bf16[256,256]{1,0:T(8,128)(2,1)S(1)}, bf16[256,256]{1,0:T(8,128)(2,1)S(1)}, bf16[256,256]{1,0:T(8,128)(2,1)...) custom-call(s32[3]{0:T(128)S(1)} %pad_add_fusion.place_ref, bf16[128,384]{1,0:T(8,128)(2,1)S(1)} %finish.1.refs_0_, ...), custom_call_target="tpu_custom_call" | custom-call | tf_op jit(solution)/shard_map/gradient/pallas_call | solution.py:190
  129.1 1.8 %collective-permute-start.51 = (bf16[256,256]{1,0:T(8,128)(2,1)S(1)}, bf16[256,256]{1,0:T(8,128)(2,1)S(1)}, u32[]{:S(2)}, u32[]{:S(2)}) collective-permute-start(bf16[256,256]{1,0:T(8,128)(2,1)S(1)} %get-tuple-element.175), channel_id=1, source_target_pairs={{0,24},{1,25},{2,26},{3,27},{4,28},{5,29},{6,30},{7,31},{8,16},{9,... | collective-permute-start | bytes 393224 | tf_op jit(solution)/shard_map/ppermute | solution.py:40
  131.3 2.2 %collective-permute-start.53 = (bf16[256,256]{1,0:T(8,128)(2,1)S(1)}, bf16[256,256]{1,0:T(8,128)(2,1)S(1)}, u32[]{:S(2)}, u32[]{:S(2)}) collective-permute-start(bf16[256,256]{1,0:T(8,128)(2,1)S(1)} %get-tuple-element.177), channel_id=1, source_target_pairs={{0,8},{1,9},{2,10},{3,11},{4,12},{5,13},{6,14},{7,15},{8,0},{9,1},... | collective-permute-start | bytes 393224 | tf_op jit(solution)/shard_map/ppermute | solution.py:40
  133.5 2.1 %loss.1 = f32[1,1]{1,0:T(1,128)} custom-call(s32[3]{0:T(128)S(1)} %pad_add_fusion.place_ref, bf16[2,512,512]{2,1,0:T(8,128)(2,1)S(1)} %get-tuple-element.180.gram_ref, f32[1,1]{1,0:T(1,128)} %get-tuple-element.181.share_ref), custom_call_target="tpu_custom_call" | custom-call | tf_op jit(solution)/shard_map/loss/pallas_call | solution.py:190
  135.6 1.8 %collective-permute-done.51.refs_1_ = bf16[256,256]{1,0:T(8,128)(2,1)S(1)} collective-permute-done((bf16[256,256]{1,0:T(8,128)(2,1)S(1)}, bf16[256,256]{1,0:T(8,128)(2,1)S(1)}, u32[]{:S(2)}, u32[]{:S(2)}) %collective-permute-start.51) | collective-permute-done | bytes 131104 | tf_op jit(solution)/shard_map/ppermute | solution.py:40
  137.4 5.9 %collective-permute-done.52.refs_2_ = bf16[256,256]{1,0:T(8,128)(2,1)S(1)} collective-permute-done((bf16[256,256]{1,0:T(8,128)(2,1)S(1)}, bf16[256,256]{1,0:T(8,128)(2,1)S(1)}, u32[]{:S(2)}, u32[]{:S(2)}) %collective-permute-start.52) | collective-permute-done | bytes 131104 | tf_op jit(solution)/shard_map/ppermute | solution.py:40
  143.3 1.4 place.1
  (70 shorter events, 11.4 us)
Async XLA Ops:
  1.6 9.1 %collective-permute-start.10 = (bf16[32,1024]{1,0:T(8,128)(2,1)S(1)}, bf16[32,1024]{1,0:T(8,128)(2,1)S(1)}, u32[]{:S(2)}, u32[]{:S(2)}) collective-permute-start(bf16[32,1024]{1,0:T(8,128)(2,1)S(1)} %get-tuple-element.190), channel_id=1, source_target_pairs={{0,6},{1,7},{2,4},{3,5},{4,2},{5,3},{6,0},{7,1},{8,14},{9,15},{10,... | collective-permute-start | bytes 196616 | tf_op jit(solution)/shard_map/ppermute | solution.py:40
  5.6 5.2 %collective-permute-start.9 = (bf16[32,1024]{1,0:T(8,128)(2,1)S(1)}, bf16[32,1024]{1,0:T(8,128)(2,1)S(1)}, u32[]{:S(2)}, u32[]{:S(2)}) collective-permute-start(bf16[32,1024]{1,0:T(8,128)(2,1)S(1)} %get-tuple-element.191), channel_id=1, source_target_pairs={{0,4},{1,5},{2,6},{3,7},{4,0},{5,1},{6,2},{7,3},{8,12},{9,13},{10,... | collective-permute-start | bytes 196616 | tf_op jit(solution)/shard_map/ppermute | solution.py:40
  6.1 4.7 %collective-permute-start.8 = (bf16[32,1024]{1,0:T(8,128)(2,1)S(1)}, bf16[32,1024]{1,0:T(8,128)(2,1)S(1)}, u32[]{:S(2)}, u32[]{:S(2)}) collective-permute-start(bf16[32,1024]{1,0:T(8,128)(2,1)S(1)} %get-tuple-element.192), channel_id=1, source_target_pairs={{0,2},{1,3},{2,0},{3,1},{4,6},{5,7},{6,4},{7,5},{8,10},{9,11},{10,... | collective-permute-start | bytes 196616 | tf_op jit(solution)/shard_map/ppermute | solution.py:40
  7.2 8.9 %collective-permute-start.16 = (bf16[32,1024]{1,0:T(8,128)(2,1)S(1)}, bf16[32,1024]{1,0:T(8,128)(2,1)S(1)}, u32[]{:S(2)}, u32[]{:S(2)}) collective-permute-start(bf16[32,1024]{1,0:T(8,128)(2,1)S(1)} %get-tuple-element.186), channel_id=1, source_target_pairs={{0,6},{1,7},{2,4},{3,5},{4,2},{5,3},{6,0},{7,1},{8,14},{9,15},{10,... | collective-permute-start | bytes 196616 | tf_op jit(solution)/shard_map/ppermute | solution.py:40
  10.1 6.5 %collective-permute-start.15 = (bf16[32,1024]{1,0:T(8,128)(2,1)S(1)}, bf16[32,1024]{1,0:T(8,128)(2,1)S(1)}, u32[]{:S(2)}, u32[]{:S(2)}) collective-permute-start(bf16[32,1024]{1,0:T(8,128)(2,1)S(1)} %get-tuple-element.187), channel_id=1, source_target_pairs={{0,4},{1,5},{2,6},{3,7},{4,0},{5,1},{6,2},{7,3},{8,12},{9,13},{10,... | collective-permute-start | bytes 196616 | tf_op jit(solution)/shard_map/ppermute | solution.py:40
  10.7 5.9 %collective-permute-start.14 = (bf16[32,1024]{1,0:T(8,128)(2,1)S(1)}, bf16[32,1024]{1,0:T(8,128)(2,1)S(1)}, u32[]{:S(2)}, u32[]{:S(2)}) collective-permute-start(bf16[32,1024]{1,0:T(8,128)(2,1)S(1)} %get-tuple-element.188), channel_id=1, source_target_pairs={{0,2},{1,3},{2,0},{3,1},{4,6},{5,7},{6,4},{7,5},{8,10},{9,11},{10,... | collective-permute-start | bytes 196616 | tf_op jit(solution)/shard_map/ppermute | solution.py:40
  11.4 5.2 %collective-permute-start.11 = (bf16[32,1024]{1,0:T(8,128)(2,1)S(1)}, bf16[32,1024]{1,0:T(8,128)(2,1)S(1)}, u32[]{:S(2)}, u32[]{:S(2)}) collective-permute-start(bf16[32,1024]{1,0:T(8,128)(2,1)S(1)} %get-tuple-element.110), channel_id=1, source_target_pairs={{0,8},{1,9},{2,10},{3,11},{4,12},{5,13},{6,14},{7,15},{8,0},{9,1},... | collective-permute-start | bytes 196616 | tf_op jit(solution)/shard_map/ppermute | solution.py:40
  13.5 6.6 %collective-permute-start.12 = (bf16[32,1024]{1,0:T(8,128)(2,1)S(1)}, bf16[32,1024]{1,0:T(8,128)(2,1)S(1)}, u32[]{:S(2)}, u32[]{:S(2)}) collective-permute-start(bf16[32,1024]{1,0:T(8,128)(2,1)S(1)} %get-tuple-element.111), channel_id=1, source_target_pairs={{0,16},{1,17},{2,18},{3,19},{4,20},{5,21},{6,22},{7,23},{8,24},{9,... | collective-permute-start | bytes 196616 | tf_op jit(solution)/shard_map/ppermute | solution.py:40
  16.1 6.1 %collective-permute-start.13 = (bf16[32,1024]{1,0:T(8,128)(2,1)S(1)}, bf16[32,1024]{1,0:T(8,128)(2,1)S(1)}, u32[]{:S(2)}, u32[]{:S(2)}) collective-permute-start(bf16[32,1024]{1,0:T(8,128)(2,1)S(1)} %get-tuple-element.112), channel_id=1, source_target_pairs={{0,24},{1,25},{2,26},{3,27},{4,28},{5,29},{6,30},{7,31},{8,16},{9,... | collective-permute-start | bytes 196616 | tf_op jit(solution)/shard_map/ppermute | solution.py:40
  22.7 15.0 %collective-permute-start.19 = (bf16[128,1024]{1,0:T(8,128)(2,1)S(1)}, bf16[128,1024]{1,0:T(8,128)(2,1)S(1)}, u32[]{:S(2)}, u32[]{:S(2)}) collective-permute-start(bf16[128,1024]{1,0:T(8,128)(2,1)S(1)} %lay.2.refs_0_), channel_id=1, source_target_pairs={{0,6},{1,7},{2,4},{3,5},{4,2},{5,3},{6,0},{7,1},{8,14},{9,15},{10,... | collective-permute-start | bytes 786440 | tf_op jit(solution)/shard_map/ppermute | solution.py:40
  25.2 12.5 %collective-permute-start.18 = (bf16[128,1024]{1,0:T(8,128)(2,1)S(1)}, bf16[128,1024]{1,0:T(8,128)(2,1)S(1)}, u32[]{:S(2)}, u32[]{:S(2)}) collective-permute-start(bf16[128,1024]{1,0:T(8,128)(2,1)S(1)} %lay.2.refs_0_), channel_id=1, source_target_pairs={{0,4},{1,5},{2,6},{3,7},{4,0},{5,1},{6,2},{7,3},{8,12},{9,13},{10,... | collective-permute-start | bytes 786440 | tf_op jit(solution)/shard_map/ppermute | solution.py:40
  25.7 12.0 %collective-permute-start.17 = (bf16[128,1024]{1,0:T(8,128)(2,1)S(1)}, bf16[128,1024]{1,0:T(8,128)(2,1)S(1)}, u32[]{:S(2)}, u32[]{:S(2)}) collective-permute-start(bf16[128,1024]{1,0:T(8,128)(2,1)S(1)} %lay.2.refs_0_), channel_id=1, source_target_pairs={{0,2},{1,3},{2,0},{3,1},{4,6},{5,7},{6,4},{7,5},{8,10},{9,11},{10,... | collective-permute-start | bytes 786440 | tf_op jit(solution)/shard_map/ppermute | solution.py:40
  26.3 6.2 %collective-permute-start.22 = (bf16[32,1024]{1,0:T(8,128)(2,1)S(1)}, bf16[32,1024]{1,0:T(8,128)(2,1)S(1)}, u32[]{:S(2)}, u32[]{:S(2)}) collective-permute-start(bf16[32,1024]{1,0:T(8,128)(2,1)S(1)} %get-tuple-element.182), channel_id=1, source_target_pairs={{0,24},{1,25},{2,26},{3,27},{4,28},{5,29},{6,30},{7,31},{8,16},{9,... | collective-permute-start | bytes 196616 | tf_op jit(solution)/shard_map/ppermute | solution.py:40
  27.1 7.6 %collective-permute-start.20 = (bf16[32,1024]{1,0:T(8,128)(2,1)S(1)}, bf16[32,1024]{1,0:T(8,128)(2,1)S(1)}, u32[]{:S(2)}, u32[]{:S(2)}) collective-permute-start(bf16[32,1024]{1,0:T(8,128)(2,1)S(1)} %get-tuple-element.183), channel_id=1, source_target_pairs={{0,8},{1,9},{2,10},{3,11},{4,12},{5,13},{6,14},{7,15},{8,0},{9,1},... | collective-permute-start | bytes 196616 | tf_op jit(solution)/shard_map/ppermute | solution.py:40
  32.5 5.2 %collective-permute-start.21 = (bf16[32,1024]{1,0:T(8,128)(2,1)S(1)}, bf16[32,1024]{1,0:T(8,128)(2,1)S(1)}, u32[]{:S(2)}, u32[]{:S(2)}) collective-permute-start(bf16[32,1024]{1,0:T(8,128)(2,1)S(1)} %get-tuple-element.184), channel_id=1, source_target_pairs={{0,16},{1,17},{2,18},{3,19},{4,20},{5,21},{6,22},{7,23},{8,24},{9,... | collective-permute-start | bytes 196616 | tf_op jit(solution)/shard_map/ppermute | solution.py:40
  37.7 4.2 %collective-permute-start.23 = (bf16[128,1024]{1,0:T(8,128)(2,1)S(1)}, bf16[128,1024]{1,0:T(8,128)(2,1)S(1)}, u32[]{:S(2)}, u32[]{:S(2)}) collective-permute-start(bf16[128,1024]{1,0:T(8,128)(2,1)S(1)} %lay.2.refs_0_), channel_id=1, source_target_pairs={{0,1},{1,0},{2,3},{3,2},{4,5},{5,4},{6,7},{7,6},{8,9},{9,8},{10,11... | collective-permute-start | bytes 786440 | tf_op jit(solution)/shard_map/ppermute | solution.py:40
  37.8 4.1 %collective-permute-start.24 = (bf16[128,1024]{1,0:T(8,128)(2,1)S(1)}, bf16[128,1024]{1,0:T(8,128)(2,1)S(1)}, u32[]{:S(2)}, u32[]{:S(2)}) collective-permute-start(bf16[128,1024]{1,0:T(8,128)(2,1)S(1)} %collective-permute-done.17.refs_1_), channel_id=1, source_target_pairs={{0,1},{1,0},{2,3},{3,2},{4,5},{5,4},{6,7},{7,6},{8,9},{9,8},{10,11... | collective-permute-start | bytes 786440 | tf_op jit(solution)/shard_map/ppermute | solution.py:40
  38.3 3.6 %collective-permute-start.25 = (bf16[128,1024]{1,0:T(8,128)(2,1)S(1)}, bf16[128,1024]{1,0:T(8,128)(2,1)S(1)}, u32[]{:S(2)}, u32[]{:S(2)}) collective-permute-start(bf16[128,1024]{1,0:T(8,128)(2,1)S(1)} %collective-permute-done.18.refs_2_), channel_id=1, source_target_pairs={{0,1},{1,0},{2,3},{3,2},{4,5},{5,4},{6,7},{7,6},{8,9},{9,8},{10,11... | collective-permute-start | bytes 786440 | tf_op jit(solution)/shard_map/ppermute | solution.py:40
  38.3 3.5 %collective-permute-start.26 = (bf16[128,1024]{1,0:T(8,128)(2,1)S(1)}, bf16[128,1024]{1,0:T(8,128)(2,1)S(1)}, u32[]{:S(2)}, u32[]{:S(2)}) collective-permute-start(bf16[128,1024]{1,0:T(8,128)(2,1)S(1)} %collective-permute-done.19.refs_3_), channel_id=1, source_target_pairs={{0,1},{1,0},{2,3},{3,2},{4,5},{5,4},{6,7},{7,6},{8,9},{9,8},{10,11... | collective-permute-start | bytes 786440 | tf_op jit(solution)/shard_map/ppermute | solution.py:40
  39.3 10.9 %collective-permute-start.27 = (bf16[128,1024]{1,0:T(8,128)(2,1)S(1)}, bf16[128,1024]{1,0:T(8,128)(2,1)}, u32[]{:S(2)}, u32[]{:S(2)}) collective-permute-start(bf16[128,1024]{1,0:T(8,128)(2,1)S(1)} %lay.3), channel_id=1, source_target_pairs={{0,6},{1,7},{2,4},{3,5},{4,2},{5,3},{6,0},{7,1},{8,14},{9,15},{10,... | collective-permute-start | bytes 786440 | tf_op jit(solution)/shard_map/ppermute | solution.py:40
  45.8 23.0 %collective-permute-start.31 = (bf16[528,256]{1,0:T(8,128)(2,1)S(1)}, bf16[528,256]{1,0:T(8,128)(2,1)S(1)}, u32[]{:S(2)}, u32[]{:S(2)}) collective-permute-start(bf16[528,256]{1,0:T(8,128)(2,1)S(1)} %get-tuple-element.144), channel_id=1, source_target_pairs={{0,24},{1,25},{2,26},{3,27},{4,28},{5,29},{6,30},{7,31},{8,16},{9,... | collective-permute-start | bytes 811016 | tf_op jit(solution)/shard_map/ppermute | solution.py:40
  47.4 23.6 %collective-permute-start.32 = (bf16[528,256]{1,0:T(8,128)(2,1)S(1)}, bf16[528,256]{1,0:T(8,128)(2,1)S(1)}, u32[]{:S(2)}, u32[]{:S(2)}) collective-permute-start(bf16[528,256]{1,0:T(8,128)(2,1)S(1)} %get-tuple-element.145), channel_id=1, source_target_pairs={{0,16},{1,17},{2,18},{3,19},{4,20},{5,21},{6,22},{7,23},{8,24},{9,... | collective-permute-start | bytes 811016 | tf_op jit(solution)/shard_map/ppermute | solution.py:40
  47.5 23.6 %collective-permute-start.33 = (bf16[528,256]{1,0:T(8,128)(2,1)S(1)}, bf16[528,256]{1,0:T(8,128)(2,1)S(1)}, u32[]{:S(2)}, u32[]{:S(2)}) collective-permute-start(bf16[528,256]{1,0:T(8,128)(2,1)S(1)} %get-tuple-element.146), channel_id=1, source_target_pairs={{0,8},{1,9},{2,10},{3,11},{4,12},{5,13},{6,14},{7,15},{8,0},{9,1},... | collective-permute-start | bytes 811016 | tf_op jit(solution)/shard_map/ppermute | solution.py:40
  50.2 7.2 %collective-permute-start.4 = (bf16[128,1024]{1,0:T(8,128)(2,1)S(1)}, bf16[128,1024]{1,0:T(8,128)(2,1)S(1)}, u32[]{:S(2)}, u32[]{:S(2)}) collective-permute-start(bf16[128,1024]{1,0:T(8,128)(2,1)S(1)} %get-tuple-element.16.refs_0_), channel_id=1, source_target_pairs={{0,2},{1,3},{2,0},{3,1},{4,6},{5,7},{6,4},{7,5},{8,10},{9,11},{10,... | collective-permute-start | bytes 786440 | tf_op jit(solution)/shard_map/cond/branch_1_fun/ppermute | solution.py:40
  50.8 6.9 %collective-permute-start.5 = (bf16[128,1024]{1,0:T(8,128)(2,1)S(1)}, bf16[128,1024]{1,0:T(8,128)(2,1)S(1)}, u32[]{:S(2)}, u32[]{:S(2)}) collective-permute-start(bf16[128,1024]{1,0:T(8,128)(2,1)S(1)} %get-tuple-element.16.refs_0_), channel_id=1, source_target_pairs={{0,4},{1,5},{2,6},{3,7},{4,0},{5,1},{6,2},{7,3},{8,12},{9,13},{10,... | collective-permute-start | bytes 786440 | tf_op jit(solution)/shard_map/cond/branch_1_fun/ppermute | solution.py:40
  57.7 3.9 %collective-permute-start.7 = (bf16[256,1024]{1,0:T(8,128)(2,1)S(1)}, bf16[256,1024]{1,0:T(8,128)(2,1)S(1)}, u32[]{:S(2)}, u32[]{:S(2)}) collective-permute-start(bf16[256,1024]{1,0:T(8,128)(2,1)S(1)} %pad_maximum_fusion.1), channel_id=1, source_target_pairs={{0,1},{1,0},{2,3},{3,2},{4,5},{5,4},{6,7},{7,6},{8,9},{9,8},{10,11... | collective-permute-start | bytes 1572872 | tf_op jit(solution)/shard_map/cond/branch_1_fun/ppermute | solution.py:40
  58.8 2.8 %collective-permute-start.6 = (bf16[256,1024]{1,0:T(8,128)(2,1)S(1)}, bf16[256,1024]{1,0:T(8,128)(2,1)S(1)}, u32[]{:S(2)}, u32[]{:S(2)}) collective-permute-start(bf16[256,1024]{1,0:T(8,128)(2,1)S(1)} %pad_maximum_fusion), channel_id=1, source_target_pairs={{0,1},{1,0},{2,3},{3,2},{4,5},{5,4},{6,7},{7,6},{8,9},{9,8},{10,11... | collective-permute-start | bytes 1572872 | tf_op jit(solution)/shard_map/cond/branch_1_fun/ppermute | solution.py:40
  66.6 24.2 %collective-permute-start.28 = (bf16[528,256]{1,0:T(8,128)(2,1)}, bf16[528,256]{1,0:T(8,128)(2,1)S(1)}, u32[]{:S(2)}, u32[]{:S(2)}) collective-permute-start(bf16[528,256]{1,0:T(8,128)(2,1)} %get-tuple-element.140), channel_id=1, source_target_pairs={{0,8},{1,9},{2,10},{3,11},{4,12},{5,13},{6,14},{7,15},{8,0},{9,1},... | collective-permute-start | bytes 811016 | tf_op jit(solution)/shard_map/ppermute | solution.py:40
  66.9 25.8 %collective-permute-start.29 = (bf16[528,256]{1,0:T(8,128)(2,1)}, bf16[528,256]{1,0:T(8,128)(2,1)S(1)}, u32[]{:S(2)}, u32[]{:S(2)}) collective-permute-start(bf16[528,256]{1,0:T(8,128)(2,1)} %get-tuple-element.141), channel_id=1, source_target_pairs={{0,16},{1,17},{2,18},{3,19},{4,20},{5,21},{6,22},{7,23},{8,24},{9,... | collective-permute-start | bytes 811016 | tf_op jit(solution)/shard_map/ppermute | solution.py:40
  68.7 23.9 %collective-permute-start.30 = (bf16[528,256]{1,0:T(8,128)(2,1)}, bf16[528,256]{1,0:T(8,128)(2,1)S(1)}, u32[]{:S(2)}, u32[]{:S(2)}) collective-permute-start(bf16[528,256]{1,0:T(8,128)(2,1)} %get-tuple-element.142), channel_id=1, source_target_pairs={{0,24},{1,25},{2,26},{3,27},{4,28},{5,29},{6,30},{7,31},{8,16},{9,... | collective-permute-start | bytes 811016 | tf_op jit(solution)/shard_map/ppermute | solution.py:40
  74.4 2.1 %collective-permute-start = (f32[256,512]{1,0:T(8,128)}, f32[256,512]{1,0:T(8,128)S(1)}, u32[]{:S(2)}, u32[]{:S(2)}) collective-permute-start(f32[256,512]{1,0:T(8,128)} %get-tuple-element.26), channel_id=1, source_target_pairs={{0,1},{1,0},{2,3},{3,2},{4,5},{5,4},{6,7},{7,6},{8,9},{9,8},{10,11... | collective-permute-start | bytes 1572872 | tf_op jit(solution)/shard_map/cond/branch_1_fun/ppermute | solution.py:40
  77.9 5.4 %collective-permute-start.2 = (bf16[208,128]{1,0:T(8,128)(2,1)S(1)}, bf16[208,128]{1,0:T(8,128)(2,1)S(1)}, u32[]{:S(2)}, u32[]{:S(2)}) collective-permute-start(bf16[208,128]{1,0:T(8,128)(2,1)S(1)} %get-tuple-element.29), channel_id=1, source_target_pairs={{0,6},{1,7},{2,4},{3,5},{4,2},{5,3},{6,0},{7,1},{8,14},{9,15},{10,... | collective-permute-start | bytes 159752 | tf_op jit(solution)/shard_map/cond/branch_1_fun/ppermute | solution.py:40
  79.4 5.3 %collective-permute-start.1 = (bf16[208,128]{1,0:T(8,128)(2,1)S(1)}, bf16[208,128]{1,0:T(8,128)(2,1)S(1)}, u32[]{:S(2)}, u32[]{:S(2)}) collective-permute-start(bf16[208,128]{1,0:T(8,128)(2,1)S(1)} %get-tuple-element.28), channel_id=1, source_target_pairs={{0,2},{1,3},{2,0},{3,1},{4,6},{5,7},{6,4},{7,5},{8,10},{9,11},{10,... | collective-permute-start | bytes 159752 | tf_op jit(solution)/shard_map/cond/branch_1_fun/ppermute | solution.py:40
  83.2 4.1 %collective-permute-start.3 = (bf16[208,128]{1,0:T(8,128)(2,1)S(1)}, bf16[208,128]{1,0:T(8,128)(2,1)S(1)}, u32[]{:S(2)}, u32[]{:S(2)}) collective-permute-start(bf16[208,128]{1,0:T(8,128)(2,1)S(1)} %get-tuple-element.31), channel_id=1, source_target_pairs={{0,4},{1,5},{2,6},{3,7},{4,0},{5,1},{6,2},{7,3},{8,12},{9,13},{10,... | collective-permute-start | bytes 159752 | tf_op jit(solution)/shard_map/cond/branch_1_fun/ppermute | solution.py:40
  88.2 4.5 %collective-permute-start.34 = (bf16[64,128]{1,0:T(8,128)(2,1)S(1)}, bf16[64,128]{1,0:T(8,128)(2,1)S(1)}, u32[]{:S(2)}, u32[]{:S(2)}) collective-permute-start(bf16[64,128]{1,0:T(8,128)(2,1)S(1)} %get-tuple-element.150), channel_id=1, source_target_pairs={{0,8},{1,9},{2,10},{3,11},{4,12},{5,13},{6,14},{7,15},{8,0},{9,1},... | collective-permute-start | bytes 49160 | tf_op jit(solution)/shard_map/ppermute | solution.py:40
  88.3 6.3 %collective-permute-start.35 = (bf16[64,128]{1,0:T(8,128)(2,1)S(1)}, bf16[64,128]{1,0:T(8,128)(2,1)S(1)}, u32[]{:S(2)}, u32[]{:S(2)}) collective-permute-start(bf16[64,128]{1,0:T(8,128)(2,1)S(1)} %get-tuple-element.151), channel_id=1, source_target_pairs={{0,16},{1,17},{2,18},{3,19},{4,20},{5,21},{6,22},{7,23},{8,24},{9,... | collective-permute-start | bytes 49160 | tf_op jit(solution)/shard_map/ppermute | solution.py:40
  90.8 5.5 %collective-permute-start.36 = (bf16[64,128]{1,0:T(8,128)(2,1)S(1)}, bf16[64,128]{1,0:T(8,128)(2,1)S(1)}, u32[]{:S(2)}, u32[]{:S(2)}) collective-permute-start(bf16[64,128]{1,0:T(8,128)(2,1)S(1)} %get-tuple-element.152), channel_id=1, source_target_pairs={{0,24},{1,25},{2,26},{3,27},{4,28},{5,29},{6,30},{7,31},{8,16},{9,... | collective-permute-start | bytes 49160 | tf_op jit(solution)/shard_map/ppermute | solution.py:40
  99.0 2.0 %collective-permute-start.37 = (f32[256,512]{1,0:T(8,128)S(1)}, f32[256,512]{1,0:T(8,128)S(1)}, u32[]{:S(2)}, u32[]{:S(2)}) collective-permute-start(f32[256,512]{1,0:T(8,128)S(1)} %get-tuple-element.159), channel_id=1, source_target_pairs={{0,1},{1,0},{2,3},{3,2},{4,5},{5,4},{6,7},{7,6},{8,9},{9,8},{10,11... | collective-permute-start | bytes 1572872 | tf_op jit(solution)/shard_map/ppermute | solution.py:40
  101.8 4.2 %collective-permute-start.38 = (bf16[208,128]{1,0:T(8,128)(2,1)S(1)}, bf16[208,128]{1,0:T(8,128)(2,1)S(1)}, u32[]{:S(2)}, u32[]{:S(2)}) collective-permute-start(bf16[208,128]{1,0:T(8,128)(2,1)S(1)} %get-tuple-element.161), channel_id=1, source_target_pairs={{0,2},{1,3},{2,0},{3,1},{4,6},{5,7},{6,4},{7,5},{8,10},{9,11},{10,... | collective-permute-start | bytes 159752 | tf_op jit(solution)/shard_map/ppermute | solution.py:40
  103.0 4.7 %collective-permute-start.39 = (bf16[208,128]{1,0:T(8,128)(2,1)S(1)}, bf16[208,128]{1,0:T(8,128)(2,1)S(1)}, u32[]{:S(2)}, u32[]{:S(2)}) collective-permute-start(bf16[208,128]{1,0:T(8,128)(2,1)S(1)} %get-tuple-element.162), channel_id=1, source_target_pairs={{0,4},{1,5},{2,6},{3,7},{4,0},{5,1},{6,2},{7,3},{8,12},{9,13},{10,... | collective-permute-start | bytes 159752 | tf_op jit(solution)/shard_map/ppermute | solution.py:40
  103.5 5.0 %collective-permute-start.40 = (bf16[208,128]{1,0:T(8,128)(2,1)S(1)}, bf16[208,128]{1,0:T(8,128)(2,1)S(1)}, u32[]{:S(2)}, u32[]{:S(2)}) collective-permute-start(bf16[208,128]{1,0:T(8,128)(2,1)S(1)} %get-tuple-element.163), channel_id=1, source_target_pairs={{0,6},{1,7},{2,4},{3,5},{4,2},{5,3},{6,0},{7,1},{8,14},{9,15},{10,... | collective-permute-start | bytes 159752 | tf_op jit(solution)/shard_map/ppermute | solution.py:40
  109.4 6.7 %collective-permute-start.43 = (bf16[256,128]{1,0:T(8,128)(2,1)S(1)}, bf16[256,128]{1,0:T(8,128)(2,1)S(1)}, u32[]{:S(2)}, u32[]{:S(2)}) collective-permute-start(bf16[256,128]{1,0:T(8,128)(2,1)S(1)} %code.1.refs_0_), channel_id=1, source_target_pairs={{0,24},{1,25},{2,26},{3,27},{4,28},{5,29},{6,30},{7,31},{8,16},{9,... | collective-permute-start | bytes 196616 | tf_op jit(solution)/shard_map/ppermute | solution.py:40
  111.7 5.7 %collective-permute-start.42 = (bf16[256,128]{1,0:T(8,128)(2,1)S(1)}, bf16[256,128]{1,0:T(8,128)(2,1)S(1)}, u32[]{:S(2)}, u32[]{:S(2)}) collective-permute-start(bf16[256,128]{1,0:T(8,128)(2,1)S(1)} %code.1.refs_0_), channel_id=1, source_target_pairs={{0,16},{1,17},{2,18},{3,19},{4,20},{5,21},{6,22},{7,23},{8,24},{9,... | collective-permute-start | bytes 196616 | tf_op jit(solution)/shard_map/ppermute | solution.py:40
  111.7 5.7 %collective-permute-start.41 = (bf16[256,128]{1,0:T(8,128)(2,1)S(1)}, bf16[256,128]{1,0:T(8,128)(2,1)S(1)}, u32[]{:S(2)}, u32[]{:S(2)}) collective-permute-start(bf16[256,128]{1,0:T(8,128)(2,1)S(1)} %code.1.refs_0_), channel_id=1, source_target_pairs={{0,8},{1,9},{2,10},{3,11},{4,12},{5,13},{6,14},{7,15},{8,0},{9,1},... | collective-permute-start | bytes 196616 | tf_op jit(solution)/shard_map/ppermute | solution.py:40
  118.4 5.6 %collective-permute-start.46 = (bf16[128,384]{1,0:T(8,128)(2,1)S(1)}, bf16[128,384]{1,0:T(8,128)(2,1)S(1)}, u32[]{:S(2)}, u32[]{:S(2)}) collective-permute-start(bf16[128,384]{1,0:T(8,128)(2,1)S(1)} %finish.1.refs_0_), channel_id=1, source_target_pairs={{0,6},{1,7},{2,4},{3,5},{4,2},{5,3},{6,0},{7,1},{8,14},{9,15},{10,... | collective-permute-start | bytes 294920 | tf_op jit(solution)/shard_map/ppermute | solution.py:40
  119.9 5.1 %collective-permute-start.45 = (bf16[128,384]{1,0:T(8,128)(2,1)S(1)}, bf16[128,384]{1,0:T(8,128)(2,1)S(1)}, u32[]{:S(2)}, u32[]{:S(2)}) collective-permute-start(bf16[128,384]{1,0:T(8,128)(2,1)S(1)} %finish.1.refs_0_), channel_id=1, source_target_pairs={{0,4},{1,5},{2,6},{3,7},{4,0},{5,1},{6,2},{7,3},{8,12},{9,13},{10,... | collective-permute-start | bytes 294920 | tf_op jit(solution)/shard_map/ppermute | solution.py:40
  121.2 4.6 %collective-permute-start.44 = (bf16[128,384]{1,0:T(8,128)(2,1)S(1)}, bf16[128,384]{1,0:T(8,128)(2,1)S(1)}, u32[]{:S(2)}, u32[]{:S(2)}) collective-permute-start(bf16[128,384]{1,0:T(8,128)(2,1)S(1)} %finish.1.refs_0_), channel_id=1, source_target_pairs={{0,2},{1,3},{2,0},{3,1},{4,6},{5,7},{6,4},{7,5},{8,10},{9,11},{10,... | collective-permute-start | bytes 294920 | tf_op jit(solution)/shard_map/ppermute | solution.py:40
  122.0 3.9 %collective-permute-start.47 = (bf16[128,384]{1,0:T(8,128)(2,1)S(1)}, bf16[128,384]{1,0:T(8,128)(2,1)S(1)}, u32[]{:S(2)}, u32[]{:S(2)}) collective-permute-start(bf16[128,384]{1,0:T(8,128)(2,1)S(1)} %finish.1.refs_0_), channel_id=1, source_target_pairs={{0,1},{1,0},{2,3},{3,2},{4,5},{5,4},{6,7},{7,6},{8,9},{9,8},{10,11... | collective-permute-start | bytes 294920 | tf_op jit(solution)/shard_map/ppermute | solution.py:40
  124.0 1.8 %collective-permute-start.50 = (bf16[128,384]{1,0:T(8,128)(2,1)S(1)}, bf16[128,384]{1,0:T(8,128)(2,1)S(1)}, u32[]{:S(2)}, u32[]{:S(2)}) collective-permute-start(bf16[128,384]{1,0:T(8,128)(2,1)S(1)} %collective-permute-done.46.refs_3_), channel_id=1, source_target_pairs={{0,1},{1,0},{2,3},{3,2},{4,5},{5,4},{6,7},{7,6},{8,9},{9,8},{10,11... | collective-permute-start | bytes 294920 | tf_op jit(solution)/shard_map/ppermute | solution.py:40
  125.0 1.3 collective-permute-start.49
  125.8 1.3 collective-permute-start.48
  129.1 8.3 %collective-permute-start.51 = (bf16[256,256]{1,0:T(8,128)(2,1)S(1)}, bf16[256,256]{1,0:T(8,128)(2,1)S(1)}, u32[]{:S(2)}, u32[]{:S(2)}) collective-permute-start(bf16[256,256]{1,0:T(8,128)(2,1)S(1)} %get-tuple-element.175), channel_id=1, source_target_pairs={{0,24},{1,25},{2,26},{3,27},{4,28},{5,29},{6,30},{7,31},{8,16},{9,... | collective-permute-start | bytes 393224 | tf_op jit(solution)/shard_map/ppermute | solution.py:40
  131.0 12.3 %collective-permute-start.52 = (bf16[256,256]{1,0:T(8,128)(2,1)S(1)}, bf16[256,256]{1,0:T(8,128)(2,1)S(1)}, u32[]{:S(2)}, u32[]{:S(2)}) collective-permute-start(bf16[256,256]{1,0:T(8,128)(2,1)S(1)} %get-tuple-element.176), channel_id=1, source_target_pairs={{0,16},{1,17},{2,18},{3,19},{4,20},{5,21},{6,22},{7,23},{8,24},{9,... | collective-permute-start | bytes 393224 | tf_op jit(solution)/shard_map/ppermute | solution.py:40
  131.3 12.0 %collective-permute-start.53 = (bf16[256,256]{1,0:T(8,128)(2,1)S(1)}, bf16[256,256]{1,0:T(8,128)(2,1)S(1)}, u32[]{:S(2)}, u32[]{:S(2)}) collective-permute-start(bf16[256,256]{1,0:T(8,128)(2,1)S(1)} %get-tuple-element.177), channel_id=1, source_target_pairs={{0,8},{1,9},{2,10},{3,11},{4,12},{5,13},{6,14},{7,15},{8,0},{9,1},... | collective-permute-start | bytes 393224 | tf_op jit(solution)/shard_map/ppermute | solution.py:40

commit v17 on v15

--- a/solution.py
+++ b/solution.py
@@ -470,12 +470,12 @@
     )(place_array, *args)
 
 
-def gradient_kernel(place_ref, *refs, n, k):
+def gradient_kernel(place_ref, *refs, n, k, which):
     grams, refs = refs[: n * k], refs[n * k :]
-    packed, norms, scales, coeff_ref, refs = refs[0:2], refs[2:4], refs[4:6], refs[6], refs[7:]
+    packed_ref, norm_ref, other_ref, scale_ref, coeff_ref, refs = *refs[:5], refs[5:]
     outs = [refs[0], *refs[n - 1 : 0 : -1]]
-    share_ref, gram_ref, whole_ref = refs[n:]
-    batch, columns = norms[0].shape
+    gram_ref, share_ref, whole_ref = refs[n:]
+    batch, columns = norm_ref.shape
     height = grams[0].shape[0] // 2
     width = batch // BLOCKS
     for i in range(k):
@@ -485,56 +485,55 @@
             block = block // (2 * n // BLOCKS)
             for j in range(KEPT):
                 to = pl.ds(pl.multiple_of(lax.rem(block + j, BLOCKS) * width, width), width)
-                for view in range(2):
-                    gram_ref[view, at, to] = grams[i * n + step][
-                        view * height : (view + 1) * height, j * width : (j + 1) * width
-                    ]
+                gram_ref[at, to] = grams[i * n + step][
+                    which * height : (which + 1) * height, j * width : (j + 1) * width
+                ]
     blocks = [slice(i * width, (i + 1) * width) for i in range(BLOCKS)]
-    for view in range(2):
-        for i in range(BLOCKS):
-            other = gram_ref[view, blocks[i - 1], blocks[i]].astype(F32).T
-            gram_ref[view, blocks[i], blocks[i - 1]] = other.astype(BF16)
-    tail = gram_ref[1, blocks[3], blocks[1]].astype(F32)
-    row = lax.broadcasted_iota(jnp.int32, tail.shape, 0)
-    column = lax.broadcasted_iota(jnp.int32, tail.shape, 1)
-    taken = (row == width - 1) & (column < 3)
-    mirror = gram_ref[1, blocks[1], blocks[3]].astype(F32).T
-    share = jnp.sum(jnp.where(taken, tail, 0.0), keepdims=True)
-    gram_ref[1, blocks[3], blocks[1]] = jnp.where(taken, mirror, tail).astype(BF16)
+    for i in range(BLOCKS):
+        other = gram_ref[blocks[i - 1], blocks[i]].astype(F32).T
+        gram_ref[blocks[i], blocks[i - 1]] = other.astype(BF16)
+    share = jnp.zeros((1, 1), F32)
+    if which == 1:
+        tail = gram_ref[blocks[3], blocks[1]].astype(F32)
+        row = lax.broadcasted_iota(jnp.int32, tail.shape, 0)
+        column = lax.broadcasted_iota(jnp.int32, tail.shape, 1)
+        taken = (row == width - 1) & (column < 3)
+        mirror = gram_ref[blocks[1], blocks[3]].astype(F32).T
+        share = jnp.sum(jnp.where(taken, tail, 0.0), keepdims=True)
+        gram_ref[blocks[3], blocks[1]] = jnp.where(taken, mirror, tail).astype(BF16)
+    share_ref[...] = share
     factor = 2.0 * off_weight / batch
     rows = batch // n
-    for view in (1, 0):
-        norm = norms[view][...]
-        grad = (
-            factor * jnp.dot(gram_ref[1 - view], packed[view][...], preferred_element_type=F32)
-            + coeff_ref[...] * norms[1 - view][...]
-        )
-        first = jnp.sum(grad, 0, keepdims=True) / batch
-        second = jnp.sum(grad * norm, 0, keepdims=True) / batch
-        whole_ref[view] = (scales[view][...] * (grad - first - norm * second)).astype(BF16)
-        for step in range(n):
-            at = pl.multiple_of((place_ref[0] ^ step) * rows, rows)
-            outs[step][view * rows : (view + 1) * rows, :] = whole_ref[view, pl.ds(at, rows), :]
-    share_ref[...] = share
-
-
-def loss_kernel(place_ref, gram_ref, share_ref, loss_ref):
-    batch = gram_ref.shape[1]
-    frob = jnp.sum(gram_ref[0].astype(F32) * gram_ref[1].astype(F32), keepdims=True)
+    norm = norm_ref[...]
+    grad = (
+        factor * jnp.dot(gram_ref[...], packed_ref[...], preferred_element_type=F32)
+        + coeff_ref[...] * other_ref[...]
+    )
+    first = jnp.sum(grad, 0, keepdims=True) / batch
+    second = jnp.sum(grad * norm, 0, keepdims=True) / batch
+    whole_ref[...] = (scale_ref[...] * (grad - first - norm * second)).astype(BF16)
+    for step in range(n):
+        at = pl.multiple_of((place_ref[0] ^ step) * rows, rows)
+        outs[step][...] = whole_ref[pl.ds(at, rows), :]
+
+
+def loss_kernel(place_ref, first_ref, second_ref, share_ref, loss_ref):
+    batch = first_ref.shape[1]
+    frob = jnp.sum(first_ref[...].astype(F32) * second_ref[...].astype(F32), keepdims=True)
     loss_ref[...] = (share_ref[...] + off_weight * (frob / (batch * batch))) / D
 
 
-def gradient(place, place_array, grams, packed, norms, scales, coeff):
-    batch, columns = norms[0].shape
-    return local(
-        functools.partial(gradient_kernel, n=place.n, k=place.k),
+def gradient(place, place_array, grams, which, packed, norm, other, scale, coeff):
+    batch, columns = norm.shape
+    first, *others, gram, share = local(
+        functools.partial(gradient_kernel, n=place.n, k=place.k, which=which),
         place_array,
-        (*grams, *packed, *norms, *scales, coeff),
-        [((2 * batch // place.n, columns), BF16)] * place.n
-        + [((1, 1), F32), ((2, batch, batch), BF16)],
+        (*grams, packed, norm, other, scale, coeff),
+        [((batch // place.n, columns), BF16)] * place.n + [((batch, batch), BF16), ((1, 1), F32)],
         "gradient",
-        scratch_shapes=[pltpu.VMEM((2, batch, columns), BF16)],
-    )
+        scratch_shapes=[pltpu.VMEM((batch, columns), BF16)],
+    )
+    return [first, *others[::-1]], gram, share
 
 
 def place_kernel(place_ref, *refs, n):
@@ -609,23 +608,25 @@
     )
     grams = sends(place, "a", [part] * n)
     grams += [place.send(part, lambda z, a, b: (z, a, b ^ 1)) for part in grams]
-    first, *others, share, grams = gradient(
-        place,
-        place_array,
-        grams,
-        (packed_1, packed_2),
-        (norm_1, norm_2),
-        (scale_1, scale_2),
-        coeff,
-    )
-    out_1, out_2 = local(
-        functools.partial(place_kernel, n=n),
-        place_array,
-        [first, *sends(place, "z", [first, *others[::-1]])[:0:-1]],
-        [(h_first.shape, BF16)] * 2,
-        "place",
-    )
-    (loss,) = local(loss_kernel, place_array, (grams, share), [((1, 1), F32)], "loss")
+    grads_2, gram_1, _ = gradient(
+        place, place_array, grams, 0, packed_2, norm_2, norm_1, scale_2, coeff
+    )
+    grads_1, gram_2, share = gradient(
+        place, place_array, grams, 1, packed_1, norm_1, norm_2, scale_1, coeff
+    )
+    outs = []
+    for grads in (grads_1, grads_2):
+        met = sends(place, "z", grads)
+        (out,) = local(
+            functools.partial(place_kernel, n=n),
+            place_array,
+            [met[0], *met[:0:-1]],
+            [(h_first.shape, BF16)],
+            "place",
+        )
+        outs.append(out)
+    out_1, out_2 = outs
+    (loss,) = local(loss_kernel, place_array, (gram_1, gram_2, share), [((1, 1), F32)], "loss")
     return (out_1, out_2, loss.reshape(()))
 
 

time: 145 us -> 145 us (level)
  waiting for transfers between devices: 52.1 us -> 44.9 us
  starting transfers between devices: 56.4 us -> 60.8 us
  Pallas kernels: 31.9 us -> 34.5 us
    ppermute x54 -> x57, waiting for transfers between devices: 52.1 us -> 44.9 us  [send(): return lax.ppermute(value, ('dp', 'mp'), pairs)]
    ppermute x54 -> x57, starting transfers between devices: 56.4 us -> 60.8 us  [send(): return lax.ppermute(value, ('dp', 'mp'), pairs)]
    pallas_call x12 -> x14, Pallas kernels: 12.6 us -> 15.2 us  [local(): pl.pallas_call(kernel, in_specs=[pl.BlockSpec(memory_space=pltpu.SMEM)] +...]
  transfers between devices with their start and end apart: 54 -> 57, of which waited for: 24 -> 23; matrix products, arithmetic and copies ran while one was open for 1% -> 1% of each run, Pallas kernels for 16% -> 18%
where the time goes in v17:
time: 145 us; the launch traced here: 144 us
  starting transfers between devices  60.8 us (42%)
  waiting for transfers between devices  44.9 us (31%)
  Pallas kernels  34.5 us (24%)
  local copies, waits for them, and re-layouts  1.91 us (1%)
    ppermute x57, starting transfers between devices, send(): return lax.ppermute(value, ('dp', 'mp'), pairs)  60.8 us
    ppermute x57, waiting for transfers between devices, send(): return lax.ppermute(value, ('dp', 'mp'), pairs)  44.9 us
    pallas_call x14, Pallas kernels, local(): pl.pallas_call(kernel, in_specs=[pl.BlockSpec(memory_space=pltpu.SMEM)] +...  15.2 us
    pallas_call x2, Pallas kernels, project(): pl.pallas_call(functools.partial(project_kernel, counts=counts, n=n, k=k)...  8.92 us
    pallas_call x2, Pallas kernels, normalize_parts(): pl.pallas_call(functools.partial(normalize_kernel, n=n, k=k, order=order,...  6.01 us
    pallas_call x2, Pallas kernels, fetch(): pl.pallas_call(fetch_kernel, in_specs=[pl.BlockSpec(memory_space=pl.ANY)]...  4.39 us
  transfers between devices with their start and end apart: 57, of which 23 were waited for; matrix products, arithmetic and copies ran while one was open for 1% of the time, Pallas kernels for 18%

profile of v17, /device:TPU:0, one launch (start us, length us, event | category | flops | bytes accessed | tf_op | source)
XLA Modules:
  0.0 144.2 jit_solution(2607849018902054511)
XLA Ops:
  0.7 1.0 dynamic-slice_bitcast_fusion.4
  1.6 4.0 %collective-permute-start.10 = (bf16[32,1024]{1,0:T(8,128)(2,1)S(1)}, bf16[32,1024]{1,0:T(8,128)(2,1)S(1)}, u32[]{:S(2)}, u32[]{:S(2)}) collective-permute-start(bf16[32,1024]{1,0:T(8,128)(2,1)S(1)} %get-tuple-element.196), channel_id=1, source_target_pairs={{0,6},{1,7},{2,4},{3,5},{4,2},{5,3},{6,0},{7,1},{8,14},{9,15},{10,... | collective-permute-start | bytes 196616 | tf_op jit(solution)/shard_map/ppermute | solution.py:40
  6.2 1.0 dynamic-slice_bitcast_fusion
  7.2 2.9 %collective-permute-start.16 = (bf16[32,1024]{1,0:T(8,128)(2,1)S(1)}, bf16[32,1024]{1,0:T(8,128)(2,1)S(1)}, u32[]{:S(2)}, u32[]{:S(2)}) collective-permute-start(bf16[32,1024]{1,0:T(8,128)(2,1)S(1)} %get-tuple-element.192), channel_id=1, source_target_pairs={{0,6},{1,7},{2,4},{3,5},{4,2},{5,3},{6,0},{7,1},{8,14},{9,15},{10,... | collective-permute-start | bytes 196616 | tf_op jit(solution)/shard_map/ppermute | solution.py:40
  11.4 2.0 %collective-permute-start.11 = (bf16[32,1024]{1,0:T(8,128)(2,1)S(1)}, bf16[32,1024]{1,0:T(8,128)(2,1)S(1)}, u32[]{:S(2)}, u32[]{:S(2)}) collective-permute-start(bf16[32,1024]{1,0:T(8,128)(2,1)S(1)} %get-tuple-element.113), channel_id=1, source_target_pairs={{0,8},{1,9},{2,10},{3,11},{4,12},{5,13},{6,14},{7,15},{8,0},{9,1},... | collective-permute-start | bytes 196616 | tf_op jit(solution)/shard_map/ppermute | solution.py:40
  13.5 2.6 %collective-permute-start.12 = (bf16[32,1024]{1,0:T(8,128)(2,1)S(1)}, bf16[32,1024]{1,0:T(8,128)(2,1)S(1)}, u32[]{:S(2)}, u32[]{:S(2)}) collective-permute-start(bf16[32,1024]{1,0:T(8,128)(2,1)S(1)} %get-tuple-element.114), channel_id=1, source_target_pairs={{0,16},{1,17},{2,18},{3,19},{4,20},{5,21},{6,22},{7,23},{8,24},{9,... | collective-permute-start | bytes 196616 | tf_op jit(solution)/shard_map/ppermute | solution.py:40
  16.6 3.4 %collective-permute-done.12.refs_2_ = bf16[32,1024]{1,0:T(8,128)(2,1)S(1)} collective-permute-done((bf16[32,1024]{1,0:T(8,128)(2,1)S(1)}, bf16[32,1024]{1,0:T(8,128)(2,1)S(1)}, u32[]{:S(2)}, u32[]{:S(2)}) %collective-permute-start.12) | collective-permute-done | bytes 65568 | tf_op jit(solution)/shard_map/ppermute | solution.py:40
  20.0 2.1 %collective-permute-done.13.refs_1_ = bf16[32,1024]{1,0:T(8,128)(2,1)S(1)} collective-permute-done((bf16[32,1024]{1,0:T(8,128)(2,1)S(1)}, bf16[32,1024]{1,0:T(8,128)(2,1)S(1)}, u32[]{:S(2)}, u32[]{:S(2)}) %collective-permute-start.13) | collective-permute-done | bytes 65568 | tf_op jit(solution)/shard_map/ppermute | solution.py:40
  22.7 2.5 %collective-permute-start.19 = (bf16[128,1024]{1,0:T(8,128)(2,1)S(1)}, bf16[128,1024]{1,0:T(8,128)(2,1)S(1)}, u32[]{:S(2)}, u32[]{:S(2)}) collective-permute-start(bf16[128,1024]{1,0:T(8,128)(2,1)S(1)} %lay.2.refs_0_), channel_id=1, source_target_pairs={{0,6},{1,7},{2,4},{3,5},{4,2},{5,3},{6,0},{7,1},{8,14},{9,15},{10,... | collective-permute-start | bytes 786440 | tf_op jit(solution)/shard_map/ppermute | solution.py:40
  26.3 0.9 collective-permute-start.22
  27.2 5.4 %collective-permute-done.22.refs_1_ = bf16[32,1024]{1,0:T(8,128)(2,1)S(1)} collective-permute-done((bf16[32,1024]{1,0:T(8,128)(2,1)S(1)}, bf16[32,1024]{1,0:T(8,128)(2,1)S(1)}, u32[]{:S(2)}, u32[]{:S(2)}) %collective-permute-start.22) | collective-permute-done | bytes 65568 | tf_op jit(solution)/shard_map/ppermute | solution.py:40
  32.5 2.2 %fetch.3.refs_8_ = bf16[2048,1024]{1,0:T(8,128)(2,1)S(1)} custom-call(bf16[2048,1024]{1,0:T(8,128)(2,1)} %weight_ref), custom_call_target="tpu_custom_call" | custom-call | bytes 8388608 | tf_op jit(solution)/shard_map/fetch/pallas_call | solution.py:265
  34.7 2.9 %collective-permute-done.21.refs_2_ = bf16[32,1024]{1,0:T(8,128)(2,1)S(1)} collective-permute-done((bf16[32,1024]{1,0:T(8,128)(2,1)S(1)}, bf16[32,1024]{1,0:T(8,128)(2,1)S(1)}, u32[]{:S(2)}, u32[]{:S(2)}) %collective-permute-start.21) | collective-permute-done | bytes 65568 | tf_op jit(solution)/shard_map/ppermute | solution.py:40
  39.3 2.5 %collective-permute-start.27 = (bf16[128,1024]{1,0:T(8,128)(2,1)S(1)}, bf16[128,1024]{1,0:T(8,128)(2,1)}, u32[]{:S(2)}, u32[]{:S(2)}) collective-permute-start(bf16[128,1024]{1,0:T(8,128)(2,1)S(1)} %lay.3), channel_id=1, source_target_pairs={{0,6},{1,7},{2,4},{3,5},{4,2},{5,3},{6,0},{7,1},{8,14},{9,15},{10,... | collective-permute-start | bytes 786440 | tf_op jit(solution)/shard_map/ppermute | solution.py:40
  41.9 3.9 %project.3 = (f32[512,256]{1,0:T(8,128)S(1)}, bf16[528,256]{1,0:T(8,128)(2,1)S(1)}, bf16[528,256]{1,0:T(8,128)(2,1)S(1)}, bf16[528,256]{1,0:T(8,128)(2,1)S(1)}) custom-call(s32[3]{0:T(128)S(1)} %pad_add_fusion.place_ref, bf16[128,1024]{1,0:T(8,128)(2,1)S(1)} %lay.2.refs_0_, bf16[128,1024]{1,0:T(8,128)(2,1)S(1)} %collective-permute-done.17.refs_1_, ...), custom_call_target="tpu_custom_call" | custom-call | flops 2147483648 | bytes 7864320 | tf_op jit(solution)/shard_map/project/pallas_call | solution.py:378
  45.8 1.7 %collective-permute-start.31 = (bf16[528,256]{1,0:T(8,128)(2,1)S(1)}, bf16[528,256]{1,0:T(8,128)(2,1)S(1)}, u32[]{:S(2)}, u32[]{:S(2)}) collective-permute-start(bf16[528,256]{1,0:T(8,128)(2,1)S(1)} %get-tuple-element.147), channel_id=1, source_target_pairs={{0,24},{1,25},{2,26},{3,27},{4,28},{5,29},{6,30},{7,31},{8,16},{9,... | collective-permute-start | bytes 811016 | tf_op jit(solution)/shard_map/ppermute | solution.py:40
  47.5 2.8 %collective-permute-start.33 = (bf16[528,256]{1,0:T(8,128)(2,1)S(1)}, bf16[528,256]{1,0:T(8,128)(2,1)S(1)}, u32[]{:S(2)}, u32[]{:S(2)}) collective-permute-start(bf16[528,256]{1,0:T(8,128)(2,1)S(1)} %get-tuple-element.149), channel_id=1, source_target_pairs={{0,8},{1,9},{2,10},{3,11},{4,12},{5,13},{6,14},{7,15},{8,0},{9,1},... | collective-permute-start | bytes 811016 | tf_op jit(solution)/shard_map/ppermute | solution.py:40
  50.2 16.4 %conditional.2 = (f32[512,256]{1,0:T(8,128)S(1)}, bf16[528,256]{1,0:T(8,128)(2,1)}, bf16[528,256]{1,0:T(8,128)(2,1)}, bf16[528,256]{1,0:T(8,128)(2,1)}) conditional(s32[]{:T(128)} %convert_element_type.4, () %tuple.35, (bf16[128,1024]{1,0:T(8,128)(2,1)S(1)}, bf16[128,1024]{1,0:T(8,128)(2,1)}, bf16[2048,1024]{1,0:T(8,128)(2,1)}, s32[3]{0:T(128)S(1)}) %tuple.36), branch_computations={%region_0.1_spmd, %region_1.2_spmd} | conditional | flops 2149580800 | bytes 24641728 | solution.py:232
  50.8 1.0 collective-permute-start.5
  51.8 5.6 %collective-permute-done.4.refs_2_ = bf16[128,1024]{1,0:T(8,128)(2,1)S(1)} collective-permute-done((bf16[128,1024]{1,0:T(8,128)(2,1)S(1)}, bf16[128,1024]{1,0:T(8,128)(2,1)S(1)}, u32[]{:S(2)}, u32[]{:S(2)}) %collective-permute-start.4) | collective-permute-done | bytes 262176 | tf_op jit(solution)/shard_map/cond/branch_1_fun/ppermute | solution.py:40
  57.8 1.0 pad_maximum_fusion
  59.4 2.2 %fetch.2.refs_6_ = bf16[2048,1024]{1,0:T(8,128)(2,1)S(1)} custom-call(bf16[2048,1024]{1,0:T(8,128)(2,1)} %get-tuple-element.19.weight_ref), custom_call_target="tpu_custom_call" | custom-call | bytes 8388608 | tf_op jit(solution)/shard_map/cond/branch_1_fun/fetch/pallas_call | solution.py:265
  61.6 5.0 %project.2 = (f32[512,256]{1,0:T(8,128)S(1)}, bf16[528,256]{1,0:T(8,128)(2,1)}, bf16[528,256]{1,0:T(8,128)(2,1)}, bf16[528,256]{1,0:T(8,128)(2,1)}) custom-call(s32[3]{0:T(128)S(1)} %get-tuple-element.14.place_ref, bf16[128,1024]{1,0:T(8,128)(2,1)S(1)} %get-tuple-element.16.refs_0_, bf16[128,1024]{1,0:T(8,128)(2,1)} %get-tuple-element.17.refs_1_, ...), custom_call_target="tpu_custom_call" | custom-call | flops 2147483648 | bytes 7864320 | tf_op jit(solution)/shard_map/cond/branch_1_fun/project/pallas_call | solution.py:378
  66.9 1.8 %collective-permute-start.29 = (bf16[528,256]{1,0:T(8,128)(2,1)}, bf16[528,256]{1,0:T(8,128)(2,1)S(1)}, u32[]{:S(2)}, u32[]{:S(2)}) collective-permute-start(bf16[528,256]{1,0:T(8,128)(2,1)} %get-tuple-element.144), channel_id=1, source_target_pairs={{0,16},{1,17},{2,18},{3,19},{4,20},{5,21},{6,22},{7,23},{8,24},{9,... | collective-permute-start | bytes 811016 | tf_op jit(solution)/shard_map/ppermute | solution.py:40
  68.8 2.3 %collective-permute-start.30 = (bf16[528,256]{1,0:T(8,128)(2,1)}, bf16[528,256]{1,0:T(8,128)(2,1)S(1)}, u32[]{:S(2)}, u32[]{:S(2)}) collective-permute-start(bf16[528,256]{1,0:T(8,128)(2,1)} %get-tuple-element.145), channel_id=1, source_target_pairs={{0,24},{1,25},{2,26},{3,27},{4,28},{5,29},{6,30},{7,31},{8,16},{9,... | collective-permute-start | bytes 811016 | tf_op jit(solution)/shard_map/ppermute | solution.py:40
  71.0 3.4 %normalize.2 = (f32[512,256]{1,0:T(8,128)S(1)}, bf16[512,256]{1,0:T(8,128)(2,1)S(1)}, f32[1,256]{1,0:T(1,128)S(1)}, f32[256,512]{1,0:T(8,128)}, f32[256,512]{1,0:T(8,128)}) custom-call(s32[3]{0:T(128)S(1)} %pad_add_fusion.place_ref, f32[512,256]{1,0:T(8,128)S(1)} %get-tuple-element.146.refs_0_, bf16[528,256]{1,0:T(8,128)(2,1)S(1)} %collective-permute-done.31.refs_1_, ...), custom_call_target="tpu_custom_call" | custom-call | flops 134217728 | bytes 3145728 | tf_op jit(solution)/shard_map/normalize/pallas_call | solution.py:458
  74.4 13.5 %conditional.3 = ((f32[16,384]{1,0:T(8,128)S(1)}, bf16[64,128]{1,0:T(8,128)(2,1)S(1)}, bf16[64,128]{1,0:T(8,128)(2,1)S(1)}, bf16[64,128]{1,0:T(8,128)(2,1)S(1)})) conditional(s32[]{:T(128)} %convert_element_type.4, () %tuple.38, (f32[256,512]{1,0:T(8,128)}, s32[3]{0:T(128)S(1)}, f32[256,512]{1,0:T(8,128)}) %tuple.39), branch_computations={%region_2.3_spmd, %region_3.4_spmd} | conditional | bytes 2736296 | solution.py:232
  74.4 2.1 %collective-permute-done.met_ref = f32[256,512]{1,0:T(8,128)S(1)} collective-permute-done((f32[256,512]{1,0:T(8,128)}, f32[256,512]{1,0:T(8,128)S(1)}, u32[]{:S(2)}, u32[]{:S(2)}) %collective-permute-start) | collective-permute-done | bytes 524320 | tf_op jit(solution)/shard_map/cond/branch_1_fun/ppermute | solution.py:40
  76.5 1.3 halve.2
  77.8 1.6 %collective-permute-start.1 = (bf16[208,128]{1,0:T(8,128)(2,1)S(1)}, bf16[208,128]{1,0:T(8,128)(2,1)S(1)}, u32[]{:S(2)}, u32[]{:S(2)}) collective-permute-start(bf16[208,128]{1,0:T(8,128)(2,1)S(1)} %get-tuple-element.28), channel_id=1, source_target_pairs={{0,2},{1,3},{2,0},{3,1},{4,6},{5,7},{6,4},{7,5},{8,10},{9,11},{10,... | collective-permute-start | bytes 159752 | tf_op jit(solution)/shard_map/cond/branch_1_fun/ppermute | solution.py:40
  79.9 2.1 %collective-permute-done.1.refs_1_ = bf16[208,128]{1,0:T(8,128)(2,1)S(1)} collective-permute-done((bf16[208,128]{1,0:T(8,128)(2,1)S(1)}, bf16[208,128]{1,0:T(8,128)(2,1)S(1)}, u32[]{:S(2)}, u32[]{:S(2)}) %collective-permute-start.1) | collective-permute-done | bytes 53280 | tf_op jit(solution)/shard_map/cond/branch_1_fun/ppermute | solution.py:40
  82.0 1.4 collective-permute-start.3
  83.5 3.5 %collective-permute-done.3.refs_3_ = bf16[208,128]{1,0:T(8,128)(2,1)S(1)} collective-permute-done((bf16[208,128]{1,0:T(8,128)(2,1)S(1)}, bf16[208,128]{1,0:T(8,128)(2,1)S(1)}, u32[]{:S(2)}, u32[]{:S(2)}) %collective-permute-start.3) | collective-permute-done | bytes 53280 | tf_op jit(solution)/shard_map/cond/branch_1_fun/ppermute | solution.py:40
  87.1 0.8 plane.1
  88.0 2.4 %collective-permute-start.35 = (bf16[64,128]{1,0:T(8,128)(2,1)S(1)}, bf16[64,128]{1,0:T(8,128)(2,1)S(1)}, u32[]{:S(2)}, u32[]{:S(2)}) collective-permute-start(bf16[64,128]{1,0:T(8,128)(2,1)S(1)} %get-tuple-element.154), channel_id=1, source_target_pairs={{0,16},{1,17},{2,18},{3,19},{4,20},{5,21},{6,22},{7,23},{8,24},{9,... | collective-permute-start | bytes 49160 | tf_op jit(solution)/shard_map/ppermute | solution.py:40
  90.4 2.0 %collective-permute-start.36 = (bf16[64,128]{1,0:T(8,128)(2,1)S(1)}, bf16[64,128]{1,0:T(8,128)(2,1)S(1)}, u32[]{:S(2)}, u32[]{:S(2)}) collective-permute-start(bf16[64,128]{1,0:T(8,128)(2,1)S(1)} %get-tuple-element.155), channel_id=1, source_target_pairs={{0,24},{1,25},{2,26},{3,27},{4,28},{5,29},{6,30},{7,31},{8,16},{9,... | collective-permute-start | bytes 49160 | tf_op jit(solution)/shard_map/ppermute | solution.py:40
  92.4 2.2 %collective-permute-done.35.refs_2_ = bf16[64,128]{1,0:T(8,128)(2,1)S(1)} collective-permute-done((bf16[64,128]{1,0:T(8,128)(2,1)S(1)}, bf16[64,128]{1,0:T(8,128)(2,1)S(1)}, u32[]{:S(2)}, u32[]{:S(2)}) %collective-permute-start.35) | collective-permute-done | bytes 16416 | tf_op jit(solution)/shard_map/ppermute | solution.py:40
  94.6 1.3 collective-permute-done.36.refs_3_
  95.9 2.6 %normalize.3 = (f32[512,256]{1,0:T(8,128)S(1)}, bf16[512,256]{1,0:T(8,128)(2,1)S(1)}, f32[1,256]{1,0:T(1,128)S(1)}, f32[256,512]{1,0:T(8,128)S(1)}, f32[256,512]{1,0:T(8,128)S(1)}, /*index=5*/f32[1,256]{1,0:T(1,128)S(1)}) custom-call(s32[3]{0:T(128)S(1)} %pad_add_fusion.place_ref, f32[512,256]{1,0:T(8,128)S(1)} %get-tuple-element.156.refs_0_, ...), custom_call_target="tpu_custom_call" | custom-call | flops 134217728 | bytes 3145728 | tf_op jit(solution)/shard_map/normalize/pallas_call | solution.py:458
  98.6 1.9 %collective-permute-done.37.met_ref = f32[256,512]{1,0:T(8,128)S(1)} collective-permute-done((f32[256,512]{1,0:T(8,128)S(1)}, f32[256,512]{1,0:T(8,128)S(1)}, u32[]{:S(2)}, u32[]{:S(2)}) %collective-permute-start.37) | collective-permute-done | bytes 524320 | tf_op jit(solution)/shard_map/ppermute | solution.py:40
  100.5 0.8 halve.3
  101.3 1.3 collective-permute-start.38
  103.2 1.7 %collective-permute-start.40 = (bf16[208,128]{1,0:T(8,128)(2,1)S(1)}, bf16[208,128]{1,0:T(8,128)(2,1)S(1)}, u32[]{:S(2)}, u32[]{:S(2)}) collective-permute-start(bf16[208,128]{1,0:T(8,128)(2,1)S(1)} %get-tuple-element.166), channel_id=1, source_target_pairs={{0,6},{1,7},{2,4},{3,5},{4,2},{5,3},{6,0},{7,1},{8,14},{9,15},{10,... | collective-permute-start | bytes 159752 | tf_op jit(solution)/shard_map/ppermute | solution.py:40
  105.5 1.8 %collective-permute-done.39.refs_2_ = bf16[208,128]{1,0:T(8,128)(2,1)S(1)} collective-permute-done((bf16[208,128]{1,0:T(8,128)(2,1)S(1)}, bf16[208,128]{1,0:T(8,128)(2,1)S(1)}, u32[]{:S(2)}, u32[]{:S(2)}) %collective-permute-start.39) | collective-permute-done | bytes 53280 | tf_op jit(solution)/shard_map/ppermute | solution.py:40
  107.4 0.8 collective-permute-done.40.refs_3_
  108.2 0.8 code.1.refs_0_
  109.1 2.3 %collective-permute-start.43 = (bf16[256,128]{1,0:T(8,128)(2,1)S(1)}, bf16[256,128]{1,0:T(8,128)(2,1)S(1)}, u32[]{:S(2)}, u32[]{:S(2)}) collective-permute-start(bf16[256,128]{1,0:T(8,128)(2,1)S(1)} %code.1.refs_0_), channel_id=1, source_target_pairs={{0,24},{1,25},{2,26},{3,27},{4,28},{5,29},{6,30},{7,31},{8,16},{9,... | collective-permute-start | bytes 196616 | tf_op jit(solution)/shard_map/ppermute | solution.py:40
  111.4 2.1 %collective-permute-start.41 = (bf16[256,128]{1,0:T(8,128)(2,1)S(1)}, bf16[256,128]{1,0:T(8,128)(2,1)S(1)}, u32[]{:S(2)}, u32[]{:S(2)}) collective-permute-start(bf16[256,128]{1,0:T(8,128)(2,1)S(1)} %code.1.refs_0_), channel_id=1, source_target_pairs={{0,8},{1,9},{2,10},{3,11},{4,12},{5,13},{6,14},{7,15},{8,0},{9,1},... | collective-permute-start | bytes 196616 | tf_op jit(solution)/shard_map/ppermute | solution.py:40
  113.5 2.3 %collective-permute-done.43.refs_3_ = bf16[256,128]{1,0:T(8,128)(2,1)S(1)} collective-permute-done((bf16[256,128]{1,0:T(8,128)(2,1)S(1)}, bf16[256,128]{1,0:T(8,128)(2,1)S(1)}, u32[]{:S(2)}, u32[]{:S(2)}) %collective-permute-start.43) | collective-permute-done | bytes 65568 | tf_op jit(solution)/shard_map/ppermute | solution.py:40
  115.8 1.3 collective-permute-done.42.refs_2_
  117.1 1.0 finish.1.refs_0_
  118.1 1.6 %collective-permute-start.46 = (bf16[128,384]{1,0:T(8,128)(2,1)S(1)}, bf16[128,384]{1,0:T(8,128)(2,1)S(1)}, u32[]{:S(2)}, u32[]{:S(2)}) collective-permute-start(bf16[128,384]{1,0:T(8,128)(2,1)S(1)} %finish.1.refs_0_), channel_id=1, source_target_pairs={{0,6},{1,7},{2,4},{3,5},{4,2},{5,3},{6,0},{7,1},{8,14},{9,15},{10,... | collective-permute-start | bytes 294920 | tf_op jit(solution)/shard_map/ppermute | solution.py:40
  119.6 1.2 collective-permute-start.45
  121.7 2.1 %collective-permute-done.46.refs_3_ = bf16[128,384]{1,0:T(8,128)(2,1)S(1)} collective-permute-done((bf16[128,384]{1,0:T(8,128)(2,1)S(1)}, bf16[128,384]{1,0:T(8,128)(2,1)S(1)}, u32[]{:S(2)}, u32[]{:S(2)}) %collective-permute-start.46) | collective-permute-done | bytes 98336 | tf_op jit(solution)/shard_map/ppermute | solution.py:40
  123.7 1.0 collective-permute-done.45.refs_2_
  126.8 1.7 %gradient.2 = (bf16[128,256]{1,0:T(8,128)(2,1)S(1)}, bf16[128,256]{1,0:T(8,128)(2,1)S(1)}, bf16[128,256]{1,0:T(8,128)(2,1)S(1)}, bf16[128,256]{1,0:T(8,128)(2,1)...) custom-call(s32[3]{0:T(128)S(1)} %pad_add_fusion.place_ref, bf16[128,384]{1,0:T(8,128)(2,1)S(1)} %finish.1.refs_0_, ...), custom_call_target="tpu_custom_call" | custom-call | tf_op jit(solution)/shard_map/gradient/pallas_call | solution.py:190
  128.5 1.8 %collective-permute-start.51 = (bf16[128,256]{1,0:T(8,128)(2,1)S(1)}, bf16[128,256]{1,0:T(8,128)(2,1)S(1)}, u32[]{:S(2)}, u32[]{:S(2)}) collective-permute-start(bf16[128,256]{1,0:T(8,128)(2,1)S(1)} %get-tuple-element.176), channel_id=1, source_target_pairs={{0,24},{1,25},{2,26},{3,27},{4,28},{5,29},{6,30},{7,31},{8,16},{9,... | collective-permute-start | bytes 196616 | tf_op jit(solution)/shard_map/ppermute | solution.py:40
  130.8 2.2 %collective-permute-start.53 = (bf16[128,256]{1,0:T(8,128)(2,1)S(1)}, bf16[128,256]{1,0:T(8,128)(2,1)S(1)}, u32[]{:S(2)}, u32[]{:S(2)}) collective-permute-start(bf16[128,256]{1,0:T(8,128)(2,1)S(1)} %get-tuple-element.178), channel_id=1, source_target_pairs={{0,8},{1,9},{2,10},{3,11},{4,12},{5,13},{6,14},{7,15},{8,0},{9,1},... | collective-permute-start | bytes 196616 | tf_op jit(solution)/shard_map/ppermute | solution.py:40
  132.9 1.7 %gradient.3 = (bf16[128,256]{1,0:T(8,128)(2,1)S(1)}, bf16[128,256]{1,0:T(8,128)(2,1)S(1)}, bf16[128,256]{1,0:T(8,128)(2,1)S(1)}, bf16[128,256]{1,0:T(8,128)(2,1)...) custom-call(s32[3]{0:T(128)S(1)} %pad_add_fusion.place_ref, bf16[128,384]{1,0:T(8,128)(2,1)S(1)} %finish.1.refs_0_, ...), custom_call_target="tpu_custom_call" | custom-call | tf_op jit(solution)/shard_map/gradient/pallas_call | solution.py:190
  134.7 1.8 %collective-permute-start.54 = (bf16[128,256]{1,0:T(8,128)(2,1)S(1)}, bf16[128,256]{1,0:T(8,128)(2,1)S(1)}, u32[]{:S(2)}, u32[]{:S(2)}) collective-permute-start(bf16[128,256]{1,0:T(8,128)(2,1)S(1)} %get-tuple-element.182), channel_id=1, source_target_pairs={{0,24},{1,25},{2,26},{3,27},{4,28},{5,29},{6,30},{7,31},{8,16},{9,... | collective-permute-start | bytes 196616 | tf_op jit(solution)/shard_map/ppermute | solution.py:40
  136.5 2.5 %collective-permute-start.56 = (bf16[128,256]{1,0:T(8,128)(2,1)S(1)}, bf16[128,256]{1,0:T(8,128)(2,1)S(1)}, u32[]{:S(2)}, u32[]{:S(2)}) collective-permute-start(bf16[128,256]{1,0:T(8,128)(2,1)S(1)} %get-tuple-element.184), channel_id=1, source_target_pairs={{0,8},{1,9},{2,10},{3,11},{4,12},{5,13},{6,14},{7,15},{8,0},{9,1},... | collective-permute-start | bytes 196616 | tf_op jit(solution)/shard_map/ppermute | solution.py:40
  139.1 2.1 %loss.1 = f32[1,1]{1,0:T(1,128)} custom-call(s32[3]{0:T(128)S(1)} %pad_add_fusion.place_ref, bf16[512,512]{1,0:T(8,128)(2,1)S(1)} %get-tuple-element.185.first_ref, bf16[512,512]{1,0:T(8,128)(2,1)S(1)} %get-tuple-element.186.second_ref, f32[1,1]{1,0:T(1,128)} %get-tuple-element.187.share_ref), custom_call_target="tpu_custom_call" | custom-call | tf_op jit(solution)/shard_map/loss/pallas_call | solution.py:190
  141.2 1.3 place.2
  142.9 1.3 place.3
  (78 shorter events, 13.2 us)
Async XLA Ops:
  1.6 9.1 %collective-permute-start.10 = (bf16[32,1024]{1,0:T(8,128)(2,1)S(1)}, bf16[32,1024]{1,0:T(8,128)(2,1)S(1)}, u32[]{:S(2)}, u32[]{:S(2)}) collective-permute-start(bf16[32,1024]{1,0:T(8,128)(2,1)S(1)} %get-tuple-element.196), channel_id=1, source_target_pairs={{0,6},{1,7},{2,4},{3,5},{4,2},{5,3},{6,0},{7,1},{8,14},{9,15},{10,... | collective-permute-start | bytes 196616 | tf_op jit(solution)/shard_map/ppermute | solution.py:40
  5.6 5.2 %collective-permute-start.9 = (bf16[32,1024]{1,0:T(8,128)(2,1)S(1)}, bf16[32,1024]{1,0:T(8,128)(2,1)S(1)}, u32[]{:S(2)}, u32[]{:S(2)}) collective-permute-start(bf16[32,1024]{1,0:T(8,128)(2,1)S(1)} %get-tuple-element.197), channel_id=1, source_target_pairs={{0,4},{1,5},{2,6},{3,7},{4,0},{5,1},{6,2},{7,3},{8,12},{9,13},{10,... | collective-permute-start | bytes 196616 | tf_op jit(solution)/shard_map/ppermute | solution.py:40
  6.1 4.7 %collective-permute-start.8 = (bf16[32,1024]{1,0:T(8,128)(2,1)S(1)}, bf16[32,1024]{1,0:T(8,128)(2,1)S(1)}, u32[]{:S(2)}, u32[]{:S(2)}) collective-permute-start(bf16[32,1024]{1,0:T(8,128)(2,1)S(1)} %get-tuple-element.198), channel_id=1, source_target_pairs={{0,2},{1,3},{2,0},{3,1},{4,6},{5,7},{6,4},{7,5},{8,10},{9,11},{10,... | collective-permute-start | bytes 196616 | tf_op jit(solution)/shard_map/ppermute | solution.py:40
  7.2 8.9 %collective-permute-start.16 = (bf16[32,1024]{1,0:T(8,128)(2,1)S(1)}, bf16[32,1024]{1,0:T(8,128)(2,1)S(1)}, u32[]{:S(2)}, u32[]{:S(2)}) collective-permute-start(bf16[32,1024]{1,0:T(8,128)(2,1)S(1)} %get-tuple-element.192), channel_id=1, source_target_pairs={{0,6},{1,7},{2,4},{3,5},{4,2},{5,3},{6,0},{7,1},{8,14},{9,15},{10,... | collective-permute-start | bytes 196616 | tf_op jit(solution)/shard_map/ppermute | solution.py:40
  10.1 6.5 %collective-permute-start.15 = (bf16[32,1024]{1,0:T(8,128)(2,1)S(1)}, bf16[32,1024]{1,0:T(8,128)(2,1)S(1)}, u32[]{:S(2)}, u32[]{:S(2)}) collective-permute-start(bf16[32,1024]{1,0:T(8,128)(2,1)S(1)} %get-tuple-element.193), channel_id=1, source_target_pairs={{0,4},{1,5},{2,6},{3,7},{4,0},{5,1},{6,2},{7,3},{8,12},{9,13},{10,... | collective-permute-start | bytes 196616 | tf_op jit(solution)/shard_map/ppermute | solution.py:40
  10.7 5.9 %collective-permute-start.14 = (bf16[32,1024]{1,0:T(8,128)(2,1)S(1)}, bf16[32,1024]{1,0:T(8,128)(2,1)S(1)}, u32[]{:S(2)}, u32[]{:S(2)}) collective-permute-start(bf16[32,1024]{1,0:T(8,128)(2,1)S(1)} %get-tuple-element.194), channel_id=1, source_target_pairs={{0,2},{1,3},{2,0},{3,1},{4,6},{5,7},{6,4},{7,5},{8,10},{9,11},{10,... | collective-permute-start | bytes 196616 | tf_op jit(solution)/shard_map/ppermute | solution.py:40
  11.4 5.2 %collective-permute-start.11 = (bf16[32,1024]{1,0:T(8,128)(2,1)S(1)}, bf16[32,1024]{1,0:T(8,128)(2,1)S(1)}, u32[]{:S(2)}, u32[]{:S(2)}) collective-permute-start(bf16[32,1024]{1,0:T(8,128)(2,1)S(1)} %get-tuple-element.113), channel_id=1, source_target_pairs={{0,8},{1,9},{2,10},{3,11},{4,12},{5,13},{6,14},{7,15},{8,0},{9,1},... | collective-permute-start | bytes 196616 | tf_op jit(solution)/shard_map/ppermute | solution.py:40
  13.5 6.6 %collective-permute-start.12 = (bf16[32,1024]{1,0:T(8,128)(2,1)S(1)}, bf16[32,1024]{1,0:T(8,128)(2,1)S(1)}, u32[]{:S(2)}, u32[]{:S(2)}) collective-permute-start(bf16[32,1024]{1,0:T(8,128)(2,1)S(1)} %get-tuple-element.114), channel_id=1, source_target_pairs={{0,16},{1,17},{2,18},{3,19},{4,20},{5,21},{6,22},{7,23},{8,24},{9,... | collective-permute-start | bytes 196616 | tf_op jit(solution)/shard_map/ppermute | solution.py:40
  16.1 6.1 %collective-permute-start.13 = (bf16[32,1024]{1,0:T(8,128)(2,1)S(1)}, bf16[32,1024]{1,0:T(8,128)(2,1)S(1)}, u32[]{:S(2)}, u32[]{:S(2)}) collective-permute-start(bf16[32,1024]{1,0:T(8,128)(2,1)S(1)} %get-tuple-element.115), channel_id=1, source_target_pairs={{0,24},{1,25},{2,26},{3,27},{4,28},{5,29},{6,30},{7,31},{8,16},{9,... | collective-permute-start | bytes 196616 | tf_op jit(solution)/shard_map/ppermute | solution.py:40
  22.7 15.0 %collective-permute-start.19 = (bf16[128,1024]{1,0:T(8,128)(2,1)S(1)}, bf16[128,1024]{1,0:T(8,128)(2,1)S(1)}, u32[]{:S(2)}, u32[]{:S(2)}) collective-permute-start(bf16[128,1024]{1,0:T(8,128)(2,1)S(1)} %lay.2.refs_0_), channel_id=1, source_target_pairs={{0,6},{1,7},{2,4},{3,5},{4,2},{5,3},{6,0},{7,1},{8,14},{9,15},{10,... | collective-permute-start | bytes 786440 | tf_op jit(solution)/shard_map/ppermute | solution.py:40
  25.2 12.5 %collective-permute-start.18 = (bf16[128,1024]{1,0:T(8,128)(2,1)S(1)}, bf16[128,1024]{1,0:T(8,128)(2,1)S(1)}, u32[]{:S(2)}, u32[]{:S(2)}) collective-permute-start(bf16[128,1024]{1,0:T(8,128)(2,1)S(1)} %lay.2.refs_0_), channel_id=1, source_target_pairs={{0,4},{1,5},{2,6},{3,7},{4,0},{5,1},{6,2},{7,3},{8,12},{9,13},{10,... | collective-permute-start | bytes 786440 | tf_op jit(solution)/shard_map/ppermute | solution.py:40
  25.7 12.0 %collective-permute-start.17 = (bf16[128,1024]{1,0:T(8,128)(2,1)S(1)}, bf16[128,1024]{1,0:T(8,128)(2,1)S(1)}, u32[]{:S(2)}, u32[]{:S(2)}) collective-permute-start(bf16[128,1024]{1,0:T(8,128)(2,1)S(1)} %lay.2.refs_0_), channel_id=1, source_target_pairs={{0,2},{1,3},{2,0},{3,1},{4,6},{5,7},{6,4},{7,5},{8,10},{9,11},{10,... | collective-permute-start | bytes 786440 | tf_op jit(solution)/shard_map/ppermute | solution.py:40
  26.3 6.2 %collective-permute-start.22 = (bf16[32,1024]{1,0:T(8,128)(2,1)S(1)}, bf16[32,1024]{1,0:T(8,128)(2,1)S(1)}, u32[]{:S(2)}, u32[]{:S(2)}) collective-permute-start(bf16[32,1024]{1,0:T(8,128)(2,1)S(1)} %get-tuple-element.188), channel_id=1, source_target_pairs={{0,24},{1,25},{2,26},{3,27},{4,28},{5,29},{6,30},{7,31},{8,16},{9,... | collective-permute-start | bytes 196616 | tf_op jit(solution)/shard_map/ppermute | solution.py:40
  27.1 7.6 %collective-permute-start.20 = (bf16[32,1024]{1,0:T(8,128)(2,1)S(1)}, bf16[32,1024]{1,0:T(8,128)(2,1)S(1)}, u32[]{:S(2)}, u32[]{:S(2)}) collective-permute-start(bf16[32,1024]{1,0:T(8,128)(2,1)S(1)} %get-tuple-element.189), channel_id=1, source_target_pairs={{0,8},{1,9},{2,10},{3,11},{4,12},{5,13},{6,14},{7,15},{8,0},{9,1},... | collective-permute-start | bytes 196616 | tf_op jit(solution)/shard_map/ppermute | solution.py:40
  32.5 5.2 %collective-permute-start.21 = (bf16[32,1024]{1,0:T(8,128)(2,1)S(1)}, bf16[32,1024]{1,0:T(8,128)(2,1)S(1)}, u32[]{:S(2)}, u32[]{:S(2)}) collective-permute-start(bf16[32,1024]{1,0:T(8,128)(2,1)S(1)} %get-tuple-element.190), channel_id=1, source_target_pairs={{0,16},{1,17},{2,18},{3,19},{4,20},{5,21},{6,22},{7,23},{8,24},{9,... | collective-permute-start | bytes 196616 | tf_op jit(solution)/shard_map/ppermute | solution.py:40
  37.7 4.2 %collective-permute-start.23 = (bf16[128,1024]{1,0:T(8,128)(2,1)S(1)}, bf16[128,1024]{1,0:T(8,128)(2,1)S(1)}, u32[]{:S(2)}, u32[]{:S(2)}) collective-permute-start(bf16[128,1024]{1,0:T(8,128)(2,1)S(1)} %lay.2.refs_0_), channel_id=1, source_target_pairs={{0,1},{1,0},{2,3},{3,2},{4,5},{5,4},{6,7},{7,6},{8,9},{9,8},{10,11... | collective-permute-start | bytes 786440 | tf_op jit(solution)/shard_map/ppermute | solution.py:40
  37.8 4.1 %collective-permute-start.24 = (bf16[128,1024]{1,0:T(8,128)(2,1)S(1)}, bf16[128,1024]{1,0:T(8,128)(2,1)S(1)}, u32[]{:S(2)}, u32[]{:S(2)}) collective-permute-start(bf16[128,1024]{1,0:T(8,128)(2,1)S(1)} %collective-permute-done.17.refs_1_), channel_id=1, source_target_pairs={{0,1},{1,0},{2,3},{3,2},{4,5},{5,4},{6,7},{7,6},{8,9},{9,8},{10,11... | collective-permute-start | bytes 786440 | tf_op jit(solution)/shard_map/ppermute | solution.py:40
  38.3 3.6 %collective-permute-start.25 = (bf16[128,1024]{1,0:T(8,128)(2,1)S(1)}, bf16[128,1024]{1,0:T(8,128)(2,1)S(1)}, u32[]{:S(2)}, u32[]{:S(2)}) collective-permute-start(bf16[128,1024]{1,0:T(8,128)(2,1)S(1)} %collective-permute-done.18.refs_2_), channel_id=1, source_target_pairs={{0,1},{1,0},{2,3},{3,2},{4,5},{5,4},{6,7},{7,6},{8,9},{9,8},{10,11... | collective-permute-start | bytes 786440 | tf_op jit(solution)/shard_map/ppermute | solution.py:40
  38.3 3.5 %collective-permute-start.26 = (bf16[128,1024]{1,0:T(8,128)(2,1)S(1)}, bf16[128,1024]{1,0:T(8,128)(2,1)S(1)}, u32[]{:S(2)}, u32[]{:S(2)}) collective-permute-start(bf16[128,1024]{1,0:T(8,128)(2,1)S(1)} %collective-permute-done.19.refs_3_), channel_id=1, source_target_pairs={{0,1},{1,0},{2,3},{3,2},{4,5},{5,4},{6,7},{7,6},{8,9},{9,8},{10,11... | collective-permute-start | bytes 786440 | tf_op jit(solution)/shard_map/ppermute | solution.py:40
  39.3 10.9 %collective-permute-start.27 = (bf16[128,1024]{1,0:T(8,128)(2,1)S(1)}, bf16[128,1024]{1,0:T(8,128)(2,1)}, u32[]{:S(2)}, u32[]{:S(2)}) collective-permute-start(bf16[128,1024]{1,0:T(8,128)(2,1)S(1)} %lay.3), channel_id=1, source_target_pairs={{0,6},{1,7},{2,4},{3,5},{4,2},{5,3},{6,0},{7,1},{8,14},{9,15},{10,... | collective-permute-start | bytes 786440 | tf_op jit(solution)/shard_map/ppermute | solution.py:40
  45.8 23.0 %collective-permute-start.31 = (bf16[528,256]{1,0:T(8,128)(2,1)S(1)}, bf16[528,256]{1,0:T(8,128)(2,1)S(1)}, u32[]{:S(2)}, u32[]{:S(2)}) collective-permute-start(bf16[528,256]{1,0:T(8,128)(2,1)S(1)} %get-tuple-element.147), channel_id=1, source_target_pairs={{0,24},{1,25},{2,26},{3,27},{4,28},{5,29},{6,30},{7,31},{8,16},{9,... | collective-permute-start | bytes 811016 | tf_op jit(solution)/shard_map/ppermute | solution.py:40
  47.4 23.6 %collective-permute-start.32 = (bf16[528,256]{1,0:T(8,128)(2,1)S(1)}, bf16[528,256]{1,0:T(8,128)(2,1)S(1)}, u32[]{:S(2)}, u32[]{:S(2)}) collective-permute-start(bf16[528,256]{1,0:T(8,128)(2,1)S(1)} %get-tuple-element.148), channel_id=1, source_target_pairs={{0,16},{1,17},{2,18},{3,19},{4,20},{5,21},{6,22},{7,23},{8,24},{9,... | collective-permute-start | bytes 811016 | tf_op jit(solution)/shard_map/ppermute | solution.py:40
  47.5 23.6 %collective-permute-start.33 = (bf16[528,256]{1,0:T(8,128)(2,1)S(1)}, bf16[528,256]{1,0:T(8,128)(2,1)S(1)}, u32[]{:S(2)}, u32[]{:S(2)}) collective-permute-start(bf16[528,256]{1,0:T(8,128)(2,1)S(1)} %get-tuple-element.149), channel_id=1, source_target_pairs={{0,8},{1,9},{2,10},{3,11},{4,12},{5,13},{6,14},{7,15},{8,0},{9,1},... | collective-permute-start | bytes 811016 | tf_op jit(solution)/shard_map/ppermute | solution.py:40
  50.2 7.2 %collective-permute-start.4 = (bf16[128,1024]{1,0:T(8,128)(2,1)S(1)}, bf16[128,1024]{1,0:T(8,128)(2,1)S(1)}, u32[]{:S(2)}, u32[]{:S(2)}) collective-permute-start(bf16[128,1024]{1,0:T(8,128)(2,1)S(1)} %get-tuple-element.16.refs_0_), channel_id=1, source_target_pairs={{0,2},{1,3},{2,0},{3,1},{4,6},{5,7},{6,4},{7,5},{8,10},{9,11},{10,... | collective-permute-start | bytes 786440 | tf_op jit(solution)/shard_map/cond/branch_1_fun/ppermute | solution.py:40
  50.8 6.9 %collective-permute-start.5 = (bf16[128,1024]{1,0:T(8,128)(2,1)S(1)}, bf16[128,1024]{1,0:T(8,128)(2,1)S(1)}, u32[]{:S(2)}, u32[]{:S(2)}) collective-permute-start(bf16[128,1024]{1,0:T(8,128)(2,1)S(1)} %get-tuple-element.16.refs_0_), channel_id=1, source_target_pairs={{0,4},{1,5},{2,6},{3,7},{4,0},{5,1},{6,2},{7,3},{8,12},{9,13},{10,... | collective-permute-start | bytes 786440 | tf_op jit(solution)/shard_map/cond/branch_1_fun/ppermute | solution.py:40
  57.7 3.9 %collective-permute-start.7 = (bf16[256,1024]{1,0:T(8,128)(2,1)S(1)}, bf16[256,1024]{1,0:T(8,128)(2,1)S(1)}, u32[]{:S(2)}, u32[]{:S(2)}) collective-permute-start(bf16[256,1024]{1,0:T(8,128)(2,1)S(1)} %pad_maximum_fusion.1), channel_id=1, source_target_pairs={{0,1},{1,0},{2,3},{3,2},{4,5},{5,4},{6,7},{7,6},{8,9},{9,8},{10,11... | collective-permute-start | bytes 1572872 | tf_op jit(solution)/shard_map/cond/branch_1_fun/ppermute | solution.py:40
  58.8 2.8 %collective-permute-start.6 = (bf16[256,1024]{1,0:T(8,128)(2,1)S(1)}, bf16[256,1024]{1,0:T(8,128)(2,1)S(1)}, u32[]{:S(2)}, u32[]{:S(2)}) collective-permute-start(bf16[256,1024]{1,0:T(8,128)(2,1)S(1)} %pad_maximum_fusion), channel_id=1, source_target_pairs={{0,1},{1,0},{2,3},{3,2},{4,5},{5,4},{6,7},{7,6},{8,9},{9,8},{10,11... | collective-permute-start | bytes 1572872 | tf_op jit(solution)/shard_map/cond/branch_1_fun/ppermute | solution.py:40
  66.6 23.8 %collective-permute-start.28 = (bf16[528,256]{1,0:T(8,128)(2,1)}, bf16[528,256]{1,0:T(8,128)(2,1)S(1)}, u32[]{:S(2)}, u32[]{:S(2)}) collective-permute-start(bf16[528,256]{1,0:T(8,128)(2,1)} %get-tuple-element.143), channel_id=1, source_target_pairs={{0,8},{1,9},{2,10},{3,11},{4,12},{5,13},{6,14},{7,15},{8,0},{9,1},... | collective-permute-start | bytes 811016 | tf_op jit(solution)/shard_map/ppermute | solution.py:40
  66.9 25.5 %collective-permute-start.29 = (bf16[528,256]{1,0:T(8,128)(2,1)}, bf16[528,256]{1,0:T(8,128)(2,1)S(1)}, u32[]{:S(2)}, u32[]{:S(2)}) collective-permute-start(bf16[528,256]{1,0:T(8,128)(2,1)} %get-tuple-element.144), channel_id=1, source_target_pairs={{0,16},{1,17},{2,18},{3,19},{4,20},{5,21},{6,22},{7,23},{8,24},{9,... | collective-permute-start | bytes 811016 | tf_op jit(solution)/shard_map/ppermute | solution.py:40
  68.8 23.6 %collective-permute-start.30 = (bf16[528,256]{1,0:T(8,128)(2,1)}, bf16[528,256]{1,0:T(8,128)(2,1)S(1)}, u32[]{:S(2)}, u32[]{:S(2)}) collective-permute-start(bf16[528,256]{1,0:T(8,128)(2,1)} %get-tuple-element.145), channel_id=1, source_target_pairs={{0,24},{1,25},{2,26},{3,27},{4,28},{5,29},{6,30},{7,31},{8,16},{9,... | collective-permute-start | bytes 811016 | tf_op jit(solution)/shard_map/ppermute | solution.py:40
  74.4 2.1 %collective-permute-start = (f32[256,512]{1,0:T(8,128)}, f32[256,512]{1,0:T(8,128)S(1)}, u32[]{:S(2)}, u32[]{:S(2)}) collective-permute-start(f32[256,512]{1,0:T(8,128)} %get-tuple-element.26), channel_id=1, source_target_pairs={{0,1},{1,0},{2,3},{3,2},{4,5},{5,4},{6,7},{7,6},{8,9},{9,8},{10,11... | collective-permute-start | bytes 1572872 | tf_op jit(solution)/shard_map/cond/branch_1_fun/ppermute | solution.py:40
  77.8 4.2 %collective-permute-start.1 = (bf16[208,128]{1,0:T(8,128)(2,1)S(1)}, bf16[208,128]{1,0:T(8,128)(2,1)S(1)}, u32[]{:S(2)}, u32[]{:S(2)}) collective-permute-start(bf16[208,128]{1,0:T(8,128)(2,1)S(1)} %get-tuple-element.28), channel_id=1, source_target_pairs={{0,2},{1,3},{2,0},{3,1},{4,6},{5,7},{6,4},{7,5},{8,10},{9,11},{10,... | collective-permute-start | bytes 159752 | tf_op jit(solution)/shard_map/cond/branch_1_fun/ppermute | solution.py:40
  79.4 4.1 %collective-permute-start.2 = (bf16[208,128]{1,0:T(8,128)(2,1)S(1)}, bf16[208,128]{1,0:T(8,128)(2,1)S(1)}, u32[]{:S(2)}, u32[]{:S(2)}) collective-permute-start(bf16[208,128]{1,0:T(8,128)(2,1)S(1)} %get-tuple-element.31), channel_id=1, source_target_pairs={{0,4},{1,5},{2,6},{3,7},{4,0},{5,1},{6,2},{7,3},{8,12},{9,13},{10,... | collective-permute-start | bytes 159752 | tf_op jit(solution)/shard_map/cond/branch_1_fun/ppermute | solution.py:40
  82.0 5.0 %collective-permute-start.3 = (bf16[208,128]{1,0:T(8,128)(2,1)S(1)}, bf16[208,128]{1,0:T(8,128)(2,1)S(1)}, u32[]{:S(2)}, u32[]{:S(2)}) collective-permute-start(bf16[208,128]{1,0:T(8,128)(2,1)S(1)} %get-tuple-element.32), channel_id=1, source_target_pairs={{0,6},{1,7},{2,4},{3,5},{4,2},{5,3},{6,0},{7,1},{8,14},{9,15},{10,... | collective-permute-start | bytes 159752 | tf_op jit(solution)/shard_map/cond/branch_1_fun/ppermute | solution.py:40
  87.9 4.5 %collective-permute-start.34 = (bf16[64,128]{1,0:T(8,128)(2,1)S(1)}, bf16[64,128]{1,0:T(8,128)(2,1)S(1)}, u32[]{:S(2)}, u32[]{:S(2)}) collective-permute-start(bf16[64,128]{1,0:T(8,128)(2,1)S(1)} %get-tuple-element.153), channel_id=1, source_target_pairs={{0,8},{1,9},{2,10},{3,11},{4,12},{5,13},{6,14},{7,15},{8,0},{9,1},... | collective-permute-start | bytes 49160 | tf_op jit(solution)/shard_map/ppermute | solution.py:40
  88.0 6.6 %collective-permute-start.35 = (bf16[64,128]{1,0:T(8,128)(2,1)S(1)}, bf16[64,128]{1,0:T(8,128)(2,1)S(1)}, u32[]{:S(2)}, u32[]{:S(2)}) collective-permute-start(bf16[64,128]{1,0:T(8,128)(2,1)S(1)} %get-tuple-element.154), channel_id=1, source_target_pairs={{0,16},{1,17},{2,18},{3,19},{4,20},{5,21},{6,22},{7,23},{8,24},{9,... | collective-permute-start | bytes 49160 | tf_op jit(solution)/shard_map/ppermute | solution.py:40
  90.4 5.5 %collective-permute-start.36 = (bf16[64,128]{1,0:T(8,128)(2,1)S(1)}, bf16[64,128]{1,0:T(8,128)(2,1)S(1)}, u32[]{:S(2)}, u32[]{:S(2)}) collective-permute-start(bf16[64,128]{1,0:T(8,128)(2,1)S(1)} %get-tuple-element.155), channel_id=1, source_target_pairs={{0,24},{1,25},{2,26},{3,27},{4,28},{5,29},{6,30},{7,31},{8,16},{9,... | collective-permute-start | bytes 49160 | tf_op jit(solution)/shard_map/ppermute | solution.py:40
  98.5 2.0 %collective-permute-start.37 = (f32[256,512]{1,0:T(8,128)S(1)}, f32[256,512]{1,0:T(8,128)S(1)}, u32[]{:S(2)}, u32[]{:S(2)}) collective-permute-start(f32[256,512]{1,0:T(8,128)S(1)} %get-tuple-element.162), channel_id=1, source_target_pairs={{0,1},{1,0},{2,3},{3,2},{4,5},{5,4},{6,7},{7,6},{8,9},{9,8},{10,11... | collective-permute-start | bytes 1572872 | tf_op jit(solution)/shard_map/ppermute | solution.py:40
  101.3 4.2 %collective-permute-start.38 = (bf16[208,128]{1,0:T(8,128)(2,1)S(1)}, bf16[208,128]{1,0:T(8,128)(2,1)S(1)}, u32[]{:S(2)}, u32[]{:S(2)}) collective-permute-start(bf16[208,128]{1,0:T(8,128)(2,1)S(1)} %get-tuple-element.164), channel_id=1, source_target_pairs={{0,2},{1,3},{2,0},{3,1},{4,6},{5,7},{6,4},{7,5},{8,10},{9,11},{10,... | collective-permute-start | bytes 159752 | tf_op jit(solution)/shard_map/ppermute | solution.py:40
  102.6 4.7 %collective-permute-start.39 = (bf16[208,128]{1,0:T(8,128)(2,1)S(1)}, bf16[208,128]{1,0:T(8,128)(2,1)S(1)}, u32[]{:S(2)}, u32[]{:S(2)}) collective-permute-start(bf16[208,128]{1,0:T(8,128)(2,1)S(1)} %get-tuple-element.165), channel_id=1, source_target_pairs={{0,4},{1,5},{2,6},{3,7},{4,0},{5,1},{6,2},{7,3},{8,12},{9,13},{10,... | collective-permute-start | bytes 159752 | tf_op jit(solution)/shard_map/ppermute | solution.py:40
  103.2 5.0 %collective-permute-start.40 = (bf16[208,128]{1,0:T(8,128)(2,1)S(1)}, bf16[208,128]{1,0:T(8,128)(2,1)S(1)}, u32[]{:S(2)}, u32[]{:S(2)}) collective-permute-start(bf16[208,128]{1,0:T(8,128)(2,1)S(1)} %get-tuple-element.166), channel_id=1, source_target_pairs={{0,6},{1,7},{2,4},{3,5},{4,2},{5,3},{6,0},{7,1},{8,14},{9,15},{10,... | collective-permute-start | bytes 159752 | tf_op jit(solution)/shard_map/ppermute | solution.py:40
  109.1 6.8 %collective-permute-start.43 = (bf16[256,128]{1,0:T(8,128)(2,1)S(1)}, bf16[256,128]{1,0:T(8,128)(2,1)S(1)}, u32[]{:S(2)}, u32[]{:S(2)}) collective-permute-start(bf16[256,128]{1,0:T(8,128)(2,1)S(1)} %code.1.refs_0_), channel_id=1, source_target_pairs={{0,24},{1,25},{2,26},{3,27},{4,28},{5,29},{6,30},{7,31},{8,16},{9,... | collective-permute-start | bytes 196616 | tf_op jit(solution)/shard_map/ppermute | solution.py:40
  111.4 5.7 %collective-permute-start.42 = (bf16[256,128]{1,0:T(8,128)(2,1)S(1)}, bf16[256,128]{1,0:T(8,128)(2,1)S(1)}, u32[]{:S(2)}, u32[]{:S(2)}) collective-permute-start(bf16[256,128]{1,0:T(8,128)(2,1)S(1)} %code.1.refs_0_), channel_id=1, source_target_pairs={{0,16},{1,17},{2,18},{3,19},{4,20},{5,21},{6,22},{7,23},{8,24},{9,... | collective-permute-start | bytes 196616 | tf_op jit(solution)/shard_map/ppermute | solution.py:40
  111.4 5.7 %collective-permute-start.41 = (bf16[256,128]{1,0:T(8,128)(2,1)S(1)}, bf16[256,128]{1,0:T(8,128)(2,1)S(1)}, u32[]{:S(2)}, u32[]{:S(2)}) collective-permute-start(bf16[256,128]{1,0:T(8,128)(2,1)S(1)} %code.1.refs_0_), channel_id=1, source_target_pairs={{0,8},{1,9},{2,10},{3,11},{4,12},{5,13},{6,14},{7,15},{8,0},{9,1},... | collective-permute-start | bytes 196616 | tf_op jit(solution)/shard_map/ppermute | solution.py:40
  118.1 5.6 %collective-permute-start.46 = (bf16[128,384]{1,0:T(8,128)(2,1)S(1)}, bf16[128,384]{1,0:T(8,128)(2,1)S(1)}, u32[]{:S(2)}, u32[]{:S(2)}) collective-permute-start(bf16[128,384]{1,0:T(8,128)(2,1)S(1)} %finish.1.refs_0_), channel_id=1, source_target_pairs={{0,6},{1,7},{2,4},{3,5},{4,2},{5,3},{6,0},{7,1},{8,14},{9,15},{10,... | collective-permute-start | bytes 294920 | tf_op jit(solution)/shard_map/ppermute | solution.py:40
  119.6 5.1 %collective-permute-start.45 = (bf16[128,384]{1,0:T(8,128)(2,1)S(1)}, bf16[128,384]{1,0:T(8,128)(2,1)S(1)}, u32[]{:S(2)}, u32[]{:S(2)}) collective-permute-start(bf16[128,384]{1,0:T(8,128)(2,1)S(1)} %finish.1.refs_0_), channel_id=1, source_target_pairs={{0,4},{1,5},{2,6},{3,7},{4,0},{5,1},{6,2},{7,3},{8,12},{9,13},{10,... | collective-permute-start | bytes 294920 | tf_op jit(solution)/shard_map/ppermute | solution.py:40
  120.9 4.6 %collective-permute-start.44 = (bf16[128,384]{1,0:T(8,128)(2,1)S(1)}, bf16[128,384]{1,0:T(8,128)(2,1)S(1)}, u32[]{:S(2)}, u32[]{:S(2)}) collective-permute-start(bf16[128,384]{1,0:T(8,128)(2,1)S(1)} %finish.1.refs_0_), channel_id=1, source_target_pairs={{0,2},{1,3},{2,0},{3,1},{4,6},{5,7},{6,4},{7,5},{8,10},{9,11},{10,... | collective-permute-start | bytes 294920 | tf_op jit(solution)/shard_map/ppermute | solution.py:40
  121.7 3.9 %collective-permute-start.47 = (bf16[128,384]{1,0:T(8,128)(2,1)S(1)}, bf16[128,384]{1,0:T(8,128)(2,1)S(1)}, u32[]{:S(2)}, u32[]{:S(2)}) collective-permute-start(bf16[128,384]{1,0:T(8,128)(2,1)S(1)} %finish.1.refs_0_), channel_id=1, source_target_pairs={{0,1},{1,0},{2,3},{3,2},{4,5},{5,4},{6,7},{7,6},{8,9},{9,8},{10,11... | collective-permute-start | bytes 294920 | tf_op jit(solution)/shard_map/ppermute | solution.py:40
  123.7 1.8 %collective-permute-start.50 = (bf16[128,384]{1,0:T(8,128)(2,1)S(1)}, bf16[128,384]{1,0:T(8,128)(2,1)S(1)}, u32[]{:S(2)}, u32[]{:S(2)}) collective-permute-start(bf16[128,384]{1,0:T(8,128)(2,1)S(1)} %collective-permute-done.46.refs_3_), channel_id=1, source_target_pairs={{0,1},{1,0},{2,3},{3,2},{4,5},{5,4},{6,7},{7,6},{8,9},{9,8},{10,11... | collective-permute-start | bytes 294920 | tf_op jit(solution)/shard_map/ppermute | solution.py:40
  124.7 1.3 collective-permute-start.49
  125.5 1.3 collective-permute-start.48
  128.5 8.0 %collective-permute-start.51 = (bf16[128,256]{1,0:T(8,128)(2,1)S(1)}, bf16[128,256]{1,0:T(8,128)(2,1)S(1)}, u32[]{:S(2)}, u32[]{:S(2)}) collective-permute-start(bf16[128,256]{1,0:T(8,128)(2,1)S(1)} %get-tuple-element.176), channel_id=1, source_target_pairs={{0,24},{1,25},{2,26},{3,27},{4,28},{5,29},{6,30},{7,31},{8,16},{9,... | collective-permute-start | bytes 196616 | tf_op jit(solution)/shard_map/ppermute | solution.py:40
  130.4 10.8 %collective-permute-start.52 = (bf16[128,256]{1,0:T(8,128)(2,1)S(1)}, bf16[128,256]{1,0:T(8,128)(2,1)S(1)}, u32[]{:S(2)}, u32[]{:S(2)}) collective-permute-start(bf16[128,256]{1,0:T(8,128)(2,1)S(1)} %get-tuple-element.177), channel_id=1, source_target_pairs={{0,16},{1,17},{2,18},{3,19},{4,20},{5,21},{6,22},{7,23},{8,24},{9,... | collective-permute-start | bytes 196616 | tf_op jit(solution)/shard_map/ppermute | solution.py:40
  130.8 10.4 %collective-permute-start.53 = (bf16[128,256]{1,0:T(8,128)(2,1)S(1)}, bf16[128,256]{1,0:T(8,128)(2,1)S(1)}, u32[]{:S(2)}, u32[]{:S(2)}) collective-permute-start(bf16[128,256]{1,0:T(8,128)(2,1)S(1)} %get-tuple-element.178), channel_id=1, source_target_pairs={{0,8},{1,9},{2,10},{3,11},{4,12},{5,13},{6,14},{7,15},{8,0},{9,1},... | collective-permute-start | bytes 196616 | tf_op jit(solution)/shard_map/ppermute | solution.py:40
  134.7 7.8 %collective-permute-start.54 = (bf16[128,256]{1,0:T(8,128)(2,1)S(1)}, bf16[128,256]{1,0:T(8,128)(2,1)S(1)}, u32[]{:S(2)}, u32[]{:S(2)}) collective-permute-start(bf16[128,256]{1,0:T(8,128)(2,1)S(1)} %get-tuple-element.182), channel_id=1, source_target_pairs={{0,24},{1,25},{2,26},{3,27},{4,28},{5,29},{6,30},{7,31},{8,16},{9,... | collective-permute-start | bytes 196616 | tf_op jit(solution)/shard_map/ppermute | solution.py:40
  136.5 6.4 %collective-permute-start.55 = (bf16[128,256]{1,0:T(8,128)(2,1)S(1)}, bf16[128,256]{1,0:T(8,128)(2,1)S(1)}, u32[]{:S(2)}, u32[]{:S(2)}) collective-permute-start(bf16[128,256]{1,0:T(8,128)(2,1)S(1)} %get-tuple-element.183), channel_id=1, source_target_pairs={{0,16},{1,17},{2,18},{3,19},{4,20},{5,21},{6,22},{7,23},{8,24},{9,... | collective-permute-start | bytes 196616 | tf_op jit(solution)/shard_map/ppermute | solution.py:40
  136.5 6.4 %collective-permute-start.56 = (bf16[128,256]{1,0:T(8,128)(2,1)S(1)}, bf16[128,256]{1,0:T(8,128)(2,1)S(1)}, u32[]{:S(2)}, u32[]{:S(2)}) collective-permute-start(bf16[128,256]{1,0:T(8,128)(2,1)S(1)} %get-tuple-element.184), channel_id=1, source_target_pairs={{0,8},{1,9},{2,10},{3,11},{4,12},{5,13},{6,14},{7,15},{8,0},{9,1},... | collective-permute-start | bytes 196616 | tf_op jit(solution)/shard_map/ppermute | solution.py:40

commit v18 on v17

--- a/solution.py
+++ b/solution.py
@@ -490,8 +490,7 @@
                 ]
     blocks = [slice(i * width, (i + 1) * width) for i in range(BLOCKS)]
     for i in range(BLOCKS):
-        other = gram_ref[blocks[i - 1], blocks[i]].astype(F32).T
-        gram_ref[blocks[i], blocks[i - 1]] = other.astype(BF16)
+        gram_ref[blocks[i], blocks[i - 1]] = gram_ref[blocks[i - 1], blocks[i]].T
     share = jnp.zeros((1, 1), F32)
     if which == 1:
         tail = gram_ref[blocks[3], blocks[1]].astype(F32)

time: 145 us -> 145 us (level)
  no operation moved by 1% of the time
where the time goes in v18:
time: 145 us; the launch traced here: 144 us
  starting transfers between devices  60.8 us (42%)
  waiting for transfers between devices  45 us (31%)
  Pallas kernels  34.4 us (24%)
  local copies, waits for them, and re-layouts  1.91 us (1%)
    ppermute x57, starting transfers between devices, send(): return lax.ppermute(value, ('dp', 'mp'), pairs)  60.8 us
    ppermute x57, waiting for transfers between devices, send(): return lax.ppermute(value, ('dp', 'mp'), pairs)  45 us
    pallas_call x14, Pallas kernels, local(): pl.pallas_call(kernel, in_specs=[pl.BlockSpec(memory_space=pltpu.SMEM)] +...  15.1 us
    pallas_call x2, Pallas kernels, project(): pl.pallas_call(functools.partial(project_kernel, counts=counts, n=n, k=k)...  8.92 us
    pallas_call x2, Pallas kernels, normalize_parts(): pl.pallas_call(functools.partial(normalize_kernel, n=n, k=k, order=order,...  6.01 us
    pallas_call x2, Pallas kernels, fetch(): pl.pallas_call(fetch_kernel, in_specs=[pl.BlockSpec(memory_space=pl.ANY)]...  4.39 us
  transfers between devices with their start and end apart: 57, of which 23 were waited for; matrix products, arithmetic and copies ran while one was open for 1% of the time, Pallas kernels for 18%

profile of v18, /device:TPU:0, one launch (start us, length us, event | category | flops | bytes accessed | tf_op | source)
XLA Modules:
  0.0 144.2 jit_solution(3267654281414355010)
XLA Ops:
  0.7 1.0 dynamic-slice_bitcast_fusion.4
  1.6 4.0 %collective-permute-start.10 = (bf16[32,1024]{1,0:T(8,128)(2,1)S(1)}, bf16[32,1024]{1,0:T(8,128)(2,1)S(1)}, u32[]{:S(2)}, u32[]{:S(2)}) collective-permute-start(bf16[32,1024]{1,0:T(8,128)(2,1)S(1)} %get-tuple-element.196), channel_id=1, source_target_pairs={{0,6},{1,7},{2,4},{3,5},{4,2},{5,3},{6,0},{7,1},{8,14},{9,15},{10,... | collective-permute-start | bytes 196616 | tf_op jit(solution)/shard_map/ppermute | solution.py:40
  6.2 1.0 dynamic-slice_bitcast_fusion
  7.2 2.9 %collective-permute-start.16 = (bf16[32,1024]{1,0:T(8,128)(2,1)S(1)}, bf16[32,1024]{1,0:T(8,128)(2,1)S(1)}, u32[]{:S(2)}, u32[]{:S(2)}) collective-permute-start(bf16[32,1024]{1,0:T(8,128)(2,1)S(1)} %get-tuple-element.192), channel_id=1, source_target_pairs={{0,6},{1,7},{2,4},{3,5},{4,2},{5,3},{6,0},{7,1},{8,14},{9,15},{10,... | collective-permute-start | bytes 196616 | tf_op jit(solution)/shard_map/ppermute | solution.py:40
  11.4 2.0 %collective-permute-start.11 = (bf16[32,1024]{1,0:T(8,128)(2,1)S(1)}, bf16[32,1024]{1,0:T(8,128)(2,1)S(1)}, u32[]{:S(2)}, u32[]{:S(2)}) collective-permute-start(bf16[32,1024]{1,0:T(8,128)(2,1)S(1)} %get-tuple-element.113), channel_id=1, source_target_pairs={{0,8},{1,9},{2,10},{3,11},{4,12},{5,13},{6,14},{7,15},{8,0},{9,1},... | collective-permute-start | bytes 196616 | tf_op jit(solution)/shard_map/ppermute | solution.py:40
  13.5 2.6 %collective-permute-start.12 = (bf16[32,1024]{1,0:T(8,128)(2,1)S(1)}, bf16[32,1024]{1,0:T(8,128)(2,1)S(1)}, u32[]{:S(2)}, u32[]{:S(2)}) collective-permute-start(bf16[32,1024]{1,0:T(8,128)(2,1)S(1)} %get-tuple-element.114), channel_id=1, source_target_pairs={{0,16},{1,17},{2,18},{3,19},{4,20},{5,21},{6,22},{7,23},{8,24},{9,... | collective-permute-start | bytes 196616 | tf_op jit(solution)/shard_map/ppermute | solution.py:40
  16.6 3.4 %collective-permute-done.12.refs_2_ = bf16[32,1024]{1,0:T(8,128)(2,1)S(1)} collective-permute-done((bf16[32,1024]{1,0:T(8,128)(2,1)S(1)}, bf16[32,1024]{1,0:T(8,128)(2,1)S(1)}, u32[]{:S(2)}, u32[]{:S(2)}) %collective-permute-start.12) | collective-permute-done | bytes 65568 | tf_op jit(solution)/shard_map/ppermute | solution.py:40
  20.0 2.1 %collective-permute-done.13.refs_1_ = bf16[32,1024]{1,0:T(8,128)(2,1)S(1)} collective-permute-done((bf16[32,1024]{1,0:T(8,128)(2,1)S(1)}, bf16[32,1024]{1,0:T(8,128)(2,1)S(1)}, u32[]{:S(2)}, u32[]{:S(2)}) %collective-permute-start.13) | collective-permute-done | bytes 65568 | tf_op jit(solution)/shard_map/ppermute | solution.py:40
  22.7 2.5 %collective-permute-start.19 = (bf16[128,1024]{1,0:T(8,128)(2,1)S(1)}, bf16[128,1024]{1,0:T(8,128)(2,1)S(1)}, u32[]{:S(2)}, u32[]{:S(2)}) collective-permute-start(bf16[128,1024]{1,0:T(8,128)(2,1)S(1)} %lay.2.refs_0_), channel_id=1, source_target_pairs={{0,6},{1,7},{2,4},{3,5},{4,2},{5,3},{6,0},{7,1},{8,14},{9,15},{10,... | collective-permute-start | bytes 786440 | tf_op jit(solution)/shard_map/ppermute | solution.py:40
  26.3 0.9 collective-permute-start.22
  27.2 5.4 %collective-permute-done.22.refs_1_ = bf16[32,1024]{1,0:T(8,128)(2,1)S(1)} collective-permute-done((bf16[32,1024]{1,0:T(8,128)(2,1)S(1)}, bf16[32,1024]{1,0:T(8,128)(2,1)S(1)}, u32[]{:S(2)}, u32[]{:S(2)}) %collective-permute-start.22) | collective-permute-done | bytes 65568 | tf_op jit(solution)/shard_map/ppermute | solution.py:40
  32.5 2.2 %fetch.3.refs_8_ = bf16[2048,1024]{1,0:T(8,128)(2,1)S(1)} custom-call(bf16[2048,1024]{1,0:T(8,128)(2,1)} %weight_ref), custom_call_target="tpu_custom_call" | custom-call | bytes 8388608 | tf_op jit(solution)/shard_map/fetch/pallas_call | solution.py:265
  34.7 2.9 %collective-permute-done.21.refs_2_ = bf16[32,1024]{1,0:T(8,128)(2,1)S(1)} collective-permute-done((bf16[32,1024]{1,0:T(8,128)(2,1)S(1)}, bf16[32,1024]{1,0:T(8,128)(2,1)S(1)}, u32[]{:S(2)}, u32[]{:S(2)}) %collective-permute-start.21) | collective-permute-done | bytes 65568 | tf_op jit(solution)/shard_map/ppermute | solution.py:40
  39.3 2.5 %collective-permute-start.27 = (bf16[128,1024]{1,0:T(8,128)(2,1)S(1)}, bf16[128,1024]{1,0:T(8,128)(2,1)}, u32[]{:S(2)}, u32[]{:S(2)}) collective-permute-start(bf16[128,1024]{1,0:T(8,128)(2,1)S(1)} %lay.3), channel_id=1, source_target_pairs={{0,6},{1,7},{2,4},{3,5},{4,2},{5,3},{6,0},{7,1},{8,14},{9,15},{10,... | collective-permute-start | bytes 786440 | tf_op jit(solution)/shard_map/ppermute | solution.py:40
  41.9 3.9 %project.3 = (f32[512,256]{1,0:T(8,128)S(1)}, bf16[528,256]{1,0:T(8,128)(2,1)S(1)}, bf16[528,256]{1,0:T(8,128)(2,1)S(1)}, bf16[528,256]{1,0:T(8,128)(2,1)S(1)}) custom-call(s32[3]{0:T(128)S(1)} %pad_add_fusion.place_ref, bf16[128,1024]{1,0:T(8,128)(2,1)S(1)} %lay.2.refs_0_, bf16[128,1024]{1,0:T(8,128)(2,1)S(1)} %collective-permute-done.17.refs_1_, ...), custom_call_target="tpu_custom_call" | custom-call | flops 2147483648 | bytes 7864320 | tf_op jit(solution)/shard_map/project/pallas_call | solution.py:378
  45.8 1.7 %collective-permute-start.31 = (bf16[528,256]{1,0:T(8,128)(2,1)S(1)}, bf16[528,256]{1,0:T(8,128)(2,1)S(1)}, u32[]{:S(2)}, u32[]{:S(2)}) collective-permute-start(bf16[528,256]{1,0:T(8,128)(2,1)S(1)} %get-tuple-element.147), channel_id=1, source_target_pairs={{0,24},{1,25},{2,26},{3,27},{4,28},{5,29},{6,30},{7,31},{8,16},{9,... | collective-permute-start | bytes 811016 | tf_op jit(solution)/shard_map/ppermute | solution.py:40
  47.5 2.8 %collective-permute-start.33 = (bf16[528,256]{1,0:T(8,128)(2,1)S(1)}, bf16[528,256]{1,0:T(8,128)(2,1)S(1)}, u32[]{:S(2)}, u32[]{:S(2)}) collective-permute-start(bf16[528,256]{1,0:T(8,128)(2,1)S(1)} %get-tuple-element.149), channel_id=1, source_target_pairs={{0,8},{1,9},{2,10},{3,11},{4,12},{5,13},{6,14},{7,15},{8,0},{9,1},... | collective-permute-start | bytes 811016 | tf_op jit(solution)/shard_map/ppermute | solution.py:40
  50.2 16.4 %conditional.2 = (f32[512,256]{1,0:T(8,128)S(1)}, bf16[528,256]{1,0:T(8,128)(2,1)}, bf16[528,256]{1,0:T(8,128)(2,1)}, bf16[528,256]{1,0:T(8,128)(2,1)}) conditional(s32[]{:T(128)} %convert_element_type.4, () %tuple.35, (bf16[128,1024]{1,0:T(8,128)(2,1)S(1)}, bf16[128,1024]{1,0:T(8,128)(2,1)}, bf16[2048,1024]{1,0:T(8,128)(2,1)}, s32[3]{0:T(128)S(1)}) %tuple.36), branch_computations={%region_0.1_spmd, %region_1.2_spmd} | conditional | flops 2149580800 | bytes 24641728 | solution.py:232
  50.8 1.0 collective-permute-start.5
  51.8 5.6 %collective-permute-done.4.refs_2_ = bf16[128,1024]{1,0:T(8,128)(2,1)S(1)} collective-permute-done((bf16[128,1024]{1,0:T(8,128)(2,1)S(1)}, bf16[128,1024]{1,0:T(8,128)(2,1)S(1)}, u32[]{:S(2)}, u32[]{:S(2)}) %collective-permute-start.4) | collective-permute-done | bytes 262176 | tf_op jit(solution)/shard_map/cond/branch_1_fun/ppermute | solution.py:40
  57.8 1.0 pad_maximum_fusion
  59.4 2.2 %fetch.2.refs_6_ = bf16[2048,1024]{1,0:T(8,128)(2,1)S(1)} custom-call(bf16[2048,1024]{1,0:T(8,128)(2,1)} %get-tuple-element.19.weight_ref), custom_call_target="tpu_custom_call" | custom-call | bytes 8388608 | tf_op jit(solution)/shard_map/cond/branch_1_fun/fetch/pallas_call | solution.py:265
  61.6 5.0 %project.2 = (f32[512,256]{1,0:T(8,128)S(1)}, bf16[528,256]{1,0:T(8,128)(2,1)}, bf16[528,256]{1,0:T(8,128)(2,1)}, bf16[528,256]{1,0:T(8,128)(2,1)}) custom-call(s32[3]{0:T(128)S(1)} %get-tuple-element.14.place_ref, bf16[128,1024]{1,0:T(8,128)(2,1)S(1)} %get-tuple-element.16.refs_0_, bf16[128,1024]{1,0:T(8,128)(2,1)} %get-tuple-element.17.refs_1_, ...), custom_call_target="tpu_custom_call" | custom-call | flops 2147483648 | bytes 7864320 | tf_op jit(solution)/shard_map/cond/branch_1_fun/project/pallas_call | solution.py:378
  66.9 1.8 %collective-permute-start.29 = (bf16[528,256]{1,0:T(8,128)(2,1)}, bf16[528,256]{1,0:T(8,128)(2,1)S(1)}, u32[]{:S(2)}, u32[]{:S(2)}) collective-permute-start(bf16[528,256]{1,0:T(8,128)(2,1)} %get-tuple-element.144), channel_id=1, source_target_pairs={{0,16},{1,17},{2,18},{3,19},{4,20},{5,21},{6,22},{7,23},{8,24},{9,... | collective-permute-start | bytes 811016 | tf_op jit(solution)/shard_map/ppermute | solution.py:40
  68.8 2.3 %collective-permute-start.30 = (bf16[528,256]{1,0:T(8,128)(2,1)}, bf16[528,256]{1,0:T(8,128)(2,1)S(1)}, u32[]{:S(2)}, u32[]{:S(2)}) collective-permute-start(bf16[528,256]{1,0:T(8,128)(2,1)} %get-tuple-element.145), channel_id=1, source_target_pairs={{0,24},{1,25},{2,26},{3,27},{4,28},{5,29},{6,30},{7,31},{8,16},{9,... | collective-permute-start | bytes 811016 | tf_op jit(solution)/shard_map/ppermute | solution.py:40
  71.0 3.4 %normalize.2 = (f32[512,256]{1,0:T(8,128)S(1)}, bf16[512,256]{1,0:T(8,128)(2,1)S(1)}, f32[1,256]{1,0:T(1,128)S(1)}, f32[256,512]{1,0:T(8,128)}, f32[256,512]{1,0:T(8,128)}) custom-call(s32[3]{0:T(128)S(1)} %pad_add_fusion.place_ref, f32[512,256]{1,0:T(8,128)S(1)} %get-tuple-element.146.refs_0_, bf16[528,256]{1,0:T(8,128)(2,1)S(1)} %collective-permute-done.31.refs_1_, ...), custom_call_target="tpu_custom_call" | custom-call | flops 134217728 | bytes 3145728 | tf_op jit(solution)/shard_map/normalize/pallas_call | solution.py:458
  74.4 13.5 %conditional.3 = ((f32[16,384]{1,0:T(8,128)S(1)}, bf16[64,128]{1,0:T(8,128)(2,1)S(1)}, bf16[64,128]{1,0:T(8,128)(2,1)S(1)}, bf16[64,128]{1,0:T(8,128)(2,1)S(1)})) conditional(s32[]{:T(128)} %convert_element_type.4, () %tuple.38, (f32[256,512]{1,0:T(8,128)}, s32[3]{0:T(128)S(1)}, f32[256,512]{1,0:T(8,128)}) %tuple.39), branch_computations={%region_2.3_spmd, %region_3.4_spmd} | conditional | bytes 2736296 | solution.py:232
  74.4 2.1 %collective-permute-done.met_ref = f32[256,512]{1,0:T(8,128)S(1)} collective-permute-done((f32[256,512]{1,0:T(8,128)}, f32[256,512]{1,0:T(8,128)S(1)}, u32[]{:S(2)}, u32[]{:S(2)}) %collective-permute-start) | collective-permute-done | bytes 524320 | tf_op jit(solution)/shard_map/cond/branch_1_fun/ppermute | solution.py:40
  76.5 1.3 halve.2
  77.8 1.6 %collective-permute-start.1 = (bf16[208,128]{1,0:T(8,128)(2,1)S(1)}, bf16[208,128]{1,0:T(8,128)(2,1)S(1)}, u32[]{:S(2)}, u32[]{:S(2)}) collective-permute-start(bf16[208,128]{1,0:T(8,128)(2,1)S(1)} %get-tuple-element.28), channel_id=1, source_target_pairs={{0,2},{1,3},{2,0},{3,1},{4,6},{5,7},{6,4},{7,5},{8,10},{9,11},{10,... | collective-permute-start | bytes 159752 | tf_op jit(solution)/shard_map/cond/branch_1_fun/ppermute | solution.py:40
  79.9 2.1 %collective-permute-done.1.refs_1_ = bf16[208,128]{1,0:T(8,128)(2,1)S(1)} collective-permute-done((bf16[208,128]{1,0:T(8,128)(2,1)S(1)}, bf16[208,128]{1,0:T(8,128)(2,1)S(1)}, u32[]{:S(2)}, u32[]{:S(2)}) %collective-permute-start.1) | collective-permute-done | bytes 53280 | tf_op jit(solution)/shard_map/cond/branch_1_fun/ppermute | solution.py:40
  82.0 1.4 collective-permute-start.3
  83.5 3.5 %collective-permute-done.3.refs_3_ = bf16[208,128]{1,0:T(8,128)(2,1)S(1)} collective-permute-done((bf16[208,128]{1,0:T(8,128)(2,1)S(1)}, bf16[208,128]{1,0:T(8,128)(2,1)S(1)}, u32[]{:S(2)}, u32[]{:S(2)}) %collective-permute-start.3) | collective-permute-done | bytes 53280 | tf_op jit(solution)/shard_map/cond/branch_1_fun/ppermute | solution.py:40
  87.1 0.8 plane.1
  88.0 2.4 %collective-permute-start.35 = (bf16[64,128]{1,0:T(8,128)(2,1)S(1)}, bf16[64,128]{1,0:T(8,128)(2,1)S(1)}, u32[]{:S(2)}, u32[]{:S(2)}) collective-permute-start(bf16[64,128]{1,0:T(8,128)(2,1)S(1)} %get-tuple-element.154), channel_id=1, source_target_pairs={{0,16},{1,17},{2,18},{3,19},{4,20},{5,21},{6,22},{7,23},{8,24},{9,... | collective-permute-start | bytes 49160 | tf_op jit(solution)/shard_map/ppermute | solution.py:40
  90.4 2.0 %collective-permute-start.36 = (bf16[64,128]{1,0:T(8,128)(2,1)S(1)}, bf16[64,128]{1,0:T(8,128)(2,1)S(1)}, u32[]{:S(2)}, u32[]{:S(2)}) collective-permute-start(bf16[64,128]{1,0:T(8,128)(2,1)S(1)} %get-tuple-element.155), channel_id=1, source_target_pairs={{0,24},{1,25},{2,26},{3,27},{4,28},{5,29},{6,30},{7,31},{8,16},{9,... | collective-permute-start | bytes 49160 | tf_op jit(solution)/shard_map/ppermute | solution.py:40
  92.4 2.2 %collective-permute-done.35.refs_2_ = bf16[64,128]{1,0:T(8,128)(2,1)S(1)} collective-permute-done((bf16[64,128]{1,0:T(8,128)(2,1)S(1)}, bf16[64,128]{1,0:T(8,128)(2,1)S(1)}, u32[]{:S(2)}, u32[]{:S(2)}) %collective-permute-start.35) | collective-permute-done | bytes 16416 | tf_op jit(solution)/shard_map/ppermute | solution.py:40
  94.6 1.3 collective-permute-done.36.refs_3_
  95.9 2.6 %normalize.3 = (f32[512,256]{1,0:T(8,128)S(1)}, bf16[512,256]{1,0:T(8,128)(2,1)S(1)}, f32[1,256]{1,0:T(1,128)S(1)}, f32[256,512]{1,0:T(8,128)S(1)}, f32[256,512]{1,0:T(8,128)S(1)}, /*index=5*/f32[1,256]{1,0:T(1,128)S(1)}) custom-call(s32[3]{0:T(128)S(1)} %pad_add_fusion.place_ref, f32[512,256]{1,0:T(8,128)S(1)} %get-tuple-element.156.refs_0_, ...), custom_call_target="tpu_custom_call" | custom-call | flops 134217728 | bytes 3145728 | tf_op jit(solution)/shard_map/normalize/pallas_call | solution.py:458
  98.6 1.9 %collective-permute-done.37.met_ref = f32[256,512]{1,0:T(8,128)S(1)} collective-permute-done((f32[256,512]{1,0:T(8,128)S(1)}, f32[256,512]{1,0:T(8,128)S(1)}, u32[]{:S(2)}, u32[]{:S(2)}) %collective-permute-start.37) | collective-permute-done | bytes 524320 | tf_op jit(solution)/shard_map/ppermute | solution.py:40
  100.5 0.8 halve.3
  101.3 1.3 collective-permute-start.38
  103.2 1.7 %collective-permute-start.40 = (bf16[208,128]{1,0:T(8,128)(2,1)S(1)}, bf16[208,128]{1,0:T(8,128)(2,1)S(1)}, u32[]{:S(2)}, u32[]{:S(2)}) collective-permute-start(bf16[208,128]{1,0:T(8,128)(2,1)S(1)} %get-tuple-element.166), channel_id=1, source_target_pairs={{0,6},{1,7},{2,4},{3,5},{4,2},{5,3},{6,0},{7,1},{8,14},{9,15},{10,... | collective-permute-start | bytes 159752 | tf_op jit(solution)/shard_map/ppermute | solution.py:40
  105.5 1.8 %collective-permute-done.39.refs_2_ = bf16[208,128]{1,0:T(8,128)(2,1)S(1)} collective-permute-done((bf16[208,128]{1,0:T(8,128)(2,1)S(1)}, bf16[208,128]{1,0:T(8,128)(2,1)S(1)}, u32[]{:S(2)}, u32[]{:S(2)}) %collective-permute-start.39) | collective-permute-done | bytes 53280 | tf_op jit(solution)/shard_map/ppermute | solution.py:40
  107.4 0.8 collective-permute-done.40.refs_3_
  108.2 0.8 code.1.refs_0_
  109.1 2.3 %collective-permute-start.43 = (bf16[256,128]{1,0:T(8,128)(2,1)S(1)}, bf16[256,128]{1,0:T(8,128)(2,1)S(1)}, u32[]{:S(2)}, u32[]{:S(2)}) collective-permute-start(bf16[256,128]{1,0:T(8,128)(2,1)S(1)} %code.1.refs_0_), channel_id=1, source_target_pairs={{0,24},{1,25},{2,26},{3,27},{4,28},{5,29},{6,30},{7,31},{8,16},{9,... | collective-permute-start | bytes 196616 | tf_op jit(solution)/shard_map/ppermute | solution.py:40
  111.4 2.1 %collective-permute-start.41 = (bf16[256,128]{1,0:T(8,128)(2,1)S(1)}, bf16[256,128]{1,0:T(8,128)(2,1)S(1)}, u32[]{:S(2)}, u32[]{:S(2)}) collective-permute-start(bf16[256,128]{1,0:T(8,128)(2,1)S(1)} %code.1.refs_0_), channel_id=1, source_target_pairs={{0,8},{1,9},{2,10},{3,11},{4,12},{5,13},{6,14},{7,15},{8,0},{9,1},... | collective-permute-start | bytes 196616 | tf_op jit(solution)/shard_map/ppermute | solution.py:40
  113.5 2.3 %collective-permute-done.43.refs_3_ = bf16[256,128]{1,0:T(8,128)(2,1)S(1)} collective-permute-done((bf16[256,128]{1,0:T(8,128)(2,1)S(1)}, bf16[256,128]{1,0:T(8,128)(2,1)S(1)}, u32[]{:S(2)}, u32[]{:S(2)}) %collective-permute-start.43) | collective-permute-done | bytes 65568 | tf_op jit(solution)/shard_map/ppermute | solution.py:40
  115.8 1.3 collective-permute-done.42.refs_2_
  117.1 1.0 finish.1.refs_0_
  118.1 1.6 %collective-permute-start.46 = (bf16[128,384]{1,0:T(8,128)(2,1)S(1)}, bf16[128,384]{1,0:T(8,128)(2,1)S(1)}, u32[]{:S(2)}, u32[]{:S(2)}) collective-permute-start(bf16[128,384]{1,0:T(8,128)(2,1)S(1)} %finish.1.refs_0_), channel_id=1, source_target_pairs={{0,6},{1,7},{2,4},{3,5},{4,2},{5,3},{6,0},{7,1},{8,14},{9,15},{10,... | collective-permute-start | bytes 294920 | tf_op jit(solution)/shard_map/ppermute | solution.py:40
  119.6 1.2 collective-permute-start.45
  121.7 2.1 %collective-permute-done.46.refs_3_ = bf16[128,384]{1,0:T(8,128)(2,1)S(1)} collective-permute-done((bf16[128,384]{1,0:T(8,128)(2,1)S(1)}, bf16[128,384]{1,0:T(8,128)(2,1)S(1)}, u32[]{:S(2)}, u32[]{:S(2)}) %collective-permute-start.46) | collective-permute-done | bytes 98336 | tf_op jit(solution)/shard_map/ppermute | solution.py:40
  123.7 1.0 collective-permute-done.45.refs_2_
  126.8 1.7 %gradient.2 = (bf16[128,256]{1,0:T(8,128)(2,1)S(1)}, bf16[128,256]{1,0:T(8,128)(2,1)S(1)}, bf16[128,256]{1,0:T(8,128)(2,1)S(1)}, bf16[128,256]{1,0:T(8,128)(2,1)...) custom-call(s32[3]{0:T(128)S(1)} %pad_add_fusion.place_ref, bf16[128,384]{1,0:T(8,128)(2,1)S(1)} %finish.1.refs_0_, ...), custom_call_target="tpu_custom_call" | custom-call | tf_op jit(solution)/shard_map/gradient/pallas_call | solution.py:190
  128.5 1.8 %collective-permute-start.51 = (bf16[128,256]{1,0:T(8,128)(2,1)S(1)}, bf16[128,256]{1,0:T(8,128)(2,1)S(1)}, u32[]{:S(2)}, u32[]{:S(2)}) collective-permute-start(bf16[128,256]{1,0:T(8,128)(2,1)S(1)} %get-tuple-element.176), channel_id=1, source_target_pairs={{0,24},{1,25},{2,26},{3,27},{4,28},{5,29},{6,30},{7,31},{8,16},{9,... | collective-permute-start | bytes 196616 | tf_op jit(solution)/shard_map/ppermute | solution.py:40
  130.7 2.2 %collective-permute-start.53 = (bf16[128,256]{1,0:T(8,128)(2,1)S(1)}, bf16[128,256]{1,0:T(8,128)(2,1)S(1)}, u32[]{:S(2)}, u32[]{:S(2)}) collective-permute-start(bf16[128,256]{1,0:T(8,128)(2,1)S(1)} %get-tuple-element.178), channel_id=1, source_target_pairs={{0,8},{1,9},{2,10},{3,11},{4,12},{5,13},{6,14},{7,15},{8,0},{9,1},... | collective-permute-start | bytes 196616 | tf_op jit(solution)/shard_map/ppermute | solution.py:40
  132.9 1.7 %gradient.3 = (bf16[128,256]{1,0:T(8,128)(2,1)S(1)}, bf16[128,256]{1,0:T(8,128)(2,1)S(1)}, bf16[128,256]{1,0:T(8,128)(2,1)S(1)}, bf16[128,256]{1,0:T(8,128)(2,1)...) custom-call(s32[3]{0:T(128)S(1)} %pad_add_fusion.place_ref, bf16[128,384]{1,0:T(8,128)(2,1)S(1)} %finish.1.refs_0_, ...), custom_call_target="tpu_custom_call" | custom-call | tf_op jit(solution)/shard_map/gradient/pallas_call | solution.py:190
  134.6 1.8 %collective-permute-start.54 = (bf16[128,256]{1,0:T(8,128)(2,1)S(1)}, bf16[128,256]{1,0:T(8,128)(2,1)S(1)}, u32[]{:S(2)}, u32[]{:S(2)}) collective-permute-start(bf16[128,256]{1,0:T(8,128)(2,1)S(1)} %get-tuple-element.182), channel_id=1, source_target_pairs={{0,24},{1,25},{2,26},{3,27},{4,28},{5,29},{6,30},{7,31},{8,16},{9,... | collective-permute-start | bytes 196616 | tf_op jit(solution)/shard_map/ppermute | solution.py:40
  136.4 2.5 %collective-permute-start.56 = (bf16[128,256]{1,0:T(8,128)(2,1)S(1)}, bf16[128,256]{1,0:T(8,128)(2,1)S(1)}, u32[]{:S(2)}, u32[]{:S(2)}) collective-permute-start(bf16[128,256]{1,0:T(8,128)(2,1)S(1)} %get-tuple-element.184), channel_id=1, source_target_pairs={{0,8},{1,9},{2,10},{3,11},{4,12},{5,13},{6,14},{7,15},{8,0},{9,1},... | collective-permute-start | bytes 196616 | tf_op jit(solution)/shard_map/ppermute | solution.py:40
  139.0 2.1 %loss.1 = f32[1,1]{1,0:T(1,128)} custom-call(s32[3]{0:T(128)S(1)} %pad_add_fusion.place_ref, bf16[512,512]{1,0:T(8,128)(2,1)S(1)} %get-tuple-element.185.first_ref, bf16[512,512]{1,0:T(8,128)(2,1)S(1)} %get-tuple-element.186.second_ref, f32[1,1]{1,0:T(1,128)} %get-tuple-element.187.share_ref), custom_call_target="tpu_custom_call" | custom-call | tf_op jit(solution)/shard_map/loss/pallas_call | solution.py:190
  141.1 1.3 place.2
  142.9 1.3 place.3
  (78 shorter events, 13.3 us)
Async XLA Ops:
  1.6 9.1 %collective-permute-start.10 = (bf16[32,1024]{1,0:T(8,128)(2,1)S(1)}, bf16[32,1024]{1,0:T(8,128)(2,1)S(1)}, u32[]{:S(2)}, u32[]{:S(2)}) collective-permute-start(bf16[32,1024]{1,0:T(8,128)(2,1)S(1)} %get-tuple-element.196), channel_id=1, source_target_pairs={{0,6},{1,7},{2,4},{3,5},{4,2},{5,3},{6,0},{7,1},{8,14},{9,15},{10,... | collective-permute-start | bytes 196616 | tf_op jit(solution)/shard_map/ppermute | solution.py:40
  5.6 5.2 %collective-permute-start.9 = (bf16[32,1024]{1,0:T(8,128)(2,1)S(1)}, bf16[32,1024]{1,0:T(8,128)(2,1)S(1)}, u32[]{:S(2)}, u32[]{:S(2)}) collective-permute-start(bf16[32,1024]{1,0:T(8,128)(2,1)S(1)} %get-tuple-element.197), channel_id=1, source_target_pairs={{0,4},{1,5},{2,6},{3,7},{4,0},{5,1},{6,2},{7,3},{8,12},{9,13},{10,... | collective-permute-start | bytes 196616 | tf_op jit(solution)/shard_map/ppermute | solution.py:40
  6.1 4.7 %collective-permute-start.8 = (bf16[32,1024]{1,0:T(8,128)(2,1)S(1)}, bf16[32,1024]{1,0:T(8,128)(2,1)S(1)}, u32[]{:S(2)}, u32[]{:S(2)}) collective-permute-start(bf16[32,1024]{1,0:T(8,128)(2,1)S(1)} %get-tuple-element.198), channel_id=1, source_target_pairs={{0,2},{1,3},{2,0},{3,1},{4,6},{5,7},{6,4},{7,5},{8,10},{9,11},{10,... | collective-permute-start | bytes 196616 | tf_op jit(solution)/shard_map/ppermute | solution.py:40
  7.2 8.9 %collective-permute-start.16 = (bf16[32,1024]{1,0:T(8,128)(2,1)S(1)}, bf16[32,1024]{1,0:T(8,128)(2,1)S(1)}, u32[]{:S(2)}, u32[]{:S(2)}) collective-permute-start(bf16[32,1024]{1,0:T(8,128)(2,1)S(1)} %get-tuple-element.192), channel_id=1, source_target_pairs={{0,6},{1,7},{2,4},{3,5},{4,2},{5,3},{6,0},{7,1},{8,14},{9,15},{10,... | collective-permute-start | bytes 196616 | tf_op jit(solution)/shard_map/ppermute | solution.py:40
  10.1 6.5 %collective-permute-start.15 = (bf16[32,1024]{1,0:T(8,128)(2,1)S(1)}, bf16[32,1024]{1,0:T(8,128)(2,1)S(1)}, u32[]{:S(2)}, u32[]{:S(2)}) collective-permute-start(bf16[32,1024]{1,0:T(8,128)(2,1)S(1)} %get-tuple-element.193), channel_id=1, source_target_pairs={{0,4},{1,5},{2,6},{3,7},{4,0},{5,1},{6,2},{7,3},{8,12},{9,13},{10,... | collective-permute-start | bytes 196616 | tf_op jit(solution)/shard_map/ppermute | solution.py:40
  10.7 5.9 %collective-permute-start.14 = (bf16[32,1024]{1,0:T(8,128)(2,1)S(1)}, bf16[32,1024]{1,0:T(8,128)(2,1)S(1)}, u32[]{:S(2)}, u32[]{:S(2)}) collective-permute-start(bf16[32,1024]{1,0:T(8,128)(2,1)S(1)} %get-tuple-element.194), channel_id=1, source_target_pairs={{0,2},{1,3},{2,0},{3,1},{4,6},{5,7},{6,4},{7,5},{8,10},{9,11},{10,... | collective-permute-start | bytes 196616 | tf_op jit(solution)/shard_map/ppermute | solution.py:40
  11.4 5.2 %collective-permute-start.11 = (bf16[32,1024]{1,0:T(8,128)(2,1)S(1)}, bf16[32,1024]{1,0:T(8,128)(2,1)S(1)}, u32[]{:S(2)}, u32[]{:S(2)}) collective-permute-start(bf16[32,1024]{1,0:T(8,128)(2,1)S(1)} %get-tuple-element.113), channel_id=1, source_target_pairs={{0,8},{1,9},{2,10},{3,11},{4,12},{5,13},{6,14},{7,15},{8,0},{9,1},... | collective-permute-start | bytes 196616 | tf_op jit(solution)/shard_map/ppermute | solution.py:40
  13.5 6.6 %collective-permute-start.12 = (bf16[32,1024]{1,0:T(8,128)(2,1)S(1)}, bf16[32,1024]{1,0:T(8,128)(2,1)S(1)}, u32[]{:S(2)}, u32[]{:S(2)}) collective-permute-start(bf16[32,1024]{1,0:T(8,128)(2,1)S(1)} %get-tuple-element.114), channel_id=1, source_target_pairs={{0,16},{1,17},{2,18},{3,19},{4,20},{5,21},{6,22},{7,23},{8,24},{9,... | collective-permute-start | bytes 196616 | tf_op jit(solution)/shard_map/ppermute | solution.py:40
  16.1 6.1 %collective-permute-start.13 = (bf16[32,1024]{1,0:T(8,128)(2,1)S(1)}, bf16[32,1024]{1,0:T(8,128)(2,1)S(1)}, u32[]{:S(2)}, u32[]{:S(2)}) collective-permute-start(bf16[32,1024]{1,0:T(8,128)(2,1)S(1)} %get-tuple-element.115), channel_id=1, source_target_pairs={{0,24},{1,25},{2,26},{3,27},{4,28},{5,29},{6,30},{7,31},{8,16},{9,... | collective-permute-start | bytes 196616 | tf_op jit(solution)/shard_map/ppermute | solution.py:40
  22.7 15.0 %collective-permute-start.19 = (bf16[128,1024]{1,0:T(8,128)(2,1)S(1)}, bf16[128,1024]{1,0:T(8,128)(2,1)S(1)}, u32[]{:S(2)}, u32[]{:S(2)}) collective-permute-start(bf16[128,1024]{1,0:T(8,128)(2,1)S(1)} %lay.2.refs_0_), channel_id=1, source_target_pairs={{0,6},{1,7},{2,4},{3,5},{4,2},{5,3},{6,0},{7,1},{8,14},{9,15},{10,... | collective-permute-start | bytes 786440 | tf_op jit(solution)/shard_map/ppermute | solution.py:40
  25.2 12.5 %collective-permute-start.18 = (bf16[128,1024]{1,0:T(8,128)(2,1)S(1)}, bf16[128,1024]{1,0:T(8,128)(2,1)S(1)}, u32[]{:S(2)}, u32[]{:S(2)}) collective-permute-start(bf16[128,1024]{1,0:T(8,128)(2,1)S(1)} %lay.2.refs_0_), channel_id=1, source_target_pairs={{0,4},{1,5},{2,6},{3,7},{4,0},{5,1},{6,2},{7,3},{8,12},{9,13},{10,... | collective-permute-start | bytes 786440 | tf_op jit(solution)/shard_map/ppermute | solution.py:40
  25.7 12.0 %collective-permute-start.17 = (bf16[128,1024]{1,0:T(8,128)(2,1)S(1)}, bf16[128,1024]{1,0:T(8,128)(2,1)S(1)}, u32[]{:S(2)}, u32[]{:S(2)}) collective-permute-start(bf16[128,1024]{1,0:T(8,128)(2,1)S(1)} %lay.2.refs_0_), channel_id=1, source_target_pairs={{0,2},{1,3},{2,0},{3,1},{4,6},{5,7},{6,4},{7,5},{8,10},{9,11},{10,... | collective-permute-start | bytes 786440 | tf_op jit(solution)/shard_map/ppermute | solution.py:40
  26.3 6.2 %collective-permute-start.22 = (bf16[32,1024]{1,0:T(8,128)(2,1)S(1)}, bf16[32,1024]{1,0:T(8,128)(2,1)S(1)}, u32[]{:S(2)}, u32[]{:S(2)}) collective-permute-start(bf16[32,1024]{1,0:T(8,128)(2,1)S(1)} %get-tuple-element.188), channel_id=1, source_target_pairs={{0,24},{1,25},{2,26},{3,27},{4,28},{5,29},{6,30},{7,31},{8,16},{9,... | collective-permute-start | bytes 196616 | tf_op jit(solution)/shard_map/ppermute | solution.py:40
  27.1 7.6 %collective-permute-start.20 = (bf16[32,1024]{1,0:T(8,128)(2,1)S(1)}, bf16[32,1024]{1,0:T(8,128)(2,1)S(1)}, u32[]{:S(2)}, u32[]{:S(2)}) collective-permute-start(bf16[32,1024]{1,0:T(8,128)(2,1)S(1)} %get-tuple-element.189), channel_id=1, source_target_pairs={{0,8},{1,9},{2,10},{3,11},{4,12},{5,13},{6,14},{7,15},{8,0},{9,1},... | collective-permute-start | bytes 196616 | tf_op jit(solution)/shard_map/ppermute | solution.py:40
  32.5 5.2 %collective-permute-start.21 = (bf16[32,1024]{1,0:T(8,128)(2,1)S(1)}, bf16[32,1024]{1,0:T(8,128)(2,1)S(1)}, u32[]{:S(2)}, u32[]{:S(2)}) collective-permute-start(bf16[32,1024]{1,0:T(8,128)(2,1)S(1)} %get-tuple-element.190), channel_id=1, source_target_pairs={{0,16},{1,17},{2,18},{3,19},{4,20},{5,21},{6,22},{7,23},{8,24},{9,... | collective-permute-start | bytes 196616 | tf_op jit(solution)/shard_map/ppermute | solution.py:40
  37.7 4.2 %collective-permute-start.23 = (bf16[128,1024]{1,0:T(8,128)(2,1)S(1)}, bf16[128,1024]{1,0:T(8,128)(2,1)S(1)}, u32[]{:S(2)}, u32[]{:S(2)}) collective-permute-start(bf16[128,1024]{1,0:T(8,128)(2,1)S(1)} %lay.2.refs_0_), channel_id=1, source_target_pairs={{0,1},{1,0},{2,3},{3,2},{4,5},{5,4},{6,7},{7,6},{8,9},{9,8},{10,11... | collective-permute-start | bytes 786440 | tf_op jit(solution)/shard_map/ppermute | solution.py:40
  37.8 4.1 %collective-permute-start.24 = (bf16[128,1024]{1,0:T(8,128)(2,1)S(1)}, bf16[128,1024]{1,0:T(8,128)(2,1)S(1)}, u32[]{:S(2)}, u32[]{:S(2)}) collective-permute-start(bf16[128,1024]{1,0:T(8,128)(2,1)S(1)} %collective-permute-done.17.refs_1_), channel_id=1, source_target_pairs={{0,1},{1,0},{2,3},{3,2},{4,5},{5,4},{6,7},{7,6},{8,9},{9,8},{10,11... | collective-permute-start | bytes 786440 | tf_op jit(solution)/shard_map/ppermute | solution.py:40
  38.3 3.6 %collective-permute-start.25 = (bf16[128,1024]{1,0:T(8,128)(2,1)S(1)}, bf16[128,1024]{1,0:T(8,128)(2,1)S(1)}, u32[]{:S(2)}, u32[]{:S(2)}) collective-permute-start(bf16[128,1024]{1,0:T(8,128)(2,1)S(1)} %collective-permute-done.18.refs_2_), channel_id=1, source_target_pairs={{0,1},{1,0},{2,3},{3,2},{4,5},{5,4},{6,7},{7,6},{8,9},{9,8},{10,11... | collective-permute-start | bytes 786440 | tf_op jit(solution)/shard_map/ppermute | solution.py:40
  38.3 3.5 %collective-permute-start.26 = (bf16[128,1024]{1,0:T(8,128)(2,1)S(1)}, bf16[128,1024]{1,0:T(8,128)(2,1)S(1)}, u32[]{:S(2)}, u32[]{:S(2)}) collective-permute-start(bf16[128,1024]{1,0:T(8,128)(2,1)S(1)} %collective-permute-done.19.refs_3_), channel_id=1, source_target_pairs={{0,1},{1,0},{2,3},{3,2},{4,5},{5,4},{6,7},{7,6},{8,9},{9,8},{10,11... | collective-permute-start | bytes 786440 | tf_op jit(solution)/shard_map/ppermute | solution.py:40
  39.3 10.9 %collective-permute-start.27 = (bf16[128,1024]{1,0:T(8,128)(2,1)S(1)}, bf16[128,1024]{1,0:T(8,128)(2,1)}, u32[]{:S(2)}, u32[]{:S(2)}) collective-permute-start(bf16[128,1024]{1,0:T(8,128)(2,1)S(1)} %lay.3), channel_id=1, source_target_pairs={{0,6},{1,7},{2,4},{3,5},{4,2},{5,3},{6,0},{7,1},{8,14},{9,15},{10,... | collective-permute-start | bytes 786440 | tf_op jit(solution)/shard_map/ppermute | solution.py:40
  45.8 23.0 %collective-permute-start.31 = (bf16[528,256]{1,0:T(8,128)(2,1)S(1)}, bf16[528,256]{1,0:T(8,128)(2,1)S(1)}, u32[]{:S(2)}, u32[]{:S(2)}) collective-permute-start(bf16[528,256]{1,0:T(8,128)(2,1)S(1)} %get-tuple-element.147), channel_id=1, source_target_pairs={{0,24},{1,25},{2,26},{3,27},{4,28},{5,29},{6,30},{7,31},{8,16},{9,... | collective-permute-start | bytes 811016 | tf_op jit(solution)/shard_map/ppermute | solution.py:40
  47.4 23.6 %collective-permute-start.32 = (bf16[528,256]{1,0:T(8,128)(2,1)S(1)}, bf16[528,256]{1,0:T(8,128)(2,1)S(1)}, u32[]{:S(2)}, u32[]{:S(2)}) collective-permute-start(bf16[528,256]{1,0:T(8,128)(2,1)S(1)} %get-tuple-element.148), channel_id=1, source_target_pairs={{0,16},{1,17},{2,18},{3,19},{4,20},{5,21},{6,22},{7,23},{8,24},{9,... | collective-permute-start | bytes 811016 | tf_op jit(solution)/shard_map/ppermute | solution.py:40
  47.5 23.6 %collective-permute-start.33 = (bf16[528,256]{1,0:T(8,128)(2,1)S(1)}, bf16[528,256]{1,0:T(8,128)(2,1)S(1)}, u32[]{:S(2)}, u32[]{:S(2)}) collective-permute-start(bf16[528,256]{1,0:T(8,128)(2,1)S(1)} %get-tuple-element.149), channel_id=1, source_target_pairs={{0,8},{1,9},{2,10},{3,11},{4,12},{5,13},{6,14},{7,15},{8,0},{9,1},... | collective-permute-start | bytes 811016 | tf_op jit(solution)/shard_map/ppermute | solution.py:40
  50.2 7.2 %collective-permute-start.4 = (bf16[128,1024]{1,0:T(8,128)(2,1)S(1)}, bf16[128,1024]{1,0:T(8,128)(2,1)S(1)}, u32[]{:S(2)}, u32[]{:S(2)}) collective-permute-start(bf16[128,1024]{1,0:T(8,128)(2,1)S(1)} %get-tuple-element.16.refs_0_), channel_id=1, source_target_pairs={{0,2},{1,3},{2,0},{3,1},{4,6},{5,7},{6,4},{7,5},{8,10},{9,11},{10,... | collective-permute-start | bytes 786440 | tf_op jit(solution)/shard_map/cond/branch_1_fun/ppermute | solution.py:40
  50.8 6.9 %collective-permute-start.5 = (bf16[128,1024]{1,0:T(8,128)(2,1)S(1)}, bf16[128,1024]{1,0:T(8,128)(2,1)S(1)}, u32[]{:S(2)}, u32[]{:S(2)}) collective-permute-start(bf16[128,1024]{1,0:T(8,128)(2,1)S(1)} %get-tuple-element.16.refs_0_), channel_id=1, source_target_pairs={{0,4},{1,5},{2,6},{3,7},{4,0},{5,1},{6,2},{7,3},{8,12},{9,13},{10,... | collective-permute-start | bytes 786440 | tf_op jit(solution)/shard_map/cond/branch_1_fun/ppermute | solution.py:40
  57.7 3.9 %collective-permute-start.7 = (bf16[256,1024]{1,0:T(8,128)(2,1)S(1)}, bf16[256,1024]{1,0:T(8,128)(2,1)S(1)}, u32[]{:S(2)}, u32[]{:S(2)}) collective-permute-start(bf16[256,1024]{1,0:T(8,128)(2,1)S(1)} %pad_maximum_fusion.1), channel_id=1, source_target_pairs={{0,1},{1,0},{2,3},{3,2},{4,5},{5,4},{6,7},{7,6},{8,9},{9,8},{10,11... | collective-permute-start | bytes 1572872 | tf_op jit(solution)/shard_map/cond/branch_1_fun/ppermute | solution.py:40
  58.8 2.8 %collective-permute-start.6 = (bf16[256,1024]{1,0:T(8,128)(2,1)S(1)}, bf16[256,1024]{1,0:T(8,128)(2,1)S(1)}, u32[]{:S(2)}, u32[]{:S(2)}) collective-permute-start(bf16[256,1024]{1,0:T(8,128)(2,1)S(1)} %pad_maximum_fusion), channel_id=1, source_target_pairs={{0,1},{1,0},{2,3},{3,2},{4,5},{5,4},{6,7},{7,6},{8,9},{9,8},{10,11... | collective-permute-start | bytes 1572872 | tf_op jit(solution)/shard_map/cond/branch_1_fun/ppermute | solution.py:40
  66.6 23.8 %collective-permute-start.28 = (bf16[528,256]{1,0:T(8,128)(2,1)}, bf16[528,256]{1,0:T(8,128)(2,1)S(1)}, u32[]{:S(2)}, u32[]{:S(2)}) collective-permute-start(bf16[528,256]{1,0:T(8,128)(2,1)} %get-tuple-element.143), channel_id=1, source_target_pairs={{0,8},{1,9},{2,10},{3,11},{4,12},{5,13},{6,14},{7,15},{8,0},{9,1},... | collective-permute-start | bytes 811016 | tf_op jit(solution)/shard_map/ppermute | solution.py:40
  66.9 25.5 %collective-permute-start.29 = (bf16[528,256]{1,0:T(8,128)(2,1)}, bf16[528,256]{1,0:T(8,128)(2,1)S(1)}, u32[]{:S(2)}, u32[]{:S(2)}) collective-permute-start(bf16[528,256]{1,0:T(8,128)(2,1)} %get-tuple-element.144), channel_id=1, source_target_pairs={{0,16},{1,17},{2,18},{3,19},{4,20},{5,21},{6,22},{7,23},{8,24},{9,... | collective-permute-start | bytes 811016 | tf_op jit(solution)/shard_map/ppermute | solution.py:40
  68.8 23.6 %collective-permute-start.30 = (bf16[528,256]{1,0:T(8,128)(2,1)}, bf16[528,256]{1,0:T(8,128)(2,1)S(1)}, u32[]{:S(2)}, u32[]{:S(2)}) collective-permute-start(bf16[528,256]{1,0:T(8,128)(2,1)} %get-tuple-element.145), channel_id=1, source_target_pairs={{0,24},{1,25},{2,26},{3,27},{4,28},{5,29},{6,30},{7,31},{8,16},{9,... | collective-permute-start | bytes 811016 | tf_op jit(solution)/shard_map/ppermute | solution.py:40
  74.4 2.1 %collective-permute-start = (f32[256,512]{1,0:T(8,128)}, f32[256,512]{1,0:T(8,128)S(1)}, u32[]{:S(2)}, u32[]{:S(2)}) collective-permute-start(f32[256,512]{1,0:T(8,128)} %get-tuple-element.26), channel_id=1, source_target_pairs={{0,1},{1,0},{2,3},{3,2},{4,5},{5,4},{6,7},{7,6},{8,9},{9,8},{10,11... | collective-permute-start | bytes 1572872 | tf_op jit(solution)/shard_map/cond/branch_1_fun/ppermute | solution.py:40
  77.8 4.2 %collective-permute-start.1 = (bf16[208,128]{1,0:T(8,128)(2,1)S(1)}, bf16[208,128]{1,0:T(8,128)(2,1)S(1)}, u32[]{:S(2)}, u32[]{:S(2)}) collective-permute-start(bf16[208,128]{1,0:T(8,128)(2,1)S(1)} %get-tuple-element.28), channel_id=1, source_target_pairs={{0,2},{1,3},{2,0},{3,1},{4,6},{5,7},{6,4},{7,5},{8,10},{9,11},{10,... | collective-permute-start | bytes 159752 | tf_op jit(solution)/shard_map/cond/branch_1_fun/ppermute | solution.py:40
  79.4 4.1 %collective-permute-start.2 = (bf16[208,128]{1,0:T(8,128)(2,1)S(1)}, bf16[208,128]{1,0:T(8,128)(2,1)S(1)}, u32[]{:S(2)}, u32[]{:S(2)}) collective-permute-start(bf16[208,128]{1,0:T(8,128)(2,1)S(1)} %get-tuple-element.31), channel_id=1, source_target_pairs={{0,4},{1,5},{2,6},{3,7},{4,0},{5,1},{6,2},{7,3},{8,12},{9,13},{10,... | collective-permute-start | bytes 159752 | tf_op jit(solution)/shard_map/cond/branch_1_fun/ppermute | solution.py:40
  82.0 5.0 %collective-permute-start.3 = (bf16[208,128]{1,0:T(8,128)(2,1)S(1)}, bf16[208,128]{1,0:T(8,128)(2,1)S(1)}, u32[]{:S(2)}, u32[]{:S(2)}) collective-permute-start(bf16[208,128]{1,0:T(8,128)(2,1)S(1)} %get-tuple-element.32), channel_id=1, source_target_pairs={{0,6},{1,7},{2,4},{3,5},{4,2},{5,3},{6,0},{7,1},{8,14},{9,15},{10,... | collective-permute-start | bytes 159752 | tf_op jit(solution)/shard_map/cond/branch_1_fun/ppermute | solution.py:40
  87.9 4.5 %collective-permute-start.34 = (bf16[64,128]{1,0:T(8,128)(2,1)S(1)}, bf16[64,128]{1,0:T(8,128)(2,1)S(1)}, u32[]{:S(2)}, u32[]{:S(2)}) collective-permute-start(bf16[64,128]{1,0:T(8,128)(2,1)S(1)} %get-tuple-element.153), channel_id=1, source_target_pairs={{0,8},{1,9},{2,10},{3,11},{4,12},{5,13},{6,14},{7,15},{8,0},{9,1},... | collective-permute-start | bytes 49160 | tf_op jit(solution)/shard_map/ppermute | solution.py:40
  88.0 6.6 %collective-permute-start.35 = (bf16[64,128]{1,0:T(8,128)(2,1)S(1)}, bf16[64,128]{1,0:T(8,128)(2,1)S(1)}, u32[]{:S(2)}, u32[]{:S(2)}) collective-permute-start(bf16[64,128]{1,0:T(8,128)(2,1)S(1)} %get-tuple-element.154), channel_id=1, source_target_pairs={{0,16},{1,17},{2,18},{3,19},{4,20},{5,21},{6,22},{7,23},{8,24},{9,... | collective-permute-start | bytes 49160 | tf_op jit(solution)/shard_map/ppermute | solution.py:40
  90.4 5.5 %collective-permute-start.36 = (bf16[64,128]{1,0:T(8,128)(2,1)S(1)}, bf16[64,128]{1,0:T(8,128)(2,1)S(1)}, u32[]{:S(2)}, u32[]{:S(2)}) collective-permute-start(bf16[64,128]{1,0:T(8,128)(2,1)S(1)} %get-tuple-element.155), channel_id=1, source_target_pairs={{0,24},{1,25},{2,26},{3,27},{4,28},{5,29},{6,30},{7,31},{8,16},{9,... | collective-permute-start | bytes 49160 | tf_op jit(solution)/shard_map/ppermute | solution.py:40
  98.5 2.0 %collective-permute-start.37 = (f32[256,512]{1,0:T(8,128)S(1)}, f32[256,512]{1,0:T(8,128)S(1)}, u32[]{:S(2)}, u32[]{:S(2)}) collective-permute-start(f32[256,512]{1,0:T(8,128)S(1)} %get-tuple-element.162), channel_id=1, source_target_pairs={{0,1},{1,0},{2,3},{3,2},{4,5},{5,4},{6,7},{7,6},{8,9},{9,8},{10,11... | collective-permute-start | bytes 1572872 | tf_op jit(solution)/shard_map/ppermute | solution.py:40
  101.3 4.2 %collective-permute-start.38 = (bf16[208,128]{1,0:T(8,128)(2,1)S(1)}, bf16[208,128]{1,0:T(8,128)(2,1)S(1)}, u32[]{:S(2)}, u32[]{:S(2)}) collective-permute-start(bf16[208,128]{1,0:T(8,128)(2,1)S(1)} %get-tuple-element.164), channel_id=1, source_target_pairs={{0,2},{1,3},{2,0},{3,1},{4,6},{5,7},{6,4},{7,5},{8,10},{9,11},{10,... | collective-permute-start | bytes 159752 | tf_op jit(solution)/shard_map/ppermute | solution.py:40
  102.6 4.7 %collective-permute-start.39 = (bf16[208,128]{1,0:T(8,128)(2,1)S(1)}, bf16[208,128]{1,0:T(8,128)(2,1)S(1)}, u32[]{:S(2)}, u32[]{:S(2)}) collective-permute-start(bf16[208,128]{1,0:T(8,128)(2,1)S(1)} %get-tuple-element.165), channel_id=1, source_target_pairs={{0,4},{1,5},{2,6},{3,7},{4,0},{5,1},{6,2},{7,3},{8,12},{9,13},{10,... | collective-permute-start | bytes 159752 | tf_op jit(solution)/shard_map/ppermute | solution.py:40
  103.2 5.0 %collective-permute-start.40 = (bf16[208,128]{1,0:T(8,128)(2,1)S(1)}, bf16[208,128]{1,0:T(8,128)(2,1)S(1)}, u32[]{:S(2)}, u32[]{:S(2)}) collective-permute-start(bf16[208,128]{1,0:T(8,128)(2,1)S(1)} %get-tuple-element.166), channel_id=1, source_target_pairs={{0,6},{1,7},{2,4},{3,5},{4,2},{5,3},{6,0},{7,1},{8,14},{9,15},{10,... | collective-permute-start | bytes 159752 | tf_op jit(solution)/shard_map/ppermute | solution.py:40
  109.1 6.8 %collective-permute-start.43 = (bf16[256,128]{1,0:T(8,128)(2,1)S(1)}, bf16[256,128]{1,0:T(8,128)(2,1)S(1)}, u32[]{:S(2)}, u32[]{:S(2)}) collective-permute-start(bf16[256,128]{1,0:T(8,128)(2,1)S(1)} %code.1.refs_0_), channel_id=1, source_target_pairs={{0,24},{1,25},{2,26},{3,27},{4,28},{5,29},{6,30},{7,31},{8,16},{9,... | collective-permute-start | bytes 196616 | tf_op jit(solution)/shard_map/ppermute | solution.py:40
  111.4 5.7 %collective-permute-start.42 = (bf16[256,128]{1,0:T(8,128)(2,1)S(1)}, bf16[256,128]{1,0:T(8,128)(2,1)S(1)}, u32[]{:S(2)}, u32[]{:S(2)}) collective-permute-start(bf16[256,128]{1,0:T(8,128)(2,1)S(1)} %code.1.refs_0_), channel_id=1, source_target_pairs={{0,16},{1,17},{2,18},{3,19},{4,20},{5,21},{6,22},{7,23},{8,24},{9,... | collective-permute-start | bytes 196616 | tf_op jit(solution)/shard_map/ppermute | solution.py:40
  111.4 5.7 %collective-permute-start.41 = (bf16[256,128]{1,0:T(8,128)(2,1)S(1)}, bf16[256,128]{1,0:T(8,128)(2,1)S(1)}, u32[]{:S(2)}, u32[]{:S(2)}) collective-permute-start(bf16[256,128]{1,0:T(8,128)(2,1)S(1)} %code.1.refs_0_), channel_id=1, source_target_pairs={{0,8},{1,9},{2,10},{3,11},{4,12},{5,13},{6,14},{7,15},{8,0},{9,1},... | collective-permute-start | bytes 196616 | tf_op jit(solution)/shard_map/ppermute | solution.py:40
  118.1 5.6 %collective-permute-start.46 = (bf16[128,384]{1,0:T(8,128)(2,1)S(1)}, bf16[128,384]{1,0:T(8,128)(2,1)S(1)}, u32[]{:S(2)}, u32[]{:S(2)}) collective-permute-start(bf16[128,384]{1,0:T(8,128)(2,1)S(1)} %finish.1.refs_0_), channel_id=1, source_target_pairs={{0,6},{1,7},{2,4},{3,5},{4,2},{5,3},{6,0},{7,1},{8,14},{9,15},{10,... | collective-permute-start | bytes 294920 | tf_op jit(solution)/shard_map/ppermute | solution.py:40
  119.6 5.1 %collective-permute-start.45 = (bf16[128,384]{1,0:T(8,128)(2,1)S(1)}, bf16[128,384]{1,0:T(8,128)(2,1)S(1)}, u32[]{:S(2)}, u32[]{:S(2)}) collective-permute-start(bf16[128,384]{1,0:T(8,128)(2,1)S(1)} %finish.1.refs_0_), channel_id=1, source_target_pairs={{0,4},{1,5},{2,6},{3,7},{4,0},{5,1},{6,2},{7,3},{8,12},{9,13},{10,... | collective-permute-start | bytes 294920 | tf_op jit(solution)/shard_map/ppermute | solution.py:40
  120.9 4.6 %collective-permute-start.44 = (bf16[128,384]{1,0:T(8,128)(2,1)S(1)}, bf16[128,384]{1,0:T(8,128)(2,1)S(1)}, u32[]{:S(2)}, u32[]{:S(2)}) collective-permute-start(bf16[128,384]{1,0:T(8,128)(2,1)S(1)} %finish.1.refs_0_), channel_id=1, source_target_pairs={{0,2},{1,3},{2,0},{3,1},{4,6},{5,7},{6,4},{7,5},{8,10},{9,11},{10,... | collective-permute-start | bytes 294920 | tf_op jit(solution)/shard_map/ppermute | solution.py:40
  121.7 3.9 %collective-permute-start.47 = (bf16[128,384]{1,0:T(8,128)(2,1)S(1)}, bf16[128,384]{1,0:T(8,128)(2,1)S(1)}, u32[]{:S(2)}, u32[]{:S(2)}) collective-permute-start(bf16[128,384]{1,0:T(8,128)(2,1)S(1)} %finish.1.refs_0_), channel_id=1, source_target_pairs={{0,1},{1,0},{2,3},{3,2},{4,5},{5,4},{6,7},{7,6},{8,9},{9,8},{10,11... | collective-permute-start | bytes 294920 | tf_op jit(solution)/shard_map/ppermute | solution.py:40
  123.7 1.8 %collective-permute-start.50 = (bf16[128,384]{1,0:T(8,128)(2,1)S(1)}, bf16[128,384]{1,0:T(8,128)(2,1)S(1)}, u32[]{:S(2)}, u32[]{:S(2)}) collective-permute-start(bf16[128,384]{1,0:T(8,128)(2,1)S(1)} %collective-permute-done.46.refs_3_), channel_id=1, source_target_pairs={{0,1},{1,0},{2,3},{3,2},{4,5},{5,4},{6,7},{7,6},{8,9},{9,8},{10,11... | collective-permute-start | bytes 294920 | tf_op jit(solution)/shard_map/ppermute | solution.py:40
  124.7 1.3 collective-permute-start.49
  125.5 1.3 collective-permute-start.48
  128.5 7.9 %collective-permute-start.51 = (bf16[128,256]{1,0:T(8,128)(2,1)S(1)}, bf16[128,256]{1,0:T(8,128)(2,1)S(1)}, u32[]{:S(2)}, u32[]{:S(2)}) collective-permute-start(bf16[128,256]{1,0:T(8,128)(2,1)S(1)} %get-tuple-element.176), channel_id=1, source_target_pairs={{0,24},{1,25},{2,26},{3,27},{4,28},{5,29},{6,30},{7,31},{8,16},{9,... | collective-permute-start | bytes 196616 | tf_op jit(solution)/shard_map/ppermute | solution.py:40
  130.3 10.7 %collective-permute-start.52 = (bf16[128,256]{1,0:T(8,128)(2,1)S(1)}, bf16[128,256]{1,0:T(8,128)(2,1)S(1)}, u32[]{:S(2)}, u32[]{:S(2)}) collective-permute-start(bf16[128,256]{1,0:T(8,128)(2,1)S(1)} %get-tuple-element.177), channel_id=1, source_target_pairs={{0,16},{1,17},{2,18},{3,19},{4,20},{5,21},{6,22},{7,23},{8,24},{9,... | collective-permute-start | bytes 196616 | tf_op jit(solution)/shard_map/ppermute | solution.py:40
  130.7 10.3 %collective-permute-start.53 = (bf16[128,256]{1,0:T(8,128)(2,1)S(1)}, bf16[128,256]{1,0:T(8,128)(2,1)S(1)}, u32[]{:S(2)}, u32[]{:S(2)}) collective-permute-start(bf16[128,256]{1,0:T(8,128)(2,1)S(1)} %get-tuple-element.178), channel_id=1, source_target_pairs={{0,8},{1,9},{2,10},{3,11},{4,12},{5,13},{6,14},{7,15},{8,0},{9,1},... | collective-permute-start | bytes 196616 | tf_op jit(solution)/shard_map/ppermute | solution.py:40
  134.6 7.8 %collective-permute-start.54 = (bf16[128,256]{1,0:T(8,128)(2,1)S(1)}, bf16[128,256]{1,0:T(8,128)(2,1)S(1)}, u32[]{:S(2)}, u32[]{:S(2)}) collective-permute-start(bf16[128,256]{1,0:T(8,128)(2,1)S(1)} %get-tuple-element.182), channel_id=1, source_target_pairs={{0,24},{1,25},{2,26},{3,27},{4,28},{5,29},{6,30},{7,31},{8,16},{9,... | collective-permute-start | bytes 196616 | tf_op jit(solution)/shard_map/ppermute | solution.py:40
  136.4 6.5 %collective-permute-start.55 = (bf16[128,256]{1,0:T(8,128)(2,1)S(1)}, bf16[128,256]{1,0:T(8,128)(2,1)S(1)}, u32[]{:S(2)}, u32[]{:S(2)}) collective-permute-start(bf16[128,256]{1,0:T(8,128)(2,1)S(1)} %get-tuple-element.183), channel_id=1, source_target_pairs={{0,16},{1,17},{2,18},{3,19},{4,20},{5,21},{6,22},{7,23},{8,24},{9,... | collective-permute-start | bytes 196616 | tf_op jit(solution)/shard_map/ppermute | solution.py:40
  136.4 6.5 %collective-permute-start.56 = (bf16[128,256]{1,0:T(8,128)(2,1)S(1)}, bf16[128,256]{1,0:T(8,128)(2,1)S(1)}, u32[]{:S(2)}, u32[]{:S(2)}) collective-permute-start(bf16[128,256]{1,0:T(8,128)(2,1)S(1)} %get-tuple-element.184), channel_id=1, source_target_pairs={{0,8},{1,9},{2,10},{3,11},{4,12},{5,13},{6,14},{7,15},{8,0},{9,1},... | collective-permute-start | bytes 196616 | tf_op jit(solution)/shard_map/ppermute | solution.py:40

commit v19 on v18

--- a/solution.py
+++ b/solution.py
@@ -247,7 +247,7 @@
 
 
 def lay_kernel(place_ref, *refs, n):
-    parts, outs = [refs[0], *refs[n - 1 : 0 : -1]], refs[n:]
+    parts, outs = refs[:n], refs[n:]
     few = parts[0].shape[0] // len(outs)
     for step in range(n):
         at = pl.ds(pl.multiple_of((place_ref[0] ^ step) * few, few), few)
@@ -306,7 +306,7 @@
     (laid,) = local(
         functools.partial(lay_kernel, n=place.n),
         place_array,
-        [parts[0], *parts[:0:-1]],
+        parts,
         [((rows * place.n, width), BF16)],
         "lay",
         pinned=True,

time: 145 us -> 145 us (level)
  no operation moved by 1% of the time
where the time goes in v19:
time: 145 us; the launch traced here: 144 us
  starting transfers between devices  60.8 us (42%)
  waiting for transfers between devices  45 us (31%)
  Pallas kernels  34.4 us (24%)
  local copies, waits for them, and re-layouts  1.91 us (1%)
    ppermute x57, starting transfers between devices, send(): return lax.ppermute(value, ('dp', 'mp'), pairs)  60.8 us
    ppermute x57, waiting for transfers between devices, send(): return lax.ppermute(value, ('dp', 'mp'), pairs)  45 us
    pallas_call x14, Pallas kernels, local(): pl.pallas_call(kernel, in_specs=[pl.BlockSpec(memory_space=pltpu.SMEM)] +...  15.1 us
    pallas_call x2, Pallas kernels, project(): pl.pallas_call(functools.partial(project_kernel, counts=counts, n=n, k=k)...  8.92 us
    pallas_call x2, Pallas kernels, normalize_parts(): pl.pallas_call(functools.partial(normalize_kernel, n=n, k=k, order=order,...  6.01 us
    pallas_call x2, Pallas kernels, fetch(): pl.pallas_call(fetch_kernel, in_specs=[pl.BlockSpec(memory_space=pl.ANY)]...  4.39 us
  transfers between devices with their start and end apart: 57, of which 23 were waited for; matrix products, arithmetic and copies ran while one was open for 1% of the time, Pallas kernels for 18%

profile of v19, /device:TPU:0, one launch (start us, length us, event | category | flops | bytes accessed | tf_op | source)
XLA Modules:
  0.0 144.2 jit_solution(13559973894687417460)
XLA Ops:
  0.7 1.0 dynamic-slice_bitcast_fusion.4
  1.6 4.0 %collective-permute-start.10 = (bf16[32,1024]{1,0:T(8,128)(2,1)S(1)}, bf16[32,1024]{1,0:T(8,128)(2,1)S(1)}, u32[]{:S(2)}, u32[]{:S(2)}) collective-permute-start(bf16[32,1024]{1,0:T(8,128)(2,1)S(1)} %get-tuple-element.196), channel_id=1, source_target_pairs={{0,6},{1,7},{2,4},{3,5},{4,2},{5,3},{6,0},{7,1},{8,14},{9,15},{10,... | collective-permute-start | bytes 196616 | tf_op jit(solution)/shard_map/ppermute | solution.py:40
  6.2 1.0 dynamic-slice_bitcast_fusion
  7.2 2.9 %collective-permute-start.16 = (bf16[32,1024]{1,0:T(8,128)(2,1)S(1)}, bf16[32,1024]{1,0:T(8,128)(2,1)S(1)}, u32[]{:S(2)}, u32[]{:S(2)}) collective-permute-start(bf16[32,1024]{1,0:T(8,128)(2,1)S(1)} %get-tuple-element.192), channel_id=1, source_target_pairs={{0,6},{1,7},{2,4},{3,5},{4,2},{5,3},{6,0},{7,1},{8,14},{9,15},{10,... | collective-permute-start | bytes 196616 | tf_op jit(solution)/shard_map/ppermute | solution.py:40
  11.4 2.0 %collective-permute-start.11 = (bf16[32,1024]{1,0:T(8,128)(2,1)S(1)}, bf16[32,1024]{1,0:T(8,128)(2,1)S(1)}, u32[]{:S(2)}, u32[]{:S(2)}) collective-permute-start(bf16[32,1024]{1,0:T(8,128)(2,1)S(1)} %get-tuple-element.113), channel_id=1, source_target_pairs={{0,8},{1,9},{2,10},{3,11},{4,12},{5,13},{6,14},{7,15},{8,0},{9,1},... | collective-permute-start | bytes 196616 | tf_op jit(solution)/shard_map/ppermute | solution.py:40
  13.5 2.6 %collective-permute-start.12 = (bf16[32,1024]{1,0:T(8,128)(2,1)S(1)}, bf16[32,1024]{1,0:T(8,128)(2,1)S(1)}, u32[]{:S(2)}, u32[]{:S(2)}) collective-permute-start(bf16[32,1024]{1,0:T(8,128)(2,1)S(1)} %get-tuple-element.114), channel_id=1, source_target_pairs={{0,16},{1,17},{2,18},{3,19},{4,20},{5,21},{6,22},{7,23},{8,24},{9,... | collective-permute-start | bytes 196616 | tf_op jit(solution)/shard_map/ppermute | solution.py:40
  16.6 3.4 %collective-permute-done.12.refs_2_ = bf16[32,1024]{1,0:T(8,128)(2,1)S(1)} collective-permute-done((bf16[32,1024]{1,0:T(8,128)(2,1)S(1)}, bf16[32,1024]{1,0:T(8,128)(2,1)S(1)}, u32[]{:S(2)}, u32[]{:S(2)}) %collective-permute-start.12) | collective-permute-done | bytes 65568 | tf_op jit(solution)/shard_map/ppermute | solution.py:40
  20.0 2.1 %collective-permute-done.13.refs_3_ = bf16[32,1024]{1,0:T(8,128)(2,1)S(1)} collective-permute-done((bf16[32,1024]{1,0:T(8,128)(2,1)S(1)}, bf16[32,1024]{1,0:T(8,128)(2,1)S(1)}, u32[]{:S(2)}, u32[]{:S(2)}) %collective-permute-start.13) | collective-permute-done | bytes 65568 | tf_op jit(solution)/shard_map/ppermute | solution.py:40
  22.7 2.5 %collective-permute-start.19 = (bf16[128,1024]{1,0:T(8,128)(2,1)S(1)}, bf16[128,1024]{1,0:T(8,128)(2,1)S(1)}, u32[]{:S(2)}, u32[]{:S(2)}) collective-permute-start(bf16[128,1024]{1,0:T(8,128)(2,1)S(1)} %lay.2.refs_0_), channel_id=1, source_target_pairs={{0,6},{1,7},{2,4},{3,5},{4,2},{5,3},{6,0},{7,1},{8,14},{9,15},{10,... | collective-permute-start | bytes 786440 | tf_op jit(solution)/shard_map/ppermute | solution.py:40
  26.3 0.9 collective-permute-start.22
  27.2 5.4 %collective-permute-done.22.refs_3_ = bf16[32,1024]{1,0:T(8,128)(2,1)S(1)} collective-permute-done((bf16[32,1024]{1,0:T(8,128)(2,1)S(1)}, bf16[32,1024]{1,0:T(8,128)(2,1)S(1)}, u32[]{:S(2)}, u32[]{:S(2)}) %collective-permute-start.22) | collective-permute-done | bytes 65568 | tf_op jit(solution)/shard_map/ppermute | solution.py:40
  32.5 2.2 %fetch.3.refs_8_ = bf16[2048,1024]{1,0:T(8,128)(2,1)S(1)} custom-call(bf16[2048,1024]{1,0:T(8,128)(2,1)} %weight_ref), custom_call_target="tpu_custom_call" | custom-call | bytes 8388608 | tf_op jit(solution)/shard_map/fetch/pallas_call | solution.py:265
  34.7 2.9 %collective-permute-done.21.refs_2_ = bf16[32,1024]{1,0:T(8,128)(2,1)S(1)} collective-permute-done((bf16[32,1024]{1,0:T(8,128)(2,1)S(1)}, bf16[32,1024]{1,0:T(8,128)(2,1)S(1)}, u32[]{:S(2)}, u32[]{:S(2)}) %collective-permute-start.21) | collective-permute-done | bytes 65568 | tf_op jit(solution)/shard_map/ppermute | solution.py:40
  39.3 2.5 %collective-permute-start.27 = (bf16[128,1024]{1,0:T(8,128)(2,1)S(1)}, bf16[128,1024]{1,0:T(8,128)(2,1)}, u32[]{:S(2)}, u32[]{:S(2)}) collective-permute-start(bf16[128,1024]{1,0:T(8,128)(2,1)S(1)} %lay.3), channel_id=1, source_target_pairs={{0,6},{1,7},{2,4},{3,5},{4,2},{5,3},{6,0},{7,1},{8,14},{9,15},{10,... | collective-permute-start | bytes 786440 | tf_op jit(solution)/shard_map/ppermute | solution.py:40
  41.9 3.9 %project.3 = (f32[512,256]{1,0:T(8,128)S(1)}, bf16[528,256]{1,0:T(8,128)(2,1)S(1)}, bf16[528,256]{1,0:T(8,128)(2,1)S(1)}, bf16[528,256]{1,0:T(8,128)(2,1)S(1)}) custom-call(s32[3]{0:T(128)S(1)} %pad_add_fusion.place_ref, bf16[128,1024]{1,0:T(8,128)(2,1)S(1)} %lay.2.refs_0_, bf16[128,1024]{1,0:T(8,128)(2,1)S(1)} %collective-permute-done.17.refs_1_, ...), custom_call_target="tpu_custom_call" | custom-call | flops 2147483648 | bytes 7864320 | tf_op jit(solution)/shard_map/project/pallas_call | solution.py:378
  45.8 1.7 %collective-permute-start.31 = (bf16[528,256]{1,0:T(8,128)(2,1)S(1)}, bf16[528,256]{1,0:T(8,128)(2,1)S(1)}, u32[]{:S(2)}, u32[]{:S(2)}) collective-permute-start(bf16[528,256]{1,0:T(8,128)(2,1)S(1)} %get-tuple-element.147), channel_id=1, source_target_pairs={{0,24},{1,25},{2,26},{3,27},{4,28},{5,29},{6,30},{7,31},{8,16},{9,... | collective-permute-start | bytes 811016 | tf_op jit(solution)/shard_map/ppermute | solution.py:40
  47.5 2.8 %collective-permute-start.33 = (bf16[528,256]{1,0:T(8,128)(2,1)S(1)}, bf16[528,256]{1,0:T(8,128)(2,1)S(1)}, u32[]{:S(2)}, u32[]{:S(2)}) collective-permute-start(bf16[528,256]{1,0:T(8,128)(2,1)S(1)} %get-tuple-element.149), channel_id=1, source_target_pairs={{0,8},{1,9},{2,10},{3,11},{4,12},{5,13},{6,14},{7,15},{8,0},{9,1},... | collective-permute-start | bytes 811016 | tf_op jit(solution)/shard_map/ppermute | solution.py:40
  50.2 16.4 %conditional.2 = (f32[512,256]{1,0:T(8,128)S(1)}, bf16[528,256]{1,0:T(8,128)(2,1)}, bf16[528,256]{1,0:T(8,128)(2,1)}, bf16[528,256]{1,0:T(8,128)(2,1)}) conditional(s32[]{:T(128)} %convert_element_type.4, () %tuple.35, (bf16[128,1024]{1,0:T(8,128)(2,1)S(1)}, bf16[128,1024]{1,0:T(8,128)(2,1)}, bf16[2048,1024]{1,0:T(8,128)(2,1)}, s32[3]{0:T(128)S(1)}) %tuple.36), branch_computations={%region_0.1_spmd, %region_1.2_spmd} | conditional | flops 2149580800 | bytes 24641728 | solution.py:232
  50.8 1.0 collective-permute-start.5
  51.8 5.6 %collective-permute-done.4.refs_2_ = bf16[128,1024]{1,0:T(8,128)(2,1)S(1)} collective-permute-done((bf16[128,1024]{1,0:T(8,128)(2,1)S(1)}, bf16[128,1024]{1,0:T(8,128)(2,1)S(1)}, u32[]{:S(2)}, u32[]{:S(2)}) %collective-permute-start.4) | collective-permute-done | bytes 262176 | tf_op jit(solution)/shard_map/cond/branch_1_fun/ppermute | solution.py:40
  57.8 1.0 pad_maximum_fusion
  59.4 2.2 %fetch.2.refs_6_ = bf16[2048,1024]{1,0:T(8,128)(2,1)S(1)} custom-call(bf16[2048,1024]{1,0:T(8,128)(2,1)} %get-tuple-element.19.weight_ref), custom_call_target="tpu_custom_call" | custom-call | bytes 8388608 | tf_op jit(solution)/shard_map/cond/branch_1_fun/fetch/pallas_call | solution.py:265
  61.6 5.0 %project.2 = (f32[512,256]{1,0:T(8,128)S(1)}, bf16[528,256]{1,0:T(8,128)(2,1)}, bf16[528,256]{1,0:T(8,128)(2,1)}, bf16[528,256]{1,0:T(8,128)(2,1)}) custom-call(s32[3]{0:T(128)S(1)} %get-tuple-element.14.place_ref, bf16[128,1024]{1,0:T(8,128)(2,1)S(1)} %get-tuple-element.16.refs_0_, bf16[128,1024]{1,0:T(8,128)(2,1)} %get-tuple-element.17.refs_1_, ...), custom_call_target="tpu_custom_call" | custom-call | flops 2147483648 | bytes 7864320 | tf_op jit(solution)/shard_map/cond/branch_1_fun/project/pallas_call | solution.py:378
  66.9 1.8 %collective-permute-start.29 = (bf16[528,256]{1,0:T(8,128)(2,1)}, bf16[528,256]{1,0:T(8,128)(2,1)S(1)}, u32[]{:S(2)}, u32[]{:S(2)}) collective-permute-start(bf16[528,256]{1,0:T(8,128)(2,1)} %get-tuple-element.144), channel_id=1, source_target_pairs={{0,16},{1,17},{2,18},{3,19},{4,20},{5,21},{6,22},{7,23},{8,24},{9,... | collective-permute-start | bytes 811016 | tf_op jit(solution)/shard_map/ppermute | solution.py:40
  68.8 2.3 %collective-permute-start.30 = (bf16[528,256]{1,0:T(8,128)(2,1)}, bf16[528,256]{1,0:T(8,128)(2,1)S(1)}, u32[]{:S(2)}, u32[]{:S(2)}) collective-permute-start(bf16[528,256]{1,0:T(8,128)(2,1)} %get-tuple-element.145), channel_id=1, source_target_pairs={{0,24},{1,25},{2,26},{3,27},{4,28},{5,29},{6,30},{7,31},{8,16},{9,... | collective-permute-start | bytes 811016 | tf_op jit(solution)/shard_map/ppermute | solution.py:40
  71.0 3.4 %normalize.2 = (f32[512,256]{1,0:T(8,128)S(1)}, bf16[512,256]{1,0:T(8,128)(2,1)S(1)}, f32[1,256]{1,0:T(1,128)S(1)}, f32[256,512]{1,0:T(8,128)}, f32[256,512]{1,0:T(8,128)}) custom-call(s32[3]{0:T(128)S(1)} %pad_add_fusion.place_ref, f32[512,256]{1,0:T(8,128)S(1)} %get-tuple-element.146.refs_0_, bf16[528,256]{1,0:T(8,128)(2,1)S(1)} %collective-permute-done.31.refs_1_, ...), custom_call_target="tpu_custom_call" | custom-call | flops 134217728 | bytes 3145728 | tf_op jit(solution)/shard_map/normalize/pallas_call | solution.py:458
  74.4 13.5 %conditional.3 = ((f32[16,384]{1,0:T(8,128)S(1)}, bf16[64,128]{1,0:T(8,128)(2,1)S(1)}, bf16[64,128]{1,0:T(8,128)(2,1)S(1)}, bf16[64,128]{1,0:T(8,128)(2,1)S(1)})) conditional(s32[]{:T(128)} %convert_element_type.4, () %tuple.38, (f32[256,512]{1,0:T(8,128)}, s32[3]{0:T(128)S(1)}, f32[256,512]{1,0:T(8,128)}) %tuple.39), branch_computations={%region_2.3_spmd, %region_3.4_spmd} | conditional | bytes 2736296 | solution.py:232
  74.4 2.1 %collective-permute-done.met_ref = f32[256,512]{1,0:T(8,128)S(1)} collective-permute-done((f32[256,512]{1,0:T(8,128)}, f32[256,512]{1,0:T(8,128)S(1)}, u32[]{:S(2)}, u32[]{:S(2)}) %collective-permute-start) | collective-permute-done | bytes 524320 | tf_op jit(solution)/shard_map/cond/branch_1_fun/ppermute | solution.py:40
  76.5 1.3 halve.2
  77.8 1.6 %collective-permute-start.1 = (bf16[208,128]{1,0:T(8,128)(2,1)S(1)}, bf16[208,128]{1,0:T(8,128)(2,1)S(1)}, u32[]{:S(2)}, u32[]{:S(2)}) collective-permute-start(bf16[208,128]{1,0:T(8,128)(2,1)S(1)} %get-tuple-element.28), channel_id=1, source_target_pairs={{0,2},{1,3},{2,0},{3,1},{4,6},{5,7},{6,4},{7,5},{8,10},{9,11},{10,... | collective-permute-start | bytes 159752 | tf_op jit(solution)/shard_map/cond/branch_1_fun/ppermute | solution.py:40
  79.9 2.1 %collective-permute-done.1.refs_1_ = bf16[208,128]{1,0:T(8,128)(2,1)S(1)} collective-permute-done((bf16[208,128]{1,0:T(8,128)(2,1)S(1)}, bf16[208,128]{1,0:T(8,128)(2,1)S(1)}, u32[]{:S(2)}, u32[]{:S(2)}) %collective-permute-start.1) | collective-permute-done | bytes 53280 | tf_op jit(solution)/shard_map/cond/branch_1_fun/ppermute | solution.py:40
  82.0 1.4 collective-permute-start.3
  83.5 3.5 %collective-permute-done.3.refs_3_ = bf16[208,128]{1,0:T(8,128)(2,1)S(1)} collective-permute-done((bf16[208,128]{1,0:T(8,128)(2,1)S(1)}, bf16[208,128]{1,0:T(8,128)(2,1)S(1)}, u32[]{:S(2)}, u32[]{:S(2)}) %collective-permute-start.3) | collective-permute-done | bytes 53280 | tf_op jit(solution)/shard_map/cond/branch_1_fun/ppermute | solution.py:40
  87.1 0.8 plane.1
  88.0 2.4 %collective-permute-start.35 = (bf16[64,128]{1,0:T(8,128)(2,1)S(1)}, bf16[64,128]{1,0:T(8,128)(2,1)S(1)}, u32[]{:S(2)}, u32[]{:S(2)}) collective-permute-start(bf16[64,128]{1,0:T(8,128)(2,1)S(1)} %get-tuple-element.154), channel_id=1, source_target_pairs={{0,16},{1,17},{2,18},{3,19},{4,20},{5,21},{6,22},{7,23},{8,24},{9,... | collective-permute-start | bytes 49160 | tf_op jit(solution)/shard_map/ppermute | solution.py:40
  90.4 2.0 %collective-permute-start.36 = (bf16[64,128]{1,0:T(8,128)(2,1)S(1)}, bf16[64,128]{1,0:T(8,128)(2,1)S(1)}, u32[]{:S(2)}, u32[]{:S(2)}) collective-permute-start(bf16[64,128]{1,0:T(8,128)(2,1)S(1)} %get-tuple-element.155), channel_id=1, source_target_pairs={{0,24},{1,25},{2,26},{3,27},{4,28},{5,29},{6,30},{7,31},{8,16},{9,... | collective-permute-start | bytes 49160 | tf_op jit(solution)/shard_map/ppermute | solution.py:40
  92.4 2.2 %collective-permute-done.35.refs_2_ = bf16[64,128]{1,0:T(8,128)(2,1)S(1)} collective-permute-done((bf16[64,128]{1,0:T(8,128)(2,1)S(1)}, bf16[64,128]{1,0:T(8,128)(2,1)S(1)}, u32[]{:S(2)}, u32[]{:S(2)}) %collective-permute-start.35) | collective-permute-done | bytes 16416 | tf_op jit(solution)/shard_map/ppermute | solution.py:40
  94.6 1.3 collective-permute-done.36.refs_3_
  95.9 2.6 %normalize.3 = (f32[512,256]{1,0:T(8,128)S(1)}, bf16[512,256]{1,0:T(8,128)(2,1)S(1)}, f32[1,256]{1,0:T(1,128)S(1)}, f32[256,512]{1,0:T(8,128)S(1)}, f32[256,512]{1,0:T(8,128)S(1)}, /*index=5*/f32[1,256]{1,0:T(1,128)S(1)}) custom-call(s32[3]{0:T(128)S(1)} %pad_add_fusion.place_ref, f32[512,256]{1,0:T(8,128)S(1)} %get-tuple-element.156.refs_0_, ...), custom_call_target="tpu_custom_call" | custom-call | flops 134217728 | bytes 3145728 | tf_op jit(solution)/shard_map/normalize/pallas_call | solution.py:458
  98.6 1.9 %collective-permute-done.37.met_ref = f32[256,512]{1,0:T(8,128)S(1)} collective-permute-done((f32[256,512]{1,0:T(8,128)S(1)}, f32[256,512]{1,0:T(8,128)S(1)}, u32[]{:S(2)}, u32[]{:S(2)}) %collective-permute-start.37) | collective-permute-done | bytes 524320 | tf_op jit(solution)/shard_map/ppermute | solution.py:40
  100.5 0.8 halve.3
  101.3 1.3 collective-permute-start.38
  103.2 1.7 %collective-permute-start.40 = (bf16[208,128]{1,0:T(8,128)(2,1)S(1)}, bf16[208,128]{1,0:T(8,128)(2,1)S(1)}, u32[]{:S(2)}, u32[]{:S(2)}) collective-permute-start(bf16[208,128]{1,0:T(8,128)(2,1)S(1)} %get-tuple-element.166), channel_id=1, source_target_pairs={{0,6},{1,7},{2,4},{3,5},{4,2},{5,3},{6,0},{7,1},{8,14},{9,15},{10,... | collective-permute-start | bytes 159752 | tf_op jit(solution)/shard_map/ppermute | solution.py:40
  105.5 1.8 %collective-permute-done.39.refs_2_ = bf16[208,128]{1,0:T(8,128)(2,1)S(1)} collective-permute-done((bf16[208,128]{1,0:T(8,128)(2,1)S(1)}, bf16[208,128]{1,0:T(8,128)(2,1)S(1)}, u32[]{:S(2)}, u32[]{:S(2)}) %collective-permute-start.39) | collective-permute-done | bytes 53280 | tf_op jit(solution)/shard_map/ppermute | solution.py:40
  107.4 0.8 collective-permute-done.40.refs_3_
  108.2 0.8 code.1.refs_0_
  109.1 2.3 %collective-permute-start.43 = (bf16[256,128]{1,0:T(8,128)(2,1)S(1)}, bf16[256,128]{1,0:T(8,128)(2,1)S(1)}, u32[]{:S(2)}, u32[]{:S(2)}) collective-permute-start(bf16[256,128]{1,0:T(8,128)(2,1)S(1)} %code.1.refs_0_), channel_id=1, source_target_pairs={{0,24},{1,25},{2,26},{3,27},{4,28},{5,29},{6,30},{7,31},{8,16},{9,... | collective-permute-start | bytes 196616 | tf_op jit(solution)/shard_map/ppermute | solution.py:40
  111.4 2.1 %collective-permute-start.41 = (bf16[256,128]{1,0:T(8,128)(2,1)S(1)}, bf16[256,128]{1,0:T(8,128)(2,1)S(1)}, u32[]{:S(2)}, u32[]{:S(2)}) collective-permute-start(bf16[256,128]{1,0:T(8,128)(2,1)S(1)} %code.1.refs_0_), channel_id=1, source_target_pairs={{0,8},{1,9},{2,10},{3,11},{4,12},{5,13},{6,14},{7,15},{8,0},{9,1},... | collective-permute-start | bytes 196616 | tf_op jit(solution)/shard_map/ppermute | solution.py:40
  113.5 2.3 %collective-permute-done.43.refs_3_ = bf16[256,128]{1,0:T(8,128)(2,1)S(1)} collective-permute-done((bf16[256,128]{1,0:T(8,128)(2,1)S(1)}, bf16[256,128]{1,0:T(8,128)(2,1)S(1)}, u32[]{:S(2)}, u32[]{:S(2)}) %collective-permute-start.43) | collective-permute-done | bytes 65568 | tf_op jit(solution)/shard_map/ppermute | solution.py:40
  115.8 1.3 collective-permute-done.42.refs_2_
  117.1 1.0 finish.1.refs_0_
  118.1 1.6 %collective-permute-start.46 = (bf16[128,384]{1,0:T(8,128)(2,1)S(1)}, bf16[128,384]{1,0:T(8,128)(2,1)S(1)}, u32[]{:S(2)}, u32[]{:S(2)}) collective-permute-start(bf16[128,384]{1,0:T(8,128)(2,1)S(1)} %finish.1.refs_0_), channel_id=1, source_target_pairs={{0,6},{1,7},{2,4},{3,5},{4,2},{5,3},{6,0},{7,1},{8,14},{9,15},{10,... | collective-permute-start | bytes 294920 | tf_op jit(solution)/shard_map/ppermute | solution.py:40
  119.6 1.2 collective-permute-start.45
  121.7 2.1 %collective-permute-done.46.refs_3_ = bf16[128,384]{1,0:T(8,128)(2,1)S(1)} collective-permute-done((bf16[128,384]{1,0:T(8,128)(2,1)S(1)}, bf16[128,384]{1,0:T(8,128)(2,1)S(1)}, u32[]{:S(2)}, u32[]{:S(2)}) %collective-permute-start.46) | collective-permute-done | bytes 98336 | tf_op jit(solution)/shard_map/ppermute | solution.py:40
  123.7 1.0 collective-permute-done.45.refs_2_
  126.8 1.7 %gradient.2 = (bf16[128,256]{1,0:T(8,128)(2,1)S(1)}, bf16[128,256]{1,0:T(8,128)(2,1)S(1)}, bf16[128,256]{1,0:T(8,128)(2,1)S(1)}, bf16[128,256]{1,0:T(8,128)(2,1)...) custom-call(s32[3]{0:T(128)S(1)} %pad_add_fusion.place_ref, bf16[128,384]{1,0:T(8,128)(2,1)S(1)} %finish.1.refs_0_, ...), custom_call_target="tpu_custom_call" | custom-call | tf_op jit(solution)/shard_map/gradient/pallas_call | solution.py:190
  128.5 1.8 %collective-permute-start.51 = (bf16[128,256]{1,0:T(8,128)(2,1)S(1)}, bf16[128,256]{1,0:T(8,128)(2,1)S(1)}, u32[]{:S(2)}, u32[]{:S(2)}) collective-permute-start(bf16[128,256]{1,0:T(8,128)(2,1)S(1)} %get-tuple-element.176), channel_id=1, source_target_pairs={{0,24},{1,25},{2,26},{3,27},{4,28},{5,29},{6,30},{7,31},{8,16},{9,... | collective-permute-start | bytes 196616 | tf_op jit(solution)/shard_map/ppermute | solution.py:40
  130.7 2.2 %collective-permute-start.53 = (bf16[128,256]{1,0:T(8,128)(2,1)S(1)}, bf16[128,256]{1,0:T(8,128)(2,1)S(1)}, u32[]{:S(2)}, u32[]{:S(2)}) collective-permute-start(bf16[128,256]{1,0:T(8,128)(2,1)S(1)} %get-tuple-element.178), channel_id=1, source_target_pairs={{0,8},{1,9},{2,10},{3,11},{4,12},{5,13},{6,14},{7,15},{8,0},{9,1},... | collective-permute-start | bytes 196616 | tf_op jit(solution)/shard_map/ppermute | solution.py:40
  132.9 1.7 %gradient.3 = (bf16[128,256]{1,0:T(8,128)(2,1)S(1)}, bf16[128,256]{1,0:T(8,128)(2,1)S(1)}, bf16[128,256]{1,0:T(8,128)(2,1)S(1)}, bf16[128,256]{1,0:T(8,128)(2,1)...) custom-call(s32[3]{0:T(128)S(1)} %pad_add_fusion.place_ref, bf16[128,384]{1,0:T(8,128)(2,1)S(1)} %finish.1.refs_0_, ...), custom_call_target="tpu_custom_call" | custom-call | tf_op jit(solution)/shard_map/gradient/pallas_call | solution.py:190
  134.6 1.8 %collective-permute-start.54 = (bf16[128,256]{1,0:T(8,128)(2,1)S(1)}, bf16[128,256]{1,0:T(8,128)(2,1)S(1)}, u32[]{:S(2)}, u32[]{:S(2)}) collective-permute-start(bf16[128,256]{1,0:T(8,128)(2,1)S(1)} %get-tuple-element.182), channel_id=1, source_target_pairs={{0,24},{1,25},{2,26},{3,27},{4,28},{5,29},{6,30},{7,31},{8,16},{9,... | collective-permute-start | bytes 196616 | tf_op jit(solution)/shard_map/ppermute | solution.py:40
  136.4 2.5 %collective-permute-start.56 = (bf16[128,256]{1,0:T(8,128)(2,1)S(1)}, bf16[128,256]{1,0:T(8,128)(2,1)S(1)}, u32[]{:S(2)}, u32[]{:S(2)}) collective-permute-start(bf16[128,256]{1,0:T(8,128)(2,1)S(1)} %get-tuple-element.184), channel_id=1, source_target_pairs={{0,8},{1,9},{2,10},{3,11},{4,12},{5,13},{6,14},{7,15},{8,0},{9,1},... | collective-permute-start | bytes 196616 | tf_op jit(solution)/shard_map/ppermute | solution.py:40
  139.0 2.1 %loss.1 = f32[1,1]{1,0:T(1,128)} custom-call(s32[3]{0:T(128)S(1)} %pad_add_fusion.place_ref, bf16[512,512]{1,0:T(8,128)(2,1)S(1)} %get-tuple-element.185.first_ref, bf16[512,512]{1,0:T(8,128)(2,1)S(1)} %get-tuple-element.186.second_ref, f32[1,1]{1,0:T(1,128)} %get-tuple-element.187.share_ref), custom_call_target="tpu_custom_call" | custom-call | tf_op jit(solution)/shard_map/loss/pallas_call | solution.py:190
  141.1 1.3 place.2
  142.9 1.3 place.3
  (78 shorter events, 13.3 us)
Async XLA Ops:
  1.6 9.1 %collective-permute-start.10 = (bf16[32,1024]{1,0:T(8,128)(2,1)S(1)}, bf16[32,1024]{1,0:T(8,128)(2,1)S(1)}, u32[]{:S(2)}, u32[]{:S(2)}) collective-permute-start(bf16[32,1024]{1,0:T(8,128)(2,1)S(1)} %get-tuple-element.196), channel_id=1, source_target_pairs={{0,6},{1,7},{2,4},{3,5},{4,2},{5,3},{6,0},{7,1},{8,14},{9,15},{10,... | collective-permute-start | bytes 196616 | tf_op jit(solution)/shard_map/ppermute | solution.py:40
  5.6 5.2 %collective-permute-start.9 = (bf16[32,1024]{1,0:T(8,128)(2,1)S(1)}, bf16[32,1024]{1,0:T(8,128)(2,1)S(1)}, u32[]{:S(2)}, u32[]{:S(2)}) collective-permute-start(bf16[32,1024]{1,0:T(8,128)(2,1)S(1)} %get-tuple-element.197), channel_id=1, source_target_pairs={{0,4},{1,5},{2,6},{3,7},{4,0},{5,1},{6,2},{7,3},{8,12},{9,13},{10,... | collective-permute-start | bytes 196616 | tf_op jit(solution)/shard_map/ppermute | solution.py:40
  6.1 4.7 %collective-permute-start.8 = (bf16[32,1024]{1,0:T(8,128)(2,1)S(1)}, bf16[32,1024]{1,0:T(8,128)(2,1)S(1)}, u32[]{:S(2)}, u32[]{:S(2)}) collective-permute-start(bf16[32,1024]{1,0:T(8,128)(2,1)S(1)} %get-tuple-element.198), channel_id=1, source_target_pairs={{0,2},{1,3},{2,0},{3,1},{4,6},{5,7},{6,4},{7,5},{8,10},{9,11},{10,... | collective-permute-start | bytes 196616 | tf_op jit(solution)/shard_map/ppermute | solution.py:40
  7.2 8.9 %collective-permute-start.16 = (bf16[32,1024]{1,0:T(8,128)(2,1)S(1)}, bf16[32,1024]{1,0:T(8,128)(2,1)S(1)}, u32[]{:S(2)}, u32[]{:S(2)}) collective-permute-start(bf16[32,1024]{1,0:T(8,128)(2,1)S(1)} %get-tuple-element.192), channel_id=1, source_target_pairs={{0,6},{1,7},{2,4},{3,5},{4,2},{5,3},{6,0},{7,1},{8,14},{9,15},{10,... | collective-permute-start | bytes 196616 | tf_op jit(solution)/shard_map/ppermute | solution.py:40
  10.1 6.5 %collective-permute-start.15 = (bf16[32,1024]{1,0:T(8,128)(2,1)S(1)}, bf16[32,1024]{1,0:T(8,128)(2,1)S(1)}, u32[]{:S(2)}, u32[]{:S(2)}) collective-permute-start(bf16[32,1024]{1,0:T(8,128)(2,1)S(1)} %get-tuple-element.193), channel_id=1, source_target_pairs={{0,4},{1,5},{2,6},{3,7},{4,0},{5,1},{6,2},{7,3},{8,12},{9,13},{10,... | collective-permute-start | bytes 196616 | tf_op jit(solution)/shard_map/ppermute | solution.py:40
  10.7 5.9 %collective-permute-start.14 = (bf16[32,1024]{1,0:T(8,128)(2,1)S(1)}, bf16[32,1024]{1,0:T(8,128)(2,1)S(1)}, u32[]{:S(2)}, u32[]{:S(2)}) collective-permute-start(bf16[32,1024]{1,0:T(8,128)(2,1)S(1)} %get-tuple-element.194), channel_id=1, source_target_pairs={{0,2},{1,3},{2,0},{3,1},{4,6},{5,7},{6,4},{7,5},{8,10},{9,11},{10,... | collective-permute-start | bytes 196616 | tf_op jit(solution)/shard_map/ppermute | solution.py:40
  11.4 5.2 %collective-permute-start.11 = (bf16[32,1024]{1,0:T(8,128)(2,1)S(1)}, bf16[32,1024]{1,0:T(8,128)(2,1)S(1)}, u32[]{:S(2)}, u32[]{:S(2)}) collective-permute-start(bf16[32,1024]{1,0:T(8,128)(2,1)S(1)} %get-tuple-element.113), channel_id=1, source_target_pairs={{0,8},{1,9},{2,10},{3,11},{4,12},{5,13},{6,14},{7,15},{8,0},{9,1},... | collective-permute-start | bytes 196616 | tf_op jit(solution)/shard_map/ppermute | solution.py:40
  13.5 6.6 %collective-permute-start.12 = (bf16[32,1024]{1,0:T(8,128)(2,1)S(1)}, bf16[32,1024]{1,0:T(8,128)(2,1)S(1)}, u32[]{:S(2)}, u32[]{:S(2)}) collective-permute-start(bf16[32,1024]{1,0:T(8,128)(2,1)S(1)} %get-tuple-element.114), channel_id=1, source_target_pairs={{0,16},{1,17},{2,18},{3,19},{4,20},{5,21},{6,22},{7,23},{8,24},{9,... | collective-permute-start | bytes 196616 | tf_op jit(solution)/shard_map/ppermute | solution.py:40
  16.1 6.1 %collective-permute-start.13 = (bf16[32,1024]{1,0:T(8,128)(2,1)S(1)}, bf16[32,1024]{1,0:T(8,128)(2,1)S(1)}, u32[]{:S(2)}, u32[]{:S(2)}) collective-permute-start(bf16[32,1024]{1,0:T(8,128)(2,1)S(1)} %get-tuple-element.115), channel_id=1, source_target_pairs={{0,24},{1,25},{2,26},{3,27},{4,28},{5,29},{6,30},{7,31},{8,16},{9,... | collective-permute-start | bytes 196616 | tf_op jit(solution)/shard_map/ppermute | solution.py:40
  22.7 15.0 %collective-permute-start.19 = (bf16[128,1024]{1,0:T(8,128)(2,1)S(1)}, bf16[128,1024]{1,0:T(8,128)(2,1)S(1)}, u32[]{:S(2)}, u32[]{:S(2)}) collective-permute-start(bf16[128,1024]{1,0:T(8,128)(2,1)S(1)} %lay.2.refs_0_), channel_id=1, source_target_pairs={{0,6},{1,7},{2,4},{3,5},{4,2},{5,3},{6,0},{7,1},{8,14},{9,15},{10,... | collective-permute-start | bytes 786440 | tf_op jit(solution)/shard_map/ppermute | solution.py:40
  25.2 12.5 %collective-permute-start.18 = (bf16[128,1024]{1,0:T(8,128)(2,1)S(1)}, bf16[128,1024]{1,0:T(8,128)(2,1)S(1)}, u32[]{:S(2)}, u32[]{:S(2)}) collective-permute-start(bf16[128,1024]{1,0:T(8,128)(2,1)S(1)} %lay.2.refs_0_), channel_id=1, source_target_pairs={{0,4},{1,5},{2,6},{3,7},{4,0},{5,1},{6,2},{7,3},{8,12},{9,13},{10,... | collective-permute-start | bytes 786440 | tf_op jit(solution)/shard_map/ppermute | solution.py:40
  25.7 12.0 %collective-permute-start.17 = (bf16[128,1024]{1,0:T(8,128)(2,1)S(1)}, bf16[128,1024]{1,0:T(8,128)(2,1)S(1)}, u32[]{:S(2)}, u32[]{:S(2)}) collective-permute-start(bf16[128,1024]{1,0:T(8,128)(2,1)S(1)} %lay.2.refs_0_), channel_id=1, source_target_pairs={{0,2},{1,3},{2,0},{3,1},{4,6},{5,7},{6,4},{7,5},{8,10},{9,11},{10,... | collective-permute-start | bytes 786440 | tf_op jit(solution)/shard_map/ppermute | solution.py:40
  26.3 6.2 %collective-permute-start.22 = (bf16[32,1024]{1,0:T(8,128)(2,1)S(1)}, bf16[32,1024]{1,0:T(8,128)(2,1)S(1)}, u32[]{:S(2)}, u32[]{:S(2)}) collective-permute-start(bf16[32,1024]{1,0:T(8,128)(2,1)S(1)} %get-tuple-element.188), channel_id=1, source_target_pairs={{0,24},{1,25},{2,26},{3,27},{4,28},{5,29},{6,30},{7,31},{8,16},{9,... | collective-permute-start | bytes 196616 | tf_op jit(solution)/shard_map/ppermute | solution.py:40
  27.1 7.6 %collective-permute-start.20 = (bf16[32,1024]{1,0:T(8,128)(2,1)S(1)}, bf16[32,1024]{1,0:T(8,128)(2,1)S(1)}, u32[]{:S(2)}, u32[]{:S(2)}) collective-permute-start(bf16[32,1024]{1,0:T(8,128)(2,1)S(1)} %get-tuple-element.189), channel_id=1, source_target_pairs={{0,8},{1,9},{2,10},{3,11},{4,12},{5,13},{6,14},{7,15},{8,0},{9,1},... | collective-permute-start | bytes 196616 | tf_op jit(solution)/shard_map/ppermute | solution.py:40
  32.5 5.2 %collective-permute-start.21 = (bf16[32,1024]{1,0:T(8,128)(2,1)S(1)}, bf16[32,1024]{1,0:T(8,128)(2,1)S(1)}, u32[]{:S(2)}, u32[]{:S(2)}) collective-permute-start(bf16[32,1024]{1,0:T(8,128)(2,1)S(1)} %get-tuple-element.190), channel_id=1, source_target_pairs={{0,16},{1,17},{2,18},{3,19},{4,20},{5,21},{6,22},{7,23},{8,24},{9,... | collective-permute-start | bytes 196616 | tf_op jit(solution)/shard_map/ppermute | solution.py:40
  37.7 4.2 %collective-permute-start.23 = (bf16[128,1024]{1,0:T(8,128)(2,1)S(1)}, bf16[128,1024]{1,0:T(8,128)(2,1)S(1)}, u32[]{:S(2)}, u32[]{:S(2)}) collective-permute-start(bf16[128,1024]{1,0:T(8,128)(2,1)S(1)} %lay.2.refs_0_), channel_id=1, source_target_pairs={{0,1},{1,0},{2,3},{3,2},{4,5},{5,4},{6,7},{7,6},{8,9},{9,8},{10,11... | collective-permute-start | bytes 786440 | tf_op jit(solution)/shard_map/ppermute | solution.py:40
  37.8 4.1 %collective-permute-start.24 = (bf16[128,1024]{1,0:T(8,128)(2,1)S(1)}, bf16[128,1024]{1,0:T(8,128)(2,1)S(1)}, u32[]{:S(2)}, u32[]{:S(2)}) collective-permute-start(bf16[128,1024]{1,0:T(8,128)(2,1)S(1)} %collective-permute-done.17.refs_1_), channel_id=1, source_target_pairs={{0,1},{1,0},{2,3},{3,2},{4,5},{5,4},{6,7},{7,6},{8,9},{9,8},{10,11... | collective-permute-start | bytes 786440 | tf_op jit(solution)/shard_map/ppermute | solution.py:40
  38.3 3.6 %collective-permute-start.25 = (bf16[128,1024]{1,0:T(8,128)(2,1)S(1)}, bf16[128,1024]{1,0:T(8,128)(2,1)S(1)}, u32[]{:S(2)}, u32[]{:S(2)}) collective-permute-start(bf16[128,1024]{1,0:T(8,128)(2,1)S(1)} %collective-permute-done.18.refs_2_), channel_id=1, source_target_pairs={{0,1},{1,0},{2,3},{3,2},{4,5},{5,4},{6,7},{7,6},{8,9},{9,8},{10,11... | collective-permute-start | bytes 786440 | tf_op jit(solution)/shard_map/ppermute | solution.py:40
  38.3 3.5 %collective-permute-start.26 = (bf16[128,1024]{1,0:T(8,128)(2,1)S(1)}, bf16[128,1024]{1,0:T(8,128)(2,1)S(1)}, u32[]{:S(2)}, u32[]{:S(2)}) collective-permute-start(bf16[128,1024]{1,0:T(8,128)(2,1)S(1)} %collective-permute-done.19.refs_3_), channel_id=1, source_target_pairs={{0,1},{1,0},{2,3},{3,2},{4,5},{5,4},{6,7},{7,6},{8,9},{9,8},{10,11... | collective-permute-start | bytes 786440 | tf_op jit(solution)/shard_map/ppermute | solution.py:40
  39.3 10.9 %collective-permute-start.27 = (bf16[128,1024]{1,0:T(8,128)(2,1)S(1)}, bf16[128,1024]{1,0:T(8,128)(2,1)}, u32[]{:S(2)}, u32[]{:S(2)}) collective-permute-start(bf16[128,1024]{1,0:T(8,128)(2,1)S(1)} %lay.3), channel_id=1, source_target_pairs={{0,6},{1,7},{2,4},{3,5},{4,2},{5,3},{6,0},{7,1},{8,14},{9,15},{10,... | collective-permute-start | bytes 786440 | tf_op jit(solution)/shard_map/ppermute | solution.py:40
  45.8 23.0 %collective-permute-start.31 = (bf16[528,256]{1,0:T(8,128)(2,1)S(1)}, bf16[528,256]{1,0:T(8,128)(2,1)S(1)}, u32[]{:S(2)}, u32[]{:S(2)}) collective-permute-start(bf16[528,256]{1,0:T(8,128)(2,1)S(1)} %get-tuple-element.147), channel_id=1, source_target_pairs={{0,24},{1,25},{2,26},{3,27},{4,28},{5,29},{6,30},{7,31},{8,16},{9,... | collective-permute-start | bytes 811016 | tf_op jit(solution)/shard_map/ppermute | solution.py:40
  47.4 23.6 %collective-permute-start.32 = (bf16[528,256]{1,0:T(8,128)(2,1)S(1)}, bf16[528,256]{1,0:T(8,128)(2,1)S(1)}, u32[]{:S(2)}, u32[]{:S(2)}) collective-permute-start(bf16[528,256]{1,0:T(8,128)(2,1)S(1)} %get-tuple-element.148), channel_id=1, source_target_pairs={{0,16},{1,17},{2,18},{3,19},{4,20},{5,21},{6,22},{7,23},{8,24},{9,... | collective-permute-start | bytes 811016 | tf_op jit(solution)/shard_map/ppermute | solution.py:40
  47.5 23.6 %collective-permute-start.33 = (bf16[528,256]{1,0:T(8,128)(2,1)S(1)}, bf16[528,256]{1,0:T(8,128)(2,1)S(1)}, u32[]{:S(2)}, u32[]{:S(2)}) collective-permute-start(bf16[528,256]{1,0:T(8,128)(2,1)S(1)} %get-tuple-element.149), channel_id=1, source_target_pairs={{0,8},{1,9},{2,10},{3,11},{4,12},{5,13},{6,14},{7,15},{8,0},{9,1},... | collective-permute-start | bytes 811016 | tf_op jit(solution)/shard_map/ppermute | solution.py:40
  50.2 7.2 %collective-permute-start.4 = (bf16[128,1024]{1,0:T(8,128)(2,1)S(1)}, bf16[128,1024]{1,0:T(8,128)(2,1)S(1)}, u32[]{:S(2)}, u32[]{:S(2)}) collective-permute-start(bf16[128,1024]{1,0:T(8,128)(2,1)S(1)} %get-tuple-element.16.refs_0_), channel_id=1, source_target_pairs={{0,2},{1,3},{2,0},{3,1},{4,6},{5,7},{6,4},{7,5},{8,10},{9,11},{10,... | collective-permute-start | bytes 786440 | tf_op jit(solution)/shard_map/cond/branch_1_fun/ppermute | solution.py:40
  50.8 6.9 %collective-permute-start.5 = (bf16[128,1024]{1,0:T(8,128)(2,1)S(1)}, bf16[128,1024]{1,0:T(8,128)(2,1)S(1)}, u32[]{:S(2)}, u32[]{:S(2)}) collective-permute-start(bf16[128,1024]{1,0:T(8,128)(2,1)S(1)} %get-tuple-element.16.refs_0_), channel_id=1, source_target_pairs={{0,4},{1,5},{2,6},{3,7},{4,0},{5,1},{6,2},{7,3},{8,12},{9,13},{10,... | collective-permute-start | bytes 786440 | tf_op jit(solution)/shard_map/cond/branch_1_fun/ppermute | solution.py:40
  57.7 3.9 %collective-permute-start.7 = (bf16[256,1024]{1,0:T(8,128)(2,1)S(1)}, bf16[256,1024]{1,0:T(8,128)(2,1)S(1)}, u32[]{:S(2)}, u32[]{:S(2)}) collective-permute-start(bf16[256,1024]{1,0:T(8,128)(2,1)S(1)} %pad_maximum_fusion.1), channel_id=1, source_target_pairs={{0,1},{1,0},{2,3},{3,2},{4,5},{5,4},{6,7},{7,6},{8,9},{9,8},{10,11... | collective-permute-start | bytes 1572872 | tf_op jit(solution)/shard_map/cond/branch_1_fun/ppermute | solution.py:40
  58.8 2.8 %collective-permute-start.6 = (bf16[256,1024]{1,0:T(8,128)(2,1)S(1)}, bf16[256,1024]{1,0:T(8,128)(2,1)S(1)}, u32[]{:S(2)}, u32[]{:S(2)}) collective-permute-start(bf16[256,1024]{1,0:T(8,128)(2,1)S(1)} %pad_maximum_fusion), channel_id=1, source_target_pairs={{0,1},{1,0},{2,3},{3,2},{4,5},{5,4},{6,7},{7,6},{8,9},{9,8},{10,11... | collective-permute-start | bytes 1572872 | tf_op jit(solution)/shard_map/cond/branch_1_fun/ppermute | solution.py:40
  66.6 23.8 %collective-permute-start.28 = (bf16[528,256]{1,0:T(8,128)(2,1)}, bf16[528,256]{1,0:T(8,128)(2,1)S(1)}, u32[]{:S(2)}, u32[]{:S(2)}) collective-permute-start(bf16[528,256]{1,0:T(8,128)(2,1)} %get-tuple-element.143), channel_id=1, source_target_pairs={{0,8},{1,9},{2,10},{3,11},{4,12},{5,13},{6,14},{7,15},{8,0},{9,1},... | collective-permute-start | bytes 811016 | tf_op jit(solution)/shard_map/ppermute | solution.py:40
  66.9 25.5 %collective-permute-start.29 = (bf16[528,256]{1,0:T(8,128)(2,1)}, bf16[528,256]{1,0:T(8,128)(2,1)S(1)}, u32[]{:S(2)}, u32[]{:S(2)}) collective-permute-start(bf16[528,256]{1,0:T(8,128)(2,1)} %get-tuple-element.144), channel_id=1, source_target_pairs={{0,16},{1,17},{2,18},{3,19},{4,20},{5,21},{6,22},{7,23},{8,24},{9,... | collective-permute-start | bytes 811016 | tf_op jit(solution)/shard_map/ppermute | solution.py:40
  68.8 23.6 %collective-permute-start.30 = (bf16[528,256]{1,0:T(8,128)(2,1)}, bf16[528,256]{1,0:T(8,128)(2,1)S(1)}, u32[]{:S(2)}, u32[]{:S(2)}) collective-permute-start(bf16[528,256]{1,0:T(8,128)(2,1)} %get-tuple-element.145), channel_id=1, source_target_pairs={{0,24},{1,25},{2,26},{3,27},{4,28},{5,29},{6,30},{7,31},{8,16},{9,... | collective-permute-start | bytes 811016 | tf_op jit(solution)/shard_map/ppermute | solution.py:40
  74.4 2.1 %collective-permute-start = (f32[256,512]{1,0:T(8,128)}, f32[256,512]{1,0:T(8,128)S(1)}, u32[]{:S(2)}, u32[]{:S(2)}) collective-permute-start(f32[256,512]{1,0:T(8,128)} %get-tuple-element.26), channel_id=1, source_target_pairs={{0,1},{1,0},{2,3},{3,2},{4,5},{5,4},{6,7},{7,6},{8,9},{9,8},{10,11... | collective-permute-start | bytes 1572872 | tf_op jit(solution)/shard_map/cond/branch_1_fun/ppermute | solution.py:40
  77.8 4.2 %collective-permute-start.1 = (bf16[208,128]{1,0:T(8,128)(2,1)S(1)}, bf16[208,128]{1,0:T(8,128)(2,1)S(1)}, u32[]{:S(2)}, u32[]{:S(2)}) collective-permute-start(bf16[208,128]{1,0:T(8,128)(2,1)S(1)} %get-tuple-element.28), channel_id=1, source_target_pairs={{0,2},{1,3},{2,0},{3,1},{4,6},{5,7},{6,4},{7,5},{8,10},{9,11},{10,... | collective-permute-start | bytes 159752 | tf_op jit(solution)/shard_map/cond/branch_1_fun/ppermute | solution.py:40
  79.4 4.1 %collective-permute-start.2 = (bf16[208,128]{1,0:T(8,128)(2,1)S(1)}, bf16[208,128]{1,0:T(8,128)(2,1)S(1)}, u32[]{:S(2)}, u32[]{:S(2)}) collective-permute-start(bf16[208,128]{1,0:T(8,128)(2,1)S(1)} %get-tuple-element.31), channel_id=1, source_target_pairs={{0,4},{1,5},{2,6},{3,7},{4,0},{5,1},{6,2},{7,3},{8,12},{9,13},{10,... | collective-permute-start | bytes 159752 | tf_op jit(solution)/shard_map/cond/branch_1_fun/ppermute | solution.py:40
  82.0 5.0 %collective-permute-start.3 = (bf16[208,128]{1,0:T(8,128)(2,1)S(1)}, bf16[208,128]{1,0:T(8,128)(2,1)S(1)}, u32[]{:S(2)}, u32[]{:S(2)}) collective-permute-start(bf16[208,128]{1,0:T(8,128)(2,1)S(1)} %get-tuple-element.32), channel_id=1, source_target_pairs={{0,6},{1,7},{2,4},{3,5},{4,2},{5,3},{6,0},{7,1},{8,14},{9,15},{10,... | collective-permute-start | bytes 159752 | tf_op jit(solution)/shard_map/cond/branch_1_fun/ppermute | solution.py:40
  87.9 4.5 %collective-permute-start.34 = (bf16[64,128]{1,0:T(8,128)(2,1)S(1)}, bf16[64,128]{1,0:T(8,128)(2,1)S(1)}, u32[]{:S(2)}, u32[]{:S(2)}) collective-permute-start(bf16[64,128]{1,0:T(8,128)(2,1)S(1)} %get-tuple-element.153), channel_id=1, source_target_pairs={{0,8},{1,9},{2,10},{3,11},{4,12},{5,13},{6,14},{7,15},{8,0},{9,1},... | collective-permute-start | bytes 49160 | tf_op jit(solution)/shard_map/ppermute | solution.py:40
  88.0 6.6 %collective-permute-start.35 = (bf16[64,128]{1,0:T(8,128)(2,1)S(1)}, bf16[64,128]{1,0:T(8,128)(2,1)S(1)}, u32[]{:S(2)}, u32[]{:S(2)}) collective-permute-start(bf16[64,128]{1,0:T(8,128)(2,1)S(1)} %get-tuple-element.154), channel_id=1, source_target_pairs={{0,16},{1,17},{2,18},{3,19},{4,20},{5,21},{6,22},{7,23},{8,24},{9,... | collective-permute-start | bytes 49160 | tf_op jit(solution)/shard_map/ppermute | solution.py:40
  90.4 5.5 %collective-permute-start.36 = (bf16[64,128]{1,0:T(8,128)(2,1)S(1)}, bf16[64,128]{1,0:T(8,128)(2,1)S(1)}, u32[]{:S(2)}, u32[]{:S(2)}) collective-permute-start(bf16[64,128]{1,0:T(8,128)(2,1)S(1)} %get-tuple-element.155), channel_id=1, source_target_pairs={{0,24},{1,25},{2,26},{3,27},{4,28},{5,29},{6,30},{7,31},{8,16},{9,... | collective-permute-start | bytes 49160 | tf_op jit(solution)/shard_map/ppermute | solution.py:40
  98.5 2.0 %collective-permute-start.37 = (f32[256,512]{1,0:T(8,128)S(1)}, f32[256,512]{1,0:T(8,128)S(1)}, u32[]{:S(2)}, u32[]{:S(2)}) collective-permute-start(f32[256,512]{1,0:T(8,128)S(1)} %get-tuple-element.162), channel_id=1, source_target_pairs={{0,1},{1,0},{2,3},{3,2},{4,5},{5,4},{6,7},{7,6},{8,9},{9,8},{10,11... | collective-permute-start | bytes 1572872 | tf_op jit(solution)/shard_map/ppermute | solution.py:40
  101.3 4.2 %collective-permute-start.38 = (bf16[208,128]{1,0:T(8,128)(2,1)S(1)}, bf16[208,128]{1,0:T(8,128)(2,1)S(1)}, u32[]{:S(2)}, u32[]{:S(2)}) collective-permute-start(bf16[208,128]{1,0:T(8,128)(2,1)S(1)} %get-tuple-element.164), channel_id=1, source_target_pairs={{0,2},{1,3},{2,0},{3,1},{4,6},{5,7},{6,4},{7,5},{8,10},{9,11},{10,... | collective-permute-start | bytes 159752 | tf_op jit(solution)/shard_map/ppermute | solution.py:40
  102.6 4.7 %collective-permute-start.39 = (bf16[208,128]{1,0:T(8,128)(2,1)S(1)}, bf16[208,128]{1,0:T(8,128)(2,1)S(1)}, u32[]{:S(2)}, u32[]{:S(2)}) collective-permute-start(bf16[208,128]{1,0:T(8,128)(2,1)S(1)} %get-tuple-element.165), channel_id=1, source_target_pairs={{0,4},{1,5},{2,6},{3,7},{4,0},{5,1},{6,2},{7,3},{8,12},{9,13},{10,... | collective-permute-start | bytes 159752 | tf_op jit(solution)/shard_map/ppermute | solution.py:40
  103.2 5.0 %collective-permute-start.40 = (bf16[208,128]{1,0:T(8,128)(2,1)S(1)}, bf16[208,128]{1,0:T(8,128)(2,1)S(1)}, u32[]{:S(2)}, u32[]{:S(2)}) collective-permute-start(bf16[208,128]{1,0:T(8,128)(2,1)S(1)} %get-tuple-element.166), channel_id=1, source_target_pairs={{0,6},{1,7},{2,4},{3,5},{4,2},{5,3},{6,0},{7,1},{8,14},{9,15},{10,... | collective-permute-start | bytes 159752 | tf_op jit(solution)/shard_map/ppermute | solution.py:40
  109.1 6.8 %collective-permute-start.43 = (bf16[256,128]{1,0:T(8,128)(2,1)S(1)}, bf16[256,128]{1,0:T(8,128)(2,1)S(1)}, u32[]{:S(2)}, u32[]{:S(2)}) collective-permute-start(bf16[256,128]{1,0:T(8,128)(2,1)S(1)} %code.1.refs_0_), channel_id=1, source_target_pairs={{0,24},{1,25},{2,26},{3,27},{4,28},{5,29},{6,30},{7,31},{8,16},{9,... | collective-permute-start | bytes 196616 | tf_op jit(solution)/shard_map/ppermute | solution.py:40
  111.4 5.7 %collective-permute-start.42 = (bf16[256,128]{1,0:T(8,128)(2,1)S(1)}, bf16[256,128]{1,0:T(8,128)(2,1)S(1)}, u32[]{:S(2)}, u32[]{:S(2)}) collective-permute-start(bf16[256,128]{1,0:T(8,128)(2,1)S(1)} %code.1.refs_0_), channel_id=1, source_target_pairs={{0,16},{1,17},{2,18},{3,19},{4,20},{5,21},{6,22},{7,23},{8,24},{9,... | collective-permute-start | bytes 196616 | tf_op jit(solution)/shard_map/ppermute | solution.py:40
  111.4 5.7 %collective-permute-start.41 = (bf16[256,128]{1,0:T(8,128)(2,1)S(1)}, bf16[256,128]{1,0:T(8,128)(2,1)S(1)}, u32[]{:S(2)}, u32[]{:S(2)}) collective-permute-start(bf16[256,128]{1,0:T(8,128)(2,1)S(1)} %code.1.refs_0_), channel_id=1, source_target_pairs={{0,8},{1,9},{2,10},{3,11},{4,12},{5,13},{6,14},{7,15},{8,0},{9,1},... | collective-permute-start | bytes 196616 | tf_op jit(solution)/shard_map/ppermute | solution.py:40
  118.1 5.6 %collective-permute-start.46 = (bf16[128,384]{1,0:T(8,128)(2,1)S(1)}, bf16[128,384]{1,0:T(8,128)(2,1)S(1)}, u32[]{:S(2)}, u32[]{:S(2)}) collective-permute-start(bf16[128,384]{1,0:T(8,128)(2,1)S(1)} %finish.1.refs_0_), channel_id=1, source_target_pairs={{0,6},{1,7},{2,4},{3,5},{4,2},{5,3},{6,0},{7,1},{8,14},{9,15},{10,... | collective-permute-start | bytes 294920 | tf_op jit(solution)/shard_map/ppermute | solution.py:40
  119.6 5.1 %collective-permute-start.45 = (bf16[128,384]{1,0:T(8,128)(2,1)S(1)}, bf16[128,384]{1,0:T(8,128)(2,1)S(1)}, u32[]{:S(2)}, u32[]{:S(2)}) collective-permute-start(bf16[128,384]{1,0:T(8,128)(2,1)S(1)} %finish.1.refs_0_), channel_id=1, source_target_pairs={{0,4},{1,5},{2,6},{3,7},{4,0},{5,1},{6,2},{7,3},{8,12},{9,13},{10,... | collective-permute-start | bytes 294920 | tf_op jit(solution)/shard_map/ppermute | solution.py:40
  120.9 4.6 %collective-permute-start.44 = (bf16[128,384]{1,0:T(8,128)(2,1)S(1)}, bf16[128,384]{1,0:T(8,128)(2,1)S(1)}, u32[]{:S(2)}, u32[]{:S(2)}) collective-permute-start(bf16[128,384]{1,0:T(8,128)(2,1)S(1)} %finish.1.refs_0_), channel_id=1, source_target_pairs={{0,2},{1,3},{2,0},{3,1},{4,6},{5,7},{6,4},{7,5},{8,10},{9,11},{10,... | collective-permute-start | bytes 294920 | tf_op jit(solution)/shard_map/ppermute | solution.py:40
  121.7 3.9 %collective-permute-start.47 = (bf16[128,384]{1,0:T(8,128)(2,1)S(1)}, bf16[128,384]{1,0:T(8,128)(2,1)S(1)}, u32[]{:S(2)}, u32[]{:S(2)}) collective-permute-start(bf16[128,384]{1,0:T(8,128)(2,1)S(1)} %finish.1.refs_0_), channel_id=1, source_target_pairs={{0,1},{1,0},{2,3},{3,2},{4,5},{5,4},{6,7},{7,6},{8,9},{9,8},{10,11... | collective-permute-start | bytes 294920 | tf_op jit(solution)/shard_map/ppermute | solution.py:40
  123.7 1.8 %collective-permute-start.50 = (bf16[128,384]{1,0:T(8,128)(2,1)S(1)}, bf16[128,384]{1,0:T(8,128)(2,1)S(1)}, u32[]{:S(2)}, u32[]{:S(2)}) collective-permute-start(bf16[128,384]{1,0:T(8,128)(2,1)S(1)} %collective-permute-done.46.refs_3_), channel_id=1, source_target_pairs={{0,1},{1,0},{2,3},{3,2},{4,5},{5,4},{6,7},{7,6},{8,9},{9,8},{10,11... | collective-permute-start | bytes 294920 | tf_op jit(solution)/shard_map/ppermute | solution.py:40
  124.7 1.3 collective-permute-start.49
  125.5 1.3 collective-permute-start.48
  128.5 7.9 %collective-permute-start.51 = (bf16[128,256]{1,0:T(8,128)(2,1)S(1)}, bf16[128,256]{1,0:T(8,128)(2,1)S(1)}, u32[]{:S(2)}, u32[]{:S(2)}) collective-permute-start(bf16[128,256]{1,0:T(8,128)(2,1)S(1)} %get-tuple-element.176), channel_id=1, source_target_pairs={{0,24},{1,25},{2,26},{3,27},{4,28},{5,29},{6,30},{7,31},{8,16},{9,... | collective-permute-start | bytes 196616 | tf_op jit(solution)/shard_map/ppermute | solution.py:40
  130.3 10.7 %collective-permute-start.52 = (bf16[128,256]{1,0:T(8,128)(2,1)S(1)}, bf16[128,256]{1,0:T(8,128)(2,1)S(1)}, u32[]{:S(2)}, u32[]{:S(2)}) collective-permute-start(bf16[128,256]{1,0:T(8,128)(2,1)S(1)} %get-tuple-element.177), channel_id=1, source_target_pairs={{0,16},{1,17},{2,18},{3,19},{4,20},{5,21},{6,22},{7,23},{8,24},{9,... | collective-permute-start | bytes 196616 | tf_op jit(solution)/shard_map/ppermute | solution.py:40
  130.7 10.3 %collective-permute-start.53 = (bf16[128,256]{1,0:T(8,128)(2,1)S(1)}, bf16[128,256]{1,0:T(8,128)(2,1)S(1)}, u32[]{:S(2)}, u32[]{:S(2)}) collective-permute-start(bf16[128,256]{1,0:T(8,128)(2,1)S(1)} %get-tuple-element.178), channel_id=1, source_target_pairs={{0,8},{1,9},{2,10},{3,11},{4,12},{5,13},{6,14},{7,15},{8,0},{9,1},... | collective-permute-start | bytes 196616 | tf_op jit(solution)/shard_map/ppermute | solution.py:40
  134.6 7.8 %collective-permute-start.54 = (bf16[128,256]{1,0:T(8,128)(2,1)S(1)}, bf16[128,256]{1,0:T(8,128)(2,1)S(1)}, u32[]{:S(2)}, u32[]{:S(2)}) collective-permute-start(bf16[128,256]{1,0:T(8,128)(2,1)S(1)} %get-tuple-element.182), channel_id=1, source_target_pairs={{0,24},{1,25},{2,26},{3,27},{4,28},{5,29},{6,30},{7,31},{8,16},{9,... | collective-permute-start | bytes 196616 | tf_op jit(solution)/shard_map/ppermute | solution.py:40
  136.4 6.5 %collective-permute-start.55 = (bf16[128,256]{1,0:T(8,128)(2,1)S(1)}, bf16[128,256]{1,0:T(8,128)(2,1)S(1)}, u32[]{:S(2)}, u32[]{:S(2)}) collective-permute-start(bf16[128,256]{1,0:T(8,128)(2,1)S(1)} %get-tuple-element.183), channel_id=1, source_target_pairs={{0,16},{1,17},{2,18},{3,19},{4,20},{5,21},{6,22},{7,23},{8,24},{9,... | collective-permute-start | bytes 196616 | tf_op jit(solution)/shard_map/ppermute | solution.py:40
  136.4 6.5 %collective-permute-start.56 = (bf16[128,256]{1,0:T(8,128)(2,1)S(1)}, bf16[128,256]{1,0:T(8,128)(2,1)S(1)}, u32[]{:S(2)}, u32[]{:S(2)}) collective-permute-start(bf16[128,256]{1,0:T(8,128)(2,1)S(1)} %get-tuple-element.184), channel_id=1, source_target_pairs={{0,8},{1,9},{2,10},{3,11},{4,12},{5,13},{6,14},{7,15},{8,0},{9,1},... | collective-permute-start | bytes 196616 | tf_op jit(solution)/shard_map/ppermute | solution.py:40
